TPU v7x, 256 devices: a whole 4x4x8 slice. The times are simulated.
256 devices in a mesh: dp: 32 (over y, z_hi, core), expert: 8 (over x, z_lo).
Axes of the slice: x: 4, y: 4, z: 8 (z_hi: 4, z_lo: 2; z = z_hi * 2 + z_lo), core: 2. Of those that a mesh axis runs over, the one named last changes fastest.
Arguments:
- tokens: bfloat16 [65536, 2048], P(('dp', 'expert')), may hold values from -6 to 6
- grad_out: bfloat16 [65536, 2048], P(('dp', 'expert')), may hold values from -6 to 6
- router_weight: bfloat16 [2048, 8], replicated, may hold values from -0.125 to 0.125
- weight_in: bfloat16 [8, 2048, 1024], P('expert'), may hold values from -0.125 to 0.125
- weight_out: bfloat16 [8, 1024, 2048], P('expert'), may hold values from -0.1875 to 0.1875
- expert_ids: int32 [65536, 2], P(('dp', 'expert')), may hold values from 0 to 7, as said below
- slot_index: int32 [65536, 2], P(('dp', 'expert')), may hold values from 0 to 63, as said below
- keep_mask: int32 [65536, 2], P(('dp', 'expert')), may hold values from 0 to 1
Outputs:
- grad_tokens: bfloat16 [65536, 2048], P(('dp', 'expert'))
- grad_router: float32 [2048, 8], replicated
- grad_w_in: float32 [8, 2048, 1024], P('expert', 'dp')
- grad_w_out: float32 [8, 1024, 2048], P('expert', 'dp')
Inputs may be any that keep to these rules, and one draw needn't show every extreme that they name: `expert_ids`: each row names 2 different experts. `slot_index`: within the 256 rows of one device, the kept assignments to one expert hold different slots; a dropped assignment has slot 0.
All inputs are finite; a program needn't handle non-finite values.
Results may differ from a plain program's by a relative error of at most 0.0062.
Values may be sent and summed in bfloat16 or wider, within the bound.
No kernel may reach another device: no remote copies, remote signals or barrier semaphores. Data moves between devices by JAX's collectives and lax.ppermute only.
A program may use at most 128 MiB of HBM per device.

v0:
```python
import jax
import jax.numpy as jnp
from jax import lax
from jax.sharding import PartitionSpec as P


def gelu_parts(hidden_pre):
    normal_cdf = 0.5 * (1.0 + jax.scipy.special.erf(hidden_pre * 0.7071067811865476))
    normal_pdf = jnp.exp(-0.5 * hidden_pre * hidden_pre) * 0.3989422804014327
    return (normal_cdf, normal_pdf)


def contract_rows(left, right):
    return lax.dot_general(
        left, right, (((0,), (0,)), ((), ())), preferred_element_type=jnp.float32
    )


def contract_cols(left, right):
    return lax.dot_general(
        left, right, (((1,), (1,)), ((), ())), preferred_element_type=jnp.float32
    )


def batch_dot(left, right, left_dim, right_dim):
    return lax.dot_general(
        left, right, (((left_dim,), (right_dim,)), ((0,), (0,))), preferred_element_type=jnp.float32
    )


def per_device(
    tokens, grad_out, router_weight, weight_in, weight_out, expert_ids, slot_index, keep_mask
):
    group_size = lax.axis_size("expert")
    replicas = lax.axis_size("dp")
    tok_rows, model_width = tokens.shape
    local_experts = weight_in.shape[0]
    experts = group_size * local_experts
    capacity = tok_rows * expert_ids.shape[1] // experts
    slot_count = experts * capacity
    grad_scale = float(tok_rows * replicas * group_size) ** (-0.5)
    logits = jnp.dot(tokens, router_weight, preferred_element_type=jnp.float32)
    exp_logits = jnp.exp(logits)
    router_probs = exp_logits / jnp.sum(exp_logits, axis=1, keepdims=True)
    picked = expert_ids[:, :, None] == jnp.arange(experts, dtype=jnp.int32)[None, None, :]
    chosen = jnp.sum(jnp.where(picked, router_probs[:, None, :], 0.0), axis=2)
    keep_float = keep_mask.astype(jnp.float32)
    denominator = jnp.sum(keep_float * chosen, axis=1) + (1.0 - jnp.max(keep_float, axis=1))
    combine = keep_float * chosen / denominator[:, None]
    combine_b = combine.astype(jnp.bfloat16)
    target = expert_ids * capacity + slot_index
    slot_iota = jnp.arange(slot_count, dtype=jnp.int32)[:, None]
    first_hit = (slot_iota == target[None, :, 0]) & (keep_mask[None, :, 0] == 1)
    second_hit = (slot_iota == target[None, :, 1]) & (keep_mask[None, :, 1] == 1)
    dispatch = (first_hit | second_hit).astype(jnp.bfloat16)
    send_tokens = jnp.dot(dispatch, tokens, preferred_element_type=jnp.float32).astype(jnp.bfloat16)
    send_grads = jnp.dot(dispatch, grad_out, preferred_element_type=jnp.float32).astype(
        jnp.bfloat16
    )
    gate_wide = combine_b.astype(jnp.float32)
    send_gates = jnp.sum(
        jnp.where(first_hit, gate_wide[None, :, 0], 0.0)
        + jnp.where(second_hit, gate_wide[None, :, 1], 0.0),
        axis=1,
    ).astype(jnp.bfloat16)
    recv_tokens, recv_grads, recv_gates = (
        lax.all_to_all(
            send_tokens.reshape(group_size, local_experts, capacity, model_width),
            "expert",
            split_axis=0,
            concat_axis=0,
            tiled=True,
        ),
        lax.all_to_all(
            send_grads.reshape(group_size, local_experts, capacity, model_width),
            "expert",
            split_axis=0,
            concat_axis=0,
            tiled=True,
        ),
        lax.all_to_all(
            send_gates.reshape(group_size, local_experts, capacity),
            "expert",
            split_axis=0,
            concat_axis=0,
            tiled=True,
        ),
    )
    expert_slots = group_size * capacity
    slot_tokens = jnp.swapaxes(recv_tokens, 0, 1).reshape(local_experts, expert_slots, model_width)
    slot_grads = jnp.swapaxes(recv_grads, 0, 1).reshape(local_experts, expert_slots, model_width)
    slot_gates = jnp.swapaxes(recv_gates, 0, 1).reshape(local_experts, expert_slots)
    hidden_pre = batch_dot(slot_tokens, weight_in, 2, 1)
    normal_cdf, normal_pdf = gelu_parts(hidden_pre)
    hidden_act = (hidden_pre * normal_cdf).astype(jnp.bfloat16)
    expert_out = batch_dot(hidden_act, weight_out, 2, 1)
    grads_wide = slot_grads.astype(jnp.float32)
    slot_combine_grad = jnp.sum(expert_out * grads_wide, axis=2).astype(jnp.bfloat16)
    scaled_grads = (slot_gates.astype(jnp.float32)[:, :, None] * grads_wide).astype(jnp.bfloat16)
    grad_act = batch_dot(scaled_grads, weight_out, 2, 2)
    grad_pre = (grad_act * (normal_cdf + hidden_pre * normal_pdf)).astype(jnp.bfloat16)
    grad_slots = batch_dot(grad_pre, weight_in, 2, 2).astype(jnp.bfloat16)
    back_grads, back_combine = (
        lax.all_to_all(
            jnp.swapaxes(
                grad_slots.reshape(local_experts, group_size, capacity, model_width), 0, 1
            ),
            "expert",
            split_axis=0,
            concat_axis=0,
            tiled=True,
        ),
        lax.all_to_all(
            jnp.swapaxes(slot_combine_grad.reshape(local_experts, group_size, capacity), 0, 1),
            "expert",
            split_axis=0,
            concat_axis=0,
            tiled=True,
        ),
    )
    flat_grads = back_grads.reshape(slot_count, model_width)
    flat_combine = back_combine.reshape(slot_count).astype(jnp.float32)
    safe_target = jnp.where(keep_mask == 1, target, 0)
    gathered = jnp.take(flat_grads, safe_target.reshape(-1), axis=0).reshape(
        tok_rows, 2, model_width
    )
    expert_grad = jnp.sum(
        jnp.where(keep_mask[:, :, None] == 1, gathered.astype(jnp.float32), 0.0), axis=1
    )
    combine_grad = jnp.where(keep_mask == 1, jnp.take(flat_combine, safe_target), 0.0)
    weighted_sum = jnp.sum(combine_grad * combine, axis=1)
    chosen_grad = keep_float * (combine_grad - weighted_sum[:, None]) / denominator[:, None]
    probs_grad = jnp.sum(jnp.where(picked, chosen_grad[:, :, None], 0.0), axis=1)
    logit_grad = router_probs * (
        probs_grad - jnp.sum(probs_grad * router_probs, axis=1, keepdims=True)
    )
    logit_b = logit_grad.astype(jnp.bfloat16)
    grad_tokens = (expert_grad + contract_cols(logit_b, router_weight)).astype(jnp.bfloat16)
    router_part = contract_rows(tokens, logit_b) * grad_scale
    grad_router = lax.psum(router_part, ("dp", "expert"))
    columns = hidden_act
    outer_share = lax.psum_scatter(
        jnp.swapaxes(batch_dot(columns, scaled_grads, 1, 1), 0, 1) * grad_scale,
        "dp",
        scatter_dimension=0,
        tiled=True,
    )
    columns = slot_tokens
    inner_share = lax.psum_scatter(
        jnp.swapaxes(batch_dot(columns, grad_pre, 1, 1), 0, 1) * grad_scale,
        "dp",
        scatter_dimension=0,
        tiled=True,
    )
    return (
        grad_tokens,
        grad_router,
        jnp.swapaxes(inner_share, 0, 1),
        jnp.swapaxes(outer_share, 0, 1),
    )


def solution(mesh):
    placed = (
        P(("dp", "expert"), None),
        P(("dp", "expert"), None),
        P(),
        P("expert", None, None),
        P("expert", None, None),
        P(("dp", "expert"), None),
        P(("dp", "expert"), None),
        P(("dp", "expert"), None),
    )
    return jax.shard_map(
        per_device,
        mesh=mesh,
        in_specs=placed,
        out_specs=(
            P(("dp", "expert"), None),
            P(),
            P("expert", "dp", None),
            P("expert", "dp", None),
        ),
        check_vma=False,
    )
```

profile of v0, /device:TPU:2, one launch (start us, length us, event | category | flops | bytes accessed | tf_op | source)
XLA Modules:
  0.0 390.6 jit_solution(8379416582626130455)
XLA Ops:
  8.0 0.0 copy-start
  8.0 0.8 compare_reduce_fusion.1
  8.8 0.7 compare_select_fusion.1
  9.5 0.0 copy-done
  9.6 2.0 convolution_convert_fusion
  11.6 6.2 %all-to-all-start.2 = ((bf16[8,1,64,2048]{3,2,1,0:T(8,128)(2,1)}), bf16[8,1,64,2048]{3,2,1,0:T(8,128)(2,1)S(1)}, u32[]{:S(2)}, u32[]{:S(2)}) async-start(bf16[8,1,64,2048]{3,2,1,0:T(8,128)(2,1)} %bitcast.10), calls=%async_computation.2 | async-start | bytes 4194304 | tf_op jit(solution)/shard_map/all_to_all | solution.py:67
  17.8 3.3 convolution_convert_fusion.1
  21.1 21.9 %all-to-all-done.2 = bf16[8,1,64,2048]{3,2,1,0:T(8,128)(2,1)S(1)} async-done(((bf16[8,1,64,2048]{3,2,1,0:T(8,128)(2,1)}), bf16[8,1,64,2048]{3,2,1,0:T(8,128)(2,1)S(1)}, u32[]{:S(2)}, u32[]{:S(2)}) %all-to-all-start.2) | async-done | bytes 2097184 | tf_op jit(solution)/shard_map/all_to_all | solution.py:67
  43.0 0.0 copy-start.1
  43.0 0.0 copy-start.3
  43.0 0.0 copy-start.5
  43.0 1.4 copy-done.1
  44.4 5.3 %all-to-all-start.1 = ((bf16[8,1,64,2048]{3,2,1,0:T(8,128)(2,1)}), bf16[8,1,64,2048]{3,2,1,0:T(8,128)(2,1)S(1)}, u32[]{:S(2)}, u32[]{:S(2)}) async-start(bf16[8,1,64,2048]{3,2,1,0:T(8,128)(2,1)} %bitcast.69), calls=%async_computation.1 | async-start | bytes 4194304 | tf_op jit(solution)/shard_map/all_to_all | solution.py:74
  49.7 0.1 copy.87
  49.8 0.1 reshape.275
  50.0 0.0 copy-done.3
  50.0 0.4 fusion.38
  50.4 0.0 copy-done.5
  50.4 0.0 copy-done.4
  50.5 6.5 %fusion.4 = f32[512,1024]{1,0:T(8,128)} fusion(bf16[512,2048]{1,0:T(8,128)(2,1)} %bitcast.70, bf16[1,2048,1024]{2,1,0:T(8,128)(2,1)} %param.11), kind=kOutput, calls=%fused_computation.10 | convolution fusion | flops 2147483648 | bytes 8388608 | tf_op jit(solution)/shard_map/dot_general | solution.py:26
  56.9 17.1 %all-to-all-done.1 = bf16[8,1,64,2048]{3,2,1,0:T(8,128)(2,1)S(1)} async-done(((bf16[8,1,64,2048]{3,2,1,0:T(8,128)(2,1)}), bf16[8,1,64,2048]{3,2,1,0:T(8,128)(2,1)S(1)}, u32[]{:S(2)}, u32[]{:S(2)}) %all-to-all-start.1) | async-done | bytes 2097184 | tf_op jit(solution)/shard_map/all_to_all | solution.py:74
  74.0 5.3 %fusion = bf16[512]{0:T(512)(128)(2,1)S(1)} fusion(bf16[8,1,64,2048]{3,2,1,0:T(8,128)(2,1)S(1)} %all-to-all-done.1, bf16[1,1024,2048]{2,1,0:T(8,128)(2,1)} %param.12, f32[512,1024]{1,0:T(8,128)} %fusion.4), kind=kOutput, calls=%fused_computation.6 | convolution fusion | flops 2153250304 | bytes 8389632 | tf_op jit(solution)/shard_map/dot_general | solution.py:26
  79.2 0.7 convert_element_type.168
  79.9 5.2 %all-to-all-start.4 = ((bf16[8,1,64]{2,1,0:T(2,128)(2,1)}), bf16[8,1,64]{2,1,0:T(2,128)(2,1)S(1)}, u32[]{:S(2)}, u32[]{:S(2)}) async-start(bf16[8,1,64]{2,1,0:T(2,128)(2,1)} %convert_element_type.168), calls=%async_computation.4 | async-start | bytes 8192 | tf_op jit(solution)/shard_map/all_to_all | solution.py:113
  85.2 4.6 %all-to-all-done.4 = bf16[8,1,64]{2,1,0:T(2,128)(2,1)S(1)} async-done(((bf16[8,1,64]{2,1,0:T(2,128)(2,1)}), bf16[8,1,64]{2,1,0:T(2,128)(2,1)S(1)}, u32[]{:S(2)}, u32[]{:S(2)}) %all-to-all-start.4) | async-done | bytes 1056 | tf_op jit(solution)/shard_map/all_to_all | solution.py:113
  89.8 0.1 reshape.264
  89.9 3.5 gather_fusion.1
  93.4 0.1 reshape.274
  93.6 0.1 copy.88
  93.7 0.3 add_reduce_fusion
  94.0 0.7 convert_element_type.167
  94.7 4.7 %all-to-all-start = ((bf16[8,1,64]{2,1,0:T(2,128)(2,1)}), bf16[8,1,64]{2,1,0:T(2,128)(2,1)S(1)}, u32[]{:S(2)}, u32[]{:S(2)}) async-start(bf16[8,1,64]{2,1,0:T(2,128)(2,1)} %convert_element_type.167), calls=%async_computation | async-start | bytes 8192 | tf_op jit(solution)/shard_map/all_to_all | solution.py:81
  99.3 0.0 all-reduce.2.cloned.1.call-start
  99.4 0.9 fusion.14
  100.3 0.0 all-reduce.2.cloned.1.call-update
  100.3 0.0 reduce-scatter.5.cloned.1.call-start
  100.4 3.6 all-to-all-done
  104.0 0.1 reshape.261
  104.1 0.4 fusion.1
  104.5 1.2 copy-done.8
  105.7 5.7 %multiply_bitcast_fusion = f32[1024,1,2048]{2,0,1:T(8,128)} fusion(bf16[512,2048]{1,0:T(8,128)(2,1)S(1)} %fusion.1, f32[512,1024]{1,0:T(8,128)S(1)} %copy-done.8), kind=kOutput, calls=%fused_computation.2 | convolution fusion | flops 2152202240 | bytes 12582912 | tf_op jit(solution)/shard_map/dot_general | solution.py:26
  111.3 0.0 reduce-scatter.5.cloned.1.call-update
  111.4 0.2 reduce-scatter.3.cloned.1.call-start
  111.6 0.0 copy-start.2
  111.6 5.9 %fusion.20 = bf16[512,1024]{1,0:T(8,128)(2,1)S(1)} fusion(f32[512,1024]{1,0:T(8,128)} %fusion.4, bf16[1,1024,2048]{2,1,0:T(8,128)(2,1)} %param.12, f32[512]{0:T(512)S(1)} %reshape.261, bf16[1,512,1,1,1,1,2048]{6,1,5,4,3,2,0:T(8,128)(2,1)S(1)} %bitcast.68), kind=kOutput, calls=%fused_computation.32 | convolution fusion | flops 2155872256 | bytes 9439232 | tf_op jit(solution)/shard_map/dot_general | solution.py:26
  117.5 0.0 copy-start.6
  117.5 1.0 copy-done.6
  118.5 0.0 copy-done.2
  118.5 5.6 %multiply_bitcast_fusion.1 = f32[2048,1,1024]{2,0,1:T(8,128)} fusion(bf16[512,2048]{1,0:T(8,128)(2,1)S(1)} %bitcast.71, bf16[512,1024]{1,0:T(8,128)(2,1)S(1)} %fusion.20), kind=kOutput, calls=%fused_computation.3 | convolution fusion | flops 2149580800 | bytes 11534336 | tf_op jit(solution)/shard_map/dot_general | solution.py:26
  124.1 0.0 reduce-scatter.3.cloned.1.call-update
  124.1 1.3 copy-done.7
  125.4 6.1 %fusion.10 = bf16[512,2048]{1,0:T(8,128)(2,1)} fusion(bf16[512,1024]{1,0:T(8,128)(2,1)S(1)} %copy-done.7, bf16[1,2048,1024]{2,1,0:T(8,128)(2,1)} %param.11), kind=kOutput, calls=%fused_computation.20 | convolution fusion | flops 2148532224 | bytes 7340032 | tf_op jit(solution)/shard_map/dot_general | solution.py:26
  131.5 5.0 %all-to-all-start.3 = ((bf16[8,1,64,2048]{3,2,1,0:T(8,128)(2,1)}), bf16[8,1,64,2048]{3,2,1,0:T(8,128)(2,1)S(1)}, u32[]{:S(2)}, u32[]{:S(2)}) async-start(bf16[8,1,64,2048]{3,2,1,0:T(8,128)(2,1)} %bitcast.72), calls=%async_computation.3 | async-start | bytes 4194304 | tf_op jit(solution)/shard_map/all_to_all | solution.py:104
  136.4 0.1 copy.85
  136.6 0.2 copy.79
  136.8 0.1 reshape.260
  136.9 0.2 copy.80
  137.1 21.6 %all-to-all-done.3 = bf16[8,1,64,2048]{3,2,1,0:T(8,128)(2,1)S(1)} async-done(((bf16[8,1,64,2048]{3,2,1,0:T(8,128)(2,1)}), bf16[8,1,64,2048]{3,2,1,0:T(8,128)(2,1)S(1)}, u32[]{:S(2)}, u32[]{:S(2)}) %all-to-all-start.3) | async-done | bytes 2097184 | tf_op jit(solution)/shard_map/all_to_all | solution.py:104
  158.7 3.3 gather_fusion
  162.0 4.4 %gather.11 = bf16[256,2,2048]{2,1,0:T(2,128)(2,1)} reshape(bf16[512,2048]{1,0:T(8,128)(2,1)} %gather_fusion) | data formatting | bytes 4194304 | tf_op jit(solution)/shard_map/jit(_take)/gather | solution.py:124
  166.4 7.7 %select_reduce_fusion = f32[256,2048]{1,0:T(8,128)S(1)} fusion(pred[256,2]{1,0:T(8,128)(4,1)S(1)} %copy.79, bf16[256,2,2048]{2,1,0:T(2,128)(2,1)} %gather.11, pred[256,2]{1,0:T(8,128)(4,1)S(1)} %copy.80), kind=kLoop, calls=%fused_computation.16 | loop fusion | flops 3670016 | bytes 4195328 | tf_op jit(solution)/shard_map/reduce_sum | solution.py:127
  174.1 1.5 fusion.13
  175.5 206.2 %all-reduce.2.cloned.1.call-done = f32[2048,8]{0,1:T(8,128)} async-done(((f32[2048,8]{0,1:T(8,128)}), f32[2048,8]{0,1:T(8,128)}) %all-reduce.2.cloned.1.call-update) | async-done | bytes 65552 | tf_op jit(solution)/shard_map/psum | solution.py:140
  381.7 1.5 copy.90
  (21 shorter events, 0.2 us)
Async XLA Ops:
  8.0 1.6 copy-start
  11.6 31.4 %all-to-all-start.2 = ((bf16[8,1,64,2048]{3,2,1,0:T(8,128)(2,1)}), bf16[8,1,64,2048]{3,2,1,0:T(8,128)(2,1)S(1)}, u32[]{:S(2)}, u32[]{:S(2)}) async-start(bf16[8,1,64,2048]{3,2,1,0:T(8,128)(2,1)} %bitcast.10), calls=%async_computation.2 | async-start | bytes 4194304 | tf_op jit(solution)/shard_map/all_to_all | solution.py:67
  43.0 1.4 copy-start.1
  43.0 7.0 %copy-start.3 = (bf16[2048,8]{0,1:T(8,128)(2,1)S(1)}, bf16[2048,8]{0,1:T(8,128)(2,1)}, u32[]{:S(2)}) copy-start(bf16[2048,8]{0,1:T(8,128)(2,1)} %param.10) | copy-start | bytes 98308
  43.0 7.4 %copy-start.5 = (s32[256,2]{0,1:T(2,128)S(1)}, s32[256,2]{0,1:T(2,128)}, u32[]{:S(2)}) copy-start(s32[256,2]{0,1:T(2,128)} %param.13) | copy-start | bytes 6148
  43.0 7.4 %copy-start.4 = (s32[256,2]{0,1:T(2,128)S(1)}, s32[256,2]{0,1:T(2,128)}, u32[]{:S(2)}) copy-start(s32[256,2]{0,1:T(2,128)} %param.15) | copy-start | bytes 6148
  44.4 29.6 %all-to-all-start.1 = ((bf16[8,1,64,2048]{3,2,1,0:T(8,128)(2,1)}), bf16[8,1,64,2048]{3,2,1,0:T(8,128)(2,1)S(1)}, u32[]{:S(2)}, u32[]{:S(2)}) async-start(bf16[8,1,64,2048]{3,2,1,0:T(8,128)(2,1)} %bitcast.69), calls=%async_computation.1 | async-start | bytes 4194304 | tf_op jit(solution)/shard_map/all_to_all | solution.py:74
  79.9 9.9 %all-to-all-start.4 = ((bf16[8,1,64]{2,1,0:T(2,128)(2,1)}), bf16[8,1,64]{2,1,0:T(2,128)(2,1)S(1)}, u32[]{:S(2)}, u32[]{:S(2)}) async-start(bf16[8,1,64]{2,1,0:T(2,128)(2,1)} %convert_element_type.168), calls=%async_computation.4 | async-start | bytes 8192 | tf_op jit(solution)/shard_map/all_to_all | solution.py:113
  94.7 9.3 %all-to-all-start = ((bf16[8,1,64]{2,1,0:T(2,128)(2,1)}), bf16[8,1,64]{2,1,0:T(2,128)(2,1)S(1)}, u32[]{:S(2)}, u32[]{:S(2)}) async-start(bf16[8,1,64]{2,1,0:T(2,128)(2,1)} %convert_element_type.167), calls=%async_computation | async-start | bytes 8192 | tf_op jit(solution)/shard_map/all_to_all | solution.py:81
  99.3 282.4 %all-reduce.2.cloned.1.call-start = ((), (), s32[]{:S(2)}) async-start(), calls=%async_computation.7 | async-start | bytes 131072 | tf_op jit(solution)/shard_map/psum | solution.py:140
  100.3 281.4 %reduce-scatter.5.cloned.1.call-start = ((), (), s32[]{:S(2)}) async-start(), calls=%async_computation.9 | async-start | bytes 8650752 | tf_op jit(solution)/shard_map/reduce_scatter | solution.py:142
  104.1 1.6 copy-start.8
  111.4 270.4 %reduce-scatter.3.cloned.1.call-start = ((), (), s32[]{:S(2)}) async-start(), calls=%async_computation.8 | async-start | bytes 8650752 | tf_op jit(solution)/shard_map/reduce_scatter | solution.py:149
  111.6 6.9 %copy-start.2 = (bf16[8,1,64,2048]{3,2,1,0:T(8,128)(2,1)S(1)}, bf16[8,1,64,2048]{3,2,1,0:T(8,128)(2,1)}, u32[]{:S(2)}) copy-start(bf16[8,1,64,2048]{3,2,1,0:T(8,128)(2,1)} %copy-done.1) | copy-start | bytes 6291460
  117.5 1.0 copy-start.6
  124.1 1.3 copy-start.7
  131.5 27.2 %all-to-all-start.3 = ((bf16[8,1,64,2048]{3,2,1,0:T(8,128)(2,1)}), bf16[8,1,64,2048]{3,2,1,0:T(8,128)(2,1)S(1)}, u32[]{:S(2)}, u32[]{:S(2)}) async-start(bf16[8,1,64,2048]{3,2,1,0:T(8,128)(2,1)} %bitcast.72), calls=%async_computation.3 | async-start | bytes 4194304 | tf_op jit(solution)/shard_map/all_to_all | solution.py:104
Sparse Core Ops, SparseCore 0:
  106.2 275.4 all-reduce.1
Sparse Core Ops, SparseCore 1:
  111.5 122.2 reduce-scatter.4
  238.7 119.1 reduce-scatter.2
where the time goes:
time: 394 us; the launch traced here: 391 us
  waiting for transfers between devices  275 us (70%)
  matrix products  43.1 us (11%)
  starting transfers between devices  26.6 us (7%)
  local copies, waits for them, and re-layouts  20.2 us (5%)
  between operations  15.7 us (4%)
  other arithmetic  10.1 us (3%)
    psum x1, waiting for transfers between devices, per_device(): grad_router = lax.psum(router_part, ('dp', 'expert'))  206 us
    dot_general x6, matrix products, batch_dot(): lax.dot_general(left, right, (((left_dim,), (right_dim,)), ((0,), (0,))),...  34.9 us
    all_to_all x1, waiting for transfers between devices, per_device(): lax.all_to_all(send_tokens.reshape(group_size, local_experts, capacity, m...  21.9 us
    all_to_all x1, waiting for transfers between devices, per_device(): lax.all_to_all(jnp.swapaxes(grad_slots.reshape(local_experts, group_size,...  21.6 us
    all_to_all x1, waiting for transfers between devices, per_device(): lax.all_to_all(send_grads.reshape(group_size, local_experts, capacity, mo...  17.1 us
  transfers between devices with their start and end apart: 8, of which 6 were waited for; matrix products, arithmetic and copies ran while one was open for 13% of the time, Pallas kernels for 0%

commit v1 on v0

v1 whole, which is shorter than its diff:
```python
import jax
import jax.numpy as jnp
from jax import lax
from jax.sharding import Mesh, PartitionSpec as P

FINE = ("y", "zh", "core", "x", "zl")
FINE_SHAPE = (4, 4, 2, 4, 2)
GROUP = ("x", "zl")
F32 = jnp.float32
BF16 = jnp.bfloat16


def gelu_parts(hidden_pre):
    normal_cdf = 0.5 * (1.0 + jax.scipy.special.erf(hidden_pre * 0.7071067811865476))
    normal_pdf = jnp.exp(-0.5 * hidden_pre * hidden_pre) * 0.3989422804014327
    return (normal_cdf, normal_pdf)


def contract_rows(left, right):
    return lax.dot_general(left, right, (((0,), (0,)), ((), ())), preferred_element_type=F32)


def contract_cols(left, right):
    return lax.dot_general(left, right, (((1,), (1,)), ((), ())), preferred_element_type=F32)


def swap(values, axis, mask):
    size = lax.axis_size(axis)
    return lax.ppermute(values, axis, [(i, i ^ mask) for i in range(size)])


def exchange(values, axes):
    return lax.all_to_all(values, axes, split_axis=0, concat_axis=0, tiled=True)


def xor_blocks(values, me, blocks):
    width = values.shape[1] // blocks
    parts = [
        lax.dynamic_slice_in_dim(values, (me ^ r) * width, width, axis=1) for r in range(blocks)
    ]
    return jnp.concatenate(parts, axis=1)


def reduce_share(left, right, scale):
    rows = left.shape[1] // 4
    cols = right.shape[1]
    half = cols // 2
    right_a, right_b = right[:, :half], right[:, half:]
    send_a = contract_rows(left[:, rows : 3 * rows], right_a).astype(BF16)
    send_b = contract_rows(left[:, 2 * rows :], right_b).astype(BF16)
    got_a = swap(send_a, "y", 1).astype(F32)
    got_b = swap(send_b, "y", 3).astype(F32)
    far_a = contract_rows(left[:, 3 * rows :], right_a)
    far_b = contract_rows(left[:, rows : 2 * rows], right_b)
    near_a = contract_rows(left[:, :rows], right_a)
    near_b = contract_rows(left[:, :rows], right_b)
    far_a = (far_a + got_a[rows:]).astype(BF16)
    far_b = (far_b + got_b[:rows]).astype(BF16)
    got_far_a = swap(far_a, "y", 3).astype(F32)
    got_far_b = swap(far_b, "y", 1).astype(F32)
    near_a = near_a + got_a[:rows] + got_far_a
    near_b = near_b + got_b[rows:] + got_far_b
    near = jnp.concatenate([near_a, near_b], axis=1).astype(BF16)
    share = rows // 8
    pieces = exchange(near.reshape(8, share, cols), ("zh", "core")).astype(F32)
    total = jnp.sum(pieces.reshape(4, 2, share, cols), axis=0) * scale
    return jnp.concatenate([total[0], total[1]], axis=1)[None]


def per_device(
    tokens, grad_out, router_weight, weight_in, weight_out, expert_ids, slot_index, keep_mask
):
    tok_rows, model_width = tokens.shape
    experts = 8
    weight_in = weight_in[0]
    weight_out = weight_out[0]
    capacity = tok_rows * expert_ids.shape[1] // experts
    slot_count = experts * capacity
    grad_scale = float(tok_rows * 256) ** (-0.5)
    core = lax.axis_index("core")
    my_y = lax.axis_index("y")

    target = expert_ids * capacity + slot_index
    slot_iota = jnp.arange(slot_count, dtype=jnp.int32)[:, None]
    first_hit = (slot_iota == target[None, :, 0]) & (keep_mask[None, :, 0] == 1)
    second_hit = (slot_iota == target[None, :, 1]) & (keep_mask[None, :, 1] == 1)
    dispatch = (first_hit | second_hit).astype(BF16)

    send_tokens = jnp.dot(dispatch, tokens, preferred_element_type=F32).astype(BF16)
    slot_tokens = exchange(
        send_tokens.reshape(experts, capacity, model_width), GROUP
    ).reshape(slot_count, model_width)

    send_grads = jnp.dot(dispatch, grad_out, preferred_element_type=F32).astype(BF16)
    slot_grads = exchange(
        send_grads.reshape(experts, capacity, model_width), GROUP
    ).reshape(slot_count, model_width)

    logits = jnp.dot(tokens, router_weight, preferred_element_type=F32)
    exp_logits = jnp.exp(logits)
    router_probs = exp_logits / jnp.sum(exp_logits, axis=1, keepdims=True)
    picked = expert_ids[:, :, None] == jnp.arange(experts, dtype=jnp.int32)[None, None, :]
    chosen = jnp.sum(jnp.where(picked, router_probs[:, None, :], 0.0), axis=2)
    keep_float = keep_mask.astype(F32)
    denominator = jnp.sum(keep_float * chosen, axis=1) + (1.0 - jnp.max(keep_float, axis=1))
    combine = keep_float * chosen / denominator[:, None]
    gate_wide = combine.astype(BF16).astype(F32)
    send_gates = jnp.sum(
        jnp.where(first_hit, gate_wide[None, :, 0], 0.0)
        + jnp.where(second_hit, gate_wide[None, :, 1], 0.0),
        axis=1,
    ).astype(BF16)
    slot_gates = exchange(send_gates.reshape(experts, capacity), GROUP).reshape(slot_count, 1)
    gates = slot_gates.astype(F32)

    other_tokens = swap(slot_tokens, "core", 1)
    hidden_pre = jnp.dot(slot_tokens, weight_in, preferred_element_type=F32)
    normal_cdf, normal_pdf = gelu_parts(hidden_pre)
    hidden_act = (hidden_pre * normal_cdf).astype(BF16)
    act_slope = normal_cdf + hidden_pre * normal_pdf
    scaled_act = (gates * hidden_act.astype(F32)).astype(BF16)
    other_act = swap(scaled_act, "core", 1)
    left_in = xor_blocks(jnp.concatenate([slot_tokens, other_tokens], axis=0), my_y, 4)
    left_out = xor_blocks(jnp.concatenate([scaled_act, other_act], axis=0), my_y, 4)

    half_width = model_width // 2
    my_grads = lax.dynamic_slice_in_dim(slot_grads, core * half_width, half_width, axis=1)
    give_grads = lax.dynamic_slice_in_dim(slot_grads, (1 - core) * half_width, half_width, axis=1)
    right_out = jnp.concatenate([my_grads, swap(give_grads, "core", 1)], axis=0)

    grad_act = contract_cols(slot_grads, weight_out)
    slot_combine_grad = jnp.sum(hidden_act.astype(F32) * grad_act, axis=1).astype(BF16)
    grad_pre = (gates * grad_act * act_slope).astype(BF16)

    half_hidden = grad_pre.shape[1] // 2
    my_pre = lax.dynamic_slice_in_dim(grad_pre, core * half_hidden, half_hidden, axis=1)
    give_pre = lax.dynamic_slice_in_dim(grad_pre, (1 - core) * half_hidden, half_hidden, axis=1)
    right_in = jnp.concatenate([my_pre, swap(give_pre, "core", 1)], axis=0)

    flat_combine = exchange(slot_combine_grad.reshape(experts, capacity), GROUP).reshape(
        slot_count
    )
    grad_slots = contract_cols(grad_pre, weight_in).astype(BF16)
    flat_grads = exchange(
        grad_slots.reshape(experts, capacity, model_width), GROUP
    ).reshape(slot_count, model_width)

    outer_share = reduce_share(left_out, right_out, grad_scale)
    inner_share = reduce_share(left_in, right_in, grad_scale)

    combine_wide = flat_combine.astype(F32)[:, None]
    combine_grad = jnp.stack(
        [
            jnp.sum(jnp.where(first_hit, combine_wide, 0.0), axis=0),
            jnp.sum(jnp.where(second_hit, combine_wide, 0.0), axis=0),
        ],
        axis=1,
    )
    weighted_sum = jnp.sum(combine_grad * combine, axis=1)
    chosen_grad = keep_float * (combine_grad - weighted_sum[:, None]) / denominator[:, None]
    probs_grad = jnp.sum(jnp.where(picked, chosen_grad[:, :, None], 0.0), axis=1)
    logit_grad = router_probs * (
        probs_grad - jnp.sum(probs_grad * router_probs, axis=1, keepdims=True)
    )
    logit_b = logit_grad.astype(BF16)

    router_part = contract_rows(logit_b, tokens) * grad_scale
    router_part = router_part + swap(router_part, "core", 1)
    router_row = jnp.sum(exchange(router_part, GROUP), axis=0, keepdims=True)
    rows = exchange(jnp.broadcast_to(router_row, (16, model_width)), ("y", "zh"))
    router_row = jnp.sum(rows, axis=0, keepdims=True)
    grad_router = exchange(jnp.broadcast_to(router_row, (experts, model_width)), GROUP)

    expert_grad = contract_rows(dispatch, flat_grads)
    grad_tokens = (expert_grad + contract_cols(logit_b, router_weight)).astype(BF16)
    return (grad_tokens, grad_router.T, inner_share, outer_share)


def solution(mesh):
    fine = Mesh(mesh.devices.reshape(FINE_SHAPE), FINE)
    placed = (
        P(FINE, None),
        P(FINE, None),
        P(),
        P(GROUP, None, None),
        P(GROUP, None, None),
        P(FINE, None),
        P(FINE, None),
        P(FINE, None),
    )
    return jax.shard_map(
        per_device,
        mesh=fine,
        in_specs=placed,
        out_specs=(
            P(FINE, None),
            P(),
            P(GROUP, ("y", "zh", "core"), None),
            P(GROUP, ("y", "zh", "core"), None),
        ),
        check_vma=False,
    )
```

time: 394 us -> 252 us (0.64)
  waiting for transfers between devices: 275 us -> 105 us
  starting transfers between devices: 26.6 us -> 59 us
  between operations: 15.7 us -> 1.13 us
  local copies, waits for them, and re-layouts: 20.2 us -> 9.35 us
  blocking collectives: 0 us -> 8.71 us
  other arithmetic: 10.1 us -> 18.3 us
  matrix products: 43.1 us -> 48.6 us
    psum x1 -> x0, waiting for transfers between devices: 206 us -> none  [per_device(): grad_router = lax.psum(router_part, ('dp', 'expert'))]
    dot_general x9 -> x4, matrix products: 40.7 us -> 12.3 us  [the longest x1 6.49 us: per_device(): hidden_pre = jnp.dot(slot_tokens, weight_in, preferred_element_type=F32)]
    ppermute x0 -> x13, waiting for transfers between devices: none -> 25.5 us  [swap(): return lax.ppermute(values, axis, [(i, i ^ mask) for i in range(size)])]
    all_to_all x5 -> x9, starting transfers between devices: 26.3 us -> 48.4 us  [exchange(): return lax.all_to_all(values, axes, split_axis=0, concat_axis=0, tiled=True)]
    dot_general x1 -> x14, matrix products: 0.88 us -> 21.7 us  [contract_rows(): lax.dot_general(left, right, (((0,), (0,)), ((), ())), preferred_element_...]
    dot_general x1 -> x3, matrix products: 1.45 us -> 14.6 us  [contract_cols(): lax.dot_general(left, right, (((1,), (1,)), ((), ())), preferred_element_...]
    gather x5 -> x0, local copies, waits for them, and re-layouts: 11.4 us -> none  [the longest x2 7.74 us: per_device(): jnp.take(flat_grads, safe_target.reshape(-1), axis=0)]
    all_to_all x5 -> x9, waiting for transfers between devices: 68.8 us -> 79.9 us  [exchange(): return lax.all_to_all(values, axes, split_axis=0, concat_axis=0, tiled=True)]
  transfers between devices with their start and end apart: 8 -> 22, of which waited for: 6 -> 13; matrix products, arithmetic and copies ran while one was open for 13% -> 22% of each run, Pallas kernels for 0% -> 0%
where the time goes in v1:
time: 252 us; the launch traced here: 250 us
  waiting for transfers between devices  105 us (42%)
  starting transfers between devices  59 us (23%)
  matrix products  48.6 us (19%)
  other arithmetic  18.3 us (7%)
  local copies, waits for them, and re-layouts  9.35 us (4%)
  blocking collectives  8.71 us (3%)
    all_to_all x9, waiting for transfers between devices, exchange(): return lax.all_to_all(values, axes, split_axis=0, concat_axis=0, tiled=True)  79.9 us
    all_to_all x9, starting transfers between devices, exchange(): return lax.all_to_all(values, axes, split_axis=0, concat_axis=0, tiled=True)  48.4 us
    ppermute x13, waiting for transfers between devices, swap(): return lax.ppermute(values, axis, [(i, i ^ mask) for i in range(size)])  25.5 us
    dot_general x14, matrix products, contract_rows(): lax.dot_general(left, right, (((0,), (0,)), ((), ())), preferred_element_...  21.7 us
    dot_general x3, matrix products, contract_cols(): lax.dot_general(left, right, (((1,), (1,)), ((), ())), preferred_element_...  14.6 us
    ppermute x13, starting transfers between devices, swap(): return lax.ppermute(values, axis, [(i, i ^ mask) for i in range(size)])  10.6 us
    all_to_all x1, blocking collectives, exchange(): return lax.all_to_all(values, axes, split_axis=0, concat_axis=0, tiled=True)  8.71 us
    dot_general x1, matrix products, per_device(): hidden_pre = jnp.dot(slot_tokens, weight_in, preferred_element_type=F32)  6.49 us
  transfers between devices with their start and end apart: 22, of which 13 were waited for; matrix products, arithmetic and copies ran while one was open for 22% of the time, Pallas kernels for 0%

profile of v1, /device:TPU:2, one launch (start us, length us, event | category | flops | bytes accessed | tf_op | source)
XLA Modules:
  0.0 250.4 jit_solution(2870028427792111492)
XLA Ops:
  0.6 0.8 multiply_add_fusion
  1.4 0.8 compare_reduce_fusion.1
  2.2 2.1 convolution_convert_fusion
  4.3 6.2 %all-to-all-start.2 = ((bf16[8,64,2048]{2,1,0:T(8,128)(2,1)}), bf16[8,64,2048]{2,1,0:T(8,128)(2,1)S(1)}, u32[]{:S(2)}, u32[]{:S(2)}) async-start(bf16[8,64,2048]{2,1,0:T(8,128)(2,1)} %bitcast.7), calls=%async_computation.2 | async-start | bytes 4194304 | tf_op jit(solution)/shard_map/all_to_all | solution.py:33
  10.5 3.3 %convolution_convert_fusion.1 = bf16[512,2048]{1,0:T(8,128)(2,1)} fusion(bf16[256,2048]{1,0:T(8,128)(2,1)} %param.9, s32[256]{0:T(256)S(1)} %bitcast.88, s32[256]{0:T(256)S(1)} %bitcast.84, pred[256]{0:T(512)(128)(4,1)S(1)} %get-tuple-element.10, pred[256]{0:T(512)(128)(4,1)S(1)} %get-tuple-element.9), kind=kOutput, calls=%fused_computation.17 | convolution fusion | flops 538574848 | bytes 3148288 | tf_op jit(solution)/shard_map/dot_general | solution.py:94
  13.8 21.9 %all-to-all-done.2 = bf16[8,64,2048]{2,1,0:T(8,128)(2,1)S(1)} async-done(((bf16[8,64,2048]{2,1,0:T(8,128)(2,1)}), bf16[8,64,2048]{2,1,0:T(8,128)(2,1)S(1)}, u32[]{:S(2)}, u32[]{:S(2)}) %all-to-all-start.2) | async-done | bytes 2097184 | tf_op jit(solution)/shard_map/all_to_all | solution.py:33
  35.7 1.3 copy-done.7
  37.0 5.3 %all-to-all-start.1 = ((bf16[8,64,2048]{2,1,0:T(8,128)(2,1)}), bf16[8,64,2048]{2,1,0:T(8,128)(2,1)S(1)}, u32[]{:S(2)}, u32[]{:S(2)}) async-start(bf16[8,64,2048]{2,1,0:T(8,128)(2,1)} %bitcast.70), calls=%async_computation.1 | async-start | bytes 4194304 | tf_op jit(solution)/shard_map/all_to_all | solution.py:33
  42.8 6.5 %fusion.2 = f32[512,1024]{1,0:T(8,128)} fusion(bf16[512,2048]{1,0:T(8,128)(2,1)} %bitcast.71, bf16[1,2048,1024]{2,1,0:T(8,128)(2,1)} %param.11), kind=kOutput, calls=%fused_computation.10 | convolution fusion | flops 2147483648 | bytes 8388608 | tf_op jit(solution)/shard_map/dot_general | solution.py:117
  49.3 17.3 %all-to-all-done.1 = bf16[8,64,2048]{2,1,0:T(8,128)(2,1)S(1)} async-done(((bf16[8,64,2048]{2,1,0:T(8,128)(2,1)}), bf16[8,64,2048]{2,1,0:T(8,128)(2,1)S(1)}, u32[]{:S(2)}, u32[]{:S(2)}) %all-to-all-start.1) | async-done | bytes 2097184 | tf_op jit(solution)/shard_map/all_to_all | solution.py:33
  66.6 7.2 %fusion.10 = (bf16[512]{0:T(512)(128)(2,1)S(1)}, bf16[512,1024]{1,0:T(8,128)(2,1)}, f32[512,1024]{1,0:T(8,128)}) fusion(f32[512,1024]{1,0:T(8,128)} %fusion.2, bf16[512,2048]{1,0:T(8,128)(2,1)S(1)} %bitcast.67, bf16[1,1024,2048]{2,1,0:T(8,128)(2,1)} %param.12), kind=kOutput, calls=%fused_computation.31 | convolution fusion | flops 2151677440 | bytes 11535360 | tf_op jit(solution)/shard_map/dot_general | solution.py:24
  74.5 5.3 %all-to-all-start.4 = ((bf16[8,1,64]{2,1,0:T(2,128)(2,1)}), bf16[8,1,64]{2,1,0:T(2,128)(2,1)S(1)}, u32[]{:S(2)}, u32[]{:S(2)}) async-start(bf16[8,1,64]{2,1,0:T(2,128)(2,1)} %convert_element_type.180), calls=%async_computation.4 | async-start | bytes 8192 | tf_op jit(solution)/shard_map/all_to_all | solution.py:33
  79.8 4.6 %all-to-all-done.4 = bf16[8,1,64]{2,1,0:T(2,128)(2,1)S(1)} async-done(((bf16[8,1,64]{2,1,0:T(2,128)(2,1)}), bf16[8,1,64]{2,1,0:T(2,128)(2,1)S(1)}, u32[]{:S(2)}, u32[]{:S(2)}) %all-to-all-start.4) | async-done | bytes 1056 | tf_op jit(solution)/shard_map/all_to_all | solution.py:33
  85.7 4.7 %all-to-all-start = ((bf16[8,1,64]{2,1,0:T(2,128)(2,1)}), bf16[8,1,64]{2,1,0:T(2,128)(2,1)S(1)}, u32[]{:S(2)}, u32[]{:S(2)}) async-start(bf16[8,1,64]{2,1,0:T(2,128)(2,1)} %convert_element_type.179), calls=%async_computation | async-start | bytes 8192 | tf_op jit(solution)/shard_map/all_to_all | solution.py:33
  90.3 4.7 %all-to-all-done = bf16[8,1,64]{2,1,0:T(2,128)(2,1)S(1)} async-done(((bf16[8,1,64]{2,1,0:T(2,128)(2,1)}), bf16[8,1,64]{2,1,0:T(2,128)(2,1)S(1)}, u32[]{:S(2)}, u32[]{:S(2)}) %all-to-all-start) | async-done | bytes 1056 | tf_op jit(solution)/shard_map/all_to_all | solution.py:33
  95.1 4.0 %fusion.11 = (bf16[512,1024]{1,0:T(8,128)(2,1)S(1)}, bf16[512,1024]{1,0:T(8,128)(2,1)}) fusion(bf16[512,1024]{1,0:T(8,128)(2,1)} %get-tuple-element.14, f32[512]{0:T(512)S(1)} %reshape.156, f32[512,1024]{1,0:T(8,128)} %fusion.2, f32[512,1024]{1,0:T(8,128)} %get-tuple-element.35), kind=kLoop, calls=%fused_computation.32 | loop fusion | flops 7340032 | bytes 7342080 | tf_op jit(solution)/shard_map/convert_element_type | solution.py:121
  100.3 1.5 collective-permute-done.7
  102.0 1.3 collective-permute-done.8
  103.3 1.5 convolution_convert_fusion.3
  104.8 1.6 collective-permute-start.9
  106.4 1.6 convolution_convert_fusion.2
  108.0 2.2 collective-permute-start.11
  110.3 8.7 %all_to_all.61 = f32[8,1,2048]{2,1,0:T(1,128)S(1)} all-to-all(f32[8,1,2048]{2,1,0:T(1,128)S(1)} %copy.29), channel_id=1, replica_groups=mesh['y'=4,'zh'=4,'core'=2,'x'=4,'zl'=2] {'x','zl'}, dimensions={0} | all-to-all | bytes 131072 | tf_op jit(solution)/shard_map/all_to_all | solution.py:33
  119.1 0.7 broadcast_in_dim.96
  119.8 8.2 %all-to-all-start.6 = ((f32[16,1,2048]{2,1,0:T(1,128)}), f32[16,1,2048]{2,1,0:T(1,128)S(1)}, u32[]{:S(2)}, u32[]{:S(2)}) async-start(f32[16,1,2048]{2,1,0:T(1,128)} %broadcast_in_dim.96), calls=%async_computation.6 | async-start | bytes 262144 | tf_op jit(solution)/shard_map/all_to_all | solution.py:33
  128.0 1.2 convert_element_type.170
  129.2 2.7 %fusion.38 = bf16[256,512]{1,0:T(8,128)(2,1)} fusion(bf16[1024,256]{1,0:T(8,128)(2,1)} %copy-done.20, f32[512,512]{1,0:T(8,128)S(1)} %convert_element_type.170, bf16[512,1024]{1,0:T(8,128)(2,1)S(1)} %get-tuple-element.21, bf16[512,1024]{1,0:T(8,128)(2,1)} %copy-done.3), kind=kOutput, calls=%fused_computation.69 | convolution fusion | flops 270794752 | bytes 3407872 | tf_op jit(solution)/shard_map/dot_general | solution.py:20
  131.9 3.1 %collective-permute-start.10 = (bf16[256,512]{1,0:T(8,128)(2,1)}, bf16[256,512]{1,0:T(8,128)(2,1)S(1)}, u32[]{:S(2)}, u32[]{:S(2)}) collective-permute-start(bf16[256,512]{1,0:T(8,128)(2,1)} %fusion.38), channel_id=1, source_target_pairs={{0,192},{64,128},{128,64},{192,0},{1,193},{65,129},{129,65},{193,1... | collective-permute-start | bytes 786440 | tf_op jit(solution)/shard_map/ppermute | solution.py:29
  135.1 3.6 %all-to-all-done.6 = f32[16,1,2048]{2,1,0:T(1,128)S(1)} async-done(((f32[16,1,2048]{2,1,0:T(1,128)}), f32[16,1,2048]{2,1,0:T(1,128)S(1)}, u32[]{:S(2)}, u32[]{:S(2)}) %all-to-all-start.6) | async-done | bytes 131104 | tf_op jit(solution)/shard_map/all_to_all | solution.py:33
  138.7 0.7 reduce_sum.137
  139.3 1.4 broadcast_in_dim.97
  140.7 4.8 %all-to-all-start.7 = ((f32[8,1,2048]{2,1,0:T(1,128)}), f32[8,1,2048]{2,1,0:T(1,128)S(1)}, u32[]{:S(2)}, u32[]{:S(2)}) async-start(f32[8,1,2048]{2,1,0:T(1,128)} %broadcast_in_dim.97), calls=%async_computation.7 | async-start | bytes 131072 | tf_op jit(solution)/shard_map/all_to_all | solution.py:33
  145.5 1.2 convert_element_type.174
  146.7 1.8 fusion.39
  149.3 5.6 %collective-permute-done.12 = bf16[256,512]{1,0:T(8,128)(2,1)S(1)} collective-permute-done((bf16[256,512]{1,0:T(8,128)(2,1)S(1)}, bf16[256,512]{1,0:T(8,128)(2,1)S(1)}, u32[]{:S(2)}, u32[]{:S(2)}) %collective-permute-start.12) | collective-permute-done | bytes 262176 | tf_op jit(solution)/shard_map/ppermute | solution.py:29
  155.5 0.9 pad_maximum_fusion.3
  156.4 5.0 %all-to-all-start.9 = ((bf16[8,32,1024]{2,1,0:T(8,128)(2,1)}), bf16[8,32,1024]{2,1,0:T(8,128)(2,1)S(1)}, u32[]{:S(2)}, u32[]{:S(2)}) async-start(bf16[8,32,1024]{2,1,0:T(8,128)(2,1)} %pad_maximum_fusion.3), calls=%async_computation.9 | async-start | bytes 1048576 | tf_op jit(solution)/shard_map/all_to_all | solution.py:33
  161.4 5.9 %fusion.6 = bf16[512,2048]{1,0:T(8,128)(2,1)} fusion(bf16[512,1024]{1,0:T(8,128)(2,1)S(1)} %copy-done.9, bf16[1,2048,1024]{2,1,0:T(8,128)(2,1)} %param.11), kind=kOutput, calls=%fused_computation.15 | convolution fusion | flops 2148532224 | bytes 7340032 | tf_op jit(solution)/shard_map/dot_general | solution.py:24
  167.3 12.4 %all-to-all-done.9 = bf16[8,32,1024]{2,1,0:T(8,128)(2,1)S(1)} async-done(((bf16[8,32,1024]{2,1,0:T(8,128)(2,1)}), bf16[8,32,1024]{2,1,0:T(8,128)(2,1)S(1)}, u32[]{:S(2)}, u32[]{:S(2)}) %all-to-all-start.9) | async-done | bytes 524320 | tf_op jit(solution)/shard_map/all_to_all | solution.py:33
  179.8 0.9 copy-done.12
  180.6 4.8 %all-to-all-start.3 = ((bf16[8,64,2048]{2,1,0:T(8,128)(2,1)}), bf16[8,64,2048]{2,1,0:T(8,128)(2,1)S(1)}, u32[]{:S(2)}, u32[]{:S(2)}) async-start(bf16[8,64,2048]{2,1,0:T(8,128)(2,1)} %bitcast.76), calls=%async_computation.3 | async-start | bytes 4194304 | tf_op jit(solution)/shard_map/all_to_all | solution.py:33
  185.4 2.3 constant_dynamic-slice_fusion.3
  187.8 2.1 fusion.47
  190.0 2.7 %fusion.29 = bf16[1024,256]{1,0:T(8,128)(2,1)} fusion(bf16[1024,512]{1,0:T(8,128)(2,1)S(1)} %get-tuple-element.16, bf16[1024,512]{1,0:T(8,128)(2,1)S(1)} %get-tuple-element.15, bf16[512,512]{1,0:T(8,128)(2,1)S(1)} %copy-done.18, bf16[512,512]{1,0:T(8,128)(2,1)} %collective-permute-done.2), kind=kOutput, calls=%fused_computation.52 | convolution fusion | flops 542375936 | bytes 3670016 | tf_op jit(solution)/shard_map/dot_general | solution.py:20
  193.1 2.5 %fusion.26 = bf16[1024,256]{1,0:T(8,128)(2,1)} fusion(bf16[1024,512]{1,0:T(8,128)(2,1)S(1)} %get-tuple-element.17, bf16[1024,512]{1,0:T(8,128)(2,1)S(1)} %get-tuple-element.16, bf16[512,512]{1,0:T(8,128)(2,1)} %collective-permute-done.2, bf16[512,512]{1,0:T(8,128)(2,1)S(1)} %copy-done.18), kind=kOutput, calls=%fused_computation.51 | convolution fusion | flops 542375936 | bytes 3670016 | tf_op jit(solution)/shard_map/dot_general | solution.py:20
  195.6 1.2 collective-permute-start.5
  197.4 9.9 %collective-permute-done.3 = bf16[1024,256]{1,0:T(8,128)(2,1)} collective-permute-done((bf16[1024,256]{1,0:T(8,128)(2,1)}, bf16[1024,256]{1,0:T(8,128)(2,1)}, u32[]{:S(2)}, u32[]{:S(2)}) %collective-permute-start.3) | collective-permute-done | bytes 524320 | tf_op jit(solution)/shard_map/ppermute | solution.py:29
  207.3 1.1 convert_element_type.161
  208.5 1.9 fusion.36
  210.4 0.7 collective-permute-start.4
  211.2 1.1 convert_element_type.165
  212.3 1.6 fusion.37
  213.9 0.8 collective-permute-start.6
  214.8 7.0 %collective-permute-done.6 = bf16[512,256]{1,0:T(8,128)(2,1)S(1)} collective-permute-done((bf16[512,256]{1,0:T(8,128)(2,1)S(1)}, bf16[512,256]{1,0:T(8,128)(2,1)S(1)}, u32[]{:S(2)}, u32[]{:S(2)}) %collective-permute-start.6) | collective-permute-done | bytes 262176 | tf_op jit(solution)/shard_map/ppermute | solution.py:29
  221.8 1.6 fusion.42
  223.4 1.6 fusion.43
  225.1 0.8 pad_maximum_fusion.2
  225.9 4.2 %all-to-all-start.8 = ((bf16[8,64,512]{2,1,0:T(8,128)(2,1)}), bf16[8,64,512]{2,1,0:T(8,128)(2,1)}, u32[]{:S(2)}, u32[]{:S(2)}) async-start(bf16[8,64,512]{2,1,0:T(8,128)(2,1)} %pad_maximum_fusion.2), calls=%async_computation.8 | async-start | bytes 1048576 | tf_op jit(solution)/shard_map/all_to_all | solution.py:33
  230.1 0.7 maximum_bitcast_fusion.1
  230.8 0.8 fusion.68
  231.6 1.4 fusion.9
  233.1 15.4 %all-to-all-done.8 = bf16[8,64,512]{2,1,0:T(8,128)(2,1)} async-done(((bf16[8,64,512]{2,1,0:T(8,128)(2,1)}), bf16[8,64,512]{2,1,0:T(8,128)(2,1)}, u32[]{:S(2)}, u32[]{:S(2)}) %all-to-all-start.8) | async-done | bytes 524320 | tf_op jit(solution)/shard_map/all_to_all | solution.py:33
  248.5 1.1 convert_reduce_fusion.1
  249.7 0.7 maximum_bitcast_fusion
  (103 shorter events, 6.6 us)
Async XLA Ops:
  0.6 1.6 copy-start
  2.2 82.3 %copy-start.24 = (pred[256]{0:T(512)(128)(4,1)}, pred[256]{0:T(512)(128)(4,1)S(1)}, u32[]{:S(2)}) copy-start(pred[256]{0:T(512)(128)(4,1)S(1)} %get-tuple-element.10) | copy-start | bytes 772
  4.3 31.4 %all-to-all-start.2 = ((bf16[8,64,2048]{2,1,0:T(8,128)(2,1)}), bf16[8,64,2048]{2,1,0:T(8,128)(2,1)S(1)}, u32[]{:S(2)}, u32[]{:S(2)}) async-start(bf16[8,64,2048]{2,1,0:T(8,128)(2,1)} %bitcast.7), calls=%async_computation.2 | async-start | bytes 4194304 | tf_op jit(solution)/shard_map/all_to_all | solution.py:33
  35.7 1.3 copy-start.7
  35.7 6.6 %copy-start.21 = (bf16[2048,8]{0,1:T(8,128)(2,1)S(1)}, bf16[2048,8]{0,1:T(8,128)(2,1)}, u32[]{:S(2)}) copy-start(bf16[2048,8]{0,1:T(8,128)(2,1)} %param.10) | copy-start | bytes 98308
  35.7 7.0 %copy-start.26 = (s32[256,2]{0,1:T(2,128)S(1)}, s32[256,2]{0,1:T(2,128)}, u32[]{:S(2)}) copy-start(s32[256,2]{0,1:T(2,128)} %param.13) | copy-start | bytes 6148
  35.7 7.1 %copy-start.23 = (s32[256,2]{0,1:T(2,128)S(1)}, s32[256,2]{0,1:T(2,128)}, u32[]{:S(2)}) copy-start(s32[256,2]{0,1:T(2,128)} %param.15) | copy-start | bytes 6148
  37.0 29.6 %all-to-all-start.1 = ((bf16[8,64,2048]{2,1,0:T(8,128)(2,1)}), bf16[8,64,2048]{2,1,0:T(8,128)(2,1)S(1)}, u32[]{:S(2)}, u32[]{:S(2)}) async-start(bf16[8,64,2048]{2,1,0:T(8,128)(2,1)} %bitcast.70), calls=%async_computation.1 | async-start | bytes 4194304 | tf_op jit(solution)/shard_map/all_to_all | solution.py:33
  66.6 7.2 %copy-start.5 = (bf16[8,64,2048]{2,1,0:T(8,128)(2,1)}, bf16[8,64,2048]{2,1,0:T(8,128)(2,1)S(1)}, u32[]{:S(2)}) copy-start(bf16[8,64,2048]{2,1,0:T(8,128)(2,1)S(1)} %all-to-all-done.1) | copy-start | bytes 6291460
  74.5 9.9 %all-to-all-start.4 = ((bf16[8,1,64]{2,1,0:T(2,128)(2,1)}), bf16[8,1,64]{2,1,0:T(2,128)(2,1)S(1)}, u32[]{:S(2)}, u32[]{:S(2)}) async-start(bf16[8,1,64]{2,1,0:T(2,128)(2,1)} %convert_element_type.180), calls=%async_computation.4 | async-start | bytes 8192 | tf_op jit(solution)/shard_map/all_to_all | solution.py:33
  85.7 9.3 %all-to-all-start = ((bf16[8,1,64]{2,1,0:T(2,128)(2,1)}), bf16[8,1,64]{2,1,0:T(2,128)(2,1)S(1)}, u32[]{:S(2)}, u32[]{:S(2)}) async-start(bf16[8,1,64]{2,1,0:T(2,128)(2,1)} %convert_element_type.179), calls=%async_computation | async-start | bytes 8192 | tf_op jit(solution)/shard_map/all_to_all | solution.py:33
  95.1 4.1 %copy-start.6 = (bf16[8,64,2048]{2,1,0:T(8,128)(2,1)S(1)}, bf16[8,64,2048]{2,1,0:T(8,128)(2,1)}, u32[]{:S(2)}) copy-start(bf16[8,64,2048]{2,1,0:T(8,128)(2,1)} %copy-done.5) | copy-start | bytes 6291460
  99.1 2.7 %collective-permute-start.7 = (bf16[512,1024]{1,0:T(8,128)(2,1)S(1)}, bf16[512,1024]{1,0:T(8,128)(2,1)S(1)}, u32[]{:S(2)}, u32[]{:S(2)}) collective-permute-start(bf16[512,1024]{1,0:T(8,128)(2,1)S(1)} %get-tuple-element.29), channel_id=1, source_target_pairs={{0,8},{8,0},{1,9},{9,1},{2,10},{10,2},{3,11},{11,3},{4,12},{12,4},... | collective-permute-start | bytes 3145736 | tf_op jit(solution)/shard_map/ppermute | solution.py:29
  99.3 4.0 %collective-permute-start.8 = (bf16[512,1024]{1,0:T(8,128)(2,1)S(1)}, bf16[512,1024]{1,0:T(8,128)(2,1)S(1)}, u32[]{:S(2)}, u32[]{:S(2)}) collective-permute-start(bf16[512,1024]{1,0:T(8,128)(2,1)S(1)} %get-tuple-element.22), channel_id=1, source_target_pairs={{0,8},{8,0},{1,9},{9,1},{2,10},{10,2},{3,11},{11,3},{4,12},{12,4},... | collective-permute-start | bytes 3145736 | tf_op jit(solution)/shard_map/ppermute | solution.py:29
  100.2 10.0 %collective-permute-start = (f32[8,2048]{1,0:T(8,128)S(1)}, f32[8,2048]{1,0:T(8,128)S(1)}, u32[]{:S(2)}, u32[]{:S(2)}) collective-permute-start(f32[8,2048]{1,0:T(8,128)S(1)} %convolution_multiply_fusion), channel_id=1, source_target_pairs={{0,8},{8,0},{1,9},{9,1},{2,10},{10,2},{3,11},{11,3},{4,12},{12,4},... | collective-permute-start | bytes 196616 | tf_op jit(solution)/shard_map/ppermute | solution.py:29
  101.8 3.0 %copy-start.1 = (bf16[512,1024]{1,0:T(8,128)(2,1)}, bf16[512,1024]{1,0:T(8,128)(2,1)S(1)}, u32[]{:S(2)}) copy-start(bf16[512,1024]{1,0:T(8,128)(2,1)S(1)} %collective-permute-done.7) | copy-start | bytes 3145732
  102.0 2.8 %copy-start.14 = (bf16[1024,256]{1,0:T(8,128)(2,1)}, bf16[1024,256]{1,0:T(8,128)(2,1)S(1)}, u32[]{:S(2)}) copy-start(bf16[1024,256]{1,0:T(8,128)(2,1)S(1)} %get-tuple-element.18) | copy-start | bytes 1572868
  102.0 4.4 %copy-start.20 = (bf16[1024,256]{1,0:T(8,128)(2,1)}, bf16[1024,256]{1,0:T(8,128)(2,1)S(1)}, u32[]{:S(2)}) copy-start(bf16[1024,256]{1,0:T(8,128)(2,1)S(1)} %get-tuple-element.20) | copy-start | bytes 1572868
  103.3 3.1 %copy-start.3 = (bf16[512,1024]{1,0:T(8,128)(2,1)}, bf16[512,1024]{1,0:T(8,128)(2,1)S(1)}, u32[]{:S(2)}) copy-start(bf16[512,1024]{1,0:T(8,128)(2,1)S(1)} %collective-permute-done.8) | copy-start | bytes 3145732
  104.8 23.1 %collective-permute-start.9 = (bf16[512,512]{1,0:T(8,128)(2,1)}, bf16[512,512]{1,0:T(8,128)(2,1)}, u32[]{:S(2)}, u32[]{:S(2)}) collective-permute-start(bf16[512,512]{1,0:T(8,128)(2,1)} %convolution_convert_fusion.3), channel_id=1, source_target_pairs={{0,64},{64,0},{128,192},{192,128},{1,65},{65,1},{129,193},{193,129... | collective-permute-start | bytes 1572872 | tf_op jit(solution)/shard_map/ppermute | solution.py:29
  108.0 37.5 %collective-permute-start.11 = (bf16[512,512]{1,0:T(8,128)(2,1)}, bf16[512,512]{1,0:T(8,128)(2,1)}, u32[]{:S(2)}, u32[]{:S(2)}) collective-permute-start(bf16[512,512]{1,0:T(8,128)(2,1)} %convolution_convert_fusion.2), channel_id=1, source_target_pairs={{0,192},{64,128},{128,64},{192,0},{1,193},{65,129},{129,65},{193,1... | collective-permute-start | bytes 1572872 | tf_op jit(solution)/shard_map/ppermute | solution.py:29
  119.8 18.8 %all-to-all-start.6 = ((f32[16,1,2048]{2,1,0:T(1,128)}), f32[16,1,2048]{2,1,0:T(1,128)S(1)}, u32[]{:S(2)}, u32[]{:S(2)}) async-start(f32[16,1,2048]{2,1,0:T(1,128)} %broadcast_in_dim.96), calls=%async_computation.6 | async-start | bytes 262144 | tf_op jit(solution)/shard_map/all_to_all | solution.py:33
  129.2 2.8 %copy-start.10 = (f32[512,512]{1,0:T(8,128)}, f32[512,512]{1,0:T(8,128)S(1)}, u32[]{:S(2)}) copy-start(f32[512,512]{1,0:T(8,128)S(1)} %convert_element_type.170) | copy-start | bytes 3145732
  131.9 16.7 %collective-permute-start.10 = (bf16[256,512]{1,0:T(8,128)(2,1)}, bf16[256,512]{1,0:T(8,128)(2,1)S(1)}, u32[]{:S(2)}, u32[]{:S(2)}) collective-permute-start(bf16[256,512]{1,0:T(8,128)(2,1)} %fusion.38), channel_id=1, source_target_pairs={{0,192},{64,128},{128,64},{192,0},{1,193},{65,129},{129,65},{193,1... | collective-permute-start | bytes 786440 | tf_op jit(solution)/shard_map/ppermute | solution.py:29
  135.1 52.7 %collective-permute-start.1 = (bf16[512,2048]{1,0:T(8,128)(2,1)}, bf16[512,2048]{1,0:T(8,128)(2,1)}, u32[]{:S(2)}, u32[]{:S(2)}) collective-permute-start(bf16[512,2048]{1,0:T(8,128)(2,1)} %bitcast.72), channel_id=1, source_target_pairs={{0,8},{8,0},{1,9},{9,1},{2,10},{10,2},{3,11},{11,3},{4,12},{12,4},... | collective-permute-start | bytes 6291464 | tf_op jit(solution)/shard_map/ppermute | solution.py:29
  140.7 15.7 %all-to-all-start.7 = ((f32[8,1,2048]{2,1,0:T(1,128)}), f32[8,1,2048]{2,1,0:T(1,128)S(1)}, u32[]{:S(2)}, u32[]{:S(2)}) async-start(f32[8,1,2048]{2,1,0:T(1,128)} %broadcast_in_dim.97), calls=%async_computation.7 | async-start | bytes 131072 | tf_op jit(solution)/shard_map/all_to_all | solution.py:33
  146.7 2.0 copy-start.2
  146.7 2.0 copy-start.4
  146.7 2.2 copy-start.11
  148.5 6.5 %collective-permute-start.12 = (bf16[256,512]{1,0:T(8,128)(2,1)S(1)}, bf16[256,512]{1,0:T(8,128)(2,1)S(1)}, u32[]{:S(2)}, u32[]{:S(2)}) collective-permute-start(bf16[256,512]{1,0:T(8,128)(2,1)S(1)} %fusion.39), channel_id=1, source_target_pairs={{0,64},{64,0},{128,192},{192,128},{1,65},{65,1},{129,193},{193,129... | collective-permute-start | bytes 786440 | tf_op jit(solution)/shard_map/ppermute | solution.py:29
  155.5 5.9 %copy-start.9 = (bf16[512,1024]{1,0:T(8,128)(2,1)S(1)}, bf16[512,1024]{1,0:T(8,128)(2,1)}, u32[]{:S(2)}) copy-start(bf16[512,1024]{1,0:T(8,128)(2,1)} %get-tuple-element.30) | copy-start | bytes 3145732
  156.4 23.4 %all-to-all-start.9 = ((bf16[8,32,1024]{2,1,0:T(8,128)(2,1)}), bf16[8,32,1024]{2,1,0:T(8,128)(2,1)S(1)}, u32[]{:S(2)}, u32[]{:S(2)}) async-start(bf16[8,32,1024]{2,1,0:T(8,128)(2,1)} %pad_maximum_fusion.3), calls=%async_computation.9 | async-start | bytes 1048576 | tf_op jit(solution)/shard_map/all_to_all | solution.py:33
  179.8 0.9 copy-start.12
  180.6 45.3 %all-to-all-start.3 = ((bf16[8,64,2048]{2,1,0:T(8,128)(2,1)}), bf16[8,64,2048]{2,1,0:T(8,128)(2,1)S(1)}, u32[]{:S(2)}, u32[]{:S(2)}) async-start(bf16[8,64,2048]{2,1,0:T(8,128)(2,1)} %bitcast.76), calls=%async_computation.3 | async-start | bytes 4194304 | tf_op jit(solution)/shard_map/all_to_all | solution.py:33
  187.8 2.3 collective-permute-start.2
  187.8 2.3 copy-start.18
  189.9 2.9 %copy-start.15 = (bf16[1024,512]{1,0:T(8,128)(2,1)}, bf16[1024,512]{1,0:T(8,128)(2,1)S(1)}, u32[]{:S(2)}) copy-start(bf16[1024,512]{1,0:T(8,128)(2,1)S(1)} %get-tuple-element.15) | copy-start | bytes 3145732
  189.9 3.2 %copy-start.17 = (bf16[1024,512]{1,0:T(8,128)(2,1)}, bf16[1024,512]{1,0:T(8,128)(2,1)S(1)}, u32[]{:S(2)}) copy-start(bf16[1024,512]{1,0:T(8,128)(2,1)S(1)} %get-tuple-element.17) | copy-start | bytes 3145732
  192.8 14.6 %collective-permute-start.3 = (bf16[1024,256]{1,0:T(8,128)(2,1)}, bf16[1024,256]{1,0:T(8,128)(2,1)}, u32[]{:S(2)}, u32[]{:S(2)}) collective-permute-start(bf16[1024,256]{1,0:T(8,128)(2,1)} %fusion.29), channel_id=1, source_target_pairs={{0,64},{64,0},{128,192},{192,128},{1,65},{65,1},{129,193},{193,129... | collective-permute-start | bytes 1572872 | tf_op jit(solution)/shard_map/ppermute | solution.py:29
  195.6 15.6 %collective-permute-start.5 = (bf16[1024,256]{1,0:T(8,128)(2,1)}, bf16[1024,256]{1,0:T(8,128)(2,1)}, u32[]{:S(2)}, u32[]{:S(2)}) collective-permute-start(bf16[1024,256]{1,0:T(8,128)(2,1)} %fusion.26), channel_id=1, source_target_pairs={{0,192},{64,128},{128,64},{192,0},{1,193},{65,129},{129,65},{193,1... | collective-permute-start | bytes 1572872 | tf_op jit(solution)/shard_map/ppermute | solution.py:29
  208.5 3.8 %copy-start.16 = (bf16[1024,512]{1,0:T(8,128)(2,1)S(1)}, bf16[1024,512]{1,0:T(8,128)(2,1)}, u32[]{:S(2)}) copy-start(bf16[1024,512]{1,0:T(8,128)(2,1)} %copy-done.15) | copy-start | bytes 3145732
  208.5 3.8 %copy-start.19 = (bf16[512,512]{1,0:T(8,128)(2,1)S(1)}, bf16[512,512]{1,0:T(8,128)(2,1)}, u32[]{:S(2)}) copy-start(bf16[512,512]{1,0:T(8,128)(2,1)} %get-tuple-element.23) | copy-start | bytes 1572868
  210.4 4.2 %copy-start.13 = (bf16[8,32,1024]{2,1,0:T(8,128)(2,1)S(1)}, bf16[8,32,1024]{2,1,0:T(8,128)(2,1)}, u32[]{:S(2)}) copy-start(bf16[8,32,1024]{2,1,0:T(8,128)(2,1)} %copy-done.12) | copy-start | bytes 1572868
  210.4 13.0 %collective-permute-start.4 = (bf16[512,256]{1,0:T(8,128)(2,1)S(1)}, bf16[512,256]{1,0:T(8,128)(2,1)S(1)}, u32[]{:S(2)}, u32[]{:S(2)}) collective-permute-start(bf16[512,256]{1,0:T(8,128)(2,1)S(1)} %fusion.36), channel_id=1, source_target_pairs={{0,192},{64,128},{128,64},{192,0},{1,193},{65,129},{129,65},{193,1... | collective-permute-start | bytes 786440 | tf_op jit(solution)/shard_map/ppermute | solution.py:29
  212.3 9.5 %copy-start.8 = (bf16[8,64,2048]{2,1,0:T(8,128)(2,1)S(1)}, bf16[8,64,2048]{2,1,0:T(8,128)(2,1)}, u32[]{:S(2)}) copy-start(bf16[8,64,2048]{2,1,0:T(8,128)(2,1)} %copy-done.7) | copy-start | bytes 6291460
  213.9 7.9 %collective-permute-start.6 = (bf16[512,256]{1,0:T(8,128)(2,1)S(1)}, bf16[512,256]{1,0:T(8,128)(2,1)S(1)}, u32[]{:S(2)}, u32[]{:S(2)}) collective-permute-start(bf16[512,256]{1,0:T(8,128)(2,1)S(1)} %fusion.37), channel_id=1, source_target_pairs={{0,64},{64,0},{128,192},{192,128},{1,65},{65,1},{129,193},{193,129... | collective-permute-start | bytes 786440 | tf_op jit(solution)/shard_map/ppermute | solution.py:29
  225.1 5.8 %copy-start.25 = (pred[256]{0:T(512)(128)(4,1)S(1)}, pred[256]{0:T(512)(128)(4,1)}, u32[]{:S(2)}) copy-start(pred[256]{0:T(512)(128)(4,1)} %copy-done.24) | copy-start | bytes 772
  225.9 22.5 %all-to-all-start.8 = ((bf16[8,64,512]{2,1,0:T(8,128)(2,1)}), bf16[8,64,512]{2,1,0:T(8,128)(2,1)}, u32[]{:S(2)}, u32[]{:S(2)}) async-start(bf16[8,64,512]{2,1,0:T(8,128)(2,1)} %pad_maximum_fusion.2), calls=%async_computation.8 | async-start | bytes 1048576 | tf_op jit(solution)/shard_map/all_to_all | solution.py:33
  230.8 0.8 copy-start.22

commit v2 on v1

v2 whole, which is shorter than its diff:
```python
import jax
import jax.numpy as jnp
from jax import lax
from jax.sharding import Mesh, PartitionSpec as P

FINE = ("y", "zh", "core", "x", "zl")
FINE_SHAPE = (4, 4, 2, 4, 2)
GROUP = ("x", "zl")
EXTRA = 128
ROUTER_STEPS = (
    ("core", 1),
    ("x", 1),
    ("x", 3),
    ("zl", 1),
    ("y", 1),
    ("y", 3),
    ("zh", 1),
    ("zh", 3),
)
F32 = jnp.float32
BF16 = jnp.bfloat16


def gelu_parts(hidden_pre):
    normal_cdf = 0.5 * (1.0 + jax.scipy.special.erf(hidden_pre * 0.7071067811865476))
    normal_pdf = jnp.exp(-0.5 * hidden_pre * hidden_pre) * 0.3989422804014327
    return (normal_cdf, normal_pdf)


def contract_rows(left, right):
    return lax.dot_general(left, right, (((0,), (0,)), ((), ())), preferred_element_type=F32)


def contract_cols(left, right):
    return lax.dot_general(left, right, (((1,), (1,)), ((), ())), preferred_element_type=F32)


def swap(values, axis, mask):
    size = lax.axis_size(axis)
    return lax.ppermute(values, axis, [(i, i ^ mask) for i in range(size)])


def exchange(values, axes):
    return lax.all_to_all(values, axes, split_axis=0, concat_axis=0, tiled=True)


def xor_blocks(values, me, blocks):
    width = values.shape[1] // blocks
    parts = [
        lax.dynamic_slice_in_dim(values, (me ^ r) * width, width, axis=1) for r in range(blocks)
    ]
    return jnp.concatenate(parts, axis=1)


def tie(*values):
    return lax.optimization_barrier(values)


def first_parts(left, right):
    rows = left.shape[1] // 4
    half = right.shape[1] // 2
    part_a = contract_rows(left[:, rows : 3 * rows], right[:, :half]).astype(BF16)
    part_b = contract_rows(left[:, 2 * rows :], right[:, half:]).astype(BF16)
    return part_a, part_b


def second_parts(left, right, got_a, got_b):
    rows = left.shape[1] // 4
    half = right.shape[1] // 2
    part_a = contract_rows(left[:, 3 * rows :], right[:, :half]) + got_a[rows:].astype(F32)
    part_b = contract_rows(left[:, rows : 2 * rows], right[:, half:]) + got_b[:rows].astype(F32)
    return part_a.astype(BF16), part_b.astype(BF16)


def own_parts(left, right, got_a, got_b, far_a, far_b):
    rows = left.shape[1] // 4
    half = right.shape[1] // 2
    near_a = contract_rows(left[:, :rows], right[:, :half]) + got_a[:rows].astype(F32)
    near_b = contract_rows(left[:, :rows], right[:, half:]) + got_b[rows:].astype(F32)
    near_a = near_a + far_a.astype(F32)
    near_b = near_b + far_b.astype(F32)
    return jnp.concatenate([near_a, near_b], axis=1)


def finish(near, scale):
    zh = lax.axis_index("zh")
    block = near.shape[0] // 4
    mine = lax.dynamic_slice_in_dim(near, zh * block, block, axis=0)
    near_b16 = near.astype(BF16)
    for r in (1, 2, 3):
        piece = lax.dynamic_slice_in_dim(near_b16, (zh ^ r) * block, block, axis=0)
        mine = mine + swap(piece, "zh", r).astype(F32)
    core = lax.axis_index("core")
    share = block // 2
    mine = mine * scale
    keep = lax.dynamic_slice_in_dim(mine, core * share, share, axis=0)
    give = lax.dynamic_slice_in_dim(mine, (1 - core) * share, share, axis=0)
    got = swap(give, "core", 1)
    first = jnp.where(core == 0, keep, got)
    second = jnp.where(core == 0, got, keep)
    return jnp.concatenate([first, second], axis=1)[None]


def per_device(
    tokens, grad_out, router_weight, weight_in, weight_out, expert_ids, slot_index, keep_mask
):
    tok_rows, model_width = tokens.shape
    experts = 8
    weight_in = weight_in[0]
    weight_out = weight_out[0]
    capacity = tok_rows * expert_ids.shape[1] // experts
    slot_count = experts * capacity
    grad_scale = float(tok_rows * 256) ** (-0.5)
    core = lax.axis_index("core")
    my_y = lax.axis_index("y")

    target = expert_ids * capacity + slot_index
    slot_iota = jnp.arange(slot_count, dtype=jnp.int32)[:, None]
    first_hit = (slot_iota == target[None, :, 0]) & (keep_mask[None, :, 0] == 1)
    second_hit = (slot_iota == target[None, :, 1]) & (keep_mask[None, :, 1] == 1)
    dispatch = (first_hit | second_hit).astype(BF16)

    send_tokens = jnp.dot(dispatch, tokens, preferred_element_type=F32).astype(BF16)
    slot_tokens = exchange(
        send_tokens.reshape(experts, capacity, model_width), GROUP
    ).reshape(slot_count, model_width)

    logits = jnp.dot(tokens, router_weight, preferred_element_type=F32)
    exp_logits = jnp.exp(logits)
    router_probs = exp_logits / jnp.sum(exp_logits, axis=1, keepdims=True)
    picked = expert_ids[:, :, None] == jnp.arange(experts, dtype=jnp.int32)[None, None, :]
    chosen = jnp.sum(jnp.where(picked, router_probs[:, None, :], 0.0), axis=2)
    keep_float = keep_mask.astype(F32)
    denominator = jnp.sum(keep_float * chosen, axis=1) + (1.0 - jnp.max(keep_float, axis=1))
    combine = keep_float * chosen / denominator[:, None]
    gate_lanes = jnp.sum(jnp.where(picked, combine[:, :, None], 0.0), axis=1).astype(BF16)
    gate_lanes = jnp.pad(gate_lanes, ((0, 0), (0, EXTRA - experts)))
    send_grads = jnp.dot(dispatch, grad_out, preferred_element_type=F32).astype(BF16)
    send_gates = jnp.dot(dispatch, gate_lanes, preferred_element_type=F32).astype(BF16)
    received = exchange(
        jnp.concatenate([send_grads, send_gates], axis=1).reshape(
            experts, capacity, model_width + EXTRA
        ),
        GROUP,
    ).reshape(slot_count, model_width + EXTRA)
    other_tokens = swap(slot_tokens, "core", 1)
    hidden_pre = jnp.dot(slot_tokens, weight_in, preferred_element_type=F32)
    normal_cdf, normal_pdf = gelu_parts(hidden_pre)
    hidden_act = (hidden_pre * normal_cdf).astype(BF16)
    act_slope = normal_cdf + hidden_pre * normal_pdf
    other_act = swap(hidden_act, "core", 1)
    left_in = xor_blocks(jnp.concatenate([slot_tokens, other_tokens], axis=0), my_y, 4)
    left_out = xor_blocks(jnp.concatenate([hidden_act, other_act], axis=0), my_y, 4)

    received, left_in, left_out, hidden_act, act_slope = lax.optimization_barrier(
        (received, left_in, left_out, hidden_act, act_slope)
    )
    slot_grads = received[:, :model_width]
    lane = jnp.arange(EXTRA, dtype=jnp.int32)[None, :]
    gates = jnp.sum(
        jnp.where(lane == lax.axis_index(GROUP), received[:, model_width:].astype(F32), 0.0),
        axis=1,
        keepdims=True,
    )

    half_width = model_width // 2
    scaled_grads = (gates * slot_grads.astype(F32)).astype(BF16)
    my_grads = lax.dynamic_slice_in_dim(scaled_grads, core * half_width, half_width, axis=1)
    give_grads = lax.dynamic_slice_in_dim(scaled_grads, (1 - core) * half_width, half_width, axis=1)
    slot_grads, give_grads = tie(slot_grads, give_grads)
    other_grads = swap(give_grads, "core", 1)

    grad_act = contract_cols(slot_grads, weight_out)
    slot_combine_grad = jnp.sum(hidden_act.astype(F32) * grad_act, axis=1).astype(BF16)
    grad_pre = (gates * grad_act * act_slope).astype(BF16)
    grad_pre, slot_combine_grad, other_grads = tie(grad_pre, slot_combine_grad, other_grads)
    flat_combine = exchange(slot_combine_grad.reshape(experts, capacity), GROUP).reshape(
        slot_count
    )

    half_hidden = grad_pre.shape[1] // 2
    my_pre = lax.dynamic_slice_in_dim(grad_pre, core * half_hidden, half_hidden, axis=1)
    give_pre = lax.dynamic_slice_in_dim(grad_pre, (1 - core) * half_hidden, half_hidden, axis=1)
    other_pre = swap(give_pre, "core", 1)

    right_out = jnp.concatenate([my_grads, other_grads], axis=0)
    out_a, out_b = first_parts(left_out, right_out)
    _, _, grad_pre, other_pre = tie(out_a, out_b, grad_pre, other_pre)
    out_a, out_b = swap(out_a, "y", 1), swap(out_b, "y", 3)

    right_in = jnp.concatenate([my_pre, other_pre], axis=0)
    in_a, in_b = first_parts(left_in, right_in)
    _, _, grad_pre = tie(in_a, in_b, grad_pre)
    in_a, in_b = swap(in_a, "y", 1), swap(in_b, "y", 3)

    grad_slots = contract_cols(grad_pre, weight_in).astype(BF16)
    grad_slots, flat_combine = tie(grad_slots, flat_combine)
    flat_grads = exchange(
        grad_slots.reshape(experts, capacity, model_width), GROUP
    ).reshape(slot_count, model_width)

    far_a, far_b = second_parts(left_out, right_out, out_a, out_b)
    _, _, flat_combine = tie(far_a, far_b, flat_combine)
    far_a, far_b = swap(far_a, "y", 3), swap(far_b, "y", 1)

    combine_wide = flat_combine.astype(F32)[:, None]
    combine_grad = jnp.stack(
        [
            jnp.sum(jnp.where(first_hit, combine_wide, 0.0), axis=0),
            jnp.sum(jnp.where(second_hit, combine_wide, 0.0), axis=0),
        ],
        axis=1,
    )
    weighted_sum = jnp.sum(combine_grad * combine, axis=1)
    chosen_grad = keep_float * (combine_grad - weighted_sum[:, None]) / denominator[:, None]
    probs_grad = jnp.sum(jnp.where(picked, chosen_grad[:, :, None], 0.0), axis=1)
    logit_grad = router_probs * (
        probs_grad - jnp.sum(probs_grad * router_probs, axis=1, keepdims=True)
    )
    logit_b = logit_grad.astype(BF16)

    router_part = contract_rows(logit_b, tokens) * grad_scale
    for axis, mask in ROUTER_STEPS:
        router_part = router_part + swap(router_part, axis, mask)

    near_in_far = second_parts(left_in, right_in, in_a, in_b)
    in_far_a, in_far_b = swap(near_in_far[0], "y", 3), swap(near_in_far[1], "y", 1)
    outer = own_parts(left_out, right_out, out_a, out_b, far_a, far_b)
    outer_share = finish(outer, grad_scale)
    inner = own_parts(left_in, right_in, in_a, in_b, in_far_a, in_far_b)
    inner_share = finish(inner, grad_scale)

    expert_grad = contract_rows(dispatch, flat_grads)
    grad_tokens = (expert_grad + contract_cols(logit_b, router_weight)).astype(BF16)
    return (grad_tokens, router_part.T, inner_share, outer_share)


def solution(mesh):
    fine = Mesh(mesh.devices.reshape(FINE_SHAPE), FINE)
    placed = (
        P(FINE, None),
        P(FINE, None),
        P(),
        P(GROUP, None, None),
        P(GROUP, None, None),
        P(FINE, None),
        P(FINE, None),
        P(FINE, None),
    )
    return jax.shard_map(
        per_device,
        mesh=fine,
        in_specs=placed,
        out_specs=(
            P(FINE, None),
            P(),
            P(GROUP, ("y", "zh", "core"), None),
            P(GROUP, ("y", "zh", "core"), None),
        ),
        check_vma=False,
    )
```

time: 252 us -> 212 us (0.84)
  waiting for transfers between devices: 105 us -> 71.4 us
  blocking collectives: 8.71 us -> 0 us
    all_to_all x9 -> x4, waiting for transfers between devices: 79.9 us -> 28.7 us  [exchange(): return lax.all_to_all(values, axes, split_axis=0, concat_axis=0, tiled=True)]
    all_to_all x9 -> x4, starting transfers between devices: 48.4 us -> 21.9 us  [exchange(): return lax.all_to_all(values, axes, split_axis=0, concat_axis=0, tiled=True)]
    ppermute x13 -> x28, starting transfers between devices: 10.6 us -> 36.7 us  [swap(): return lax.ppermute(values, axis, [(i, i ^ mask) for i in range(size)])]
    ppermute x13 -> x28, waiting for transfers between devices: 25.5 us -> 42.7 us  [swap(): return lax.ppermute(values, axis, [(i, i ^ mask) for i in range(size)])]
    all_to_all x1 -> x0, blocking collectives: 8.71 us -> none  [exchange(): return lax.all_to_all(values, axes, split_axis=0, concat_axis=0, tiled=True)]
    convert_element_type x7 -> x3, other arithmetic: 8.62 us -> 0.52 us  [the longest x1 0.41 us: per_device(): scaled_grads = (gates * slot_grads.astype(F32)).astype(BF16)]
    dot_general x14, matrix products: 21.7 us -> 28.9 us  [contract_rows(): lax.dot_general(left, right, (((0,), (0,)), ((), ())), preferred_element_...]
    concatenate x3 -> x4, other arithmetic: 1.92 us -> 7.26 us  [the longest x2 3.99 us: xor_blocks(): return jnp.concatenate(parts, axis=1)]
  transfers between devices with their start and end apart: 22 -> 32, of which waited for: 13 -> 18; matrix products, arithmetic and copies ran while one was open for 22% -> 29% of each run, Pallas kernels for 0% -> 0%
where the time goes in v2:
time: 212 us; the launch traced here: 210 us
  waiting for transfers between devices  71.4 us (34%)
  starting transfers between devices  58.6 us (28%)
  matrix products  50.9 us (24%)
  other arithmetic  18.7 us (9%)
  local copies, waits for them, and re-layouts  9.35 us (4%)
    ppermute x28, waiting for transfers between devices, swap(): return lax.ppermute(values, axis, [(i, i ^ mask) for i in range(size)])  42.7 us
    ppermute x28, starting transfers between devices, swap(): return lax.ppermute(values, axis, [(i, i ^ mask) for i in range(size)])  36.7 us
    dot_general x14, matrix products, contract_rows(): lax.dot_general(left, right, (((0,), (0,)), ((), ())), preferred_element_...  28.9 us
    all_to_all x4, waiting for transfers between devices, exchange(): return lax.all_to_all(values, axes, split_axis=0, concat_axis=0, tiled=True)  28.7 us
    all_to_all x4, starting transfers between devices, exchange(): return lax.all_to_all(values, axes, split_axis=0, concat_axis=0, tiled=True)  21.9 us
    dot_general x3, matrix products, contract_cols(): lax.dot_general(left, right, (((1,), (1,)), ((), ())), preferred_element_...  10.9 us
    dot_general x1, matrix products, per_device(): hidden_pre = jnp.dot(slot_tokens, weight_in, preferred_element_type=F32)  7.47 us
  transfers between devices with their start and end apart: 32, of which 18 were waited for; matrix products, arithmetic and copies ran while one was open for 29% of the time, Pallas kernels for 0%

profile of v2, /device:TPU:2, one launch (start us, length us, event | category | flops | bytes accessed | tf_op | source)
XLA Modules:
  0.0 210.0 jit_solution(13651759133944700104)
XLA Ops:
  2.2 2.1 convolution_convert_fusion
  4.3 6.3 %all-to-all-start.1 = ((bf16[8,64,2048]{2,1,0:T(8,128)(2,1)}), bf16[8,64,2048]{2,1,0:T(8,128)(2,1)S(1)}, u32[]{:S(2)}, u32[]{:S(2)}) async-start(bf16[8,64,2048]{2,1,0:T(8,128)(2,1)} %bitcast.50), calls=%async_computation.1 | async-start | bytes 4194304 | tf_op jit(solution)/shard_map/all_to_all | solution.py:44
  12.6 1.6 pad_maximum_fusion.1
  14.2 21.6 %all-to-all-done.1 = bf16[8,64,2048]{2,1,0:T(8,128)(2,1)S(1)} async-done(((bf16[8,64,2048]{2,1,0:T(8,128)(2,1)}), bf16[8,64,2048]{2,1,0:T(8,128)(2,1)S(1)}, u32[]{:S(2)}, u32[]{:S(2)}) %all-to-all-start.1) | async-done | bytes 2097184 | tf_op jit(solution)/shard_map/all_to_all | solution.py:44
  35.9 1.3 copy-done.1
  37.2 5.3 %all-to-all-start = ((bf16[8,64,2176]{2,1,0:T(8,128)(2,1)}), bf16[8,64,2176]{2,1,0:T(8,128)(2,1)S(1)}, u32[]{:S(2)}, u32[]{:S(2)}) async-start(bf16[8,64,2176]{2,1,0:T(8,128)(2,1)} %bitcast.45), calls=%async_computation | async-start | bytes 4456448 | tf_op jit(solution)/shard_map/all_to_all | solution.py:44
  42.5 7.5 %fusion.13 = (f32[512,1024]{1,0:T(8,128)}, bf16[512,1024]{1,0:T(8,128)(2,1)}) fusion(bf16[512,2048]{1,0:T(8,128)(2,1)} %bitcast.47, bf16[1,2048,1024]{2,1,0:T(8,128)(2,1)} %param.11), kind=kOutput, calls=%fused_computation.35 | convolution fusion | flops 2152726528 | bytes 9437184 | tf_op jit(solution)/shard_map/dot_general | solution.py:147
  50.5 2.6 %collective-permute-done.1 = bf16[512,1024]{1,0:T(8,128)(2,1)} collective-permute-done((bf16[512,1024]{1,0:T(8,128)(2,1)}, bf16[512,1024]{1,0:T(8,128)(2,1)}, u32[]{:S(2)}, u32[]{:S(2)}) %collective-permute-start.1) | collective-permute-done | bytes 1048608 | tf_op jit(solution)/shard_map/ppermute | solution.py:40
  53.1 1.7 fusion.43
  54.8 1.7 pad_maximum_fusion.2
  57.1 2.0 fusion.28
  59.1 2.3 %pad_maximum_fusion = bf16[1024,2048]{1,0:T(8,128)(2,1)} fusion(bf16[1024,512]{1,0:T(8,128)(2,1)S(1)} %get-tuple-element.45, bf16[1024,512]{1,0:T(8,128)(2,1)S(1)} %get-tuple-element.44, bf16[1024,512]{1,0:T(8,128)(2,1)S(1)} %get-tuple-element.43, bf16[1024,512]{1,0:T(8,128)(2,1)S(1)} %get-tuple-element.42), kind=kLoop, calls=%fused_computation.8 | loop fusion | flops 16777216 | bytes 8388608 | tf_op jit(solution)/shard_map/concatenate | solution.py:52
  61.4 7.1 %all-to-all-done = bf16[8,64,2176]{2,1,0:T(8,128)(2,1)S(1)} async-done(((bf16[8,64,2176]{2,1,0:T(8,128)(2,1)}), bf16[8,64,2176]{2,1,0:T(8,128)(2,1)S(1)}, u32[]{:S(2)}, u32[]{:S(2)}) %all-to-all-start) | async-done | bytes 2228256 | tf_op jit(solution)/shard_map/all_to_all | solution.py:44
  68.4 1.6 slice.100
  70.6 1.6 constant_dynamic-slice_fusion.9
  73.0 5.7 %multiply_reduce_fusion = (bf16[512]{0:T(512)(128)(2,1)S(1)}, bf16[512,1024]{1,0:T(8,128)(2,1)S(1)}) fusion(bf16[512,1024]{1,0:T(8,128)(2,1)} %get-tuple-element.24, f32[512,1024]{1,0:T(8,128)} %get-tuple-element.23, f32[512]{0:T(512)S(1)} %select_reduce_fusion.2, bf16[512,2048]{1,0:T(8,128)(2,1)S(1)} %copy-done.6, bf16[1,1024,2048]{2,1,0:T(8,128)(2,1)} %param.12), kind=kOutput, calls=%fused_computation.41 | convolution fusion | flops 2150628864 | bytes 10488832 | tf_op jit(solution)/shard_map/dot_general | solution.py:35
  78.7 0.9 copy-done.11
  79.7 1.1 constant_dynamic-slice_fusion.8
  81.4 5.0 %all-to-all-start.2 = ((bf16[8,1,64]{2,1,0:T(2,128)(2,1)}), bf16[8,1,64]{2,1,0:T(2,128)(2,1)S(1)}, u32[]{:S(2)}, u32[]{:S(2)}) async-start(bf16[8,1,64]{2,1,0:T(2,128)(2,1)} %all_to_all.20), calls=%async_computation.2 | async-start | bytes 8192 | tf_op jit(solution)/shard_map/all_to_all | solution.py:44
  86.4 2.8 %convolution_convert_fusion.3 = bf16[512,512]{1,0:T(8,128)(2,1)} fusion(bf16[1024,1024]{1,0:T(8,128)(2,1)S(1)} %copy-done.5, bf16[512,1024]{1,0:T(8,128)(2,1)} %get-tuple-element.46, bf16[512,1024]{1,0:T(8,128)(2,1)} %collective-permute-done.2), kind=kOutput, calls=%fused_computation.50 | convolution fusion | flops 539230208 | bytes 3670016 | tf_op jit(solution)/shard_map/dot_general | solution.py:31
  89.3 2.6 %convolution_convert_fusion.2 = bf16[512,512]{1,0:T(8,128)(2,1)} fusion(bf16[1024,1024]{1,0:T(8,128)(2,1)S(1)} %copy-done.5, bf16[512,1024]{1,0:T(8,128)(2,1)} %collective-permute-done.2, bf16[512,1024]{1,0:T(8,128)(2,1)S(1)} %copy-done.8), kind=kOutput, calls=%fused_computation.49 | convolution fusion | flops 539230208 | bytes 3670016 | tf_op jit(solution)/shard_map/dot_general | solution.py:31
  91.9 1.6 collective-permute-start.4
  93.5 2.2 %collective-permute-start.5 = (bf16[512,512]{1,0:T(8,128)(2,1)}, bf16[512,512]{1,0:T(8,128)(2,1)}, u32[]{:S(2)}, u32[]{:S(2)}) collective-permute-start(bf16[512,512]{1,0:T(8,128)(2,1)} %convolution_convert_fusion.2), channel_id=1, source_target_pairs={{0,192},{64,128},{128,64},{192,0},{1,193},{65,129},{129,65},{193,1... | collective-permute-start | bytes 1572872 | tf_op jit(solution)/shard_map/ppermute | solution.py:40
  95.8 3.4 %fusion.18 = bf16[1024,256]{1,0:T(8,128)(2,1)} fusion(bf16[1024,2048]{1,0:T(8,128)(2,1)} %pad_maximum_fusion, bf16[512,512]{1,0:T(8,128)(2,1)} %get-tuple-element.57, bf16[512,512]{1,0:T(8,128)(2,1)} %collective-permute-done.3), kind=kOutput, calls=%fused_computation.47 | convolution fusion | flops 538181632 | bytes 3670016 | tf_op jit(solution)/shard_map/dot_general | solution.py:31
  99.2 2.7 %fusion.21 = bf16[1024,256]{1,0:T(8,128)(2,1)} fusion(bf16[1024,2048]{1,0:T(8,128)(2,1)S(1)} %copy-done.3, bf16[512,512]{1,0:T(8,128)(2,1)} %collective-permute-done.3, bf16[512,512]{1,0:T(8,128)(2,1)S(1)} %copy-done.15), kind=kOutput, calls=%fused_computation.48 | convolution fusion | flops 538181632 | bytes 3670016 | tf_op jit(solution)/shard_map/dot_general | solution.py:31
  101.8 3.7 %fusion.6 = bf16[512,2048]{1,0:T(8,128)(2,1)} fusion(bf16[512,1024]{1,0:T(8,128)(2,1)S(1)} %copy-done.12, bf16[1,2048,1024]{2,1,0:T(8,128)(2,1)S(1)} %copy-done.21), kind=kOutput, calls=%fused_computation.17 | convolution fusion | flops 2148532224 | bytes 7340032 | tf_op jit(solution)/shard_map/dot_general | solution.py:35
  106.3 2.3 %add_convert_fusion.3 = bf16[256,512]{1,0:T(8,128)(2,1)} fusion(bf16[1024,1024]{1,0:T(8,128)(2,1)S(1)} %copy-done.5, bf16[512,512]{1,0:T(8,128)(2,1)} %collective-permute-done.4, bf16[512,1024]{1,0:T(8,128)(2,1)S(1)} %copy-done.9, bf16[512,1024]{1,0:T(8,128)(2,1)} %collective-permute-done.2), kind=kOutput, calls=%fused_computation.96 | convolution fusion | flops 270925824 | bytes 3145728 | tf_op jit(solution)/shard_map/dot_general | solution.py:31
  108.8 2.3 %add_convert_fusion.2 = bf16[256,512]{1,0:T(8,128)(2,1)} fusion(bf16[1024,1024]{1,0:T(8,128)(2,1)S(1)} %copy-done.5, bf16[512,512]{1,0:T(8,128)(2,1)} %collective-permute-done.5, bf16[512,1024]{1,0:T(8,128)(2,1)} %collective-permute-done.2, bf16[512,1024]{1,0:T(8,128)(2,1)S(1)} %copy-done.9), kind=kOutput, calls=%fused_computation.93 | convolution fusion | flops 270925824 | bytes 3145728 | tf_op jit(solution)/shard_map/dot_general | solution.py:31
  111.8 1.2 collective-permute-done.6
  113.7 2.5 %fusion.59 = f32[256,512]{1,0:T(8,128)} fusion(bf16[1024,1024]{1,0:T(8,128)(2,1)S(1)} %copy-done.5, bf16[512,1024]{1,0:T(8,128)(2,1)} %get-tuple-element.46, bf16[512,1024]{1,0:T(8,128)(2,1)} %collective-permute-done.2), kind=kOutput, calls=%fused_computation.106 | convolution fusion | flops 270532608 | bytes 3145728 | tf_op jit(solution)/shard_map/dot_general | solution.py:31
  116.2 1.2 collective-permute-done.7
  117.4 1.5 collective-permute-start.8
  118.9 2.3 %fusion.57 = f32[256,512]{1,0:T(8,128)} fusion(bf16[1024,1024]{1,0:T(8,128)(2,1)S(1)} %copy-done.5, bf16[512,1024]{1,0:T(8,128)(2,1)} %collective-permute-done.2, bf16[512,1024]{1,0:T(8,128)(2,1)S(1)} %copy-done.10), kind=kOutput, calls=%fused_computation.104 | convolution fusion | flops 270532608 | bytes 3145728 | tf_op jit(solution)/shard_map/dot_general | solution.py:31
  121.2 1.4 collective-permute-start.14
  122.6 2.2 %collective-permute-start.22 = (bf16[256,512]{1,0:T(8,128)(2,1)}, bf16[256,512]{1,0:T(8,128)(2,1)S(1)}, u32[]{:S(2)}, u32[]{:S(2)}) collective-permute-start(bf16[256,512]{1,0:T(8,128)(2,1)} %add_convert_fusion.3), channel_id=1, source_target_pairs={{0,192},{64,128},{128,64},{192,0},{1,193},{65,129},{129,65},{193,1... | collective-permute-start | bytes 786440 | tf_op jit(solution)/shard_map/ppermute | solution.py:40
  124.9 1.5 collective-permute-start.9
  126.4 2.5 %fusion.39 = f32[512,256]{1,0:T(8,128)} fusion(bf16[1024,2048]{1,0:T(8,128)(2,1)} %pad_maximum_fusion, bf16[512,512]{1,0:T(8,128)(2,1)S(1)} %copy-done.16, bf16[512,512]{1,0:T(8,128)(2,1)} %collective-permute-done.3), kind=kOutput, calls=%fused_computation.77 | convolution fusion | flops 269484032 | bytes 2621440 | tf_op jit(solution)/shard_map/dot_general | solution.py:31
  129.6 5.3 %all-to-all-start.3 = ((bf16[8,64,2048]{2,1,0:T(8,128)(2,1)}), bf16[8,64,2048]{2,1,0:T(8,128)(2,1)S(1)}, u32[]{:S(2)}, u32[]{:S(2)}) async-start(bf16[8,64,2048]{2,1,0:T(8,128)(2,1)} %bitcast.51), calls=%async_computation.3 | async-start | bytes 4194304 | tf_op jit(solution)/shard_map/all_to_all | solution.py:44
  135.8 1.6 collective-permute-start.10
  137.5 1.4 convert_add_fusion.1
  138.8 1.9 collective-permute-done.23
  140.8 1.1 convert_add_fusion
  142.1 5.5 %collective-permute-start.26 = (bf16[64,1024]{1,0:T(8,128)(2,1)S(1)}, bf16[64,1024]{1,0:T(8,128)(2,1)S(1)}, u32[]{:S(2)}, u32[]{:S(2)}) collective-permute-start(bf16[64,1024]{1,0:T(8,128)(2,1)S(1)} %get-tuple-element.59), channel_id=1, source_target_pairs={{0,48},{16,32},{32,16},{48,0},{1,49},{17,33},{33,17},{49,1},{2,50}... | collective-permute-start | bytes 393224 | tf_op jit(solution)/shard_map/ppermute | solution.py:40
  147.5 1.4 collective-permute-start.25
  149.0 1.0 collective-permute-start.24
  150.0 2.9 %collective-permute-start.11 = (f32[8,2048]{1,0:T(8,128)S(1)}, f32[8,2048]{1,0:T(8,128)S(1)}, u32[]{:S(2)}, u32[]{:S(2)}) collective-permute-start(f32[8,2048]{1,0:T(8,128)S(1)} %add.202), channel_id=1, source_target_pairs={{0,192},{64,128},{128,64},{192,0},{1,193},{65,129},{129,65},{193,1... | collective-permute-start | bytes 196616 | tf_op jit(solution)/shard_map/ppermute | solution.py:40
  152.9 1.4 fusion.37
  154.4 1.4 collective-permute-done.11
  155.8 3.0 %collective-permute-start.16 = (bf16[1024,256]{1,0:T(8,128)(2,1)S(1)}, bf16[1024,256]{1,0:T(8,128)(2,1)S(1)}, u32[]{:S(2)}, u32[]{:S(2)}) collective-permute-start(bf16[1024,256]{1,0:T(8,128)(2,1)S(1)} %copy-done.22), channel_id=1, source_target_pairs={{0,192},{64,128},{128,64},{192,0},{1,193},{65,129},{129,65},{193,1... | collective-permute-start | bytes 1572872 | tf_op jit(solution)/shard_map/ppermute | solution.py:40
  158.8 13.0 %collective-permute-done.26 = bf16[64,1024]{1,0:T(8,128)(2,1)S(1)} collective-permute-done((bf16[64,1024]{1,0:T(8,128)(2,1)S(1)}, bf16[64,1024]{1,0:T(8,128)(2,1)S(1)}, u32[]{:S(2)}, u32[]{:S(2)}) %collective-permute-start.26) | collective-permute-done | bytes 131104 | tf_op jit(solution)/shard_map/ppermute | solution.py:40
  172.0 4.9 %collective-permute-done.12 = f32[8,2048]{1,0:T(8,128)S(1)} collective-permute-done((f32[8,2048]{1,0:T(8,128)S(1)}, f32[8,2048]{1,0:T(8,128)S(1)}, u32[]{:S(2)}, u32[]{:S(2)}) %collective-permute-start.12) | collective-permute-done | bytes 65568 | tf_op jit(solution)/shard_map/ppermute | solution.py:40
  177.1 1.5 add_convert_fusion.1
  179.6 1.4 add_convert_fusion
  181.0 1.0 collective-permute-start.17
  182.0 1.4 collective-permute-done.13
  184.1 2.2 %collective-permute-done.15 = bf16[512,256]{1,0:T(8,128)(2,1)S(1)} collective-permute-done((bf16[512,256]{1,0:T(8,128)(2,1)S(1)}, bf16[512,256]{1,0:T(8,128)(2,1)S(1)}, u32[]{:S(2)}, u32[]{:S(2)}) %collective-permute-start.15) | collective-permute-done | bytes 262176 | tf_op jit(solution)/shard_map/ppermute | solution.py:40
  186.3 1.0 convert_add_fusion.3
  187.6 4.2 %collective-permute-start.20 = (bf16[128,512]{1,0:T(8,128)(2,1)S(1)}, bf16[128,512]{1,0:T(8,128)(2,1)S(1)}, u32[]{:S(2)}, u32[]{:S(2)}) collective-permute-start(bf16[128,512]{1,0:T(8,128)(2,1)S(1)} %get-tuple-element.62), channel_id=1, source_target_pairs={{0,48},{16,32},{32,16},{48,0},{1,49},{17,33},{33,17},{49,1},{2,50}... | collective-permute-start | bytes 393224 | tf_op jit(solution)/shard_map/ppermute | solution.py:40
  191.8 1.0 collective-permute-start.19
  192.8 1.5 collective-permute-start.18
  194.3 7.4 %collective-permute-done.20 = bf16[128,512]{1,0:T(8,128)(2,1)S(1)} collective-permute-done((bf16[128,512]{1,0:T(8,128)(2,1)S(1)}, bf16[128,512]{1,0:T(8,128)(2,1)S(1)}, u32[]{:S(2)}, u32[]{:S(2)}) %collective-permute-start.20) | collective-permute-done | bytes 131104 | tf_op jit(solution)/shard_map/ppermute | solution.py:40
  201.7 1.8 collective-permute-done.19
  203.5 2.0 collective-permute-done.18
  208.5 1.5 fusion.9
  (122 shorter events, 15.9 us)
Async XLA Ops:
  0.6 1.6 copy-start
  4.3 6.3 %copy-start.18 = (bf16[2048,8]{0,1:T(8,128)(2,1)S(1)}, bf16[2048,8]{0,1:T(8,128)(2,1)}, u32[]{:S(2)}) copy-start(bf16[2048,8]{0,1:T(8,128)(2,1)} %param.10) | copy-start | bytes 98308
  4.3 6.8 %copy-start.20 = (s32[256,2]{0,1:T(2,128)S(1)}, s32[256,2]{0,1:T(2,128)}, u32[]{:S(2)}) copy-start(s32[256,2]{0,1:T(2,128)} %param.13) | copy-start | bytes 6148
  4.3 6.8 %copy-start.19 = (s32[256,2]{0,1:T(2,128)S(1)}, s32[256,2]{0,1:T(2,128)}, u32[]{:S(2)}) copy-start(s32[256,2]{0,1:T(2,128)} %param.15) | copy-start | bytes 6148
  4.3 31.5 %all-to-all-start.1 = ((bf16[8,64,2048]{2,1,0:T(8,128)(2,1)}), bf16[8,64,2048]{2,1,0:T(8,128)(2,1)S(1)}, u32[]{:S(2)}, u32[]{:S(2)}) async-start(bf16[8,64,2048]{2,1,0:T(8,128)(2,1)} %bitcast.50), calls=%async_computation.1 | async-start | bytes 4194304 | tf_op jit(solution)/shard_map/all_to_all | solution.py:44
  10.6 1.2 copy-start.7
  35.9 1.3 copy-start.1
  37.2 31.3 %all-to-all-start = ((bf16[8,64,2176]{2,1,0:T(8,128)(2,1)}), bf16[8,64,2176]{2,1,0:T(8,128)(2,1)S(1)}, u32[]{:S(2)}, u32[]{:S(2)}) async-start(bf16[8,64,2176]{2,1,0:T(8,128)(2,1)} %bitcast.45), calls=%async_computation | async-start | bytes 4456448 | tf_op jit(solution)/shard_map/all_to_all | solution.py:44
  42.5 14.0 %collective-permute-start = (bf16[512,2048]{1,0:T(8,128)(2,1)}, bf16[512,2048]{1,0:T(8,128)(2,1)}, u32[]{:S(2)}, u32[]{:S(2)}) collective-permute-start(bf16[512,2048]{1,0:T(8,128)(2,1)} %bitcast.46), channel_id=1, source_target_pairs={{0,8},{8,0},{1,9},{9,1},{2,10},{10,2},{3,11},{11,3},{4,12},{12,4},... | collective-permute-start | bytes 6291464 | tf_op jit(solution)/shard_map/ppermute | solution.py:40
  50.0 3.1 %collective-permute-start.1 = (bf16[512,1024]{1,0:T(8,128)(2,1)}, bf16[512,1024]{1,0:T(8,128)(2,1)}, u32[]{:S(2)}, u32[]{:S(2)}) collective-permute-start(bf16[512,1024]{1,0:T(8,128)(2,1)} %get-tuple-element.24), channel_id=1, source_target_pairs={{0,8},{8,0},{1,9},{9,1},{2,10},{10,2},{3,11},{11,3},{4,12},{12,4},... | collective-permute-start | bytes 3145736 | tf_op jit(solution)/shard_map/ppermute | solution.py:40
  54.8 2.3 %copy-start.2 = (bf16[8,64,2048]{2,1,0:T(8,128)(2,1)S(1)}, bf16[8,64,2048]{2,1,0:T(8,128)(2,1)}, u32[]{:S(2)}) copy-start(bf16[8,64,2048]{2,1,0:T(8,128)(2,1)} %copy-done.1) | copy-start | bytes 6291460
  70.6 2.3 %copy-start.6 = (bf16[512,2048]{1,0:T(8,128)(2,1)S(1)}, bf16[512,2048]{1,0:T(8,128)(2,1)}, u32[]{:S(2)}) copy-start(bf16[512,2048]{1,0:T(8,128)(2,1)} %slice.100) | copy-start | bytes 6291460
  72.2 6.5 %collective-permute-start.2 = (bf16[512,1024]{1,0:T(8,128)(2,1)}, bf16[512,1024]{1,0:T(8,128)(2,1)}, u32[]{:S(2)}, u32[]{:S(2)}) collective-permute-start(bf16[512,1024]{1,0:T(8,128)(2,1)} %get-tuple-element.25), channel_id=1, source_target_pairs={{0,8},{8,0},{1,9},{9,1},{2,10},{10,2},{3,11},{11,3},{4,12},{12,4},... | collective-permute-start | bytes 3145736 | tf_op jit(solution)/shard_map/ppermute | solution.py:40
  78.7 1.0 copy-start.11
  78.7 7.7 %copy-start.5 = (bf16[1024,1024]{1,0:T(8,128)(2,1)S(1)}, bf16[1024,1024]{1,0:T(8,128)(2,1)}, u32[]{:S(2)}) copy-start(bf16[1024,1024]{1,0:T(8,128)(2,1)} %pad_maximum_fusion.2) | copy-start | bytes 6291460
  80.7 15.0 %collective-permute-start.3 = (bf16[512,512]{1,0:T(8,128)(2,1)}, bf16[512,512]{1,0:T(8,128)(2,1)}, u32[]{:S(2)}, u32[]{:S(2)}) collective-permute-start(bf16[512,512]{1,0:T(8,128)(2,1)} %get-tuple-element.56), channel_id=1, source_target_pairs={{0,8},{8,0},{1,9},{9,1},{2,10},{10,2},{3,11},{11,3},{4,12},{12,4},... | collective-permute-start | bytes 1572872 | tf_op jit(solution)/shard_map/ppermute | solution.py:40
  81.4 14.2 %all-to-all-start.2 = ((bf16[8,1,64]{2,1,0:T(2,128)(2,1)}), bf16[8,1,64]{2,1,0:T(2,128)(2,1)S(1)}, u32[]{:S(2)}, u32[]{:S(2)}) async-start(bf16[8,1,64]{2,1,0:T(2,128)(2,1)} %all_to_all.20), calls=%async_computation.2 | async-start | bytes 8192 | tf_op jit(solution)/shard_map/all_to_all | solution.py:44
  86.4 2.8 %copy-start.8 = (bf16[512,1024]{1,0:T(8,128)(2,1)S(1)}, bf16[512,1024]{1,0:T(8,128)(2,1)}, u32[]{:S(2)}) copy-start(bf16[512,1024]{1,0:T(8,128)(2,1)} %get-tuple-element.46) | copy-start | bytes 3145732
  91.9 14.4 %collective-permute-start.4 = (bf16[512,512]{1,0:T(8,128)(2,1)}, bf16[512,512]{1,0:T(8,128)(2,1)}, u32[]{:S(2)}, u32[]{:S(2)}) collective-permute-start(bf16[512,512]{1,0:T(8,128)(2,1)} %convolution_convert_fusion.3), channel_id=1, source_target_pairs={{0,64},{64,0},{128,192},{192,128},{1,65},{65,1},{129,193},{193,129... | collective-permute-start | bytes 1572872 | tf_op jit(solution)/shard_map/ppermute | solution.py:40
  93.5 15.3 %collective-permute-start.5 = (bf16[512,512]{1,0:T(8,128)(2,1)}, bf16[512,512]{1,0:T(8,128)(2,1)}, u32[]{:S(2)}, u32[]{:S(2)}) collective-permute-start(bf16[512,512]{1,0:T(8,128)(2,1)} %convolution_convert_fusion.2), channel_id=1, source_target_pairs={{0,192},{64,128},{128,64},{192,0},{1,193},{65,129},{129,65},{193,1... | collective-permute-start | bytes 1572872 | tf_op jit(solution)/shard_map/ppermute | solution.py:40
  95.8 3.4 %copy-start.3 = (bf16[1024,2048]{1,0:T(8,128)(2,1)S(1)}, bf16[1024,2048]{1,0:T(8,128)(2,1)}, u32[]{:S(2)}) copy-start(bf16[1024,2048]{1,0:T(8,128)(2,1)} %pad_maximum_fusion) | copy-start | bytes 12582916
  95.8 3.4 %copy-start.15 = (bf16[512,512]{1,0:T(8,128)(2,1)S(1)}, bf16[512,512]{1,0:T(8,128)(2,1)}, u32[]{:S(2)}) copy-start(bf16[512,512]{1,0:T(8,128)(2,1)} %get-tuple-element.57) | copy-start | bytes 1572868
  99.1 2.7 %copy-start.12 = (bf16[512,1024]{1,0:T(8,128)(2,1)S(1)}, bf16[512,1024]{1,0:T(8,128)(2,1)}, u32[]{:S(2)}) copy-start(bf16[512,1024]{1,0:T(8,128)(2,1)} %copy-done.11) | copy-start | bytes 3145732
  99.1 2.7 %copy-start.21 = (bf16[1,2048,1024]{2,1,0:T(8,128)(2,1)S(1)}, bf16[1,2048,1024]{2,1,0:T(8,128)(2,1)}, u32[]{:S(2)}) copy-start(bf16[1,2048,1024]{2,1,0:T(8,128)(2,1)} %param.11) | copy-start | bytes 12582916
  101.8 4.4 %copy-start.9 = (bf16[512,1024]{1,0:T(8,128)(2,1)S(1)}, bf16[512,1024]{1,0:T(8,128)(2,1)}, u32[]{:S(2)}) copy-start(bf16[512,1024]{1,0:T(8,128)(2,1)} %get-tuple-element.46) | copy-start | bytes 3145732
  111.7 1.3 collective-permute-start.6
  113.0 5.9 %copy-start.10 = (bf16[512,1024]{1,0:T(8,128)(2,1)S(1)}, bf16[512,1024]{1,0:T(8,128)(2,1)}, u32[]{:S(2)}) copy-start(bf16[512,1024]{1,0:T(8,128)(2,1)} %get-tuple-element.46) | copy-start | bytes 3145732
  113.0 4.4 %collective-permute-start.7 = (f32[8,2048]{1,0:T(8,128)S(1)}, f32[8,2048]{1,0:T(8,128)S(1)}, u32[]{:S(2)}, u32[]{:S(2)}) collective-permute-start(f32[8,2048]{1,0:T(8,128)S(1)} %add.198), channel_id=1, source_target_pairs={{0,2},{2,0},{4,6},{6,4},{1,3},{3,1},{5,7},{7,5},{8,10},{10,8},{12,... | collective-permute-start | bytes 196616 | tf_op jit(solution)/shard_map/ppermute | solution.py:40
  116.2 10.2 %copy-start.16 = (bf16[512,512]{1,0:T(8,128)(2,1)S(1)}, bf16[512,512]{1,0:T(8,128)(2,1)}, u32[]{:S(2)}) copy-start(bf16[512,512]{1,0:T(8,128)(2,1)} %get-tuple-element.57) | copy-start | bytes 1572868
  117.4 7.5 %collective-permute-start.8 = (f32[8,2048]{1,0:T(8,128)S(1)}, f32[8,2048]{1,0:T(8,128)S(1)}, u32[]{:S(2)}, u32[]{:S(2)}) collective-permute-start(f32[8,2048]{1,0:T(8,128)S(1)} %add.199), channel_id=1, source_target_pairs={{0,6},{2,4},{4,2},{6,0},{1,7},{3,5},{5,3},{7,1},{8,14},{10,12},{12... | collective-permute-start | bytes 196616 | tf_op jit(solution)/shard_map/ppermute | solution.py:40
  121.2 55.8 %collective-permute-start.14 = (bf16[1024,256]{1,0:T(8,128)(2,1)}, bf16[1024,256]{1,0:T(8,128)(2,1)}, u32[]{:S(2)}, u32[]{:S(2)}) collective-permute-start(bf16[1024,256]{1,0:T(8,128)(2,1)} %fusion.18), channel_id=1, source_target_pairs={{0,64},{64,0},{128,192},{192,128},{1,65},{65,1},{129,193},{193,129... | collective-permute-start | bytes 1572872 | tf_op jit(solution)/shard_map/ppermute | solution.py:40
  122.6 14.8 %collective-permute-start.22 = (bf16[256,512]{1,0:T(8,128)(2,1)}, bf16[256,512]{1,0:T(8,128)(2,1)S(1)}, u32[]{:S(2)}, u32[]{:S(2)}) collective-permute-start(bf16[256,512]{1,0:T(8,128)(2,1)} %add_convert_fusion.3), channel_id=1, source_target_pairs={{0,192},{64,128},{128,64},{192,0},{1,193},{65,129},{129,65},{193,1... | collective-permute-start | bytes 786440 | tf_op jit(solution)/shard_map/ppermute | solution.py:40
  124.9 10.1 %collective-permute-start.9 = (f32[8,2048]{1,0:T(8,128)S(1)}, f32[8,2048]{1,0:T(8,128)}, u32[]{:S(2)}, u32[]{:S(2)}) collective-permute-start(f32[8,2048]{1,0:T(8,128)S(1)} %add.200), channel_id=1, source_target_pairs={{0,1},{1,0},{2,3},{3,2},{4,5},{5,4},{6,7},{7,6},{8,9},{9,8},{10,11... | collective-permute-start | bytes 196616 | tf_op jit(solution)/shard_map/ppermute | solution.py:40
  128.9 11.9 %collective-permute-start.23 = (bf16[256,512]{1,0:T(8,128)(2,1)}, bf16[256,512]{1,0:T(8,128)(2,1)}, u32[]{:S(2)}, u32[]{:S(2)}) collective-permute-start(bf16[256,512]{1,0:T(8,128)(2,1)} %add_convert_fusion.2), channel_id=1, source_target_pairs={{0,64},{64,0},{128,192},{192,128},{1,65},{65,1},{129,193},{193,129... | collective-permute-start | bytes 786440 | tf_op jit(solution)/shard_map/ppermute | solution.py:40
  129.6 78.1 %all-to-all-start.3 = ((bf16[8,64,2048]{2,1,0:T(8,128)(2,1)}), bf16[8,64,2048]{2,1,0:T(8,128)(2,1)S(1)}, u32[]{:S(2)}, u32[]{:S(2)}) async-start(bf16[8,64,2048]{2,1,0:T(8,128)(2,1)} %bitcast.51), calls=%async_computation.3 | async-start | bytes 4194304 | tf_op jit(solution)/shard_map/all_to_all | solution.py:44
  134.9 5.9 %copy-start.14 = (f32[256,512]{1,0:T(8,128)S(1)}, f32[256,512]{1,0:T(8,128)}, u32[]{:S(2)}) copy-start(f32[256,512]{1,0:T(8,128)} %fusion.57) | copy-start | bytes 1572868
  135.8 14.2 %collective-permute-start.10 = (f32[8,2048]{1,0:T(8,128)S(1)}, f32[8,2048]{1,0:T(8,128)S(1)}, u32[]{:S(2)}, u32[]{:S(2)}) collective-permute-start(f32[8,2048]{1,0:T(8,128)S(1)} %add.201), channel_id=1, source_target_pairs={{0,64},{64,0},{128,192},{192,128},{1,65},{65,1},{129,193},{193,129... | collective-permute-start | bytes 196616 | tf_op jit(solution)/shard_map/ppermute | solution.py:40
  137.5 15.5 %copy-start.4 = (bf16[1024,2048]{1,0:T(8,128)(2,1)S(1)}, bf16[1024,2048]{1,0:T(8,128)(2,1)}, u32[]{:S(2)}) copy-start(bf16[1024,2048]{1,0:T(8,128)(2,1)} %pad_maximum_fusion) | copy-start | bytes 12582916
  138.8 14.1 %copy-start.17 = (bf16[512,512]{1,0:T(8,128)(2,1)S(1)}, bf16[512,512]{1,0:T(8,128)(2,1)}, u32[]{:S(2)}) copy-start(bf16[512,512]{1,0:T(8,128)(2,1)} %get-tuple-element.57) | copy-start | bytes 1572868
  142.0 13.8 %copy-start.22 = (bf16[1024,256]{1,0:T(8,128)(2,1)S(1)}, bf16[1024,256]{1,0:T(8,128)(2,1)}, u32[]{:S(2)}) copy-start(bf16[1024,256]{1,0:T(8,128)(2,1)} %fusion.21) | copy-start | bytes 1572868
  142.1 29.7 %collective-permute-start.26 = (bf16[64,1024]{1,0:T(8,128)(2,1)S(1)}, bf16[64,1024]{1,0:T(8,128)(2,1)S(1)}, u32[]{:S(2)}, u32[]{:S(2)}) collective-permute-start(bf16[64,1024]{1,0:T(8,128)(2,1)S(1)} %get-tuple-element.59), channel_id=1, source_target_pairs={{0,48},{16,32},{32,16},{48,0},{1,49},{17,33},{33,17},{49,1},{2,50}... | collective-permute-start | bytes 393224 | tf_op jit(solution)/shard_map/ppermute | solution.py:40
  147.5 24.3 %collective-permute-start.25 = (bf16[64,1024]{1,0:T(8,128)(2,1)S(1)}, bf16[64,1024]{1,0:T(8,128)(2,1)S(1)}, u32[]{:S(2)}, u32[]{:S(2)}) collective-permute-start(bf16[64,1024]{1,0:T(8,128)(2,1)S(1)} %get-tuple-element.60), channel_id=1, source_target_pairs={{0,32},{16,48},{32,0},{48,16},{1,33},{17,49},{33,1},{49,17},{2,34}... | collective-permute-start | bytes 393224 | tf_op jit(solution)/shard_map/ppermute | solution.py:40
  149.0 22.8 %collective-permute-start.24 = (bf16[64,1024]{1,0:T(8,128)(2,1)S(1)}, bf16[64,1024]{1,0:T(8,128)(2,1)S(1)}, u32[]{:S(2)}, u32[]{:S(2)}) collective-permute-start(bf16[64,1024]{1,0:T(8,128)(2,1)S(1)} %get-tuple-element.58), channel_id=1, source_target_pairs={{0,16},{16,0},{32,48},{48,32},{1,17},{17,1},{33,49},{49,33},{2,18}... | collective-permute-start | bytes 393224 | tf_op jit(solution)/shard_map/ppermute | solution.py:40
  150.0 5.8 %collective-permute-start.11 = (f32[8,2048]{1,0:T(8,128)S(1)}, f32[8,2048]{1,0:T(8,128)S(1)}, u32[]{:S(2)}, u32[]{:S(2)}) collective-permute-start(f32[8,2048]{1,0:T(8,128)S(1)} %add.202), channel_id=1, source_target_pairs={{0,192},{64,128},{128,64},{192,0},{1,193},{65,129},{129,65},{193,1... | collective-permute-start | bytes 196616 | tf_op jit(solution)/shard_map/ppermute | solution.py:40
  155.8 23.8 %collective-permute-start.16 = (bf16[1024,256]{1,0:T(8,128)(2,1)S(1)}, bf16[1024,256]{1,0:T(8,128)(2,1)S(1)}, u32[]{:S(2)}, u32[]{:S(2)}) collective-permute-start(bf16[1024,256]{1,0:T(8,128)(2,1)S(1)} %copy-done.22), channel_id=1, source_target_pairs={{0,192},{64,128},{128,64},{192,0},{1,193},{65,129},{129,65},{193,1... | collective-permute-start | bytes 1572872 | tf_op jit(solution)/shard_map/ppermute | solution.py:40
  171.8 5.2 %collective-permute-start.12 = (f32[8,2048]{1,0:T(8,128)S(1)}, f32[8,2048]{1,0:T(8,128)S(1)}, u32[]{:S(2)}, u32[]{:S(2)}) collective-permute-start(f32[8,2048]{1,0:T(8,128)S(1)} %add.203), channel_id=1, source_target_pairs={{0,16},{16,0},{32,48},{48,32},{1,17},{17,1},{33,49},{49,33},{2,18}... | collective-permute-start | bytes 196616 | tf_op jit(solution)/shard_map/ppermute | solution.py:40
  171.9 22.4 %collective-permute-start.27 = (f32[32,1024]{1,0:T(8,128)S(1)}, f32[32,1024]{1,0:T(8,128)S(1)}, u32[]{:S(2)}, u32[]{:S(2)}) collective-permute-start(f32[32,1024]{1,0:T(8,128)S(1)} %constant_dynamic-slice_fusion), channel_id=1, source_target_pairs={{0,8},{8,0},{1,9},{9,1},{2,10},{10,2},{3,11},{11,3},{4,12},{12,4},... | collective-permute-start | bytes 393224 | tf_op jit(solution)/shard_map/ppermute | solution.py:40
  177.0 6.5 %collective-permute-start.13 = (f32[8,2048]{1,0:T(8,128)S(1)}, f32[8,2048]{1,0:T(8,128)S(1)}, u32[]{:S(2)}, u32[]{:S(2)}) collective-permute-start(f32[8,2048]{1,0:T(8,128)S(1)} %add.204), channel_id=1, source_target_pairs={{0,48},{16,32},{32,16},{48,0},{1,49},{17,33},{33,17},{49,1},{2,50}... | collective-permute-start | bytes 196616 | tf_op jit(solution)/shard_map/ppermute | solution.py:40
  178.6 7.7 %copy-start.13 = (f32[512,256]{1,0:T(8,128)S(1)}, f32[512,256]{1,0:T(8,128)}, u32[]{:S(2)}) copy-start(f32[512,256]{1,0:T(8,128)} %fusion.39) | copy-start | bytes 1572868
  178.6 7.7 %collective-permute-start.15 = (bf16[512,256]{1,0:T(8,128)(2,1)S(1)}, bf16[512,256]{1,0:T(8,128)(2,1)S(1)}, u32[]{:S(2)}, u32[]{:S(2)}) collective-permute-start(bf16[512,256]{1,0:T(8,128)(2,1)S(1)} %add_convert_fusion.1), channel_id=1, source_target_pairs={{0,192},{64,128},{128,64},{192,0},{1,193},{65,129},{129,65},{193,1... | collective-permute-start | bytes 786440 | tf_op jit(solution)/shard_map/ppermute | solution.py:40
  181.0 6.5 %collective-permute-start.17 = (bf16[512,256]{1,0:T(8,128)(2,1)S(1)}, bf16[512,256]{1,0:T(8,128)(2,1)S(1)}, u32[]{:S(2)}, u32[]{:S(2)}) collective-permute-start(bf16[512,256]{1,0:T(8,128)(2,1)S(1)} %add_convert_fusion), channel_id=1, source_target_pairs={{0,64},{64,0},{128,192},{192,128},{1,65},{65,1},{129,193},{193,129... | collective-permute-start | bytes 786440 | tf_op jit(solution)/shard_map/ppermute | solution.py:40
  187.6 14.1 %collective-permute-start.20 = (bf16[128,512]{1,0:T(8,128)(2,1)S(1)}, bf16[128,512]{1,0:T(8,128)(2,1)S(1)}, u32[]{:S(2)}, u32[]{:S(2)}) collective-permute-start(bf16[128,512]{1,0:T(8,128)(2,1)S(1)} %get-tuple-element.62), channel_id=1, source_target_pairs={{0,48},{16,32},{32,16},{48,0},{1,49},{17,33},{33,17},{49,1},{2,50}... | collective-permute-start | bytes 393224 | tf_op jit(solution)/shard_map/ppermute | solution.py:40
  191.8 11.6 %collective-permute-start.19 = (bf16[128,512]{1,0:T(8,128)(2,1)S(1)}, bf16[128,512]{1,0:T(8,128)(2,1)S(1)}, u32[]{:S(2)}, u32[]{:S(2)}) collective-permute-start(bf16[128,512]{1,0:T(8,128)(2,1)S(1)} %get-tuple-element.63), channel_id=1, source_target_pairs={{0,32},{16,48},{32,0},{48,16},{1,33},{17,49},{33,1},{49,17},{2,34}... | collective-permute-start | bytes 393224 | tf_op jit(solution)/shard_map/ppermute | solution.py:40
  192.8 12.6 %collective-permute-start.18 = (bf16[128,512]{1,0:T(8,128)(2,1)S(1)}, bf16[128,512]{1,0:T(8,128)(2,1)S(1)}, u32[]{:S(2)}, u32[]{:S(2)}) collective-permute-start(bf16[128,512]{1,0:T(8,128)(2,1)S(1)} %get-tuple-element.61), channel_id=1, source_target_pairs={{0,16},{16,0},{32,48},{48,32},{1,17},{17,1},{33,49},{49,33},{2,18}... | collective-permute-start | bytes 393224 | tf_op jit(solution)/shard_map/ppermute | solution.py:40
  205.6 1.4 collective-permute-start.21

commit v3 on v2

v3 whole, which is shorter than its diff:
```python
import jax
import jax.numpy as jnp
from jax import lax
from jax.experimental import pallas as pl
from jax.experimental.pallas import tpu as pltpu
from jax.sharding import Mesh, PartitionSpec as P

FINE = ("y", "zh", "core", "x", "zl")
FINE_SHAPE = (4, 4, 2, 4, 2)
GROUP = ("x", "zl")
EXTRA = 128
ROUTER_STEPS = (
    ("core", 1),
    ("x", 1),
    ("x", 3),
    ("zl", 1),
    ("y", 1),
    ("y", 3),
    ("zh", 1),
    ("zh", 3),
)
F32 = jnp.float32
BF16 = jnp.bfloat16


def gelu_parts(hidden_pre):
    normal_cdf = 0.5 * (1.0 + jax.scipy.special.erf(hidden_pre * 0.7071067811865476))
    normal_pdf = jnp.exp(-0.5 * hidden_pre * hidden_pre) * 0.3989422804014327
    return (normal_cdf, normal_pdf)


def contract_rows(left, right):
    return lax.dot_general(left, right, (((0,), (0,)), ((), ())), preferred_element_type=F32)


def contract_cols(left, right):
    return lax.dot_general(left, right, (((1,), (1,)), ((), ())), preferred_element_type=F32)


def swap(values, axis, mask):
    size = lax.axis_size(axis)
    return lax.ppermute(values, axis, [(i, i ^ mask) for i in range(size)])


def exchange(values, axes):
    return lax.all_to_all(values, axes, split_axis=0, concat_axis=0, tiled=True)


def tie(*values):
    return lax.optimization_barrier(values)


def call(body, pos, grid, inputs, in_blocks, outputs, out_blocks):
    return pl.pallas_call(
        body,
        grid_spec=pltpu.PrefetchScalarGridSpec(
            num_scalar_prefetch=1,
            grid=(grid,),
            in_specs=[pl.BlockSpec(shape, index) for shape, index in in_blocks],
            out_specs=[pl.BlockSpec(shape, index) for shape, index in out_blocks],
        ),
        out_shape=[jax.ShapeDtypeStruct(shape, dtype) for shape, dtype in outputs],
        cost_estimate=pl.CostEstimate(flops=1000, bytes_accessed=1000, transcendentals=0),
        compiler_params=pltpu.CompilerParams(vmem_limit_bytes=40 * 1024 * 1024),
    )(pos, *inputs)


def gate_of(pos, lanes):
    lane = lax.broadcasted_iota(jnp.int32, lanes.shape, 1)
    return jnp.sum(jnp.where(lane == pos[2], lanes.astype(F32), 0.0), axis=1, keepdims=True)


def scale_grads(pos, received):
    slots, wide = received.shape
    width = wide - EXTRA
    half = width // 2
    rows = slots // 4

    def body(pos_ref, rec, mine, give):
        gate = gate_of(pos_ref, rec[:, width:])
        core = pos_ref[1]
        for out, which in ((mine, core), (give, 1 - core)):
            start = pl.multiple_of(which * half, half)
            out[...] = (gate * rec[:, pl.ds(start, half)].astype(F32)).astype(BF16)

    block = ((rows, half), lambda i, pos: (i, 0))
    return call(
        body,
        pos,
        4,
        [received],
        [((rows, wide), lambda i, pos: (i, 0))],
        [((slots, half), BF16)] * 2,
        [block, block],
    )


def pre_grads(pos, received, weight_out, act, slope):
    slots, wide = received.shape
    hidden, width = weight_out.shape
    step = hidden // 4

    def body(pos_ref, rec, weight, act_ref, slope_ref, grad_pre, give, gate_grad):
        i = pl.program_id(0)
        grad_act = lax.dot_general(
            rec[:, :width], weight[...], (((1,), (1,)), ((), ())), preferred_element_type=F32
        )
        gate = gate_of(pos_ref, rec[:, width:])
        part = jnp.sum(act_ref[...].astype(F32) * grad_act, axis=1, keepdims=True)
        value = (gate * grad_act * slope_ref[...]).astype(BF16)
        grad_pre[...] = value

        @pl.when(i < 2)
        def _():
            give[...] = value

        @pl.when(i == 0)
        def _():
            gate_grad[...] = part

        @pl.when(i > 0)
        def _():
            gate_grad[...] += part

    order = lambda i, pos: i ^ (2 * (1 - pos[1]))
    column = ((slots, step), lambda i, pos: (0, order(i, pos)))
    return call(
        body,
        pos,
        4,
        [received, weight_out, act, slope],
        [
            ((slots, wide), lambda i, pos: (0, 0)),
            ((step, width), lambda i, pos: (order(i, pos), 0)),
            column,
            column,
        ],
        [((slots, hidden), BF16), ((slots, hidden // 2), BF16), ((slots, 1), F32)],
        [
            column,
            ((slots, step), lambda i, pos: (0, jnp.minimum(i, 1))),
            ((slots, 1), lambda i, pos: (0, 0)),
        ],
    )


def parts(pos, left, right, own_offset, kept):
    left_mine, left_other = left
    right_mine, right_other = right
    slots = left_mine.shape[0]
    width = left_mine.shape[1] // 4
    cols = right_other.shape[1] // 2
    dtype = F32 if kept else BF16

    def mask(i):
        if kept:
            return jnp.where(i == 1, 3, jnp.where(i == 3, 1, 0))
        return jnp.where(i == 0, 1, jnp.where(i == 2, 3, 2))

    def body(pos_ref, lm, lo, rm, ro, out_a, out_b):
        dims = (((0,), (0,)), ((), ()))
        value = lax.dot_general(lm[...], rm[...], dims, preferred_element_type=F32)
        value = value + lax.dot_general(lo[...], ro[...], dims, preferred_element_type=F32)
        value = value.astype(dtype)
        i = pl.program_id(0)

        @pl.when(i < 2)
        def _():
            out_a[...] = value

        @pl.when(i >= 2)
        def _():
            out_b[...] = value

    left_block = ((slots, width), lambda i, pos: (0, pos[0] ^ mask(i)))
    return call(
        body,
        pos,
        4,
        [left_mine, left_other, right_mine, right_other],
        [
            left_block,
            left_block,
            ((slots, cols), lambda i, pos: (0, own_offset * pos[1] + i // 2)),
            ((slots, cols), lambda i, pos: (0, i // 2)),
        ],
        [((2 * width, cols), dtype)] * 2,
        [
            ((width, cols), lambda i, pos: (jnp.minimum(i, 1), 0)),
            ((width, cols), lambda i, pos: (jnp.maximum(i, 2) - 2, 0)),
        ],
    )


def slot_grads_of(pos, grad_pre, weight_in):
    slots, hidden = grad_pre.shape
    width = weight_in.shape[0]
    step = width // 4

    def body(pos_ref, grad, weight, out):
        out[...] = lax.dot_general(
            grad[...], weight[...], (((1,), (1,)), ((), ())), preferred_element_type=F32
        ).astype(BF16)

    return call(
        body,
        pos,
        4,
        [grad_pre, weight_in],
        [((slots, hidden), lambda i, pos: (0, 0)), ((step, hidden), lambda i, pos: (i, 0))],
        [((slots, width), BF16)],
        [((slots, step), lambda i, pos: (0, i))],
    )[0]


def zh_sum(near_a, near_b):
    zh = lax.axis_index("zh")
    block = near_a.shape[0] // 4

    def rows_of(r):
        return jnp.concatenate(
            [
                lax.dynamic_slice_in_dim(near, (zh ^ r) * block, block, axis=0)
                for near in (near_a, near_b)
            ],
            axis=1,
        )

    return rows_of(0), [swap(rows_of(r).astype(BF16), "zh", r) for r in (1, 2, 3)]


def zh_total(mine, got, scale):
    for piece in got:
        mine = mine + piece.astype(F32)
    return mine * scale


def core_total(mine):
    core = lax.axis_index("core")
    share = mine.shape[0] // 2
    keep = lax.dynamic_slice_in_dim(mine, core * share, share, axis=0)
    give = lax.dynamic_slice_in_dim(mine, (1 - core) * share, share, axis=0)
    got = swap(give, "core", 1)
    first = jnp.where(core == 0, keep, got)
    second = jnp.where(core == 0, got, keep)
    return jnp.concatenate([first, second], axis=1)[None]


def per_device(
    tokens, grad_out, router_weight, weight_in, weight_out, expert_ids, slot_index, keep_mask
):
    tok_rows, model_width = tokens.shape
    experts = 8
    weight_in = weight_in[0]
    weight_out = weight_out[0]
    capacity = tok_rows * expert_ids.shape[1] // experts
    slot_count = experts * capacity
    grad_scale = float(tok_rows * 256) ** (-0.5)
    core = lax.axis_index("core")
    my_y = lax.axis_index("y")

    target = expert_ids * capacity + slot_index
    slot_iota = jnp.arange(slot_count, dtype=jnp.int32)[:, None]
    first_hit = (slot_iota == target[None, :, 0]) & (keep_mask[None, :, 0] == 1)
    second_hit = (slot_iota == target[None, :, 1]) & (keep_mask[None, :, 1] == 1)
    dispatch = (first_hit | second_hit).astype(BF16)

    send_tokens = jnp.dot(dispatch, tokens, preferred_element_type=F32).astype(BF16)
    slot_tokens = exchange(
        send_tokens.reshape(experts, capacity, model_width), GROUP
    ).reshape(slot_count, model_width)

    logits = jnp.dot(tokens, router_weight, preferred_element_type=F32)
    exp_logits = jnp.exp(logits)
    router_probs = exp_logits / jnp.sum(exp_logits, axis=1, keepdims=True)
    picked = expert_ids[:, :, None] == jnp.arange(experts, dtype=jnp.int32)[None, None, :]
    chosen = jnp.sum(jnp.where(picked, router_probs[:, None, :], 0.0), axis=2)
    keep_float = keep_mask.astype(F32)
    denominator = jnp.sum(keep_float * chosen, axis=1) + (1.0 - jnp.max(keep_float, axis=1))
    combine = keep_float * chosen / denominator[:, None]
    gate_lanes = jnp.sum(jnp.where(picked, combine[:, :, None], 0.0), axis=1).astype(BF16)
    gate_lanes = jnp.pad(gate_lanes, ((0, 0), (0, EXTRA - experts)))
    send_grads = jnp.dot(dispatch, grad_out, preferred_element_type=F32).astype(BF16)
    send_gates = jnp.dot(dispatch, gate_lanes, preferred_element_type=F32).astype(BF16)
    received = exchange(
        jnp.concatenate([send_grads, send_gates], axis=1).reshape(
            experts, capacity, model_width + EXTRA
        ),
        GROUP,
    ).reshape(slot_count, model_width + EXTRA)
    other_tokens = swap(slot_tokens, "core", 1)
    hidden_pre = jnp.dot(slot_tokens, weight_in, preferred_element_type=F32)
    normal_cdf, normal_pdf = gelu_parts(hidden_pre)
    hidden_act = (hidden_pre * normal_cdf).astype(BF16)
    act_slope = normal_cdf + hidden_pre * normal_pdf
    other_act = swap(hidden_act, "core", 1)
    left_in = (slot_tokens, other_tokens)
    left_out = (hidden_act, other_act)
    pos = jnp.stack([my_y, core, lax.axis_index(GROUP)]).astype(jnp.int32)

    received, left_in, left_out, act_slope = tie(received, left_in, left_out, act_slope)
    my_out, give_out = scale_grads(pos, received)
    other_out = swap(give_out, "core", 1)
    received, _ = tie(received, give_out)
    grad_pre, give_in, slot_combine_grad = pre_grads(
        pos, received, weight_out, hidden_act, act_slope
    )
    other_in = swap(give_in, "core", 1)
    flat_combine = exchange(
        slot_combine_grad.astype(BF16).reshape(experts, capacity), GROUP
    ).reshape(slot_count)

    send_out_a, send_out_b = parts(pos, left_out, (my_out, other_out), 0, False)
    got_out_a, got_out_b = swap(send_out_a, "y", 1), swap(send_out_b, "y", 3)
    grad_pre, _ = tie(grad_pre, send_out_a)
    send_in_a, send_in_b = parts(pos, left_in, (grad_pre, other_in), 2, False)
    got_in_a, got_in_b = swap(send_in_a, "y", 1), swap(send_in_b, "y", 3)

    grad_pre, _ = tie(grad_pre, send_in_a)
    grad_slots = slot_grads_of(pos, grad_pre, weight_in)
    grad_slots, flat_combine = tie(grad_slots, flat_combine)
    flat_grads = exchange(
        grad_slots.reshape(experts, capacity, model_width), GROUP
    ).reshape(slot_count, model_width)

    my_out, grad_pre, flat_combine, _ = tie(my_out, grad_pre, flat_combine, grad_slots)
    keep_out_a, keep_out_b = parts(pos, left_out, (my_out, other_out), 0, True)
    grad_pre, _ = tie(grad_pre, keep_out_a)
    keep_in_a, keep_in_b = parts(pos, left_in, (grad_pre, other_in), 2, True)
    flat_combine, _ = tie(flat_combine, keep_in_a)

    combine_wide = flat_combine.astype(F32)[:, None]
    combine_grad = jnp.stack(
        [
            jnp.sum(jnp.where(first_hit, combine_wide, 0.0), axis=0),
            jnp.sum(jnp.where(second_hit, combine_wide, 0.0), axis=0),
        ],
        axis=1,
    )
    weighted_sum = jnp.sum(combine_grad * combine, axis=1)
    chosen_grad = keep_float * (combine_grad - weighted_sum[:, None]) / denominator[:, None]
    probs_grad = jnp.sum(jnp.where(picked, chosen_grad[:, :, None], 0.0), axis=1)
    logit_grad = router_probs * (
        probs_grad - jnp.sum(probs_grad * router_probs, axis=1, keepdims=True)
    )
    logit_b = logit_grad.astype(BF16)

    def router_steps(value, steps):
        for axis, mask in steps:
            value = value + swap(value, axis, mask)
        return value

    router_part = contract_rows(logit_b, tokens) * grad_scale

    def far_of(keep, got):
        rows = keep.shape[0] // 2
        return (keep[rows:] + got[rows:].astype(F32)).astype(BF16)

    def near_of(keep, got, got_far):
        rows = keep.shape[0] // 2
        return keep[:rows] + got[:rows].astype(F32) + got_far.astype(F32)

    got_out_a, got_out_b, _ = tie(got_out_a, got_out_b, router_part)
    far_a, far_b = far_of(keep_out_a, got_out_a), far_of(keep_out_b, got_out_b)
    far_out_a, far_out_b = swap(far_a, "y", 3), swap(far_b, "y", 1)

    got_in_a, got_in_b, _, _ = tie(got_in_a, got_in_b, far_a, far_b)
    far_a, far_b = far_of(keep_in_a, got_in_a), far_of(keep_in_b, got_in_b)
    far_in_a, far_in_b = swap(far_a, "y", 3), swap(far_b, "y", 1)
    router_part, _, _ = tie(router_part, far_a, far_b)
    router_part = router_steps(router_part, ROUTER_STEPS[:1])

    far_out_a, far_out_b, _ = tie(far_out_a, far_out_b, router_part)
    near_a = near_of(keep_out_a, got_out_a, far_out_a)
    near_b = near_of(keep_out_b, got_out_b, far_out_b)
    mine_out, zh_out = zh_sum(near_a, near_b)
    flat_grads, _, _ = tie(flat_grads, near_a, near_b)

    expert_grad = contract_rows(dispatch, flat_grads)
    grad_tokens = (expert_grad + contract_cols(logit_b, router_weight)).astype(BF16)
    router_part, _ = tie(router_part, grad_tokens)
    router_part = router_steps(router_part, ROUTER_STEPS[1:2])

    far_in_a, far_in_b, _ = tie(far_in_a, far_in_b, router_part)
    near_a = near_of(keep_in_a, got_in_a, far_in_a)
    near_b = near_of(keep_in_b, got_in_b, far_in_b)
    mine_in, zh_in = zh_sum(near_a, near_b)
    router_part, _, _ = tie(router_part, near_a, near_b)
    router_part = router_steps(router_part, ROUTER_STEPS[2:5])

    mine_out, zh_out, _ = tie(mine_out, zh_out, router_part)
    mine_out = zh_total(mine_out, zh_out, grad_scale)
    router_part, _ = tie(router_part, mine_out)
    router_part = router_steps(router_part, ROUTER_STEPS[5:6])
    mine_in, zh_in, _ = tie(mine_in, zh_in, router_part)
    mine_in = zh_total(mine_in, zh_in, grad_scale)
    router_part, _ = tie(router_part, mine_in)
    router_part = router_steps(router_part, ROUTER_STEPS[6:])
    return (grad_tokens, router_part.T, core_total(mine_in), core_total(mine_out))


def solution(mesh):
    fine = Mesh(mesh.devices.reshape(FINE_SHAPE), FINE)
    placed = (
        P(FINE, None),
        P(FINE, None),
        P(),
        P(GROUP, None, None),
        P(GROUP, None, None),
        P(FINE, None),
        P(FINE, None),
        P(FINE, None),
    )
    return jax.shard_map(
        per_device,
        mesh=fine,
        in_specs=placed,
        out_specs=(
            P(FINE, None),
            P(),
            P(GROUP, ("y", "zh", "core"), None),
            P(GROUP, ("y", "zh", "core"), None),
        ),
        check_vma=False,
    )
```

time: 212 us -> 224 us (1.057)
  matrix products: 50.9 us -> 15 us
  Pallas kernels: 0 us -> 31.7 us
  waiting for transfers between devices: 71.4 us -> 85.5 us
  blocking collectives: 0 us -> 9 us
  starting transfers between devices: 58.6 us -> 53.4 us
  other arithmetic: 18.7 us -> 13.7 us
  local copies, waits for them, and re-layouts: 9.35 us -> 11.9 us
    pallas_call x0 -> x7, Pallas kernels: none -> 31.7 us  [call(): pl.pallas_call(body, grid_spec=pltpu.PrefetchScalarGridSpec(num_scalar_pr...]
    dot_general x14 -> x2, matrix products: 28.9 us -> 2.61 us  [contract_rows(): lax.dot_general(left, right, (((0,), (0,)), ((), ())), preferred_element_...]
    all_to_all x4 -> x3, waiting for transfers between devices: 28.7 us -> 39.5 us  [exchange(): return lax.all_to_all(values, axes, split_axis=0, concat_axis=0, tiled=True)]
    dot_general x3 -> x1, matrix products: 10.9 us -> 1.45 us  [contract_cols(): lax.dot_general(left, right, (((1,), (1,)), ((), ())), preferred_element_...]
    all_to_all x0 -> x1, blocking collectives: none -> 9 us  [exchange(): return lax.all_to_all(values, axes, split_axis=0, concat_axis=0, tiled=True)]
    concatenate x4 -> x8, other arithmetic: 7.61 us -> 0.1 us  [rows_of(): jnp.concatenate([lax.dynamic_slice_in_dim(near, (zh ^ r) * block, block,...]
    unnamed x46 -> x80, local copies, waits for them, and re-layouts: 4.17 us -> 11.5 us
    all_to_all x4 -> x3, starting transfers between devices: 21.9 us -> 17.3 us  [exchange(): return lax.all_to_all(values, axes, split_axis=0, concat_axis=0, tiled=True)]
  transfers between devices with their start and end apart: 32 -> 31, of which waited for: 18 -> 11; matrix products, arithmetic and copies ran while one was open for 29% -> 11% of each run, Pallas kernels for 0% -> 9%
where the time goes in v3:
time: 224 us; the launch traced here: 222 us
  waiting for transfers between devices  85.5 us (38%)
  starting transfers between devices  53.4 us (24%)
  Pallas kernels  31.7 us (14%)
  matrix products  15 us (7%)
  other arithmetic  13.7 us (6%)
  local copies, waits for them, and re-layouts  11.9 us (5%)
  blocking collectives  9 us (4%)
    ppermute x28, waiting for transfers between devices, swap(): return lax.ppermute(values, axis, [(i, i ^ mask) for i in range(size)])  46 us
    all_to_all x3, waiting for transfers between devices, exchange(): return lax.all_to_all(values, axes, split_axis=0, concat_axis=0, tiled=True)  39.5 us
    ppermute x28, starting transfers between devices, swap(): return lax.ppermute(values, axis, [(i, i ^ mask) for i in range(size)])  36.1 us
    pallas_call x7, Pallas kernels, call(): pl.pallas_call(body, grid_spec=pltpu.PrefetchScalarGridSpec(num_scalar_pr...  31.7 us
    all_to_all x3, starting transfers between devices, exchange(): return lax.all_to_all(values, axes, split_axis=0, concat_axis=0, tiled=True)  17.3 us
    unnamed x80, local copies, waits for them, and re-layouts  11.5 us
    all_to_all x1, blocking collectives, exchange(): return lax.all_to_all(values, axes, split_axis=0, concat_axis=0, tiled=True)  9 us
    dot_general x1, matrix products, per_device(): hidden_pre = jnp.dot(slot_tokens, weight_in, preferred_element_type=F32)  7.44 us
  transfers between devices with their start and end apart: 31, of which 11 were waited for; matrix products, arithmetic and copies ran while one was open for 11% of the time, Pallas kernels for 9%

profile of v3, /device:TPU:2, one launch (start us, length us, event | category | flops | bytes accessed | tf_op | source)
XLA Modules:
  0.0 221.7 jit_solution(8286421795659820885)
XLA Ops:
  0.6 0.8 multiply_add_fusion
  1.4 0.8 compare_reduce_fusion.1
  2.2 2.1 convolution_convert_fusion
  4.3 6.3 %all-to-all-start.1 = ((bf16[8,64,2048]{2,1,0:T(8,128)(2,1)}), bf16[8,64,2048]{2,1,0:T(8,128)(2,1)S(1)}, u32[]{:S(2)}, u32[]{:S(2)}) async-start(bf16[8,64,2048]{2,1,0:T(8,128)(2,1)} %bitcast.45), calls=%async_computation.1 | async-start | bytes 4194304 | tf_op jit(solution)/shard_map/all_to_all | solution.py:46
  11.9 0.8 convolution_convert_fusion.1
  12.6 1.6 pad_maximum_fusion
  14.3 21.6 %all-to-all-done.1 = bf16[8,64,2048]{2,1,0:T(8,128)(2,1)S(1)} async-done(((bf16[8,64,2048]{2,1,0:T(8,128)(2,1)}), bf16[8,64,2048]{2,1,0:T(8,128)(2,1)S(1)}, u32[]{:S(2)}, u32[]{:S(2)}) %all-to-all-start.1) | async-done | bytes 2097184 | tf_op jit(solution)/shard_map/all_to_all | solution.py:46
  35.9 1.3 copy-done.1
  37.2 5.3 %all-to-all-start = ((bf16[8,64,2176]{2,1,0:T(8,128)(2,1)}), bf16[8,64,2176]{2,1,0:T(8,128)(2,1)S(1)}, u32[]{:S(2)}, u32[]{:S(2)}) async-start(bf16[8,64,2176]{2,1,0:T(8,128)(2,1)} %bitcast.44), calls=%async_computation | async-start | bytes 4456448 | tf_op jit(solution)/shard_map/all_to_all | solution.py:46
  42.5 7.4 %fusion.4 = (f32[512,1024]{1,0:T(8,128)}, bf16[512,1024]{1,0:T(8,128)(2,1)}) fusion(bf16[512,2048]{1,0:T(8,128)(2,1)} %bitcast.38, bf16[1,2048,1024]{2,1,0:T(8,128)(2,1)} %param.11), kind=kOutput, calls=%fused_computation.10 | convolution fusion | flops 2152726528 | bytes 9437184 | tf_op jit(solution)/shard_map/dot_general | solution.py:292
  50.5 17.9 %all-to-all-done = bf16[8,64,2176]{2,1,0:T(8,128)(2,1)S(1)} async-done(((bf16[8,64,2176]{2,1,0:T(8,128)(2,1)}), bf16[8,64,2176]{2,1,0:T(8,128)(2,1)S(1)}, u32[]{:S(2)}, u32[]{:S(2)}) %all-to-all-start) | async-done | bytes 2228256 | tf_op jit(solution)/shard_map/all_to_all | solution.py:46
  68.5 2.5 %shard_map.111 = (bf16[512,1024]{1,0:T(8,128)(2,1)S(1)}, bf16[512,1024]{1,0:T(8,128)(2,1)}) custom-call(s32[3]{0:T(128)S(1)} %pad_add_fusion.pos_ref, bf16[512,2176]{1,0:T(8,128)(2,1)S(1)} %bitcast.35), custom_call_target="tpu_custom_call" | custom-call | flops 1000 | bytes 1000 | tf_op jit(solution)/shard_map/pallas_call | solution.py:54
  71.0 1.0 copy-done.7
  72.1 2.2 copy-done.10
  74.2 6.0 %shard_map.112 = (bf16[512,1024]{1,0:T(8,128)(2,1)S(1)}, bf16[512,512]{1,0:T(8,128)(2,1)}, f32[512,1]{1,0:T(8,128)S(1)}) custom-call(s32[3]{0:T(128)S(1)} %pad_add_fusion.pos_ref, bf16[512,2176]{1,0:T(8,128)(2,1)S(1)} %bitcast.36, bf16[1024,2048]{1,0:T(8,128)(2,1)S(1)} %bitcast.42, bf16[512,1024]{1,0:T(8,128)(2,1)} %get-tuple-element.60.act_ref.lm, ...), custom_call_target="tpu_custom_call" | custom-call | flops 1000 | bytes 1000 | tf_op jit(solution)/shard_map/pallas_call | solution.py:54
  80.2 1.0 copy-done.3
  81.9 9.0 %all_to_all.25 = bf16[8,1,64]{2,1,0:T(2,128)(2,1)S(1)} all-to-all(bf16[8,1,64]{2,1,0:T(2,128)(2,1)S(1)} %all_to_all.20), channel_id=1, replica_groups=mesh['y'=4,'zh'=4,'core'=2,'x'=4,'zl'=2] {'x','zl'}, dimensions={0} | all-to-all | bytes 2048 | tf_op jit(solution)/shard_map/all_to_all | solution.py:46
  91.0 1.2 copy-done.8
  92.3 5.0 %shard_map.113 = (bf16[512,512]{1,0:T(8,128)(2,1)S(1)}, bf16[512,512]{1,0:T(8,128)(2,1)S(1)}) custom-call(s32[3]{0:T(128)S(1)} %pad_add_fusion.pos_ref, bf16[512,1024]{1,0:T(8,128)(2,1)} %get-tuple-element.60.act_ref.lm, bf16[512,1024]{1,0:T(8,128)(2,1)} %collective-permute-done.1.lo, bf16[512,1024]{1,0:T(8,128)(2,1)S(1)} %copy-done.8, ...), custom_call_target="tpu_custom_call" | custom-call | flops 1000 | bytes 1000 | tf_op jit(solution)/shard_map/pallas_call | solution.py:54
  97.3 0.8 copy-done.24
  98.1 0.8 copy-done.26
  98.9 4.9 %shard_map.114 = (bf16[1024,256]{1,0:T(8,128)(2,1)S(1)}, bf16[1024,256]{1,0:T(8,128)(2,1)S(1)}) custom-call(s32[3]{0:T(128)S(1)} %pad_add_fusion.pos_ref, bf16[512,2048]{1,0:T(8,128)(2,1)S(1)} %bitcast.39, bf16[512,2048]{1,0:T(8,128)(2,1)} %collective-permute-done.lo, bf16[512,1024]{1,0:T(8,128)(2,1)S(1)} %copy-done.4, ...), custom_call_target="tpu_custom_call" | custom-call | flops 1000 | bytes 1000 | tf_op jit(solution)/shard_map/pallas_call | solution.py:54
  103.9 3.7 %shard_map.115 = bf16[512,2048]{1,0:T(8,128)(2,1)S(1)} custom-call(s32[3]{0:T(128)S(1)} %pad_add_fusion.pos_ref, bf16[512,1024]{1,0:T(8,128)(2,1)S(1)} %copy-done.4, bf16[2048,1024]{1,0:T(8,128)(2,1)S(1)} %bitcast.43), custom_call_target="tpu_custom_call" | custom-call | flops 1000 | bytes 1000 | tf_op jit(solution)/shard_map/pallas_call | solution.py:54
  107.6 1.3 copy-done.6
  108.9 5.7 %all-to-all-start.3 = ((bf16[8,64,2048]{2,1,0:T(8,128)(2,1)}), bf16[8,64,2048]{2,1,0:T(8,128)(2,1)}, u32[]{:S(2)}, u32[]{:S(2)}) async-start(bf16[8,64,2048]{2,1,0:T(8,128)(2,1)} %bitcast.41), calls=%async_computation.3 | async-start | bytes 4194304 | tf_op jit(solution)/shard_map/all_to_all | solution.py:46
  114.6 1.6 collective-permute-start.4
  116.6 1.2 copy-done.9
  117.9 4.6 %shard_map.116 = (f32[512,512]{1,0:T(8,128)S(1)}, f32[512,512]{1,0:T(8,128)S(1)}) custom-call(s32[3]{0:T(128)S(1)} %pad_add_fusion.pos_ref, bf16[512,1024]{1,0:T(8,128)(2,1)} %get-tuple-element.60.act_ref.lm, bf16[512,1024]{1,0:T(8,128)(2,1)} %collective-permute-done.1.lo, bf16[512,1024]{1,0:T(8,128)(2,1)S(1)} %copy-done.9, ...), custom_call_target="tpu_custom_call" | custom-call | flops 1000 | bytes 1000 | tf_op jit(solution)/shard_map/pallas_call | solution.py:54
  122.5 5.0 %shard_map.117 = (f32[1024,256]{1,0:T(8,128)S(1)}, f32[1024,256]{1,0:T(8,128)S(1)}) custom-call(s32[3]{0:T(128)S(1)} %pad_add_fusion.pos_ref, bf16[512,2048]{1,0:T(8,128)(2,1)S(1)} %bitcast.40, bf16[512,2048]{1,0:T(8,128)(2,1)} %collective-permute-done.lo, bf16[512,1024]{1,0:T(8,128)(2,1)S(1)} %copy-done.5, bf16[512,512]{1,0:T(8,128)(2,1)} %collective-permute-done.3.ro), custom_call_target="tpu_custom_call" | custom-call | flops 1000 | bytes 1000 | tf_op jit(solution)/shard_map/pallas_call | solution.py:54
  127.6 3.1 %collective-permute-start.5 = (bf16[512,512]{1,0:T(8,128)(2,1)S(1)}, bf16[512,512]{1,0:T(8,128)(2,1)S(1)}, u32[]{:S(2)}, u32[]{:S(2)}) collective-permute-start(bf16[512,512]{1,0:T(8,128)(2,1)S(1)} %copy-done.25), channel_id=1, source_target_pairs={{0,192},{64,128},{128,64},{192,0},{1,193},{65,129},{129,65},{193,1... | collective-permute-start | bytes 1572872 | tf_op jit(solution)/shard_map/ppermute | solution.py:42
  131.7 12.1 %collective-permute-done.5 = bf16[512,512]{1,0:T(8,128)(2,1)S(1)} collective-permute-done((bf16[512,512]{1,0:T(8,128)(2,1)S(1)}, bf16[512,512]{1,0:T(8,128)(2,1)S(1)}, u32[]{:S(2)}, u32[]{:S(2)}) %collective-permute-start.5) | collective-permute-done | bytes 524320 | tf_op jit(solution)/shard_map/ppermute | solution.py:42
  143.8 0.9 add_convert_fusion.2
  145.1 0.8 add_convert_fusion.3
  145.8 2.6 %collective-permute-start.6 = (bf16[256,512]{1,0:T(8,128)(2,1)}, bf16[256,512]{1,0:T(8,128)(2,1)}, u32[]{:S(2)}, u32[]{:S(2)}) collective-permute-start(bf16[256,512]{1,0:T(8,128)(2,1)} %add_convert_fusion.3), channel_id=1, source_target_pairs={{0,192},{64,128},{128,64},{192,0},{1,193},{65,129},{129,65},{193,1... | collective-permute-start | bytes 786440 | tf_op jit(solution)/shard_map/ppermute | solution.py:42
  148.5 6.3 %collective-permute-done.9 = bf16[1024,256]{1,0:T(8,128)(2,1)S(1)} collective-permute-done((bf16[1024,256]{1,0:T(8,128)(2,1)S(1)}, bf16[1024,256]{1,0:T(8,128)(2,1)S(1)}, u32[]{:S(2)}, u32[]{:S(2)}) %collective-permute-start.9) | collective-permute-done | bytes 524320 | tf_op jit(solution)/shard_map/ppermute | solution.py:42
  154.8 0.8 add_convert_fusion.1
  155.6 0.8 add_convert_fusion
  156.9 2.7 %collective-permute-start.12 = (bf16[512,256]{1,0:T(8,128)(2,1)}, bf16[512,256]{1,0:T(8,128)(2,1)}, u32[]{:S(2)}, u32[]{:S(2)}) collective-permute-start(bf16[512,256]{1,0:T(8,128)(2,1)} %add_convert_fusion.1), channel_id=1, source_target_pairs={{0,192},{64,128},{128,64},{192,0},{1,193},{65,129},{129,65},{193,1... | collective-permute-start | bytes 786440 | tf_op jit(solution)/shard_map/ppermute | solution.py:42
  159.6 0.8 add.160
  160.5 1.3 convert_add_fusion.2
  162.0 5.5 %collective-permute-start.19 = (bf16[64,1024]{1,0:T(8,128)(2,1)S(1)}, bf16[64,1024]{1,0:T(8,128)(2,1)S(1)}, u32[]{:S(2)}, u32[]{:S(2)}) collective-permute-start(bf16[64,1024]{1,0:T(8,128)(2,1)S(1)} %pad_maximum_fusion.5), channel_id=1, source_target_pairs={{0,48},{16,32},{32,16},{48,0},{1,49},{17,33},{33,17},{49,1},{2,50}... | collective-permute-start | bytes 393224 | tf_op jit(solution)/shard_map/ppermute | solution.py:42
  167.5 1.5 collective-permute-start.18
  169.1 2.4 %fusion.13 = f32[256,2048]{1,0:T(8,128)S(1)} fusion(bf16[512,2048]{1,0:T(8,128)(2,1)} %bitcast.12, s32[256]{0:T(256)S(1)} %bitcast.55, s32[256]{0:T(256)S(1)} %bitcast.50, pred[256]{0:T(512)(128)(4,1)S(1)} %copy-done.39, pred[256]{0:T(512)(128)(4,1)S(1)} %get-tuple-element.108), kind=kOutput, calls=%fused_computation.89 | convolution fusion | flops 537526272 | bytes 4196864 | tf_op jit(solution)/shard_map/dot_general | solution.py:33
  171.5 1.4 fusion
  173.5 3.7 %collective-permute-done.11 = f32[8,2048]{1,0:T(8,128)S(1)} collective-permute-done((f32[8,2048]{1,0:T(8,128)S(1)}, f32[8,2048]{1,0:T(8,128)S(1)}, u32[]{:S(2)}, u32[]{:S(2)}) %collective-permute-start.11) | collective-permute-done | bytes 65568 | tf_op jit(solution)/shard_map/ppermute | solution.py:42
  177.2 0.9 collective-permute-start.17
  178.2 1.0 convert_add_fusion
  179.3 1.0 convert_add_fusion.1
  180.4 1.6 collective-permute-start.14
  182.0 4.2 %collective-permute-start.23 = (bf16[128,512]{1,0:T(8,128)(2,1)S(1)}, bf16[128,512]{1,0:T(8,128)(2,1)S(1)}, u32[]{:S(2)}, u32[]{:S(2)}) collective-permute-start(bf16[128,512]{1,0:T(8,128)(2,1)S(1)} %pad_maximum_fusion.8), channel_id=1, source_target_pairs={{0,48},{16,32},{32,16},{48,0},{1,49},{17,33},{33,17},{49,1},{2,50}... | collective-permute-start | bytes 393224 | tf_op jit(solution)/shard_map/ppermute | solution.py:42
  186.2 1.6 collective-permute-start.15
  187.8 3.5 %collective-permute-done.15 = f32[8,2048]{1,0:T(8,128)S(1)} collective-permute-done((f32[8,2048]{1,0:T(8,128)S(1)}, f32[8,2048]{1,0:T(8,128)S(1)}, u32[]{:S(2)}, u32[]{:S(2)}) %collective-permute-start.15) | collective-permute-done | bytes 65568 | tf_op jit(solution)/shard_map/ppermute | solution.py:42
  191.4 1.4 collective-permute-start.16
  192.8 2.9 %collective-permute-done.16 = f32[8,2048]{1,0:T(8,128)S(1)} collective-permute-done((f32[8,2048]{1,0:T(8,128)S(1)}, f32[8,2048]{1,0:T(8,128)S(1)}, u32[]{:S(2)}, u32[]{:S(2)}) %collective-permute-start.16) | collective-permute-done | bytes 65568 | tf_op jit(solution)/shard_map/ppermute | solution.py:42
  195.7 2.8 %collective-permute-start.22 = (bf16[128,512]{1,0:T(8,128)(2,1)S(1)}, bf16[128,512]{1,0:T(8,128)(2,1)S(1)}, u32[]{:S(2)}, u32[]{:S(2)}) collective-permute-start(bf16[128,512]{1,0:T(8,128)(2,1)S(1)} %pad_maximum_fusion.7), channel_id=1, source_target_pairs={{0,32},{16,48},{32,0},{48,16},{1,33},{17,49},{33,1},{49,17},{2,34}... | collective-permute-start | bytes 393224 | tf_op jit(solution)/shard_map/ppermute | solution.py:42
  198.5 1.9 collective-permute-start.21
  200.5 1.2 collective-permute-start.20
  201.8 4.2 %collective-permute-done.20 = f32[8,2048]{1,0:T(8,128)S(1)} collective-permute-done((f32[8,2048]{1,0:T(8,128)S(1)}, f32[8,2048]{1,0:T(8,128)S(1)}, u32[]{:S(2)}, u32[]{:S(2)}) %collective-permute-start.20) | collective-permute-done | bytes 65568 | tf_op jit(solution)/shard_map/ppermute | solution.py:42
  206.1 3.2 %collective-permute-done.21 = bf16[128,512]{1,0:T(8,128)(2,1)S(1)} collective-permute-done((bf16[128,512]{1,0:T(8,128)(2,1)S(1)}, bf16[128,512]{1,0:T(8,128)(2,1)S(1)}, u32[]{:S(2)}, u32[]{:S(2)}) %collective-permute-start.21) | collective-permute-done | bytes 131104 | tf_op jit(solution)/shard_map/ppermute | solution.py:42
  209.6 5.0 %collective-permute-done.24 = f32[8,2048]{1,0:T(8,128)S(1)} collective-permute-done((f32[8,2048]{1,0:T(8,128)S(1)}, f32[8,2048]{1,0:T(8,128)S(1)}, u32[]{:S(2)}, u32[]{:S(2)}) %collective-permute-start.24) | collective-permute-done | bytes 65568 | tf_op jit(solution)/shard_map/ppermute | solution.py:42
  214.8 0.7 maximum_bitcast_fusion.1
  215.5 0.7 maximum_bitcast_fusion
  216.2 4.8 %collective-permute-done.25 = f32[8,2048]{1,0:T(8,128)S(1)} collective-permute-done((f32[8,2048]{1,0:T(8,128)S(1)}, f32[8,2048]{1,0:T(8,128)S(1)}, u32[]{:S(2)}, u32[]{:S(2)}) %collective-permute-start.25) | collective-permute-done | bytes 65568 | tf_op jit(solution)/shard_map/ppermute | solution.py:42
  221.1 0.6 add_bitcast_fusion
  (155 shorter events, 6.4 us)
Async XLA Ops:
  0.6 1.6 copy-start
  2.2 128.5 %copy-start.38 = (pred[256]{0:T(512)(128)(4,1)}, pred[256]{0:T(512)(128)(4,1)S(1)}, u32[]{:S(2)}) copy-start(pred[256]{0:T(512)(128)(4,1)S(1)} %get-tuple-element.109) | copy-start | bytes 772
  4.3 6.3 %copy-start.34 = (bf16[2048,8]{0,1:T(8,128)(2,1)S(1)}, bf16[2048,8]{0,1:T(8,128)(2,1)}, u32[]{:S(2)}) copy-start(bf16[2048,8]{0,1:T(8,128)(2,1)} %param.10) | copy-start | bytes 98308
  4.3 6.8 %copy-start.37 = (s32[256,2]{0,1:T(2,128)S(1)}, s32[256,2]{0,1:T(2,128)}, u32[]{:S(2)}) copy-start(s32[256,2]{0,1:T(2,128)} %param.13) | copy-start | bytes 6148
  4.3 6.8 %copy-start.36 = (s32[256,2]{0,1:T(2,128)S(1)}, s32[256,2]{0,1:T(2,128)}, u32[]{:S(2)}) copy-start(s32[256,2]{0,1:T(2,128)} %param.15) | copy-start | bytes 6148
  4.3 31.5 %all-to-all-start.1 = ((bf16[8,64,2048]{2,1,0:T(8,128)(2,1)}), bf16[8,64,2048]{2,1,0:T(8,128)(2,1)S(1)}, u32[]{:S(2)}, u32[]{:S(2)}) async-start(bf16[8,64,2048]{2,1,0:T(8,128)(2,1)} %bitcast.45), calls=%async_computation.1 | async-start | bytes 4194304 | tf_op jit(solution)/shard_map/all_to_all | solution.py:46
  35.9 1.3 copy-start.1
  37.2 31.3 %all-to-all-start = ((bf16[8,64,2176]{2,1,0:T(8,128)(2,1)}), bf16[8,64,2176]{2,1,0:T(8,128)(2,1)S(1)}, u32[]{:S(2)}, u32[]{:S(2)}) async-start(bf16[8,64,2176]{2,1,0:T(8,128)(2,1)} %bitcast.44), calls=%async_computation | async-start | bytes 4456448 | tf_op jit(solution)/shard_map/all_to_all | solution.py:46
  42.5 26.0 %collective-permute-start = (bf16[512,2048]{1,0:T(8,128)(2,1)}, bf16[512,2048]{1,0:T(8,128)(2,1)}, u32[]{:S(2)}, u32[]{:S(2)}) collective-permute-start(bf16[512,2048]{1,0:T(8,128)(2,1)} %bitcast.37), channel_id=1, source_target_pairs={{0,8},{8,0},{1,9},{9,1},{2,10},{10,2},{3,11},{11,3},{4,12},{12,4},... | collective-permute-start | bytes 6291464 | tf_op jit(solution)/shard_map/ppermute | solution.py:42
  49.9 18.5 %collective-permute-start.1 = (bf16[512,1024]{1,0:T(8,128)(2,1)}, bf16[512,1024]{1,0:T(8,128)(2,1)}, u32[]{:S(2)}, u32[]{:S(2)}) collective-permute-start(bf16[512,1024]{1,0:T(8,128)(2,1)} %get-tuple-element.60.act_ref.lm), channel_id=1, source_target_pairs={{0,8},{8,0},{1,9},{9,1},{2,10},{10,2},{3,11},{11,3},{4,12},{12,4},... | collective-permute-start | bytes 3145736 | tf_op jit(solution)/shard_map/ppermute | solution.py:42
  68.4 3.6 %copy-start.12 = (f32[512,1024]{1,0:T(8,128)S(1)}, f32[512,1024]{1,0:T(8,128)}, u32[]{:S(2)}) copy-start(f32[512,1024]{1,0:T(8,128)} %get-tuple-element.58.slope_ref) | copy-start | bytes 6291460
  72.0 19.0 %collective-permute-start.2 = (bf16[512,1024]{1,0:T(8,128)(2,1)}, bf16[512,1024]{1,0:T(8,128)(2,1)}, u32[]{:S(2)}, u32[]{:S(2)}) collective-permute-start(bf16[512,1024]{1,0:T(8,128)(2,1)} %get-tuple-element.56), channel_id=1, source_target_pairs={{0,8},{8,0},{1,9},{9,1},{2,10},{10,2},{3,11},{11,3},{4,12},{12,4},... | collective-permute-start | bytes 3145736 | tf_op jit(solution)/shard_map/ppermute | solution.py:42
  72.1 2.2 copy-start.10
  81.2 17.7 %collective-permute-start.3 = (bf16[512,512]{1,0:T(8,128)(2,1)}, bf16[512,512]{1,0:T(8,128)(2,1)}, u32[]{:S(2)}, u32[]{:S(2)}) collective-permute-start(bf16[512,512]{1,0:T(8,128)(2,1)} %get-tuple-element.67), channel_id=1, source_target_pairs={{0,8},{8,0},{1,9},{9,1},{2,10},{10,2},{3,11},{11,3},{4,12},{12,4},... | collective-permute-start | bytes 1572872 | tf_op jit(solution)/shard_map/ppermute | solution.py:42
  92.3 6.7 %copy-start.2 = (bf16[8,64,2048]{2,1,0:T(8,128)(2,1)S(1)}, bf16[8,64,2048]{2,1,0:T(8,128)(2,1)}, u32[]{:S(2)}) copy-start(bf16[8,64,2048]{2,1,0:T(8,128)(2,1)} %copy-done.1) | copy-start | bytes 6291460
  92.3 6.7 %copy-start.4 = (bf16[512,1024]{1,0:T(8,128)(2,1)S(1)}, bf16[512,1024]{1,0:T(8,128)(2,1)}, u32[]{:S(2)}) copy-start(bf16[512,1024]{1,0:T(8,128)(2,1)} %copy-done.3) | copy-start | bytes 3145732
  98.9 4.9 %copy-start.11 = (bf16[1,2048,1024]{2,1,0:T(8,128)(2,1)S(1)}, bf16[1,2048,1024]{2,1,0:T(8,128)(2,1)}, u32[]{:S(2)}) copy-start(bf16[1,2048,1024]{2,1,0:T(8,128)(2,1)} %param.11) | copy-start | bytes 12582916
  103.9 3.7 %copy-start.21 = (bf16[1024,256]{1,0:T(8,128)(2,1)}, bf16[1024,256]{1,0:T(8,128)(2,1)S(1)}, u32[]{:S(2)}) copy-start(bf16[1024,256]{1,0:T(8,128)(2,1)S(1)} %get-tuple-element.84) | copy-start | bytes 1572868
  103.9 3.7 %copy-start.23 = (bf16[1024,256]{1,0:T(8,128)(2,1)}, bf16[1024,256]{1,0:T(8,128)(2,1)S(1)}, u32[]{:S(2)}) copy-start(bf16[1024,256]{1,0:T(8,128)(2,1)S(1)} %get-tuple-element.68) | copy-start | bytes 1572868
  107.6 1.4 copy-start.6
  108.9 60.1 %all-to-all-start.3 = ((bf16[8,64,2048]{2,1,0:T(8,128)(2,1)}), bf16[8,64,2048]{2,1,0:T(8,128)(2,1)}, u32[]{:S(2)}, u32[]{:S(2)}) async-start(bf16[8,64,2048]{2,1,0:T(8,128)(2,1)} %bitcast.41), calls=%async_computation.3 | async-start | bytes 4194304 | tf_op jit(solution)/shard_map/all_to_all | solution.py:46
  114.6 7.9 %copy-start.5 = (bf16[512,1024]{1,0:T(8,128)(2,1)S(1)}, bf16[512,1024]{1,0:T(8,128)(2,1)}, u32[]{:S(2)}) copy-start(bf16[512,1024]{1,0:T(8,128)(2,1)} %copy-done.3) | copy-start | bytes 3145732
  114.6 17.0 %collective-permute-start.4 = (bf16[512,512]{1,0:T(8,128)(2,1)}, bf16[512,512]{1,0:T(8,128)(2,1)S(1)}, u32[]{:S(2)}, u32[]{:S(2)}) collective-permute-start(bf16[512,512]{1,0:T(8,128)(2,1)} %copy-done.26), channel_id=1, source_target_pairs={{0,64},{64,0},{128,192},{192,128},{1,65},{65,1},{129,193},{193,129... | collective-permute-start | bytes 1572872 | tf_op jit(solution)/shard_map/ppermute | solution.py:42
  116.2 32.3 %collective-permute-start.8 = (bf16[1024,256]{1,0:T(8,128)(2,1)}, bf16[1024,256]{1,0:T(8,128)(2,1)S(1)}, u32[]{:S(2)}, u32[]{:S(2)}) collective-permute-start(bf16[1024,256]{1,0:T(8,128)(2,1)} %copy-done.23), channel_id=1, source_target_pairs={{0,64},{64,0},{128,192},{192,128},{1,65},{65,1},{129,193},{193,129... | collective-permute-start | bytes 1572872 | tf_op jit(solution)/shard_map/ppermute | solution.py:42
  122.5 21.3 %copy-start.19 = (f32[512,512]{1,0:T(8,128)}, f32[512,512]{1,0:T(8,128)S(1)}, u32[]{:S(2)}) copy-start(f32[512,512]{1,0:T(8,128)S(1)} %get-tuple-element.82) | copy-start | bytes 3145732
  122.5 22.6 %copy-start.17 = (f32[512,512]{1,0:T(8,128)}, f32[512,512]{1,0:T(8,128)S(1)}, u32[]{:S(2)}) copy-start(f32[512,512]{1,0:T(8,128)S(1)} %get-tuple-element.74) | copy-start | bytes 3145732
  122.5 5.1 %copy-start.25 = (bf16[512,512]{1,0:T(8,128)(2,1)S(1)}, bf16[512,512]{1,0:T(8,128)(2,1)}, u32[]{:S(2)}) copy-start(bf16[512,512]{1,0:T(8,128)(2,1)} %copy-done.24) | copy-start | bytes 1572868
  122.5 8.5 %copy-start.22 = (bf16[1024,256]{1,0:T(8,128)(2,1)S(1)}, bf16[1024,256]{1,0:T(8,128)(2,1)}, u32[]{:S(2)}) copy-start(bf16[1024,256]{1,0:T(8,128)(2,1)} %copy-done.21) | copy-start | bytes 1572868
  127.6 28.0 %copy-start.13 = (f32[1024,256]{1,0:T(8,128)}, f32[1024,256]{1,0:T(8,128)S(1)}, u32[]{:S(2)}) copy-start(f32[1024,256]{1,0:T(8,128)S(1)} %get-tuple-element.79) | copy-start | bytes 3145732
  127.6 28.0 %copy-start.15 = (f32[1024,256]{1,0:T(8,128)}, f32[1024,256]{1,0:T(8,128)S(1)}, u32[]{:S(2)}) copy-start(f32[1024,256]{1,0:T(8,128)S(1)} %get-tuple-element.86) | copy-start | bytes 3145732
  127.6 16.2 %collective-permute-start.5 = (bf16[512,512]{1,0:T(8,128)(2,1)S(1)}, bf16[512,512]{1,0:T(8,128)(2,1)S(1)}, u32[]{:S(2)}, u32[]{:S(2)}) collective-permute-start(bf16[512,512]{1,0:T(8,128)(2,1)S(1)} %copy-done.25), channel_id=1, source_target_pairs={{0,192},{64,128},{128,64},{192,0},{1,193},{65,129},{129,65},{193,1... | collective-permute-start | bytes 1572872 | tf_op jit(solution)/shard_map/ppermute | solution.py:42
  131.1 23.7 %collective-permute-start.9 = (bf16[1024,256]{1,0:T(8,128)(2,1)S(1)}, bf16[1024,256]{1,0:T(8,128)(2,1)S(1)}, u32[]{:S(2)}, u32[]{:S(2)}) collective-permute-start(bf16[1024,256]{1,0:T(8,128)(2,1)S(1)} %copy-done.22), channel_id=1, source_target_pairs={{0,192},{64,128},{128,64},{192,0},{1,193},{65,129},{129,65},{193,1... | collective-permute-start | bytes 1572872 | tf_op jit(solution)/shard_map/ppermute | solution.py:42
  131.7 24.7 %copy-start.28 = (bf16[512,512]{1,0:T(8,128)(2,1)}, bf16[512,512]{1,0:T(8,128)(2,1)S(1)}, u32[]{:S(2)}) copy-start(bf16[512,512]{1,0:T(8,128)(2,1)S(1)} %collective-permute-done.4) | copy-start | bytes 1572868
  143.8 12.6 %copy-start.29 = (bf16[512,512]{1,0:T(8,128)(2,1)}, bf16[512,512]{1,0:T(8,128)(2,1)S(1)}, u32[]{:S(2)}) copy-start(bf16[512,512]{1,0:T(8,128)(2,1)S(1)} %collective-permute-done.5) | copy-start | bytes 1572868
  144.7 15.8 %copy-start.20 = (f32[512,512]{1,0:T(8,128)S(1)}, f32[512,512]{1,0:T(8,128)}, u32[]{:S(2)}) copy-start(f32[512,512]{1,0:T(8,128)} %copy-done.19) | copy-start | bytes 3145732
  144.7 15.8 %collective-permute-start.7 = (bf16[256,512]{1,0:T(8,128)(2,1)}, bf16[256,512]{1,0:T(8,128)(2,1)S(1)}, u32[]{:S(2)}, u32[]{:S(2)}) collective-permute-start(bf16[256,512]{1,0:T(8,128)(2,1)} %add_convert_fusion.2), channel_id=1, source_target_pairs={{0,64},{64,0},{128,192},{192,128},{1,65},{65,1},{129,193},{193,129... | collective-permute-start | bytes 786440 | tf_op jit(solution)/shard_map/ppermute | solution.py:42
  145.8 14.7 %copy-start.18 = (f32[512,512]{1,0:T(8,128)S(1)}, f32[512,512]{1,0:T(8,128)}, u32[]{:S(2)}) copy-start(f32[512,512]{1,0:T(8,128)} %copy-done.17) | copy-start | bytes 3145732
  145.8 14.6 %collective-permute-start.6 = (bf16[256,512]{1,0:T(8,128)(2,1)}, bf16[256,512]{1,0:T(8,128)(2,1)}, u32[]{:S(2)}, u32[]{:S(2)}) collective-permute-start(bf16[256,512]{1,0:T(8,128)(2,1)} %add_convert_fusion.3), channel_id=1, source_target_pairs={{0,192},{64,128},{128,64},{192,0},{1,193},{65,129},{129,65},{193,1... | collective-permute-start | bytes 786440 | tf_op jit(solution)/shard_map/ppermute | solution.py:42
  148.5 7.9 %copy-start.30 = (bf16[1024,256]{1,0:T(8,128)(2,1)}, bf16[1024,256]{1,0:T(8,128)(2,1)S(1)}, u32[]{:S(2)}) copy-start(bf16[1024,256]{1,0:T(8,128)(2,1)S(1)} %collective-permute-done.8) | copy-start | bytes 1572868
  154.8 1.6 copy-start.32
  156.4 3.2 %collective-permute-start.10 = (f32[8,2048]{1,0:T(8,128)S(1)}, f32[8,2048]{1,0:T(8,128)}, u32[]{:S(2)}, u32[]{:S(2)}) collective-permute-start(f32[8,2048]{1,0:T(8,128)S(1)} %convolution_multiply_fusion), channel_id=1, source_target_pairs={{0,8},{8,0},{1,9},{9,1},{2,10},{10,2},{3,11},{11,3},{4,12},{12,4},... | collective-permute-start | bytes 196616 | tf_op jit(solution)/shard_map/ppermute | solution.py:42
  156.5 21.6 %collective-permute-start.13 = (bf16[512,256]{1,0:T(8,128)(2,1)}, bf16[512,256]{1,0:T(8,128)(2,1)}, u32[]{:S(2)}, u32[]{:S(2)}) collective-permute-start(bf16[512,256]{1,0:T(8,128)(2,1)} %add_convert_fusion), channel_id=1, source_target_pairs={{0,64},{64,0},{128,192},{192,128},{1,65},{65,1},{129,193},{193,129... | collective-permute-start | bytes 786440 | tf_op jit(solution)/shard_map/ppermute | solution.py:42
  156.9 21.3 %collective-permute-start.12 = (bf16[512,256]{1,0:T(8,128)(2,1)}, bf16[512,256]{1,0:T(8,128)(2,1)}, u32[]{:S(2)}, u32[]{:S(2)}) collective-permute-start(bf16[512,256]{1,0:T(8,128)(2,1)} %add_convert_fusion.1), channel_id=1, source_target_pairs={{0,192},{64,128},{128,64},{192,0},{1,193},{65,129},{129,65},{193,1... | collective-permute-start | bytes 786440 | tf_op jit(solution)/shard_map/ppermute | solution.py:42
  160.5 8.6 %copy-start.39 = (pred[256]{0:T(512)(128)(4,1)S(1)}, pred[256]{0:T(512)(128)(4,1)}, u32[]{:S(2)}) copy-start(pred[256]{0:T(512)(128)(4,1)} %copy-done.38) | copy-start | bytes 772
  162.0 36.6 %collective-permute-start.19 = (bf16[64,1024]{1,0:T(8,128)(2,1)S(1)}, bf16[64,1024]{1,0:T(8,128)(2,1)S(1)}, u32[]{:S(2)}, u32[]{:S(2)}) collective-permute-start(bf16[64,1024]{1,0:T(8,128)(2,1)S(1)} %pad_maximum_fusion.5), channel_id=1, source_target_pairs={{0,48},{16,32},{32,16},{48,0},{1,49},{17,33},{33,17},{49,1},{2,50}... | collective-permute-start | bytes 393224 | tf_op jit(solution)/shard_map/ppermute | solution.py:42
  167.5 33.0 %collective-permute-start.18 = (bf16[64,1024]{1,0:T(8,128)(2,1)S(1)}, bf16[64,1024]{1,0:T(8,128)(2,1)S(1)}, u32[]{:S(2)}, u32[]{:S(2)}) collective-permute-start(bf16[64,1024]{1,0:T(8,128)(2,1)S(1)} %pad_maximum_fusion.4), channel_id=1, source_target_pairs={{0,32},{16,48},{32,0},{48,16},{1,33},{17,49},{33,1},{49,17},{2,34}... | collective-permute-start | bytes 393224 | tf_op jit(solution)/shard_map/ppermute | solution.py:42
  169.1 2.4 %copy-start.35 = (bf16[2048,8]{0,1:T(8,128)(2,1)S(1)}, bf16[2048,8]{0,1:T(8,128)(2,1)}, u32[]{:S(2)}) copy-start(bf16[2048,8]{0,1:T(8,128)(2,1)} %param.10) | copy-start | bytes 98308
  171.5 6.7 %copy-start.16 = (f32[1024,256]{1,0:T(8,128)S(1)}, f32[1024,256]{1,0:T(8,128)}, u32[]{:S(2)}) copy-start(f32[1024,256]{1,0:T(8,128)} %copy-done.15) | copy-start | bytes 3145732
  171.5 6.7 %copy-start.33 = (bf16[1024,256]{1,0:T(8,128)(2,1)S(1)}, bf16[1024,256]{1,0:T(8,128)(2,1)}, u32[]{:S(2)}) copy-start(bf16[1024,256]{1,0:T(8,128)(2,1)} %copy-done.32) | copy-start | bytes 1572868
  171.5 7.8 %copy-start.14 = (f32[1024,256]{1,0:T(8,128)S(1)}, f32[1024,256]{1,0:T(8,128)}, u32[]{:S(2)}) copy-start(f32[1024,256]{1,0:T(8,128)} %copy-done.13) | copy-start | bytes 3145732
  171.5 7.8 %copy-start.31 = (bf16[1024,256]{1,0:T(8,128)(2,1)S(1)}, bf16[1024,256]{1,0:T(8,128)(2,1)}, u32[]{:S(2)}) copy-start(bf16[1024,256]{1,0:T(8,128)(2,1)} %copy-done.30) | copy-start | bytes 1572868
  172.9 4.3 %collective-permute-start.11 = (f32[8,2048]{1,0:T(8,128)S(1)}, f32[8,2048]{1,0:T(8,128)S(1)}, u32[]{:S(2)}, u32[]{:S(2)}) collective-permute-start(f32[8,2048]{1,0:T(8,128)S(1)} %add.160), channel_id=1, source_target_pairs={{0,2},{2,0},{4,6},{6,4},{1,3},{3,1},{5,7},{7,5},{8,10},{10,8},{12,... | collective-permute-start | bytes 196616 | tf_op jit(solution)/shard_map/ppermute | solution.py:42
  177.2 23.2 %collective-permute-start.17 = (bf16[64,1024]{1,0:T(8,128)(2,1)S(1)}, bf16[64,1024]{1,0:T(8,128)(2,1)S(1)}, u32[]{:S(2)}, u32[]{:S(2)}) collective-permute-start(bf16[64,1024]{1,0:T(8,128)(2,1)S(1)} %pad_maximum_fusion.3), channel_id=1, source_target_pairs={{0,16},{16,0},{32,48},{48,32},{1,17},{17,1},{33,49},{49,33},{2,18}... | collective-permute-start | bytes 393224 | tf_op jit(solution)/shard_map/ppermute | solution.py:42
  180.4 5.8 %collective-permute-start.14 = (f32[8,2048]{1,0:T(8,128)S(1)}, f32[8,2048]{1,0:T(8,128)S(1)}, u32[]{:S(2)}, u32[]{:S(2)}) collective-permute-start(f32[8,2048]{1,0:T(8,128)S(1)} %add.165), channel_id=1, source_target_pairs={{0,6},{2,4},{4,2},{6,0},{1,7},{3,5},{5,3},{7,1},{8,14},{10,12},{12... | collective-permute-start | bytes 196616 | tf_op jit(solution)/shard_map/ppermute | solution.py:42
  182.0 24.1 %collective-permute-start.23 = (bf16[128,512]{1,0:T(8,128)(2,1)S(1)}, bf16[128,512]{1,0:T(8,128)(2,1)S(1)}, u32[]{:S(2)}, u32[]{:S(2)}) collective-permute-start(bf16[128,512]{1,0:T(8,128)(2,1)S(1)} %pad_maximum_fusion.8), channel_id=1, source_target_pairs={{0,48},{16,32},{32,16},{48,0},{1,49},{17,33},{33,17},{49,1},{2,50}... | collective-permute-start | bytes 393224 | tf_op jit(solution)/shard_map/ppermute | solution.py:42
  186.2 5.1 %collective-permute-start.15 = (f32[8,2048]{1,0:T(8,128)S(1)}, f32[8,2048]{1,0:T(8,128)S(1)}, u32[]{:S(2)}, u32[]{:S(2)}) collective-permute-start(f32[8,2048]{1,0:T(8,128)S(1)} %add.170), channel_id=1, source_target_pairs={{0,1},{1,0},{2,3},{3,2},{4,5},{5,4},{6,7},{7,6},{8,9},{9,8},{10,11... | collective-permute-start | bytes 196616 | tf_op jit(solution)/shard_map/ppermute | solution.py:42
  191.4 4.4 %collective-permute-start.16 = (f32[8,2048]{1,0:T(8,128)S(1)}, f32[8,2048]{1,0:T(8,128)S(1)}, u32[]{:S(2)}, u32[]{:S(2)}) collective-permute-start(f32[8,2048]{1,0:T(8,128)S(1)} %add.171), channel_id=1, source_target_pairs={{0,64},{64,0},{128,192},{192,128},{1,65},{65,1},{129,193},{193,129... | collective-permute-start | bytes 196616 | tf_op jit(solution)/shard_map/ppermute | solution.py:42
  195.7 10.4 %collective-permute-start.22 = (bf16[128,512]{1,0:T(8,128)(2,1)S(1)}, bf16[128,512]{1,0:T(8,128)(2,1)S(1)}, u32[]{:S(2)}, u32[]{:S(2)}) collective-permute-start(bf16[128,512]{1,0:T(8,128)(2,1)S(1)} %pad_maximum_fusion.7), channel_id=1, source_target_pairs={{0,32},{16,48},{32,0},{48,16},{1,33},{17,49},{33,1},{49,17},{2,34}... | collective-permute-start | bytes 393224 | tf_op jit(solution)/shard_map/ppermute | solution.py:42
  198.5 10.8 %collective-permute-start.21 = (bf16[128,512]{1,0:T(8,128)(2,1)S(1)}, bf16[128,512]{1,0:T(8,128)(2,1)S(1)}, u32[]{:S(2)}, u32[]{:S(2)}) collective-permute-start(bf16[128,512]{1,0:T(8,128)(2,1)S(1)} %pad_maximum_fusion.6), channel_id=1, source_target_pairs={{0,16},{16,0},{32,48},{48,32},{1,17},{17,1},{33,49},{49,33},{2,18}... | collective-permute-start | bytes 393224 | tf_op jit(solution)/shard_map/ppermute | solution.py:42
  200.5 5.6 %collective-permute-start.20 = (f32[8,2048]{1,0:T(8,128)S(1)}, f32[8,2048]{1,0:T(8,128)S(1)}, u32[]{:S(2)}, u32[]{:S(2)}) collective-permute-start(f32[8,2048]{1,0:T(8,128)S(1)} %add.172), channel_id=1, source_target_pairs={{0,192},{64,128},{128,64},{192,0},{1,193},{65,129},{129,65},{193,1... | collective-permute-start | bytes 196616 | tf_op jit(solution)/shard_map/ppermute | solution.py:42
  201.7 13.0 %collective-permute-start.27 = (f32[32,1024]{1,0:T(8,128)S(1)}, f32[32,1024]{1,0:T(8,128)S(1)}, u32[]{:S(2)}, u32[]{:S(2)}) collective-permute-start(f32[32,1024]{1,0:T(8,128)S(1)} %constant_dynamic-slice_fusion), channel_id=1, source_target_pairs={{0,8},{8,0},{1,9},{9,1},{2,10},{10,2},{3,11},{11,3},{4,12},{12,4},... | collective-permute-start | bytes 393224 | tf_op jit(solution)/shard_map/ppermute | solution.py:42
  209.4 5.3 %collective-permute-start.24 = (f32[8,2048]{1,0:T(8,128)S(1)}, f32[8,2048]{1,0:T(8,128)S(1)}, u32[]{:S(2)}, u32[]{:S(2)}) collective-permute-start(f32[8,2048]{1,0:T(8,128)S(1)} %add.180), channel_id=1, source_target_pairs={{0,16},{16,0},{32,48},{48,32},{1,17},{17,1},{33,49},{49,33},{2,18}... | collective-permute-start | bytes 196616 | tf_op jit(solution)/shard_map/ppermute | solution.py:42
  209.5 6.0 %collective-permute-start.26 = (f32[64,512]{1,0:T(8,128)S(1)}, f32[64,512]{1,0:T(8,128)S(1)}, u32[]{:S(2)}, u32[]{:S(2)}) collective-permute-start(f32[64,512]{1,0:T(8,128)S(1)} %constant_dynamic-slice_fusion.1), channel_id=1, source_target_pairs={{0,8},{8,0},{1,9},{9,1},{2,10},{10,2},{3,11},{11,3},{4,12},{12,4},... | collective-permute-start | bytes 393224 | tf_op jit(solution)/shard_map/ppermute | solution.py:42
  214.6 6.5 %collective-permute-start.25 = (f32[8,2048]{1,0:T(8,128)S(1)}, f32[8,2048]{1,0:T(8,128)S(1)}, u32[]{:S(2)}, u32[]{:S(2)}) collective-permute-start(f32[8,2048]{1,0:T(8,128)S(1)} %add.188), channel_id=1, source_target_pairs={{0,48},{16,32},{32,16},{48,0},{1,49},{17,33},{33,17},{49,1},{2,50}... | collective-permute-start | bytes 196616 | tf_op jit(solution)/shard_map/ppermute | solution.py:42
  (7 other events, 7.3 us)

commit v4 on v3

--- a/solution.py
+++ b/solution.py
@@ -19,6 +19,8 @@
     ("zh", 1),
     ("zh", 3),
 )
+COST_IN = 1000
+COST_SLOTS = 1000
 F32 = jnp.float32
 BF16 = jnp.bfloat16
 
@@ -50,18 +52,15 @@
     return lax.optimization_barrier(values)
 
 
-def call(body, pos, grid, inputs, in_blocks, outputs, out_blocks):
+def call(body, pos, inputs, outputs, cost=1000):
+    vmem = pl.BlockSpec(memory_space=pltpu.VMEM)
     return pl.pallas_call(
         body,
-        grid_spec=pltpu.PrefetchScalarGridSpec(
-            num_scalar_prefetch=1,
-            grid=(grid,),
-            in_specs=[pl.BlockSpec(shape, index) for shape, index in in_blocks],
-            out_specs=[pl.BlockSpec(shape, index) for shape, index in out_blocks],
-        ),
+        in_specs=[pl.BlockSpec(memory_space=pltpu.SMEM)] + [vmem] * len(inputs),
+        out_specs=[vmem] * len(outputs),
         out_shape=[jax.ShapeDtypeStruct(shape, dtype) for shape, dtype in outputs],
-        cost_estimate=pl.CostEstimate(flops=1000, bytes_accessed=1000, transcendentals=0),
-        compiler_params=pltpu.CompilerParams(vmem_limit_bytes=40 * 1024 * 1024),
+        cost_estimate=pl.CostEstimate(flops=cost, bytes_accessed=1000, transcendentals=0),
+        compiler_params=pltpu.CompilerParams(vmem_limit_bytes=20 * 1024 * 1024),
     )(pos, *inputs)
 
 
@@ -70,147 +69,106 @@
     return jnp.sum(jnp.where(lane == pos[2], lanes.astype(F32), 0.0), axis=1, keepdims=True)
 
 
-def scale_grads(pos, received):
+def scale_grads(pos, received, expert_out):
     slots, wide = received.shape
     width = wide - EXTRA
     half = width // 2
     rows = slots // 4
 
-    def body(pos_ref, rec, mine, give):
-        gate = gate_of(pos_ref, rec[:, width:])
+    def body(pos_ref, rec, expert, mine, give, gate_grad):
         core = pos_ref[1]
-        for out, which in ((mine, core), (give, 1 - core)):
-            start = pl.multiple_of(which * half, half)
-            out[...] = (gate * rec[:, pl.ds(start, half)].astype(F32)).astype(BF16)
-
-    block = ((rows, half), lambda i, pos: (i, 0))
+        for r in range(0, slots, rows):
+            at = slice(r, r + rows)
+            gate = gate_of(pos_ref, rec[at, width:])
+            for out, which in ((mine, core), (give, 1 - core)):
+                start = pl.multiple_of(which * half, half)
+                out[at, :] = (gate * rec[at, pl.ds(start, half)].astype(F32)).astype(BF16)
+            gate_grad[at, :] = jnp.sum(
+                expert[at, :] * rec[at, :width].astype(F32), axis=1, keepdims=True
+            )
+
     return call(
         body,
         pos,
-        4,
-        [received],
-        [((rows, wide), lambda i, pos: (i, 0))],
-        [((slots, half), BF16)] * 2,
-        [block, block],
-    )
-
-
-def pre_grads(pos, received, weight_out, act, slope):
+        [received, expert_out],
+        [((slots, half), BF16), ((slots, half), BF16), ((slots, 1), F32)],
+    )
+
+
+def pre_grads(pos, received, weight_out, slope):
     slots, wide = received.shape
     hidden, width = weight_out.shape
     step = hidden // 4
 
-    def body(pos_ref, rec, weight, act_ref, slope_ref, grad_pre, give, gate_grad):
-        i = pl.program_id(0)
-        grad_act = lax.dot_general(
-            rec[:, :width], weight[...], (((1,), (1,)), ((), ())), preferred_element_type=F32
-        )
+    def body(pos_ref, rec, weight, slope_ref, grad_pre, give):
         gate = gate_of(pos_ref, rec[:, width:])
-        part = jnp.sum(act_ref[...].astype(F32) * grad_act, axis=1, keepdims=True)
-        value = (gate * grad_act * slope_ref[...]).astype(BF16)
-        grad_pre[...] = value
-
-        @pl.when(i < 2)
-        def _():
-            give[...] = value
-
-        @pl.when(i == 0)
-        def _():
-            gate_grad[...] = part
-
-        @pl.when(i > 0)
-        def _():
-            gate_grad[...] += part
-
-    order = lambda i, pos: i ^ (2 * (1 - pos[1]))
-    column = ((slots, step), lambda i, pos: (0, order(i, pos)))
+        for i in range(4):
+            at = slice(i * step, (i + 1) * step)
+            grad_act = lax.dot_general(
+                rec[:, :width], weight[at, :], (((1,), (1,)), ((), ())), preferred_element_type=F32
+            )
+            grad_pre[:, at] = (gate * grad_act * slope_ref[:, at]).astype(BF16)
+        start = pl.multiple_of((1 - pos_ref[1]) * (hidden // 2), hidden // 2)
+        give[...] = grad_pre[:, pl.ds(start, hidden // 2)]
+
     return call(
         body,
         pos,
-        4,
-        [received, weight_out, act, slope],
-        [
-            ((slots, wide), lambda i, pos: (0, 0)),
-            ((step, width), lambda i, pos: (order(i, pos), 0)),
-            column,
-            column,
-        ],
-        [((slots, hidden), BF16), ((slots, hidden // 2), BF16), ((slots, 1), F32)],
-        [
-            column,
-            ((slots, step), lambda i, pos: (0, jnp.minimum(i, 1))),
-            ((slots, 1), lambda i, pos: (0, 0)),
-        ],
-    )
-
-
-def parts(pos, left, right, own_offset, kept):
+        [received, weight_out, slope],
+        [((slots, hidden), BF16), ((slots, hidden // 2), BF16)],
+    )
+
+
+def parts(pos, left, right, own_offset, kept, cost=1000):
     left_mine, left_other = left
     right_mine, right_other = right
-    slots = left_mine.shape[0]
     width = left_mine.shape[1] // 4
     cols = right_other.shape[1] // 2
     dtype = F32 if kept else BF16
-
-    def mask(i):
-        if kept:
-            return jnp.where(i == 1, 3, jnp.where(i == 3, 1, 0))
-        return jnp.where(i == 0, 1, jnp.where(i == 2, 3, 2))
-
-    def body(pos_ref, lm, lo, rm, ro, out_a, out_b):
+    masks = ((0, 3), (0, 1)) if kept else ((1, 2), (3, 2))
+
+    def body(pos_ref, lm, lo, rm, ro, *outs):
         dims = (((0,), (0,)), ((), ()))
-        value = lax.dot_general(lm[...], rm[...], dims, preferred_element_type=F32)
-        value = value + lax.dot_general(lo[...], ro[...], dims, preferred_element_type=F32)
-        value = value.astype(dtype)
-        i = pl.program_id(0)
-
-        @pl.when(i < 2)
-        def _():
-            out_a[...] = value
-
-        @pl.when(i >= 2)
-        def _():
-            out_b[...] = value
-
-    left_block = ((slots, width), lambda i, pos: (0, pos[0] ^ mask(i)))
+        for i in range(2):
+            own = pl.multiple_of((own_offset * pos_ref[1] + i) * cols, cols)
+            for j in range(2):
+                start = pl.multiple_of((pos_ref[0] ^ masks[i][j]) * width, width)
+                value = lax.dot_general(
+                    lm[:, pl.ds(start, width)],
+                    rm[:, pl.ds(own, cols)],
+                    dims,
+                    preferred_element_type=F32,
+                )
+                value = value + lax.dot_general(
+                    lo[:, pl.ds(start, width)],
+                    ro[:, i * cols : (i + 1) * cols],
+                    dims,
+                    preferred_element_type=F32,
+                )
+                outs[i][j * width : (j + 1) * width, :] = value.astype(dtype)
+
     return call(
         body,
         pos,
-        4,
         [left_mine, left_other, right_mine, right_other],
-        [
-            left_block,
-            left_block,
-            ((slots, cols), lambda i, pos: (0, own_offset * pos[1] + i // 2)),
-            ((slots, cols), lambda i, pos: (0, i // 2)),
-        ],
         [((2 * width, cols), dtype)] * 2,
-        [
-            ((width, cols), lambda i, pos: (jnp.minimum(i, 1), 0)),
-            ((width, cols), lambda i, pos: (jnp.maximum(i, 2) - 2, 0)),
-        ],
-    )
-
-
-def slot_grads_of(pos, grad_pre, weight_in):
+        cost,
+    )
+
+
+def slot_grads_of(pos, grad_pre, weight_in, cost=1000):
     slots, hidden = grad_pre.shape
     width = weight_in.shape[0]
     step = width // 4
 
     def body(pos_ref, grad, weight, out):
-        out[...] = lax.dot_general(
-            grad[...], weight[...], (((1,), (1,)), ((), ())), preferred_element_type=F32
-        ).astype(BF16)
-
-    return call(
-        body,
-        pos,
-        4,
-        [grad_pre, weight_in],
-        [((slots, hidden), lambda i, pos: (0, 0)), ((step, hidden), lambda i, pos: (i, 0))],
-        [((slots, width), BF16)],
-        [((slots, step), lambda i, pos: (0, i))],
-    )[0]
+        for i in range(4):
+            at = slice(i * step, (i + 1) * step)
+            out[:, at] = lax.dot_general(
+                grad[...], weight[at, :], (((1,), (1,)), ((), ())), preferred_element_type=F32
+            ).astype(BF16)
+
+    return call(body, pos, [grad_pre, weight_in], [((slots, width), BF16)], cost)[0]
 
 
 def zh_sum(near_a, near_b):
@@ -298,26 +256,28 @@
     left_out = (hidden_act, other_act)
     pos = jnp.stack([my_y, core, lax.axis_index(GROUP)]).astype(jnp.int32)
 
-    received, left_in, left_out, act_slope = tie(received, left_in, left_out, act_slope)
-    my_out, give_out = scale_grads(pos, received)
+    expert_out = jnp.dot(hidden_act, weight_out, preferred_element_type=F32)
+
+    received, left_in, left_out, act_slope, expert_out = tie(
+        received, left_in, left_out, act_slope, expert_out
+    )
+    my_out, give_out, slot_combine_grad = scale_grads(pos, received, expert_out)
     other_out = swap(give_out, "core", 1)
     received, _ = tie(received, give_out)
-    grad_pre, give_in, slot_combine_grad = pre_grads(
-        pos, received, weight_out, hidden_act, act_slope
-    )
+    grad_pre, give_in = pre_grads(pos, received, weight_out, act_slope)
     other_in = swap(give_in, "core", 1)
+
+    send_out_a, send_out_b = parts(pos, left_out, (my_out, other_out), 0, False)
+    got_out_a, got_out_b = swap(send_out_a, "y", 1), swap(send_out_b, "y", 3)
+    grad_pre, slot_combine_grad, _, _ = tie(grad_pre, slot_combine_grad, send_out_a, send_out_b)
     flat_combine = exchange(
         slot_combine_grad.astype(BF16).reshape(experts, capacity), GROUP
     ).reshape(slot_count)
-
-    send_out_a, send_out_b = parts(pos, left_out, (my_out, other_out), 0, False)
-    got_out_a, got_out_b = swap(send_out_a, "y", 1), swap(send_out_b, "y", 3)
-    grad_pre, _ = tie(grad_pre, send_out_a)
-    send_in_a, send_in_b = parts(pos, left_in, (grad_pre, other_in), 2, False)
+    send_in_a, send_in_b = parts(pos, left_in, (grad_pre, other_in), 2, False, COST_IN)
     got_in_a, got_in_b = swap(send_in_a, "y", 1), swap(send_in_b, "y", 3)
 
-    grad_pre, _ = tie(grad_pre, send_in_a)
-    grad_slots = slot_grads_of(pos, grad_pre, weight_in)
+    grad_pre, _, _ = tie(grad_pre, send_in_a, send_in_b)
+    grad_slots = slot_grads_of(pos, grad_pre, weight_in, COST_SLOTS)
     grad_slots, flat_combine = tie(grad_slots, flat_combine)
     flat_grads = exchange(
         grad_slots.reshape(experts, capacity, model_width), GROUP
@@ -327,7 +287,28 @@
     keep_out_a, keep_out_b = parts(pos, left_out, (my_out, other_out), 0, True)
     grad_pre, _ = tie(grad_pre, keep_out_a)
     keep_in_a, keep_in_b = parts(pos, left_in, (grad_pre, other_in), 2, True)
-    flat_combine, _ = tie(flat_combine, keep_in_a)
+
+    def router_steps(value, steps):
+        for axis, mask in steps:
+            value = value + swap(value, axis, mask)
+        return value
+
+    def far_of(keep, got):
+        rows = keep.shape[0] // 2
+        return (keep[rows:] + got[rows:].astype(F32)).astype(BF16)
+
+    def near_of(keep, got, got_far):
+        rows = keep.shape[0] // 2
+        return keep[:rows] + got[:rows].astype(F32) + got_far.astype(F32)
+
+    got_out_a, got_out_b, _ = tie(got_out_a, got_out_b, keep_in_a)
+    far_a, far_b = far_of(keep_out_a, got_out_a), far_of(keep_out_b, got_out_b)
+    far_out_a, far_out_b = swap(far_a, "y", 3), swap(far_b, "y", 1)
+
+    got_in_a, got_in_b, _, _ = tie(got_in_a, got_in_b, far_a, far_b)
+    far_a, far_b = far_of(keep_in_a, got_in_a), far_of(keep_in_b, got_in_b)
+    far_in_a, far_in_b = swap(far_a, "y", 3), swap(far_b, "y", 1)
+    flat_combine, _, _ = tie(flat_combine, far_a, far_b)
 
     combine_wide = flat_combine.astype(F32)[:, None]
     combine_grad = jnp.stack(
@@ -345,29 +326,7 @@
     )
     logit_b = logit_grad.astype(BF16)
 
-    def router_steps(value, steps):
-        for axis, mask in steps:
-            value = value + swap(value, axis, mask)
-        return value
-
     router_part = contract_rows(logit_b, tokens) * grad_scale
-
-    def far_of(keep, got):
-        rows = keep.shape[0] // 2
-        return (keep[rows:] + got[rows:].astype(F32)).astype(BF16)
-
-    def near_of(keep, got, got_far):
-        rows = keep.shape[0] // 2
-        return keep[:rows] + got[:rows].astype(F32) + got_far.astype(F32)
-
-    got_out_a, got_out_b, _ = tie(got_out_a, got_out_b, router_part)
-    far_a, far_b = far_of(keep_out_a, got_out_a), far_of(keep_out_b, got_out_b)
-    far_out_a, far_out_b = swap(far_a, "y", 3), swap(far_b, "y", 1)
-
-    got_in_a, got_in_b, _, _ = tie(got_in_a, got_in_b, far_a, far_b)
-    far_a, far_b = far_of(keep_in_a, got_in_a), far_of(keep_in_b, got_in_b)
-    far_in_a, far_in_b = swap(far_a, "y", 3), swap(far_b, "y", 1)
-    router_part, _, _ = tie(router_part, far_a, far_b)
     router_part = router_steps(router_part, ROUTER_STEPS[:1])
 
     far_out_a, far_out_b, _ = tie(far_out_a, far_out_b, router_part)

time: 224 us -> 195 us (0.87)
  waiting for transfers between devices: 85.5 us -> 61.4 us
  Pallas kernels: 31.7 us -> 22.3 us
  blocking collectives: 9 us -> 0 us
  matrix products: 15 us -> 21.9 us
  starting transfers between devices: 53.4 us -> 56 us
    ppermute x28, waiting for transfers between devices: 46 us -> 28.7 us  [swap(): return lax.ppermute(values, axis, [(i, i ^ mask) for i in range(size)])]
    pallas_call x7, Pallas kernels: 31.7 us -> 22.3 us  [call(): pl.pallas_call(body, in_specs=[pl.BlockSpec(memory_space=pltpu.SMEM)] + [...]
    all_to_all x1 -> x0, blocking collectives: 9 us -> none  [exchange(): return lax.all_to_all(values, axes, split_axis=0, concat_axis=0, tiled=True)]
    dot_general x0 -> x1, matrix products: none -> 6.89 us  [per_device(): expert_out = jnp.dot(hidden_act, weight_out, preferred_element_type=F32)]
    all_to_all x3 -> x4, waiting for transfers between devices: 39.5 us -> 32.7 us  [exchange(): return lax.all_to_all(values, axes, split_axis=0, concat_axis=0, tiled=True)]
    all_to_all x3 -> x4, starting transfers between devices: 17.3 us -> 22.3 us  [exchange(): return lax.all_to_all(values, axes, split_axis=0, concat_axis=0, tiled=True)]
    ppermute x28, starting transfers between devices: 36.1 us -> 33.6 us  [swap(): return lax.ppermute(values, axis, [(i, i ^ mask) for i in range(size)])]
    unnamed x80 -> x74, local copies, waits for them, and re-layouts: 11.5 us -> 12.5 us
  transfers between devices with their start and end apart: 31 -> 32, of which waited for: 11 -> 10; matrix products, arithmetic and copies ran while one was open for 11% -> 18% of each run, Pallas kernels for 9% -> 11%
where the time goes in v4:
time: 195 us; the launch traced here: 192 us
  waiting for transfers between devices  61.4 us (31%)
  starting transfers between devices  56 us (29%)
  Pallas kernels  22.3 us (11%)
  matrix products  21.9 us (11%)
  other arithmetic  15.7 us (8%)
  local copies, waits for them, and re-layouts  13.5 us (7%)
    ppermute x28, starting transfers between devices, swap(): return lax.ppermute(values, axis, [(i, i ^ mask) for i in range(size)])  33.6 us
    all_to_all x4, waiting for transfers between devices, exchange(): return lax.all_to_all(values, axes, split_axis=0, concat_axis=0, tiled=True)  32.7 us
    ppermute x28, waiting for transfers between devices, swap(): return lax.ppermute(values, axis, [(i, i ^ mask) for i in range(size)])  28.7 us
    all_to_all x4, starting transfers between devices, exchange(): return lax.all_to_all(values, axes, split_axis=0, concat_axis=0, tiled=True)  22.3 us
    pallas_call x7, Pallas kernels, call(): pl.pallas_call(body, in_specs=[pl.BlockSpec(memory_space=pltpu.SMEM)] + [...  22.3 us
    unnamed x74, local copies, waits for them, and re-layouts  12.5 us
    dot_general x1, matrix products, per_device(): hidden_pre = jnp.dot(slot_tokens, weight_in, preferred_element_type=F32)  7.45 us
    dot_general x1, matrix products, per_device(): expert_out = jnp.dot(hidden_act, weight_out, preferred_element_type=F32)  6.89 us
  transfers between devices with their start and end apart: 32, of which 10 were waited for; matrix products, arithmetic and copies ran while one was open for 18% of the time, Pallas kernels for 11%

profile of v4, /device:TPU:2, one launch (start us, length us, event | category | flops | bytes accessed | tf_op | source)
XLA Modules:
  0.0 192.1 jit_solution(4982127547527457715)
XLA Ops:
  0.6 0.8 multiply_add_fusion
  1.4 0.8 compare_reduce_fusion.1
  2.2 2.1 %convolution_convert_fusion = bf16[512,2048]{1,0:T(8,128)(2,1)} fusion(bf16[256,2048]{1,0:T(8,128)(2,1)S(1)} %copy-done, s32[256]{0:T(256)S(1)} %bitcast.54, s32[256]{0:T(256)S(1)} %bitcast.49, pred[256]{0:T(512)(128)(4,1)S(1)} %get-tuple-element.111, pred[256]{0:T(512)(128)(4,1)S(1)} %get-tuple-element.110), kind=kOutput, calls=%fused_computation.1 | convolution fusion | flops 538574848 | bytes 3148288 | tf_op jit(solution)/shard_map/dot_general | solution.py:226
  4.3 6.3 %all-to-all-start.1 = ((bf16[8,64,2048]{2,1,0:T(8,128)(2,1)}), bf16[8,64,2048]{2,1,0:T(8,128)(2,1)S(1)}, u32[]{:S(2)}, u32[]{:S(2)}) async-start(bf16[8,64,2048]{2,1,0:T(8,128)(2,1)} %bitcast.48), calls=%async_computation.1 | async-start | bytes 4194304 | tf_op jit(solution)/shard_map/all_to_all | solution.py:48
  11.9 0.8 convolution_convert_fusion.1
  12.6 1.6 pad_maximum_fusion
  14.2 21.7 %all-to-all-done.1 = bf16[8,64,2048]{2,1,0:T(8,128)(2,1)S(1)} async-done(((bf16[8,64,2048]{2,1,0:T(8,128)(2,1)}), bf16[8,64,2048]{2,1,0:T(8,128)(2,1)S(1)}, u32[]{:S(2)}, u32[]{:S(2)}) %all-to-all-start.1) | async-done | bytes 2097184 | tf_op jit(solution)/shard_map/all_to_all | solution.py:48
  35.9 1.3 copy-done.1
  37.2 5.3 %all-to-all-start = ((bf16[8,64,2176]{2,1,0:T(8,128)(2,1)}), bf16[8,64,2176]{2,1,0:T(8,128)(2,1)S(1)}, u32[]{:S(2)}, u32[]{:S(2)}) async-start(bf16[8,64,2176]{2,1,0:T(8,128)(2,1)} %bitcast.47), calls=%async_computation | async-start | bytes 4456448 | tf_op jit(solution)/shard_map/all_to_all | solution.py:48
  42.5 7.5 %fusion.4 = (f32[512,1024]{1,0:T(8,128)}, bf16[512,1024]{1,0:T(8,128)(2,1)}) fusion(bf16[512,2048]{1,0:T(8,128)(2,1)} %bitcast.41, bf16[1,2048,1024]{2,1,0:T(8,128)(2,1)} %param.11), kind=kOutput, calls=%fused_computation.10 | convolution fusion | flops 2152726528 | bytes 9437184 | tf_op jit(solution)/shard_map/dot_general | solution.py:250
  50.5 6.9 %fusion.10.expert = f32[512,2048]{1,0:T(8,128)} fusion(bf16[512,1024]{1,0:T(8,128)(2,1)} %get-tuple-element.63.lm, bf16[1,1024,2048]{2,1,0:T(8,128)(2,1)} %param.12), kind=kOutput, calls=%fused_computation.86 | convolution fusion | flops 2147483648 | bytes 9437184 | tf_op jit(solution)/shard_map/dot_general | solution.py:259
  57.4 11.0 %all-to-all-done = bf16[8,64,2176]{2,1,0:T(8,128)(2,1)S(1)} async-done(((bf16[8,64,2176]{2,1,0:T(8,128)(2,1)}), bf16[8,64,2176]{2,1,0:T(8,128)(2,1)S(1)}, u32[]{:S(2)}, u32[]{:S(2)}) %all-to-all-start) | async-done | bytes 2228256 | tf_op jit(solution)/shard_map/all_to_all | solution.py:48
  68.4 2.2 %copy-done.14 = f32[512,2048]{1,0:T(8,128)S(1)} copy-done((f32[512,2048]{1,0:T(8,128)S(1)}, f32[512,2048]{1,0:T(8,128)}, u32[]{:S(2)}) %copy-start.14) | copy-done | bytes 4194328
  70.6 1.3 shard_map.111
  72.0 0.8 copy-done.12
  72.8 1.1 copy-done.15
  73.9 3.7 %shard_map.112 = (bf16[512,1024]{1,0:T(8,128)(2,1)S(1)}, bf16[512,512]{1,0:T(8,128)(2,1)}) custom-call(s32[3]{0:T(128)S(1)} %pad_add_fusion.pos_ref, bf16[512,2176]{1,0:T(8,128)(2,1)S(1)} %bitcast.39, bf16[1024,2048]{1,0:T(8,128)(2,1)S(1)} %bitcast.45, f32[512,1024]{1,0:T(8,128)S(1)} %copy-done.15), custom_call_target="tpu_custom_call" | custom-call | flops 1000 | bytes 1000 | tf_op jit(solution)/shard_map/pallas_call | solution.py:57
  77.6 4.5 %shard_map.113 = (bf16[512,512]{1,0:T(8,128)(2,1)}, bf16[512,512]{1,0:T(8,128)(2,1)}) custom-call(s32[3]{0:T(128)S(1)} %pad_add_fusion.pos_ref, bf16[512,1024]{1,0:T(8,128)(2,1)} %get-tuple-element.63.lm, bf16[512,1024]{1,0:T(8,128)(2,1)} %collective-permute-done.1.lo, bf16[512,1024]{1,0:T(8,128)(2,1)S(1)} %get-tuple-element.78.rm, ...), custom_call_target="tpu_custom_call" | custom-call | flops 1000 | bytes 1000 | tf_op jit(solution)/shard_map/pallas_call | solution.py:57
  82.1 1.6 collective-permute-start.4
  83.7 2.2 %collective-permute-start.5 = (bf16[512,512]{1,0:T(8,128)(2,1)}, bf16[512,512]{1,0:T(8,128)(2,1)}, u32[]{:S(2)}, u32[]{:S(2)}) collective-permute-start(bf16[512,512]{1,0:T(8,128)(2,1)} %get-tuple-element.67), channel_id=1, source_target_pairs={{0,192},{64,128},{128,64},{192,0},{1,193},{65,129},{129,65},{193,1... | collective-permute-start | bytes 1572872 | tf_op jit(solution)/shard_map/ppermute | solution.py:44
  86.7 5.0 %all-to-all-start.2 = ((bf16[8,1,64]{2,1,0:T(2,128)(2,1)}), bf16[8,1,64]{2,1,0:T(2,128)(2,1)S(1)}, u32[]{:S(2)}, u32[]{:S(2)}) async-start(bf16[8,1,64]{2,1,0:T(2,128)(2,1)} %all_to_all.20), calls=%async_computation.2 | async-start | bytes 8192 | tf_op jit(solution)/shard_map/all_to_all | solution.py:48
  91.7 1.2 copy-done.4
  92.9 3.2 %shard_map.114 = (bf16[1024,256]{1,0:T(8,128)(2,1)S(1)}, bf16[1024,256]{1,0:T(8,128)(2,1)S(1)}) custom-call(s32[3]{0:T(128)S(1)} %pad_add_fusion.pos_ref, bf16[512,2048]{1,0:T(8,128)(2,1)S(1)} %bitcast.42, bf16[512,2048]{1,0:T(8,128)(2,1)} %collective-permute-done.lo, bf16[512,1024]{1,0:T(8,128)(2,1)S(1)} %copy-done.4, ...), custom_call_target="tpu_custom_call" | custom-call | flops 1000 | bytes 1000 | tf_op jit(solution)/shard_map/pallas_call | solution.py:57
  96.2 0.8 copy-done.24
  97.0 0.8 copy-done.25
  97.8 2.9 %shard_map.115 = bf16[512,2048]{1,0:T(8,128)(2,1)S(1)} custom-call(s32[3]{0:T(128)S(1)} %pad_add_fusion.pos_ref, bf16[512,1024]{1,0:T(8,128)(2,1)S(1)} %copy-done.5, bf16[2048,1024]{1,0:T(8,128)(2,1)S(1)} %bitcast.46), custom_call_target="tpu_custom_call" | custom-call | flops 1000 | bytes 1000 | tf_op jit(solution)/shard_map/pallas_call | solution.py:57
  100.7 1.3 copy-done.7
  102.2 5.7 %all-to-all-start.3 = ((bf16[8,64,2048]{2,1,0:T(8,128)(2,1)}), bf16[8,64,2048]{2,1,0:T(8,128)(2,1)}, u32[]{:S(2)}, u32[]{:S(2)}) async-start(bf16[8,64,2048]{2,1,0:T(8,128)(2,1)} %bitcast.44), calls=%async_computation.3 | async-start | bytes 4194304 | tf_op jit(solution)/shard_map/all_to_all | solution.py:48
  109.2 1.2 copy-done.9
  110.4 1.2 copy-done.11
  111.6 2.8 %shard_map.116 = (f32[512,512]{1,0:T(8,128)S(1)}, f32[512,512]{1,0:T(8,128)S(1)}) custom-call(s32[3]{0:T(128)S(1)} %pad_add_fusion.pos_ref, bf16[512,1024]{1,0:T(8,128)(2,1)} %get-tuple-element.63.lm, bf16[512,1024]{1,0:T(8,128)(2,1)} %collective-permute-done.1.lo, bf16[512,1024]{1,0:T(8,128)(2,1)S(1)} %copy-done.9, bf16[512,1024]{1,0:T(8,128)(2,1)S(1)} %copy-done.11), custom_call_target="tpu_custom_call" | custom-call | flops 1000 | bytes 1000 | tf_op jit(solution)/shard_map/pallas_call | solution.py:57
  114.5 3.8 %shard_map.117 = (f32[1024,256]{1,0:T(8,128)S(1)}, f32[1024,256]{1,0:T(8,128)S(1)}) custom-call(s32[3]{0:T(128)S(1)} %pad_add_fusion.pos_ref, bf16[512,2048]{1,0:T(8,128)(2,1)S(1)} %bitcast.43, bf16[512,2048]{1,0:T(8,128)(2,1)} %collective-permute-done.lo, bf16[512,1024]{1,0:T(8,128)(2,1)S(1)} %copy-done.6, bf16[512,512]{1,0:T(8,128)(2,1)} %collective-permute-done.3.ro), custom_call_target="tpu_custom_call" | custom-call | flops 1000 | bytes 1000 | tf_op jit(solution)/shard_map/pallas_call | solution.py:57
  118.4 1.9 %add_convert_fusion.2 = bf16[256,512]{1,0:T(8,128)(2,1)} fusion(f32[512,512]{1,0:T(8,128)S(1)} %get-tuple-element.84, bf16[512,512]{1,0:T(8,128)(2,1)} %collective-permute-done.5), kind=kLoop, calls=%fused_computation.23 | loop fusion | flops 393216 | bytes 1048576 | tf_op jit(solution)/shard_map/convert_element_type | solution.py:298
  120.3 1.2 collective-permute-start.7
  121.5 1.7 add_convert_fusion.3
  123.3 2.2 %collective-permute-start.6 = (bf16[256,512]{1,0:T(8,128)(2,1)}, bf16[256,512]{1,0:T(8,128)(2,1)}, u32[]{:S(2)}, u32[]{:S(2)}) collective-permute-start(bf16[256,512]{1,0:T(8,128)(2,1)} %add_convert_fusion.3), channel_id=1, source_target_pairs={{0,192},{64,128},{128,64},{192,0},{1,193},{65,129},{129,65},{193,1... | collective-permute-start | bytes 786440 | tf_op jit(solution)/shard_map/ppermute | solution.py:44
  125.5 0.9 add_convert_fusion.1
  126.4 0.8 add_convert_fusion
  127.8 1.0 collective-permute-start.13
  129.3 0.8 add.160
  130.2 1.0 collective-permute-done.6
  131.2 1.3 convert_add_fusion.2
  132.6 5.5 %collective-permute-start.19 = (bf16[64,1024]{1,0:T(8,128)(2,1)S(1)}, bf16[64,1024]{1,0:T(8,128)(2,1)S(1)}, u32[]{:S(2)}, u32[]{:S(2)}) collective-permute-start(bf16[64,1024]{1,0:T(8,128)(2,1)S(1)} %pad_maximum_fusion.5), channel_id=1, source_target_pairs={{0,48},{16,32},{32,16},{48,0},{1,49},{17,33},{33,17},{49,1},{2,50}... | collective-permute-start | bytes 393224 | tf_op jit(solution)/shard_map/ppermute | solution.py:44
  138.1 1.5 collective-permute-start.18
  139.7 2.4 %fusion.15 = f32[256,2048]{1,0:T(8,128)S(1)} fusion(bf16[512,2048]{1,0:T(8,128)(2,1)} %bitcast.12, s32[256]{0:T(256)S(1)} %bitcast.58, s32[256]{0:T(256)S(1)} %bitcast.53, pred[256]{0:T(512)(128)(4,1)S(1)} %copy-done.36, pred[256]{0:T(512)(128)(4,1)S(1)} %get-tuple-element.110), kind=kOutput, calls=%fused_computation.91 | convolution fusion | flops 537526272 | bytes 4196864 | tf_op jit(solution)/shard_map/dot_general | solution.py:35
  142.2 1.4 fusion
  143.7 4.2 %collective-permute-done.11 = f32[8,2048]{1,0:T(8,128)S(1)} collective-permute-done((f32[8,2048]{1,0:T(8,128)S(1)}, f32[8,2048]{1,0:T(8,128)S(1)}, u32[]{:S(2)}, u32[]{:S(2)}) %collective-permute-start.11) | collective-permute-done | bytes 65568 | tf_op jit(solution)/shard_map/ppermute | solution.py:44
  147.9 0.9 collective-permute-start.17
  148.9 1.0 convert_add_fusion
  149.9 1.0 convert_add_fusion.1
  151.1 1.6 collective-permute-start.14
  152.6 4.2 %collective-permute-start.23 = (bf16[128,512]{1,0:T(8,128)(2,1)S(1)}, bf16[128,512]{1,0:T(8,128)(2,1)S(1)}, u32[]{:S(2)}, u32[]{:S(2)}) collective-permute-start(bf16[128,512]{1,0:T(8,128)(2,1)S(1)} %pad_maximum_fusion.8), channel_id=1, source_target_pairs={{0,48},{16,32},{32,16},{48,0},{1,49},{17,33},{33,17},{49,1},{2,50}... | collective-permute-start | bytes 393224 | tf_op jit(solution)/shard_map/ppermute | solution.py:44
  156.9 1.6 collective-permute-start.15
  158.5 3.5 %collective-permute-done.15 = f32[8,2048]{1,0:T(8,128)S(1)} collective-permute-done((f32[8,2048]{1,0:T(8,128)S(1)}, f32[8,2048]{1,0:T(8,128)S(1)}, u32[]{:S(2)}, u32[]{:S(2)}) %collective-permute-start.15) | collective-permute-done | bytes 65568 | tf_op jit(solution)/shard_map/ppermute | solution.py:44
  162.4 3.9 %collective-permute-done.16 = f32[8,2048]{1,0:T(8,128)S(1)} collective-permute-done((f32[8,2048]{1,0:T(8,128)S(1)}, f32[8,2048]{1,0:T(8,128)S(1)}, u32[]{:S(2)}, u32[]{:S(2)}) %collective-permute-start.16) | collective-permute-done | bytes 65568 | tf_op jit(solution)/shard_map/ppermute | solution.py:44
  166.4 2.8 %collective-permute-start.22 = (bf16[128,512]{1,0:T(8,128)(2,1)S(1)}, bf16[128,512]{1,0:T(8,128)(2,1)S(1)}, u32[]{:S(2)}, u32[]{:S(2)}) collective-permute-start(bf16[128,512]{1,0:T(8,128)(2,1)S(1)} %pad_maximum_fusion.7), channel_id=1, source_target_pairs={{0,32},{16,48},{32,0},{48,16},{1,33},{17,49},{33,1},{49,17},{2,34}... | collective-permute-start | bytes 393224 | tf_op jit(solution)/shard_map/ppermute | solution.py:44
  169.2 1.9 collective-permute-start.21
  171.1 2.3 %collective-permute-start.20 = (f32[8,2048]{1,0:T(8,128)S(1)}, f32[8,2048]{1,0:T(8,128)S(1)}, u32[]{:S(2)}, u32[]{:S(2)}) collective-permute-start(f32[8,2048]{1,0:T(8,128)S(1)} %add.172), channel_id=1, source_target_pairs={{0,192},{64,128},{128,64},{192,0},{1,193},{65,129},{129,65},{193,1... | collective-permute-start | bytes 196616 | tf_op jit(solution)/shard_map/ppermute | solution.py:44
  173.5 3.2 %collective-permute-done.20 = f32[8,2048]{1,0:T(8,128)S(1)} collective-permute-done((f32[8,2048]{1,0:T(8,128)S(1)}, f32[8,2048]{1,0:T(8,128)S(1)}, u32[]{:S(2)}, u32[]{:S(2)}) %collective-permute-start.20) | collective-permute-done | bytes 65568 | tf_op jit(solution)/shard_map/ppermute | solution.py:44
  176.7 2.9 %collective-permute-done.21 = bf16[128,512]{1,0:T(8,128)(2,1)S(1)} collective-permute-done((bf16[128,512]{1,0:T(8,128)(2,1)S(1)}, bf16[128,512]{1,0:T(8,128)(2,1)S(1)}, u32[]{:S(2)}, u32[]{:S(2)}) %collective-permute-start.21) | collective-permute-done | bytes 131104 | tf_op jit(solution)/shard_map/ppermute | solution.py:44
  179.9 5.1 %collective-permute-done.24 = f32[8,2048]{1,0:T(8,128)S(1)} collective-permute-done((f32[8,2048]{1,0:T(8,128)S(1)}, f32[8,2048]{1,0:T(8,128)S(1)}, u32[]{:S(2)}, u32[]{:S(2)}) %collective-permute-start.24) | collective-permute-done | bytes 65568 | tf_op jit(solution)/shard_map/ppermute | solution.py:44
  185.2 0.7 maximum_bitcast_fusion.1
  185.9 0.7 maximum_bitcast_fusion
  186.7 4.8 %collective-permute-done.25 = f32[8,2048]{1,0:T(8,128)S(1)} collective-permute-done((f32[8,2048]{1,0:T(8,128)S(1)}, f32[8,2048]{1,0:T(8,128)S(1)}, u32[]{:S(2)}, u32[]{:S(2)}) %collective-permute-start.25) | collective-permute-done | bytes 65568 | tf_op jit(solution)/shard_map/ppermute | solution.py:44
  (151 shorter events, 7.5 us)
Async XLA Ops:
  0.6 1.6 copy-start
  2.2 124.9 %copy-start.35 = (pred[256]{0:T(512)(128)(4,1)}, pred[256]{0:T(512)(128)(4,1)S(1)}, u32[]{:S(2)}) copy-start(pred[256]{0:T(512)(128)(4,1)S(1)} %get-tuple-element.111) | copy-start | bytes 772
  4.3 6.3 %copy-start.31 = (bf16[2048,8]{0,1:T(8,128)(2,1)S(1)}, bf16[2048,8]{0,1:T(8,128)(2,1)}, u32[]{:S(2)}) copy-start(bf16[2048,8]{0,1:T(8,128)(2,1)} %param.10) | copy-start | bytes 98308
  4.3 6.8 %copy-start.34 = (s32[256,2]{0,1:T(2,128)S(1)}, s32[256,2]{0,1:T(2,128)}, u32[]{:S(2)}) copy-start(s32[256,2]{0,1:T(2,128)} %param.13) | copy-start | bytes 6148
  4.3 6.8 %copy-start.33 = (s32[256,2]{0,1:T(2,128)S(1)}, s32[256,2]{0,1:T(2,128)}, u32[]{:S(2)}) copy-start(s32[256,2]{0,1:T(2,128)} %param.15) | copy-start | bytes 6148
  4.3 31.5 %all-to-all-start.1 = ((bf16[8,64,2048]{2,1,0:T(8,128)(2,1)}), bf16[8,64,2048]{2,1,0:T(8,128)(2,1)S(1)}, u32[]{:S(2)}, u32[]{:S(2)}) async-start(bf16[8,64,2048]{2,1,0:T(8,128)(2,1)} %bitcast.48), calls=%async_computation.1 | async-start | bytes 4194304 | tf_op jit(solution)/shard_map/all_to_all | solution.py:48
  35.9 1.3 copy-start.1
  37.2 31.3 %all-to-all-start = ((bf16[8,64,2176]{2,1,0:T(8,128)(2,1)}), bf16[8,64,2176]{2,1,0:T(8,128)(2,1)S(1)}, u32[]{:S(2)}, u32[]{:S(2)}) async-start(bf16[8,64,2176]{2,1,0:T(8,128)(2,1)} %bitcast.47), calls=%async_computation | async-start | bytes 4456448 | tf_op jit(solution)/shard_map/all_to_all | solution.py:48
  42.5 26.0 %collective-permute-start = (bf16[512,2048]{1,0:T(8,128)(2,1)}, bf16[512,2048]{1,0:T(8,128)(2,1)}, u32[]{:S(2)}, u32[]{:S(2)}) collective-permute-start(bf16[512,2048]{1,0:T(8,128)(2,1)} %bitcast.40), channel_id=1, source_target_pairs={{0,8},{8,0},{1,9},{9,1},{2,10},{10,2},{3,11},{11,3},{4,12},{12,4},... | collective-permute-start | bytes 6291464 | tf_op jit(solution)/shard_map/ppermute | solution.py:44
  49.9 18.5 %collective-permute-start.1 = (bf16[512,1024]{1,0:T(8,128)(2,1)}, bf16[512,1024]{1,0:T(8,128)(2,1)}, u32[]{:S(2)}, u32[]{:S(2)}) collective-permute-start(bf16[512,1024]{1,0:T(8,128)(2,1)} %get-tuple-element.63.lm), channel_id=1, source_target_pairs={{0,8},{8,0},{1,9},{9,1},{2,10},{10,2},{3,11},{11,3},{4,12},{12,4},... | collective-permute-start | bytes 3145736 | tf_op jit(solution)/shard_map/ppermute | solution.py:44
  68.4 2.2 %copy-start.14 = (f32[512,2048]{1,0:T(8,128)S(1)}, f32[512,2048]{1,0:T(8,128)}, u32[]{:S(2)}) copy-start(f32[512,2048]{1,0:T(8,128)} %fusion.10.expert) | copy-start | bytes 12582916
  70.6 2.2 %copy-start.12 = (bf16[1,1024,2048]{2,1,0:T(8,128)(2,1)S(1)}, bf16[1,1024,2048]{2,1,0:T(8,128)(2,1)}, u32[]{:S(2)}) copy-start(bf16[1,1024,2048]{2,1,0:T(8,128)(2,1)} %param.12) | copy-start | bytes 12582916
  70.6 3.2 %copy-start.15 = (f32[512,1024]{1,0:T(8,128)S(1)}, f32[512,1024]{1,0:T(8,128)}, u32[]{:S(2)}) copy-start(f32[512,1024]{1,0:T(8,128)} %get-tuple-element.60.slope_ref) | copy-start | bytes 6291460
  71.9 5.7 %copy-start.8 = (bf16[512,1024]{1,0:T(8,128)(2,1)}, bf16[512,1024]{1,0:T(8,128)(2,1)S(1)}, u32[]{:S(2)}) copy-start(bf16[512,1024]{1,0:T(8,128)(2,1)S(1)} %get-tuple-element.78.rm) | copy-start | bytes 3145732
  71.9 5.7 %collective-permute-start.2 = (bf16[512,1024]{1,0:T(8,128)(2,1)S(1)}, bf16[512,1024]{1,0:T(8,128)(2,1)S(1)}, u32[]{:S(2)}, u32[]{:S(2)}) collective-permute-start(bf16[512,1024]{1,0:T(8,128)(2,1)S(1)} %get-tuple-element.58), channel_id=1, source_target_pairs={{0,8},{8,0},{1,9},{9,1},{2,10},{10,2},{3,11},{11,3},{4,12},{12,4},... | collective-permute-start | bytes 3145736 | tf_op jit(solution)/shard_map/ppermute | solution.py:44
  77.6 4.5 %copy-start.3 = (bf16[512,1024]{1,0:T(8,128)(2,1)}, bf16[512,1024]{1,0:T(8,128)(2,1)S(1)}, u32[]{:S(2)}) copy-start(bf16[512,1024]{1,0:T(8,128)(2,1)S(1)} %get-tuple-element.81.rm.grad) | copy-start | bytes 3145732
  77.6 14.1 %collective-permute-start.3 = (bf16[512,512]{1,0:T(8,128)(2,1)}, bf16[512,512]{1,0:T(8,128)(2,1)}, u32[]{:S(2)}, u32[]{:S(2)}) collective-permute-start(bf16[512,512]{1,0:T(8,128)(2,1)} %get-tuple-element.71), channel_id=1, source_target_pairs={{0,8},{8,0},{1,9},{9,1},{2,10},{10,2},{3,11},{11,3},{4,12},{12,4},... | collective-permute-start | bytes 1572872 | tf_op jit(solution)/shard_map/ppermute | solution.py:44
  77.6 4.5 %copy-start.10 = (bf16[512,1024]{1,0:T(8,128)(2,1)}, bf16[512,1024]{1,0:T(8,128)(2,1)S(1)}, u32[]{:S(2)}) copy-start(bf16[512,1024]{1,0:T(8,128)(2,1)S(1)} %collective-permute-done.2.ro) | copy-start | bytes 3145732
  77.6 14.1 %copy-start.2 = (bf16[8,64,2048]{2,1,0:T(8,128)(2,1)S(1)}, bf16[8,64,2048]{2,1,0:T(8,128)(2,1)}, u32[]{:S(2)}) copy-start(bf16[8,64,2048]{2,1,0:T(8,128)(2,1)} %copy-done.1) | copy-start | bytes 6291460
  82.1 36.2 %collective-permute-start.4 = (bf16[512,512]{1,0:T(8,128)(2,1)}, bf16[512,512]{1,0:T(8,128)(2,1)}, u32[]{:S(2)}, u32[]{:S(2)}) collective-permute-start(bf16[512,512]{1,0:T(8,128)(2,1)} %get-tuple-element.66), channel_id=1, source_target_pairs={{0,64},{64,0},{128,192},{192,128},{1,65},{65,1},{129,193},{193,129... | collective-permute-start | bytes 1572872 | tf_op jit(solution)/shard_map/ppermute | solution.py:44
  83.7 34.6 %collective-permute-start.5 = (bf16[512,512]{1,0:T(8,128)(2,1)}, bf16[512,512]{1,0:T(8,128)(2,1)}, u32[]{:S(2)}, u32[]{:S(2)}) collective-permute-start(bf16[512,512]{1,0:T(8,128)(2,1)} %get-tuple-element.67), channel_id=1, source_target_pairs={{0,192},{64,128},{128,64},{192,0},{1,193},{65,129},{129,65},{193,1... | collective-permute-start | bytes 1572872 | tf_op jit(solution)/shard_map/ppermute | solution.py:44
  86.7 15.4 %all-to-all-start.2 = ((bf16[8,1,64]{2,1,0:T(2,128)(2,1)}), bf16[8,1,64]{2,1,0:T(2,128)(2,1)S(1)}, u32[]{:S(2)}, u32[]{:S(2)}) async-start(bf16[8,1,64]{2,1,0:T(2,128)(2,1)} %all_to_all.20), calls=%async_computation.2 | async-start | bytes 8192 | tf_op jit(solution)/shard_map/all_to_all | solution.py:48
  91.7 1.2 copy-start.4
  92.9 4.8 %copy-start.5 = (bf16[512,1024]{1,0:T(8,128)(2,1)S(1)}, bf16[512,1024]{1,0:T(8,128)(2,1)}, u32[]{:S(2)}) copy-start(bf16[512,1024]{1,0:T(8,128)(2,1)} %copy-done.3) | copy-start | bytes 3145732
  92.9 4.8 %copy-start.13 = (bf16[1,2048,1024]{2,1,0:T(8,128)(2,1)S(1)}, bf16[1,2048,1024]{2,1,0:T(8,128)(2,1)}, u32[]{:S(2)}) copy-start(bf16[1,2048,1024]{2,1,0:T(8,128)(2,1)} %param.11) | copy-start | bytes 12582916
  100.7 1.4 copy-start.7
  102.2 37.5 %all-to-all-start.3 = ((bf16[8,64,2048]{2,1,0:T(8,128)(2,1)}), bf16[8,64,2048]{2,1,0:T(8,128)(2,1)}, u32[]{:S(2)}, u32[]{:S(2)}) async-start(bf16[8,64,2048]{2,1,0:T(8,128)(2,1)} %bitcast.44), calls=%async_computation.3 | async-start | bytes 4194304 | tf_op jit(solution)/shard_map/all_to_all | solution.py:48
  107.9 6.6 %copy-start.6 = (bf16[512,1024]{1,0:T(8,128)(2,1)S(1)}, bf16[512,1024]{1,0:T(8,128)(2,1)}, u32[]{:S(2)}) copy-start(bf16[512,1024]{1,0:T(8,128)(2,1)} %copy-done.3) | copy-start | bytes 3145732
  107.9 17.6 %collective-permute-start.8 = (bf16[1024,256]{1,0:T(8,128)(2,1)}, bf16[1024,256]{1,0:T(8,128)(2,1)S(1)}, u32[]{:S(2)}, u32[]{:S(2)}) collective-permute-start(bf16[1024,256]{1,0:T(8,128)(2,1)} %copy-done.25), channel_id=1, source_target_pairs={{0,64},{64,0},{128,192},{192,128},{1,65},{65,1},{129,193},{193,129... | collective-permute-start | bytes 1572872 | tf_op jit(solution)/shard_map/ppermute | solution.py:44
  108.6 16.9 %collective-permute-start.9 = (bf16[1024,256]{1,0:T(8,128)(2,1)}, bf16[1024,256]{1,0:T(8,128)(2,1)S(1)}, u32[]{:S(2)}, u32[]{:S(2)}) collective-permute-start(bf16[1024,256]{1,0:T(8,128)(2,1)} %copy-done.24), channel_id=1, source_target_pairs={{0,192},{64,128},{128,64},{192,0},{1,193},{65,129},{129,65},{193,1... | collective-permute-start | bytes 1572872 | tf_op jit(solution)/shard_map/ppermute | solution.py:44
  114.5 3.9 %copy-start.22 = (f32[512,512]{1,0:T(8,128)}, f32[512,512]{1,0:T(8,128)S(1)}, u32[]{:S(2)}) copy-start(f32[512,512]{1,0:T(8,128)S(1)} %get-tuple-element.84) | copy-start | bytes 3145732
  114.5 7.0 %copy-start.20 = (f32[512,512]{1,0:T(8,128)}, f32[512,512]{1,0:T(8,128)S(1)}, u32[]{:S(2)}) copy-start(f32[512,512]{1,0:T(8,128)S(1)} %get-tuple-element.79) | copy-start | bytes 3145732
  118.3 8.8 %copy-start.16 = (f32[1024,256]{1,0:T(8,128)}, f32[1024,256]{1,0:T(8,128)S(1)}, u32[]{:S(2)}) copy-start(f32[1024,256]{1,0:T(8,128)S(1)} %get-tuple-element.82) | copy-start | bytes 3145732
  118.3 8.8 %copy-start.18 = (f32[1024,256]{1,0:T(8,128)}, f32[1024,256]{1,0:T(8,128)S(1)}, u32[]{:S(2)}) copy-start(f32[1024,256]{1,0:T(8,128)S(1)} %get-tuple-element.88) | copy-start | bytes 3145732
  120.3 10.9 %copy-start.23 = (f32[512,512]{1,0:T(8,128)S(1)}, f32[512,512]{1,0:T(8,128)}, u32[]{:S(2)}) copy-start(f32[512,512]{1,0:T(8,128)} %copy-done.22) | copy-start | bytes 3145732
  120.3 9.8 %collective-permute-start.7 = (bf16[256,512]{1,0:T(8,128)(2,1)}, bf16[256,512]{1,0:T(8,128)(2,1)S(1)}, u32[]{:S(2)}, u32[]{:S(2)}) collective-permute-start(bf16[256,512]{1,0:T(8,128)(2,1)} %add_convert_fusion.2), channel_id=1, source_target_pairs={{0,64},{64,0},{128,192},{192,128},{1,65},{65,1},{129,193},{193,129... | collective-permute-start | bytes 786440 | tf_op jit(solution)/shard_map/ppermute | solution.py:44
  123.3 7.9 %copy-start.21 = (f32[512,512]{1,0:T(8,128)S(1)}, f32[512,512]{1,0:T(8,128)}, u32[]{:S(2)}) copy-start(f32[512,512]{1,0:T(8,128)} %copy-done.20) | copy-start | bytes 3145732
  123.3 7.9 %collective-permute-start.6 = (bf16[256,512]{1,0:T(8,128)(2,1)}, bf16[256,512]{1,0:T(8,128)(2,1)}, u32[]{:S(2)}, u32[]{:S(2)}) collective-permute-start(bf16[256,512]{1,0:T(8,128)(2,1)} %add_convert_fusion.3), channel_id=1, source_target_pairs={{0,192},{64,128},{128,64},{192,0},{1,193},{65,129},{129,65},{193,1... | collective-permute-start | bytes 786440 | tf_op jit(solution)/shard_map/ppermute | solution.py:44
  125.5 1.7 copy-start.27
  125.5 1.9 %copy-start.29 = (bf16[1024,256]{1,0:T(8,128)(2,1)}, bf16[1024,256]{1,0:T(8,128)(2,1)S(1)}, u32[]{:S(2)}) copy-start(bf16[1024,256]{1,0:T(8,128)(2,1)S(1)} %collective-permute-done.9) | copy-start | bytes 1572868
  127.7 1.6 collective-permute-start.10
  127.8 21.0 %collective-permute-start.13 = (bf16[512,256]{1,0:T(8,128)(2,1)}, bf16[512,256]{1,0:T(8,128)(2,1)}, u32[]{:S(2)}, u32[]{:S(2)}) collective-permute-start(bf16[512,256]{1,0:T(8,128)(2,1)} %add_convert_fusion), channel_id=1, source_target_pairs={{0,64},{64,0},{128,192},{192,128},{1,65},{65,1},{129,193},{193,129... | collective-permute-start | bytes 786440 | tf_op jit(solution)/shard_map/ppermute | solution.py:44
  128.8 20.0 %collective-permute-start.12 = (bf16[512,256]{1,0:T(8,128)(2,1)}, bf16[512,256]{1,0:T(8,128)(2,1)}, u32[]{:S(2)}, u32[]{:S(2)}) collective-permute-start(bf16[512,256]{1,0:T(8,128)(2,1)} %add_convert_fusion.1), channel_id=1, source_target_pairs={{0,192},{64,128},{128,64},{192,0},{1,193},{65,129},{129,65},{193,1... | collective-permute-start | bytes 786440 | tf_op jit(solution)/shard_map/ppermute | solution.py:44
  130.2 9.6 %copy-start.36 = (pred[256]{0:T(512)(128)(4,1)S(1)}, pred[256]{0:T(512)(128)(4,1)}, u32[]{:S(2)}) copy-start(pred[256]{0:T(512)(128)(4,1)} %copy-done.35) | copy-start | bytes 772
  132.6 36.5 %collective-permute-start.19 = (bf16[64,1024]{1,0:T(8,128)(2,1)S(1)}, bf16[64,1024]{1,0:T(8,128)(2,1)S(1)}, u32[]{:S(2)}, u32[]{:S(2)}) collective-permute-start(bf16[64,1024]{1,0:T(8,128)(2,1)S(1)} %pad_maximum_fusion.5), channel_id=1, source_target_pairs={{0,48},{16,32},{32,16},{48,0},{1,49},{17,33},{33,17},{49,1},{2,50}... | collective-permute-start | bytes 393224 | tf_op jit(solution)/shard_map/ppermute | solution.py:44
  138.1 33.0 %collective-permute-start.18 = (bf16[64,1024]{1,0:T(8,128)(2,1)S(1)}, bf16[64,1024]{1,0:T(8,128)(2,1)S(1)}, u32[]{:S(2)}, u32[]{:S(2)}) collective-permute-start(bf16[64,1024]{1,0:T(8,128)(2,1)S(1)} %pad_maximum_fusion.4), channel_id=1, source_target_pairs={{0,32},{16,48},{32,0},{48,16},{1,33},{17,49},{33,1},{49,17},{2,34}... | collective-permute-start | bytes 393224 | tf_op jit(solution)/shard_map/ppermute | solution.py:44
  139.7 2.4 %copy-start.32 = (bf16[2048,8]{0,1:T(8,128)(2,1)S(1)}, bf16[2048,8]{0,1:T(8,128)(2,1)}, u32[]{:S(2)}) copy-start(bf16[2048,8]{0,1:T(8,128)(2,1)} %param.10) | copy-start | bytes 98308
  142.1 6.7 %copy-start.19 = (f32[1024,256]{1,0:T(8,128)S(1)}, f32[1024,256]{1,0:T(8,128)}, u32[]{:S(2)}) copy-start(f32[1024,256]{1,0:T(8,128)} %copy-done.18) | copy-start | bytes 3145732
  142.1 6.7 %copy-start.30 = (bf16[1024,256]{1,0:T(8,128)(2,1)S(1)}, bf16[1024,256]{1,0:T(8,128)(2,1)}, u32[]{:S(2)}) copy-start(bf16[1024,256]{1,0:T(8,128)(2,1)} %copy-done.29) | copy-start | bytes 1572868
  142.1 7.7 %copy-start.17 = (f32[1024,256]{1,0:T(8,128)S(1)}, f32[1024,256]{1,0:T(8,128)}, u32[]{:S(2)}) copy-start(f32[1024,256]{1,0:T(8,128)} %copy-done.16) | copy-start | bytes 3145732
  142.1 7.7 %copy-start.28 = (bf16[1024,256]{1,0:T(8,128)(2,1)S(1)}, bf16[1024,256]{1,0:T(8,128)(2,1)}, u32[]{:S(2)}) copy-start(bf16[1024,256]{1,0:T(8,128)(2,1)} %copy-done.27) | copy-start | bytes 1572868
  143.6 4.3 %collective-permute-start.11 = (f32[8,2048]{1,0:T(8,128)S(1)}, f32[8,2048]{1,0:T(8,128)S(1)}, u32[]{:S(2)}, u32[]{:S(2)}) collective-permute-start(f32[8,2048]{1,0:T(8,128)S(1)} %add.160), channel_id=1, source_target_pairs={{0,2},{2,0},{4,6},{6,4},{1,3},{3,1},{5,7},{7,5},{8,10},{10,8},{12,... | collective-permute-start | bytes 196616 | tf_op jit(solution)/shard_map/ppermute | solution.py:44
  147.9 23.2 %collective-permute-start.17 = (bf16[64,1024]{1,0:T(8,128)(2,1)S(1)}, bf16[64,1024]{1,0:T(8,128)(2,1)S(1)}, u32[]{:S(2)}, u32[]{:S(2)}) collective-permute-start(bf16[64,1024]{1,0:T(8,128)(2,1)S(1)} %pad_maximum_fusion.3), channel_id=1, source_target_pairs={{0,16},{16,0},{32,48},{48,32},{1,17},{17,1},{33,49},{49,33},{2,18}... | collective-permute-start | bytes 393224 | tf_op jit(solution)/shard_map/ppermute | solution.py:44
  151.1 5.8 %collective-permute-start.14 = (f32[8,2048]{1,0:T(8,128)S(1)}, f32[8,2048]{1,0:T(8,128)S(1)}, u32[]{:S(2)}, u32[]{:S(2)}) collective-permute-start(f32[8,2048]{1,0:T(8,128)S(1)} %add.165), channel_id=1, source_target_pairs={{0,6},{2,4},{4,2},{6,0},{1,7},{3,5},{5,3},{7,1},{8,14},{10,12},{12... | collective-permute-start | bytes 196616 | tf_op jit(solution)/shard_map/ppermute | solution.py:44
  152.6 24.1 %collective-permute-start.23 = (bf16[128,512]{1,0:T(8,128)(2,1)S(1)}, bf16[128,512]{1,0:T(8,128)(2,1)S(1)}, u32[]{:S(2)}, u32[]{:S(2)}) collective-permute-start(bf16[128,512]{1,0:T(8,128)(2,1)S(1)} %pad_maximum_fusion.8), channel_id=1, source_target_pairs={{0,48},{16,32},{32,16},{48,0},{1,49},{17,33},{33,17},{49,1},{2,50}... | collective-permute-start | bytes 393224 | tf_op jit(solution)/shard_map/ppermute | solution.py:44
  156.9 5.1 %collective-permute-start.15 = (f32[8,2048]{1,0:T(8,128)S(1)}, f32[8,2048]{1,0:T(8,128)S(1)}, u32[]{:S(2)}, u32[]{:S(2)}) collective-permute-start(f32[8,2048]{1,0:T(8,128)S(1)} %add.170), channel_id=1, source_target_pairs={{0,1},{1,0},{2,3},{3,2},{4,5},{5,4},{6,7},{7,6},{8,9},{9,8},{10,11... | collective-permute-start | bytes 196616 | tf_op jit(solution)/shard_map/ppermute | solution.py:44
  162.0 4.4 %collective-permute-start.16 = (f32[8,2048]{1,0:T(8,128)S(1)}, f32[8,2048]{1,0:T(8,128)S(1)}, u32[]{:S(2)}, u32[]{:S(2)}) collective-permute-start(f32[8,2048]{1,0:T(8,128)S(1)} %add.171), channel_id=1, source_target_pairs={{0,64},{64,0},{128,192},{192,128},{1,65},{65,1},{129,193},{193,129... | collective-permute-start | bytes 196616 | tf_op jit(solution)/shard_map/ppermute | solution.py:44
  166.4 10.4 %collective-permute-start.22 = (bf16[128,512]{1,0:T(8,128)(2,1)S(1)}, bf16[128,512]{1,0:T(8,128)(2,1)S(1)}, u32[]{:S(2)}, u32[]{:S(2)}) collective-permute-start(bf16[128,512]{1,0:T(8,128)(2,1)S(1)} %pad_maximum_fusion.7), channel_id=1, source_target_pairs={{0,32},{16,48},{32,0},{48,16},{1,33},{17,49},{33,1},{49,17},{2,34}... | collective-permute-start | bytes 393224 | tf_op jit(solution)/shard_map/ppermute | solution.py:44
  169.2 10.4 %collective-permute-start.21 = (bf16[128,512]{1,0:T(8,128)(2,1)S(1)}, bf16[128,512]{1,0:T(8,128)(2,1)S(1)}, u32[]{:S(2)}, u32[]{:S(2)}) collective-permute-start(bf16[128,512]{1,0:T(8,128)(2,1)S(1)} %pad_maximum_fusion.6), channel_id=1, source_target_pairs={{0,16},{16,0},{32,48},{48,32},{1,17},{17,1},{33,49},{49,33},{2,18}... | collective-permute-start | bytes 393224 | tf_op jit(solution)/shard_map/ppermute | solution.py:44
  171.1 5.6 %collective-permute-start.20 = (f32[8,2048]{1,0:T(8,128)S(1)}, f32[8,2048]{1,0:T(8,128)S(1)}, u32[]{:S(2)}, u32[]{:S(2)}) collective-permute-start(f32[8,2048]{1,0:T(8,128)S(1)} %add.172), channel_id=1, source_target_pairs={{0,192},{64,128},{128,64},{192,0},{1,193},{65,129},{129,65},{193,1... | collective-permute-start | bytes 196616 | tf_op jit(solution)/shard_map/ppermute | solution.py:44
  173.4 11.7 %collective-permute-start.27 = (f32[32,1024]{1,0:T(8,128)S(1)}, f32[32,1024]{1,0:T(8,128)S(1)}, u32[]{:S(2)}, u32[]{:S(2)}) collective-permute-start(f32[32,1024]{1,0:T(8,128)S(1)} %constant_dynamic-slice_fusion), channel_id=1, source_target_pairs={{0,8},{8,0},{1,9},{9,1},{2,10},{10,2},{3,11},{11,3},{4,12},{12,4},... | collective-permute-start | bytes 393224 | tf_op jit(solution)/shard_map/ppermute | solution.py:44
  179.7 5.4 %collective-permute-start.24 = (f32[8,2048]{1,0:T(8,128)S(1)}, f32[8,2048]{1,0:T(8,128)S(1)}, u32[]{:S(2)}, u32[]{:S(2)}) collective-permute-start(f32[8,2048]{1,0:T(8,128)S(1)} %add.180), channel_id=1, source_target_pairs={{0,16},{16,0},{32,48},{48,32},{1,17},{17,1},{33,49},{49,33},{2,18}... | collective-permute-start | bytes 196616 | tf_op jit(solution)/shard_map/ppermute | solution.py:44
  179.8 6.1 %collective-permute-start.26 = (f32[64,512]{1,0:T(8,128)S(1)}, f32[64,512]{1,0:T(8,128)S(1)}, u32[]{:S(2)}, u32[]{:S(2)}) collective-permute-start(f32[64,512]{1,0:T(8,128)S(1)} %constant_dynamic-slice_fusion.1), channel_id=1, source_target_pairs={{0,8},{8,0},{1,9},{9,1},{2,10},{10,2},{3,11},{11,3},{4,12},{12,4},... | collective-permute-start | bytes 393224 | tf_op jit(solution)/shard_map/ppermute | solution.py:44
  185.0 6.5 %collective-permute-start.25 = (f32[8,2048]{1,0:T(8,128)S(1)}, f32[8,2048]{1,0:T(8,128)S(1)}, u32[]{:S(2)}, u32[]{:S(2)}) collective-permute-start(f32[8,2048]{1,0:T(8,128)S(1)} %add.188), channel_id=1, source_target_pairs={{0,48},{16,32},{32,16},{48,0},{1,49},{17,33},{33,17},{49,1},{2,50}... | collective-permute-start | bytes 196616 | tf_op jit(solution)/shard_map/ppermute | solution.py:44
  (5 other events, 5.3 us)

commit v5 on v4

v5 whole, which is shorter than its diff:
```python
import jax
import jax.numpy as jnp
from jax import lax
from jax.experimental import pallas as pl
from jax.experimental.pallas import tpu as pltpu
from jax.sharding import Mesh, PartitionSpec as P

FINE = ("y", "zh", "core", "x", "zl")
FINE_SHAPE = (4, 4, 2, 4, 2)
GROUP = ("x", "zl")
EXTRA = 128
ROUTER_STEPS = (
    ("core", 1),
    ("x", 1),
    ("x", 3),
    ("zl", 1),
    ("y", 1),
    ("y", 3),
    ("zh", 1),
    ("zh", 3),
)
VMEM_LIMIT = 14 * 1024 * 1024
F32 = jnp.float32
BF16 = jnp.bfloat16


def gelu_parts(hidden_pre):
    normal_cdf = 0.5 * (1.0 + jax.scipy.special.erf(hidden_pre * 0.7071067811865476))
    normal_pdf = jnp.exp(-0.5 * hidden_pre * hidden_pre) * 0.3989422804014327
    return (normal_cdf, normal_pdf)


def contract_rows(left, right):
    return lax.dot_general(left, right, (((0,), (0,)), ((), ())), preferred_element_type=F32)


def contract_cols(left, right):
    return lax.dot_general(left, right, (((1,), (1,)), ((), ())), preferred_element_type=F32)


def swap(values, axis, mask):
    size = lax.axis_size(axis)
    return lax.ppermute(values, axis, [(i, i ^ mask) for i in range(size)])


def exchange(values, axes):
    return lax.all_to_all(values, axes, split_axis=0, concat_axis=0, tiled=True)


def tie(*values):
    return lax.optimization_barrier(values)


def call(body, pos, inputs, outputs):
    vmem = pl.BlockSpec(memory_space=pltpu.VMEM)
    return pl.pallas_call(
        body,
        in_specs=[pl.BlockSpec(memory_space=pltpu.SMEM)] + [vmem] * len(inputs),
        out_specs=[vmem] * len(outputs),
        out_shape=[jax.ShapeDtypeStruct(shape, dtype) for shape, dtype in outputs],
        cost_estimate=pl.CostEstimate(flops=1000, bytes_accessed=1000, transcendentals=0),
        compiler_params=pltpu.CompilerParams(vmem_limit_bytes=VMEM_LIMIT),
    )(pos, *inputs)


def gate_of(pos, lanes):
    lane = lax.broadcasted_iota(jnp.int32, lanes.shape, 1)
    return jnp.sum(jnp.where(lane == pos[2], lanes.astype(F32), 0.0), axis=1, keepdims=True)


def scale_grads(pos, received, expert_out):
    slots, wide = received.shape
    width = wide - EXTRA
    half = width // 2
    rows = slots // 4

    def body(pos_ref, rec, expert, mine, give, gate_grad):
        core = pos_ref[1]
        for r in range(0, slots, rows):
            at = slice(r, r + rows)
            gate = gate_of(pos_ref, rec[at, width:])
            for out, which in ((mine, core), (give, 1 - core)):
                start = pl.multiple_of(which * half, half)
                out[at, :] = (gate * rec[at, pl.ds(start, half)].astype(F32)).astype(BF16)
            gate_grad[at, :] = jnp.sum(
                expert[at, :].astype(F32) * rec[at, :width].astype(F32),
                axis=1,
                keepdims=True,
            )

    return call(
        body,
        pos,
        [received, expert_out],
        [((slots, half), BF16), ((slots, half), BF16), ((slots, 1), F32)],
    )


def pre_grads(pos, received, weight_out, slope):
    slots, wide = received.shape
    hidden, width = weight_out.shape
    step = hidden // 4

    def body(pos_ref, rec, weight, slope_ref, grad_pre, give):
        gate = gate_of(pos_ref, rec[:, width:])
        for i in range(4):
            at = slice(i * step, (i + 1) * step)
            grad_act = lax.dot_general(
                rec[:, :width], weight[at, :], (((1,), (1,)), ((), ())), preferred_element_type=F32
            )
            grad_pre[:, at] = (gate * grad_act * slope_ref[:, at]).astype(BF16)
        start = pl.multiple_of((1 - pos_ref[1]) * (hidden // 2), hidden // 2)
        give[...] = grad_pre[:, pl.ds(start, hidden // 2)]

    return call(
        body,
        pos,
        [received, weight_out, slope],
        [((slots, hidden), BF16), ((slots, hidden // 2), BF16)],
    )


def row_products(pos_ref, refs, own_offset, masks, width, cols):
    lm, lo, rm, ro = refs
    dims = (((0,), (0,)), ((), ()))
    for i in range(2):
        own = pl.multiple_of((own_offset * pos_ref[1] + i) * cols, cols)
        for j in range(2):
            start = pl.multiple_of((pos_ref[0] ^ masks[i][j]) * width, width)
            value = lax.dot_general(
                lm[:, pl.ds(start, width)],
                rm[:, pl.ds(own, cols)],
                dims,
                preferred_element_type=F32,
            )
            value = value + lax.dot_general(
                lo[:, pl.ds(start, width)],
                ro[:, i * cols : (i + 1) * cols],
                dims,
                preferred_element_type=F32,
            )
            yield i, j, value


def sent_parts(pos, left, right, own_offset):
    width = left[0].shape[1] // 4
    cols = right[1].shape[1] // 2

    def body(pos_ref, lm, lo, rm, ro, *outs):
        refs = (lm, lo, rm, ro)
        for i, j, value in row_products(
            pos_ref, refs, own_offset, ((1, 2), (3, 2)), width, cols
        ):
            outs[i][j * width : (j + 1) * width, :] = value.astype(BF16)

    return call(body, pos, [*left, *right], [((2 * width, cols), BF16)] * 2)


def kept_parts(pos, left, right, own_offset, got):
    width = left[0].shape[1] // 4
    cols = right[1].shape[1] // 2

    def body(pos_ref, lm, lo, rm, ro, got_a, got_b, near_a, near_b, far_a, far_b):
        refs = (lm, lo, rm, ro)
        for i, j, value in row_products(
            pos_ref, refs, own_offset, ((0, 3), (0, 1)), width, cols
        ):
            value = value + (got_a, got_b)[i][j * width : (j + 1) * width, :].astype(F32)
            if j == 0:
                (near_a, near_b)[i][...] = value
            else:
                (far_a, far_b)[i][...] = value.astype(BF16)

    return call(
        body,
        pos,
        [*left, *right, *got],
        [((width, cols), F32)] * 2 + [((width, cols), BF16)] * 2,
    )


def zh_pieces(pos, near, far, scale):
    rows, cols = near[0].shape
    block = rows // 4

    def body(pos_ref, near_a, near_b, far_a, far_b, mine, *pieces):
        for r in range(4):
            at = pl.ds(pl.multiple_of((pos_ref[3] ^ r) * block, block), block)
            for i, (n, f) in enumerate(((near_a, far_a), (near_b, far_b))):
                value = (n[at, :] + f[at, :].astype(F32)) * scale
                here = slice(i * cols, (i + 1) * cols)
                if r == 0:
                    mine[:, here] = value
                else:
                    pieces[r - 1][:, here] = value.astype(BF16)

    shape = (block, 2 * cols)
    return call(body, pos, [*near, *far], [(shape, F32)] + [(shape, BF16)] * 3)


def zh_total(pos, mine, got):
    rows, cols = mine.shape
    share = rows // 2

    def body(pos_ref, own, one, two, three, keep, give):
        core = pos_ref[1]
        for out, which in ((keep, core), (give, 1 - core)):
            at = pl.ds(pl.multiple_of(which * share, share), share)
            value = own[at, :] + one[at, :].astype(F32)
            out[...] = value + two[at, :].astype(F32) + three[at, :].astype(F32)

    return call(body, pos, [mine, *got], [((share, cols), F32)] * 2)


def both_halves(pos, keep, got):
    rows, cols = keep.shape

    def body(pos_ref, own, other, out):
        core = pos_ref[1]
        out[:, pl.ds(pl.multiple_of(core * cols, cols), cols)] = own[...]
        out[:, pl.ds(pl.multiple_of((1 - core) * cols, cols), cols)] = other[...]

    return call(body, pos, [keep, got], [((rows, 2 * cols), F32)])[0][None]


def token_grads(pos, dispatch, flat_grads, logit_lanes, weight_lanes):
    rows, width = dispatch.shape[1], flat_grads.shape[1]
    step = width // 4

    def body(pos_ref, disp, flat, logit, weight, out):
        for i in range(4):
            at = slice(i * step, (i + 1) * step)
            value = lax.dot_general(
                disp[...], flat[:, at], (((0,), (0,)), ((), ())), preferred_element_type=F32
            )
            value = value + lax.dot_general(
                logit[...], weight[at, :], (((1,), (1,)), ((), ())), preferred_element_type=F32
            )
            out[:, at] = value.astype(BF16)

    return call(
        body, pos, [dispatch, flat_grads, logit_lanes, weight_lanes], [((rows, width), BF16)]
    )[0]


def slot_grads_of(pos, grad_pre, weight_in):
    slots, hidden = grad_pre.shape
    width = weight_in.shape[0]
    step = width // 4

    def body(pos_ref, grad, weight, out):
        for i in range(4):
            at = slice(i * step, (i + 1) * step)
            out[:, at] = lax.dot_general(
                grad[...], weight[at, :], (((1,), (1,)), ((), ())), preferred_element_type=F32
            ).astype(BF16)

    return call(body, pos, [grad_pre, weight_in], [((slots, width), BF16)])[0]


def per_device(
    tokens, grad_out, router_weight, weight_in, weight_out, expert_ids, slot_index, keep_mask
):
    tok_rows, model_width = tokens.shape
    experts = 8
    weight_in = weight_in[0]
    weight_out = weight_out[0]
    capacity = tok_rows * expert_ids.shape[1] // experts
    slot_count = experts * capacity
    grad_scale = float(tok_rows * 256) ** (-0.5)
    core = lax.axis_index("core")
    my_y = lax.axis_index("y")

    target = expert_ids * capacity + slot_index
    slot_iota = jnp.arange(slot_count, dtype=jnp.int32)[:, None]
    first_hit = (slot_iota == target[None, :, 0]) & (keep_mask[None, :, 0] == 1)
    second_hit = (slot_iota == target[None, :, 1]) & (keep_mask[None, :, 1] == 1)
    dispatch = (first_hit | second_hit).astype(BF16)

    send_tokens = jnp.dot(dispatch, tokens, preferred_element_type=F32).astype(BF16)
    slot_tokens = exchange(
        send_tokens.reshape(experts, capacity, model_width), GROUP
    ).reshape(slot_count, model_width)

    logits = jnp.dot(tokens, router_weight, preferred_element_type=F32)
    exp_logits = jnp.exp(logits)
    router_probs = exp_logits / jnp.sum(exp_logits, axis=1, keepdims=True)
    picked = expert_ids[:, :, None] == jnp.arange(experts, dtype=jnp.int32)[None, None, :]
    chosen = jnp.sum(jnp.where(picked, router_probs[:, None, :], 0.0), axis=2)
    keep_float = keep_mask.astype(F32)
    denominator = jnp.sum(keep_float * chosen, axis=1) + (1.0 - jnp.max(keep_float, axis=1))
    combine = keep_float * chosen / denominator[:, None]
    gate_lanes = jnp.sum(jnp.where(picked, combine[:, :, None], 0.0), axis=1).astype(BF16)
    gate_lanes = jnp.pad(gate_lanes, ((0, 0), (0, EXTRA - experts)))
    send_grads = jnp.dot(dispatch, grad_out, preferred_element_type=F32).astype(BF16)
    send_gates = jnp.dot(dispatch, gate_lanes, preferred_element_type=F32).astype(BF16)
    received = exchange(
        jnp.concatenate([send_grads, send_gates], axis=1).reshape(
            experts, capacity, model_width + EXTRA
        ),
        GROUP,
    ).reshape(slot_count, model_width + EXTRA)
    other_tokens = swap(slot_tokens, "core", 1)
    hidden_pre = jnp.dot(slot_tokens, weight_in, preferred_element_type=F32)
    normal_cdf, normal_pdf = gelu_parts(hidden_pre)
    hidden_act = (hidden_pre * normal_cdf).astype(BF16)
    act_slope = normal_cdf + hidden_pre * normal_pdf
    other_act = swap(hidden_act, "core", 1)
    left_in = (slot_tokens, other_tokens)
    left_out = (hidden_act, other_act)
    pos = jnp.stack([my_y, core, lax.axis_index(GROUP), lax.axis_index("zh")]).astype(jnp.int32)

    expert_out = jnp.dot(hidden_act, weight_out, preferred_element_type=F32).astype(BF16)
    weight_lanes = jnp.pad(router_weight, ((0, 0), (0, EXTRA - experts)))

    received, left_in, left_out, act_slope, expert_out = tie(
        received, left_in, left_out, act_slope, expert_out
    )
    my_out, give_out, slot_combine_grad = scale_grads(pos, received, expert_out)
    other_out = swap(give_out, "core", 1)
    flat_combine = exchange(
        slot_combine_grad.astype(BF16).reshape(experts, capacity), GROUP
    ).reshape(slot_count)
    received, _ = tie(received, give_out)
    grad_pre, give_in = pre_grads(pos, received, weight_out, act_slope)
    other_in = swap(give_in, "core", 1)

    sent = sent_parts(pos, left_out, (my_out, other_out), 0)
    got_out = (swap(sent[0], "y", 1), swap(sent[1], "y", 3))
    pre_for_slots, _ = tie(grad_pre, sent)
    grad_slots = slot_grads_of(pos, pre_for_slots, weight_in)
    grad_slots, flat_combine = tie(grad_slots, flat_combine)
    flat_grads = exchange(
        grad_slots.reshape(experts, capacity, model_width), GROUP
    ).reshape(slot_count, model_width)
    grad_pre, flat_combine, _ = tie(grad_pre, flat_combine, grad_slots)
    sent = sent_parts(pos, left_in, (grad_pre, other_in), 2)
    got_in = (swap(sent[0], "y", 1), swap(sent[1], "y", 3))
    my_out, flat_combine, _ = tie(my_out, flat_combine, sent)

    combine_wide = flat_combine.astype(F32)[:, None]
    combine_grad = jnp.stack(
        [
            jnp.sum(jnp.where(first_hit, combine_wide, 0.0), axis=0),
            jnp.sum(jnp.where(second_hit, combine_wide, 0.0), axis=0),
        ],
        axis=1,
    )
    weighted_sum = jnp.sum(combine_grad * combine, axis=1)
    chosen_grad = keep_float * (combine_grad - weighted_sum[:, None]) / denominator[:, None]
    probs_grad = jnp.sum(jnp.where(picked, chosen_grad[:, :, None], 0.0), axis=1)
    logit_grad = router_probs * (
        probs_grad - jnp.sum(probs_grad * router_probs, axis=1, keepdims=True)
    )
    logit_b = logit_grad.astype(BF16)

    logit_lanes = jnp.pad(logit_b, ((0, 0), (0, EXTRA - experts)))

    router_part = contract_rows(logit_b, tokens) * grad_scale

    def router_step(step, value, *until):
        got = swap(value, *ROUTER_STEPS[step])
        value, got, _ = tie(value, got, until)
        return value + got

    my_out, _ = tie(my_out, router_part)
    *near_out, far_a, far_b = kept_parts(pos, left_out, (my_out, other_out), 0, got_out)
    far_out = (swap(far_a, "y", 3), swap(far_b, "y", 1))
    router_part = router_step(0, router_part, far_a)

    grad_pre, router_part, _ = tie(grad_pre, router_part, far_a)
    *near_in, far_a, far_b = kept_parts(pos, left_in, (grad_pre, other_in), 2, got_in)
    far_in = (swap(far_a, "y", 3), swap(far_b, "y", 1))
    router_part = router_step(1, router_part, far_a)

    near_out, router_part, _ = tie(near_out, router_part, far_a)
    mine_out, *pieces = zh_pieces(pos, near_out, far_out, grad_scale)
    zh_out = [swap(piece, "zh", r + 1) for r, piece in enumerate(pieces)]
    router_part = router_step(2, router_part, mine_out)

    near_in, router_part, _ = tie(near_in, router_part, mine_out)
    mine_in, *pieces = zh_pieces(pos, near_in, far_in, grad_scale)
    zh_in = [swap(piece, "zh", r + 1) for r, piece in enumerate(pieces)]
    router_part = router_step(3, router_part, mine_in)

    mine_out, router_part, _ = tie(mine_out, router_part, mine_in)
    keep_out, give = zh_total(pos, mine_out, zh_out)
    other_half_out = swap(give, "core", 1)
    router_part = router_step(4, router_part, keep_out)

    mine_in, router_part, _ = tie(mine_in, router_part, keep_out)
    keep_in, give = zh_total(pos, mine_in, zh_in)
    other_half_in = swap(give, "core", 1)
    router_part = router_step(5, router_part, keep_in)

    dispatch, router_part, _ = tie(dispatch, router_part, keep_in)
    grad_tokens = token_grads(pos, dispatch, flat_grads, logit_lanes, weight_lanes)
    router_part = router_step(6, router_part, grad_tokens)
    router_part = router_step(7, router_part)
    outer_share = both_halves(pos, keep_out, other_half_out)
    inner_share = both_halves(pos, keep_in, other_half_in)
    return (grad_tokens, router_part.T, inner_share, outer_share)


def solution(mesh):
    fine = Mesh(mesh.devices.reshape(FINE_SHAPE), FINE)
    placed = (
        P(FINE, None),
        P(FINE, None),
        P(),
        P(GROUP, None, None),
        P(GROUP, None, None),
        P(FINE, None),
        P(FINE, None),
        P(FINE, None),
    )
    return jax.shard_map(
        per_device,
        mesh=fine,
        in_specs=placed,
        out_specs=(
            P(FINE, None),
            P(),
            P(GROUP, ("y", "zh", "core"), None),
            P(GROUP, ("y", "zh", "core"), None),
        ),
        check_vma=False,
    )
```

time: 195 us -> 199 us (1.021)
  the two profiles are of different devices: /device:TPU:2 before, /device:TPU:46 now
where the time goes in v5:
time: 199 us; the launch traced here: 198 us
  starting transfers between devices  64.6 us (32%)
  waiting for transfers between devices  58.8 us (30%)
  Pallas kernels  30.9 us (16%)
  local copies, waits for them, and re-layouts  18.8 us (9%)
  matrix products  18.7 us (9%)
  other arithmetic  5.02 us (3%)
    ppermute x28, starting transfers between devices, swap(): return lax.ppermute(values, axis, [(i, i ^ mask) for i in range(size)])  40.8 us
    pallas_call x14, Pallas kernels, call(): pl.pallas_call(body, in_specs=[pl.BlockSpec(memory_space=pltpu.SMEM)] + [...  30.9 us
    all_to_all x4, waiting for transfers between devices, exchange(): return lax.all_to_all(values, axes, split_axis=0, concat_axis=0, tiled=True)  30.4 us
    ppermute x28, waiting for transfers between devices, swap(): return lax.ppermute(values, axis, [(i, i ^ mask) for i in range(size)])  28.4 us
    all_to_all x4, starting transfers between devices, exchange(): return lax.all_to_all(values, axes, split_axis=0, concat_axis=0, tiled=True)  23.9 us
    unnamed x57, local copies, waits for them, and re-layouts  17.5 us
    dot_general x1, matrix products, per_device(): hidden_pre = jnp.dot(slot_tokens, weight_in, preferred_element_type=F32)  7.42 us
    dot_general x1, matrix products, per_device(): jnp.dot(hidden_act, weight_out, preferred_element_type=F32).astype(BF16)  6.23 us
  transfers between devices with their start and end apart: 32, of which 12 were waited for; matrix products, arithmetic and copies ran while one was open for 10% of the time, Pallas kernels for 11%

profile of v5, /device:TPU:46, one launch (start us, length us, event | category | flops | bytes accessed | tf_op | source)
XLA Modules:
  0.0 197.9 jit_solution(1999741585459999174)
XLA Ops:
  0.6 0.8 multiply_add_fusion
  1.4 0.8 compare_reduce_fusion.1
  2.2 2.1 %convolution_convert_fusion.1 = bf16[512,2048]{1,0:T(8,128)(2,1)} fusion(bf16[256,2048]{1,0:T(8,128)(2,1)S(1)} %copy-done, s32[256]{0:T(256)S(1)} %bitcast.52, s32[256]{0:T(256)S(1)} %bitcast.47, pred[256]{0:T(512)(128)(4,1)S(1)} %get-tuple-element.159, pred[256]{0:T(512)(128)(4,1)S(1)} %get-tuple-element.158), kind=kOutput, calls=%fused_computation.2 | convolution fusion | flops 538574848 | bytes 3148288 | tf_op jit(solution)/shard_map/dot_general | solution.py:280
  4.4 5.8 %all-to-all-start.1 = ((bf16[8,64,2048]{2,1,0:T(8,128)(2,1)}), bf16[8,64,2048]{2,1,0:T(8,128)(2,1)S(1)}, u32[]{:S(2)}, u32[]{:S(2)}) async-start(bf16[8,64,2048]{2,1,0:T(8,128)(2,1)} %bitcast.44), calls=%async_computation.1 | async-start | bytes 4194304 | tf_op jit(solution)/shard_map/all_to_all | solution.py:47
  11.3 2.0 convolution_convert_fusion.2
  13.3 1.5 pad_maximum_fusion
  14.8 19.6 %all-to-all-done.1 = bf16[8,64,2048]{2,1,0:T(8,128)(2,1)S(1)} async-done(((bf16[8,64,2048]{2,1,0:T(8,128)(2,1)}), bf16[8,64,2048]{2,1,0:T(8,128)(2,1)S(1)}, u32[]{:S(2)}, u32[]{:S(2)}) %all-to-all-start.1) | async-done | bytes 2097184 | tf_op jit(solution)/shard_map/all_to_all | solution.py:47
  34.4 1.4 copy-done.1
  35.8 6.3 %all-to-all-start = ((bf16[8,64,2176]{2,1,0:T(8,128)(2,1)}), bf16[8,64,2176]{2,1,0:T(8,128)(2,1)S(1)}, u32[]{:S(2)}, u32[]{:S(2)}) async-start(bf16[8,64,2176]{2,1,0:T(8,128)(2,1)} %bitcast.43), calls=%async_computation | async-start | bytes 4456448 | tf_op jit(solution)/shard_map/all_to_all | solution.py:47
  42.1 7.4 %fusion.3 = (f32[512,1024]{1,0:T(8,128)}, bf16[512,1024]{1,0:T(8,128)(2,1)}) fusion(bf16[512,2048]{1,0:T(8,128)(2,1)} %bitcast.37, bf16[1,2048,1024]{2,1,0:T(8,128)(2,1)} %param.11), kind=kOutput, calls=%fused_computation.9 | convolution fusion | flops 2152726528 | bytes 9437184 | tf_op jit(solution)/shard_map/dot_general | solution.py:304
  50.1 6.2 %convolution_convert_fusion.expert = bf16[512,2048]{1,0:T(8,128)(2,1)} fusion(bf16[512,1024]{1,0:T(8,128)(2,1)} %get-tuple-element.87.lm, bf16[1,1024,2048]{2,1,0:T(8,128)(2,1)} %param.12), kind=kOutput, calls=%fused_computation.1 | convolution fusion | flops 2148532224 | bytes 7340032 | tf_op jit(solution)/shard_map/dot_general | solution.py:313
  56.3 10.7 %all-to-all-done = bf16[8,64,2176]{2,1,0:T(8,128)(2,1)S(1)} async-done(((bf16[8,64,2176]{2,1,0:T(8,128)(2,1)}), bf16[8,64,2176]{2,1,0:T(8,128)(2,1)S(1)}, u32[]{:S(2)}, u32[]{:S(2)}) %all-to-all-start) | async-done | bytes 2228256 | tf_op jit(solution)/shard_map/all_to_all | solution.py:47
  67.1 1.6 copy-done.13
  68.7 2.4 %shard_map.111 = (bf16[512,1024]{1,0:T(8,128)(2,1)S(1)}, bf16[512,1024]{1,0:T(8,128)(2,1)}, f32[512,1]{1,0:T(8,128)S(1)}) custom-call(s32[4]{0:T(128)S(1)} %pad_add_fusion.pos_ref, bf16[512,2176]{1,0:T(8,128)(2,1)S(1)} %bitcast.34, bf16[512,2048]{1,0:T(8,128)(2,1)S(1)} %copy-done.13), custom_call_target="tpu_custom_call" | custom-call | flops 1000 | bytes 1000 | tf_op jit(solution)/shard_map/pallas_call | solution.py:56
  71.1 1.0 copy-done.10
  72.3 0.7 all_to_all.20
  73.0 6.0 %all-to-all-start.2 = ((bf16[8,1,64]{2,1,0:T(2,128)(2,1)}), bf16[8,1,64]{2,1,0:T(2,128)(2,1)S(1)}, u32[]{:S(2)}, u32[]{:S(2)}) async-start(bf16[8,1,64]{2,1,0:T(2,128)(2,1)} %all_to_all.20), calls=%async_computation.2 | async-start | bytes 8192 | tf_op jit(solution)/shard_map/all_to_all | solution.py:47
  78.9 2.2 %copy-done.8 = bf16[1,1024,2048]{2,1,0:T(8,128)(2,1)S(1)} copy-done((bf16[1,1024,2048]{2,1,0:T(8,128)(2,1)S(1)}, bf16[1,1024,2048]{2,1,0:T(8,128)(2,1)}, u32[]{:S(2)}) %copy-start.8) | copy-done | bytes 4194328
  81.1 1.6 copy-done.14
  82.7 2.9 %shard_map.112 = (bf16[512,1024]{1,0:T(8,128)(2,1)S(1)}, bf16[512,512]{1,0:T(8,128)(2,1)S(1)}) custom-call(s32[4]{0:T(128)S(1)} %pad_add_fusion.pos_ref, bf16[512,2176]{1,0:T(8,128)(2,1)S(1)} %bitcast.35, bf16[1024,2048]{1,0:T(8,128)(2,1)S(1)} %bitcast.41, f32[512,1024]{1,0:T(8,128)S(1)} %copy-done.14), custom_call_target="tpu_custom_call" | custom-call | flops 1000 | bytes 1000 | tf_op jit(solution)/shard_map/pallas_call | solution.py:56
  85.7 1.1 copy-done.3
  86.7 0.8 copy-done.19
  87.6 1.2 copy-done.11
  88.9 3.3 %shard_map.113 = (bf16[512,512]{1,0:T(8,128)(2,1)S(1)}, bf16[512,512]{1,0:T(8,128)(2,1)S(1)}) custom-call(s32[4]{0:T(128)S(1)} %pad_add_fusion.pos_ref, bf16[512,1024]{1,0:T(8,128)(2,1)} %get-tuple-element.87.lm, bf16[512,1024]{1,0:T(8,128)(2,1)} %collective-permute-done.1.lo, bf16[512,1024]{1,0:T(8,128)(2,1)S(1)} %copy-done.11, ...), custom_call_target="tpu_custom_call" | custom-call | flops 1000 | bytes 1000 | tf_op jit(solution)/shard_map/pallas_call | solution.py:56
  92.2 0.8 copy-done.17
  92.9 0.8 copy-done.18
  93.8 2.2 %copy-done.9 = bf16[1,2048,1024]{2,1,0:T(8,128)(2,1)S(1)} copy-done((bf16[1,2048,1024]{2,1,0:T(8,128)(2,1)S(1)}, bf16[1,2048,1024]{2,1,0:T(8,128)(2,1)}, u32[]{:S(2)}) %copy-start.9) | copy-done | bytes 4194328
  95.9 2.9 %shard_map.114 = bf16[512,2048]{1,0:T(8,128)(2,1)S(1)} custom-call(s32[4]{0:T(128)S(1)} %pad_add_fusion.pos_ref, bf16[512,1024]{1,0:T(8,128)(2,1)S(1)} %copy-done.4, bf16[2048,1024]{1,0:T(8,128)(2,1)S(1)} %bitcast.42), custom_call_target="tpu_custom_call" | custom-call | flops 1000 | bytes 1000 | tf_op jit(solution)/shard_map/pallas_call | solution.py:56
  98.9 1.3 copy-done.7
  100.2 5.8 %all-to-all-start.3 = ((bf16[8,64,2048]{2,1,0:T(8,128)(2,1)}), bf16[8,64,2048]{2,1,0:T(8,128)(2,1)}, u32[]{:S(2)}, u32[]{:S(2)}) async-start(bf16[8,64,2048]{2,1,0:T(8,128)(2,1)} %bitcast.40), calls=%async_computation.3 | async-start | bytes 4194304 | tf_op jit(solution)/shard_map/all_to_all | solution.py:47
  106.5 2.4 %collective-permute-start.6 = (bf16[512,512]{1,0:T(8,128)(2,1)}, bf16[512,512]{1,0:T(8,128)(2,1)}, u32[]{:S(2)}, u32[]{:S(2)}) collective-permute-start(bf16[512,512]{1,0:T(8,128)(2,1)} %copy-done.17), channel_id=1, source_target_pairs={{0,192},{64,128},{128,64},{192,0},{1,193},{65,129},{129,65},{193,1... | collective-permute-start | bytes 1572872 | tf_op jit(solution)/shard_map/ppermute | solution.py:43
  108.9 1.2 copy-done.5
  110.1 4.0 %shard_map.115 = (bf16[1024,256]{1,0:T(8,128)(2,1)}, bf16[1024,256]{1,0:T(8,128)(2,1)}) custom-call(s32[4]{0:T(128)S(1)} %pad_add_fusion.pos_ref, bf16[512,2048]{1,0:T(8,128)(2,1)S(1)} %bitcast.38, bf16[512,2048]{1,0:T(8,128)(2,1)} %collective-permute-done.lo, bf16[512,1024]{1,0:T(8,128)(2,1)S(1)} %copy-done.5, bf16[512,512]{1,0:T(8,128)(2,1)S(1)} %collective-permute-done.3.ro), custom_call_target="tpu_custom_call" | custom-call | flops 1000 | bytes 1000 | tf_op jit(solution)/shard_map/pallas_call | solution.py:56
  114.1 1.3 collective-permute-start.7
  115.4 0.8 collective-permute-start.8
  117.5 3.6 %collective-permute-done.5.got_a = bf16[512,512]{1,0:T(8,128)(2,1)} collective-permute-done((bf16[512,512]{1,0:T(8,128)(2,1)}, bf16[512,512]{1,0:T(8,128)(2,1)}, u32[]{:S(2)}, u32[]{:S(2)}) %collective-permute-start.5) | collective-permute-done | bytes 524320 | tf_op jit(solution)/shard_map/ppermute | solution.py:43
  121.0 0.8 collective-permute-done.6.got_b
  121.9 3.5 %shard_map.116 = (f32[256,512]{1,0:T(8,128)S(1)}, f32[256,512]{1,0:T(8,128)S(1)}, bf16[256,512]{1,0:T(8,128)(2,1)S(1)}, bf16[256,512]{1,0:T(8,128)(2,1)S(1)}) custom-call(s32[4]{0:T(128)S(1)} %pad_add_fusion.pos_ref, bf16[512,1024]{1,0:T(8,128)(2,1)} %get-tuple-element.87.lm, bf16[512,1024]{1,0:T(8,128)(2,1)} %collective-permute-done.1.lo, ...), custom_call_target="tpu_custom_call" | custom-call | flops 1000 | bytes 1000 | tf_op jit(solution)/shard_map/pallas_call | solution.py:56
  125.3 2.2 %collective-permute-start.11 = (bf16[256,512]{1,0:T(8,128)(2,1)S(1)}, bf16[256,512]{1,0:T(8,128)(2,1)S(1)}, u32[]{:S(2)}, u32[]{:S(2)}) collective-permute-start(bf16[256,512]{1,0:T(8,128)(2,1)S(1)} %get-tuple-element.104), channel_id=1, source_target_pairs={{0,192},{64,128},{128,64},{192,0},{1,193},{65,129},{129,65},{193,1... | collective-permute-start | bytes 786440 | tf_op jit(solution)/shard_map/ppermute | solution.py:43
  127.5 2.5 %collective-permute-start.12 = (bf16[256,512]{1,0:T(8,128)(2,1)S(1)}, bf16[256,512]{1,0:T(8,128)(2,1)S(1)}, u32[]{:S(2)}, u32[]{:S(2)}) collective-permute-start(bf16[256,512]{1,0:T(8,128)(2,1)S(1)} %get-tuple-element.119), channel_id=1, source_target_pairs={{0,64},{64,0},{128,192},{192,128},{1,65},{65,1},{129,193},{193,129... | collective-permute-start | bytes 786440 | tf_op jit(solution)/shard_map/ppermute | solution.py:43
  130.1 2.2 %collective-permute-done.7.got_a = bf16[1024,256]{1,0:T(8,128)(2,1)} collective-permute-done((bf16[1024,256]{1,0:T(8,128)(2,1)}, bf16[1024,256]{1,0:T(8,128)(2,1)}, u32[]{:S(2)}, u32[]{:S(2)}) %collective-permute-start.7) | collective-permute-done | bytes 524320 | tf_op jit(solution)/shard_map/ppermute | solution.py:43
  132.3 0.8 collective-permute-done.8.got_b
  133.1 3.2 %shard_map.117 = (f32[512,256]{1,0:T(8,128)S(1)}, f32[512,256]{1,0:T(8,128)S(1)}, bf16[512,256]{1,0:T(8,128)(2,1)S(1)}, bf16[512,256]{1,0:T(8,128)(2,1)S(1)}) custom-call(s32[4]{0:T(128)S(1)} %pad_add_fusion.pos_ref, bf16[512,2048]{1,0:T(8,128)(2,1)S(1)} %bitcast.39, bf16[512,2048]{1,0:T(8,128)(2,1)} %collective-permute-done.lo, ...), custom_call_target="tpu_custom_call" | custom-call | flops 1000 | bytes 1000 | tf_op jit(solution)/shard_map/pallas_call | solution.py:56
  136.3 2.1 %collective-permute-start.13 = (bf16[512,256]{1,0:T(8,128)(2,1)S(1)}, bf16[512,256]{1,0:T(8,128)(2,1)S(1)}, u32[]{:S(2)}, u32[]{:S(2)}) collective-permute-start(bf16[512,256]{1,0:T(8,128)(2,1)S(1)} %get-tuple-element.113), channel_id=1, source_target_pairs={{0,192},{64,128},{128,64},{192,0},{1,193},{65,129},{129,65},{193,1... | collective-permute-start | bytes 786440 | tf_op jit(solution)/shard_map/ppermute | solution.py:43
  138.5 2.6 %collective-permute-start.14 = (bf16[512,256]{1,0:T(8,128)(2,1)S(1)}, bf16[512,256]{1,0:T(8,128)(2,1)S(1)}, u32[]{:S(2)}, u32[]{:S(2)}) collective-permute-start(bf16[512,256]{1,0:T(8,128)(2,1)S(1)} %get-tuple-element.125), channel_id=1, source_target_pairs={{0,64},{64,0},{128,192},{192,128},{1,65},{65,1},{129,193},{193,129... | collective-permute-start | bytes 786440 | tf_op jit(solution)/shard_map/ppermute | solution.py:43
  141.0 0.9 collective-permute-start.9
  141.9 3.4 %collective-permute-done.9 = f32[8,2048]{1,0:T(8,128)S(1)} collective-permute-done((f32[8,2048]{1,0:T(8,128)S(1)}, f32[8,2048]{1,0:T(8,128)S(1)}, u32[]{:S(2)}, u32[]{:S(2)}) %collective-permute-start.9) | collective-permute-done | bytes 65568 | tf_op jit(solution)/shard_map/ppermute | solution.py:43
  145.3 0.6 collective-permute-start.10
  146.0 0.7 shard_map.118
  146.7 4.2 %collective-permute-done.10 = f32[8,2048]{1,0:T(8,128)S(1)} collective-permute-done((f32[8,2048]{1,0:T(8,128)S(1)}, f32[8,2048]{1,0:T(8,128)S(1)}, u32[]{:S(2)}, u32[]{:S(2)}) %collective-permute-start.10) | collective-permute-done | bytes 65568 | tf_op jit(solution)/shard_map/ppermute | solution.py:43
  150.9 0.6 collective-permute-start.15
  151.6 3.3 %collective-permute-start.17 = (bf16[64,1024]{1,0:T(8,128)(2,1)S(1)}, bf16[64,1024]{1,0:T(8,128)(2,1)S(1)}, u32[]{:S(2)}, u32[]{:S(2)}) collective-permute-start(bf16[64,1024]{1,0:T(8,128)(2,1)S(1)} %get-tuple-element.132), channel_id=1, source_target_pairs={{0,16},{16,0},{32,48},{48,32},{1,17},{17,1},{33,49},{49,33},{2,18}... | collective-permute-start | bytes 393224 | tf_op jit(solution)/shard_map/ppermute | solution.py:43
  154.8 4.5 %collective-permute-start.18 = (bf16[64,1024]{1,0:T(8,128)(2,1)S(1)}, bf16[64,1024]{1,0:T(8,128)(2,1)S(1)}, u32[]{:S(2)}, u32[]{:S(2)}) collective-permute-start(bf16[64,1024]{1,0:T(8,128)(2,1)S(1)} %get-tuple-element.133), channel_id=1, source_target_pairs={{0,32},{16,48},{32,0},{48,16},{1,33},{17,49},{33,1},{49,17},{2,34}... | collective-permute-start | bytes 393224 | tf_op jit(solution)/shard_map/ppermute | solution.py:43
  159.3 0.7 shard_map.119
  160.1 2.1 %collective-permute-start.21 = (bf16[128,512]{1,0:T(8,128)(2,1)S(1)}, bf16[128,512]{1,0:T(8,128)(2,1)S(1)}, u32[]{:S(2)}, u32[]{:S(2)}) collective-permute-start(bf16[128,512]{1,0:T(8,128)(2,1)S(1)} %get-tuple-element.140), channel_id=1, source_target_pairs={{0,16},{16,0},{32,48},{48,32},{1,17},{17,1},{33,49},{49,33},{2,18}... | collective-permute-start | bytes 393224 | tf_op jit(solution)/shard_map/ppermute | solution.py:43
  162.2 7.3 %collective-permute-done.17.one = bf16[64,1024]{1,0:T(8,128)(2,1)S(1)} collective-permute-done((bf16[64,1024]{1,0:T(8,128)(2,1)S(1)}, bf16[64,1024]{1,0:T(8,128)(2,1)S(1)}, u32[]{:S(2)}, u32[]{:S(2)}) %collective-permute-start.17) | collective-permute-done | bytes 131104 | tf_op jit(solution)/shard_map/ppermute | solution.py:43
  170.0 7.2 %collective-permute-start.23 = (bf16[128,512]{1,0:T(8,128)(2,1)S(1)}, bf16[128,512]{1,0:T(8,128)(2,1)S(1)}, u32[]{:S(2)}, u32[]{:S(2)}) collective-permute-start(bf16[128,512]{1,0:T(8,128)(2,1)S(1)} %get-tuple-element.142), channel_id=1, source_target_pairs={{0,48},{16,32},{32,16},{48,0},{1,49},{17,33},{33,17},{49,1},{2,50}... | collective-permute-start | bytes 393224 | tf_op jit(solution)/shard_map/ppermute | solution.py:43
  178.7 2.8 %collective-permute-done.23.three = bf16[128,512]{1,0:T(8,128)(2,1)S(1)} collective-permute-done((bf16[128,512]{1,0:T(8,128)(2,1)S(1)}, bf16[128,512]{1,0:T(8,128)(2,1)S(1)}, u32[]{:S(2)}, u32[]{:S(2)}) %collective-permute-start.23) | collective-permute-done | bytes 131104 | tf_op jit(solution)/shard_map/ppermute | solution.py:43
  182.2 3.6 %collective-permute-start.24 = (f32[8,2048]{1,0:T(8,128)S(1)}, f32[8,2048]{1,0:T(8,128)S(1)}, u32[]{:S(2)}, u32[]{:S(2)}) collective-permute-start(f32[8,2048]{1,0:T(8,128)S(1)} %add.63), channel_id=1, source_target_pairs={{0,16},{16,0},{32,48},{48,32},{1,17},{17,1},{33,49},{49,33},{2,18}... | collective-permute-start | bytes 196616 | tf_op jit(solution)/shard_map/ppermute | solution.py:43
  186.8 3.6 %shard_map.122 = bf16[256,2048]{1,0:T(8,128)(2,1)} custom-call(s32[4]{0:T(128)S(1)} %pad_add_fusion.pos_ref, bf16[512,256]{1,0:T(8,128)(2,1)S(1)} %fusion.16.disp, bf16[512,2048]{1,0:T(8,128)(2,1)} %bitcast.15.flat, bf16[256,128]{1,0:T(8,128)(2,1)S(1)} %pad.12.logit, bf16[2048,128]{1,0:T(8,128)(2,1)S(1)} %pad.13.weight), custom_call_target="tpu_custom_call" | custom-call | flops 1000 | bytes 1000 | tf_op jit(solution)/shard_map/pallas_call | solution.py:56
  190.4 1.3 collective-permute-start.25
  191.7 1.3 shard_map.124
  193.0 1.3 shard_map.123
  194.2 3.1 %collective-permute-done.25 = f32[8,2048]{1,0:T(8,128)S(1)} collective-permute-done((f32[8,2048]{1,0:T(8,128)S(1)}, f32[8,2048]{1,0:T(8,128)S(1)}, u32[]{:S(2)}, u32[]{:S(2)}) %collective-permute-start.25) | collective-permute-done | bytes 65568 | tf_op jit(solution)/shard_map/ppermute | solution.py:43
  (116 shorter events, 8.0 us)
Async XLA Ops:
  0.6 1.6 copy-start
  2.2 114.0 %copy-start.24 = (pred[256]{0:T(512)(128)(4,1)}, pred[256]{0:T(512)(128)(4,1)S(1)}, u32[]{:S(2)}) copy-start(pred[256]{0:T(512)(128)(4,1)S(1)} %get-tuple-element.158) | copy-start | bytes 772
  2.2 114.0 %copy-start.26 = (pred[256]{0:T(512)(128)(4,1)}, pred[256]{0:T(512)(128)(4,1)S(1)}, u32[]{:S(2)}) copy-start(pred[256]{0:T(512)(128)(4,1)S(1)} %get-tuple-element.159) | copy-start | bytes 772
  4.4 5.8 %copy-start.20 = (bf16[2048,8]{0,1:T(8,128)(2,1)S(1)}, bf16[2048,8]{0,1:T(8,128)(2,1)}, u32[]{:S(2)}) copy-start(bf16[2048,8]{0,1:T(8,128)(2,1)} %param.10) | copy-start | bytes 98308
  4.4 6.5 %copy-start.23 = (s32[256,2]{0,1:T(2,128)S(1)}, s32[256,2]{0,1:T(2,128)}, u32[]{:S(2)}) copy-start(s32[256,2]{0,1:T(2,128)} %param.13) | copy-start | bytes 6148
  4.4 6.6 %copy-start.22 = (s32[256,2]{0,1:T(2,128)S(1)}, s32[256,2]{0,1:T(2,128)}, u32[]{:S(2)}) copy-start(s32[256,2]{0,1:T(2,128)} %param.15) | copy-start | bytes 6148
  4.4 30.1 %all-to-all-start.1 = ((bf16[8,64,2048]{2,1,0:T(8,128)(2,1)}), bf16[8,64,2048]{2,1,0:T(8,128)(2,1)S(1)}, u32[]{:S(2)}, u32[]{:S(2)}) async-start(bf16[8,64,2048]{2,1,0:T(8,128)(2,1)} %bitcast.44), calls=%async_computation.1 | async-start | bytes 4194304 | tf_op jit(solution)/shard_map/all_to_all | solution.py:47
  34.4 1.4 copy-start.1
  35.8 31.3 %all-to-all-start = ((bf16[8,64,2176]{2,1,0:T(8,128)(2,1)}), bf16[8,64,2176]{2,1,0:T(8,128)(2,1)S(1)}, u32[]{:S(2)}, u32[]{:S(2)}) async-start(bf16[8,64,2176]{2,1,0:T(8,128)(2,1)} %bitcast.43), calls=%async_computation | async-start | bytes 4456448 | tf_op jit(solution)/shard_map/all_to_all | solution.py:47
  42.1 25.0 %collective-permute-start = (bf16[512,2048]{1,0:T(8,128)(2,1)}, bf16[512,2048]{1,0:T(8,128)(2,1)}, u32[]{:S(2)}, u32[]{:S(2)}) collective-permute-start(bf16[512,2048]{1,0:T(8,128)(2,1)} %bitcast.36), channel_id=1, source_target_pairs={{0,8},{8,0},{1,9},{9,1},{2,10},{10,2},{3,11},{11,3},{4,12},{12,4},... | collective-permute-start | bytes 6291464 | tf_op jit(solution)/shard_map/ppermute | solution.py:43
  49.5 17.6 %collective-permute-start.1 = (bf16[512,1024]{1,0:T(8,128)(2,1)}, bf16[512,1024]{1,0:T(8,128)(2,1)}, u32[]{:S(2)}, u32[]{:S(2)}) collective-permute-start(bf16[512,1024]{1,0:T(8,128)(2,1)} %get-tuple-element.87.lm), channel_id=1, source_target_pairs={{0,8},{8,0},{1,9},{9,1},{2,10},{10,2},{3,11},{11,3},{4,12},{12,4},... | collective-permute-start | bytes 3145736 | tf_op jit(solution)/shard_map/ppermute | solution.py:43
  67.1 1.6 copy-start.13
  71.1 1.0 copy-start.10
  72.1 15.5 %collective-permute-start.2 = (bf16[512,1024]{1,0:T(8,128)(2,1)}, bf16[512,1024]{1,0:T(8,128)(2,1)}, u32[]{:S(2)}, u32[]{:S(2)}) collective-permute-start(bf16[512,1024]{1,0:T(8,128)(2,1)} %get-tuple-element.83), channel_id=1, source_target_pairs={{0,8},{8,0},{1,9},{9,1},{2,10},{10,2},{3,11},{11,3},{4,12},{12,4},... | collective-permute-start | bytes 3145736 | tf_op jit(solution)/shard_map/ppermute | solution.py:43
  73.0 14.6 %all-to-all-start.2 = ((bf16[8,1,64]{2,1,0:T(2,128)(2,1)}), bf16[8,1,64]{2,1,0:T(2,128)(2,1)S(1)}, u32[]{:S(2)}, u32[]{:S(2)}) async-start(bf16[8,1,64]{2,1,0:T(2,128)(2,1)} %all_to_all.20), calls=%async_computation.2 | async-start | bytes 8192 | tf_op jit(solution)/shard_map/all_to_all | solution.py:47
  78.9 2.2 %copy-start.8 = (bf16[1,1024,2048]{2,1,0:T(8,128)(2,1)S(1)}, bf16[1,1024,2048]{2,1,0:T(8,128)(2,1)}, u32[]{:S(2)}) copy-start(bf16[1,1024,2048]{2,1,0:T(8,128)(2,1)} %param.12) | copy-start | bytes 12582916
  81.1 1.6 copy-start.14
  85.6 1.1 copy-start.3
  86.7 0.8 copy-start.19
  87.6 1.2 copy-start.11
  88.9 4.9 %copy-start.4 = (bf16[512,1024]{1,0:T(8,128)(2,1)S(1)}, bf16[512,1024]{1,0:T(8,128)(2,1)}, u32[]{:S(2)}) copy-start(bf16[512,1024]{1,0:T(8,128)(2,1)} %copy-done.3) | copy-start | bytes 3145732
  92.1 0.8 copy-start.17
  92.9 0.8 copy-start.18
  93.8 2.2 %copy-start.9 = (bf16[1,2048,1024]{2,1,0:T(8,128)(2,1)S(1)}, bf16[1,2048,1024]{2,1,0:T(8,128)(2,1)}, u32[]{:S(2)}) copy-start(bf16[1,2048,1024]{2,1,0:T(8,128)(2,1)} %param.11) | copy-start | bytes 12582916
  98.9 1.3 copy-start.7
  100.2 8.7 %copy-start.2 = (bf16[8,64,2048]{2,1,0:T(8,128)(2,1)S(1)}, bf16[8,64,2048]{2,1,0:T(8,128)(2,1)}, u32[]{:S(2)}) copy-start(bf16[8,64,2048]{2,1,0:T(8,128)(2,1)} %copy-done.1) | copy-start | bytes 6291460
  100.2 86.6 %all-to-all-start.3 = ((bf16[8,64,2048]{2,1,0:T(8,128)(2,1)}), bf16[8,64,2048]{2,1,0:T(8,128)(2,1)}, u32[]{:S(2)}, u32[]{:S(2)}) async-start(bf16[8,64,2048]{2,1,0:T(8,128)(2,1)} %bitcast.40), calls=%async_computation.3 | async-start | bytes 4194304 | tf_op jit(solution)/shard_map/all_to_all | solution.py:47
  106.0 2.9 %collective-permute-start.3 = (bf16[512,512]{1,0:T(8,128)(2,1)}, bf16[512,512]{1,0:T(8,128)(2,1)S(1)}, u32[]{:S(2)}, u32[]{:S(2)}) collective-permute-start(bf16[512,512]{1,0:T(8,128)(2,1)} %copy-done.19), channel_id=1, source_target_pairs={{0,8},{8,0},{1,9},{9,1},{2,10},{10,2},{3,11},{11,3},{4,12},{12,4},... | collective-permute-start | bytes 1572872 | tf_op jit(solution)/shard_map/ppermute | solution.py:43
  106.0 15.0 %collective-permute-start.5 = (bf16[512,512]{1,0:T(8,128)(2,1)}, bf16[512,512]{1,0:T(8,128)(2,1)}, u32[]{:S(2)}, u32[]{:S(2)}) collective-permute-start(bf16[512,512]{1,0:T(8,128)(2,1)} %copy-done.18), channel_id=1, source_target_pairs={{0,64},{64,0},{128,192},{192,128},{1,65},{65,1},{129,193},{193,129... | collective-permute-start | bytes 1572872 | tf_op jit(solution)/shard_map/ppermute | solution.py:43
  106.5 15.4 %collective-permute-start.6 = (bf16[512,512]{1,0:T(8,128)(2,1)}, bf16[512,512]{1,0:T(8,128)(2,1)}, u32[]{:S(2)}, u32[]{:S(2)}) collective-permute-start(bf16[512,512]{1,0:T(8,128)(2,1)} %copy-done.17), channel_id=1, source_target_pairs={{0,192},{64,128},{128,64},{192,0},{1,193},{65,129},{129,65},{193,1... | collective-permute-start | bytes 1572872 | tf_op jit(solution)/shard_map/ppermute | solution.py:43
  108.8 1.2 copy-start.5
  110.1 4.0 %copy-start.15 = (bf16[512,512]{1,0:T(8,128)(2,1)}, bf16[512,512]{1,0:T(8,128)(2,1)S(1)}, u32[]{:S(2)}) copy-start(bf16[512,512]{1,0:T(8,128)(2,1)S(1)} %collective-permute-done.3.ro) | copy-start | bytes 1572868
  114.1 18.2 %collective-permute-start.7 = (bf16[1024,256]{1,0:T(8,128)(2,1)}, bf16[1024,256]{1,0:T(8,128)(2,1)}, u32[]{:S(2)}, u32[]{:S(2)}) collective-permute-start(bf16[1024,256]{1,0:T(8,128)(2,1)} %get-tuple-element.99), channel_id=1, source_target_pairs={{0,64},{64,0},{128,192},{192,128},{1,65},{65,1},{129,193},{193,129... | collective-permute-start | bytes 1572872 | tf_op jit(solution)/shard_map/ppermute | solution.py:43
  115.4 17.7 %collective-permute-start.8 = (bf16[1024,256]{1,0:T(8,128)(2,1)}, bf16[1024,256]{1,0:T(8,128)(2,1)}, u32[]{:S(2)}, u32[]{:S(2)}) collective-permute-start(bf16[1024,256]{1,0:T(8,128)(2,1)} %get-tuple-element.100), channel_id=1, source_target_pairs={{0,192},{64,128},{128,64},{192,0},{1,193},{65,129},{129,65},{193,1... | collective-permute-start | bytes 1572872 | tf_op jit(solution)/shard_map/ppermute | solution.py:43
  117.0 4.9 %copy-start.12 = (bf16[512,1024]{1,0:T(8,128)(2,1)S(1)}, bf16[512,1024]{1,0:T(8,128)(2,1)}, u32[]{:S(2)}) copy-start(bf16[512,1024]{1,0:T(8,128)(2,1)} %copy-done.10) | copy-start | bytes 3145732
  117.4 15.7 %copy-start.6 = (bf16[512,1024]{1,0:T(8,128)(2,1)S(1)}, bf16[512,1024]{1,0:T(8,128)(2,1)}, u32[]{:S(2)}) copy-start(bf16[512,1024]{1,0:T(8,128)(2,1)} %copy-done.3) | copy-start | bytes 3145732
  117.4 15.7 %copy-start.16 = (bf16[512,512]{1,0:T(8,128)(2,1)S(1)}, bf16[512,512]{1,0:T(8,128)(2,1)}, u32[]{:S(2)}) copy-start(bf16[512,512]{1,0:T(8,128)(2,1)} %copy-done.15) | copy-start | bytes 1572868
  117.4 12.6 %collective-permute-start.4 = (f32[8,2048]{1,0:T(8,128)S(1)}, f32[8,2048]{1,0:T(8,128)S(1)}, u32[]{:S(2)}, u32[]{:S(2)}) collective-permute-start(f32[8,2048]{1,0:T(8,128)S(1)} %convolution_multiply_fusion), channel_id=1, source_target_pairs={{0,8},{8,0},{1,9},{9,1},{2,10},{10,2},{3,11},{11,3},{4,12},{12,4},... | collective-permute-start | bytes 196616 | tf_op jit(solution)/shard_map/ppermute | solution.py:43
  125.3 20.6 %collective-permute-start.11 = (bf16[256,512]{1,0:T(8,128)(2,1)S(1)}, bf16[256,512]{1,0:T(8,128)(2,1)S(1)}, u32[]{:S(2)}, u32[]{:S(2)}) collective-permute-start(bf16[256,512]{1,0:T(8,128)(2,1)S(1)} %get-tuple-element.104), channel_id=1, source_target_pairs={{0,192},{64,128},{128,64},{192,0},{1,193},{65,129},{129,65},{193,1... | collective-permute-start | bytes 786440 | tf_op jit(solution)/shard_map/ppermute | solution.py:43
  127.5 18.5 %collective-permute-start.12 = (bf16[256,512]{1,0:T(8,128)(2,1)S(1)}, bf16[256,512]{1,0:T(8,128)(2,1)S(1)}, u32[]{:S(2)}, u32[]{:S(2)}) collective-permute-start(bf16[256,512]{1,0:T(8,128)(2,1)S(1)} %get-tuple-element.119), channel_id=1, source_target_pairs={{0,64},{64,0},{128,192},{192,128},{1,65},{65,1},{129,193},{193,129... | collective-permute-start | bytes 786440 | tf_op jit(solution)/shard_map/ppermute | solution.py:43
  136.3 23.0 %collective-permute-start.13 = (bf16[512,256]{1,0:T(8,128)(2,1)S(1)}, bf16[512,256]{1,0:T(8,128)(2,1)S(1)}, u32[]{:S(2)}, u32[]{:S(2)}) collective-permute-start(bf16[512,256]{1,0:T(8,128)(2,1)S(1)} %get-tuple-element.113), channel_id=1, source_target_pairs={{0,192},{64,128},{128,64},{192,0},{1,193},{65,129},{129,65},{193,1... | collective-permute-start | bytes 786440 | tf_op jit(solution)/shard_map/ppermute | solution.py:43
  138.5 20.9 %collective-permute-start.14 = (bf16[512,256]{1,0:T(8,128)(2,1)S(1)}, bf16[512,256]{1,0:T(8,128)(2,1)S(1)}, u32[]{:S(2)}, u32[]{:S(2)}) collective-permute-start(bf16[512,256]{1,0:T(8,128)(2,1)S(1)} %get-tuple-element.125), channel_id=1, source_target_pairs={{0,64},{64,0},{128,192},{192,128},{1,65},{65,1},{129,193},{193,129... | collective-permute-start | bytes 786440 | tf_op jit(solution)/shard_map/ppermute | solution.py:43
  141.0 4.3 %collective-permute-start.9 = (f32[8,2048]{1,0:T(8,128)S(1)}, f32[8,2048]{1,0:T(8,128)S(1)}, u32[]{:S(2)}, u32[]{:S(2)}) collective-permute-start(f32[8,2048]{1,0:T(8,128)S(1)} %add.58), channel_id=1, source_target_pairs={{0,2},{2,0},{4,6},{6,4},{1,3},{3,1},{5,7},{7,5},{8,10},{10,8},{12,... | collective-permute-start | bytes 196616 | tf_op jit(solution)/shard_map/ppermute | solution.py:43
  145.3 33.1 %copy-start.25 = (pred[256]{0:T(512)(128)(4,1)S(1)}, pred[256]{0:T(512)(128)(4,1)}, u32[]{:S(2)}) copy-start(pred[256]{0:T(512)(128)(4,1)} %copy-done.24) | copy-start | bytes 772
  145.3 33.1 %copy-start.27 = (pred[256]{0:T(512)(128)(4,1)S(1)}, pred[256]{0:T(512)(128)(4,1)}, u32[]{:S(2)}) copy-start(pred[256]{0:T(512)(128)(4,1)} %copy-done.26) | copy-start | bytes 772
  145.3 5.6 %collective-permute-start.10 = (f32[8,2048]{1,0:T(8,128)S(1)}, f32[8,2048]{1,0:T(8,128)S(1)}, u32[]{:S(2)}, u32[]{:S(2)}) collective-permute-start(f32[8,2048]{1,0:T(8,128)S(1)} %add.59), channel_id=1, source_target_pairs={{0,6},{2,4},{4,2},{6,0},{1,7},{3,5},{5,3},{7,1},{8,14},{10,12},{12... | collective-permute-start | bytes 196616 | tf_op jit(solution)/shard_map/ppermute | solution.py:43
  146.7 39.7 %copy-start.21 = (bf16[2048,8]{0,1:T(8,128)(2,1)S(1)}, bf16[2048,8]{0,1:T(8,128)(2,1)}, u32[]{:S(2)}) copy-start(bf16[2048,8]{0,1:T(8,128)(2,1)} %param.10) | copy-start | bytes 98308
  150.9 9.1 %collective-permute-start.15 = (f32[8,2048]{1,0:T(8,128)S(1)}, f32[8,2048]{1,0:T(8,128)S(1)}, u32[]{:S(2)}, u32[]{:S(2)}) collective-permute-start(f32[8,2048]{1,0:T(8,128)S(1)} %add.60), channel_id=1, source_target_pairs={{0,1},{1,0},{2,3},{3,2},{4,5},{5,4},{6,7},{7,6},{8,9},{9,8},{10,11... | collective-permute-start | bytes 196616 | tf_op jit(solution)/shard_map/ppermute | solution.py:43
  151.6 18.0 %collective-permute-start.17 = (bf16[64,1024]{1,0:T(8,128)(2,1)S(1)}, bf16[64,1024]{1,0:T(8,128)(2,1)S(1)}, u32[]{:S(2)}, u32[]{:S(2)}) collective-permute-start(bf16[64,1024]{1,0:T(8,128)(2,1)S(1)} %get-tuple-element.132), channel_id=1, source_target_pairs={{0,16},{16,0},{32,48},{48,32},{1,17},{17,1},{33,49},{49,33},{2,18}... | collective-permute-start | bytes 393224 | tf_op jit(solution)/shard_map/ppermute | solution.py:43
  154.8 15.2 %collective-permute-start.18 = (bf16[64,1024]{1,0:T(8,128)(2,1)S(1)}, bf16[64,1024]{1,0:T(8,128)(2,1)S(1)}, u32[]{:S(2)}, u32[]{:S(2)}) collective-permute-start(bf16[64,1024]{1,0:T(8,128)(2,1)S(1)} %get-tuple-element.133), channel_id=1, source_target_pairs={{0,32},{16,48},{32,0},{48,16},{1,33},{17,49},{33,1},{49,17},{2,34}... | collective-permute-start | bytes 393224 | tf_op jit(solution)/shard_map/ppermute | solution.py:43
  159.3 17.9 %collective-permute-start.19 = (bf16[64,1024]{1,0:T(8,128)(2,1)S(1)}, bf16[64,1024]{1,0:T(8,128)(2,1)S(1)}, u32[]{:S(2)}, u32[]{:S(2)}) collective-permute-start(bf16[64,1024]{1,0:T(8,128)(2,1)S(1)} %get-tuple-element.134), channel_id=1, source_target_pairs={{0,48},{16,32},{32,16},{48,0},{1,49},{17,33},{33,17},{49,1},{2,50}... | collective-permute-start | bytes 393224 | tf_op jit(solution)/shard_map/ppermute | solution.py:43
  160.0 17.8 %collective-permute-start.16 = (f32[8,2048]{1,0:T(8,128)S(1)}, f32[8,2048]{1,0:T(8,128)S(1)}, u32[]{:S(2)}, u32[]{:S(2)}) collective-permute-start(f32[8,2048]{1,0:T(8,128)S(1)} %add.61), channel_id=1, source_target_pairs={{0,64},{64,0},{128,192},{192,128},{1,65},{65,1},{129,193},{193,129... | collective-permute-start | bytes 196616 | tf_op jit(solution)/shard_map/ppermute | solution.py:43
  160.1 18.5 %collective-permute-start.21 = (bf16[128,512]{1,0:T(8,128)(2,1)S(1)}, bf16[128,512]{1,0:T(8,128)(2,1)S(1)}, u32[]{:S(2)}, u32[]{:S(2)}) collective-permute-start(bf16[128,512]{1,0:T(8,128)(2,1)S(1)} %get-tuple-element.140), channel_id=1, source_target_pairs={{0,16},{16,0},{32,48},{48,32},{1,17},{17,1},{33,49},{49,33},{2,18}... | collective-permute-start | bytes 393224 | tf_op jit(solution)/shard_map/ppermute | solution.py:43
  169.5 9.1 %collective-permute-start.22 = (bf16[128,512]{1,0:T(8,128)(2,1)S(1)}, bf16[128,512]{1,0:T(8,128)(2,1)S(1)}, u32[]{:S(2)}, u32[]{:S(2)}) collective-permute-start(bf16[128,512]{1,0:T(8,128)(2,1)S(1)} %get-tuple-element.141), channel_id=1, source_target_pairs={{0,32},{16,48},{32,0},{48,16},{1,33},{17,49},{33,1},{49,17},{2,34}... | collective-permute-start | bytes 393224 | tf_op jit(solution)/shard_map/ppermute | solution.py:43
  170.0 11.5 %collective-permute-start.23 = (bf16[128,512]{1,0:T(8,128)(2,1)S(1)}, bf16[128,512]{1,0:T(8,128)(2,1)S(1)}, u32[]{:S(2)}, u32[]{:S(2)}) collective-permute-start(bf16[128,512]{1,0:T(8,128)(2,1)S(1)} %get-tuple-element.142), channel_id=1, source_target_pairs={{0,48},{16,32},{32,16},{48,0},{1,49},{17,33},{33,17},{49,1},{2,50}... | collective-permute-start | bytes 393224 | tf_op jit(solution)/shard_map/ppermute | solution.py:43
  177.9 4.4 %collective-permute-start.20 = (f32[8,2048]{1,0:T(8,128)S(1)}, f32[8,2048]{1,0:T(8,128)S(1)}, u32[]{:S(2)}, u32[]{:S(2)}) collective-permute-start(f32[8,2048]{1,0:T(8,128)S(1)} %add.62), channel_id=1, source_target_pairs={{0,192},{64,128},{128,64},{192,0},{1,193},{65,129},{129,65},{193,1... | collective-permute-start | bytes 196616 | tf_op jit(solution)/shard_map/ppermute | solution.py:43
  182.2 8.1 %collective-permute-start.24 = (f32[8,2048]{1,0:T(8,128)S(1)}, f32[8,2048]{1,0:T(8,128)S(1)}, u32[]{:S(2)}, u32[]{:S(2)}) collective-permute-start(f32[8,2048]{1,0:T(8,128)S(1)} %add.63), channel_id=1, source_target_pairs={{0,16},{16,0},{32,48},{48,32},{1,17},{17,1},{33,49},{49,33},{2,18}... | collective-permute-start | bytes 196616 | tf_op jit(solution)/shard_map/ppermute | solution.py:43
  185.9 5.8 %collective-permute-start.27 = (f32[32,1024]{1,0:T(8,128)S(1)}, f32[32,1024]{1,0:T(8,128)S(1)}, u32[]{:S(2)}, u32[]{:S(2)}) collective-permute-start(f32[32,1024]{1,0:T(8,128)S(1)} %get-tuple-element.153), channel_id=1, source_target_pairs={{0,8},{8,0},{1,9},{9,1},{2,10},{10,2},{3,11},{11,3},{4,12},{12,4},... | collective-permute-start | bytes 393224 | tf_op jit(solution)/shard_map/ppermute | solution.py:43
  185.9 7.1 %collective-permute-start.26 = (f32[64,512]{1,0:T(8,128)S(1)}, f32[64,512]{1,0:T(8,128)S(1)}, u32[]{:S(2)}, u32[]{:S(2)}) collective-permute-start(f32[64,512]{1,0:T(8,128)S(1)} %get-tuple-element.152), channel_id=1, source_target_pairs={{0,8},{8,0},{1,9},{9,1},{2,10},{10,2},{3,11},{11,3},{4,12},{12,4},... | collective-permute-start | bytes 393224 | tf_op jit(solution)/shard_map/ppermute | solution.py:43
  190.4 6.9 %collective-permute-start.25 = (f32[8,2048]{1,0:T(8,128)S(1)}, f32[8,2048]{1,0:T(8,128)S(1)}, u32[]{:S(2)}, u32[]{:S(2)}) collective-permute-start(f32[8,2048]{1,0:T(8,128)S(1)} %add.64), channel_id=1, source_target_pairs={{0,48},{16,32},{32,16},{48,0},{1,49},{17,33},{33,17},{49,1},{2,50}... | collective-permute-start | bytes 196616 | tf_op jit(solution)/shard_map/ppermute | solution.py:43

commit v6 on v5

v6 whole, which is shorter than its diff:
```python
import jax
import jax.numpy as jnp
from jax import lax
from jax.experimental import pallas as pl
from jax.experimental.pallas import tpu as pltpu
from jax.sharding import Mesh, PartitionSpec as P

FINE = ("y", "zh", "core", "x", "zl")
FINE_SHAPE = (4, 4, 2, 4, 2)
GROUP = ("x", "zl")
EXTRA = 128
ROUTER_STEPS = (
    ("core", 1),
    ("x", 1),
    ("x", 3),
    ("zl", 1),
    ("y", 1),
    ("y", 3),
    ("zh", 1),
    ("zh", 3),
)
VMEM_LIMIT = 14 * 1024 * 1024
LONG = 60_000_000_000
F32 = jnp.float32
BF16 = jnp.bfloat16


def gelu_parts(hidden_pre):
    normal_cdf = 0.5 * (1.0 + jax.scipy.special.erf(hidden_pre * 0.7071067811865476))
    normal_pdf = jnp.exp(-0.5 * hidden_pre * hidden_pre) * 0.3989422804014327
    return (normal_cdf, normal_pdf)


def contract_rows(left, right):
    return lax.dot_general(left, right, (((0,), (0,)), ((), ())), preferred_element_type=F32)


def contract_cols(left, right):
    return lax.dot_general(left, right, (((1,), (1,)), ((), ())), preferred_element_type=F32)


def swap(values, axis, mask):
    size = lax.axis_size(axis)
    return lax.ppermute(values, axis, [(i, i ^ mask) for i in range(size)])


def exchange(values, axes):
    return lax.all_to_all(values, axes, split_axis=0, concat_axis=0, tiled=True)


def tie(*values):
    return lax.optimization_barrier(values)


def call(body, pos, inputs, outputs, flops=1000):
    vmem = pl.BlockSpec(memory_space=pltpu.VMEM)
    return pl.pallas_call(
        body,
        in_specs=[pl.BlockSpec(memory_space=pltpu.SMEM)] + [vmem] * len(inputs),
        out_specs=[vmem] * len(outputs),
        out_shape=[jax.ShapeDtypeStruct(shape, dtype) for shape, dtype in outputs],
        cost_estimate=pl.CostEstimate(flops=flops, bytes_accessed=1000, transcendentals=0),
        compiler_params=pltpu.CompilerParams(vmem_limit_bytes=VMEM_LIMIT),
    )(pos, *inputs)


def gate_of(pos, lanes):
    lane = lax.broadcasted_iota(jnp.int32, lanes.shape, 1)
    return jnp.sum(jnp.where(lane == pos[2], lanes.astype(F32), 0.0), axis=1, keepdims=True)


def scale_grads(pos, received):
    slots, wide = received.shape
    half = (wide - EXTRA) // 2
    rows = slots // 4

    def body(pos_ref, rec, mine, give):
        core = pos_ref[1]
        for r in range(0, slots, rows):
            at = slice(r, r + rows)
            gate = gate_of(pos_ref, rec[at, 2 * half :])
            for out, which in ((mine, core), (give, 1 - core)):
                start = pl.multiple_of(which * half, half)
                out[at, :] = (gate * rec[at, pl.ds(start, half)].astype(F32)).astype(BF16)

    return call(body, pos, [received], [((slots, half), BF16)] * 2)


def pre_grads(pos, received, weight_out, act, slope):
    slots, wide = received.shape
    hidden, width = weight_out.shape
    step = hidden // 4

    def body(pos_ref, rec, weight, act_ref, slope_ref, grad_pre, give, gate_grad):
        gate = gate_of(pos_ref, rec[:, width:])
        total = None
        for i in range(4):
            at = slice(i * step, (i + 1) * step)
            grad_act = lax.dot_general(
                rec[:, :width], weight[at, :], (((1,), (1,)), ((), ())), preferred_element_type=F32
            )
            part = jnp.sum(act_ref[:, at].astype(F32) * grad_act, axis=1, keepdims=True)
            total = part if total is None else total + part
            grad_pre[:, at] = (gate * grad_act * slope_ref[:, at]).astype(BF16)
        gate_grad[...] = total
        start = pl.multiple_of((1 - pos_ref[1]) * (hidden // 2), hidden // 2)
        give[...] = grad_pre[:, pl.ds(start, hidden // 2)]

    return call(
        body,
        pos,
        [received, weight_out, act, slope],
        [((slots, hidden), BF16), ((slots, hidden // 2), BF16), ((slots, 1), F32)],
    )


def row_products(pos_ref, refs, own_offset, masks, width, cols):
    lm, lo, rm, ro = refs
    dims = (((0,), (0,)), ((), ()))
    for i in range(2):
        own = pl.multiple_of((own_offset * pos_ref[1] + i) * cols, cols)
        for j in range(2):
            start = pl.multiple_of((pos_ref[0] ^ masks[i][j]) * width, width)
            value = lax.dot_general(
                lm[:, pl.ds(start, width)],
                rm[:, pl.ds(own, cols)],
                dims,
                preferred_element_type=F32,
            )
            value = value + lax.dot_general(
                lo[:, pl.ds(start, width)],
                ro[:, i * cols : (i + 1) * cols],
                dims,
                preferred_element_type=F32,
            )
            yield i, j, value


def sent_parts(pos, left_out, right_out, left_in, right_in):
    width_out, width_in = left_out[0].shape[1] // 4, left_in[0].shape[1] // 4
    cols_out, cols_in = right_out[1].shape[1] // 2, right_in[1].shape[1] // 2
    masks = ((1, 2), (3, 2))

    def body(pos_ref, *refs):
        outs = refs[8:]
        for i, j, value in row_products(pos_ref, refs[:4], 0, masks, width_out, cols_out):
            outs[i][j * width_out : (j + 1) * width_out, :] = value.astype(BF16)
        for i, j, value in row_products(pos_ref, refs[4:8], 2, masks, width_in, cols_in):
            outs[i][2 * width_out :, j * cols_in : (j + 1) * cols_in] = value.astype(BF16)

    return call(
        body,
        pos,
        [*left_out, *right_out, *left_in, *right_in],
        [((2 * width_out + width_in, cols_out), BF16)] * 2,
    )


def kept_parts(pos, left_out, right_out, left_in, right_in, got):
    width_out, width_in = left_out[0].shape[1] // 4, left_in[0].shape[1] // 4
    cols_out, cols_in = right_out[1].shape[1] // 2, right_in[1].shape[1] // 2
    masks = ((0, 3), (0, 1))
    half = width_in // 2

    def body(pos_ref, *refs):
        arrived = refs[8:10]
        near_out, near_in, far = refs[10:12], refs[12:14], refs[14:16]
        for i, j, value in row_products(pos_ref, refs[:4], 0, masks, width_out, cols_out):
            at = slice(j * width_out, (j + 1) * width_out)
            value = value + arrived[i][at, :].astype(F32)
            if j == 0:
                near_out[i][...] = value
            else:
                far[i][:width_out, :] = value.astype(BF16)
        for i, j, value in row_products(pos_ref, refs[4:8], 2, masks, width_in, cols_in):
            at = slice(j * cols_in, (j + 1) * cols_in)
            value = value + arrived[i][2 * width_out :, at].astype(F32)
            if j == 0:
                near_in[i][...] = value
            else:
                value = value.astype(BF16)
                far[i][width_out:, :cols_in] = value[:half, :]
                far[i][width_out:, cols_in:] = value[half:, :]

    return call(
        body,
        pos,
        [*left_out, *right_out, *left_in, *right_in, *got],
        [((width_out, cols_out), F32)] * 2
        + [((width_in, cols_in), F32)] * 2
        + [((width_out + half, cols_out), BF16)] * 2,
        LONG,
    )


def zh_pieces(pos, near_out, near_in, far, scale):
    rows_out, cols_out = near_out[0].shape
    rows_in, cols_in = near_in[0].shape
    half = rows_in // 2
    share_out, share_in = rows_out // 8, rows_in // 8

    def body(pos_ref, out_a, out_b, in_a, in_b, far_a, far_b, pieces):
        for i, (out, inner, arrived) in enumerate(((out_a, in_a, far_a), (out_b, in_b, far_b))):
            value = (out[...] + arrived[:rows_out, :].astype(F32)) * scale
            value = value.astype(BF16).reshape(8, share_out, cols_out)
            pieces[:, :share_out, i * cols_out : (i + 1) * cols_out] = value
            for k in range(2):
                value = inner[k * half : (k + 1) * half, :]
                value = value + arrived[rows_out:, k * cols_in : (k + 1) * cols_in].astype(F32)
                value = (value * scale).astype(BF16).reshape(4, 2, share_in // 2, cols_in)
                for m in range(2):
                    start = m * 2 * cols_in + i * cols_in
                    pieces[4 * k : 4 * k + 4, share_out:, start : start + cols_in] = value[:, m]

    return call(
        body,
        pos,
        [*near_out, *near_in, *far],
        [((8, share_out + share_in // 2, 2 * cols_out), BF16)],
    )[0]


def shares(pos, pieces, share_out):
    rows, cols = pieces.shape[1:]
    rows_in = rows - share_out
    cols_in = cols // 2

    def body(pos_ref, got, outer, inner):
        for c in range(2):
            value = sum(got[2 * z + c].astype(F32) for z in range(4))
            outer[:, c * cols : (c + 1) * cols] = value[:share_out]
            at = slice(c * cols_in, (c + 1) * cols_in)
            inner[:rows_in, at] = value[share_out:, :cols_in]
            inner[rows_in:, at] = value[share_out:, cols_in:]

    outer, inner = call(
        body, pos, [pieces], [((share_out, 2 * cols), F32), ((2 * rows_in, cols), F32)]
    )
    return outer[None], inner[None]


def slot_grads_of(pos, grad_pre, weight_in, gate_grad):
    slots, hidden = grad_pre.shape
    width = weight_in.shape[0]
    step = width // 4

    def body(pos_ref, grad, weight, gate, out):
        for i in range(4):
            at = slice(i * step, (i + 1) * step)
            out[:, at] = lax.dot_general(
                grad[...], weight[at, :], (((1,), (1,)), ((), ())), preferred_element_type=F32
            ).astype(BF16)
        lane = lax.broadcasted_iota(jnp.int32, (slots, EXTRA), 1)
        out[:, width:] = jnp.where(lane == pos_ref[2], gate[...], 0.0).astype(BF16)

    return call(
        body, pos, [grad_pre, weight_in, gate_grad], [((slots, width + EXTRA), BF16)]
    )[0]


def token_grads(pos, dispatch, back, tokens, weight_lanes, probs, combine, keep, denominator, scale):
    rows, width = tokens.shape
    experts = 8
    step = width // 4

    def body(pos_ref, disp, flat, tok, weight, p_ref, c_ref, k_ref, d_ref, out, router):
        dims = (((0,), (0,)), ((), ()))
        combine_grad = lax.dot_general(
            disp[...], flat[:, width:], dims, preferred_element_type=F32
        )
        weighted = jnp.sum(combine_grad * c_ref[...], axis=1, keepdims=True)
        probs_grad = k_ref[...] * (combine_grad - weighted) / d_ref[...]
        probs = p_ref[...]
        inner = jnp.sum(probs_grad * probs, axis=1, keepdims=True)
        logit_b = (probs * (probs_grad - inner)).astype(BF16)
        for i in range(4):
            at = slice(i * step, (i + 1) * step)
            part = lax.dot_general(logit_b, tok[:, at], dims, preferred_element_type=F32)
            router[:, at] = part[:experts] * scale
            value = lax.dot_general(disp[...], flat[:, at], dims, preferred_element_type=F32)
            value = value + lax.dot_general(
                logit_b, weight[at, :], (((1,), (1,)), ((), ())), preferred_element_type=F32
            )
            out[:, at] = value.astype(BF16)

    return call(
        body,
        pos,
        [dispatch, back, tokens, weight_lanes, probs, combine, keep, denominator],
        [((rows, width), BF16), ((experts, width), F32)],
    )


def per_device(
    tokens, grad_out, router_weight, weight_in, weight_out, expert_ids, slot_index, keep_mask
):
    tok_rows, model_width = tokens.shape
    experts = 8
    weight_in = weight_in[0]
    weight_out = weight_out[0]
    capacity = tok_rows * expert_ids.shape[1] // experts
    slot_count = experts * capacity
    grad_scale = float(tok_rows * 256) ** (-0.5)
    core = lax.axis_index("core")
    my_y = lax.axis_index("y")

    target = expert_ids * capacity + slot_index
    slot_iota = jnp.arange(slot_count, dtype=jnp.int32)[:, None]
    first_hit = (slot_iota == target[None, :, 0]) & (keep_mask[None, :, 0] == 1)
    second_hit = (slot_iota == target[None, :, 1]) & (keep_mask[None, :, 1] == 1)
    dispatch = (first_hit | second_hit).astype(BF16)

    send_tokens = jnp.dot(dispatch, tokens, preferred_element_type=F32).astype(BF16)
    slot_tokens = exchange(
        send_tokens.reshape(experts, capacity, model_width), GROUP
    ).reshape(slot_count, model_width)

    logits = jnp.dot(tokens, router_weight, preferred_element_type=F32)
    exp_logits = jnp.exp(logits)
    router_probs = exp_logits / jnp.sum(exp_logits, axis=1, keepdims=True)
    picked = expert_ids[:, :, None] == jnp.arange(experts, dtype=jnp.int32)[None, None, :]
    chosen = jnp.sum(jnp.where(picked, router_probs[:, None, :], 0.0), axis=2)
    keep_float = keep_mask.astype(F32)
    denominator = jnp.sum(keep_float * chosen, axis=1) + (1.0 - jnp.max(keep_float, axis=1))
    combine = keep_float * chosen / denominator[:, None]
    def lanes(values, fill=0.0):
        return jnp.pad(values, ((0, 0), (0, EXTRA - experts)), constant_values=fill)

    probs_lanes = lanes(router_probs)
    combine_lanes = lanes(jnp.sum(jnp.where(picked, combine[:, :, None], 0.0), axis=1))
    keep_lanes = lanes(jnp.sum(jnp.where(picked, keep_float[:, :, None], 0.0), axis=1))
    denominator_lanes = jnp.broadcast_to(denominator[:, None], (tok_rows, EXTRA))
    weight_lanes = lanes(router_weight)
    gate_lanes = combine_lanes.astype(BF16)
    send_grads = jnp.dot(dispatch, grad_out, preferred_element_type=F32).astype(BF16)
    send_gates = jnp.dot(dispatch, gate_lanes, preferred_element_type=F32).astype(BF16)
    received = exchange(
        jnp.concatenate([send_grads, send_gates], axis=1).reshape(
            experts, capacity, model_width + EXTRA
        ),
        GROUP,
    ).reshape(slot_count, model_width + EXTRA)
    other_tokens = swap(slot_tokens, "core", 1)
    hidden_pre = jnp.dot(slot_tokens, weight_in, preferred_element_type=F32)
    normal_cdf, normal_pdf = gelu_parts(hidden_pre)
    hidden_act = (hidden_pre * normal_cdf).astype(BF16)
    act_slope = normal_cdf + hidden_pre * normal_pdf
    other_act = swap(hidden_act, "core", 1)
    left_in = (slot_tokens, other_tokens)
    left_out = (hidden_act, other_act)
    pos = jnp.stack([my_y, core, lax.axis_index(GROUP), lax.axis_index("zh")]).astype(jnp.int32)


    (received, left_in, left_out, act_slope, dispatch, weight_lanes) = tie(
        received, left_in, left_out, act_slope, dispatch, weight_lanes
    )
    probs_lanes, combine_lanes, keep_lanes, denominator_lanes, _ = tie(
        probs_lanes, combine_lanes, keep_lanes, denominator_lanes, act_slope
    )
    my_out, give_out = scale_grads(pos, received)
    right_out = (my_out, swap(give_out, "core", 1))
    received, _ = tie(received, give_out)
    grad_pre, give_in, gate_grad = pre_grads(
        pos, received, weight_out, left_out[0], act_slope
    )
    right_in = (grad_pre, swap(give_in, "core", 1))

    sent = sent_parts(pos, left_out, right_out, left_in, right_in)
    got = (swap(sent[0], "y", 1), swap(sent[1], "y", 3))
    pre_for_slots, _ = tie(grad_pre, sent)
    grad_slots = slot_grads_of(pos, pre_for_slots, weight_in, gate_grad)
    back = exchange(
        grad_slots.reshape(experts, capacity, model_width + EXTRA), GROUP
    ).reshape(slot_count, model_width + EXTRA)

    left_in, left_out, right_in, right_out, _ = tie(
        left_in, left_out, right_in, right_out, grad_slots
    )
    *near, far_a, far_b = kept_parts(pos, left_out, right_out, left_in, right_in, got)
    far = (swap(far_a, "y", 3), swap(far_b, "y", 1))

    back, _ = tie(back, far_a)
    grad_tokens, router_part = token_grads(
        pos,
        dispatch,
        back,
        tokens,
        weight_lanes,
        probs_lanes,
        combine_lanes,
        keep_lanes,
        denominator_lanes,
        grad_scale,
    )

    def router_steps(value, first, last):
        for axis, mask in ROUTER_STEPS[first:last]:
            value = value + swap(value, axis, mask)
        return value

    router_part = router_steps(router_part, 0, 2)
    near, _ = tie(near, router_part)
    pieces = zh_pieces(pos, near[:2], near[2:], far, grad_scale)
    router_part, _ = tie(router_part, pieces)
    got = exchange(pieces, ("zh", "core"))
    router_part = router_steps(router_part, 2, 8)
    got, router_part = tie(got, router_part)
    outer_share, inner_share = shares(pos, got, near[0].shape[0] // 8)
    return (grad_tokens, router_part.T, inner_share, outer_share)


def solution(mesh):
    fine = Mesh(mesh.devices.reshape(FINE_SHAPE), FINE)
    placed = (
        P(FINE, None),
        P(FINE, None),
        P(),
        P(GROUP, None, None),
        P(GROUP, None, None),
        P(FINE, None),
        P(FINE, None),
        P(FINE, None),
    )
    return jax.shard_map(
        per_device,
        mesh=fine,
        in_specs=placed,
        out_specs=(
            P(FINE, None),
            P(),
            P(GROUP, ("y", "zh", "core"), None),
            P(GROUP, ("y", "zh", "core"), None),
        ),
        check_vma=False,
    )
```

time: 199 us -> 207 us (1.040)
  the two profiles are of different devices: /device:TPU:46 before, /device:TPU:2 now
where the time goes in v6:
time: 207 us; the launch traced here: 206 us
  waiting for transfers between devices  94.3 us (46%)
  starting transfers between devices  42.9 us (21%)
  Pallas kernels  30.9 us (15%)
  local copies, waits for them, and re-layouts  19.3 us (9%)
  matrix products  12.2 us (6%)
  other arithmetic  4.93 us (2%)
    ppermute x16, waiting for transfers between devices, swap(): return lax.ppermute(values, axis, [(i, i ^ mask) for i in range(size)])  59.4 us
    all_to_all x4, waiting for transfers between devices, exchange(): return lax.all_to_all(values, axes, split_axis=0, concat_axis=0, tiled=True)  34.9 us
    pallas_call x8, Pallas kernels, call(): pl.pallas_call(body, in_specs=[pl.BlockSpec(memory_space=pltpu.SMEM)] + [...  30.9 us
    all_to_all x4, starting transfers between devices, exchange(): return lax.all_to_all(values, axes, split_axis=0, concat_axis=0, tiled=True)  25.6 us
    ppermute x16, starting transfers between devices, swap(): return lax.ppermute(values, axis, [(i, i ^ mask) for i in range(size)])  17.3 us
    unnamed x79, local copies, waits for them, and re-layouts  14.8 us
    dot_general x1, matrix products, per_device(): hidden_pre = jnp.dot(slot_tokens, weight_in, preferred_element_type=F32)  7.46 us
  transfers between devices with their start and end apart: 20, of which 13 were waited for; matrix products, arithmetic and copies ran while one was open for 9% of the time, Pallas kernels for 9%

profile of v6, /device:TPU:2, one launch (start us, length us, event | category | flops | bytes accessed | tf_op | source)
XLA Modules:
  0.0 205.6 jit_solution(14198539575468288788)
XLA Ops:
  0.6 0.8 compare_reduce_fusion.1
  1.5 0.7 multiply_add_fusion
  2.2 3.3 %convolution_convert_fusion = bf16[512,2048]{1,0:T(8,128)(2,1)} fusion(bf16[256,2048]{1,0:T(8,128)(2,1)} %tok.1, s32[256]{0:T(256)S(1)} %bitcast.37, s32[256]{0:T(256)S(1)} %bitcast.33, pred[256]{0:T(512)(128)(4,1)S(1)} %get-tuple-element.101, pred[256]{0:T(512)(128)(4,1)S(1)} %get-tuple-element.100), kind=kOutput, calls=%fused_computation.1 | convolution fusion | flops 538574848 | bytes 3148288 | tf_op jit(solution)/shard_map/dot_general | solution.py:313
  5.5 6.6 %all-to-all-start.1 = ((bf16[8,64,2048]{2,1,0:T(8,128)(2,1)}), bf16[8,64,2048]{2,1,0:T(8,128)(2,1)}, u32[]{:S(2)}, u32[]{:S(2)}) async-start(bf16[8,64,2048]{2,1,0:T(8,128)(2,1)} %bitcast.31), calls=%async_computation.1 | async-start | bytes 4194304 | tf_op jit(solution)/shard_map/all_to_all | solution.py:48
  12.2 0.4 fusion.17
  13.0 0.5 copy-done.35
  14.0 0.7 convolution_convert_fusion.1
  14.8 1.6 pad_maximum_fusion
  16.4 20.8 %all-to-all-done.1 = bf16[8,64,2048]{2,1,0:T(8,128)(2,1)} async-done(((bf16[8,64,2048]{2,1,0:T(8,128)(2,1)}), bf16[8,64,2048]{2,1,0:T(8,128)(2,1)}, u32[]{:S(2)}, u32[]{:S(2)}) %all-to-all-start.1) | async-done | bytes 2097184 | tf_op jit(solution)/shard_map/all_to_all | solution.py:48
  37.2 5.3 %all-to-all-start = ((bf16[8,64,2176]{2,1,0:T(8,128)(2,1)}), bf16[8,64,2176]{2,1,0:T(8,128)(2,1)S(1)}, u32[]{:S(2)}, u32[]{:S(2)}) async-start(bf16[8,64,2176]{2,1,0:T(8,128)(2,1)} %bitcast.30), calls=%async_computation | async-start | bytes 4456448 | tf_op jit(solution)/shard_map/all_to_all | solution.py:48
  42.5 7.5 %fusion.3 = (f32[512,1024]{1,0:T(8,128)}, bf16[512,1024]{1,0:T(8,128)(2,1)}) fusion(bf16[512,2048]{1,0:T(8,128)(2,1)} %bitcast.9.refs_4_, bf16[1,2048,1024]{2,1,0:T(8,128)(2,1)} %param.11), kind=kOutput, calls=%fused_computation.7 | convolution fusion | flops 2152726528 | bytes 9437184 | tf_op jit(solution)/shard_map/dot_general | solution.py:344
  49.9 0.5 collective-permute-start.1
  50.4 1.0 copy.28
  51.5 2.0 pad.15.weight
  53.5 0.9 fusion.12.disp
  54.4 14.1 %all-to-all-done = bf16[8,64,2176]{2,1,0:T(8,128)(2,1)S(1)} async-done(((bf16[8,64,2176]{2,1,0:T(8,128)(2,1)}), bf16[8,64,2176]{2,1,0:T(8,128)(2,1)S(1)}, u32[]{:S(2)}, u32[]{:S(2)}) %all-to-all-start) | async-done | bytes 2228256 | tf_op jit(solution)/shard_map/all_to_all | solution.py:48
  68.4 1.0 shard_map.111
  69.5 0.5 copy-done.7
  70.0 2.2 %copy-done.3 = bf16[1,1024,2048]{2,1,0:T(8,128)(2,1)S(1)} copy-done((bf16[1,1024,2048]{2,1,0:T(8,128)(2,1)S(1)}, bf16[1,1024,2048]{2,1,0:T(8,128)(2,1)}, u32[]{:S(2)}) %copy-start.3) | copy-done | bytes 4194328
  72.2 3.8 %shard_map.112 = (bf16[512,1024]{1,0:T(8,128)(2,1)S(1)}, bf16[512,512]{1,0:T(8,128)(2,1)S(1)}, f32[512,1]{1,0:T(8,128)S(1)}) custom-call(s32[4]{0:T(128)S(1)} %pad_add_fusion.pos_ref, bf16[512,2176]{1,0:T(8,128)(2,1)S(1)} %bitcast.27, bf16[1024,2048]{1,0:T(8,128)(2,1)S(1)} %bitcast.28, bf16[512,1024]{1,0:T(8,128)(2,1)} %get-tuple-element.67.act_ref.refs_0_, ...), custom_call_target="tpu_custom_call" | custom-call | flops 1000 | bytes 1000 | tf_op jit(solution)/shard_map/pallas_call | solution.py:57
  76.3 1.9 collective-permute-done.3.refs_7_
  78.2 6.9 %shard_map.113 = (bf16[1024,512]{1,0:T(8,128)(2,1)}, bf16[1024,512]{1,0:T(8,128)(2,1)}) custom-call(s32[4]{0:T(128)S(1)} %pad_add_fusion.pos_ref, bf16[512,1024]{1,0:T(8,128)(2,1)} %get-tuple-element.67.act_ref.refs_0_, bf16[512,1024]{1,0:T(8,128)(2,1)} %collective-permute-done.1.refs_1_, bf16[512,1024]{1,0:T(8,128)(2,1)S(1)} %get-tuple-element.69.refs_2_, ...), custom_call_target="tpu_custom_call" | custom-call | flops 1000 | bytes 1000 | tf_op jit(solution)/shard_map/pallas_call | solution.py:57
  85.1 1.6 collective-permute-start.4
  86.8 2.2 %collective-permute-start.5 = (bf16[1024,512]{1,0:T(8,128)(2,1)}, bf16[1024,512]{1,0:T(8,128)(2,1)}, u32[]{:S(2)}, u32[]{:S(2)}) collective-permute-start(bf16[1024,512]{1,0:T(8,128)(2,1)} %get-tuple-element.64), channel_id=1, source_target_pairs={{0,192},{64,128},{128,64},{192,0},{1,193},{65,129},{129,65},{193,1... | collective-permute-start | bytes 3145736 | tf_op jit(solution)/shard_map/ppermute | solution.py:44
  89.0 4.3 %shard_map.114 = bf16[512,2176]{1,0:T(8,128)(2,1)} custom-call(s32[4]{0:T(128)S(1)} %pad_add_fusion.pos_ref, bf16[512,1024]{1,0:T(8,128)(2,1)S(1)} %get-tuple-element.73.refs_6_.grad, bf16[2048,1024]{1,0:T(8,128)(2,1)S(1)} %bitcast.29, f32[512,1]{1,0:T(8,128)S(1)} %get-tuple-element.66.gate), custom_call_target="tpu_custom_call" | custom-call | flops 1000 | bytes 1000 | tf_op jit(solution)/shard_map/pallas_call | solution.py:57
  93.3 6.1 %all-to-all-start.2 = ((bf16[8,64,2176]{2,1,0:T(8,128)(2,1)}), bf16[8,64,2176]{2,1,0:T(8,128)(2,1)}, u32[]{:S(2)}, u32[]{:S(2)}) async-start(bf16[8,64,2176]{2,1,0:T(8,128)(2,1)} %bitcast.12), calls=%async_computation.2 | async-start | bytes 4456448 | tf_op jit(solution)/shard_map/all_to_all | solution.py:48
  99.4 11.3 %collective-permute-done.4.refs_8_ = bf16[1024,512]{1,0:T(8,128)(2,1)} collective-permute-done((bf16[1024,512]{1,0:T(8,128)(2,1)}, bf16[1024,512]{1,0:T(8,128)(2,1)}, u32[]{:S(2)}, u32[]{:S(2)}) %collective-permute-start.4) | collective-permute-done | bytes 1048608 | tf_op jit(solution)/shard_map/ppermute | solution.py:44
  110.7 2.5 %collective-permute-done.5.refs_9_ = bf16[1024,512]{1,0:T(8,128)(2,1)} collective-permute-done((bf16[1024,512]{1,0:T(8,128)(2,1)}, bf16[1024,512]{1,0:T(8,128)(2,1)}, u32[]{:S(2)}, u32[]{:S(2)}) %collective-permute-start.5) | collective-permute-done | bytes 1048608 | tf_op jit(solution)/shard_map/ppermute | solution.py:44
  113.2 1.2 copy-done.10
  114.5 1.2 copy-done.12
  115.7 1.0 copy-done.22
  116.7 6.7 %shard_map.115 = (f32[256,512]{1,0:T(8,128)S(1)}, f32[256,512]{1,0:T(8,128)S(1)}, f32[512,256]{1,0:T(8,128)S(1)}, f32[512,256]{1,0:T(8,128)S(1)}, bf16[512,512]{1,0:T(8,128)(2,1)}, /*index=5*/bf16[512,512]{1,0:T(8,128)(2,1)}) custom-call(s32[4]{0:T(128)S(1)} %pad_add_fusion.pos_ref, bf16[512,1024]{1,0:T(8,128)(2,1)} %get-tuple-element.67.act_ref.refs_0_, ...), custom_call_target="tpu_custom_call" | custom-call | flops 60000002048 | bytes 1000 | tf_op jit(solution)/shard_map/pallas_call | solution.py:57
  123.5 0.8 copy-done.13
  124.3 0.8 copy-done.15
  125.1 0.8 copy-done.17
  125.9 0.8 copy-done.19
  126.7 2.3 %collective-permute-start.8 = (bf16[512,512]{1,0:T(8,128)(2,1)}, bf16[512,512]{1,0:T(8,128)(2,1)}, u32[]{:S(2)}, u32[]{:S(2)}) collective-permute-start(bf16[512,512]{1,0:T(8,128)(2,1)} %get-tuple-element.75), channel_id=1, source_target_pairs={{0,192},{64,128},{128,64},{192,0},{1,193},{65,129},{129,65},{193,1... | collective-permute-start | bytes 1572872 | tf_op jit(solution)/shard_map/ppermute | solution.py:44
  129.0 0.7 pad.14.c_ref
  129.8 0.7 pad.17.k_ref
  130.5 0.8 broadcast_in_dim.52.d_ref
  131.2 1.0 copy-done.8
  132.3 0.9 copy-done.23
  133.2 0.9 copy-done.24
  134.1 0.9 copy-done.25
  135.0 4.3 %shard_map.116 = (bf16[256,2048]{1,0:T(8,128)(2,1)}, f32[8,2048]{1,0:T(8,128)S(1)}) custom-call(s32[4]{0:T(128)S(1)} %pad_add_fusion.pos_ref, bf16[512,256]{1,0:T(8,128)(2,1)S(1)} %fusion.12.disp, bf16[512,2176]{1,0:T(8,128)(2,1)} %bitcast.13.flat, bf16[256,2048]{1,0:T(8,128)(2,1)S(1)} %copy-done.2, bf16[2048,128]{1,0:T(8,128)(2,1)S(1)} %copy-done.8, ...), custom_call_target="tpu_custom_call" | custom-call | flops 1000 | bytes 1000 | tf_op jit(solution)/shard_map/pallas_call | solution.py:57
  139.3 1.3 collective-permute-done.6
  140.6 1.9 collective-permute-start.7
  142.5 2.5 %collective-permute-done.7 = f32[8,2048]{1,0:T(8,128)S(1)} collective-permute-done((f32[8,2048]{1,0:T(8,128)S(1)}, f32[8,2048]{1,0:T(8,128)S(1)}, u32[]{:S(2)}, u32[]{:S(2)}) %collective-permute-start.7) | collective-permute-done | bytes 65568 | tf_op jit(solution)/shard_map/ppermute | solution.py:44
  145.0 2.4 %shard_map.117 = bf16[8,64,1024]{2,1,0:T(8,128)(2,1)} custom-call(s32[4]{0:T(128)S(1)} %pad_add_fusion.pos_ref, f32[256,512]{1,0:T(8,128)S(1)} %copy-done.14, f32[256,512]{1,0:T(8,128)S(1)} %copy-done.16, f32[512,256]{1,0:T(8,128)S(1)} %copy-done.18, f32[512,256]{1,0:T(8,128)S(1)} %copy-done.20, bf16[512,512]{1,0:T(8,128)(2,1)} %collective-permute-done.8.far_a, ...), custom_call_target="tpu_custom_call" | custom-call | flops 1000 | bytes 1000 | tf_op jit(solution)/shard_map/pallas_call | solution.py:57
  147.5 7.6 %all-to-all-start.3 = ((bf16[8,64,1024]{2,1,0:T(8,128)(2,1)}), bf16[8,64,1024]{2,1,0:T(8,128)(2,1)S(1)}, u32[]{:S(2)}, u32[]{:S(2)}) async-start(bf16[8,64,1024]{2,1,0:T(8,128)(2,1)} %shard_map.117), calls=%async_computation.3 | async-start | bytes 2097152 | tf_op jit(solution)/shard_map/all_to_all | solution.py:48
  155.1 0.8 collective-permute-start.10
  155.8 3.7 %collective-permute-done.10 = f32[8,2048]{1,0:T(8,128)S(1)} collective-permute-done((f32[8,2048]{1,0:T(8,128)S(1)}, f32[8,2048]{1,0:T(8,128)S(1)}, u32[]{:S(2)}, u32[]{:S(2)}) %collective-permute-start.10) | collective-permute-done | bytes 65568 | tf_op jit(solution)/shard_map/ppermute | solution.py:44
  159.6 1.2 collective-permute-start.11
  160.8 20.9 %collective-permute-done.11 = f32[8,2048]{1,0:T(8,128)S(1)} collective-permute-done((f32[8,2048]{1,0:T(8,128)S(1)}, f32[8,2048]{1,0:T(8,128)S(1)}, u32[]{:S(2)}, u32[]{:S(2)}) %collective-permute-start.11) | collective-permute-done | bytes 65568 | tf_op jit(solution)/shard_map/ppermute | solution.py:44
  181.7 1.4 collective-permute-start.12
  183.1 2.9 %collective-permute-done.12 = f32[8,2048]{1,0:T(8,128)S(1)} collective-permute-done((f32[8,2048]{1,0:T(8,128)S(1)}, f32[8,2048]{1,0:T(8,128)S(1)}, u32[]{:S(2)}, u32[]{:S(2)}) %collective-permute-start.12) | collective-permute-done | bytes 65568 | tf_op jit(solution)/shard_map/ppermute | solution.py:44
  186.0 1.1 collective-permute-start.13
  187.1 4.5 %collective-permute-done.13 = f32[8,2048]{1,0:T(8,128)S(1)} collective-permute-done((f32[8,2048]{1,0:T(8,128)S(1)}, f32[8,2048]{1,0:T(8,128)S(1)}, u32[]{:S(2)}, u32[]{:S(2)}) %collective-permute-start.13) | collective-permute-done | bytes 65568 | tf_op jit(solution)/shard_map/ppermute | solution.py:44
  191.6 0.8 collective-permute-start.14
  192.4 4.6 %collective-permute-done.14 = f32[8,2048]{1,0:T(8,128)S(1)} collective-permute-done((f32[8,2048]{1,0:T(8,128)S(1)}, f32[8,2048]{1,0:T(8,128)S(1)}, u32[]{:S(2)}, u32[]{:S(2)}) %collective-permute-start.14) | collective-permute-done | bytes 65568 | tf_op jit(solution)/shard_map/ppermute | solution.py:44
  197.0 3.2 %collective-permute-start.15 = (f32[8,2048]{1,0:T(8,128)S(1)}, f32[8,2048]{1,0:T(8,128)S(1)}, u32[]{:S(2)}, u32[]{:S(2)}) collective-permute-start(f32[8,2048]{1,0:T(8,128)S(1)} %add.66), channel_id=1, source_target_pairs={{0,48},{16,32},{32,16},{48,0},{1,49},{17,33},{33,17},{49,1},{2,50}... | collective-permute-start | bytes 196616 | tf_op jit(solution)/shard_map/ppermute | solution.py:44
  200.2 3.3 %collective-permute-done.15 = f32[8,2048]{1,0:T(8,128)S(1)} collective-permute-done((f32[8,2048]{1,0:T(8,128)S(1)}, f32[8,2048]{1,0:T(8,128)S(1)}, u32[]{:S(2)}, u32[]{:S(2)}) %collective-permute-start.15) | collective-permute-done | bytes 65568 | tf_op jit(solution)/shard_map/ppermute | solution.py:44
  203.5 0.6 add.67
  204.2 1.4 shard_map.118
  (98 shorter events, 1.6 us)
Async XLA Ops:
  0.6 13.4 %copy-start = (bf16[256,2048]{1,0:T(8,128)(2,1)S(1)}, bf16[256,2048]{1,0:T(8,128)(2,1)}, u32[]{:S(2)}) copy-start(bf16[256,2048]{1,0:T(8,128)(2,1)} %param.9) | copy-start | bytes 3145732
  1.5 12.5 %copy-start.37 = (pred[256]{0:T(512)(128)(4,1)}, pred[256]{0:T(512)(128)(4,1)S(1)}, u32[]{:S(2)}) copy-start(pred[256]{0:T(512)(128)(4,1)S(1)} %get-tuple-element.100) | copy-start | bytes 772
  1.5 12.5 %copy-start.38 = (pred[256]{0:T(512)(128)(4,1)}, pred[256]{0:T(512)(128)(4,1)S(1)}, u32[]{:S(2)}) copy-start(pred[256]{0:T(512)(128)(4,1)S(1)} %get-tuple-element.101) | copy-start | bytes 772
  2.2 11.8 %copy-start.34 = (s32[256,1]{0,1:T(1,128)}, s32[256,1]{0,1:T(1,128)S(1)}, u32[]{:S(2)}) copy-start(s32[256,1]{0,1:T(1,128)S(1)} %get-tuple-element.107) | copy-start | bytes 3076
  5.5 6.6 %copy-start.32 = (s32[256,2]{0,1:T(2,128)S(1)}, s32[256,2]{0,1:T(2,128)}, u32[]{:S(2)}) copy-start(s32[256,2]{0,1:T(2,128)} %param.15) | copy-start | bytes 6148
  5.5 6.7 %copy-start.1 = (bf16[256,2048]{1,0:T(8,128)(2,1)S(1)}, bf16[256,2048]{1,0:T(8,128)(2,1)}, u32[]{:S(2)}) copy-start(bf16[256,2048]{1,0:T(8,128)(2,1)} %tok.1) | copy-start | bytes 3145732
  5.5 6.7 %copy-start.30 = (bf16[2048,8]{0,1:T(8,128)(2,1)S(1)}, bf16[2048,8]{0,1:T(8,128)(2,1)}, u32[]{:S(2)}) copy-start(bf16[2048,8]{0,1:T(8,128)(2,1)} %param.10) | copy-start | bytes 98308
  5.5 7.4 %copy-start.33 = (s32[256,2]{0,1:T(2,128)S(1)}, s32[256,2]{0,1:T(2,128)}, u32[]{:S(2)}) copy-start(s32[256,2]{0,1:T(2,128)} %param.13) | copy-start | bytes 6148
  5.5 31.6 %all-to-all-start.1 = ((bf16[8,64,2048]{2,1,0:T(8,128)(2,1)}), bf16[8,64,2048]{2,1,0:T(8,128)(2,1)}, u32[]{:S(2)}, u32[]{:S(2)}) async-start(bf16[8,64,2048]{2,1,0:T(8,128)(2,1)} %bitcast.31), calls=%async_computation.1 | async-start | bytes 4194304 | tf_op jit(solution)/shard_map/all_to_all | solution.py:48
  12.9 1.9 copy-start.26
  13.0 0.6 copy-start.35
  13.7 2.7 %copy-start.28 = (f32[256,8]{1,0:T(8,128)}, f32[256,8]{1,0:T(8,128)S(1)}, u32[]{:S(2)}) copy-start(f32[256,8]{1,0:T(8,128)S(1)} %copy.26) | copy-start | bytes 24580
  37.2 31.3 %all-to-all-start = ((bf16[8,64,2176]{2,1,0:T(8,128)(2,1)}), bf16[8,64,2176]{2,1,0:T(8,128)(2,1)S(1)}, u32[]{:S(2)}, u32[]{:S(2)}) async-start(bf16[8,64,2176]{2,1,0:T(8,128)(2,1)} %bitcast.30), calls=%async_computation | async-start | bytes 4456448 | tf_op jit(solution)/shard_map/all_to_all | solution.py:48
  42.5 8.0 %copy-start.31 = (bf16[2048,8]{0,1:T(8,128)(2,1)S(1)}, bf16[2048,8]{0,1:T(8,128)(2,1)}, u32[]{:S(2)}) copy-start(bf16[2048,8]{0,1:T(8,128)(2,1)} %param.10) | copy-start | bytes 98308
  42.5 26.0 %collective-permute-start = (bf16[512,2048]{1,0:T(8,128)(2,1)}, bf16[512,2048]{1,0:T(8,128)(2,1)}, u32[]{:S(2)}, u32[]{:S(2)}) collective-permute-start(bf16[512,2048]{1,0:T(8,128)(2,1)} %bitcast.9.refs_4_), channel_id=1, source_target_pairs={{0,8},{8,0},{1,9},{9,1},{2,10},{10,2},{3,11},{11,3},{4,12},{12,4},... | collective-permute-start | bytes 6291464 | tf_op jit(solution)/shard_map/ppermute | solution.py:44
  49.9 18.5 %collective-permute-start.1 = (bf16[512,1024]{1,0:T(8,128)(2,1)}, bf16[512,1024]{1,0:T(8,128)(2,1)}, u32[]{:S(2)}, u32[]{:S(2)}) collective-permute-start(bf16[512,1024]{1,0:T(8,128)(2,1)} %get-tuple-element.67.act_ref.refs_0_), channel_id=1, source_target_pairs={{0,8},{8,0},{1,9},{9,1},{2,10},{10,2},{3,11},{11,3},{4,12},{12,4},... | collective-permute-start | bytes 3145736 | tf_op jit(solution)/shard_map/ppermute | solution.py:44
  68.4 1.6 copy-start.7
  69.4 8.8 %copy-start.9 = (bf16[512,1024]{1,0:T(8,128)(2,1)}, bf16[512,1024]{1,0:T(8,128)(2,1)S(1)}, u32[]{:S(2)}) copy-start(bf16[512,1024]{1,0:T(8,128)(2,1)S(1)} %get-tuple-element.69.refs_2_) | copy-start | bytes 3145732
  69.4 8.8 %collective-permute-start.2 = (bf16[512,1024]{1,0:T(8,128)(2,1)S(1)}, bf16[512,1024]{1,0:T(8,128)(2,1)S(1)}, u32[]{:S(2)}, u32[]{:S(2)}) collective-permute-start(bf16[512,1024]{1,0:T(8,128)(2,1)S(1)} %get-tuple-element.53), channel_id=1, source_target_pairs={{0,8},{8,0},{1,9},{9,1},{2,10},{10,2},{3,11},{11,3},{4,12},{12,4},... | collective-permute-start | bytes 3145736 | tf_op jit(solution)/shard_map/ppermute | solution.py:44
  70.0 2.2 %copy-start.3 = (bf16[1,1024,2048]{2,1,0:T(8,128)(2,1)S(1)}, bf16[1,1024,2048]{2,1,0:T(8,128)(2,1)}, u32[]{:S(2)}) copy-start(bf16[1,1024,2048]{2,1,0:T(8,128)(2,1)} %param.12) | copy-start | bytes 12582916
  76.0 12.9 %copy-start.5 = (bf16[512,1024]{1,0:T(8,128)(2,1)}, bf16[512,1024]{1,0:T(8,128)(2,1)S(1)}, u32[]{:S(2)}) copy-start(bf16[512,1024]{1,0:T(8,128)(2,1)S(1)} %get-tuple-element.73.refs_6_.grad) | copy-start | bytes 3145732
  76.0 2.2 %collective-permute-start.3 = (bf16[512,512]{1,0:T(8,128)(2,1)S(1)}, bf16[512,512]{1,0:T(8,128)(2,1)S(1)}, u32[]{:S(2)}, u32[]{:S(2)}) collective-permute-start(bf16[512,512]{1,0:T(8,128)(2,1)S(1)} %get-tuple-element.62), channel_id=1, source_target_pairs={{0,8},{8,0},{1,9},{9,1},{2,10},{10,2},{3,11},{11,3},{4,12},{12,4},... | collective-permute-start | bytes 1572872 | tf_op jit(solution)/shard_map/ppermute | solution.py:44
  78.2 6.9 %copy-start.21 = (bf16[512,512]{1,0:T(8,128)(2,1)}, bf16[512,512]{1,0:T(8,128)(2,1)S(1)}, u32[]{:S(2)}) copy-start(bf16[512,512]{1,0:T(8,128)(2,1)S(1)} %collective-permute-done.3.refs_7_) | copy-start | bytes 1572868
  78.2 6.9 %copy-start.11 = (bf16[512,1024]{1,0:T(8,128)(2,1)}, bf16[512,1024]{1,0:T(8,128)(2,1)S(1)}, u32[]{:S(2)}) copy-start(bf16[512,1024]{1,0:T(8,128)(2,1)S(1)} %collective-permute-done.2.refs_3_) | copy-start | bytes 3145732
  78.2 10.7 %copy-start.4 = (bf16[1,2048,1024]{2,1,0:T(8,128)(2,1)S(1)}, bf16[1,2048,1024]{2,1,0:T(8,128)(2,1)}, u32[]{:S(2)}) copy-start(bf16[1,2048,1024]{2,1,0:T(8,128)(2,1)} %param.11) | copy-start | bytes 12582916
  85.1 25.6 %collective-permute-start.4 = (bf16[1024,512]{1,0:T(8,128)(2,1)}, bf16[1024,512]{1,0:T(8,128)(2,1)}, u32[]{:S(2)}, u32[]{:S(2)}) collective-permute-start(bf16[1024,512]{1,0:T(8,128)(2,1)} %get-tuple-element.63), channel_id=1, source_target_pairs={{0,64},{64,0},{128,192},{192,128},{1,65},{65,1},{129,193},{193,129... | collective-permute-start | bytes 3145736 | tf_op jit(solution)/shard_map/ppermute | solution.py:44
  86.8 26.4 %collective-permute-start.5 = (bf16[1024,512]{1,0:T(8,128)(2,1)}, bf16[1024,512]{1,0:T(8,128)(2,1)}, u32[]{:S(2)}, u32[]{:S(2)}) collective-permute-start(bf16[1024,512]{1,0:T(8,128)(2,1)} %get-tuple-element.64), channel_id=1, source_target_pairs={{0,192},{64,128},{128,64},{192,0},{1,193},{65,129},{129,65},{193,1... | collective-permute-start | bytes 3145736 | tf_op jit(solution)/shard_map/ppermute | solution.py:44
  93.3 20.0 %copy-start.6 = (bf16[512,1024]{1,0:T(8,128)(2,1)S(1)}, bf16[512,1024]{1,0:T(8,128)(2,1)}, u32[]{:S(2)}) copy-start(bf16[512,1024]{1,0:T(8,128)(2,1)} %copy-done.5) | copy-start | bytes 3145732
  93.3 35.7 %copy-start.27 = (f32[256,8]{1,0:T(8,128)S(1)}, f32[256,8]{1,0:T(8,128)}, u32[]{:S(2)}) copy-start(f32[256,8]{1,0:T(8,128)} %copy-done.26) | copy-start | bytes 24580
  93.3 37.2 %copy-start.36 = (f32[256]{0:T(256)S(1)}, f32[256]{0:T(256)}, u32[]{:S(2)}) copy-start(f32[256]{0:T(256)} %copy-done.35) | copy-start | bytes 3076
  93.3 38.0 %all-to-all-start.2 = ((bf16[8,64,2176]{2,1,0:T(8,128)(2,1)}), bf16[8,64,2176]{2,1,0:T(8,128)(2,1)}, u32[]{:S(2)}, u32[]{:S(2)}) async-start(bf16[8,64,2176]{2,1,0:T(8,128)(2,1)} %bitcast.12), calls=%async_computation.2 | async-start | bytes 4456448 | tf_op jit(solution)/shard_map/all_to_all | solution.py:48
  99.4 31.8 %copy-start.2 = (bf16[256,2048]{1,0:T(8,128)(2,1)S(1)}, bf16[256,2048]{1,0:T(8,128)(2,1)}, u32[]{:S(2)}) copy-start(bf16[256,2048]{1,0:T(8,128)(2,1)} %tok.1) | copy-start | bytes 3145732
  113.2 1.2 copy-start.10
  114.5 1.2 copy-start.12
  115.7 1.0 copy-start.22
  116.7 12.3 %copy-start.29 = (f32[256,8]{1,0:T(8,128)S(1)}, f32[256,8]{1,0:T(8,128)}, u32[]{:S(2)}) copy-start(f32[256,8]{1,0:T(8,128)} %copy-done.28) | copy-start | bytes 24580
  123.5 0.8 copy-start.13
  124.3 0.8 copy-start.15
  125.1 0.8 copy-start.17
  125.9 0.8 copy-start.19
  126.7 18.3 %collective-permute-start.9 = (bf16[512,512]{1,0:T(8,128)(2,1)}, bf16[512,512]{1,0:T(8,128)(2,1)}, u32[]{:S(2)}, u32[]{:S(2)}) collective-permute-start(bf16[512,512]{1,0:T(8,128)(2,1)} %get-tuple-element.92), channel_id=1, source_target_pairs={{0,64},{64,0},{128,192},{192,128},{1,65},{65,1},{129,193},{193,129... | collective-permute-start | bytes 1572872 | tf_op jit(solution)/shard_map/ppermute | solution.py:44
  126.7 18.3 %collective-permute-start.8 = (bf16[512,512]{1,0:T(8,128)(2,1)}, bf16[512,512]{1,0:T(8,128)(2,1)}, u32[]{:S(2)}, u32[]{:S(2)}) collective-permute-start(bf16[512,512]{1,0:T(8,128)(2,1)} %get-tuple-element.75), channel_id=1, source_target_pairs={{0,192},{64,128},{128,64},{192,0},{1,193},{65,129},{129,65},{193,1... | collective-permute-start | bytes 1572872 | tf_op jit(solution)/shard_map/ppermute | solution.py:44
  131.2 1.0 copy-start.8
  132.3 0.9 copy-start.23
  133.2 0.9 copy-start.24
  134.1 0.9 copy-start.25
  135.0 10.0 %copy-start.14 = (f32[256,512]{1,0:T(8,128)S(1)}, f32[256,512]{1,0:T(8,128)}, u32[]{:S(2)}) copy-start(f32[256,512]{1,0:T(8,128)} %copy-done.13) | copy-start | bytes 1572868
  135.0 10.0 %copy-start.16 = (f32[256,512]{1,0:T(8,128)S(1)}, f32[256,512]{1,0:T(8,128)}, u32[]{:S(2)}) copy-start(f32[256,512]{1,0:T(8,128)} %copy-done.15) | copy-start | bytes 1572868
  135.0 10.0 %copy-start.18 = (f32[512,256]{1,0:T(8,128)S(1)}, f32[512,256]{1,0:T(8,128)}, u32[]{:S(2)}) copy-start(f32[512,256]{1,0:T(8,128)} %copy-done.17) | copy-start | bytes 1572868
  135.0 10.0 %copy-start.20 = (f32[512,256]{1,0:T(8,128)S(1)}, f32[512,256]{1,0:T(8,128)}, u32[]{:S(2)}) copy-start(f32[512,256]{1,0:T(8,128)} %copy-done.19) | copy-start | bytes 1572868
  139.3 1.3 collective-permute-start.6
  140.6 4.4 %collective-permute-start.7 = (f32[8,2048]{1,0:T(8,128)S(1)}, f32[8,2048]{1,0:T(8,128)S(1)}, u32[]{:S(2)}, u32[]{:S(2)}) collective-permute-start(f32[8,2048]{1,0:T(8,128)S(1)} %add.60), channel_id=1, source_target_pairs={{0,2},{2,0},{4,6},{6,4},{1,3},{3,1},{5,7},{7,5},{8,10},{10,8},{12,... | collective-permute-start | bytes 196616 | tf_op jit(solution)/shard_map/ppermute | solution.py:44
  147.5 56.7 %all-to-all-start.3 = ((bf16[8,64,1024]{2,1,0:T(8,128)(2,1)}), bf16[8,64,1024]{2,1,0:T(8,128)(2,1)S(1)}, u32[]{:S(2)}, u32[]{:S(2)}) async-start(bf16[8,64,1024]{2,1,0:T(8,128)(2,1)} %shard_map.117), calls=%async_computation.3 | async-start | bytes 2097152 | tf_op jit(solution)/shard_map/all_to_all | solution.py:48
  155.1 4.5 %collective-permute-start.10 = (f32[8,2048]{1,0:T(8,128)S(1)}, f32[8,2048]{1,0:T(8,128)S(1)}, u32[]{:S(2)}, u32[]{:S(2)}) collective-permute-start(f32[8,2048]{1,0:T(8,128)S(1)} %add.61), channel_id=1, source_target_pairs={{0,6},{2,4},{4,2},{6,0},{1,7},{3,5},{5,3},{7,1},{8,14},{10,12},{12... | collective-permute-start | bytes 196616 | tf_op jit(solution)/shard_map/ppermute | solution.py:44
  159.6 22.1 %collective-permute-start.11 = (f32[8,2048]{1,0:T(8,128)S(1)}, f32[8,2048]{1,0:T(8,128)S(1)}, u32[]{:S(2)}, u32[]{:S(2)}) collective-permute-start(f32[8,2048]{1,0:T(8,128)S(1)} %add.62), channel_id=1, source_target_pairs={{0,1},{1,0},{2,3},{3,2},{4,5},{5,4},{6,7},{7,6},{8,9},{9,8},{10,11... | collective-permute-start | bytes 196616 | tf_op jit(solution)/shard_map/ppermute | solution.py:44
  181.7 4.4 %collective-permute-start.12 = (f32[8,2048]{1,0:T(8,128)S(1)}, f32[8,2048]{1,0:T(8,128)S(1)}, u32[]{:S(2)}, u32[]{:S(2)}) collective-permute-start(f32[8,2048]{1,0:T(8,128)S(1)} %add.63), channel_id=1, source_target_pairs={{0,64},{64,0},{128,192},{192,128},{1,65},{65,1},{129,193},{193,129... | collective-permute-start | bytes 196616 | tf_op jit(solution)/shard_map/ppermute | solution.py:44
  186.0 5.6 %collective-permute-start.13 = (f32[8,2048]{1,0:T(8,128)S(1)}, f32[8,2048]{1,0:T(8,128)S(1)}, u32[]{:S(2)}, u32[]{:S(2)}) collective-permute-start(f32[8,2048]{1,0:T(8,128)S(1)} %add.64), channel_id=1, source_target_pairs={{0,192},{64,128},{128,64},{192,0},{1,193},{65,129},{129,65},{193,1... | collective-permute-start | bytes 196616 | tf_op jit(solution)/shard_map/ppermute | solution.py:44
  191.6 5.3 %collective-permute-start.14 = (f32[8,2048]{1,0:T(8,128)S(1)}, f32[8,2048]{1,0:T(8,128)S(1)}, u32[]{:S(2)}, u32[]{:S(2)}) collective-permute-start(f32[8,2048]{1,0:T(8,128)S(1)} %add.65), channel_id=1, source_target_pairs={{0,16},{16,0},{32,48},{48,32},{1,17},{17,1},{33,49},{49,33},{2,18}... | collective-permute-start | bytes 196616 | tf_op jit(solution)/shard_map/ppermute | solution.py:44
  197.0 6.6 %collective-permute-start.15 = (f32[8,2048]{1,0:T(8,128)S(1)}, f32[8,2048]{1,0:T(8,128)S(1)}, u32[]{:S(2)}, u32[]{:S(2)}) collective-permute-start(f32[8,2048]{1,0:T(8,128)S(1)} %add.66), channel_id=1, source_target_pairs={{0,48},{16,32},{32,16},{48,0},{1,49},{17,33},{33,17},{49,1},{2,50}... | collective-permute-start | bytes 196616 | tf_op jit(solution)/shard_map/ppermute | solution.py:44

commit v7 on v6

--- a/solution.py
+++ b/solution.py
@@ -9,18 +9,9 @@
 FINE_SHAPE = (4, 4, 2, 4, 2)
 GROUP = ("x", "zl")
 EXTRA = 128
-ROUTER_STEPS = (
-    ("core", 1),
-    ("x", 1),
-    ("x", 3),
-    ("zl", 1),
-    ("y", 1),
-    ("y", 3),
-    ("zh", 1),
-    ("zh", 3),
-)
-VMEM_LIMIT = 14 * 1024 * 1024
-LONG = 60_000_000_000
+VMEM_LIMIT = 16 * 1024 * 1024
+COST_SLOTS = 1000
+LONG = 26_000_000_000
 F32 = jnp.float32
 BF16 = jnp.bfloat16
 
@@ -52,16 +43,19 @@
     return lax.optimization_barrier(values)
 
 
-def call(body, pos, inputs, outputs, flops=1000):
+def call(body, pos, inputs, outputs, flops=1000, far=(), scratch=()):
     vmem = pl.BlockSpec(memory_space=pltpu.VMEM)
     return pl.pallas_call(
         body,
-        in_specs=[pl.BlockSpec(memory_space=pltpu.SMEM)] + [vmem] * len(inputs),
+        in_specs=[pl.BlockSpec(memory_space=pltpu.SMEM)]
+        + [vmem] * len(inputs)
+        + [pl.BlockSpec(memory_space=pl.ANY)] * len(far),
         out_specs=[vmem] * len(outputs),
         out_shape=[jax.ShapeDtypeStruct(shape, dtype) for shape, dtype in outputs],
+        scratch_shapes=scratch,
         cost_estimate=pl.CostEstimate(flops=flops, bytes_accessed=1000, transcendentals=0),
         compiler_params=pltpu.CompilerParams(vmem_limit_bytes=VMEM_LIMIT),
-    )(pos, *inputs)
+    )(pos, *inputs, *far)
 
 
 def gate_of(pos, lanes):
@@ -91,26 +85,49 @@
     hidden, width = weight_out.shape
     step = hidden // 4
 
-    def body(pos_ref, rec, weight, act_ref, slope_ref, grad_pre, give, gate_grad):
+    def body(pos_ref, rec, weight, act_ref, slope_ref, grad_pre, give, gate_grad, w, a, g, sems):
+        copies = []
+        for i in range(4):
+            at = slice(i * step, (i + 1) * step)
+            moves = (
+                (weight.at[at, :], w.at[at, :]),
+                (act_ref.at[:, at], a.at[i]),
+                (slope_ref.at[:, at], g.at[i]),
+            )
+            copies.append(
+                [pltpu.make_async_copy(x, y, sems.at[i, k]) for k, (x, y) in enumerate(moves)]
+            )
+            for copy in copies[i]:
+                copy.start()
         gate = gate_of(pos_ref, rec[:, width:])
         total = None
         for i in range(4):
             at = slice(i * step, (i + 1) * step)
+            for copy in copies[i]:
+                copy.wait()
             grad_act = lax.dot_general(
-                rec[:, :width], weight[at, :], (((1,), (1,)), ((), ())), preferred_element_type=F32
-            )
-            part = jnp.sum(act_ref[:, at].astype(F32) * grad_act, axis=1, keepdims=True)
+                rec[:, :width], w[at, :], (((1,), (1,)), ((), ())), preferred_element_type=F32
+            )
+            part = jnp.sum(a[i].astype(F32) * grad_act, axis=1, keepdims=True)
             total = part if total is None else total + part
-            grad_pre[:, at] = (gate * grad_act * slope_ref[:, at]).astype(BF16)
-        gate_grad[...] = total
+            grad_pre[:, at] = (gate * grad_act * g[i]).astype(BF16)
         start = pl.multiple_of((1 - pos_ref[1]) * (hidden // 2), hidden // 2)
         give[...] = grad_pre[:, pl.ds(start, hidden // 2)]
+        lane = lax.broadcasted_iota(jnp.int32, (slots, EXTRA), 1)
+        gate_grad[...] = jnp.where(lane == pos_ref[2], total, 0.0).astype(BF16)
 
     return call(
         body,
         pos,
-        [received, weight_out, act, slope],
-        [((slots, hidden), BF16), ((slots, hidden // 2), BF16), ((slots, 1), F32)],
+        [received],
+        [((slots, hidden), BF16), ((slots, hidden // 2), BF16), ((slots, EXTRA), BF16)],
+        far=[weight_out, act, slope],
+        scratch=[
+            pltpu.VMEM((hidden, width), BF16),
+            pltpu.VMEM((4, slots, step), BF16),
+            pltpu.VMEM((4, slots, step), F32),
+            pltpu.SemaphoreType.DMA((4, 3)),
+        ],
     )
 
 
@@ -137,76 +154,117 @@
 
 
 def sent_parts(pos, left_out, right_out, left_in, right_in):
+    slots = left_in[0].shape[0]
     width_out, width_in = left_out[0].shape[1] // 4, left_in[0].shape[1] // 4
     cols_out, cols_in = right_out[1].shape[1] // 2, right_in[1].shape[1] // 2
     masks = ((1, 2), (3, 2))
 
     def body(pos_ref, *refs):
-        outs = refs[8:]
+        out_refs, right_refs = refs[:4], refs[4:6]
+        lefts, outs, (buffer, sems) = refs[6:8], refs[8:10], refs[10:]
+        copies = []
+        for k in range(2):
+            for r in (1, 2, 3):
+                start = pl.multiple_of((pos_ref[0] ^ r) * width_in, width_in)
+                copy = pltpu.make_async_copy(
+                    lefts[k].at[:, pl.ds(start, width_in)], buffer.at[k, r - 1], sems.at[k, r - 1]
+                )
+                copy.start()
+                copies.append(copy)
+        for i, j, value in row_products(pos_ref, out_refs, 0, masks, width_out, cols_out):
+            outs[i][j * width_out : (j + 1) * width_out, :] = value.astype(BF16)
+        for copy in copies:
+            copy.wait()
+        dims = (((0,), (0,)), ((), ()))
+        for i in range(2):
+            own = pl.multiple_of((2 * pos_ref[1] + i) * cols_in, cols_in)
+            for j in range(2):
+                r = masks[i][j] - 1
+                value = lax.dot_general(
+                    buffer[0, r],
+                    right_refs[0][:, pl.ds(own, cols_in)],
+                    dims,
+                    preferred_element_type=F32,
+                )
+                value = value + lax.dot_general(
+                    buffer[1, r],
+                    right_refs[1][:, i * cols_in : (i + 1) * cols_in],
+                    dims,
+                    preferred_element_type=F32,
+                )
+                outs[i][2 * width_out :, j * cols_in : (j + 1) * cols_in] = value.astype(BF16)
+
+    return call(
+        body,
+        pos,
+        [*left_out, *right_out, *right_in],
+        [((2 * width_out + width_in, cols_out), BF16)] * 2,
+        far=[*left_in],
+        scratch=[pltpu.VMEM((2, 3, slots, width_in), BF16), pltpu.SemaphoreType.DMA((2, 3))],
+    )
+
+
+def kept_parts(pos, left_out, right_out, left_in, right_in):
+    width_out, width_in = left_out[0].shape[1] // 4, left_in[0].shape[1] // 4
+    cols_out, cols_in = right_out[1].shape[1] // 2, right_in[1].shape[1] // 2
+    masks = ((0, 3), (0, 1))
+    half = width_in // 2
+
+    def body(pos_ref, *refs):
+        near_out, near_in, far = refs[8:10], refs[10:12], refs[12:14]
         for i, j, value in row_products(pos_ref, refs[:4], 0, masks, width_out, cols_out):
-            outs[i][j * width_out : (j + 1) * width_out, :] = value.astype(BF16)
+            if j == 0:
+                near_out[i][...] = value
+            else:
+                far[i][:width_out, :] = value
         for i, j, value in row_products(pos_ref, refs[4:8], 2, masks, width_in, cols_in):
-            outs[i][2 * width_out :, j * cols_in : (j + 1) * cols_in] = value.astype(BF16)
+            if j == 0:
+                near_in[i][...] = value
+            else:
+                far[i][width_out:, :cols_in] = value[:half, :]
+                far[i][width_out:, cols_in:] = value[half:, :]
 
     return call(
         body,
         pos,
         [*left_out, *right_out, *left_in, *right_in],
-        [((2 * width_out + width_in, cols_out), BF16)] * 2,
-    )
-
-
-def kept_parts(pos, left_out, right_out, left_in, right_in, got):
-    width_out, width_in = left_out[0].shape[1] // 4, left_in[0].shape[1] // 4
-    cols_out, cols_in = right_out[1].shape[1] // 2, right_in[1].shape[1] // 2
-    masks = ((0, 3), (0, 1))
-    half = width_in // 2
-
-    def body(pos_ref, *refs):
-        arrived = refs[8:10]
-        near_out, near_in, far = refs[10:12], refs[12:14], refs[14:16]
-        for i, j, value in row_products(pos_ref, refs[:4], 0, masks, width_out, cols_out):
-            at = slice(j * width_out, (j + 1) * width_out)
-            value = value + arrived[i][at, :].astype(F32)
-            if j == 0:
-                near_out[i][...] = value
-            else:
-                far[i][:width_out, :] = value.astype(BF16)
-        for i, j, value in row_products(pos_ref, refs[4:8], 2, masks, width_in, cols_in):
-            at = slice(j * cols_in, (j + 1) * cols_in)
-            value = value + arrived[i][2 * width_out :, at].astype(F32)
-            if j == 0:
-                near_in[i][...] = value
-            else:
-                value = value.astype(BF16)
-                far[i][width_out:, :cols_in] = value[:half, :]
-                far[i][width_out:, cols_in:] = value[half:, :]
-
-    return call(
-        body,
-        pos,
-        [*left_out, *right_out, *left_in, *right_in, *got],
         [((width_out, cols_out), F32)] * 2
         + [((width_in, cols_in), F32)] * 2
-        + [((width_out + half, cols_out), BF16)] * 2,
-        LONG,
-    )
-
-
-def zh_pieces(pos, near_out, near_in, far, scale):
+        + [((width_out + half, cols_out), F32)] * 2,
+    )
+
+
+def far_sums(pos, far, got):
+    rows, cols = far[0].shape
+    half, wide = rows // 2, cols // 2
+
+    def body(pos_ref, far_a, far_b, got_a, got_b, out_a, out_b):
+        for mine, arrived, out in ((far_a, got_a, out_a), (far_b, got_b, out_b)):
+            out[:half, :] = (mine[:half, :] + arrived[half:rows, :].astype(F32)).astype(BF16)
+            for k in range(2):
+                at = slice(k * wide, (k + 1) * wide)
+                value = arrived[rows + k * half : rows + (k + 1) * half, wide:].astype(F32)
+                out[half:, at] = (mine[half:, at] + value).astype(BF16)
+
+    return call(body, pos, [*far, *got], [((rows, cols), BF16)] * 2, LONG)
+
+
+def zh_pieces(pos, near_out, near_in, got, far, scale):
     rows_out, cols_out = near_out[0].shape
     rows_in, cols_in = near_in[0].shape
     half = rows_in // 2
     share_out, share_in = rows_out // 8, rows_in // 8
 
-    def body(pos_ref, out_a, out_b, in_a, in_b, far_a, far_b, pieces):
-        for i, (out, inner, arrived) in enumerate(((out_a, in_a, far_a), (out_b, in_b, far_b))):
-            value = (out[...] + arrived[:rows_out, :].astype(F32)) * scale
-            value = value.astype(BF16).reshape(8, share_out, cols_out)
+    def body(pos_ref, out_a, out_b, in_a, in_b, got_a, got_b, far_a, far_b, pieces):
+        sets = ((out_a, in_a, got_a, far_a), (out_b, in_b, got_b, far_b))
+        for i, (out, inner, first, second) in enumerate(sets):
+            value = out[...] + first[:rows_out, :].astype(F32) + second[:rows_out, :].astype(F32)
+            value = (value * scale).astype(BF16).reshape(8, share_out, cols_out)
             pieces[:, :share_out, i * cols_out : (i + 1) * cols_out] = value
             for k in range(2):
-                value = inner[k * half : (k + 1) * half, :]
-                value = value + arrived[rows_out:, k * cols_in : (k + 1) * cols_in].astype(F32)
+                at = slice(2 * rows_out + k * half, 2 * rows_out + (k + 1) * half)
+                value = inner[k * half : (k + 1) * half, :] + first[at, :cols_in].astype(F32)
+                value = value + second[rows_out:, k * cols_in : (k + 1) * cols_in].astype(F32)
                 value = (value * scale).astype(BF16).reshape(4, 2, share_in // 2, cols_in)
                 for m in range(2):
                     start = m * 2 * cols_in + i * cols_in
@@ -215,7 +273,7 @@
     return call(
         body,
         pos,
-        [*near_out, *near_in, *far],
+        [*near_out, *near_in, *got, *far],
         [((8, share_out + share_in // 2, 2 * cols_out), BF16)],
     )[0]
 
@@ -239,56 +297,66 @@
     return outer[None], inner[None]
 
 
-def slot_grads_of(pos, grad_pre, weight_in, gate_grad):
+def slot_grads_of(pos, grad_pre, weight_in):
     slots, hidden = grad_pre.shape
     width = weight_in.shape[0]
     step = width // 4
 
-    def body(pos_ref, grad, weight, gate, out):
+    def body(pos_ref, grad, weight, out):
         for i in range(4):
             at = slice(i * step, (i + 1) * step)
             out[:, at] = lax.dot_general(
                 grad[...], weight[at, :], (((1,), (1,)), ((), ())), preferred_element_type=F32
             ).astype(BF16)
-        lane = lax.broadcasted_iota(jnp.int32, (slots, EXTRA), 1)
-        out[:, width:] = jnp.where(lane == pos_ref[2], gate[...], 0.0).astype(BF16)
-
-    return call(
-        body, pos, [grad_pre, weight_in, gate_grad], [((slots, width + EXTRA), BF16)]
-    )[0]
-
-
-def token_grads(pos, dispatch, back, tokens, weight_lanes, probs, combine, keep, denominator, scale):
+
+    return call(body, pos, [grad_pre, weight_in], [((slots, width), BF16)], COST_SLOTS)[0]
+
+
+def router_grads(pos, dispatch, gate_back, tokens, probs, combine, keep, denominator, scale):
     rows, width = tokens.shape
     experts = 8
     step = width // 4
 
-    def body(pos_ref, disp, flat, tok, weight, p_ref, c_ref, k_ref, d_ref, out, router):
+    def body(pos_ref, disp, back, tok, p_ref, c_ref, k_ref, d_ref, logit, router):
         dims = (((0,), (0,)), ((), ()))
-        combine_grad = lax.dot_general(
-            disp[...], flat[:, width:], dims, preferred_element_type=F32
-        )
+        combine_grad = lax.dot_general(disp[...], back[...], dims, preferred_element_type=F32)
         weighted = jnp.sum(combine_grad * c_ref[...], axis=1, keepdims=True)
         probs_grad = k_ref[...] * (combine_grad - weighted) / d_ref[...]
         probs = p_ref[...]
         inner = jnp.sum(probs_grad * probs, axis=1, keepdims=True)
         logit_b = (probs * (probs_grad - inner)).astype(BF16)
+        logit[...] = logit_b
         for i in range(4):
             at = slice(i * step, (i + 1) * step)
             part = lax.dot_general(logit_b, tok[:, at], dims, preferred_element_type=F32)
             router[:, at] = part[:experts] * scale
-            value = lax.dot_general(disp[...], flat[:, at], dims, preferred_element_type=F32)
-            value = value + lax.dot_general(
-                logit_b, weight[at, :], (((1,), (1,)), ((), ())), preferred_element_type=F32
-            )
-            out[:, at] = value.astype(BF16)
 
     return call(
         body,
         pos,
-        [dispatch, back, tokens, weight_lanes, probs, combine, keep, denominator],
-        [((rows, width), BF16), ((experts, width), F32)],
-    )
+        [dispatch, gate_back, tokens, probs, combine, keep, denominator],
+        [((rows, EXTRA), BF16), ((experts, width), F32)],
+    )
+
+
+def token_grads(pos, dispatch, back, logit_lanes, weight_lanes):
+    rows, width = dispatch.shape[1], back.shape[1]
+    step = width // 4
+
+    def body(pos_ref, disp, flat, logit, weight, out):
+        for i in range(4):
+            at = slice(i * step, (i + 1) * step)
+            value = lax.dot_general(
+                disp[...], flat[:, at], (((0,), (0,)), ((), ())), preferred_element_type=F32
+            )
+            value = value + lax.dot_general(
+                logit[...], weight[at, :], (((1,), (1,)), ((), ())), preferred_element_type=F32
+            )
+            out[:, at] = value.astype(BF16)
+
+    return call(
+        body, pos, [dispatch, back, logit_lanes, weight_lanes], [((rows, width), BF16)]
+    )[0]
 
 
 def per_device(
@@ -351,12 +419,11 @@
     pos = jnp.stack([my_y, core, lax.axis_index(GROUP), lax.axis_index("zh")]).astype(jnp.int32)
 
 
-    (received, left_in, left_out, act_slope, dispatch, weight_lanes) = tie(
-        received, left_in, left_out, act_slope, dispatch, weight_lanes
-    )
-    probs_lanes, combine_lanes, keep_lanes, denominator_lanes, _ = tie(
-        probs_lanes, combine_lanes, keep_lanes, denominator_lanes, act_slope
-    )
+    token_side = (dispatch, weight_lanes, probs_lanes, combine_lanes, keep_lanes, denominator_lanes)
+    received, left_in, left_out, act_slope, token_side = tie(
+        received, left_in, left_out, act_slope, token_side
+    )
+    dispatch, weight_lanes, probs_lanes, combine_lanes, keep_lanes, denominator_lanes = token_side
     my_out, give_out = scale_grads(pos, received)
     right_out = (my_out, swap(give_out, "core", 1))
     received, _ = tie(received, give_out)
@@ -367,25 +434,22 @@
 
     sent = sent_parts(pos, left_out, right_out, left_in, right_in)
     got = (swap(sent[0], "y", 1), swap(sent[1], "y", 3))
-    pre_for_slots, _ = tie(grad_pre, sent)
-    grad_slots = slot_grads_of(pos, pre_for_slots, weight_in, gate_grad)
+    gate_grad, grad_pre, _ = tie(gate_grad, grad_pre, sent)
+    gate_back = exchange(gate_grad.reshape(experts, capacity, EXTRA), GROUP).reshape(
+        slot_count, EXTRA
+    )
+    grad_slots = slot_grads_of(pos, grad_pre, weight_in)
+    grad_slots, gate_back = tie(grad_slots, gate_back)
     back = exchange(
-        grad_slots.reshape(experts, capacity, model_width + EXTRA), GROUP
-    ).reshape(slot_count, model_width + EXTRA)
-
-    left_in, left_out, right_in, right_out, _ = tie(
-        left_in, left_out, right_in, right_out, grad_slots
-    )
-    *near, far_a, far_b = kept_parts(pos, left_out, right_out, left_in, right_in, got)
-    far = (swap(far_a, "y", 3), swap(far_b, "y", 1))
-
-    back, _ = tie(back, far_a)
-    grad_tokens, router_part = token_grads(
+        grad_slots.reshape(experts, capacity, model_width), GROUP
+    ).reshape(slot_count, model_width)
+
+    gate_back, _ = tie(gate_back, grad_slots)
+    logit_lanes, router_part = router_grads(
         pos,
         dispatch,
-        back,
+        gate_back,
         tokens,
-        weight_lanes,
         probs_lanes,
         combine_lanes,
         keep_lanes,
@@ -393,17 +457,31 @@
         grad_scale,
     )
 
-    def router_steps(value, first, last):
-        for axis, mask in ROUTER_STEPS[first:last]:
-            value = value + swap(value, axis, mask)
-        return value
-
-    router_part = router_steps(router_part, 0, 2)
-    near, _ = tie(near, router_part)
-    pieces = zh_pieces(pos, near[:2], near[2:], far, grad_scale)
-    router_part, _ = tie(router_part, pieces)
+    def router_round(value, axes, one, two):
+        near, far, both = (swap(value, axes, mask) for mask in (one, two, one ^ two))
+        return (value + near) + (far + both)
+
+    left_in, left_out, right_in, right_out, _ = tie(
+        left_in, left_out, right_in, right_out, router_part
+    )
+    *near, far_a, far_b = kept_parts(pos, left_out, right_out, left_in, right_in)
+    router_part, _ = tie(router_part, far_a)
+    router_part = router_round(router_part, ("core", "zl"), 1, 2)
+    got, far_a, far_b, router_part = tie(got, far_a, far_b, router_part)
+    far_a, far_b = far_sums(pos, (far_a, far_b), got)
+    far = (swap(far_a, "y", 3), swap(far_b, "y", 1))
+
+    router_part, _ = tie(router_part, far_a)
+    router_part = router_round(router_part, "zh", 1, 3)
+    near, far, router_part = tie(near, far, router_part)
+    pieces = zh_pieces(pos, near[:2], near[2:], got, far, grad_scale)
     got = exchange(pieces, ("zh", "core"))
-    router_part = router_steps(router_part, 2, 8)
+
+    back, router_part, _ = tie(back, router_part, pieces)
+    grad_tokens = token_grads(pos, dispatch, back, logit_lanes, weight_lanes)
+    router_part, _ = tie(router_part, grad_tokens)
+    router_part = router_round(router_part, "x", 1, 3)
+    router_part = router_round(router_part, "y", 1, 3)
     got, router_part = tie(got, router_part)
     outer_share, inner_share = shares(pos, got, near[0].shape[0] // 8)
     return (grad_tokens, router_part.T, inner_share, outer_share)

time: 207 us -> 200 us (0.966)
  waiting for transfers between devices: 94.3 us -> 63.6 us
  starting transfers between devices: 42.9 us -> 55.1 us
  local copies, waits for them, and re-layouts: 19.3 us -> 25.5 us
  Pallas kernels: 30.9 us -> 33.6 us
  matrix products: 12.2 us -> 14.7 us
    ppermute x16 -> x20, waiting for transfers between devices: 59.4 us -> 24.4 us  [swap(): return lax.ppermute(values, axis, [(i, i ^ mask) for i in range(size)])]
    ppermute x16 -> x20, starting transfers between devices: 17.3 us -> 24.8 us  [swap(): return lax.ppermute(values, axis, [(i, i ^ mask) for i in range(size)])]
    unnamed x79 -> x69, local copies, waits for them, and re-layouts: 14.8 us -> 19.6 us
    all_to_all x4 -> x5, starting transfers between devices: 25.6 us -> 30.3 us  [exchange(): return lax.all_to_all(values, axes, split_axis=0, concat_axis=0, tiled=True)]
    all_to_all x4 -> x5, waiting for transfers between devices: 34.9 us -> 39.2 us  [exchange(): return lax.all_to_all(values, axes, split_axis=0, concat_axis=0, tiled=True)]
    pallas_call x8 -> x10, Pallas kernels: 30.9 us -> 33.6 us  [call(): pl.pallas_call(body, in_specs=[pl.BlockSpec(memory_space=pltpu.SMEM)] + [...]
  transfers between devices with their start and end apart: 20 -> 25, of which waited for: 13 -> 15; matrix products, arithmetic and copies ran while one was open for 9% -> 11% of each run, Pallas kernels for 9% -> 12%
where the time goes in v7:
time: 200 us; the launch traced here: 198 us
  waiting for transfers between devices  63.6 us (32%)
  starting transfers between devices  55.1 us (28%)
  Pallas kernels  33.6 us (17%)
  local copies, waits for them, and re-layouts  25.5 us (13%)
  matrix products  14.7 us (7%)
  other arithmetic  4.84 us (2%)
    all_to_all x5, waiting for transfers between devices, exchange(): return lax.all_to_all(values, axes, split_axis=0, concat_axis=0, tiled=True)  39.2 us
    pallas_call x10, Pallas kernels, call(): pl.pallas_call(body, in_specs=[pl.BlockSpec(memory_space=pltpu.SMEM)] + [...  33.6 us
    all_to_all x5, starting transfers between devices, exchange(): return lax.all_to_all(values, axes, split_axis=0, concat_axis=0, tiled=True)  30.3 us
    ppermute x20, starting transfers between devices, swap(): return lax.ppermute(values, axis, [(i, i ^ mask) for i in range(size)])  24.8 us
    ppermute x20, waiting for transfers between devices, swap(): return lax.ppermute(values, axis, [(i, i ^ mask) for i in range(size)])  24.4 us
    unnamed x69, local copies, waits for them, and re-layouts  19.6 us
    dot_general x1, matrix products, per_device(): hidden_pre = jnp.dot(slot_tokens, weight_in, preferred_element_type=F32)  7.47 us
  transfers between devices with their start and end apart: 25, of which 15 were waited for; matrix products, arithmetic and copies ran while one was open for 11% of the time, Pallas kernels for 12%

profile of v7, /device:TPU:2, one launch (start us, length us, event | category | flops | bytes accessed | tf_op | source)
XLA Modules:
  0.0 198.5 jit_solution(11796189809778034786)
XLA Ops:
  0.6 0.8 compare_reduce_fusion.1
  1.5 0.7 multiply_add_fusion
  2.2 3.3 %convolution_convert_fusion = bf16[512,2048]{1,0:T(8,128)(2,1)} fusion(bf16[256,2048]{1,0:T(8,128)(2,1)} %tok.1, s32[256]{0:T(256)S(1)} %bitcast.46, s32[256]{0:T(256)S(1)} %bitcast.42, pred[256]{0:T(512)(128)(4,1)S(1)} %get-tuple-element.135, pred[256]{0:T(512)(128)(4,1)S(1)} %get-tuple-element.134), kind=kOutput, calls=%fused_computation.1 | convolution fusion | flops 538574848 | bytes 3148288 | tf_op jit(solution)/shard_map/dot_general | solution.py:381
  5.6 6.3 %all-to-all-start.1 = ((bf16[8,64,2048]{2,1,0:T(8,128)(2,1)}), bf16[8,64,2048]{2,1,0:T(8,128)(2,1)S(1)}, u32[]{:S(2)}, u32[]{:S(2)}) async-start(bf16[8,64,2048]{2,1,0:T(8,128)(2,1)} %bitcast.40), calls=%async_computation.1 | async-start | bytes 4194304 | tf_op jit(solution)/shard_map/all_to_all | solution.py:39
  11.9 1.6 fusion.17
  14.6 0.9 convolution_convert_fusion.2
  15.5 1.4 convolution_convert_fusion.1
  16.9 1.6 pad_maximum_fusion
  18.5 18.6 %all-to-all-done.1 = bf16[8,64,2048]{2,1,0:T(8,128)(2,1)S(1)} async-done(((bf16[8,64,2048]{2,1,0:T(8,128)(2,1)}), bf16[8,64,2048]{2,1,0:T(8,128)(2,1)S(1)}, u32[]{:S(2)}, u32[]{:S(2)}) %all-to-all-start.1) | async-done | bytes 2097184 | tf_op jit(solution)/shard_map/all_to_all | solution.py:39
  37.1 1.4 copy-done.1
  38.4 5.3 %all-to-all-start = ((bf16[8,64,2176]{2,1,0:T(8,128)(2,1)}), bf16[8,64,2176]{2,1,0:T(8,128)(2,1)S(1)}, u32[]{:S(2)}, u32[]{:S(2)}) async-start(bf16[8,64,2176]{2,1,0:T(8,128)(2,1)} %bitcast.39), calls=%async_computation | async-start | bytes 4456448 | tf_op jit(solution)/shard_map/all_to_all | solution.py:39
  43.7 7.5 %fusion.3 = (f32[512,1024]{1,0:T(8,128)}, bf16[512,1024]{1,0:T(8,128)(2,1)}) fusion(bf16[512,2048]{1,0:T(8,128)(2,1)} %bitcast.31, bf16[1,2048,1024]{2,1,0:T(8,128)(2,1)} %param.11), kind=kOutput, calls=%fused_computation.7 | convolution fusion | flops 2152726528 | bytes 9437184 | tf_op jit(solution)/shard_map/dot_general | solution.py:412
  53.0 1.8 copy.28
  55.6 2.0 pad.15.weight
  57.7 0.8 fusion.12.disp
  58.4 11.3 %all-to-all-done = bf16[8,64,2176]{2,1,0:T(8,128)(2,1)S(1)} async-done(((bf16[8,64,2176]{2,1,0:T(8,128)(2,1)}), bf16[8,64,2176]{2,1,0:T(8,128)(2,1)S(1)}, u32[]{:S(2)}, u32[]{:S(2)}) %all-to-all-start) | async-done | bytes 2228256 | tf_op jit(solution)/shard_map/all_to_all | solution.py:39
  69.7 1.6 broadcast_in_dim.52.d_ref
  71.3 1.0 shard_map.111
  72.4 2.4 %copy-done.13 = bf16[1,1024,2048]{2,1,0:T(8,128)(2,1)S(1)} copy-done((bf16[1,1024,2048]{2,1,0:T(8,128)(2,1)S(1)}, bf16[1,1024,2048]{2,1,0:T(8,128)(2,1)}, u32[]{:S(2)}) %copy-start.13) | copy-done | bytes 4194328
  74.8 7.1 %shard_map.112 = (bf16[512,1024]{1,0:T(8,128)(2,1)S(1)}, bf16[512,512]{1,0:T(8,128)(2,1)S(1)}, bf16[512,128]{1,0:T(8,128)(2,1)S(1)}) custom-call(s32[4]{0:T(128)S(1)} %pad_add_fusion.pos_ref, bf16[512,2176]{1,0:T(8,128)(2,1)S(1)} %bitcast.29, bf16[1024,2048]{1,0:T(8,128)(2,1)S(1)} %bitcast.35, bf16[512,1024]{1,0:T(8,128)(2,1)} %get-tuple-element.93.act_ref.refs_0_, ...), custom_call_target="tpu_custom_call" | custom-call | flops 1000 | bytes 1000 | tf_op jit(solution)/shard_map/pallas_call | solution.py:48
  82.4 1.7 collective-permute-done.3.refs_5_.refs_7_
  84.1 7.2 %shard_map.113 = (bf16[1024,512]{1,0:T(8,128)(2,1)}, bf16[1024,512]{1,0:T(8,128)(2,1)}) custom-call(s32[4]{0:T(128)S(1)} %pad_add_fusion.pos_ref, bf16[512,1024]{1,0:T(8,128)(2,1)} %get-tuple-element.93.act_ref.refs_0_, bf16[512,1024]{1,0:T(8,128)(2,1)} %collective-permute-done.1.refs_1_, bf16[512,1024]{1,0:T(8,128)(2,1)S(1)} %get-tuple-element.95.refs_2_, ...), custom_call_target="tpu_custom_call" | custom-call | flops 1000 | bytes 1000 | tf_op jit(solution)/shard_map/pallas_call | solution.py:48
  91.4 1.6 collective-permute-start.4
  93.0 2.2 %collective-permute-start.5 = (bf16[1024,512]{1,0:T(8,128)(2,1)}, bf16[1024,512]{1,0:T(8,128)(2,1)}, u32[]{:S(2)}, u32[]{:S(2)}) collective-permute-start(bf16[1024,512]{1,0:T(8,128)(2,1)} %get-tuple-element.82), channel_id=1, source_target_pairs={{0,192},{64,128},{128,64},{192,0},{1,193},{65,129},{129,65},{193,1... | collective-permute-start | bytes 3145736 | tf_op jit(solution)/shard_map/ppermute | solution.py:35
  95.2 5.1 %all-to-all-start.2 = ((bf16[8,64,128]{2,1,0:T(8,128)(2,1)}), bf16[8,64,128]{2,1,0:T(8,128)(2,1)S(1)}, u32[]{:S(2)}, u32[]{:S(2)}) async-start(bf16[8,64,128]{2,1,0:T(8,128)(2,1)} %bitcast.38), calls=%async_computation.2 | async-start | bytes 262144 | tf_op jit(solution)/shard_map/all_to_all | solution.py:39
  100.2 1.2 copy-done.6
  101.5 2.2 %copy-done.14 = bf16[1,2048,1024]{2,1,0:T(8,128)(2,1)S(1)} copy-done((bf16[1,2048,1024]{2,1,0:T(8,128)(2,1)S(1)}, bf16[1,2048,1024]{2,1,0:T(8,128)(2,1)}, u32[]{:S(2)}) %copy-start.14) | copy-done | bytes 4194328
  103.6 2.9 %shard_map.114 = bf16[512,2048]{1,0:T(8,128)(2,1)S(1)} custom-call(s32[4]{0:T(128)S(1)} %pad_add_fusion.pos_ref, bf16[512,1024]{1,0:T(8,128)(2,1)S(1)} %copy-done.6, bf16[2048,1024]{1,0:T(8,128)(2,1)S(1)} %bitcast.36), custom_call_target="tpu_custom_call" | custom-call | flops 1000 | bytes 1000 | tf_op jit(solution)/shard_map/pallas_call | solution.py:48
  106.6 1.4 copy-done.8
  108.6 5.9 %all-to-all-start.3 = ((bf16[8,64,2048]{2,1,0:T(8,128)(2,1)}), bf16[8,64,2048]{2,1,0:T(8,128)(2,1)}, u32[]{:S(2)}, u32[]{:S(2)}) async-start(bf16[8,64,2048]{2,1,0:T(8,128)(2,1)} %bitcast.34), calls=%async_computation.3 | async-start | bytes 4194304 | tf_op jit(solution)/shard_map/all_to_all | solution.py:39
  114.5 1.2 copy-done.4
  115.7 0.9 copy-done.20
  116.6 0.9 copy-done.21
  117.5 0.9 copy-done.22
  118.4 0.9 copy-done.24
  119.3 1.3 shard_map.115
  121.2 1.2 copy-done.10
  122.5 1.2 copy-done.12
  123.7 4.6 %shard_map.116 = (f32[256,512]{1,0:T(8,128)S(1)}, f32[256,512]{1,0:T(8,128)S(1)}, f32[512,256]{1,0:T(8,128)S(1)}, f32[512,256]{1,0:T(8,128)S(1)}, f32[512,512]{1,0:T(8,128)S(1)}, /*index=5*/f32[512,512]{1,0:T(8,128)S(1)}) custom-call(s32[4]{0:T(128)S(1)} %pad_add_fusion.pos_ref, bf16[512,1024]{1,0:T(8,128)(2,1)} %get-tuple-element.93.act_ref.refs_0_, ...), custom_call_target="tpu_custom_call" | custom-call | flops 1000 | bytes 1000 | tf_op jit(solution)/shard_map/pallas_call | solution.py:48
  128.4 1.6 collective-permute-start.7
  130.6 8.0 %collective-permute-done.8 = f32[8,2048]{1,0:T(8,128)S(1)} collective-permute-done((f32[8,2048]{1,0:T(8,128)S(1)}, f32[8,2048]{1,0:T(8,128)S(1)}, u32[]{:S(2)}, u32[]{:S(2)}) %collective-permute-start.8) | collective-permute-done | bytes 65568 | tf_op jit(solution)/shard_map/ppermute | solution.py:35
  138.5 2.6 %collective-permute-done.6 = f32[8,2048]{1,0:T(8,128)S(1)} collective-permute-done((f32[8,2048]{1,0:T(8,128)S(1)}, f32[8,2048]{1,0:T(8,128)S(1)}, u32[]{:S(2)}, u32[]{:S(2)}) %collective-permute-start.6) | collective-permute-done | bytes 65568 | tf_op jit(solution)/shard_map/ppermute | solution.py:35
  141.2 1.7 shard_map.117
  142.9 0.8 collective-permute-start.10
  143.7 0.9 collective-permute-start.9
  144.6 6.3 %collective-permute-start.13 = (f32[8,2048]{1,0:T(8,128)S(1)}, f32[8,2048]{1,0:T(8,128)S(1)}, u32[]{:S(2)}, u32[]{:S(2)}) collective-permute-start(f32[8,2048]{1,0:T(8,128)S(1)} %add_add_fusion.3), channel_id=1, source_target_pairs={{0,32},{16,48},{32,0},{48,16},{1,33},{17,49},{33,1},{49,17},{2,34}... | collective-permute-start | bytes 196616 | tf_op jit(solution)/shard_map/ppermute | solution.py:35
  151.4 0.9 collective-permute-start.11
  152.3 1.7 collective-permute-done.13
  154.0 3.3 %collective-permute-done.12 = f32[8,2048]{1,0:T(8,128)S(1)} collective-permute-done((f32[8,2048]{1,0:T(8,128)S(1)}, f32[8,2048]{1,0:T(8,128)S(1)}, u32[]{:S(2)}, u32[]{:S(2)}) %collective-permute-start.12) | collective-permute-done | bytes 65568 | tf_op jit(solution)/shard_map/ppermute | solution.py:35
  157.3 0.7 collective-permute-done.9.far_a
  158.0 2.9 %shard_map.118 = bf16[8,64,1024]{2,1,0:T(8,128)(2,1)} custom-call(s32[4]{0:T(128)S(1)} %pad_add_fusion.pos_ref, f32[256,512]{1,0:T(8,128)S(1)} %get-tuple-element.117.out_a, f32[256,512]{1,0:T(8,128)S(1)} %get-tuple-element.118.out_b, f32[512,256]{1,0:T(8,128)S(1)} %get-tuple-element.119.in_a, f32[512,256]{1,0:T(8,128)S(1)} %get-tuple-element.120.in_b, ...), custom_call_target="tpu_custom_call" | custom-call | flops 1000 | bytes 1000 | tf_op jit(solution)/shard_map/pallas_call | solution.py:48
  160.9 7.7 %all-to-all-start.4 = ((bf16[8,64,1024]{2,1,0:T(8,128)(2,1)}), bf16[8,64,1024]{2,1,0:T(8,128)(2,1)S(1)}, u32[]{:S(2)}, u32[]{:S(2)}) async-start(bf16[8,64,1024]{2,1,0:T(8,128)(2,1)} %shard_map.118), calls=%async_computation.4 | async-start | bytes 2097152 | tf_op jit(solution)/shard_map/all_to_all | solution.py:39
  168.6 3.6 %shard_map.119 = bf16[256,2048]{1,0:T(8,128)(2,1)} custom-call(s32[4]{0:T(128)S(1)} %pad_add_fusion.pos_ref, bf16[512,256]{1,0:T(8,128)(2,1)S(1)} %fusion.12.disp, bf16[512,2048]{1,0:T(8,128)(2,1)} %bitcast.15.flat, bf16[256,128]{1,0:T(8,128)(2,1)S(1)} %copy-done.27, bf16[2048,128]{1,0:T(8,128)(2,1)S(1)} %copy-done.18), custom_call_target="tpu_custom_call" | custom-call | flops 1000 | bytes 1000 | tf_op jit(solution)/shard_map/pallas_call | solution.py:48
  172.2 2.1 %collective-permute-start.16 = (f32[8,2048]{1,0:T(8,128)S(1)}, f32[8,2048]{1,0:T(8,128)S(1)}, u32[]{:S(2)}, u32[]{:S(2)}) collective-permute-start(f32[8,2048]{1,0:T(8,128)S(1)} %add_add_fusion.2), channel_id=1, source_target_pairs={{0,4},{2,6},{4,0},{6,2},{1,5},{3,7},{5,1},{7,3},{8,12},{10,14},{12... | collective-permute-start | bytes 196616 | tf_op jit(solution)/shard_map/ppermute | solution.py:35
  174.2 0.9 collective-permute-start.15
  175.1 1.8 collective-permute-start.14
  176.9 1.4 collective-permute-done.16
  178.3 1.3 collective-permute-done.15
  179.8 0.7 collective-permute-start.19
  180.6 2.2 %collective-permute-start.18 = (f32[8,2048]{1,0:T(8,128)S(1)}, f32[8,2048]{1,0:T(8,128)S(1)}, u32[]{:S(2)}, u32[]{:S(2)}) collective-permute-start(f32[8,2048]{1,0:T(8,128)S(1)} %add_add_fusion.1), channel_id=1, source_target_pairs={{0,192},{64,128},{128,64},{192,0},{1,193},{65,129},{129,65},{193,1... | collective-permute-start | bytes 196616 | tf_op jit(solution)/shard_map/ppermute | solution.py:35
  182.7 0.7 collective-permute-start.17
  183.4 2.9 %collective-permute-done.19 = f32[8,2048]{1,0:T(8,128)S(1)} collective-permute-done((f32[8,2048]{1,0:T(8,128)S(1)}, f32[8,2048]{1,0:T(8,128)S(1)}, u32[]{:S(2)}, u32[]{:S(2)}) %collective-permute-start.19) | collective-permute-done | bytes 65568 | tf_op jit(solution)/shard_map/ppermute | solution.py:35
  187.6 9.4 %all-to-all-done.4.got = bf16[8,64,1024]{2,1,0:T(8,128)(2,1)S(1)} async-done(((bf16[8,64,1024]{2,1,0:T(8,128)(2,1)}), bf16[8,64,1024]{2,1,0:T(8,128)(2,1)S(1)}, u32[]{:S(2)}, u32[]{:S(2)}) %all-to-all-start.4) | async-done | bytes 1048608 | tf_op jit(solution)/shard_map/all_to_all | solution.py:39
  197.0 1.4 shard_map.120
  (96 shorter events, 8.5 us)
Async XLA Ops:
  0.6 14.9 %copy-start = (bf16[256,2048]{1,0:T(8,128)(2,1)S(1)}, bf16[256,2048]{1,0:T(8,128)(2,1)}, u32[]{:S(2)}) copy-start(bf16[256,2048]{1,0:T(8,128)(2,1)} %param.9) | copy-start | bytes 3145732
  1.5 4.1 %copy-start.32 = (pred[256]{0:T(512)(128)(4,1)}, pred[256]{0:T(512)(128)(4,1)S(1)}, u32[]{:S(2)}) copy-start(pred[256]{0:T(512)(128)(4,1)S(1)} %get-tuple-element.134) | copy-start | bytes 772
  1.5 4.1 %copy-start.33 = (pred[256]{0:T(512)(128)(4,1)}, pred[256]{0:T(512)(128)(4,1)S(1)}, u32[]{:S(2)}) copy-start(pred[256]{0:T(512)(128)(4,1)S(1)} %get-tuple-element.135) | copy-start | bytes 772
  5.5 6.4 %copy-start.29 = (s32[256,2]{0,1:T(2,128)S(1)}, s32[256,2]{0,1:T(2,128)}, u32[]{:S(2)}) copy-start(s32[256,2]{0,1:T(2,128)} %param.15) | copy-start | bytes 6148
  5.5 6.4 %copy-start.28 = (bf16[2048,8]{0,1:T(8,128)(2,1)S(1)}, bf16[2048,8]{0,1:T(8,128)(2,1)}, u32[]{:S(2)}) copy-start(bf16[2048,8]{0,1:T(8,128)(2,1)} %param.10) | copy-start | bytes 98308
  5.5 8.3 %copy-start.30 = (s32[256,2]{0,1:T(2,128)S(1)}, s32[256,2]{0,1:T(2,128)}, u32[]{:S(2)}) copy-start(s32[256,2]{0,1:T(2,128)} %param.13) | copy-start | bytes 6148
  5.6 31.5 %all-to-all-start.1 = ((bf16[8,64,2048]{2,1,0:T(8,128)(2,1)}), bf16[8,64,2048]{2,1,0:T(8,128)(2,1)S(1)}, u32[]{:S(2)}, u32[]{:S(2)}) async-start(bf16[8,64,2048]{2,1,0:T(8,128)(2,1)} %bitcast.40), calls=%async_computation.1 | async-start | bytes 4194304 | tf_op jit(solution)/shard_map/all_to_all | solution.py:39
  13.9 0.6 copy-start.31
  37.1 1.4 copy-start.1
  38.4 31.3 %all-to-all-start = ((bf16[8,64,2176]{2,1,0:T(8,128)(2,1)}), bf16[8,64,2176]{2,1,0:T(8,128)(2,1)S(1)}, u32[]{:S(2)}, u32[]{:S(2)}) async-start(bf16[8,64,2176]{2,1,0:T(8,128)(2,1)} %bitcast.39), calls=%async_computation | async-start | bytes 4456448 | tf_op jit(solution)/shard_map/all_to_all | solution.py:39
  43.7 26.0 %collective-permute-start = (bf16[512,2048]{1,0:T(8,128)(2,1)}, bf16[512,2048]{1,0:T(8,128)(2,1)}, u32[]{:S(2)}, u32[]{:S(2)}) collective-permute-start(bf16[512,2048]{1,0:T(8,128)(2,1)} %bitcast.30), channel_id=1, source_target_pairs={{0,8},{8,0},{1,9},{9,1},{2,10},{10,2},{3,11},{11,3},{4,12},{12,4},... | collective-permute-start | bytes 6291464 | tf_op jit(solution)/shard_map/ppermute | solution.py:35
  51.2 18.5 %collective-permute-start.1 = (bf16[512,1024]{1,0:T(8,128)(2,1)}, bf16[512,1024]{1,0:T(8,128)(2,1)}, u32[]{:S(2)}, u32[]{:S(2)}) collective-permute-start(bf16[512,1024]{1,0:T(8,128)(2,1)} %get-tuple-element.93.act_ref.refs_0_), channel_id=1, source_target_pairs={{0,8},{8,0},{1,9},{9,1},{2,10},{10,2},{3,11},{11,3},{4,12},{12,4},... | collective-permute-start | bytes 3145736 | tf_op jit(solution)/shard_map/ppermute | solution.py:35
  69.7 2.7 %copy-start.15 = (f32[512,1024]{1,0:T(8,128)S(1)}, f32[512,1024]{1,0:T(8,128)}, u32[]{:S(2)}) copy-start(f32[512,1024]{1,0:T(8,128)} %get-tuple-element.73.slope_ref) | copy-start | bytes 6291460
  72.3 11.9 %copy-start.9 = (bf16[512,1024]{1,0:T(8,128)(2,1)}, bf16[512,1024]{1,0:T(8,128)(2,1)S(1)}, u32[]{:S(2)}) copy-start(bf16[512,1024]{1,0:T(8,128)(2,1)S(1)} %get-tuple-element.95.refs_2_) | copy-start | bytes 3145732
  72.3 11.9 %collective-permute-start.2 = (bf16[512,1024]{1,0:T(8,128)(2,1)S(1)}, bf16[512,1024]{1,0:T(8,128)(2,1)S(1)}, u32[]{:S(2)}, u32[]{:S(2)}) collective-permute-start(bf16[512,1024]{1,0:T(8,128)(2,1)S(1)} %get-tuple-element.70), channel_id=1, source_target_pairs={{0,8},{8,0},{1,9},{9,1},{2,10},{10,2},{3,11},{11,3},{4,12},{12,4},... | collective-permute-start | bytes 3145736 | tf_op jit(solution)/shard_map/ppermute | solution.py:35
  72.4 2.5 %copy-start.13 = (bf16[1,1024,2048]{2,1,0:T(8,128)(2,1)S(1)}, bf16[1,1024,2048]{2,1,0:T(8,128)(2,1)}, u32[]{:S(2)}) copy-start(bf16[1,1024,2048]{2,1,0:T(8,128)(2,1)} %param.12) | copy-start | bytes 12582916
  74.8 9.3 %copy-start.2 = (bf16[8,64,2048]{2,1,0:T(8,128)(2,1)S(1)}, bf16[8,64,2048]{2,1,0:T(8,128)(2,1)}, u32[]{:S(2)}) copy-start(bf16[8,64,2048]{2,1,0:T(8,128)(2,1)} %copy-done.1) | copy-start | bytes 6291460
  81.9 9.4 %copy-start.5 = (bf16[512,1024]{1,0:T(8,128)(2,1)}, bf16[512,1024]{1,0:T(8,128)(2,1)S(1)}, u32[]{:S(2)}) copy-start(bf16[512,1024]{1,0:T(8,128)(2,1)S(1)} %get-tuple-element.99.refs_4_.grad.refs_6_) | copy-start | bytes 3145732
  81.9 9.4 %copy-start.25 = (bf16[512,128]{1,0:T(8,128)(2,1)}, bf16[512,128]{1,0:T(8,128)(2,1)S(1)}, u32[]{:S(2)}) copy-start(bf16[512,128]{1,0:T(8,128)(2,1)S(1)} %get-tuple-element.84) | copy-start | bytes 393220
  81.9 2.2 %collective-permute-start.3 = (bf16[512,512]{1,0:T(8,128)(2,1)S(1)}, bf16[512,512]{1,0:T(8,128)(2,1)S(1)}, u32[]{:S(2)}, u32[]{:S(2)}) collective-permute-start(bf16[512,512]{1,0:T(8,128)(2,1)S(1)} %get-tuple-element.78), channel_id=1, source_target_pairs={{0,8},{8,0},{1,9},{9,1},{2,10},{10,2},{3,11},{11,3},{4,12},{12,4},... | collective-permute-start | bytes 1572872 | tf_op jit(solution)/shard_map/ppermute | solution.py:35
  84.1 7.2 %copy-start.16 = (bf16[512,512]{1,0:T(8,128)(2,1)}, bf16[512,512]{1,0:T(8,128)(2,1)S(1)}, u32[]{:S(2)}) copy-start(bf16[512,512]{1,0:T(8,128)(2,1)S(1)} %collective-permute-done.3.refs_5_.refs_7_) | copy-start | bytes 1572868
  84.1 7.2 %copy-start.11 = (bf16[512,1024]{1,0:T(8,128)(2,1)}, bf16[512,1024]{1,0:T(8,128)(2,1)S(1)}, u32[]{:S(2)}) copy-start(bf16[512,1024]{1,0:T(8,128)(2,1)S(1)} %collective-permute-done.2.refs_3_) | copy-start | bytes 3145732
  91.4 49.8 %collective-permute-start.4 = (bf16[1024,512]{1,0:T(8,128)(2,1)}, bf16[1024,512]{1,0:T(8,128)(2,1)}, u32[]{:S(2)}, u32[]{:S(2)}) collective-permute-start(bf16[1024,512]{1,0:T(8,128)(2,1)} %get-tuple-element.81), channel_id=1, source_target_pairs={{0,64},{64,0},{128,192},{192,128},{1,65},{65,1},{129,193},{193,129... | collective-permute-start | bytes 3145736 | tf_op jit(solution)/shard_map/ppermute | solution.py:35
  93.0 48.1 %collective-permute-start.5 = (bf16[1024,512]{1,0:T(8,128)(2,1)}, bf16[1024,512]{1,0:T(8,128)(2,1)}, u32[]{:S(2)}, u32[]{:S(2)}) collective-permute-start(bf16[1024,512]{1,0:T(8,128)(2,1)} %get-tuple-element.82), channel_id=1, source_target_pairs={{0,192},{64,128},{128,64},{192,0},{1,193},{65,129},{129,65},{193,1... | collective-permute-start | bytes 3145736 | tf_op jit(solution)/shard_map/ppermute | solution.py:35
  95.2 12.8 %all-to-all-start.2 = ((bf16[8,64,128]{2,1,0:T(8,128)(2,1)}), bf16[8,64,128]{2,1,0:T(8,128)(2,1)S(1)}, u32[]{:S(2)}, u32[]{:S(2)}) async-start(bf16[8,64,128]{2,1,0:T(8,128)(2,1)} %bitcast.38), calls=%async_computation.2 | async-start | bytes 262144 | tf_op jit(solution)/shard_map/all_to_all | solution.py:39
  100.2 1.2 copy-start.6
  101.5 2.2 %copy-start.14 = (bf16[1,2048,1024]{2,1,0:T(8,128)(2,1)S(1)}, bf16[1,2048,1024]{2,1,0:T(8,128)(2,1)}, u32[]{:S(2)}) copy-start(bf16[1,2048,1024]{2,1,0:T(8,128)(2,1)} %param.11) | copy-start | bytes 12582916
  106.6 1.4 copy-start.8
  107.9 0.7 copy-start.23
  108.6 5.9 %copy-start.19 = (f32[256,128]{1,0:T(8,128)S(1)}, f32[256,128]{1,0:T(8,128)}, u32[]{:S(2)}) copy-start(f32[256,128]{1,0:T(8,128)} %pad.16.p_ref) | copy-start | bytes 393220
  108.6 12.6 %copy-start.3 = (bf16[8,64,2048]{2,1,0:T(8,128)(2,1)S(1)}, bf16[8,64,2048]{2,1,0:T(8,128)(2,1)}, u32[]{:S(2)}) copy-start(bf16[8,64,2048]{2,1,0:T(8,128)(2,1)} %copy-done.1) | copy-start | bytes 6291460
  108.6 52.3 %all-to-all-start.3 = ((bf16[8,64,2048]{2,1,0:T(8,128)(2,1)}), bf16[8,64,2048]{2,1,0:T(8,128)(2,1)}, u32[]{:S(2)}, u32[]{:S(2)}) async-start(bf16[8,64,2048]{2,1,0:T(8,128)(2,1)} %bitcast.34), calls=%async_computation.3 | async-start | bytes 4194304 | tf_op jit(solution)/shard_map/all_to_all | solution.py:39
  114.5 1.2 copy-start.4
  115.7 0.9 copy-start.20
  116.6 0.9 copy-start.21
  117.5 0.9 copy-start.22
  118.4 0.9 copy-start.24
  119.3 1.9 copy-start.7
  119.3 1.9 copy-start.17
  120.6 0.6 copy-start.26
  121.2 1.2 copy-start.10
  122.5 1.2 copy-start.12
  128.3 10.2 %collective-permute-start.8 = (f32[8,2048]{1,0:T(8,128)S(1)}, f32[8,2048]{1,0:T(8,128)S(1)}, u32[]{:S(2)}, u32[]{:S(2)}) collective-permute-start(f32[8,2048]{1,0:T(8,128)S(1)} %get-tuple-element.107), channel_id=1, source_target_pairs={{0,9},{1,8},{8,1},{9,0},{2,11},{3,10},{10,3},{11,2},{4,13},{5,12},... | collective-permute-start | bytes 196616 | tf_op jit(solution)/shard_map/ppermute | solution.py:35
  128.4 10.1 %collective-permute-start.7 = (f32[8,2048]{1,0:T(8,128)S(1)}, f32[8,2048]{1,0:T(8,128)S(1)}, u32[]{:S(2)}, u32[]{:S(2)}) collective-permute-start(f32[8,2048]{1,0:T(8,128)S(1)} %get-tuple-element.107), channel_id=1, source_target_pairs={{0,8},{1,9},{8,0},{9,1},{2,10},{3,11},{10,2},{11,3},{4,12},{5,13},... | collective-permute-start | bytes 196616 | tf_op jit(solution)/shard_map/ppermute | solution.py:35
  130.0 11.1 %collective-permute-start.6 = (f32[8,2048]{1,0:T(8,128)S(1)}, f32[8,2048]{1,0:T(8,128)S(1)}, u32[]{:S(2)}, u32[]{:S(2)}) collective-permute-start(f32[8,2048]{1,0:T(8,128)S(1)} %get-tuple-element.107), channel_id=1, source_target_pairs={{0,1},{1,0},{8,9},{9,8},{2,3},{3,2},{10,11},{11,10},{4,5},{5,4},{1... | collective-permute-start | bytes 196616 | tf_op jit(solution)/shard_map/ppermute | solution.py:35
  142.9 14.4 %collective-permute-start.10 = (bf16[512,512]{1,0:T(8,128)(2,1)S(1)}, bf16[512,512]{1,0:T(8,128)(2,1)S(1)}, u32[]{:S(2)}, u32[]{:S(2)}) collective-permute-start(bf16[512,512]{1,0:T(8,128)(2,1)S(1)} %get-tuple-element.113), channel_id=1, source_target_pairs={{0,64},{64,0},{128,192},{192,128},{1,65},{65,1},{129,193},{193,129... | collective-permute-start | bytes 1572872 | tf_op jit(solution)/shard_map/ppermute | solution.py:35
  143.7 14.3 %collective-permute-start.9 = (bf16[512,512]{1,0:T(8,128)(2,1)S(1)}, bf16[512,512]{1,0:T(8,128)(2,1)S(1)}, u32[]{:S(2)}, u32[]{:S(2)}) collective-permute-start(bf16[512,512]{1,0:T(8,128)(2,1)S(1)} %get-tuple-element.112), channel_id=1, source_target_pairs={{0,192},{64,128},{128,64},{192,0},{1,193},{65,129},{129,65},{193,1... | collective-permute-start | bytes 1572872 | tf_op jit(solution)/shard_map/ppermute | solution.py:35
  144.6 9.4 %collective-permute-start.13 = (f32[8,2048]{1,0:T(8,128)S(1)}, f32[8,2048]{1,0:T(8,128)S(1)}, u32[]{:S(2)}, u32[]{:S(2)}) collective-permute-start(f32[8,2048]{1,0:T(8,128)S(1)} %add_add_fusion.3), channel_id=1, source_target_pairs={{0,32},{16,48},{32,0},{48,16},{1,33},{17,49},{33,1},{49,17},{2,34}... | collective-permute-start | bytes 196616 | tf_op jit(solution)/shard_map/ppermute | solution.py:35
  150.9 6.4 %collective-permute-start.12 = (f32[8,2048]{1,0:T(8,128)S(1)}, f32[8,2048]{1,0:T(8,128)S(1)}, u32[]{:S(2)}, u32[]{:S(2)}) collective-permute-start(f32[8,2048]{1,0:T(8,128)S(1)} %add_add_fusion.3), channel_id=1, source_target_pairs={{0,48},{16,32},{32,16},{48,0},{1,49},{17,33},{33,17},{49,1},{2,50}... | collective-permute-start | bytes 196616 | tf_op jit(solution)/shard_map/ppermute | solution.py:35
  151.4 5.8 %collective-permute-start.11 = (f32[8,2048]{1,0:T(8,128)S(1)}, f32[8,2048]{1,0:T(8,128)S(1)}, u32[]{:S(2)}, u32[]{:S(2)}) collective-permute-start(f32[8,2048]{1,0:T(8,128)S(1)} %add_add_fusion.3), channel_id=1, source_target_pairs={{0,16},{16,0},{32,48},{48,32},{1,17},{17,1},{33,49},{49,33},{2,18}... | collective-permute-start | bytes 196616 | tf_op jit(solution)/shard_map/ppermute | solution.py:35
  160.9 7.7 %copy-start.18 = (bf16[2048,128]{1,0:T(8,128)(2,1)S(1)}, bf16[2048,128]{1,0:T(8,128)(2,1)}, u32[]{:S(2)}) copy-start(bf16[2048,128]{1,0:T(8,128)(2,1)} %pad.15.weight) | copy-start | bytes 1572868
  160.9 7.7 %copy-start.27 = (bf16[256,128]{1,0:T(8,128)(2,1)S(1)}, bf16[256,128]{1,0:T(8,128)(2,1)}, u32[]{:S(2)}) copy-start(bf16[256,128]{1,0:T(8,128)(2,1)} %copy-done.26) | copy-start | bytes 196612
  160.9 36.2 %all-to-all-start.4 = ((bf16[8,64,1024]{2,1,0:T(8,128)(2,1)}), bf16[8,64,1024]{2,1,0:T(8,128)(2,1)S(1)}, u32[]{:S(2)}, u32[]{:S(2)}) async-start(bf16[8,64,1024]{2,1,0:T(8,128)(2,1)} %shard_map.118), calls=%async_computation.4 | async-start | bytes 2097152 | tf_op jit(solution)/shard_map/all_to_all | solution.py:39
  172.2 6.1 %collective-permute-start.16 = (f32[8,2048]{1,0:T(8,128)S(1)}, f32[8,2048]{1,0:T(8,128)S(1)}, u32[]{:S(2)}, u32[]{:S(2)}) collective-permute-start(f32[8,2048]{1,0:T(8,128)S(1)} %add_add_fusion.2), channel_id=1, source_target_pairs={{0,4},{2,6},{4,0},{6,2},{1,5},{3,7},{5,1},{7,3},{8,12},{10,14},{12... | collective-permute-start | bytes 196616 | tf_op jit(solution)/shard_map/ppermute | solution.py:35
  174.2 5.3 %collective-permute-start.15 = (f32[8,2048]{1,0:T(8,128)S(1)}, f32[8,2048]{1,0:T(8,128)S(1)}, u32[]{:S(2)}, u32[]{:S(2)}) collective-permute-start(f32[8,2048]{1,0:T(8,128)S(1)} %add_add_fusion.2), channel_id=1, source_target_pairs={{0,6},{2,4},{4,2},{6,0},{1,7},{3,5},{5,3},{7,1},{8,14},{10,12},{12... | collective-permute-start | bytes 196616 | tf_op jit(solution)/shard_map/ppermute | solution.py:35
  175.1 4.7 %collective-permute-start.14 = (f32[8,2048]{1,0:T(8,128)S(1)}, f32[8,2048]{1,0:T(8,128)S(1)}, u32[]{:S(2)}, u32[]{:S(2)}) collective-permute-start(f32[8,2048]{1,0:T(8,128)S(1)} %add_add_fusion.2), channel_id=1, source_target_pairs={{0,2},{2,0},{4,6},{6,4},{1,3},{3,1},{5,7},{7,5},{8,10},{10,8},{12,... | collective-permute-start | bytes 196616 | tf_op jit(solution)/shard_map/ppermute | solution.py:35
  179.8 6.5 %collective-permute-start.19 = (f32[8,2048]{1,0:T(8,128)S(1)}, f32[8,2048]{1,0:T(8,128)S(1)}, u32[]{:S(2)}, u32[]{:S(2)}) collective-permute-start(f32[8,2048]{1,0:T(8,128)S(1)} %add_add_fusion.1), channel_id=1, source_target_pairs={{0,128},{64,192},{128,0},{192,64},{1,129},{65,193},{129,1},{193,65... | collective-permute-start | bytes 196616 | tf_op jit(solution)/shard_map/ppermute | solution.py:35
  180.6 6.1 %collective-permute-start.18 = (f32[8,2048]{1,0:T(8,128)S(1)}, f32[8,2048]{1,0:T(8,128)S(1)}, u32[]{:S(2)}, u32[]{:S(2)}) collective-permute-start(f32[8,2048]{1,0:T(8,128)S(1)} %add_add_fusion.1), channel_id=1, source_target_pairs={{0,192},{64,128},{128,64},{192,0},{1,193},{65,129},{129,65},{193,1... | collective-permute-start | bytes 196616 | tf_op jit(solution)/shard_map/ppermute | solution.py:35
  182.7 4.3 %collective-permute-start.17 = (f32[8,2048]{1,0:T(8,128)S(1)}, f32[8,2048]{1,0:T(8,128)S(1)}, u32[]{:S(2)}, u32[]{:S(2)}) collective-permute-start(f32[8,2048]{1,0:T(8,128)S(1)} %add_add_fusion.1), channel_id=1, source_target_pairs={{0,64},{64,0},{128,192},{192,128},{1,65},{65,1},{129,193},{193,129... | collective-permute-start | bytes 196616 | tf_op jit(solution)/shard_map/ppermute | solution.py:35

commit v8 on v7

--- a/solution.py
+++ b/solution.py
@@ -10,8 +10,7 @@
 GROUP = ("x", "zl")
 EXTRA = 128
 VMEM_LIMIT = 16 * 1024 * 1024
-COST_SLOTS = 1000
-LONG = 26_000_000_000
+LONG = 50_000_000_000
 F32 = jnp.float32
 BF16 = jnp.bfloat16
 
@@ -49,7 +48,7 @@
         body,
         in_specs=[pl.BlockSpec(memory_space=pltpu.SMEM)]
         + [vmem] * len(inputs)
-        + [pl.BlockSpec(memory_space=pl.ANY)] * len(far),
+        + [pl.BlockSpec(memory_space=pltpu.HBM)] * len(far),
         out_specs=[vmem] * len(outputs),
         out_shape=[jax.ShapeDtypeStruct(shape, dtype) for shape, dtype in outputs],
         scratch_shapes=scratch,
@@ -160,47 +159,58 @@
     masks = ((1, 2), (3, 2))
 
     def body(pos_ref, *refs):
-        out_refs, right_refs = refs[:4], refs[4:6]
-        lefts, outs, (buffer, sems) = refs[6:8], refs[8:10], refs[10:]
+        rights, lefts, outs = refs[:4], refs[4:8], refs[8:10]
+        buffer_out, buffer_in, sems = refs[10:]
         copies = []
-        for k in range(2):
+        for k in range(4):
+            buffer, width = (buffer_out, width_out) if k < 2 else (buffer_in, width_in)
             for r in (1, 2, 3):
-                start = pl.multiple_of((pos_ref[0] ^ r) * width_in, width_in)
+                start = pl.multiple_of((pos_ref[0] ^ r) * width, width)
                 copy = pltpu.make_async_copy(
-                    lefts[k].at[:, pl.ds(start, width_in)], buffer.at[k, r - 1], sems.at[k, r - 1]
+                    lefts[k].at[:, pl.ds(start, width)],
+                    buffer.at[k % 2, r - 1],
+                    sems.at[k, r - 1],
                 )
                 copy.start()
                 copies.append(copy)
-        for i, j, value in row_products(pos_ref, out_refs, 0, masks, width_out, cols_out):
-            outs[i][j * width_out : (j + 1) * width_out, :] = value.astype(BF16)
-        for copy in copies:
-            copy.wait()
         dims = (((0,), (0,)), ((), ()))
-        for i in range(2):
-            own = pl.multiple_of((2 * pos_ref[1] + i) * cols_in, cols_in)
-            for j in range(2):
-                r = masks[i][j] - 1
-                value = lax.dot_general(
-                    buffer[0, r],
-                    right_refs[0][:, pl.ds(own, cols_in)],
-                    dims,
-                    preferred_element_type=F32,
-                )
-                value = value + lax.dot_general(
-                    buffer[1, r],
-                    right_refs[1][:, i * cols_in : (i + 1) * cols_in],
-                    dims,
-                    preferred_element_type=F32,
-                )
-                outs[i][2 * width_out :, j * cols_in : (j + 1) * cols_in] = value.astype(BF16)
+        for part in range(2):
+            buffer, cols = (buffer_in, cols_in) if part else (buffer_out, cols_out)
+            mine, other = rights[2 * part : 2 * part + 2]
+            for copy in copies[6 * part : 6 * part + 6]:
+                copy.wait()
+            for i in range(2):
+                own = i * cols
+                if part:
+                    own = pl.multiple_of((2 * pos_ref[1] + i) * cols, cols)
+                for j in range(2):
+                    r = masks[i][j] - 1
+                    value = lax.dot_general(
+                        buffer[0, r], mine[:, pl.ds(own, cols)], dims, preferred_element_type=F32
+                    )
+                    value = value + lax.dot_general(
+                        buffer[1, r],
+                        other[:, i * cols : (i + 1) * cols],
+                        dims,
+                        preferred_element_type=F32,
+                    )
+                    value = value.astype(BF16)
+                    if part:
+                        outs[i][2 * width_out :, j * cols : (j + 1) * cols] = value
+                    else:
+                        outs[i][j * width_out : (j + 1) * width_out, :] = value
 
     return call(
         body,
         pos,
-        [*left_out, *right_out, *right_in],
+        [*right_out, *right_in],
         [((2 * width_out + width_in, cols_out), BF16)] * 2,
-        far=[*left_in],
-        scratch=[pltpu.VMEM((2, 3, slots, width_in), BF16), pltpu.SemaphoreType.DMA((2, 3))],
+        far=[*left_out, *left_in],
+        scratch=[
+            pltpu.VMEM((2, 3, slots, width_out), BF16),
+            pltpu.VMEM((2, 3, slots, width_in), BF16),
+            pltpu.SemaphoreType.DMA((4, 3)),
+        ],
     )
 
 
@@ -297,29 +307,34 @@
     return outer[None], inner[None]
 
 
-def slot_grads_of(pos, grad_pre, weight_in):
+def slot_grads_of(pos, grad_pre, weight_in, gate_grad):
     slots, hidden = grad_pre.shape
     width = weight_in.shape[0]
     step = width // 4
 
-    def body(pos_ref, grad, weight, out):
+    def body(pos_ref, grad, weight, gate, out):
         for i in range(4):
             at = slice(i * step, (i + 1) * step)
             out[:, at] = lax.dot_general(
                 grad[...], weight[at, :], (((1,), (1,)), ((), ())), preferred_element_type=F32
             ).astype(BF16)
-
-    return call(body, pos, [grad_pre, weight_in], [((slots, width), BF16)], COST_SLOTS)[0]
-
-
-def router_grads(pos, dispatch, gate_back, tokens, probs, combine, keep, denominator, scale):
+        out[:, width:] = gate[...]
+
+    return call(
+        body, pos, [grad_pre, weight_in, gate_grad], [((slots, width + EXTRA), BF16)]
+    )[0]
+
+
+def router_grads(pos, dispatch, back, tokens, probs, combine, keep, denominator, scale):
     rows, width = tokens.shape
     experts = 8
     step = width // 4
 
-    def body(pos_ref, disp, back, tok, p_ref, c_ref, k_ref, d_ref, logit, router):
+    def body(pos_ref, disp, flat, tok, p_ref, c_ref, k_ref, d_ref, logit, router):
         dims = (((0,), (0,)), ((), ()))
-        combine_grad = lax.dot_general(disp[...], back[...], dims, preferred_element_type=F32)
+        combine_grad = lax.dot_general(
+            disp[...], flat[:, width:], dims, preferred_element_type=F32
+        )
         weighted = jnp.sum(combine_grad * c_ref[...], axis=1, keepdims=True)
         probs_grad = k_ref[...] * (combine_grad - weighted) / d_ref[...]
         probs = p_ref[...]
@@ -334,13 +349,13 @@
     return call(
         body,
         pos,
-        [dispatch, gate_back, tokens, probs, combine, keep, denominator],
+        [dispatch, back, tokens, probs, combine, keep, denominator],
         [((rows, EXTRA), BF16), ((experts, width), F32)],
     )
 
 
 def token_grads(pos, dispatch, back, logit_lanes, weight_lanes):
-    rows, width = dispatch.shape[1], back.shape[1]
+    rows, width = dispatch.shape[1], back.shape[1] - EXTRA
     step = width // 4
 
     def body(pos_ref, disp, flat, logit, weight, out):
@@ -434,21 +449,25 @@
 
     sent = sent_parts(pos, left_out, right_out, left_in, right_in)
     got = (swap(sent[0], "y", 1), swap(sent[1], "y", 3))
-    gate_grad, grad_pre, _ = tie(gate_grad, grad_pre, sent)
-    gate_back = exchange(gate_grad.reshape(experts, capacity, EXTRA), GROUP).reshape(
-        slot_count, EXTRA
-    )
-    grad_slots = slot_grads_of(pos, grad_pre, weight_in)
-    grad_slots, gate_back = tie(grad_slots, gate_back)
+    pre_for_slots, _ = tie(grad_pre, sent)
+    grad_slots = slot_grads_of(pos, pre_for_slots, weight_in, gate_grad)
     back = exchange(
-        grad_slots.reshape(experts, capacity, model_width), GROUP
-    ).reshape(slot_count, model_width)
-
-    gate_back, _ = tie(gate_back, grad_slots)
+        grad_slots.reshape(experts, capacity, model_width + EXTRA), GROUP
+    ).reshape(slot_count, model_width + EXTRA)
+
+    left_in, left_out, right_in, right_out, _ = tie(
+        left_in, left_out, right_in, right_out, grad_slots
+    )
+    *near, far_a, far_b = kept_parts(pos, left_out, right_out, left_in, right_in)
+    got, far_a, far_b = tie(got, far_a, far_b)
+    far_a, far_b = far_sums(pos, (far_a, far_b), got)
+    far = (swap(far_a, "y", 3), swap(far_b, "y", 1))
+
+    back, _ = tie(back, far_a)
     logit_lanes, router_part = router_grads(
         pos,
         dispatch,
-        gate_back,
+        back,
         tokens,
         probs_lanes,
         combine_lanes,
@@ -461,17 +480,6 @@
         near, far, both = (swap(value, axes, mask) for mask in (one, two, one ^ two))
         return (value + near) + (far + both)
 
-    left_in, left_out, right_in, right_out, _ = tie(
-        left_in, left_out, right_in, right_out, router_part
-    )
-    *near, far_a, far_b = kept_parts(pos, left_out, right_out, left_in, right_in)
-    router_part, _ = tie(router_part, far_a)
-    router_part = router_round(router_part, ("core", "zl"), 1, 2)
-    got, far_a, far_b, router_part = tie(got, far_a, far_b, router_part)
-    far_a, far_b = far_sums(pos, (far_a, far_b), got)
-    far = (swap(far_a, "y", 3), swap(far_b, "y", 1))
-
-    router_part, _ = tie(router_part, far_a)
     router_part = router_round(router_part, "zh", 1, 3)
     near, far, router_part = tie(near, far, router_part)
     pieces = zh_pieces(pos, near[:2], near[2:], got, far, grad_scale)
@@ -482,6 +490,7 @@
     router_part, _ = tie(router_part, grad_tokens)
     router_part = router_round(router_part, "x", 1, 3)
     router_part = router_round(router_part, "y", 1, 3)
+    router_part = router_round(router_part, ("core", "zl"), 1, 2)
     got, router_part = tie(got, router_part)
     outer_share, inner_share = shares(pos, got, near[0].shape[0] // 8)
     return (grad_tokens, router_part.T, inner_share, outer_share)

time: 200 us -> 195 us (0.975); the launches traced: 198 us -> 191 us
  starting transfers between devices: 55.1 us -> 47.3 us
  local copies, waits for them, and re-layouts: 25.5 us -> 27.6 us
    all_to_all x5 -> x4, starting transfers between devices: 30.3 us -> 21.7 us  [exchange(): return lax.all_to_all(values, axes, split_axis=0, concat_axis=0, tiled=True)]
    all_to_all x5 -> x4, waiting for transfers between devices: 39.2 us -> 37 us  [exchange(): return lax.all_to_all(values, axes, split_axis=0, concat_axis=0, tiled=True)]
    unnamed x69 -> x81, local copies, waits for them, and re-layouts: 19.6 us -> 21.6 us
  transfers between devices with their start and end apart: 25 -> 24, of which waited for: 15 -> 17; matrix products, arithmetic and copies ran while one was open for 11% -> 11% of each run, Pallas kernels for 12% -> 11%
where the time goes in v8:
time: 195 us; the launch traced here: 191 us
  waiting for transfers between devices  62.3 us (32%)
  starting transfers between devices  47.3 us (24%)
  Pallas kernels  32.8 us (17%)
  local copies, waits for them, and re-layouts  27.6 us (14%)
  matrix products  14.7 us (8%)
  other arithmetic  5.47 us (3%)
    all_to_all x4, waiting for transfers between devices, exchange(): return lax.all_to_all(values, axes, split_axis=0, concat_axis=0, tiled=True)  37 us
    pallas_call x10, Pallas kernels, call(): pl.pallas_call(body, in_specs=[pl.BlockSpec(memory_space=pltpu.SMEM)] + [...  32.8 us
    ppermute x20, starting transfers between devices, swap(): return lax.ppermute(values, axis, [(i, i ^ mask) for i in range(size)])  25.6 us
    ppermute x20, waiting for transfers between devices, swap(): return lax.ppermute(values, axis, [(i, i ^ mask) for i in range(size)])  25.3 us
    all_to_all x4, starting transfers between devices, exchange(): return lax.all_to_all(values, axes, split_axis=0, concat_axis=0, tiled=True)  21.7 us
    unnamed x81, local copies, waits for them, and re-layouts  21.6 us
    dot_general x1, matrix products, per_device(): hidden_pre = jnp.dot(slot_tokens, weight_in, preferred_element_type=F32)  7.47 us
    pad x4, local copies, waits for them, and re-layouts, lanes(): return jnp.pad(values, ((0, 0), (0, EXTRA - experts)), constant_values=fill)  3.93 us
  transfers between devices with their start and end apart: 24, of which 17 were waited for; matrix products, arithmetic and copies ran while one was open for 11% of the time, Pallas kernels for 11%

profile of v8, /device:TPU:2, one launch (start us, length us, event | category | flops | bytes accessed | tf_op | source)
XLA Modules:
  0.0 191.2 jit_solution(2121616535879971115)
XLA Ops:
  2.2 3.3 %convolution_convert_fusion = bf16[512,2048]{1,0:T(8,128)(2,1)} fusion(bf16[256,2048]{1,0:T(8,128)(2,1)} %tok.1, s32[256]{0:T(256)S(1)} %bitcast.44, s32[256]{0:T(256)S(1)} %bitcast.40, pred[256]{0:T(512)(128)(4,1)S(1)} %get-tuple-element.123, pred[256]{0:T(512)(128)(4,1)S(1)} %get-tuple-element.122), kind=kOutput, calls=%fused_computation.1 | convolution fusion | flops 538574848 | bytes 3148288 | tf_op jit(solution)/shard_map/dot_general | solution.py:396
  5.6 6.3 %all-to-all-start.1 = ((bf16[8,64,2048]{2,1,0:T(8,128)(2,1)}), bf16[8,64,2048]{2,1,0:T(8,128)(2,1)S(1)}, u32[]{:S(2)}, u32[]{:S(2)}) async-start(bf16[8,64,2048]{2,1,0:T(8,128)(2,1)} %bitcast.38), calls=%async_computation.1 | async-start | bytes 4194304 | tf_op jit(solution)/shard_map/all_to_all | solution.py:38
  11.9 1.6 fusion.17
  14.6 0.9 convolution_convert_fusion.2
  15.6 1.4 convolution_convert_fusion.1
  16.9 1.6 pad_maximum_fusion
  18.5 18.6 %all-to-all-done.1 = bf16[8,64,2048]{2,1,0:T(8,128)(2,1)S(1)} async-done(((bf16[8,64,2048]{2,1,0:T(8,128)(2,1)}), bf16[8,64,2048]{2,1,0:T(8,128)(2,1)S(1)}, u32[]{:S(2)}, u32[]{:S(2)}) %all-to-all-start.1) | async-done | bytes 2097184 | tf_op jit(solution)/shard_map/all_to_all | solution.py:38
  37.1 1.4 copy-done.1
  38.5 5.3 %all-to-all-start = ((bf16[8,64,2176]{2,1,0:T(8,128)(2,1)}), bf16[8,64,2176]{2,1,0:T(8,128)(2,1)S(1)}, u32[]{:S(2)}, u32[]{:S(2)}) async-start(bf16[8,64,2176]{2,1,0:T(8,128)(2,1)} %bitcast.37), calls=%async_computation | async-start | bytes 4456448 | tf_op jit(solution)/shard_map/all_to_all | solution.py:38
  43.8 7.5 %fusion.3 = (f32[512,1024]{1,0:T(8,128)}, bf16[512,1024]{1,0:T(8,128)(2,1)}) fusion(bf16[512,2048]{1,0:T(8,128)(2,1)} %bitcast.31, bf16[1,2048,1024]{2,1,0:T(8,128)(2,1)} %param.11), kind=kOutput, calls=%fused_computation.7 | convolution fusion | flops 2152726528 | bytes 9437184 | tf_op jit(solution)/shard_map/dot_general | solution.py:427
  53.1 1.8 copy.28
  55.6 1.9 %pad.15.weight = bf16[2048,128]{1,0:T(8,128)(2,1)} pad(bf16[2048,8]{1,0:T(8,128)(2,1)} %copy.28, bf16[]{:T(256)} %constant.41.clone.1), padding=0_0x0_120 | pad | bytes 557058 | tf_op jit(solution)/shard_map/jit(_pad)/pad | solution.py:410
  58.5 11.3 %all-to-all-done = bf16[8,64,2176]{2,1,0:T(8,128)(2,1)S(1)} async-done(((bf16[8,64,2176]{2,1,0:T(8,128)(2,1)}), bf16[8,64,2176]{2,1,0:T(8,128)(2,1)S(1)}, u32[]{:S(2)}, u32[]{:S(2)}) %all-to-all-start) | async-done | bytes 2228256 | tf_op jit(solution)/shard_map/all_to_all | solution.py:38
  69.7 1.6 broadcast_in_dim.52.d_ref
  71.3 1.0 shard_map.111
  72.4 2.4 %copy-done.12 = bf16[1,1024,2048]{2,1,0:T(8,128)(2,1)S(1)} copy-done((bf16[1,1024,2048]{2,1,0:T(8,128)(2,1)S(1)}, bf16[1,1024,2048]{2,1,0:T(8,128)(2,1)}, u32[]{:S(2)}) %copy-start.12) | copy-done | bytes 4194328
  74.8 7.1 %shard_map.112 = (bf16[512,1024]{1,0:T(8,128)(2,1)S(1)}, bf16[512,512]{1,0:T(8,128)(2,1)S(1)}, bf16[512,128]{1,0:T(8,128)(2,1)S(1)}) custom-call(s32[4]{0:T(128)S(1)} %pad_add_fusion.pos_ref, bf16[512,2176]{1,0:T(8,128)(2,1)S(1)} %bitcast.27, bf16[1024,2048]{1,0:T(8,128)(2,1)S(1)} %bitcast.35, bf16[512,1024]{1,0:T(8,128)(2,1)} %get-tuple-element.78.act_ref.refs_4_.refs_0_, ...), custom_call_target="tpu_custom_call" | custom-call | flops 1000 | bytes 1000 | tf_op jit(solution)/shard_map/pallas_call | solution.py:47
  82.4 1.7 collective-permute-done.3.refs_3_.refs_7_
  84.1 6.4 %shard_map.113 = (bf16[1024,512]{1,0:T(8,128)(2,1)}, bf16[1024,512]{1,0:T(8,128)(2,1)}) custom-call(s32[4]{0:T(128)S(1)} %pad_add_fusion.pos_ref, bf16[512,1024]{1,0:T(8,128)(2,1)S(1)} %get-tuple-element.80.refs_0_.refs_2_, bf16[512,1024]{1,0:T(8,128)(2,1)S(1)} %collective-permute-done.2.refs_1_.refs_3_, ...), custom_call_target="tpu_custom_call" | custom-call | flops 1000 | bytes 1000 | tf_op jit(solution)/shard_map/pallas_call | solution.py:47
  90.6 1.7 collective-permute-start.4
  92.3 2.2 %collective-permute-start.5 = (bf16[1024,512]{1,0:T(8,128)(2,1)}, bf16[1024,512]{1,0:T(8,128)(2,1)}, u32[]{:S(2)}, u32[]{:S(2)}) collective-permute-start(bf16[1024,512]{1,0:T(8,128)(2,1)} %get-tuple-element.75), channel_id=1, source_target_pairs={{0,192},{64,128},{128,64},{192,0},{1,193},{65,129},{129,65},{193,1... | collective-permute-start | bytes 3145736 | tf_op jit(solution)/shard_map/ppermute | solution.py:34
  94.5 2.9 %shard_map.114 = bf16[512,2176]{1,0:T(8,128)(2,1)S(1)} custom-call(s32[4]{0:T(128)S(1)} %pad_add_fusion.pos_ref, bf16[512,1024]{1,0:T(8,128)(2,1)S(1)} %get-tuple-element.84.refs_2_.grad.refs_6_, bf16[2048,1024]{1,0:T(8,128)(2,1)S(1)} %bitcast.36, bf16[512,128]{1,0:T(8,128)(2,1)S(1)} %get-tuple-element.77.gate), custom_call_target="tpu_custom_call" | custom-call | flops 1000 | bytes 1000 | tf_op jit(solution)/shard_map/pallas_call | solution.py:47
  97.4 1.4 copy-done.7
  98.8 5.3 %all-to-all-start.2 = ((bf16[8,64,2176]{2,1,0:T(8,128)(2,1)}), bf16[8,64,2176]{2,1,0:T(8,128)(2,1)S(1)}, u32[]{:S(2)}, u32[]{:S(2)}) async-start(bf16[8,64,2176]{2,1,0:T(8,128)(2,1)} %bitcast.34), calls=%async_computation.2 | async-start | bytes 4456448 | tf_op jit(solution)/shard_map/all_to_all | solution.py:38
  104.0 1.6 copy-done.3
  105.6 1.2 copy-done.5
  106.9 1.2 copy-done.9
  108.1 1.2 copy-done.11
  109.3 1.0 copy-done.17
  110.4 4.6 %shard_map.115 = (f32[256,512]{1,0:T(8,128)S(1)}, f32[256,512]{1,0:T(8,128)S(1)}, f32[512,256]{1,0:T(8,128)S(1)}, f32[512,256]{1,0:T(8,128)S(1)}, f32[512,512]{1,0:T(8,128)S(1)}, /*index=5*/f32[512,512]{1,0:T(8,128)S(1)}) custom-call(s32[4]{0:T(128)S(1)} %pad_add_fusion.pos_ref, bf16[512,1024]{1,0:T(8,128)(2,1)} %get-tuple-element.78.act_ref.refs_4_.refs_0_, ...), custom_call_target="tpu_custom_call" | custom-call | flops 1000 | bytes 1000 | tf_op jit(solution)/shard_map/pallas_call | solution.py:47
  115.0 1.2 collective-permute-done.4.got_a
  116.3 2.5 %collective-permute-done.5.got_b = bf16[1024,512]{1,0:T(8,128)(2,1)} collective-permute-done((bf16[1024,512]{1,0:T(8,128)(2,1)}, bf16[1024,512]{1,0:T(8,128)(2,1)}, u32[]{:S(2)}, u32[]{:S(2)}) %collective-permute-start.5) | collective-permute-done | bytes 1048608 | tf_op jit(solution)/shard_map/ppermute | solution.py:34
  118.8 2.7 %shard_map.116 = (bf16[512,512]{1,0:T(8,128)(2,1)}, bf16[512,512]{1,0:T(8,128)(2,1)}) custom-call(s32[4]{0:T(128)S(1)} %pad_add_fusion.pos_ref, f32[512,512]{1,0:T(8,128)S(1)} %get-tuple-element.88.far_a, f32[512,512]{1,0:T(8,128)S(1)} %get-tuple-element.89.far_b, bf16[1024,512]{1,0:T(8,128)(2,1)} %collective-permute-done.4.got_a, ...), custom_call_target="tpu_custom_call" | custom-call | flops 49999998976 | bytes 1000 | tf_op jit(solution)/shard_map/pallas_call | solution.py:47
  121.6 2.3 %collective-permute-start.6 = (bf16[512,512]{1,0:T(8,128)(2,1)}, bf16[512,512]{1,0:T(8,128)(2,1)}, u32[]{:S(2)}, u32[]{:S(2)}) collective-permute-start(bf16[512,512]{1,0:T(8,128)(2,1)} %get-tuple-element.92), channel_id=1, source_target_pairs={{0,192},{64,128},{128,64},{192,0},{1,193},{65,129},{129,65},{193,1... | collective-permute-start | bytes 1572872 | tf_op jit(solution)/shard_map/ppermute | solution.py:34
  123.8 6.9 %all-to-all-done.2 = bf16[8,64,2176]{2,1,0:T(8,128)(2,1)S(1)} async-done(((bf16[8,64,2176]{2,1,0:T(8,128)(2,1)}), bf16[8,64,2176]{2,1,0:T(8,128)(2,1)S(1)}, u32[]{:S(2)}, u32[]{:S(2)}) %all-to-all-start.2) | async-done | bytes 2228256 | tf_op jit(solution)/shard_map/all_to_all | solution.py:38
  130.8 1.2 copy-done.6
  132.0 0.9 copy-done.27
  132.9 0.9 copy-done.28
  133.8 0.9 copy-done.29
  134.7 0.9 copy-done.30
  135.6 1.3 shard_map.117
  136.9 6.4 %collective-permute-start.10 = (f32[8,2048]{1,0:T(8,128)S(1)}, f32[8,2048]{1,0:T(8,128)S(1)}, u32[]{:S(2)}, u32[]{:S(2)}) collective-permute-start(f32[8,2048]{1,0:T(8,128)S(1)} %get-tuple-element.103), channel_id=1, source_target_pairs={{0,32},{16,48},{32,0},{48,16},{1,33},{17,49},{33,1},{49,17},{2,34}... | collective-permute-start | bytes 196616 | tf_op jit(solution)/shard_map/ppermute | solution.py:34
  143.8 0.9 collective-permute-start.8
  144.8 1.0 collective-permute-done.10
  145.8 4.0 %collective-permute-done.9 = f32[8,2048]{1,0:T(8,128)S(1)} collective-permute-done((f32[8,2048]{1,0:T(8,128)S(1)}, f32[8,2048]{1,0:T(8,128)S(1)}, u32[]{:S(2)}, u32[]{:S(2)}) %collective-permute-start.9) | collective-permute-done | bytes 65568 | tf_op jit(solution)/shard_map/ppermute | solution.py:34
  149.8 0.8 collective-permute-done.8
  151.3 2.2 %shard_map.118 = bf16[8,64,1024]{2,1,0:T(8,128)(2,1)S(1)} custom-call(s32[4]{0:T(128)S(1)} %pad_add_fusion.pos_ref, f32[256,512]{1,0:T(8,128)S(1)} %copy-done.20, f32[256,512]{1,0:T(8,128)S(1)} %copy-done.22, f32[512,256]{1,0:T(8,128)S(1)} %copy-done.24, f32[512,256]{1,0:T(8,128)S(1)} %copy-done.26, bf16[1024,512]{1,0:T(8,128)(2,1)} %collective-permute-done.4.got_a, ...), custom_call_target="tpu_custom_call" | custom-call | flops 1000 | bytes 1000 | tf_op jit(solution)/shard_map/pallas_call | solution.py:47
  153.5 1.0 copy-done.13
  154.5 4.8 %all-to-all-start.3 = ((bf16[8,64,1024]{2,1,0:T(8,128)(2,1)}), bf16[8,64,1024]{2,1,0:T(8,128)(2,1)}, u32[]{:S(2)}, u32[]{:S(2)}) async-start(bf16[8,64,1024]{2,1,0:T(8,128)(2,1)} %copy-done.13), calls=%async_computation.3 | async-start | bytes 2097152 | tf_op jit(solution)/shard_map/all_to_all | solution.py:38
  159.3 1.0 copy-done.18
  161.2 2.5 %shard_map.119 = bf16[256,2048]{1,0:T(8,128)(2,1)} custom-call(s32[4]{0:T(128)S(1)} %pad_add_fusion.pos_ref, bf16[512,256]{1,0:T(8,128)(2,1)S(1)} %fusion.12.disp, bf16[512,2176]{1,0:T(8,128)(2,1)S(1)} %bitcast.29, bf16[256,128]{1,0:T(8,128)(2,1)S(1)} %copy-done.32, bf16[2048,128]{1,0:T(8,128)(2,1)S(1)} %copy-done.18), custom_call_target="tpu_custom_call" | custom-call | flops 1000 | bytes 1000 | tf_op jit(solution)/shard_map/pallas_call | solution.py:47
  163.7 2.0 %collective-permute-start.13 = (f32[8,2048]{1,0:T(8,128)S(1)}, f32[8,2048]{1,0:T(8,128)S(1)}, u32[]{:S(2)}, u32[]{:S(2)}) collective-permute-start(f32[8,2048]{1,0:T(8,128)S(1)} %copy-done.33), channel_id=1, source_target_pairs={{0,4},{2,6},{4,0},{6,2},{1,5},{3,7},{5,1},{7,3},{8,12},{10,14},{12... | collective-permute-start | bytes 196616 | tf_op jit(solution)/shard_map/ppermute | solution.py:34
  165.6 1.0 collective-permute-start.12
  166.6 1.7 collective-permute-start.11
  168.4 1.4 collective-permute-done.13
  169.8 1.3 collective-permute-done.12
  171.1 1.2 collective-permute-start.16
  172.3 2.2 %collective-permute-start.15 = (f32[8,2048]{1,0:T(8,128)S(1)}, f32[8,2048]{1,0:T(8,128)S(1)}, u32[]{:S(2)}, u32[]{:S(2)}) collective-permute-start(f32[8,2048]{1,0:T(8,128)S(1)} %add_add_fusion.2), channel_id=1, source_target_pairs={{0,192},{64,128},{128,64},{192,0},{1,193},{65,129},{129,65},{193,1... | collective-permute-start | bytes 196616 | tf_op jit(solution)/shard_map/ppermute | solution.py:34
  174.7 2.3 %collective-permute-done.16 = f32[8,2048]{1,0:T(8,128)S(1)} collective-permute-done((f32[8,2048]{1,0:T(8,128)S(1)}, f32[8,2048]{1,0:T(8,128)S(1)}, u32[]{:S(2)}, u32[]{:S(2)}) %collective-permute-start.16) | collective-permute-done | bytes 65568 | tf_op jit(solution)/shard_map/ppermute | solution.py:34
  177.0 1.2 collective-permute-done.15
  178.8 1.6 collective-permute-start.18
  180.9 5.8 %collective-permute-done.19 = f32[8,2048]{1,0:T(8,128)S(1)} collective-permute-done((f32[8,2048]{1,0:T(8,128)S(1)}, f32[8,2048]{1,0:T(8,128)S(1)}, u32[]{:S(2)}, u32[]{:S(2)}) %collective-permute-start.19) | collective-permute-done | bytes 65568 | tf_op jit(solution)/shard_map/ppermute | solution.py:34
  186.8 1.4 collective-permute-done.17
  189.1 2.1 %shard_map.120 = (f32[32,2048]{1,0:T(8,128)}, f32[64,1024]{1,0:T(8,128)}) custom-call(s32[4]{0:T(128)S(1)} %pad_add_fusion.pos_ref, bf16[8,64,1024]{2,1,0:T(8,128)(2,1)} %all-to-all-done.3.got), custom_call_target="tpu_custom_call" | custom-call | flops 1000 | bytes 1000 | tf_op jit(solution)/shard_map/pallas_call | solution.py:47
  (106 shorter events, 11.2 us)
Async XLA Ops:
  0.6 14.9 %copy-start = (bf16[256,2048]{1,0:T(8,128)(2,1)S(1)}, bf16[256,2048]{1,0:T(8,128)(2,1)}, u32[]{:S(2)}) copy-start(bf16[256,2048]{1,0:T(8,128)(2,1)} %param.9) | copy-start | bytes 3145732
  1.5 4.1 %copy-start.38 = (pred[256]{0:T(512)(128)(4,1)}, pred[256]{0:T(512)(128)(4,1)S(1)}, u32[]{:S(2)}) copy-start(pred[256]{0:T(512)(128)(4,1)S(1)} %get-tuple-element.122) | copy-start | bytes 772
  1.5 4.1 %copy-start.39 = (pred[256]{0:T(512)(128)(4,1)}, pred[256]{0:T(512)(128)(4,1)S(1)}, u32[]{:S(2)}) copy-start(pred[256]{0:T(512)(128)(4,1)S(1)} %get-tuple-element.123) | copy-start | bytes 772
  5.5 6.4 %copy-start.35 = (s32[256,2]{0,1:T(2,128)S(1)}, s32[256,2]{0,1:T(2,128)}, u32[]{:S(2)}) copy-start(s32[256,2]{0,1:T(2,128)} %param.15) | copy-start | bytes 6148
  5.5 6.4 %copy-start.34 = (bf16[2048,8]{0,1:T(8,128)(2,1)S(1)}, bf16[2048,8]{0,1:T(8,128)(2,1)}, u32[]{:S(2)}) copy-start(bf16[2048,8]{0,1:T(8,128)(2,1)} %param.10) | copy-start | bytes 98308
  5.5 8.3 %copy-start.36 = (s32[256,2]{0,1:T(2,128)S(1)}, s32[256,2]{0,1:T(2,128)}, u32[]{:S(2)}) copy-start(s32[256,2]{0,1:T(2,128)} %param.13) | copy-start | bytes 6148
  5.6 31.5 %all-to-all-start.1 = ((bf16[8,64,2048]{2,1,0:T(8,128)(2,1)}), bf16[8,64,2048]{2,1,0:T(8,128)(2,1)S(1)}, u32[]{:S(2)}, u32[]{:S(2)}) async-start(bf16[8,64,2048]{2,1,0:T(8,128)(2,1)} %bitcast.38), calls=%async_computation.1 | async-start | bytes 4194304 | tf_op jit(solution)/shard_map/all_to_all | solution.py:38
  13.9 0.6 copy-start.37
  37.1 1.4 copy-start.1
  38.5 31.3 %all-to-all-start = ((bf16[8,64,2176]{2,1,0:T(8,128)(2,1)}), bf16[8,64,2176]{2,1,0:T(8,128)(2,1)S(1)}, u32[]{:S(2)}, u32[]{:S(2)}) async-start(bf16[8,64,2176]{2,1,0:T(8,128)(2,1)} %bitcast.37), calls=%async_computation | async-start | bytes 4456448 | tf_op jit(solution)/shard_map/all_to_all | solution.py:38
  43.7 26.0 %collective-permute-start = (bf16[512,2048]{1,0:T(8,128)(2,1)}, bf16[512,2048]{1,0:T(8,128)(2,1)}, u32[]{:S(2)}, u32[]{:S(2)}) collective-permute-start(bf16[512,2048]{1,0:T(8,128)(2,1)} %bitcast.30), channel_id=1, source_target_pairs={{0,8},{8,0},{1,9},{9,1},{2,10},{10,2},{3,11},{11,3},{4,12},{12,4},... | collective-permute-start | bytes 6291464 | tf_op jit(solution)/shard_map/ppermute | solution.py:34
  51.2 18.5 %collective-permute-start.1 = (bf16[512,1024]{1,0:T(8,128)(2,1)}, bf16[512,1024]{1,0:T(8,128)(2,1)}, u32[]{:S(2)}, u32[]{:S(2)}) collective-permute-start(bf16[512,1024]{1,0:T(8,128)(2,1)} %get-tuple-element.78.act_ref.refs_4_.refs_0_), channel_id=1, source_target_pairs={{0,8},{8,0},{1,9},{9,1},{2,10},{10,2},{3,11},{11,3},{4,12},{12,4},... | collective-permute-start | bytes 3145736 | tf_op jit(solution)/shard_map/ppermute | solution.py:34
  69.7 2.7 %copy-start.15 = (f32[512,1024]{1,0:T(8,128)S(1)}, f32[512,1024]{1,0:T(8,128)}, u32[]{:S(2)}) copy-start(f32[512,1024]{1,0:T(8,128)} %get-tuple-element.67.slope_ref) | copy-start | bytes 6291460
  72.3 11.9 %copy-start.8 = (bf16[512,1024]{1,0:T(8,128)(2,1)}, bf16[512,1024]{1,0:T(8,128)(2,1)S(1)}, u32[]{:S(2)}) copy-start(bf16[512,1024]{1,0:T(8,128)(2,1)S(1)} %get-tuple-element.80.refs_0_.refs_2_) | copy-start | bytes 3145732
  72.3 11.8 %collective-permute-start.2 = (bf16[512,1024]{1,0:T(8,128)(2,1)S(1)}, bf16[512,1024]{1,0:T(8,128)(2,1)S(1)}, u32[]{:S(2)}, u32[]{:S(2)}) collective-permute-start(bf16[512,1024]{1,0:T(8,128)(2,1)S(1)} %get-tuple-element.64), channel_id=1, source_target_pairs={{0,8},{8,0},{1,9},{9,1},{2,10},{10,2},{3,11},{11,3},{4,12},{12,4},... | collective-permute-start | bytes 3145736 | tf_op jit(solution)/shard_map/ppermute | solution.py:34
  72.4 2.5 %copy-start.12 = (bf16[1,1024,2048]{2,1,0:T(8,128)(2,1)S(1)}, bf16[1,1024,2048]{2,1,0:T(8,128)(2,1)}, u32[]{:S(2)}) copy-start(bf16[1,1024,2048]{2,1,0:T(8,128)(2,1)} %param.12) | copy-start | bytes 12582916
  74.8 9.3 %copy-start.2 = (bf16[8,64,2048]{2,1,0:T(8,128)(2,1)S(1)}, bf16[8,64,2048]{2,1,0:T(8,128)(2,1)}, u32[]{:S(2)}) copy-start(bf16[8,64,2048]{2,1,0:T(8,128)(2,1)} %copy-done.1) | copy-start | bytes 6291460
  81.9 12.5 %copy-start.4 = (bf16[512,1024]{1,0:T(8,128)(2,1)}, bf16[512,1024]{1,0:T(8,128)(2,1)S(1)}, u32[]{:S(2)}) copy-start(bf16[512,1024]{1,0:T(8,128)(2,1)S(1)} %get-tuple-element.84.refs_2_.grad.refs_6_) | copy-start | bytes 3145732
  81.9 2.2 %collective-permute-start.3 = (bf16[512,512]{1,0:T(8,128)(2,1)S(1)}, bf16[512,512]{1,0:T(8,128)(2,1)S(1)}, u32[]{:S(2)}, u32[]{:S(2)}) collective-permute-start(bf16[512,512]{1,0:T(8,128)(2,1)S(1)} %get-tuple-element.70), channel_id=1, source_target_pairs={{0,8},{8,0},{1,9},{9,1},{2,10},{10,2},{3,11},{11,3},{4,12},{12,4},... | collective-permute-start | bytes 1572872 | tf_op jit(solution)/shard_map/ppermute | solution.py:34
  84.1 6.5 %copy-start.16 = (bf16[512,512]{1,0:T(8,128)(2,1)}, bf16[512,512]{1,0:T(8,128)(2,1)S(1)}, u32[]{:S(2)}) copy-start(bf16[512,512]{1,0:T(8,128)(2,1)S(1)} %collective-permute-done.3.refs_3_.refs_7_) | copy-start | bytes 1572868
  84.1 6.5 %copy-start.10 = (bf16[512,1024]{1,0:T(8,128)(2,1)}, bf16[512,1024]{1,0:T(8,128)(2,1)S(1)}, u32[]{:S(2)}) copy-start(bf16[512,1024]{1,0:T(8,128)(2,1)S(1)} %collective-permute-done.2.refs_1_.refs_3_) | copy-start | bytes 3145732
  84.1 10.3 %copy-start.14 = (bf16[1,2048,1024]{2,1,0:T(8,128)(2,1)S(1)}, bf16[1,2048,1024]{2,1,0:T(8,128)(2,1)}, u32[]{:S(2)}) copy-start(bf16[1,2048,1024]{2,1,0:T(8,128)(2,1)} %param.11) | copy-start | bytes 12582916
  90.6 25.7 %collective-permute-start.4 = (bf16[1024,512]{1,0:T(8,128)(2,1)}, bf16[1024,512]{1,0:T(8,128)(2,1)}, u32[]{:S(2)}, u32[]{:S(2)}) collective-permute-start(bf16[1024,512]{1,0:T(8,128)(2,1)} %get-tuple-element.74), channel_id=1, source_target_pairs={{0,64},{64,0},{128,192},{192,128},{1,65},{65,1},{129,193},{193,129... | collective-permute-start | bytes 3145736 | tf_op jit(solution)/shard_map/ppermute | solution.py:34
  92.3 26.5 %collective-permute-start.5 = (bf16[1024,512]{1,0:T(8,128)(2,1)}, bf16[1024,512]{1,0:T(8,128)(2,1)}, u32[]{:S(2)}, u32[]{:S(2)}) collective-permute-start(bf16[1024,512]{1,0:T(8,128)(2,1)} %get-tuple-element.75), channel_id=1, source_target_pairs={{0,192},{64,128},{128,64},{192,0},{1,193},{65,129},{129,65},{193,1... | collective-permute-start | bytes 3145736 | tf_op jit(solution)/shard_map/ppermute | solution.py:34
  97.4 1.4 copy-start.7
  98.8 32.0 %all-to-all-start.2 = ((bf16[8,64,2176]{2,1,0:T(8,128)(2,1)}), bf16[8,64,2176]{2,1,0:T(8,128)(2,1)S(1)}, u32[]{:S(2)}, u32[]{:S(2)}) async-start(bf16[8,64,2176]{2,1,0:T(8,128)(2,1)} %bitcast.34), calls=%async_computation.2 | async-start | bytes 4456448 | tf_op jit(solution)/shard_map/all_to_all | solution.py:38
  104.0 1.6 copy-start.3
  105.6 1.2 copy-start.5
  106.9 1.2 copy-start.9
  108.1 1.2 copy-start.11
  109.3 1.0 copy-start.17
  115.0 6.4 %copy-start.19 = (f32[256,512]{1,0:T(8,128)}, f32[256,512]{1,0:T(8,128)S(1)}, u32[]{:S(2)}) copy-start(f32[256,512]{1,0:T(8,128)S(1)} %get-tuple-element.105.out_a) | copy-start | bytes 1572868
  115.0 6.4 %copy-start.21 = (f32[256,512]{1,0:T(8,128)}, f32[256,512]{1,0:T(8,128)S(1)}, u32[]{:S(2)}) copy-start(f32[256,512]{1,0:T(8,128)S(1)} %get-tuple-element.106.out_b) | copy-start | bytes 1572868
  115.0 6.4 %copy-start.23 = (f32[512,256]{1,0:T(8,128)}, f32[512,256]{1,0:T(8,128)S(1)}, u32[]{:S(2)}) copy-start(f32[512,256]{1,0:T(8,128)S(1)} %get-tuple-element.107.in_a) | copy-start | bytes 1572868
  115.0 6.4 %copy-start.25 = (f32[512,256]{1,0:T(8,128)}, f32[512,256]{1,0:T(8,128)S(1)}, u32[]{:S(2)}) copy-start(f32[512,256]{1,0:T(8,128)S(1)} %get-tuple-element.108.in_b) | copy-start | bytes 1572868
  121.5 29.8 %collective-permute-start.7 = (bf16[512,512]{1,0:T(8,128)(2,1)}, bf16[512,512]{1,0:T(8,128)(2,1)}, u32[]{:S(2)}, u32[]{:S(2)}) collective-permute-start(bf16[512,512]{1,0:T(8,128)(2,1)} %get-tuple-element.98), channel_id=1, source_target_pairs={{0,64},{64,0},{128,192},{192,128},{1,65},{65,1},{129,193},{193,129... | collective-permute-start | bytes 1572872 | tf_op jit(solution)/shard_map/ppermute | solution.py:34
  121.6 29.7 %collective-permute-start.6 = (bf16[512,512]{1,0:T(8,128)(2,1)}, bf16[512,512]{1,0:T(8,128)(2,1)}, u32[]{:S(2)}, u32[]{:S(2)}) collective-permute-start(bf16[512,512]{1,0:T(8,128)(2,1)} %get-tuple-element.92), channel_id=1, source_target_pairs={{0,192},{64,128},{128,64},{192,0},{1,193},{65,129},{129,65},{193,1... | collective-permute-start | bytes 1572872 | tf_op jit(solution)/shard_map/ppermute | solution.py:34
  130.8 1.2 copy-start.6
  132.0 0.9 copy-start.27
  132.9 0.9 copy-start.28
  133.8 0.9 copy-start.29
  134.7 0.9 copy-start.30
  135.6 15.7 %copy-start.20 = (f32[256,512]{1,0:T(8,128)S(1)}, f32[256,512]{1,0:T(8,128)}, u32[]{:S(2)}) copy-start(f32[256,512]{1,0:T(8,128)} %copy-done.19) | copy-start | bytes 1572868
  135.6 15.7 %copy-start.22 = (f32[256,512]{1,0:T(8,128)S(1)}, f32[256,512]{1,0:T(8,128)}, u32[]{:S(2)}) copy-start(f32[256,512]{1,0:T(8,128)} %copy-done.21) | copy-start | bytes 1572868
  135.6 15.7 %copy-start.24 = (f32[512,256]{1,0:T(8,128)S(1)}, f32[512,256]{1,0:T(8,128)}, u32[]{:S(2)}) copy-start(f32[512,256]{1,0:T(8,128)} %copy-done.23) | copy-start | bytes 1572868
  135.6 15.7 %copy-start.26 = (f32[512,256]{1,0:T(8,128)S(1)}, f32[512,256]{1,0:T(8,128)}, u32[]{:S(2)}) copy-start(f32[512,256]{1,0:T(8,128)} %copy-done.25) | copy-start | bytes 1572868
  136.9 14.4 %copy-start.31 = (bf16[256,128]{1,0:T(8,128)(2,1)}, bf16[256,128]{1,0:T(8,128)(2,1)S(1)}, u32[]{:S(2)}) copy-start(bf16[256,128]{1,0:T(8,128)(2,1)S(1)} %get-tuple-element.112.logit) | copy-start | bytes 196612
  136.9 8.9 %collective-permute-start.10 = (f32[8,2048]{1,0:T(8,128)S(1)}, f32[8,2048]{1,0:T(8,128)S(1)}, u32[]{:S(2)}, u32[]{:S(2)}) collective-permute-start(f32[8,2048]{1,0:T(8,128)S(1)} %get-tuple-element.103), channel_id=1, source_target_pairs={{0,32},{16,48},{32,0},{48,16},{1,33},{17,49},{33,1},{49,17},{2,34}... | collective-permute-start | bytes 196616 | tf_op jit(solution)/shard_map/ppermute | solution.py:34
  143.3 6.5 %collective-permute-start.9 = (f32[8,2048]{1,0:T(8,128)S(1)}, f32[8,2048]{1,0:T(8,128)S(1)}, u32[]{:S(2)}, u32[]{:S(2)}) collective-permute-start(f32[8,2048]{1,0:T(8,128)S(1)} %get-tuple-element.103), channel_id=1, source_target_pairs={{0,48},{16,32},{32,16},{48,0},{1,49},{17,33},{33,17},{49,1},{2,50}... | collective-permute-start | bytes 196616 | tf_op jit(solution)/shard_map/ppermute | solution.py:34
  143.8 6.8 %collective-permute-start.8 = (f32[8,2048]{1,0:T(8,128)S(1)}, f32[8,2048]{1,0:T(8,128)S(1)}, u32[]{:S(2)}, u32[]{:S(2)}) collective-permute-start(f32[8,2048]{1,0:T(8,128)S(1)} %get-tuple-element.103), channel_id=1, source_target_pairs={{0,16},{16,0},{32,48},{48,32},{1,17},{17,1},{33,49},{49,33},{2,18}... | collective-permute-start | bytes 196616 | tf_op jit(solution)/shard_map/ppermute | solution.py:34
  153.5 1.0 copy-start.13
  154.5 34.6 %all-to-all-start.3 = ((bf16[8,64,1024]{2,1,0:T(8,128)(2,1)}), bf16[8,64,1024]{2,1,0:T(8,128)(2,1)}, u32[]{:S(2)}, u32[]{:S(2)}) async-start(bf16[8,64,1024]{2,1,0:T(8,128)(2,1)} %copy-done.13), calls=%async_computation.3 | async-start | bytes 2097152 | tf_op jit(solution)/shard_map/all_to_all | solution.py:38
  159.3 1.0 copy-start.18
  160.3 0.8 copy-start.32
  161.2 2.5 %copy-start.33 = (f32[8,2048]{1,0:T(8,128)S(1)}, f32[8,2048]{1,0:T(8,128)}, u32[]{:S(2)}) copy-start(f32[8,2048]{1,0:T(8,128)} %add_add_fusion.3) | copy-start | bytes 196612
  163.7 6.1 %collective-permute-start.13 = (f32[8,2048]{1,0:T(8,128)S(1)}, f32[8,2048]{1,0:T(8,128)S(1)}, u32[]{:S(2)}, u32[]{:S(2)}) collective-permute-start(f32[8,2048]{1,0:T(8,128)S(1)} %copy-done.33), channel_id=1, source_target_pairs={{0,4},{2,6},{4,0},{6,2},{1,5},{3,7},{5,1},{7,3},{8,12},{10,14},{12... | collective-permute-start | bytes 196616 | tf_op jit(solution)/shard_map/ppermute | solution.py:34
  165.6 5.5 %collective-permute-start.12 = (f32[8,2048]{1,0:T(8,128)S(1)}, f32[8,2048]{1,0:T(8,128)S(1)}, u32[]{:S(2)}, u32[]{:S(2)}) collective-permute-start(f32[8,2048]{1,0:T(8,128)S(1)} %copy-done.33), channel_id=1, source_target_pairs={{0,6},{2,4},{4,2},{6,0},{1,7},{3,5},{5,3},{7,1},{8,14},{10,12},{12... | collective-permute-start | bytes 196616 | tf_op jit(solution)/shard_map/ppermute | solution.py:34
  166.6 4.5 %collective-permute-start.11 = (f32[8,2048]{1,0:T(8,128)S(1)}, f32[8,2048]{1,0:T(8,128)S(1)}, u32[]{:S(2)}, u32[]{:S(2)}) collective-permute-start(f32[8,2048]{1,0:T(8,128)S(1)} %copy-done.33), channel_id=1, source_target_pairs={{0,2},{2,0},{4,6},{6,4},{1,3},{3,1},{5,7},{7,5},{8,10},{10,8},{12,... | collective-permute-start | bytes 196616 | tf_op jit(solution)/shard_map/ppermute | solution.py:34
  171.1 5.9 %collective-permute-start.16 = (f32[8,2048]{1,0:T(8,128)S(1)}, f32[8,2048]{1,0:T(8,128)S(1)}, u32[]{:S(2)}, u32[]{:S(2)}) collective-permute-start(f32[8,2048]{1,0:T(8,128)S(1)} %add_add_fusion.2), channel_id=1, source_target_pairs={{0,128},{64,192},{128,0},{192,64},{1,129},{65,193},{129,1},{193,65... | collective-permute-start | bytes 196616 | tf_op jit(solution)/shard_map/ppermute | solution.py:34
  172.3 6.0 %collective-permute-start.15 = (f32[8,2048]{1,0:T(8,128)S(1)}, f32[8,2048]{1,0:T(8,128)S(1)}, u32[]{:S(2)}, u32[]{:S(2)}) collective-permute-start(f32[8,2048]{1,0:T(8,128)S(1)} %add_add_fusion.2), channel_id=1, source_target_pairs={{0,192},{64,128},{128,64},{192,0},{1,193},{65,129},{129,65},{193,1... | collective-permute-start | bytes 196616 | tf_op jit(solution)/shard_map/ppermute | solution.py:34
  174.4 4.3 %collective-permute-start.14 = (f32[8,2048]{1,0:T(8,128)S(1)}, f32[8,2048]{1,0:T(8,128)S(1)}, u32[]{:S(2)}, u32[]{:S(2)}) collective-permute-start(f32[8,2048]{1,0:T(8,128)S(1)} %add_add_fusion.2), channel_id=1, source_target_pairs={{0,64},{64,0},{128,192},{192,128},{1,65},{65,1},{129,193},{193,129... | collective-permute-start | bytes 196616 | tf_op jit(solution)/shard_map/ppermute | solution.py:34
  178.7 8.1 %collective-permute-start.19 = (f32[8,2048]{1,0:T(8,128)S(1)}, f32[8,2048]{1,0:T(8,128)S(1)}, u32[]{:S(2)}, u32[]{:S(2)}) collective-permute-start(f32[8,2048]{1,0:T(8,128)S(1)} %add_add_fusion.1), channel_id=1, source_target_pairs={{0,9},{1,8},{8,1},{9,0},{2,11},{3,10},{10,3},{11,2},{4,13},{5,12},... | collective-permute-start | bytes 196616 | tf_op jit(solution)/shard_map/ppermute | solution.py:34
  178.8 8.0 %collective-permute-start.18 = (f32[8,2048]{1,0:T(8,128)S(1)}, f32[8,2048]{1,0:T(8,128)S(1)}, u32[]{:S(2)}, u32[]{:S(2)}) collective-permute-start(f32[8,2048]{1,0:T(8,128)S(1)} %add_add_fusion.1), channel_id=1, source_target_pairs={{0,8},{1,9},{8,0},{9,1},{2,10},{3,11},{10,2},{11,3},{4,12},{5,13},... | collective-permute-start | bytes 196616 | tf_op jit(solution)/shard_map/ppermute | solution.py:34
  180.4 7.8 %collective-permute-start.17 = (f32[8,2048]{1,0:T(8,128)S(1)}, f32[8,2048]{1,0:T(8,128)S(1)}, u32[]{:S(2)}, u32[]{:S(2)}) collective-permute-start(f32[8,2048]{1,0:T(8,128)S(1)} %add_add_fusion.1), channel_id=1, source_target_pairs={{0,1},{1,0},{8,9},{9,8},{2,3},{3,2},{10,11},{11,10},{4,5},{5,4},{1... | collective-permute-start | bytes 196616 | tf_op jit(solution)/shard_map/ppermute | solution.py:34

commit v9 on v7

--- a/solution.py
+++ b/solution.py
@@ -9,9 +9,8 @@
 FINE_SHAPE = (4, 4, 2, 4, 2)
 GROUP = ("x", "zl")
 EXTRA = 128
-VMEM_LIMIT = 16 * 1024 * 1024
-COST_SLOTS = 1000
-LONG = 26_000_000_000
+VMEM_LIMIT = 20 * 1024 * 1024
+LONG = 30_000_000_000
 F32 = jnp.float32
 BF16 = jnp.bfloat16
 
@@ -49,7 +48,7 @@
         body,
         in_specs=[pl.BlockSpec(memory_space=pltpu.SMEM)]
         + [vmem] * len(inputs)
-        + [pl.BlockSpec(memory_space=pl.ANY)] * len(far),
+        + [pl.BlockSpec(memory_space=pltpu.HBM)] * len(far),
         out_specs=[vmem] * len(outputs),
         out_shape=[jax.ShapeDtypeStruct(shape, dtype) for shape, dtype in outputs],
         scratch_shapes=scratch,
@@ -85,32 +84,17 @@
     hidden, width = weight_out.shape
     step = hidden // 4
 
-    def body(pos_ref, rec, weight, act_ref, slope_ref, grad_pre, give, gate_grad, w, a, g, sems):
-        copies = []
-        for i in range(4):
-            at = slice(i * step, (i + 1) * step)
-            moves = (
-                (weight.at[at, :], w.at[at, :]),
-                (act_ref.at[:, at], a.at[i]),
-                (slope_ref.at[:, at], g.at[i]),
-            )
-            copies.append(
-                [pltpu.make_async_copy(x, y, sems.at[i, k]) for k, (x, y) in enumerate(moves)]
-            )
-            for copy in copies[i]:
-                copy.start()
+    def body(pos_ref, rec, weight, act_ref, slope_ref, grad_pre, give, gate_grad):
         gate = gate_of(pos_ref, rec[:, width:])
         total = None
         for i in range(4):
             at = slice(i * step, (i + 1) * step)
-            for copy in copies[i]:
-                copy.wait()
             grad_act = lax.dot_general(
-                rec[:, :width], w[at, :], (((1,), (1,)), ((), ())), preferred_element_type=F32
+                rec[:, :width], weight[at, :], (((1,), (1,)), ((), ())), preferred_element_type=F32
             )
-            part = jnp.sum(a[i].astype(F32) * grad_act, axis=1, keepdims=True)
+            part = jnp.sum(act_ref[:, at].astype(F32) * grad_act, axis=1, keepdims=True)
             total = part if total is None else total + part
-            grad_pre[:, at] = (gate * grad_act * g[i]).astype(BF16)
+            grad_pre[:, at] = (gate * grad_act * slope_ref[:, at]).astype(BF16)
         start = pl.multiple_of((1 - pos_ref[1]) * (hidden // 2), hidden // 2)
         give[...] = grad_pre[:, pl.ds(start, hidden // 2)]
         lane = lax.broadcasted_iota(jnp.int32, (slots, EXTRA), 1)
@@ -119,119 +103,131 @@
     return call(
         body,
         pos,
-        [received],
+        [received, weight_out, act, slope],
         [((slots, hidden), BF16), ((slots, hidden // 2), BF16), ((slots, EXTRA), BF16)],
-        far=[weight_out, act, slope],
-        scratch=[
-            pltpu.VMEM((hidden, width), BF16),
-            pltpu.VMEM((4, slots, step), BF16),
-            pltpu.VMEM((4, slots, step), F32),
-            pltpu.SemaphoreType.DMA((4, 3)),
-        ],
-    )
-
-
-def row_products(pos_ref, refs, own_offset, masks, width, cols):
-    lm, lo, rm, ro = refs
-    dims = (((0,), (0,)), ((), ()))
-    for i in range(2):
-        own = pl.multiple_of((own_offset * pos_ref[1] + i) * cols, cols)
-        for j in range(2):
-            start = pl.multiple_of((pos_ref[0] ^ masks[i][j]) * width, width)
-            value = lax.dot_general(
-                lm[:, pl.ds(start, width)],
-                rm[:, pl.ds(own, cols)],
-                dims,
-                preferred_element_type=F32,
-            )
-            value = value + lax.dot_general(
-                lo[:, pl.ds(start, width)],
-                ro[:, i * cols : (i + 1) * cols],
-                dims,
-                preferred_element_type=F32,
-            )
-            yield i, j, value
-
-
-def sent_parts(pos, left_out, right_out, left_in, right_in):
+    )
+
+
+def products(pos, left_out, right_out, left_in, right_in, masks, store, outputs, near):
     slots = left_in[0].shape[0]
-    width_out, width_in = left_out[0].shape[1] // 4, left_in[0].shape[1] // 4
-    cols_out, cols_in = right_out[1].shape[1] // 2, right_in[1].shape[1] // 2
-    masks = ((1, 2), (3, 2))
+    widths = left_out[0].shape[1] // 4, left_in[0].shape[1] // 4
+    cols = right_out[1].shape[1] // 2, right_in[1].shape[1] // 2
+    blocks = sorted({r for pair in masks for r in pair})
 
     def body(pos_ref, *refs):
-        out_refs, right_refs = refs[:4], refs[4:6]
-        lefts, outs, (buffer, sems) = refs[6:8], refs[8:10], refs[10:]
+        count = len(outputs)
+        refs = list(refs)
+        scratch = refs[8 + count :]
+        outs = refs[8 : 8 + count]
+        rights, lefts = (refs[:4], refs[4:8]) if near else (refs[4:8], refs[:4])
+        buffers, sems = scratch[:2], scratch[2]
+        held = scratch[3:7]
         copies = []
-        for k in range(2):
-            for r in (1, 2, 3):
-                start = pl.multiple_of((pos_ref[0] ^ r) * width_in, width_in)
-                copy = pltpu.make_async_copy(
-                    lefts[k].at[:, pl.ds(start, width_in)], buffer.at[k, r - 1], sems.at[k, r - 1]
-                )
-                copy.start()
-                copies.append(copy)
-        for i, j, value in row_products(pos_ref, out_refs, 0, masks, width_out, cols_out):
-            outs[i][j * width_out : (j + 1) * width_out, :] = value.astype(BF16)
+        for part in range(2):
+            width = widths[part]
+            for k in range(2):
+                for n, r in enumerate(blocks):
+                    start = pl.multiple_of((pos_ref[0] ^ r) * width, width)
+                    copies.append(
+                        pltpu.make_async_copy(
+                            lefts[2 * part + k].at[:, pl.ds(start, width)],
+                            buffers[part].at[k, n],
+                            sems.at[2 * part + k, n],
+                        )
+                    )
+            if not near:
+                for k in range(2):
+                    source = rights[2 * part + k]
+                    if part == 1 and k == 0:
+                        start = pl.multiple_of(pos_ref[1] * 2 * cols[1], 2 * cols[1])
+                        source = source.at[:, pl.ds(start, 2 * cols[1])]
+                    copies.append(
+                        pltpu.make_async_copy(
+                            source, held[2 * part + k], sems.at[2 * part + k, len(blocks)]
+                        )
+                    )
         for copy in copies:
-            copy.wait()
+            copy.start()
         dims = (((0,), (0,)), ((), ()))
-        for i in range(2):
-            own = pl.multiple_of((2 * pos_ref[1] + i) * cols_in, cols_in)
-            for j in range(2):
-                r = masks[i][j] - 1
-                value = lax.dot_general(
-                    buffer[0, r],
-                    right_refs[0][:, pl.ds(own, cols_in)],
-                    dims,
-                    preferred_element_type=F32,
-                )
-                value = value + lax.dot_general(
-                    buffer[1, r],
-                    right_refs[1][:, i * cols_in : (i + 1) * cols_in],
-                    dims,
-                    preferred_element_type=F32,
-                )
-                outs[i][2 * width_out :, j * cols_in : (j + 1) * cols_in] = value.astype(BF16)
-
+        for part in range(2):
+            each = len(copies) // 2
+            for copy in copies[part * each : (part + 1) * each]:
+                copy.wait()
+            wide = cols[part]
+            mine, other = (rights if near else held)[2 * part : 2 * part + 2]
+            for i in range(2):
+                own = i * wide
+                if part and near:
+                    own = pl.multiple_of((2 * pos_ref[1] + i) * wide, wide)
+                for j in range(2):
+                    n = blocks.index(masks[i][j])
+                    value = lax.dot_general(
+                        buffers[part][0, n],
+                        mine[:, pl.ds(own, wide)],
+                        dims,
+                        preferred_element_type=F32,
+                    )
+                    value = value + lax.dot_general(
+                        buffers[part][1, n],
+                        other[:, i * wide : (i + 1) * wide],
+                        dims,
+                        preferred_element_type=F32,
+                    )
+                    store(outs, part, i, j, value)
+
+    rights = [*right_out, *right_in]
+    lefts = [*left_out, *left_in]
+    scratch = [pltpu.VMEM((2, len(blocks), slots, width), BF16) for width in widths]
+    scratch.append(pltpu.SemaphoreType.DMA((4, len(blocks) + 1)))
+    if not near:
+        scratch += [pltpu.VMEM((slots, 2 * cols[k // 2]), BF16) for k in range(4)]
     return call(
         body,
         pos,
-        [*left_out, *right_out, *right_in],
-        [((2 * width_out + width_in, cols_out), BF16)] * 2,
-        far=[*left_in],
-        scratch=[pltpu.VMEM((2, 3, slots, width_in), BF16), pltpu.SemaphoreType.DMA((2, 3))],
-    )
+        rights if near else [],
+        outputs,
+        far=lefts if near else lefts + rights,
+        scratch=scratch,
+    )
+
+
+def sent_parts(pos, left_out, right_out, left_in, right_in):
+    width_out, width_in = left_out[0].shape[1] // 4, left_in[0].shape[1] // 4
+    cols_out, cols_in = right_out[1].shape[1] // 2, right_in[1].shape[1] // 2
+
+    def store(outs, part, i, j, value):
+        if part:
+            outs[i][2 * width_out :, j * cols_in : (j + 1) * cols_in] = value.astype(BF16)
+        else:
+            outs[i][j * width_out : (j + 1) * width_out, :] = value.astype(BF16)
+
+    outputs = [((2 * width_out + width_in, cols_out), BF16)] * 2
+    sides = (left_out, right_out, left_in, right_in)
+    return products(pos, *sides, ((1, 2), (3, 2)), store, outputs, True)
 
 
 def kept_parts(pos, left_out, right_out, left_in, right_in):
     width_out, width_in = left_out[0].shape[1] // 4, left_in[0].shape[1] // 4
     cols_out, cols_in = right_out[1].shape[1] // 2, right_in[1].shape[1] // 2
-    masks = ((0, 3), (0, 1))
     half = width_in // 2
 
-    def body(pos_ref, *refs):
-        near_out, near_in, far = refs[8:10], refs[10:12], refs[12:14]
-        for i, j, value in row_products(pos_ref, refs[:4], 0, masks, width_out, cols_out):
-            if j == 0:
-                near_out[i][...] = value
-            else:
-                far[i][:width_out, :] = value
-        for i, j, value in row_products(pos_ref, refs[4:8], 2, masks, width_in, cols_in):
-            if j == 0:
-                near_in[i][...] = value
-            else:
-                far[i][width_out:, :cols_in] = value[:half, :]
-                far[i][width_out:, cols_in:] = value[half:, :]
-
-    return call(
-        body,
-        pos,
-        [*left_out, *right_out, *left_in, *right_in],
+    def store(outs, part, i, j, value):
+        near_out, near_in, far = outs[:2], outs[2:4], outs[4:]
+        if j == 0:
+            (near_in if part else near_out)[i][...] = value
+        elif part:
+            far[i][width_out:, :cols_in] = value[:half, :]
+            far[i][width_out:, cols_in:] = value[half:, :]
+        else:
+            far[i][:width_out, :] = value
+
+    outputs = (
         [((width_out, cols_out), F32)] * 2
         + [((width_in, cols_in), F32)] * 2
-        + [((width_out + half, cols_out), F32)] * 2,
-    )
+        + [((width_out + half, cols_out), F32)] * 2
+    )
+    sides = (left_out, right_out, left_in, right_in)
+    return products(pos, *sides, ((0, 3), (0, 1)), store, outputs, False)
 
 
 def far_sums(pos, far, got):
@@ -246,7 +242,7 @@
                 value = arrived[rows + k * half : rows + (k + 1) * half, wide:].astype(F32)
                 out[half:, at] = (mine[half:, at] + value).astype(BF16)
 
-    return call(body, pos, [*far, *got], [((rows, cols), BF16)] * 2, LONG)
+    return call(body, pos, [*far, *got], [((rows, cols), BF16)] * 2)
 
 
 def zh_pieces(pos, near_out, near_in, got, far, scale):
@@ -275,6 +271,7 @@
         pos,
         [*near_out, *near_in, *got, *far],
         [((8, share_out + share_in // 2, 2 * cols_out), BF16)],
+        LONG,
     )[0]
 
 
@@ -302,40 +299,58 @@
     width = weight_in.shape[0]
     step = width // 4
 
-    def body(pos_ref, grad, weight, out):
+    def body(pos_ref, grad, weight, out, held, sems):
+        copies = []
+        for i in range(4):
+            at = pl.ds(i * step, step)
+            copies.append(pltpu.make_async_copy(weight.at[at, :], held.at[at, :], sems.at[i]))
+            copies[i].start()
         for i in range(4):
             at = slice(i * step, (i + 1) * step)
+            copies[i].wait()
             out[:, at] = lax.dot_general(
-                grad[...], weight[at, :], (((1,), (1,)), ((), ())), preferred_element_type=F32
+                grad[...], held[at, :], (((1,), (1,)), ((), ())), preferred_element_type=F32
             ).astype(BF16)
 
-    return call(body, pos, [grad_pre, weight_in], [((slots, width), BF16)], COST_SLOTS)[0]
-
-
-def router_grads(pos, dispatch, gate_back, tokens, probs, combine, keep, denominator, scale):
+    return call(
+        body,
+        pos,
+        [grad_pre],
+        [((slots, width), BF16)],
+        far=[weight_in],
+        scratch=[pltpu.VMEM((width, hidden), BF16), pltpu.SemaphoreType.DMA((4,))],
+    )[0]
+
+
+def router_grads(pos, dispatch, gate_back, token_lanes, tokens, scale):
     rows, width = tokens.shape
     experts = 8
     step = width // 4
 
-    def body(pos_ref, disp, back, tok, p_ref, c_ref, k_ref, d_ref, logit, router):
+    def body(pos_ref, disp, back, side, tok, logit, router, held, sem):
+        copy = pltpu.make_async_copy(tok, held, sem)
+        copy.start()
         dims = (((0,), (0,)), ((), ()))
         combine_grad = lax.dot_general(disp[...], back[...], dims, preferred_element_type=F32)
-        weighted = jnp.sum(combine_grad * c_ref[...], axis=1, keepdims=True)
-        probs_grad = k_ref[...] * (combine_grad - weighted) / d_ref[...]
-        probs = p_ref[...]
+        probs, combine, keep, denominator = (side[k] for k in range(4))
+        weighted = jnp.sum(combine_grad * combine, axis=1, keepdims=True)
+        probs_grad = keep * (combine_grad - weighted) / denominator
         inner = jnp.sum(probs_grad * probs, axis=1, keepdims=True)
         logit_b = (probs * (probs_grad - inner)).astype(BF16)
         logit[...] = logit_b
+        copy.wait()
         for i in range(4):
             at = slice(i * step, (i + 1) * step)
-            part = lax.dot_general(logit_b, tok[:, at], dims, preferred_element_type=F32)
+            part = lax.dot_general(logit_b, held[:, at], dims, preferred_element_type=F32)
             router[:, at] = part[:experts] * scale
 
     return call(
         body,
         pos,
-        [dispatch, gate_back, tokens, probs, combine, keep, denominator],
+        [dispatch, gate_back, token_lanes],
         [((rows, EXTRA), BF16), ((experts, width), F32)],
+        far=[tokens],
+        scratch=[pltpu.VMEM((rows, width), BF16), pltpu.SemaphoreType.DMA],
     )
 
 
@@ -394,12 +409,20 @@
     def lanes(values, fill=0.0):
         return jnp.pad(values, ((0, 0), (0, EXTRA - experts)), constant_values=fill)
 
-    probs_lanes = lanes(router_probs)
-    combine_lanes = lanes(jnp.sum(jnp.where(picked, combine[:, :, None], 0.0), axis=1))
-    keep_lanes = lanes(jnp.sum(jnp.where(picked, keep_float[:, :, None], 0.0), axis=1))
-    denominator_lanes = jnp.broadcast_to(denominator[:, None], (tok_rows, EXTRA))
+    def per_expert(values):
+        return jnp.sum(jnp.where(picked, values[:, :, None], 0.0), axis=1)
+
+    combine_full = per_expert(combine)
+    token_lanes = jnp.stack(
+        [
+            lanes(router_probs),
+            lanes(combine_full),
+            lanes(per_expert(keep_float)),
+            lanes(jnp.broadcast_to(denominator[:, None], (tok_rows, experts)), 1.0),
+        ]
+    )
     weight_lanes = lanes(router_weight)
-    gate_lanes = combine_lanes.astype(BF16)
+    gate_lanes = lanes(combine_full.astype(BF16))
     send_grads = jnp.dot(dispatch, grad_out, preferred_element_type=F32).astype(BF16)
     send_gates = jnp.dot(dispatch, gate_lanes, preferred_element_type=F32).astype(BF16)
     received = exchange(
@@ -419,11 +442,9 @@
     pos = jnp.stack([my_y, core, lax.axis_index(GROUP), lax.axis_index("zh")]).astype(jnp.int32)
 
 
-    token_side = (dispatch, weight_lanes, probs_lanes, combine_lanes, keep_lanes, denominator_lanes)
-    received, left_in, left_out, act_slope, token_side = tie(
-        received, left_in, left_out, act_slope, token_side
-    )
-    dispatch, weight_lanes, probs_lanes, combine_lanes, keep_lanes, denominator_lanes = token_side
+    received, left_in, left_out, act_slope, dispatch, weight_lanes, token_lanes = tie(
+        received, left_in, left_out, act_slope, dispatch, weight_lanes, token_lanes
+    )
     my_out, give_out = scale_grads(pos, received)
     right_out = (my_out, swap(give_out, "core", 1))
     received, _ = tie(received, give_out)
@@ -434,11 +455,11 @@
 
     sent = sent_parts(pos, left_out, right_out, left_in, right_in)
     got = (swap(sent[0], "y", 1), swap(sent[1], "y", 3))
-    gate_grad, grad_pre, _ = tie(gate_grad, grad_pre, sent)
+    pre_for_slots, gate_grad, _ = tie(grad_pre, gate_grad, sent)
     gate_back = exchange(gate_grad.reshape(experts, capacity, EXTRA), GROUP).reshape(
         slot_count, EXTRA
     )
-    grad_slots = slot_grads_of(pos, grad_pre, weight_in)
+    grad_slots = slot_grads_of(pos, pre_for_slots, weight_in)
     grad_slots, gate_back = tie(grad_slots, gate_back)
     back = exchange(
         grad_slots.reshape(experts, capacity, model_width), GROUP
@@ -446,33 +467,23 @@
 
     gate_back, _ = tie(gate_back, grad_slots)
     logit_lanes, router_part = router_grads(
-        pos,
-        dispatch,
-        gate_back,
-        tokens,
-        probs_lanes,
-        combine_lanes,
-        keep_lanes,
-        denominator_lanes,
-        grad_scale,
-    )
-
-    def router_round(value, axes, one, two):
+        pos, dispatch, gate_back, token_lanes, tokens, grad_scale
+    )
+
+    def router_round(value, axes, one, two, *until):
         near, far, both = (swap(value, axes, mask) for mask in (one, two, one ^ two))
+        value, near, far, both, _ = tie(value, near, far, both, until)
         return (value + near) + (far + both)
 
     left_in, left_out, right_in, right_out, _ = tie(
         left_in, left_out, right_in, right_out, router_part
     )
     *near, far_a, far_b = kept_parts(pos, left_out, right_out, left_in, right_in)
-    router_part, _ = tie(router_part, far_a)
-    router_part = router_round(router_part, ("core", "zl"), 1, 2)
-    got, far_a, far_b, router_part = tie(got, far_a, far_b, router_part)
+    got, far_a, far_b = tie(got, far_a, far_b)
     far_a, far_b = far_sums(pos, (far_a, far_b), got)
     far = (swap(far_a, "y", 3), swap(far_b, "y", 1))
-
-    router_part, _ = tie(router_part, far_a)
-    router_part = router_round(router_part, "zh", 1, 3)
+    router_part = router_round(router_part, "zh", 1, 3, far_a)
+
     near, far, router_part = tie(near, far, router_part)
     pieces = zh_pieces(pos, near[:2], near[2:], got, far, grad_scale)
     got = exchange(pieces, ("zh", "core"))
@@ -482,6 +493,7 @@
     router_part, _ = tie(router_part, grad_tokens)
     router_part = router_round(router_part, "x", 1, 3)
     router_part = router_round(router_part, "y", 1, 3)
+    router_part = router_round(router_part, ("core", "zl"), 1, 2)
     got, router_part = tie(got, router_part)
     outer_share, inner_share = shares(pos, got, near[0].shape[0] // 8)
     return (grad_tokens, router_part.T, inner_share, outer_share)

time: 200 us -> 182 us (0.910)
  waiting for transfers between devices: 63.6 us -> 57.9 us
  Pallas kernels: 33.6 us -> 29.1 us
  starting transfers between devices: 55.1 us -> 50.9 us
  local copies, waits for them, and re-layouts: 25.5 us -> 22.4 us
    all_to_all x5, waiting for transfers between devices: 39.2 us -> 31.1 us  [exchange(): return lax.all_to_all(values, axes, split_axis=0, concat_axis=0, tiled=True)]
    pallas_call x10, Pallas kernels: 33.6 us -> 29.1 us  [call(): pl.pallas_call(body, in_specs=[pl.BlockSpec(memory_space=pltpu.SMEM)] + [...]
    all_to_all x5, starting transfers between devices: 30.3 us -> 26.2 us  [exchange(): return lax.all_to_all(values, axes, split_axis=0, concat_axis=0, tiled=True)]
    ppermute x20, waiting for transfers between devices: 24.4 us -> 26.8 us  [swap(): return lax.ppermute(values, axis, [(i, i ^ mask) for i in range(size)])]
    unnamed x69 -> x73, local copies, waits for them, and re-layouts: 19.6 us -> 17.6 us
  transfers between devices with their start and end apart: 25 -> 25, of which waited for: 15 -> 13; matrix products, arithmetic and copies ran while one was open for 11% -> 11% of each run, Pallas kernels for 12% -> 12%
where the time goes in v9:
time: 182 us; the launch traced here: 180 us
  waiting for transfers between devices  57.9 us (32%)
  starting transfers between devices  50.9 us (28%)
  Pallas kernels  29.1 us (16%)
  local copies, waits for them, and re-layouts  22.4 us (12%)
  matrix products  13.5 us (7%)
  other arithmetic  5.07 us (3%)
    all_to_all x5, waiting for transfers between devices, exchange(): return lax.all_to_all(values, axes, split_axis=0, concat_axis=0, tiled=True)  31.1 us
    pallas_call x10, Pallas kernels, call(): pl.pallas_call(body, in_specs=[pl.BlockSpec(memory_space=pltpu.SMEM)] + [...  29.1 us
    ppermute x20, waiting for transfers between devices, swap(): return lax.ppermute(values, axis, [(i, i ^ mask) for i in range(size)])  26.8 us
    all_to_all x5, starting transfers between devices, exchange(): return lax.all_to_all(values, axes, split_axis=0, concat_axis=0, tiled=True)  26.2 us
    ppermute x20, starting transfers between devices, swap(): return lax.ppermute(values, axis, [(i, i ^ mask) for i in range(size)])  24.7 us
    unnamed x73, local copies, waits for them, and re-layouts  17.6 us
    dot_general x1, matrix products, per_device(): hidden_pre = jnp.dot(slot_tokens, weight_in, preferred_element_type=F32)  7.47 us
  transfers between devices with their start and end apart: 25, of which 13 were waited for; matrix products, arithmetic and copies ran while one was open for 11% of the time, Pallas kernels for 12%

profile of v9, /device:TPU:2, one launch (start us, length us, event | category | flops | bytes accessed | tf_op | source)
XLA Modules:
  0.0 179.9 jit_solution(16017651124668960489)
XLA Ops:
  0.6 0.8 compare_reduce_fusion.1
  1.5 0.7 multiply_add_fusion
  2.2 3.3 %convolution_convert_fusion = bf16[512,2048]{1,0:T(8,128)(2,1)} fusion(bf16[256,2048]{1,0:T(8,128)(2,1)} %tok.1, s32[256]{0:T(256)S(1)} %bitcast.54, s32[256]{0:T(256)S(1)} %bitcast.50, pred[256]{0:T(512)(128)(4,1)S(1)} %get-tuple-element.155, pred[256]{0:T(512)(128)(4,1)S(1)} %get-tuple-element.154), kind=kOutput, calls=%fused_computation.1 | convolution fusion | flops 538574848 | bytes 3148288 | tf_op jit(solution)/shard_map/dot_general | solution.py:396
  5.6 6.3 %all-to-all-start.1 = ((bf16[8,64,2048]{2,1,0:T(8,128)(2,1)}), bf16[8,64,2048]{2,1,0:T(8,128)(2,1)S(1)}, u32[]{:S(2)}, u32[]{:S(2)}) async-start(bf16[8,64,2048]{2,1,0:T(8,128)(2,1)} %bitcast.48), calls=%async_computation.1 | async-start | bytes 4194304 | tf_op jit(solution)/shard_map/all_to_all | solution.py:38
  11.9 1.6 fusion.17
  14.8 0.7 convolution_convert_fusion.1
  15.6 1.6 pad_maximum_fusion
  17.1 19.9 %all-to-all-done.1 = bf16[8,64,2048]{2,1,0:T(8,128)(2,1)S(1)} async-done(((bf16[8,64,2048]{2,1,0:T(8,128)(2,1)}), bf16[8,64,2048]{2,1,0:T(8,128)(2,1)S(1)}, u32[]{:S(2)}, u32[]{:S(2)}) %all-to-all-start.1) | async-done | bytes 2097184 | tf_op jit(solution)/shard_map/all_to_all | solution.py:38
  37.1 1.4 copy-done.1
  38.4 5.3 %all-to-all-start = ((bf16[8,64,2176]{2,1,0:T(8,128)(2,1)}), bf16[8,64,2176]{2,1,0:T(8,128)(2,1)S(1)}, u32[]{:S(2)}, u32[]{:S(2)}) async-start(bf16[8,64,2176]{2,1,0:T(8,128)(2,1)} %bitcast.47), calls=%async_computation | async-start | bytes 4456448 | tf_op jit(solution)/shard_map/all_to_all | solution.py:38
  43.7 7.5 %fusion.3 = (f32[512,1024]{1,0:T(8,128)}, bf16[512,1024]{1,0:T(8,128)(2,1)}) fusion(bf16[512,2048]{1,0:T(8,128)(2,1)} %bitcast.39, bf16[1,2048,1024]{2,1,0:T(8,128)(2,1)} %param.11), kind=kOutput, calls=%fused_computation.7 | convolution fusion | flops 2152726528 | bytes 9437184 | tf_op jit(solution)/shard_map/dot_general | solution.py:435
  51.9 1.8 copy.27
  53.6 0.8 copy.29
  54.4 2.0 %pad.22.weight = bf16[2048,128]{1,0:T(8,128)(2,1)} pad(bf16[2048,8]{1,0:T(8,128)(2,1)} %copy.27, bf16[]{:T(256)} %constant.38.clone.1), padding=0_0x0_120 | pad | bytes 557058 | tf_op jit(solution)/shard_map/jit(_pad)/pad | solution.py:410
  56.5 0.8 broadcast_in_dim.52
  57.3 0.9 pad_bitcast_fusion
  58.2 0.8 pad_maximum_fusion.1.side
  59.2 10.5 %all-to-all-done = bf16[8,64,2176]{2,1,0:T(8,128)(2,1)S(1)} async-done(((bf16[8,64,2176]{2,1,0:T(8,128)(2,1)}), bf16[8,64,2176]{2,1,0:T(8,128)(2,1)S(1)}, u32[]{:S(2)}, u32[]{:S(2)}) %all-to-all-start) | async-done | bytes 2228256 | tf_op jit(solution)/shard_map/all_to_all | solution.py:38
  69.7 1.0 shard_map.111
  71.3 2.2 %copy-done.13 = bf16[1,1024,2048]{2,1,0:T(8,128)(2,1)S(1)} copy-done((bf16[1,1024,2048]{2,1,0:T(8,128)(2,1)S(1)}, bf16[1,1024,2048]{2,1,0:T(8,128)(2,1)}, u32[]{:S(2)}) %copy-start.13) | copy-done | bytes 4194328
  73.5 3.9 %shard_map.112 = (bf16[512,1024]{1,0:T(8,128)(2,1)S(1)}, bf16[512,512]{1,0:T(8,128)(2,1)S(1)}, bf16[512,128]{1,0:T(8,128)(2,1)S(1)}) custom-call(s32[4]{0:T(128)S(1)} %pad_add_fusion.pos_ref, bf16[512,2176]{1,0:T(8,128)(2,1)S(1)} %bitcast.37, bf16[1024,2048]{1,0:T(8,128)(2,1)S(1)} %bitcast.43, bf16[512,1024]{1,0:T(8,128)(2,1)} %get-tuple-element.100.act_ref.refs_4_.refs_0_, ...), custom_call_target="tpu_custom_call" | custom-call | flops 1000 | bytes 1000 | tf_op jit(solution)/shard_map/pallas_call | solution.py:47
  77.7 1.9 %collective-permute-done.3.refs_3_.refs_7_ = bf16[512,512]{1,0:T(8,128)(2,1)S(1)} collective-permute-done((bf16[512,512]{1,0:T(8,128)(2,1)S(1)}, bf16[512,512]{1,0:T(8,128)(2,1)S(1)}, u32[]{:S(2)}, u32[]{:S(2)}) %collective-permute-start.3) | collective-permute-done | bytes 524320 | tf_op jit(solution)/shard_map/ppermute | solution.py:34
  79.6 5.7 %shard_map.113 = (bf16[1024,512]{1,0:T(8,128)(2,1)}, bf16[1024,512]{1,0:T(8,128)(2,1)}) custom-call(s32[4]{0:T(128)S(1)} %pad_add_fusion.pos_ref, bf16[512,1024]{1,0:T(8,128)(2,1)S(1)} %get-tuple-element.104.refs_0_.refs_4_, bf16[512,1024]{1,0:T(8,128)(2,1)S(1)} %collective-permute-done.2.refs_1_.refs_5_, ...), custom_call_target="tpu_custom_call" | custom-call | flops 1000 | bytes 1000 | tf_op jit(solution)/shard_map/pallas_call | solution.py:47
  85.4 1.7 collective-permute-start.4
  87.0 2.2 %collective-permute-start.5 = (bf16[1024,512]{1,0:T(8,128)(2,1)}, bf16[1024,512]{1,0:T(8,128)(2,1)}, u32[]{:S(2)}, u32[]{:S(2)}) collective-permute-start(bf16[1024,512]{1,0:T(8,128)(2,1)} %get-tuple-element.92), channel_id=1, source_target_pairs={{0,192},{64,128},{128,64},{192,0},{1,193},{65,129},{129,65},{193,1... | collective-permute-start | bytes 3145736 | tf_op jit(solution)/shard_map/ppermute | solution.py:34
  89.2 5.1 %all-to-all-start.2 = ((bf16[8,64,128]{2,1,0:T(8,128)(2,1)}), bf16[8,64,128]{2,1,0:T(8,128)(2,1)S(1)}, u32[]{:S(2)}, u32[]{:S(2)}) async-start(bf16[8,64,128]{2,1,0:T(8,128)(2,1)} %bitcast.46), calls=%async_computation.2 | async-start | bytes 262144 | tf_op jit(solution)/shard_map/all_to_all | solution.py:38
  94.3 1.2 copy-done.6
  95.5 2.2 %copy-done.14 = bf16[1,2048,1024]{2,1,0:T(8,128)(2,1)S(1)} copy-done((bf16[1,2048,1024]{2,1,0:T(8,128)(2,1)S(1)}, bf16[1,2048,1024]{2,1,0:T(8,128)(2,1)}, u32[]{:S(2)}) %copy-start.14) | copy-done | bytes 4194328
  97.7 3.8 %shard_map.114 = bf16[512,2048]{1,0:T(8,128)(2,1)S(1)} custom-call(s32[4]{0:T(128)S(1)} %pad_add_fusion.pos_ref, bf16[512,1024]{1,0:T(8,128)(2,1)S(1)} %copy-done.6, bf16[2048,1024]{1,0:T(8,128)(2,1)S(1)} %bitcast.44), custom_call_target="tpu_custom_call" | custom-call | flops 1000 | bytes 1000 | tf_op jit(solution)/shard_map/pallas_call | solution.py:47
  101.5 1.4 copy-done.8
  102.9 5.8 %all-to-all-start.3 = ((bf16[8,64,2048]{2,1,0:T(8,128)(2,1)}), bf16[8,64,2048]{2,1,0:T(8,128)(2,1)}, u32[]{:S(2)}, u32[]{:S(2)}) async-start(bf16[8,64,2048]{2,1,0:T(8,128)(2,1)} %bitcast.42), calls=%async_computation.3 | async-start | bytes 4194304 | tf_op jit(solution)/shard_map/all_to_all | solution.py:38
  108.8 1.2 copy-done.4
  110.0 1.0 copy-done.18
  111.0 1.4 shard_map.115
  112.4 0.6 copy-done.22
  113.1 1.2 copy-done.10
  114.3 1.2 copy-done.12
  115.5 4.6 %shard_map.116 = (f32[256,512]{1,0:T(8,128)S(1)}, f32[256,512]{1,0:T(8,128)S(1)}, f32[512,256]{1,0:T(8,128)S(1)}, f32[512,256]{1,0:T(8,128)S(1)}, f32[512,512]{1,0:T(8,128)S(1)}, /*index=5*/f32[512,512]{1,0:T(8,128)S(1)}) custom-call(s32[4]{0:T(128)S(1)} %pad_add_fusion.pos_ref, bf16[512,1024]{1,0:T(8,128)(2,1)} %get-tuple-element.100.act_ref.refs_4_.refs_0_, ...), custom_call_target="tpu_custom_call" | custom-call | flops 1000 | bytes 1000 | tf_op jit(solution)/shard_map/pallas_call | solution.py:47
  120.2 1.8 shard_map.117
  121.9 0.8 collective-permute-start.7
  122.7 0.6 collective-permute-start.6
  123.3 6.3 %collective-permute-start.10 = (f32[8,2048]{1,0:T(8,128)S(1)}, f32[8,2048]{1,0:T(8,128)S(1)}, u32[]{:S(2)}, u32[]{:S(2)}) collective-permute-start(f32[8,2048]{1,0:T(8,128)S(1)} %get-tuple-element.120), channel_id=1, source_target_pairs={{0,32},{16,48},{32,0},{48,16},{1,33},{17,49},{33,1},{49,17},{2,34}... | collective-permute-start | bytes 196616 | tf_op jit(solution)/shard_map/ppermute | solution.py:34
  129.6 0.5 collective-permute-start.9
  130.2 0.9 collective-permute-start.8
  131.1 10.6 %collective-permute-done.10 = f32[8,2048]{1,0:T(8,128)S(1)} collective-permute-done((f32[8,2048]{1,0:T(8,128)S(1)}, f32[8,2048]{1,0:T(8,128)S(1)}, u32[]{:S(2)}, u32[]{:S(2)}) %collective-permute-start.10) | collective-permute-done | bytes 65568 | tf_op jit(solution)/shard_map/ppermute | solution.py:34
  142.2 1.9 %shard_map.118 = bf16[8,64,1024]{2,1,0:T(8,128)(2,1)S(1)} custom-call(s32[4]{0:T(128)S(1)} %pad_add_fusion.pos_ref, f32[256,512]{1,0:T(8,128)S(1)} %get-tuple-element.125.out_a, f32[256,512]{1,0:T(8,128)S(1)} %get-tuple-element.126.out_b, f32[512,256]{1,0:T(8,128)S(1)} %get-tuple-element.127.in_a, f32[512,256]{1,0:T(8,128)S(1)} %get-tuple-element.128.in_b, ...), custom_call_target="tpu_custom_call" | custom-call | flops 30000001024 | bytes 1000 | tf_op jit(solution)/shard_map/pallas_call | solution.py:47
  144.1 1.0 copy-done.20
  145.1 3.7 %all-to-all-start.4 = ((bf16[8,64,1024]{2,1,0:T(8,128)(2,1)}), bf16[8,64,1024]{2,1,0:T(8,128)(2,1)S(1)}, u32[]{:S(2)}, u32[]{:S(2)}) async-start(bf16[8,64,1024]{2,1,0:T(8,128)(2,1)} %copy-done.20), calls=%async_computation.4 | async-start | bytes 2097152 | tf_op jit(solution)/shard_map/all_to_all | solution.py:38
  148.8 3.6 %shard_map.119 = bf16[256,2048]{1,0:T(8,128)(2,1)} custom-call(s32[4]{0:T(128)S(1)} %pad_add_fusion.pos_ref, bf16[512,256]{1,0:T(8,128)(2,1)S(1)} %fusion.12.disp, bf16[512,2048]{1,0:T(8,128)(2,1)} %bitcast.19.flat, bf16[256,128]{1,0:T(8,128)(2,1)S(1)} %copy-done.23, bf16[2048,128]{1,0:T(8,128)(2,1)S(1)} %copy-done.19), custom_call_target="tpu_custom_call" | custom-call | flops 1000 | bytes 1000 | tf_op jit(solution)/shard_map/pallas_call | solution.py:47
  152.4 2.2 %collective-permute-start.13 = (f32[8,2048]{1,0:T(8,128)S(1)}, f32[8,2048]{1,0:T(8,128)S(1)}, u32[]{:S(2)}, u32[]{:S(2)}) collective-permute-start(f32[8,2048]{1,0:T(8,128)S(1)} %add_add_fusion.3), channel_id=1, source_target_pairs={{0,4},{2,6},{4,0},{6,2},{1,5},{3,7},{5,1},{7,3},{8,12},{10,14},{12... | collective-permute-start | bytes 196616 | tf_op jit(solution)/shard_map/ppermute | solution.py:34
  154.6 2.5 %collective-permute-start.11 = (f32[8,2048]{1,0:T(8,128)S(1)}, f32[8,2048]{1,0:T(8,128)S(1)}, u32[]{:S(2)}, u32[]{:S(2)}) collective-permute-start(f32[8,2048]{1,0:T(8,128)S(1)} %add_add_fusion.3), channel_id=1, source_target_pairs={{0,2},{2,0},{4,6},{6,4},{1,3},{3,1},{5,7},{7,5},{8,10},{10,8},{12,... | collective-permute-start | bytes 196616 | tf_op jit(solution)/shard_map/ppermute | solution.py:34
  157.1 1.3 collective-permute-done.13
  158.4 1.3 collective-permute-done.12
  159.7 1.1 collective-permute-start.16
  160.8 2.3 %collective-permute-start.15 = (f32[8,2048]{1,0:T(8,128)S(1)}, f32[8,2048]{1,0:T(8,128)S(1)}, u32[]{:S(2)}, u32[]{:S(2)}) collective-permute-start(f32[8,2048]{1,0:T(8,128)S(1)} %add_add_fusion.2), channel_id=1, source_target_pairs={{0,192},{64,128},{128,64},{192,0},{1,193},{65,129},{129,65},{193,1... | collective-permute-start | bytes 196616 | tf_op jit(solution)/shard_map/ppermute | solution.py:34
  163.3 2.4 %collective-permute-done.16 = f32[8,2048]{1,0:T(8,128)S(1)} collective-permute-done((f32[8,2048]{1,0:T(8,128)S(1)}, f32[8,2048]{1,0:T(8,128)S(1)}, u32[]{:S(2)}, u32[]{:S(2)}) %collective-permute-start.16) | collective-permute-done | bytes 65568 | tf_op jit(solution)/shard_map/ppermute | solution.py:34
  165.6 1.1 collective-permute-done.15
  166.7 0.7 collective-permute-done.14
  167.6 2.2 %collective-permute-start.18 = (f32[8,2048]{1,0:T(8,128)S(1)}, f32[8,2048]{1,0:T(8,128)S(1)}, u32[]{:S(2)}, u32[]{:S(2)}) collective-permute-start(f32[8,2048]{1,0:T(8,128)S(1)} %add_add_fusion.1), channel_id=1, source_target_pairs={{0,8},{1,9},{8,0},{9,1},{2,10},{3,11},{10,2},{11,3},{4,12},{5,13},... | collective-permute-start | bytes 196616 | tf_op jit(solution)/shard_map/ppermute | solution.py:34
  169.9 5.7 %collective-permute-done.19 = f32[8,2048]{1,0:T(8,128)S(1)} collective-permute-done((f32[8,2048]{1,0:T(8,128)S(1)}, f32[8,2048]{1,0:T(8,128)S(1)}, u32[]{:S(2)}, u32[]{:S(2)}) %collective-permute-start.19) | collective-permute-done | bytes 65568 | tf_op jit(solution)/shard_map/ppermute | solution.py:34
  175.6 1.5 collective-permute-done.17
  177.1 0.6 add_add_fusion
  177.8 0.7 all-to-all-done.4.got
  178.5 1.4 shard_map.120
  (101 shorter events, 4.0 us)
Async XLA Ops:
  0.6 14.2 %copy-start = (bf16[256,2048]{1,0:T(8,128)(2,1)S(1)}, bf16[256,2048]{1,0:T(8,128)(2,1)}, u32[]{:S(2)}) copy-start(bf16[256,2048]{1,0:T(8,128)(2,1)} %param.9) | copy-start | bytes 3145732
  1.5 13.3 %copy-start.32 = (pred[256]{0:T(512)(128)(4,1)}, pred[256]{0:T(512)(128)(4,1)S(1)}, u32[]{:S(2)}) copy-start(pred[256]{0:T(512)(128)(4,1)S(1)} %get-tuple-element.154) | copy-start | bytes 772
  1.5 13.3 %copy-start.34 = (pred[256]{0:T(512)(128)(4,1)}, pred[256]{0:T(512)(128)(4,1)S(1)}, u32[]{:S(2)}) copy-start(pred[256]{0:T(512)(128)(4,1)S(1)} %get-tuple-element.155) | copy-start | bytes 772
  2.2 12.6 %copy-start.27 = (s32[256,1]{0,1:T(1,128)}, s32[256,1]{0,1:T(1,128)S(1)}, u32[]{:S(2)}) copy-start(s32[256,1]{0,1:T(1,128)S(1)} %get-tuple-element.160) | copy-start | bytes 3076
  2.2 12.6 %copy-start.29 = (s32[256,1]{0,1:T(1,128)}, s32[256,1]{0,1:T(1,128)S(1)}, u32[]{:S(2)}) copy-start(s32[256,1]{0,1:T(1,128)S(1)} %get-tuple-element.161) | copy-start | bytes 3076
  5.5 6.3 %copy-start.25 = (s32[256,2]{0,1:T(2,128)S(1)}, s32[256,2]{0,1:T(2,128)}, u32[]{:S(2)}) copy-start(s32[256,2]{0,1:T(2,128)} %param.15) | copy-start | bytes 6148
  5.5 6.3 %copy-start.24 = (bf16[2048,8]{0,1:T(8,128)(2,1)S(1)}, bf16[2048,8]{0,1:T(8,128)(2,1)}, u32[]{:S(2)}) copy-start(bf16[2048,8]{0,1:T(8,128)(2,1)} %param.10) | copy-start | bytes 98308
  5.5 8.3 %copy-start.26 = (s32[256,2]{0,1:T(2,128)S(1)}, s32[256,2]{0,1:T(2,128)}, u32[]{:S(2)}) copy-start(s32[256,2]{0,1:T(2,128)} %param.13) | copy-start | bytes 6148
  5.6 31.5 %all-to-all-start.1 = ((bf16[8,64,2048]{2,1,0:T(8,128)(2,1)}), bf16[8,64,2048]{2,1,0:T(8,128)(2,1)S(1)}, u32[]{:S(2)}, u32[]{:S(2)}) async-start(bf16[8,64,2048]{2,1,0:T(8,128)(2,1)} %bitcast.48), calls=%async_computation.1 | async-start | bytes 4194304 | tf_op jit(solution)/shard_map/all_to_all | solution.py:38
  13.9 0.6 copy-start.31
  37.1 1.4 copy-start.1
  38.4 31.3 %all-to-all-start = ((bf16[8,64,2176]{2,1,0:T(8,128)(2,1)}), bf16[8,64,2176]{2,1,0:T(8,128)(2,1)S(1)}, u32[]{:S(2)}, u32[]{:S(2)}) async-start(bf16[8,64,2176]{2,1,0:T(8,128)(2,1)} %bitcast.47), calls=%async_computation | async-start | bytes 4456448 | tf_op jit(solution)/shard_map/all_to_all | solution.py:38
  43.7 26.0 %collective-permute-start = (bf16[512,2048]{1,0:T(8,128)(2,1)}, bf16[512,2048]{1,0:T(8,128)(2,1)}, u32[]{:S(2)}, u32[]{:S(2)}) collective-permute-start(bf16[512,2048]{1,0:T(8,128)(2,1)} %bitcast.38), channel_id=1, source_target_pairs={{0,8},{8,0},{1,9},{9,1},{2,10},{10,2},{3,11},{11,3},{4,12},{12,4},... | collective-permute-start | bytes 6291464 | tf_op jit(solution)/shard_map/ppermute | solution.py:34
  51.2 18.5 %collective-permute-start.1 = (bf16[512,1024]{1,0:T(8,128)(2,1)}, bf16[512,1024]{1,0:T(8,128)(2,1)}, u32[]{:S(2)}, u32[]{:S(2)}) collective-permute-start(bf16[512,1024]{1,0:T(8,128)(2,1)} %get-tuple-element.100.act_ref.refs_4_.refs_0_), channel_id=1, source_target_pairs={{0,8},{8,0},{1,9},{9,1},{2,10},{10,2},{3,11},{11,3},{4,12},{12,4},... | collective-permute-start | bytes 3145736 | tf_op jit(solution)/shard_map/ppermute | solution.py:34
  51.8 7.2 %copy-start.28 = (s32[256,1]{0,1:T(1,128)S(1)}, s32[256,1]{0,1:T(1,128)}, u32[]{:S(2)}) copy-start(s32[256,1]{0,1:T(1,128)} %copy-done.27) | copy-start | bytes 3076
  54.4 4.6 %copy-start.30 = (s32[256,1]{0,1:T(1,128)S(1)}, s32[256,1]{0,1:T(1,128)}, u32[]{:S(2)}) copy-start(s32[256,1]{0,1:T(1,128)} %copy-done.29) | copy-start | bytes 3076
  54.4 4.6 %copy-start.33 = (pred[256]{0:T(512)(128)(4,1)S(1)}, pred[256]{0:T(512)(128)(4,1)}, u32[]{:S(2)}) copy-start(pred[256]{0:T(512)(128)(4,1)} %copy-done.32) | copy-start | bytes 772
  54.4 4.6 %copy-start.35 = (pred[256]{0:T(512)(128)(4,1)S(1)}, pred[256]{0:T(512)(128)(4,1)}, u32[]{:S(2)}) copy-start(pred[256]{0:T(512)(128)(4,1)} %copy-done.34) | copy-start | bytes 772
  69.7 1.6 copy-start.15
  70.7 8.9 %copy-start.9 = (bf16[512,1024]{1,0:T(8,128)(2,1)}, bf16[512,1024]{1,0:T(8,128)(2,1)S(1)}, u32[]{:S(2)}) copy-start(bf16[512,1024]{1,0:T(8,128)(2,1)S(1)} %get-tuple-element.104.refs_0_.refs_4_) | copy-start | bytes 3145732
  70.7 8.9 %collective-permute-start.2 = (bf16[512,1024]{1,0:T(8,128)(2,1)S(1)}, bf16[512,1024]{1,0:T(8,128)(2,1)S(1)}, u32[]{:S(2)}, u32[]{:S(2)}) collective-permute-start(bf16[512,1024]{1,0:T(8,128)(2,1)S(1)} %get-tuple-element.80), channel_id=1, source_target_pairs={{0,8},{8,0},{1,9},{9,1},{2,10},{10,2},{3,11},{11,3},{4,12},{12,4},... | collective-permute-start | bytes 3145736 | tf_op jit(solution)/shard_map/ppermute | solution.py:34
  71.3 2.2 %copy-start.13 = (bf16[1,1024,2048]{2,1,0:T(8,128)(2,1)S(1)}, bf16[1,1024,2048]{2,1,0:T(8,128)(2,1)}, u32[]{:S(2)}) copy-start(bf16[1,1024,2048]{2,1,0:T(8,128)(2,1)} %param.12) | copy-start | bytes 12582916
  73.5 6.1 %copy-start.2 = (bf16[8,64,2048]{2,1,0:T(8,128)(2,1)S(1)}, bf16[8,64,2048]{2,1,0:T(8,128)(2,1)}, u32[]{:S(2)}) copy-start(bf16[8,64,2048]{2,1,0:T(8,128)(2,1)} %copy-done.1) | copy-start | bytes 6291460
  77.4 7.9 %copy-start.5 = (bf16[512,1024]{1,0:T(8,128)(2,1)}, bf16[512,1024]{1,0:T(8,128)(2,1)S(1)}, u32[]{:S(2)}) copy-start(bf16[512,1024]{1,0:T(8,128)(2,1)S(1)} %get-tuple-element.106.refs_2_.grad.refs_6_) | copy-start | bytes 3145732
  77.4 7.9 %copy-start.21 = (bf16[512,128]{1,0:T(8,128)(2,1)}, bf16[512,128]{1,0:T(8,128)(2,1)S(1)}, u32[]{:S(2)}) copy-start(bf16[512,128]{1,0:T(8,128)(2,1)S(1)} %get-tuple-element.94) | copy-start | bytes 393220
  77.4 2.2 %collective-permute-start.3 = (bf16[512,512]{1,0:T(8,128)(2,1)S(1)}, bf16[512,512]{1,0:T(8,128)(2,1)S(1)}, u32[]{:S(2)}, u32[]{:S(2)}) collective-permute-start(bf16[512,512]{1,0:T(8,128)(2,1)S(1)} %get-tuple-element.87), channel_id=1, source_target_pairs={{0,8},{8,0},{1,9},{9,1},{2,10},{10,2},{3,11},{11,3},{4,12},{12,4},... | collective-permute-start | bytes 1572872 | tf_op jit(solution)/shard_map/ppermute | solution.py:34
  79.6 5.7 %copy-start.16 = (bf16[512,512]{1,0:T(8,128)(2,1)}, bf16[512,512]{1,0:T(8,128)(2,1)S(1)}, u32[]{:S(2)}) copy-start(bf16[512,512]{1,0:T(8,128)(2,1)S(1)} %collective-permute-done.3.refs_3_.refs_7_) | copy-start | bytes 1572868
  79.6 5.7 %copy-start.11 = (bf16[512,1024]{1,0:T(8,128)(2,1)}, bf16[512,1024]{1,0:T(8,128)(2,1)S(1)}, u32[]{:S(2)}) copy-start(bf16[512,1024]{1,0:T(8,128)(2,1)S(1)} %collective-permute-done.2.refs_1_.refs_5_) | copy-start | bytes 3145732
  85.4 34.8 %collective-permute-start.4 = (bf16[1024,512]{1,0:T(8,128)(2,1)}, bf16[1024,512]{1,0:T(8,128)(2,1)}, u32[]{:S(2)}, u32[]{:S(2)}) collective-permute-start(bf16[1024,512]{1,0:T(8,128)(2,1)} %get-tuple-element.91), channel_id=1, source_target_pairs={{0,64},{64,0},{128,192},{192,128},{1,65},{65,1},{129,193},{193,129... | collective-permute-start | bytes 3145736 | tf_op jit(solution)/shard_map/ppermute | solution.py:34
  87.0 33.2 %collective-permute-start.5 = (bf16[1024,512]{1,0:T(8,128)(2,1)}, bf16[1024,512]{1,0:T(8,128)(2,1)}, u32[]{:S(2)}, u32[]{:S(2)}) collective-permute-start(bf16[1024,512]{1,0:T(8,128)(2,1)} %get-tuple-element.92), channel_id=1, source_target_pairs={{0,192},{64,128},{128,64},{192,0},{1,193},{65,129},{129,65},{193,1... | collective-permute-start | bytes 3145736 | tf_op jit(solution)/shard_map/ppermute | solution.py:34
  89.2 13.7 %all-to-all-start.2 = ((bf16[8,64,128]{2,1,0:T(8,128)(2,1)}), bf16[8,64,128]{2,1,0:T(8,128)(2,1)S(1)}, u32[]{:S(2)}, u32[]{:S(2)}) async-start(bf16[8,64,128]{2,1,0:T(8,128)(2,1)} %bitcast.46), calls=%async_computation.2 | async-start | bytes 262144 | tf_op jit(solution)/shard_map/all_to_all | solution.py:38
  94.3 1.2 copy-start.6
  95.5 2.2 %copy-start.14 = (bf16[1,2048,1024]{2,1,0:T(8,128)(2,1)S(1)}, bf16[1,2048,1024]{2,1,0:T(8,128)(2,1)}, u32[]{:S(2)}) copy-start(bf16[1,2048,1024]{2,1,0:T(8,128)(2,1)} %param.11) | copy-start | bytes 12582916
  101.5 1.4 copy-start.8
  102.9 10.1 %copy-start.3 = (bf16[8,64,2048]{2,1,0:T(8,128)(2,1)S(1)}, bf16[8,64,2048]{2,1,0:T(8,128)(2,1)}, u32[]{:S(2)}) copy-start(bf16[8,64,2048]{2,1,0:T(8,128)(2,1)} %copy-done.1) | copy-start | bytes 6291460
  102.9 42.2 %all-to-all-start.3 = ((bf16[8,64,2048]{2,1,0:T(8,128)(2,1)}), bf16[8,64,2048]{2,1,0:T(8,128)(2,1)}, u32[]{:S(2)}, u32[]{:S(2)}) async-start(bf16[8,64,2048]{2,1,0:T(8,128)(2,1)} %bitcast.42), calls=%async_computation.3 | async-start | bytes 4194304 | tf_op jit(solution)/shard_map/all_to_all | solution.py:38
  108.8 1.2 copy-start.4
  110.0 1.0 copy-start.18
  111.0 2.0 %copy-start.7 = (bf16[512,1024]{1,0:T(8,128)(2,1)S(1)}, bf16[512,1024]{1,0:T(8,128)(2,1)}, u32[]{:S(2)}) copy-start(bf16[512,1024]{1,0:T(8,128)(2,1)} %copy-done.5) | copy-start | bytes 3145732
  111.0 2.0 %copy-start.17 = (bf16[512,512]{1,0:T(8,128)(2,1)S(1)}, bf16[512,512]{1,0:T(8,128)(2,1)}, u32[]{:S(2)}) copy-start(bf16[512,512]{1,0:T(8,128)(2,1)} %copy-done.16) | copy-start | bytes 1572868
  112.4 0.6 copy-start.22
  113.0 1.2 copy-start.10
  114.3 1.2 copy-start.12
  121.9 20.2 %collective-permute-start.7 = (bf16[512,512]{1,0:T(8,128)(2,1)S(1)}, bf16[512,512]{1,0:T(8,128)(2,1)S(1)}, u32[]{:S(2)}, u32[]{:S(2)}) collective-permute-start(bf16[512,512]{1,0:T(8,128)(2,1)S(1)} %get-tuple-element.119), channel_id=1, source_target_pairs={{0,64},{64,0},{128,192},{192,128},{1,65},{65,1},{129,193},{193,129... | collective-permute-start | bytes 1572872 | tf_op jit(solution)/shard_map/ppermute | solution.py:34
  122.7 19.4 %collective-permute-start.6 = (bf16[512,512]{1,0:T(8,128)(2,1)S(1)}, bf16[512,512]{1,0:T(8,128)(2,1)S(1)}, u32[]{:S(2)}, u32[]{:S(2)}) collective-permute-start(bf16[512,512]{1,0:T(8,128)(2,1)S(1)} %get-tuple-element.118), channel_id=1, source_target_pairs={{0,192},{64,128},{128,64},{192,0},{1,193},{65,129},{129,65},{193,1... | collective-permute-start | bytes 1572872 | tf_op jit(solution)/shard_map/ppermute | solution.py:34
  123.3 18.4 %collective-permute-start.10 = (f32[8,2048]{1,0:T(8,128)S(1)}, f32[8,2048]{1,0:T(8,128)S(1)}, u32[]{:S(2)}, u32[]{:S(2)}) collective-permute-start(f32[8,2048]{1,0:T(8,128)S(1)} %get-tuple-element.120), channel_id=1, source_target_pairs={{0,32},{16,48},{32,0},{48,16},{1,33},{17,49},{33,1},{49,17},{2,34}... | collective-permute-start | bytes 196616 | tf_op jit(solution)/shard_map/ppermute | solution.py:34
  129.6 12.5 %collective-permute-start.9 = (f32[8,2048]{1,0:T(8,128)S(1)}, f32[8,2048]{1,0:T(8,128)S(1)}, u32[]{:S(2)}, u32[]{:S(2)}) collective-permute-start(f32[8,2048]{1,0:T(8,128)S(1)} %get-tuple-element.120), channel_id=1, source_target_pairs={{0,48},{16,32},{32,16},{48,0},{1,49},{17,33},{33,17},{49,1},{2,50}... | collective-permute-start | bytes 196616 | tf_op jit(solution)/shard_map/ppermute | solution.py:34
  130.2 12.0 %collective-permute-start.8 = (f32[8,2048]{1,0:T(8,128)S(1)}, f32[8,2048]{1,0:T(8,128)S(1)}, u32[]{:S(2)}, u32[]{:S(2)}) collective-permute-start(f32[8,2048]{1,0:T(8,128)S(1)} %get-tuple-element.120), channel_id=1, source_target_pairs={{0,16},{16,0},{32,48},{48,32},{1,17},{17,1},{33,49},{49,33},{2,18}... | collective-permute-start | bytes 196616 | tf_op jit(solution)/shard_map/ppermute | solution.py:34
  144.1 1.0 copy-start.20
  145.1 3.7 %copy-start.19 = (bf16[2048,128]{1,0:T(8,128)(2,1)S(1)}, bf16[2048,128]{1,0:T(8,128)(2,1)}, u32[]{:S(2)}) copy-start(bf16[2048,128]{1,0:T(8,128)(2,1)} %pad.22.weight) | copy-start | bytes 1572868
  145.1 3.7 %copy-start.23 = (bf16[256,128]{1,0:T(8,128)(2,1)S(1)}, bf16[256,128]{1,0:T(8,128)(2,1)}, u32[]{:S(2)}) copy-start(bf16[256,128]{1,0:T(8,128)(2,1)} %copy-done.22) | copy-start | bytes 196612
  145.1 33.4 %all-to-all-start.4 = ((bf16[8,64,1024]{2,1,0:T(8,128)(2,1)}), bf16[8,64,1024]{2,1,0:T(8,128)(2,1)S(1)}, u32[]{:S(2)}, u32[]{:S(2)}) async-start(bf16[8,64,1024]{2,1,0:T(8,128)(2,1)} %copy-done.20), calls=%async_computation.4 | async-start | bytes 2097152 | tf_op jit(solution)/shard_map/all_to_all | solution.py:38
  152.4 6.0 %collective-permute-start.13 = (f32[8,2048]{1,0:T(8,128)S(1)}, f32[8,2048]{1,0:T(8,128)S(1)}, u32[]{:S(2)}, u32[]{:S(2)}) collective-permute-start(f32[8,2048]{1,0:T(8,128)S(1)} %add_add_fusion.3), channel_id=1, source_target_pairs={{0,4},{2,6},{4,0},{6,2},{1,5},{3,7},{5,1},{7,3},{8,12},{10,14},{12... | collective-permute-start | bytes 196616 | tf_op jit(solution)/shard_map/ppermute | solution.py:34
  154.6 5.1 %collective-permute-start.12 = (f32[8,2048]{1,0:T(8,128)S(1)}, f32[8,2048]{1,0:T(8,128)S(1)}, u32[]{:S(2)}, u32[]{:S(2)}) collective-permute-start(f32[8,2048]{1,0:T(8,128)S(1)} %add_add_fusion.3), channel_id=1, source_target_pairs={{0,6},{2,4},{4,2},{6,0},{1,7},{3,5},{5,3},{7,1},{8,14},{10,12},{12... | collective-permute-start | bytes 196616 | tf_op jit(solution)/shard_map/ppermute | solution.py:34
  154.6 5.1 %collective-permute-start.11 = (f32[8,2048]{1,0:T(8,128)S(1)}, f32[8,2048]{1,0:T(8,128)S(1)}, u32[]{:S(2)}, u32[]{:S(2)}) collective-permute-start(f32[8,2048]{1,0:T(8,128)S(1)} %add_add_fusion.3), channel_id=1, source_target_pairs={{0,2},{2,0},{4,6},{6,4},{1,3},{3,1},{5,7},{7,5},{8,10},{10,8},{12,... | collective-permute-start | bytes 196616 | tf_op jit(solution)/shard_map/ppermute | solution.py:34
  159.7 5.9 %collective-permute-start.16 = (f32[8,2048]{1,0:T(8,128)S(1)}, f32[8,2048]{1,0:T(8,128)S(1)}, u32[]{:S(2)}, u32[]{:S(2)}) collective-permute-start(f32[8,2048]{1,0:T(8,128)S(1)} %add_add_fusion.2), channel_id=1, source_target_pairs={{0,128},{64,192},{128,0},{192,64},{1,129},{65,193},{129,1},{193,65... | collective-permute-start | bytes 196616 | tf_op jit(solution)/shard_map/ppermute | solution.py:34
  160.8 5.9 %collective-permute-start.15 = (f32[8,2048]{1,0:T(8,128)S(1)}, f32[8,2048]{1,0:T(8,128)S(1)}, u32[]{:S(2)}, u32[]{:S(2)}) collective-permute-start(f32[8,2048]{1,0:T(8,128)S(1)} %add_add_fusion.2), channel_id=1, source_target_pairs={{0,192},{64,128},{128,64},{192,0},{1,193},{65,129},{129,65},{193,1... | collective-permute-start | bytes 196616 | tf_op jit(solution)/shard_map/ppermute | solution.py:34
  163.1 4.3 %collective-permute-start.14 = (f32[8,2048]{1,0:T(8,128)S(1)}, f32[8,2048]{1,0:T(8,128)S(1)}, u32[]{:S(2)}, u32[]{:S(2)}) collective-permute-start(f32[8,2048]{1,0:T(8,128)S(1)} %add_add_fusion.2), channel_id=1, source_target_pairs={{0,64},{64,0},{128,192},{192,128},{1,65},{65,1},{129,193},{193,129... | collective-permute-start | bytes 196616 | tf_op jit(solution)/shard_map/ppermute | solution.py:34
  167.4 8.2 %collective-permute-start.19 = (f32[8,2048]{1,0:T(8,128)S(1)}, f32[8,2048]{1,0:T(8,128)S(1)}, u32[]{:S(2)}, u32[]{:S(2)}) collective-permute-start(f32[8,2048]{1,0:T(8,128)S(1)} %add_add_fusion.1), channel_id=1, source_target_pairs={{0,9},{1,8},{8,1},{9,0},{2,11},{3,10},{10,3},{11,2},{4,13},{5,12},... | collective-permute-start | bytes 196616 | tf_op jit(solution)/shard_map/ppermute | solution.py:34
  167.6 8.0 %collective-permute-start.18 = (f32[8,2048]{1,0:T(8,128)S(1)}, f32[8,2048]{1,0:T(8,128)S(1)}, u32[]{:S(2)}, u32[]{:S(2)}) collective-permute-start(f32[8,2048]{1,0:T(8,128)S(1)} %add_add_fusion.1), channel_id=1, source_target_pairs={{0,8},{1,9},{8,0},{9,1},{2,10},{3,11},{10,2},{11,3},{4,12},{5,13},... | collective-permute-start | bytes 196616 | tf_op jit(solution)/shard_map/ppermute | solution.py:34
  169.9 7.3 %collective-permute-start.17 = (f32[8,2048]{1,0:T(8,128)S(1)}, f32[8,2048]{1,0:T(8,128)S(1)}, u32[]{:S(2)}, u32[]{:S(2)}) collective-permute-start(f32[8,2048]{1,0:T(8,128)S(1)} %add_add_fusion.1), channel_id=1, source_target_pairs={{0,1},{1,0},{8,9},{9,8},{2,3},{3,2},{10,11},{11,10},{4,5},{5,4},{1... | collective-permute-start | bytes 196616 | tf_op jit(solution)/shard_map/ppermute | solution.py:34

commit v10 on v9

--- a/solution.py
+++ b/solution.py
@@ -10,7 +10,9 @@
 GROUP = ("x", "zl")
 EXTRA = 128
 VMEM_LIMIT = 20 * 1024 * 1024
-LONG = 30_000_000_000
+ALL_VMEM = 58 * 1024 * 1024
+MOST_VMEM = 52 * 1024 * 1024
+LONG = 28_000_000_000
 F32 = jnp.float32
 BF16 = jnp.bfloat16
 
@@ -42,7 +44,7 @@
     return lax.optimization_barrier(values)
 
 
-def call(body, pos, inputs, outputs, flops=1000, far=(), scratch=()):
+def call(body, pos, inputs, outputs, flops=1000, far=(), scratch=(), vmem_limit=VMEM_LIMIT):
     vmem = pl.BlockSpec(memory_space=pltpu.VMEM)
     return pl.pallas_call(
         body,
@@ -53,7 +55,7 @@
         out_shape=[jax.ShapeDtypeStruct(shape, dtype) for shape, dtype in outputs],
         scratch_shapes=scratch,
         cost_estimate=pl.CostEstimate(flops=flops, bytes_accessed=1000, transcendentals=0),
-        compiler_params=pltpu.CompilerParams(vmem_limit_bytes=VMEM_LIMIT),
+        compiler_params=pltpu.CompilerParams(vmem_limit_bytes=vmem_limit),
     )(pos, *inputs, *far)
 
 
@@ -188,6 +190,7 @@
         outputs,
         far=lefts if near else lefts + rights,
         scratch=scratch,
+        vmem_limit=VMEM_LIMIT if near else MOST_VMEM,
     )
 
 
@@ -319,6 +322,7 @@
         [((slots, width), BF16)],
         far=[weight_in],
         scratch=[pltpu.VMEM((width, hidden), BF16), pltpu.SemaphoreType.DMA((4,))],
+        vmem_limit=ALL_VMEM,
     )[0]
 
 
@@ -351,6 +355,7 @@
         [((rows, EXTRA), BF16), ((experts, width), F32)],
         far=[tokens],
         scratch=[pltpu.VMEM((rows, width), BF16), pltpu.SemaphoreType.DMA],
+        vmem_limit=ALL_VMEM,
     )
 
 
@@ -482,7 +487,9 @@
     got, far_a, far_b = tie(got, far_a, far_b)
     far_a, far_b = far_sums(pos, (far_a, far_b), got)
     far = (swap(far_a, "y", 3), swap(far_b, "y", 1))
-    router_part = router_round(router_part, "zh", 1, 3, far_a)
+    other_router = swap(router_part, "core", 1)
+    router_part, other_router, _ = tie(router_part, other_router, far_a)
+    router_part = router_part + other_router
 
     near, far, router_part = tie(near, far, router_part)
     pieces = zh_pieces(pos, near[:2], near[2:], got, far, grad_scale)
@@ -490,10 +497,10 @@
 
     back, router_part, _ = tie(back, router_part, pieces)
     grad_tokens = token_grads(pos, dispatch, back, logit_lanes, weight_lanes)
-    router_part, _ = tie(router_part, grad_tokens)
-    router_part = router_round(router_part, "x", 1, 3)
+    router_part = router_round(router_part, "x", 1, 3, grad_tokens)
     router_part = router_round(router_part, "y", 1, 3)
-    router_part = router_round(router_part, ("core", "zl"), 1, 2)
+    router_part = router_part + swap(router_part, "zl", 1)
+    router_part = router_round(router_part, "zh", 1, 3)
     got, router_part = tie(got, router_part)
     outer_share, inner_share = shares(pos, got, near[0].shape[0] // 8)
     return (grad_tokens, router_part.T, inner_share, outer_share)

time: 182 us -> 189 us (1.038)
  Pallas kernels: 29.1 us -> 36.2 us
  local copies, waits for them, and re-layouts: 22.4 us -> 16.4 us
  waiting for transfers between devices: 57.9 us -> 61.1 us
  other arithmetic: 5.07 us -> 7.09 us
    pallas_call x10, Pallas kernels: 29.1 us -> 36.2 us  [call(): pl.pallas_call(body, in_specs=[pl.BlockSpec(memory_space=pltpu.SMEM)] + [...]
    unnamed x73 -> x55, local copies, waits for them, and re-layouts: 17.6 us -> 11 us
    ppermute x20 -> x19, waiting for transfers between devices: 26.8 us -> 32.9 us  [swap(): return lax.ppermute(values, axis, [(i, i ^ mask) for i in range(size)])]
    all_to_all x5, starting transfers between devices: 26.2 us -> 30.1 us  [exchange(): return lax.all_to_all(values, axes, split_axis=0, concat_axis=0, tiled=True)]
    all_to_all x5, waiting for transfers between devices: 31.1 us -> 28.2 us  [exchange(): return lax.all_to_all(values, axes, split_axis=0, concat_axis=0, tiled=True)]
    ppermute x20 -> x19, starting transfers between devices: 24.7 us -> 22.2 us  [swap(): return lax.ppermute(values, axis, [(i, i ^ mask) for i in range(size)])]
  transfers between devices with their start and end apart: 25 -> 24, of which waited for: 13 -> 12; matrix products, arithmetic and copies ran while one was open for 11% -> 12% of each run, Pallas kernels for 12% -> 15%
where the time goes in v10:
time: 189 us; the launch traced here: 188 us
  waiting for transfers between devices  61.1 us (32%)
  starting transfers between devices  52.3 us (28%)
  Pallas kernels  36.2 us (19%)
  local copies, waits for them, and re-layouts  16.4 us (9%)
  matrix products  13.6 us (7%)
  other arithmetic  7.09 us (4%)
    pallas_call x10, Pallas kernels, call(): pl.pallas_call(body, in_specs=[pl.BlockSpec(memory_space=pltpu.SMEM)] + [...  36.2 us
    ppermute x19, waiting for transfers between devices, swap(): return lax.ppermute(values, axis, [(i, i ^ mask) for i in range(size)])  32.9 us
    all_to_all x5, starting transfers between devices, exchange(): return lax.all_to_all(values, axes, split_axis=0, concat_axis=0, tiled=True)  30.1 us
    all_to_all x5, waiting for transfers between devices, exchange(): return lax.all_to_all(values, axes, split_axis=0, concat_axis=0, tiled=True)  28.2 us
    ppermute x19, starting transfers between devices, swap(): return lax.ppermute(values, axis, [(i, i ^ mask) for i in range(size)])  22.2 us
    unnamed x55, local copies, waits for them, and re-layouts  11 us
    dot_general x1, matrix products, per_device(): hidden_pre = jnp.dot(slot_tokens, weight_in, preferred_element_type=F32)  7.55 us
  transfers between devices with their start and end apart: 24, of which 12 were waited for; matrix products, arithmetic and copies ran while one was open for 12% of the time, Pallas kernels for 15%

profile of v10, /device:TPU:2, one launch (start us, length us, event | category | flops | bytes accessed | tf_op | source)
XLA Modules:
  0.0 187.7 jit_solution(7464511879237842359)
XLA Ops:
  0.6 0.8 compare_reduce_fusion.1
  1.5 0.7 multiply_add_fusion
  2.2 3.4 %convolution_convert_fusion = bf16[512,2048]{1,0:T(8,128)(2,1)} fusion(bf16[256,2048]{1,0:T(8,128)(2,1)} %tok.1, s32[256]{0:T(256)S(1)} %bitcast.54, s32[256]{0:T(256)S(1)} %bitcast.50, pred[256]{0:T(512)(128)(4,1)S(1)} %get-tuple-element.149, pred[256]{0:T(512)(128)(4,1)S(1)} %get-tuple-element.148), kind=kOutput, calls=%fused_computation.1 | convolution fusion | flops 538574848 | bytes 3148288 | tf_op jit(solution)/shard_map/dot_general | solution.py:401
  5.6 6.3 %all-to-all-start.1 = ((bf16[8,64,2048]{2,1,0:T(8,128)(2,1)}), bf16[8,64,2048]{2,1,0:T(8,128)(2,1)S(1)}, u32[]{:S(2)}, u32[]{:S(2)}) async-start(bf16[8,64,2048]{2,1,0:T(8,128)(2,1)} %bitcast.45), calls=%async_computation.1 | async-start | bytes 4194304 | tf_op jit(solution)/shard_map/all_to_all | solution.py:40
  11.9 1.6 fusion.17
  13.9 0.6 select_reduce_fusion
  14.6 0.3 convolution_convert_fusion.2
  14.9 0.7 convolution_convert_fusion.1
  15.6 1.6 pad_maximum_fusion
  17.3 19.9 %all-to-all-done.1 = bf16[8,64,2048]{2,1,0:T(8,128)(2,1)S(1)} async-done(((bf16[8,64,2048]{2,1,0:T(8,128)(2,1)}), bf16[8,64,2048]{2,1,0:T(8,128)(2,1)S(1)}, u32[]{:S(2)}, u32[]{:S(2)}) %all-to-all-start.1) | async-done | bytes 2097184 | tf_op jit(solution)/shard_map/all_to_all | solution.py:40
  37.1 1.3 copy-done.1
  38.4 5.3 %all-to-all-start = ((bf16[8,64,2176]{2,1,0:T(8,128)(2,1)}), bf16[8,64,2176]{2,1,0:T(8,128)(2,1)S(1)}, u32[]{:S(2)}, u32[]{:S(2)}) async-start(bf16[8,64,2176]{2,1,0:T(8,128)(2,1)} %bitcast.44), calls=%async_computation | async-start | bytes 4456448 | tf_op jit(solution)/shard_map/all_to_all | solution.py:40
  43.7 7.5 %fusion.3 = (f32[512,1024]{1,0:T(8,128)}, bf16[512,1024]{1,0:T(8,128)(2,1)}) fusion(bf16[512,2048]{1,0:T(8,128)(2,1)} %bitcast.39, bf16[1,2048,1024]{2,1,0:T(8,128)(2,1)} %param.11), kind=kOutput, calls=%fused_computation.7 | convolution fusion | flops 2152726528 | bytes 9437184 | tf_op jit(solution)/shard_map/dot_general | solution.py:440
  51.3 0.5 collective-permute-start.1
  51.9 1.8 copy.27
  53.7 1.5 copy.29
  55.2 1.9 %pad.22.weight = bf16[2048,128]{1,0:T(8,128)(2,1)} pad(bf16[2048,8]{1,0:T(8,128)(2,1)} %copy.27, bf16[]{:T(256)} %constant.38.clone.1), padding=0_0x0_120 | pad | bytes 557058 | tf_op jit(solution)/shard_map/jit(_pad)/pad | solution.py:415
  57.3 0.7 broadcast_in_dim.52
  58.0 0.9 pad_bitcast_fusion
  58.9 0.8 pad_maximum_fusion.1.side
  59.7 1.6 fusion.12.disp
  61.3 8.4 %all-to-all-done = bf16[8,64,2176]{2,1,0:T(8,128)(2,1)S(1)} async-done(((bf16[8,64,2176]{2,1,0:T(8,128)(2,1)}), bf16[8,64,2176]{2,1,0:T(8,128)(2,1)S(1)}, u32[]{:S(2)}, u32[]{:S(2)}) %all-to-all-start) | async-done | bytes 2228256 | tf_op jit(solution)/shard_map/all_to_all | solution.py:40
  69.7 1.0 shard_map.111
  70.8 0.5 copy-done.8
  71.3 2.2 %copy-done.6 = bf16[1,1024,2048]{2,1,0:T(8,128)(2,1)S(1)} copy-done((bf16[1,1024,2048]{2,1,0:T(8,128)(2,1)S(1)}, bf16[1,1024,2048]{2,1,0:T(8,128)(2,1)}, u32[]{:S(2)}) %copy-start.6) | copy-done | bytes 4194328
  73.5 4.6 %shard_map.112 = (bf16[512,1024]{1,0:T(8,128)(2,1)S(1)}, bf16[512,512]{1,0:T(8,128)(2,1)S(1)}, bf16[512,128]{1,0:T(8,128)(2,1)}) custom-call(s32[4]{0:T(128)S(1)} %pad_add_fusion.pos_ref, bf16[512,2176]{1,0:T(8,128)(2,1)S(1)} %bitcast.37, bf16[1024,2048]{1,0:T(8,128)(2,1)S(1)} %bitcast.43, bf16[512,1024]{1,0:T(8,128)(2,1)} %get-tuple-element.97.act_ref.refs_4_.refs_0_, ...), custom_call_target="tpu_custom_call" | custom-call | flops 1000 | bytes 1000 | tf_op jit(solution)/shard_map/pallas_call | solution.py:49
  78.0 1.9 %collective-permute-done.3.refs_3_.refs_7_ = bf16[512,512]{1,0:T(8,128)(2,1)S(1)} collective-permute-done((bf16[512,512]{1,0:T(8,128)(2,1)S(1)}, bf16[512,512]{1,0:T(8,128)(2,1)S(1)}, u32[]{:S(2)}, u32[]{:S(2)}) %collective-permute-start.3) | collective-permute-done | bytes 524320 | tf_op jit(solution)/shard_map/ppermute | solution.py:36
  80.0 5.6 %shard_map.113 = (bf16[1024,512]{1,0:T(8,128)(2,1)}, bf16[1024,512]{1,0:T(8,128)(2,1)}) custom-call(s32[4]{0:T(128)S(1)} %pad_add_fusion.pos_ref, bf16[512,1024]{1,0:T(8,128)(2,1)S(1)} %get-tuple-element.101.refs_0_.refs_4_, bf16[512,1024]{1,0:T(8,128)(2,1)S(1)} %collective-permute-done.2.refs_1_.refs_5_, ...), custom_call_target="tpu_custom_call" | custom-call | flops 1000 | bytes 1000 | tf_op jit(solution)/shard_map/pallas_call | solution.py:49
  85.6 1.7 collective-permute-start.4
  87.3 2.2 %collective-permute-start.5 = (bf16[1024,512]{1,0:T(8,128)(2,1)}, bf16[1024,512]{1,0:T(8,128)(2,1)}, u32[]{:S(2)}, u32[]{:S(2)}) collective-permute-start(bf16[1024,512]{1,0:T(8,128)(2,1)} %get-tuple-element.89), channel_id=1, source_target_pairs={{0,192},{64,128},{128,64},{192,0},{1,193},{65,129},{129,65},{193,1... | collective-permute-start | bytes 3145736 | tf_op jit(solution)/shard_map/ppermute | solution.py:36
  89.5 5.1 %all-to-all-start.2 = ((bf16[8,64,128]{2,1,0:T(8,128)(2,1)}), bf16[8,64,128]{2,1,0:T(8,128)(2,1)S(1)}, u32[]{:S(2)}, u32[]{:S(2)}) async-start(bf16[8,64,128]{2,1,0:T(8,128)(2,1)} %bitcast.16), calls=%async_computation.2 | async-start | bytes 262144 | tf_op jit(solution)/shard_map/all_to_all | solution.py:40
  94.5 6.8 %shard_map.114 = bf16[512,2048]{1,0:T(8,128)(2,1)} custom-call(s32[4]{0:T(128)} %copy-done.15, bf16[512,1024]{1,0:T(8,128)(2,1)} %copy-done.3, bf16[2048,1024]{1,0:T(8,128)(2,1)} %bitcast.47), custom_call_target="tpu_custom_call" | custom-call | flops 1000 | bytes 1000 | tf_op jit(solution)/shard_map/pallas_call | solution.py:49
  101.4 0.6 copy-done.18
  102.0 5.7 %all-to-all-start.3 = ((bf16[8,64,2048]{2,1,0:T(8,128)(2,1)}), bf16[8,64,2048]{2,1,0:T(8,128)(2,1)S(1)}, u32[]{:S(2)}, u32[]{:S(2)}) async-start(bf16[8,64,2048]{2,1,0:T(8,128)(2,1)} %bitcast.46), calls=%async_computation.3 | async-start | bytes 4194304 | tf_op jit(solution)/shard_map/all_to_all | solution.py:40
  107.8 3.4 %shard_map.115 = (bf16[256,128]{1,0:T(8,128)(2,1)}, f32[8,2048]{1,0:T(8,128)}) custom-call(s32[4]{0:T(128)} %copy-done.15, bf16[512,256]{1,0:T(8,128)(2,1)} %fusion.12.disp, bf16[512,128]{1,0:T(8,128)(2,1)} %bitcast.48, f32[4,256,128]{2,1,0:T(8,128)} %pad_maximum_fusion.1.side, bf16[256,2048]{1,0:T(8,128)(2,1)} %tok.1), custom_call_target="tpu_custom_call" | custom-call | flops 1000 | bytes 1000 | tf_op jit(solution)/shard_map/pallas_call | solution.py:49
  111.1 6.5 %shard_map.116 = (f32[256,512]{1,0:T(8,128)S(1)}, f32[256,512]{1,0:T(8,128)S(1)}, f32[512,256]{1,0:T(8,128)S(1)}, f32[512,256]{1,0:T(8,128)}, f32[512,512]{1,0:T(8,128)}, /*index=5*/f32[512,512]{1,0:T(8,128)}) custom-call(s32[4]{0:T(128)S(1)} %copy-done.16, bf16[512,1024]{1,0:T(8,128)(2,1)} %get-tuple-element.97.act_ref.refs_4_.refs_0_, ...), custom_call_target="tpu_custom_call" | custom-call | flops 1000 | bytes 1000 | tf_op jit(solution)/shard_map/pallas_call | solution.py:49
  117.7 1.2 copy-done.11
  118.9 1.2 copy-done.12
  120.1 1.8 shard_map.117
  121.9 0.8 collective-permute-start.7
  122.7 0.6 collective-permute-start.6
  123.3 1.3 collective-permute-done.8
  124.5 10.0 %collective-permute-done.7.far_b = bf16[512,512]{1,0:T(8,128)(2,1)S(1)} collective-permute-done((bf16[512,512]{1,0:T(8,128)(2,1)S(1)}, bf16[512,512]{1,0:T(8,128)(2,1)S(1)}, u32[]{:S(2)}, u32[]{:S(2)}) %collective-permute-start.7) | collective-permute-done | bytes 524320 | tf_op jit(solution)/shard_map/ppermute | solution.py:36
  134.6 1.6 collective-permute-done.6.far_a
  136.2 1.9 %shard_map.118 = bf16[8,64,1024]{2,1,0:T(8,128)(2,1)S(1)} custom-call(s32[4]{0:T(128)S(1)} %copy-done.16, f32[256,512]{1,0:T(8,128)S(1)} %get-tuple-element.120.out_a, f32[256,512]{1,0:T(8,128)S(1)} %get-tuple-element.121.out_b, f32[512,256]{1,0:T(8,128)S(1)} %get-tuple-element.122.in_a, f32[512,256]{1,0:T(8,128)S(1)} %copy-done.17, ...), custom_call_target="tpu_custom_call" | custom-call | flops 28000000000 | bytes 1000 | tf_op jit(solution)/shard_map/pallas_call | solution.py:49
  138.1 1.0 copy-done.13
  139.1 7.7 %all-to-all-start.4 = ((bf16[8,64,1024]{2,1,0:T(8,128)(2,1)}), bf16[8,64,1024]{2,1,0:T(8,128)(2,1)}, u32[]{:S(2)}, u32[]{:S(2)}) async-start(bf16[8,64,1024]{2,1,0:T(8,128)(2,1)} %copy-done.13), calls=%async_computation.4 | async-start | bytes 2097152 | tf_op jit(solution)/shard_map/all_to_all | solution.py:40
  146.8 2.1 %collective-permute-start.11 = (f32[8,2048]{1,0:T(8,128)S(1)}, f32[8,2048]{1,0:T(8,128)S(1)}, u32[]{:S(2)}, u32[]{:S(2)}) collective-permute-start(f32[8,2048]{1,0:T(8,128)S(1)} %add.73), channel_id=1, source_target_pairs={{0,4},{2,6},{4,0},{6,2},{1,5},{3,7},{5,1},{7,3},{8,12},{10,14},{12... | collective-permute-start | bytes 196616 | tf_op jit(solution)/shard_map/ppermute | solution.py:36
  148.9 2.6 %collective-permute-start.9 = (f32[8,2048]{1,0:T(8,128)S(1)}, f32[8,2048]{1,0:T(8,128)S(1)}, u32[]{:S(2)}, u32[]{:S(2)}) collective-permute-start(f32[8,2048]{1,0:T(8,128)S(1)} %add.73), channel_id=1, source_target_pairs={{0,2},{2,0},{4,6},{6,4},{1,3},{3,1},{5,7},{7,5},{8,10},{10,8},{12,... | collective-permute-start | bytes 196616 | tf_op jit(solution)/shard_map/ppermute | solution.py:36
  151.5 1.0 copy-done.10
  152.6 2.5 %shard_map.119 = bf16[256,2048]{1,0:T(8,128)(2,1)} custom-call(s32[4]{0:T(128)S(1)} %copy-done.16, bf16[512,256]{1,0:T(8,128)(2,1)S(1)} %copy-done.7, bf16[512,2048]{1,0:T(8,128)(2,1)S(1)} %bitcast.42, bf16[256,128]{1,0:T(8,128)(2,1)S(1)} %copy-done.14, bf16[2048,128]{1,0:T(8,128)(2,1)S(1)} %copy-done.10), custom_call_target="tpu_custom_call" | custom-call | flops 1000 | bytes 1000 | tf_op jit(solution)/shard_map/pallas_call | solution.py:49
  155.1 0.7 collective-permute-start.14
  155.8 2.2 %collective-permute-start.13 = (f32[8,2048]{1,0:T(8,128)S(1)}, f32[8,2048]{1,0:T(8,128)S(1)}, u32[]{:S(2)}, u32[]{:S(2)}) collective-permute-start(f32[8,2048]{1,0:T(8,128)S(1)} %add_add_fusion.2), channel_id=1, source_target_pairs={{0,192},{64,128},{128,64},{192,0},{1,193},{65,129},{129,65},{193,1... | collective-permute-start | bytes 196616 | tf_op jit(solution)/shard_map/ppermute | solution.py:36
  158.0 0.7 collective-permute-start.12
  158.7 2.9 %collective-permute-done.14 = f32[8,2048]{1,0:T(8,128)S(1)} collective-permute-done((f32[8,2048]{1,0:T(8,128)S(1)}, f32[8,2048]{1,0:T(8,128)S(1)}, u32[]{:S(2)}, u32[]{:S(2)}) %collective-permute-start.14) | collective-permute-done | bytes 65568 | tf_op jit(solution)/shard_map/ppermute | solution.py:36
  161.8 0.4 collective-permute-done.12
  162.3 1.6 collective-permute-start.15
  163.8 9.9 %collective-permute-done.15 = f32[8,2048]{1,0:T(8,128)S(1)} collective-permute-done((f32[8,2048]{1,0:T(8,128)S(1)}, f32[8,2048]{1,0:T(8,128)S(1)}, u32[]{:S(2)}, u32[]{:S(2)}) %collective-permute-start.15) | collective-permute-done | bytes 65568 | tf_op jit(solution)/shard_map/ppermute | solution.py:36
  173.8 4.8 %collective-permute-start.18 = (f32[8,2048]{1,0:T(8,128)S(1)}, f32[8,2048]{1,0:T(8,128)S(1)}, u32[]{:S(2)}, u32[]{:S(2)}) collective-permute-start(f32[8,2048]{1,0:T(8,128)S(1)} %add.80), channel_id=1, source_target_pairs={{0,32},{16,48},{32,0},{48,16},{1,33},{17,49},{33,1},{49,17},{2,34}... | collective-permute-start | bytes 196616 | tf_op jit(solution)/shard_map/ppermute | solution.py:36
  178.7 1.7 collective-permute-start.16
  180.4 1.7 collective-permute-done.18
  182.0 2.9 %collective-permute-done.17 = f32[8,2048]{1,0:T(8,128)S(1)} collective-permute-done((f32[8,2048]{1,0:T(8,128)S(1)}, f32[8,2048]{1,0:T(8,128)S(1)}, u32[]{:S(2)}, u32[]{:S(2)}) %collective-permute-start.17) | collective-permute-done | bytes 65568 | tf_op jit(solution)/shard_map/ppermute | solution.py:36
  185.0 0.6 add_add_fusion
  185.6 2.1 %shard_map.120 = (f32[32,2048]{1,0:T(8,128)}, f32[64,1024]{1,0:T(8,128)}) custom-call(s32[4]{0:T(128)S(1)} %copy-done.16, bf16[8,64,1024]{2,1,0:T(8,128)(2,1)} %all-to-all-done.4.got), custom_call_target="tpu_custom_call" | custom-call | flops 1000 | bytes 1000 | tf_op jit(solution)/shard_map/pallas_call | solution.py:49
  (82 shorter events, 1.2 us)
Async XLA Ops:
  0.6 14.2 %copy-start = (bf16[256,2048]{1,0:T(8,128)(2,1)S(1)}, bf16[256,2048]{1,0:T(8,128)(2,1)}, u32[]{:S(2)}) copy-start(bf16[256,2048]{1,0:T(8,128)(2,1)} %param.9) | copy-start | bytes 3145732
  1.5 13.4 %copy-start.25 = (pred[256]{0:T(512)(128)(4,1)}, pred[256]{0:T(512)(128)(4,1)S(1)}, u32[]{:S(2)}) copy-start(pred[256]{0:T(512)(128)(4,1)S(1)} %get-tuple-element.148) | copy-start | bytes 772
  1.5 13.4 %copy-start.26 = (pred[256]{0:T(512)(128)(4,1)}, pred[256]{0:T(512)(128)(4,1)S(1)}, u32[]{:S(2)}) copy-start(pred[256]{0:T(512)(128)(4,1)S(1)} %get-tuple-element.149) | copy-start | bytes 772
  2.2 12.7 %copy-start.23 = (s32[256,1]{0,1:T(1,128)}, s32[256,1]{0,1:T(1,128)S(1)}, u32[]{:S(2)}) copy-start(s32[256,1]{0,1:T(1,128)S(1)} %get-tuple-element.155) | copy-start | bytes 3076
  5.6 6.3 %copy-start.21 = (s32[256,2]{0,1:T(2,128)S(1)}, s32[256,2]{0,1:T(2,128)}, u32[]{:S(2)}) copy-start(s32[256,2]{0,1:T(2,128)} %param.15) | copy-start | bytes 6148
  5.6 6.3 %copy-start.19 = (bf16[2048,8]{0,1:T(8,128)(2,1)S(1)}, bf16[2048,8]{0,1:T(8,128)(2,1)}, u32[]{:S(2)}) copy-start(bf16[2048,8]{0,1:T(8,128)(2,1)} %param.10) | copy-start | bytes 98308
  5.6 8.3 %copy-start.22 = (s32[256,2]{0,1:T(2,128)S(1)}, s32[256,2]{0,1:T(2,128)}, u32[]{:S(2)}) copy-start(s32[256,2]{0,1:T(2,128)} %param.13) | copy-start | bytes 6148
  5.6 31.5 %all-to-all-start.1 = ((bf16[8,64,2048]{2,1,0:T(8,128)(2,1)}), bf16[8,64,2048]{2,1,0:T(8,128)(2,1)S(1)}, u32[]{:S(2)}, u32[]{:S(2)}) async-start(bf16[8,64,2048]{2,1,0:T(8,128)(2,1)} %bitcast.45), calls=%async_computation.1 | async-start | bytes 4194304 | tf_op jit(solution)/shard_map/all_to_all | solution.py:40
  13.9 0.6 copy-start.24
  37.1 1.3 copy-start.1
  38.4 31.3 %all-to-all-start = ((bf16[8,64,2176]{2,1,0:T(8,128)(2,1)}), bf16[8,64,2176]{2,1,0:T(8,128)(2,1)S(1)}, u32[]{:S(2)}, u32[]{:S(2)}) async-start(bf16[8,64,2176]{2,1,0:T(8,128)(2,1)} %bitcast.44), calls=%async_computation | async-start | bytes 4456448 | tf_op jit(solution)/shard_map/all_to_all | solution.py:40
  43.7 26.0 %collective-permute-start = (bf16[512,2048]{1,0:T(8,128)(2,1)}, bf16[512,2048]{1,0:T(8,128)(2,1)}, u32[]{:S(2)}, u32[]{:S(2)}) collective-permute-start(bf16[512,2048]{1,0:T(8,128)(2,1)} %bitcast.38), channel_id=1, source_target_pairs={{0,8},{8,0},{1,9},{9,1},{2,10},{10,2},{3,11},{11,3},{4,12},{12,4},... | collective-permute-start | bytes 6291464 | tf_op jit(solution)/shard_map/ppermute | solution.py:36
  51.3 18.4 %collective-permute-start.1 = (bf16[512,1024]{1,0:T(8,128)(2,1)}, bf16[512,1024]{1,0:T(8,128)(2,1)}, u32[]{:S(2)}, u32[]{:S(2)}) collective-permute-start(bf16[512,1024]{1,0:T(8,128)(2,1)} %get-tuple-element.97.act_ref.refs_4_.refs_0_), channel_id=1, source_target_pairs={{0,8},{8,0},{1,9},{9,1},{2,10},{10,2},{3,11},{11,3},{4,12},{12,4},... | collective-permute-start | bytes 3145736 | tf_op jit(solution)/shard_map/ppermute | solution.py:36
  57.2 22.7 %copy-start.15 = (s32[4]{0:T(128)}, s32[4]{0:T(128)S(1)}, u32[]{:S(2)}) copy-start(s32[4]{0:T(128)S(1)} %pad_add_fusion.pos_ref) | copy-start | bytes 52
  69.7 1.6 copy-start.8
  70.6 9.3 %copy-start.4 = (bf16[512,1024]{1,0:T(8,128)(2,1)}, bf16[512,1024]{1,0:T(8,128)(2,1)S(1)}, u32[]{:S(2)}) copy-start(bf16[512,1024]{1,0:T(8,128)(2,1)S(1)} %get-tuple-element.101.refs_0_.refs_4_) | copy-start | bytes 3145732
  70.7 9.3 %collective-permute-start.2 = (bf16[512,1024]{1,0:T(8,128)(2,1)S(1)}, bf16[512,1024]{1,0:T(8,128)(2,1)S(1)}, u32[]{:S(2)}, u32[]{:S(2)}) collective-permute-start(bf16[512,1024]{1,0:T(8,128)(2,1)S(1)} %get-tuple-element.77), channel_id=1, source_target_pairs={{0,8},{8,0},{1,9},{9,1},{2,10},{10,2},{3,11},{11,3},{4,12},{12,4},... | collective-permute-start | bytes 3145736 | tf_op jit(solution)/shard_map/ppermute | solution.py:36
  71.3 2.2 %copy-start.6 = (bf16[1,1024,2048]{2,1,0:T(8,128)(2,1)S(1)}, bf16[1,1024,2048]{2,1,0:T(8,128)(2,1)}, u32[]{:S(2)}) copy-start(bf16[1,1024,2048]{2,1,0:T(8,128)(2,1)} %param.12) | copy-start | bytes 12582916
  73.5 6.5 %copy-start.2 = (bf16[8,64,2048]{2,1,0:T(8,128)(2,1)S(1)}, bf16[8,64,2048]{2,1,0:T(8,128)(2,1)}, u32[]{:S(2)}) copy-start(bf16[8,64,2048]{2,1,0:T(8,128)(2,1)} %copy-done.1) | copy-start | bytes 6291460
  78.0 7.6 %copy-start.3 = (bf16[512,1024]{1,0:T(8,128)(2,1)}, bf16[512,1024]{1,0:T(8,128)(2,1)S(1)}, u32[]{:S(2)}) copy-start(bf16[512,1024]{1,0:T(8,128)(2,1)S(1)} %get-tuple-element.103.refs_2_.grad.refs_6_) | copy-start | bytes 3145732
  78.0 1.9 %collective-permute-start.3 = (bf16[512,512]{1,0:T(8,128)(2,1)S(1)}, bf16[512,512]{1,0:T(8,128)(2,1)S(1)}, u32[]{:S(2)}, u32[]{:S(2)}) collective-permute-start(bf16[512,512]{1,0:T(8,128)(2,1)S(1)} %get-tuple-element.84), channel_id=1, source_target_pairs={{0,8},{8,0},{1,9},{9,1},{2,10},{10,2},{3,11},{11,3},{4,12},{12,4},... | collective-permute-start | bytes 1572872 | tf_op jit(solution)/shard_map/ppermute | solution.py:36
  79.9 5.7 %copy-start.9 = (bf16[512,512]{1,0:T(8,128)(2,1)}, bf16[512,512]{1,0:T(8,128)(2,1)S(1)}, u32[]{:S(2)}) copy-start(bf16[512,512]{1,0:T(8,128)(2,1)S(1)} %collective-permute-done.3.refs_3_.refs_7_) | copy-start | bytes 1572868
  79.9 5.7 %copy-start.5 = (bf16[512,1024]{1,0:T(8,128)(2,1)}, bf16[512,1024]{1,0:T(8,128)(2,1)S(1)}, u32[]{:S(2)}) copy-start(bf16[512,1024]{1,0:T(8,128)(2,1)S(1)} %collective-permute-done.2.refs_1_.refs_5_) | copy-start | bytes 3145732
  85.6 32.0 %collective-permute-start.4 = (bf16[1024,512]{1,0:T(8,128)(2,1)}, bf16[1024,512]{1,0:T(8,128)(2,1)}, u32[]{:S(2)}, u32[]{:S(2)}) collective-permute-start(bf16[1024,512]{1,0:T(8,128)(2,1)} %get-tuple-element.88), channel_id=1, source_target_pairs={{0,64},{64,0},{128,192},{192,128},{1,65},{65,1},{129,193},{193,129... | collective-permute-start | bytes 3145736 | tf_op jit(solution)/shard_map/ppermute | solution.py:36
  87.3 30.3 %collective-permute-start.5 = (bf16[1024,512]{1,0:T(8,128)(2,1)}, bf16[1024,512]{1,0:T(8,128)(2,1)}, u32[]{:S(2)}, u32[]{:S(2)}) collective-permute-start(bf16[1024,512]{1,0:T(8,128)(2,1)} %get-tuple-element.89), channel_id=1, source_target_pairs={{0,192},{64,128},{128,64},{192,0},{1,193},{65,129},{129,65},{193,1... | collective-permute-start | bytes 3145736 | tf_op jit(solution)/shard_map/ppermute | solution.py:36
  89.5 11.9 %all-to-all-start.2 = ((bf16[8,64,128]{2,1,0:T(8,128)(2,1)}), bf16[8,64,128]{2,1,0:T(8,128)(2,1)S(1)}, u32[]{:S(2)}, u32[]{:S(2)}) async-start(bf16[8,64,128]{2,1,0:T(8,128)(2,1)} %bitcast.16), calls=%async_computation.2 | async-start | bytes 262144 | tf_op jit(solution)/shard_map/all_to_all | solution.py:40
  101.4 0.7 copy-start.18
  101.4 9.7 %copy-start.16 = (s32[4]{0:T(128)S(1)}, s32[4]{0:T(128)}, u32[]{:S(2)}) copy-start(s32[4]{0:T(128)} %copy-done.15) | copy-start | bytes 52
  102.0 37.1 %all-to-all-start.3 = ((bf16[8,64,2048]{2,1,0:T(8,128)(2,1)}), bf16[8,64,2048]{2,1,0:T(8,128)(2,1)S(1)}, u32[]{:S(2)}, u32[]{:S(2)}) async-start(bf16[8,64,2048]{2,1,0:T(8,128)(2,1)} %bitcast.46), calls=%async_computation.3 | async-start | bytes 4194304 | tf_op jit(solution)/shard_map/all_to_all | solution.py:40
  117.7 1.2 copy-start.11
  118.9 1.2 copy-start.12
  120.1 3.2 %copy-start.20 = (f32[8,2048]{1,0:T(8,128)S(1)}, f32[8,2048]{1,0:T(8,128)}, u32[]{:S(2)}) copy-start(f32[8,2048]{1,0:T(8,128)} %get-tuple-element.117) | copy-start | bytes 196612
  120.1 16.1 %copy-start.17 = (f32[512,256]{1,0:T(8,128)S(1)}, f32[512,256]{1,0:T(8,128)}, u32[]{:S(2)}) copy-start(f32[512,256]{1,0:T(8,128)} %get-tuple-element.123.in_b) | copy-start | bytes 1572868
  121.9 12.7 %collective-permute-start.7 = (bf16[512,512]{1,0:T(8,128)(2,1)S(1)}, bf16[512,512]{1,0:T(8,128)(2,1)S(1)}, u32[]{:S(2)}, u32[]{:S(2)}) collective-permute-start(bf16[512,512]{1,0:T(8,128)(2,1)S(1)} %get-tuple-element.116), channel_id=1, source_target_pairs={{0,64},{64,0},{128,192},{192,128},{1,65},{65,1},{129,193},{193,129... | collective-permute-start | bytes 1572872 | tf_op jit(solution)/shard_map/ppermute | solution.py:36
  122.7 13.5 %collective-permute-start.6 = (bf16[512,512]{1,0:T(8,128)(2,1)S(1)}, bf16[512,512]{1,0:T(8,128)(2,1)S(1)}, u32[]{:S(2)}, u32[]{:S(2)}) collective-permute-start(bf16[512,512]{1,0:T(8,128)(2,1)S(1)} %get-tuple-element.115), channel_id=1, source_target_pairs={{0,192},{64,128},{128,64},{192,0},{1,193},{65,129},{129,65},{193,1... | collective-permute-start | bytes 1572872 | tf_op jit(solution)/shard_map/ppermute | solution.py:36
  123.3 1.3 collective-permute-start.8
  138.1 1.0 copy-start.13
  139.1 12.4 %copy-start.7 = (bf16[512,256]{1,0:T(8,128)(2,1)S(1)}, bf16[512,256]{1,0:T(8,128)(2,1)}, u32[]{:S(2)}) copy-start(bf16[512,256]{1,0:T(8,128)(2,1)} %fusion.12.disp) | copy-start | bytes 786436
  139.1 12.4 %copy-start.14 = (bf16[256,128]{1,0:T(8,128)(2,1)S(1)}, bf16[256,128]{1,0:T(8,128)(2,1)}, u32[]{:S(2)}) copy-start(bf16[256,128]{1,0:T(8,128)(2,1)} %get-tuple-element.127.logit) | copy-start | bytes 196612
  139.1 46.5 %all-to-all-start.4 = ((bf16[8,64,1024]{2,1,0:T(8,128)(2,1)}), bf16[8,64,1024]{2,1,0:T(8,128)(2,1)}, u32[]{:S(2)}, u32[]{:S(2)}) async-start(bf16[8,64,1024]{2,1,0:T(8,128)(2,1)} %copy-done.13), calls=%async_computation.4 | async-start | bytes 2097152 | tf_op jit(solution)/shard_map/all_to_all | solution.py:40
  146.8 8.3 %collective-permute-start.11 = (f32[8,2048]{1,0:T(8,128)S(1)}, f32[8,2048]{1,0:T(8,128)S(1)}, u32[]{:S(2)}, u32[]{:S(2)}) collective-permute-start(f32[8,2048]{1,0:T(8,128)S(1)} %add.73), channel_id=1, source_target_pairs={{0,4},{2,6},{4,0},{6,2},{1,5},{3,7},{5,1},{7,3},{8,12},{10,14},{12... | collective-permute-start | bytes 196616 | tf_op jit(solution)/shard_map/ppermute | solution.py:36
  148.9 6.2 %collective-permute-start.10 = (f32[8,2048]{1,0:T(8,128)S(1)}, f32[8,2048]{1,0:T(8,128)S(1)}, u32[]{:S(2)}, u32[]{:S(2)}) collective-permute-start(f32[8,2048]{1,0:T(8,128)S(1)} %add.73), channel_id=1, source_target_pairs={{0,6},{2,4},{4,2},{6,0},{1,7},{3,5},{5,3},{7,1},{8,14},{10,12},{12... | collective-permute-start | bytes 196616 | tf_op jit(solution)/shard_map/ppermute | solution.py:36
  148.9 6.2 %collective-permute-start.9 = (f32[8,2048]{1,0:T(8,128)S(1)}, f32[8,2048]{1,0:T(8,128)S(1)}, u32[]{:S(2)}, u32[]{:S(2)}) collective-permute-start(f32[8,2048]{1,0:T(8,128)S(1)} %add.73), channel_id=1, source_target_pairs={{0,2},{2,0},{4,6},{6,4},{1,3},{3,1},{5,7},{7,5},{8,10},{10,8},{12,... | collective-permute-start | bytes 196616 | tf_op jit(solution)/shard_map/ppermute | solution.py:36
  151.5 1.0 copy-start.10
  155.1 6.5 %collective-permute-start.14 = (f32[8,2048]{1,0:T(8,128)S(1)}, f32[8,2048]{1,0:T(8,128)S(1)}, u32[]{:S(2)}, u32[]{:S(2)}) collective-permute-start(f32[8,2048]{1,0:T(8,128)S(1)} %add_add_fusion.2), channel_id=1, source_target_pairs={{0,128},{64,192},{128,0},{192,64},{1,129},{65,193},{129,1},{193,65... | collective-permute-start | bytes 196616 | tf_op jit(solution)/shard_map/ppermute | solution.py:36
  155.8 6.0 %collective-permute-start.13 = (f32[8,2048]{1,0:T(8,128)S(1)}, f32[8,2048]{1,0:T(8,128)S(1)}, u32[]{:S(2)}, u32[]{:S(2)}) collective-permute-start(f32[8,2048]{1,0:T(8,128)S(1)} %add_add_fusion.2), channel_id=1, source_target_pairs={{0,192},{64,128},{128,64},{192,0},{1,193},{65,129},{129,65},{193,1... | collective-permute-start | bytes 196616 | tf_op jit(solution)/shard_map/ppermute | solution.py:36
  158.0 4.3 %collective-permute-start.12 = (f32[8,2048]{1,0:T(8,128)S(1)}, f32[8,2048]{1,0:T(8,128)S(1)}, u32[]{:S(2)}, u32[]{:S(2)}) collective-permute-start(f32[8,2048]{1,0:T(8,128)S(1)} %add_add_fusion.2), channel_id=1, source_target_pairs={{0,64},{64,0},{128,192},{192,128},{1,65},{65,1},{129,193},{193,129... | collective-permute-start | bytes 196616 | tf_op jit(solution)/shard_map/ppermute | solution.py:36
  162.3 11.5 %collective-permute-start.15 = (f32[8,2048]{1,0:T(8,128)S(1)}, f32[8,2048]{1,0:T(8,128)S(1)}, u32[]{:S(2)}, u32[]{:S(2)}) collective-permute-start(f32[8,2048]{1,0:T(8,128)S(1)} %add_add_fusion.1), channel_id=1, source_target_pairs={{0,1},{1,0},{2,3},{3,2},{4,5},{5,4},{6,7},{7,6},{8,9},{9,8},{10,11... | collective-permute-start | bytes 196616 | tf_op jit(solution)/shard_map/ppermute | solution.py:36
  173.8 8.3 %collective-permute-start.18 = (f32[8,2048]{1,0:T(8,128)S(1)}, f32[8,2048]{1,0:T(8,128)S(1)}, u32[]{:S(2)}, u32[]{:S(2)}) collective-permute-start(f32[8,2048]{1,0:T(8,128)S(1)} %add.80), channel_id=1, source_target_pairs={{0,32},{16,48},{32,0},{48,16},{1,33},{17,49},{33,1},{49,17},{2,34}... | collective-permute-start | bytes 196616 | tf_op jit(solution)/shard_map/ppermute | solution.py:36
  178.6 6.4 %collective-permute-start.17 = (f32[8,2048]{1,0:T(8,128)S(1)}, f32[8,2048]{1,0:T(8,128)S(1)}, u32[]{:S(2)}, u32[]{:S(2)}) collective-permute-start(f32[8,2048]{1,0:T(8,128)S(1)} %add.80), channel_id=1, source_target_pairs={{0,48},{16,32},{32,16},{48,0},{1,49},{17,33},{33,17},{49,1},{2,50}... | collective-permute-start | bytes 196616 | tf_op jit(solution)/shard_map/ppermute | solution.py:36
  178.7 6.3 %collective-permute-start.16 = (f32[8,2048]{1,0:T(8,128)S(1)}, f32[8,2048]{1,0:T(8,128)S(1)}, u32[]{:S(2)}, u32[]{:S(2)}) collective-permute-start(f32[8,2048]{1,0:T(8,128)S(1)} %add.80), channel_id=1, source_target_pairs={{0,16},{16,0},{32,48},{48,32},{1,17},{17,1},{33,49},{49,33},{2,18}... | collective-permute-start | bytes 196616 | tf_op jit(solution)/shard_map/ppermute | solution.py:36

commit v11 on v10

--- a/solution.py
+++ b/solution.py
@@ -161,7 +161,7 @@
                 own = i * wide
                 if part and near:
                     own = pl.multiple_of((2 * pos_ref[1] + i) * wide, wide)
-                for j in range(2):
+                for j in range(len(masks[i])):
                     n = blocks.index(masks[i][j])
                     value = lax.dot_general(
                         buffers[part][0, n],
@@ -209,28 +209,33 @@
     return products(pos, *sides, ((1, 2), (3, 2)), store, outputs, True)
 
 
-def kept_parts(pos, left_out, right_out, left_in, right_in):
+def far_parts(pos, left_out, right_out, left_in, right_in):
     width_out, width_in = left_out[0].shape[1] // 4, left_in[0].shape[1] // 4
     cols_out, cols_in = right_out[1].shape[1] // 2, right_in[1].shape[1] // 2
     half = width_in // 2
 
     def store(outs, part, i, j, value):
-        near_out, near_in, far = outs[:2], outs[2:4], outs[4:]
-        if j == 0:
-            (near_in if part else near_out)[i][...] = value
-        elif part:
-            far[i][width_out:, :cols_in] = value[:half, :]
-            far[i][width_out:, cols_in:] = value[half:, :]
+        if part:
+            outs[i][width_out:, :cols_in] = value[:half, :]
+            outs[i][width_out:, cols_in:] = value[half:, :]
         else:
-            far[i][:width_out, :] = value
-
-    outputs = (
-        [((width_out, cols_out), F32)] * 2
-        + [((width_in, cols_in), F32)] * 2
-        + [((width_out + half, cols_out), F32)] * 2
-    )
+            outs[i][:width_out, :] = value
+
+    outputs = [((width_out + half, cols_out), F32)] * 2
     sides = (left_out, right_out, left_in, right_in)
-    return products(pos, *sides, ((0, 3), (0, 1)), store, outputs, False)
+    return products(pos, *sides, ((3,), (1,)), store, outputs, False)
+
+
+def near_parts(pos, left_out, right_out, left_in, right_in):
+    width_out, width_in = left_out[0].shape[1] // 4, left_in[0].shape[1] // 4
+    cols_out, cols_in = right_out[1].shape[1] // 2, right_in[1].shape[1] // 2
+
+    def store(outs, part, i, j, value):
+        outs[2 * part + i][...] = value
+
+    outputs = [((width_out, cols_out), F32)] * 2 + [((width_in, cols_in), F32)] * 2
+    sides = (left_out, right_out, left_in, right_in)
+    return products(pos, *sides, ((0,), (0,)), store, outputs, False)
 
 
 def far_sums(pos, far, got):
@@ -483,13 +488,15 @@
     left_in, left_out, right_in, right_out, _ = tie(
         left_in, left_out, right_in, right_out, router_part
     )
-    *near, far_a, far_b = kept_parts(pos, left_out, right_out, left_in, right_in)
+    far_a, far_b = far_parts(pos, left_out, right_out, left_in, right_in)
     got, far_a, far_b = tie(got, far_a, far_b)
     far_a, far_b = far_sums(pos, (far_a, far_b), got)
     far = (swap(far_a, "y", 3), swap(far_b, "y", 1))
-    other_router = swap(router_part, "core", 1)
-    router_part, other_router, _ = tie(router_part, other_router, far_a)
-    router_part = router_part + other_router
+    left_in, left_out, right_in, right_out, _ = tie(
+        left_in, left_out, right_in, right_out, far_a
+    )
+    near = near_parts(pos, left_out, right_out, left_in, right_in)
+    router_part = router_round(router_part, "zh", 1, 3, near)
 
     near, far, router_part = tie(near, far, router_part)
     pieces = zh_pieces(pos, near[:2], near[2:], got, far, grad_scale)
@@ -499,8 +506,8 @@
     grad_tokens = token_grads(pos, dispatch, back, logit_lanes, weight_lanes)
     router_part = router_round(router_part, "x", 1, 3, grad_tokens)
     router_part = router_round(router_part, "y", 1, 3)
+    router_part = router_part + swap(router_part, "core", 1)
     router_part = router_part + swap(router_part, "zl", 1)
-    router_part = router_round(router_part, "zh", 1, 3)
     got, router_part = tie(got, router_part)
     outer_share, inner_share = shares(pos, got, near[0].shape[0] // 8)
     return (grad_tokens, router_part.T, inner_share, outer_share)

time: 189 us -> 184 us (0.974)
  Pallas kernels: 36.2 us -> 41.1 us
  local copies, waits for them, and re-layouts: 16.4 us -> 12.2 us
  waiting for transfers between devices: 61.1 us -> 57.7 us
    ppermute x19, waiting for transfers between devices: 32.9 us -> 24 us  [swap(): return lax.ppermute(values, axis, [(i, i ^ mask) for i in range(size)])]
    all_to_all x5, waiting for transfers between devices: 28.2 us -> 33.7 us  [exchange(): return lax.all_to_all(values, axes, split_axis=0, concat_axis=0, tiled=True)]
    pallas_call x10 -> x11, Pallas kernels: 36.2 us -> 41.1 us  [call(): pl.pallas_call(body, in_specs=[pl.BlockSpec(memory_space=pltpu.SMEM)] + [...]
    all_to_all x5, starting transfers between devices: 30.1 us -> 27.8 us  [exchange(): return lax.all_to_all(values, axes, split_axis=0, concat_axis=0, tiled=True)]
    unnamed x55 -> x53, local copies, waits for them, and re-layouts: 11 us -> 9.01 us
  transfers between devices with their start and end apart: 24 -> 24, of which waited for: 12 -> 13; matrix products, arithmetic and copies ran while one was open for 12% -> 10% of each run, Pallas kernels for 15% -> 17%
where the time goes in v11:
time: 184 us; the launch traced here: 183 us
  waiting for transfers between devices  57.7 us (31%)
  starting transfers between devices  51.4 us (28%)
  Pallas kernels  41.1 us (22%)
  matrix products  12.5 us (7%)
  local copies, waits for them, and re-layouts  12.2 us (7%)
  other arithmetic  6.51 us (4%)
    pallas_call x11, Pallas kernels, call(): pl.pallas_call(body, in_specs=[pl.BlockSpec(memory_space=pltpu.SMEM)] + [...  41.1 us
    all_to_all x5, waiting for transfers between devices, exchange(): return lax.all_to_all(values, axes, split_axis=0, concat_axis=0, tiled=True)  33.7 us
    all_to_all x5, starting transfers between devices, exchange(): return lax.all_to_all(values, axes, split_axis=0, concat_axis=0, tiled=True)  27.8 us
    ppermute x19, waiting for transfers between devices, swap(): return lax.ppermute(values, axis, [(i, i ^ mask) for i in range(size)])  24 us
    ppermute x19, starting transfers between devices, swap(): return lax.ppermute(values, axis, [(i, i ^ mask) for i in range(size)])  23.6 us
    unnamed x53, local copies, waits for them, and re-layouts  9.01 us
    dot_general x1, matrix products, per_device(): hidden_pre = jnp.dot(slot_tokens, weight_in, preferred_element_type=F32)  6.49 us
  transfers between devices with their start and end apart: 24, of which 13 were waited for; matrix products, arithmetic and copies ran while one was open for 10% of the time, Pallas kernels for 17%

profile of v11, /device:TPU:2, one launch (start us, length us, event | category | flops | bytes accessed | tf_op | source)
XLA Modules:
  0.0 182.5 jit_solution(17143905264769129578)
XLA Ops:
  0.6 0.8 multiply_add_fusion
  1.4 0.8 compare_reduce_fusion.1
  2.2 3.3 %convolution_convert_fusion = bf16[512,2048]{1,0:T(8,128)(2,1)} fusion(bf16[256,2048]{1,0:T(8,128)(2,1)} %tok.1, s32[256]{0:T(256)S(1)} %bitcast.53, s32[256]{0:T(256)S(1)} %bitcast.49, pred[256]{0:T(512)(128)(4,1)S(1)} %get-tuple-element.161, pred[256]{0:T(512)(128)(4,1)S(1)} %get-tuple-element.160), kind=kOutput, calls=%fused_computation.1 | convolution fusion | flops 538574848 | bytes 3148288 | tf_op jit(solution)/shard_map/dot_general | solution.py:406
  5.6 6.3 %all-to-all-start.1 = ((bf16[8,64,2048]{2,1,0:T(8,128)(2,1)}), bf16[8,64,2048]{2,1,0:T(8,128)(2,1)S(1)}, u32[]{:S(2)}, u32[]{:S(2)}) async-start(bf16[8,64,2048]{2,1,0:T(8,128)(2,1)} %bitcast.44), calls=%async_computation.1 | async-start | bytes 4194304 | tf_op jit(solution)/shard_map/all_to_all | solution.py:40
  11.9 1.6 fusion.17
  13.9 0.6 copy-done.23
  14.5 0.3 convolution_convert_fusion.2
  14.8 0.7 convolution_convert_fusion.1
  15.6 1.6 pad_maximum_fusion
  17.2 19.9 %all-to-all-done.1 = bf16[8,64,2048]{2,1,0:T(8,128)(2,1)S(1)} async-done(((bf16[8,64,2048]{2,1,0:T(8,128)(2,1)}), bf16[8,64,2048]{2,1,0:T(8,128)(2,1)S(1)}, u32[]{:S(2)}, u32[]{:S(2)}) %all-to-all-start.1) | async-done | bytes 2097184 | tf_op jit(solution)/shard_map/all_to_all | solution.py:40
  37.1 6.0 %all-to-all-start = ((bf16[8,64,2176]{2,1,0:T(8,128)(2,1)}), bf16[8,64,2176]{2,1,0:T(8,128)(2,1)}, u32[]{:S(2)}, u32[]{:S(2)}) async-start(bf16[8,64,2176]{2,1,0:T(8,128)(2,1)} %bitcast.43), calls=%async_computation | async-start | bytes 4456448 | tf_op jit(solution)/shard_map/all_to_all | solution.py:40
  43.1 6.5 %fusion.3 = (f32[512,1024]{1,0:T(8,128)}, bf16[512,1024]{1,0:T(8,128)(2,1)}) fusion(bf16[512,2048]{1,0:T(8,128)(2,1)S(1)} %bitcast.37, bf16[1,2048,1024]{2,1,0:T(8,128)(2,1)} %param.11), kind=kOutput, calls=%fused_computation.7 | convolution fusion | flops 2152726528 | bytes 9437184 | tf_op jit(solution)/shard_map/dot_general | solution.py:445
  49.6 0.5 collective-permute-start.1
  50.1 1.0 copy.27
  51.4 1.9 %pad.22.weight = bf16[2048,128]{1,0:T(8,128)(2,1)} pad(bf16[2048,8]{1,0:T(8,128)(2,1)} %copy.27, bf16[]{:T(256)} %constant.38.clone.1), padding=0_0x0_120 | pad | bytes 557058 | tf_op jit(solution)/shard_map/jit(_pad)/pad | solution.py:420
  53.5 0.8 broadcast_in_dim.52
  54.3 0.8 pad_maximum_fusion.1.side
  55.1 1.6 fusion.12.disp
  56.7 12.0 %all-to-all-done = bf16[8,64,2176]{2,1,0:T(8,128)(2,1)} async-done(((bf16[8,64,2176]{2,1,0:T(8,128)(2,1)}), bf16[8,64,2176]{2,1,0:T(8,128)(2,1)}, u32[]{:S(2)}, u32[]{:S(2)}) %all-to-all-start) | async-done | bytes 2228256 | tf_op jit(solution)/shard_map/all_to_all | solution.py:40
  68.6 2.2 %shard_map.111 = (bf16[512,1024]{1,0:T(8,128)(2,1)S(1)}, bf16[512,1024]{1,0:T(8,128)(2,1)S(1)}) custom-call(s32[4]{0:T(128)S(1)} %pad_add_fusion.pos_ref, bf16[512,2176]{1,0:T(8,128)(2,1)} %bitcast.7.rec), custom_call_target="tpu_custom_call" | custom-call | flops 1000 | bytes 1000 | tf_op jit(solution)/shard_map/pallas_call | solution.py:49
  71.0 2.4 %copy-done.7 = bf16[1,1024,2048]{2,1,0:T(8,128)(2,1)S(1)} copy-done((bf16[1,1024,2048]{2,1,0:T(8,128)(2,1)S(1)}, bf16[1,1024,2048]{2,1,0:T(8,128)(2,1)}, u32[]{:S(2)}) %copy-start.7) | copy-done | bytes 4194328
  73.4 5.1 %shard_map.112 = (bf16[512,1024]{1,0:T(8,128)(2,1)S(1)}, bf16[512,512]{1,0:T(8,128)(2,1)S(1)}, bf16[512,128]{1,0:T(8,128)(2,1)}) custom-call(s32[4]{0:T(128)S(1)} %pad_add_fusion.pos_ref, bf16[512,2176]{1,0:T(8,128)(2,1)} %bitcast.7.rec, bf16[1024,2048]{1,0:T(8,128)(2,1)S(1)} %bitcast.42, bf16[512,1024]{1,0:T(8,128)(2,1)} %get-tuple-element.118.act_ref.refs_4_.refs_0_, ...), custom_call_target="tpu_custom_call" | custom-call | flops 1000 | bytes 1000 | tf_op jit(solution)/shard_map/pallas_call | solution.py:49
  78.7 1.7 collective-permute-done.3.refs_3_.refs_7_
  80.5 5.6 %shard_map.113 = (bf16[1024,512]{1,0:T(8,128)(2,1)}, bf16[1024,512]{1,0:T(8,128)(2,1)}) custom-call(s32[4]{0:T(128)S(1)} %pad_add_fusion.pos_ref, bf16[512,1024]{1,0:T(8,128)(2,1)S(1)} %get-tuple-element.122.refs_0_.refs_4_, bf16[512,1024]{1,0:T(8,128)(2,1)S(1)} %collective-permute-done.2.refs_1_.refs_5_, ...), custom_call_target="tpu_custom_call" | custom-call | flops 1000 | bytes 1000 | tf_op jit(solution)/shard_map/pallas_call | solution.py:49
  86.1 1.8 %collective-permute-start.4 = (bf16[1024,512]{1,0:T(8,128)(2,1)}, bf16[1024,512]{1,0:T(8,128)(2,1)}, u32[]{:S(2)}, u32[]{:S(2)}) collective-permute-start(bf16[1024,512]{1,0:T(8,128)(2,1)} %get-tuple-element.94), channel_id=1, source_target_pairs={{0,64},{64,0},{128,192},{192,128},{1,65},{65,1},{129,193},{193,129... | collective-permute-start | bytes 3145736 | tf_op jit(solution)/shard_map/ppermute | solution.py:36
  88.0 2.2 %collective-permute-start.5 = (bf16[1024,512]{1,0:T(8,128)(2,1)}, bf16[1024,512]{1,0:T(8,128)(2,1)}, u32[]{:S(2)}, u32[]{:S(2)}) collective-permute-start(bf16[1024,512]{1,0:T(8,128)(2,1)} %get-tuple-element.95), channel_id=1, source_target_pairs={{0,192},{64,128},{128,64},{192,0},{1,193},{65,129},{129,65},{193,1... | collective-permute-start | bytes 3145736 | tf_op jit(solution)/shard_map/ppermute | solution.py:36
  90.2 5.4 %all-to-all-start.2 = ((bf16[8,64,128]{2,1,0:T(8,128)(2,1)}), bf16[8,64,128]{2,1,0:T(8,128)(2,1)S(1)}, u32[]{:S(2)}, u32[]{:S(2)}) async-start(bf16[8,64,128]{2,1,0:T(8,128)(2,1)} %bitcast.16), calls=%async_computation.2 | async-start | bytes 262144 | tf_op jit(solution)/shard_map/all_to_all | solution.py:40
  95.6 6.8 %shard_map.114 = bf16[512,2048]{1,0:T(8,128)(2,1)} custom-call(s32[4]{0:T(128)} %copy-done.14, bf16[512,1024]{1,0:T(8,128)(2,1)} %copy-done.2, bf16[2048,1024]{1,0:T(8,128)(2,1)} %bitcast.46), custom_call_target="tpu_custom_call" | custom-call | flops 1000 | bytes 1000 | tf_op jit(solution)/shard_map/pallas_call | solution.py:49
  102.4 0.6 copy-done.17
  103.0 5.7 %all-to-all-start.3 = ((bf16[8,64,2048]{2,1,0:T(8,128)(2,1)}), bf16[8,64,2048]{2,1,0:T(8,128)(2,1)S(1)}, u32[]{:S(2)}, u32[]{:S(2)}) async-start(bf16[8,64,2048]{2,1,0:T(8,128)(2,1)} %bitcast.45), calls=%async_computation.3 | async-start | bytes 4194304 | tf_op jit(solution)/shard_map/all_to_all | solution.py:40
  108.8 3.4 %shard_map.115 = (bf16[256,128]{1,0:T(8,128)(2,1)}, f32[8,2048]{1,0:T(8,128)}) custom-call(s32[4]{0:T(128)} %copy-done.14, bf16[512,256]{1,0:T(8,128)(2,1)} %fusion.12.disp, bf16[512,128]{1,0:T(8,128)(2,1)} %bitcast.47, f32[4,256,128]{2,1,0:T(8,128)} %pad_maximum_fusion.1.side, bf16[256,2048]{1,0:T(8,128)(2,1)} %tok.1), custom_call_target="tpu_custom_call" | custom-call | flops 1000 | bytes 1000 | tf_op jit(solution)/shard_map/pallas_call | solution.py:49
  112.2 5.1 %shard_map.116 = (f32[512,512]{1,0:T(8,128)S(1)}, f32[512,512]{1,0:T(8,128)}) custom-call(s32[4]{0:T(128)S(1)} %copy-done.15, bf16[512,1024]{1,0:T(8,128)(2,1)} %get-tuple-element.118.act_ref.refs_4_.refs_0_, bf16[512,1024]{1,0:T(8,128)(2,1)} %collective-permute-done.1.refs_5_.refs_1_, bf16[512,2048]{1,0:T(8,128)(2,1)} %bitcast.39, ...), custom_call_target="tpu_custom_call" | custom-call | flops 1000 | bytes 1000 | tf_op jit(solution)/shard_map/pallas_call | solution.py:49
  117.3 1.2 copy-done.11
  118.5 1.8 shard_map.117
  120.3 1.1 collective-permute-start.6
  121.4 3.3 %collective-permute-start.8 = (f32[8,2048]{1,0:T(8,128)S(1)}, f32[8,2048]{1,0:T(8,128)S(1)}, u32[]{:S(2)}, u32[]{:S(2)}) collective-permute-start(f32[8,2048]{1,0:T(8,128)S(1)} %copy-done.19), channel_id=1, source_target_pairs={{0,16},{16,0},{32,48},{48,32},{1,17},{17,1},{33,49},{49,33},{2,18}... | collective-permute-start | bytes 196616 | tf_op jit(solution)/shard_map/ppermute | solution.py:36
  124.7 3.6 %collective-permute-start.9 = (f32[8,2048]{1,0:T(8,128)S(1)}, f32[8,2048]{1,0:T(8,128)S(1)}, u32[]{:S(2)}, u32[]{:S(2)}) collective-permute-start(f32[8,2048]{1,0:T(8,128)S(1)} %copy-done.19), channel_id=1, source_target_pairs={{0,48},{16,32},{32,16},{48,0},{1,49},{17,33},{33,17},{49,1},{2,50}... | collective-permute-start | bytes 196616 | tf_op jit(solution)/shard_map/ppermute | solution.py:36
  128.3 0.9 collective-permute-start.10
  129.2 4.6 %shard_map.118 = (f32[256,512]{1,0:T(8,128)S(1)}, f32[256,512]{1,0:T(8,128)S(1)}, f32[512,256]{1,0:T(8,128)S(1)}, f32[512,256]{1,0:T(8,128)}) custom-call(s32[4]{0:T(128)S(1)} %copy-done.15, bf16[512,1024]{1,0:T(8,128)(2,1)} %get-tuple-element.118.act_ref.refs_4_.refs_0_, bf16[512,1024]{1,0:T(8,128)(2,1)} %collective-permute-done.1.refs_5_.refs_1_, ...), custom_call_target="tpu_custom_call" | custom-call | flops 1000 | bytes 1000 | tf_op jit(solution)/shard_map/pallas_call | solution.py:49
  133.8 0.4 collective-permute-done.8
  134.3 6.6 %collective-permute-done.9 = f32[8,2048]{1,0:T(8,128)S(1)} collective-permute-done((f32[8,2048]{1,0:T(8,128)S(1)}, f32[8,2048]{1,0:T(8,128)S(1)}, u32[]{:S(2)}, u32[]{:S(2)}) %collective-permute-start.9) | collective-permute-done | bytes 65568 | tf_op jit(solution)/shard_map/ppermute | solution.py:36
  140.8 1.6 collective-permute-done.10
  142.5 1.0 copy-done.16
  143.5 1.9 %shard_map.119 = bf16[8,64,1024]{2,1,0:T(8,128)(2,1)S(1)} custom-call(s32[4]{0:T(128)S(1)} %copy-done.15, f32[256,512]{1,0:T(8,128)S(1)} %get-tuple-element.136.out_a, f32[256,512]{1,0:T(8,128)S(1)} %get-tuple-element.137.out_b, f32[512,256]{1,0:T(8,128)S(1)} %get-tuple-element.138.in_a, f32[512,256]{1,0:T(8,128)S(1)} %copy-done.16, ...), custom_call_target="tpu_custom_call" | custom-call | flops 28000000000 | bytes 1000 | tf_op jit(solution)/shard_map/pallas_call | solution.py:49
  145.4 1.0 copy-done.12
  146.4 4.4 %all-to-all-start.4 = ((bf16[8,64,1024]{2,1,0:T(8,128)(2,1)}), bf16[8,64,1024]{2,1,0:T(8,128)(2,1)}, u32[]{:S(2)}, u32[]{:S(2)}) async-start(bf16[8,64,1024]{2,1,0:T(8,128)(2,1)} %copy-done.12), calls=%async_computation.4 | async-start | bytes 2097152 | tf_op jit(solution)/shard_map/all_to_all | solution.py:40
  150.8 1.2 collective-permute-start.11
  152.0 1.6 collective-permute-start.12
  153.6 1.4 collective-permute-start.13
  155.0 1.0 copy-done.10
  156.0 2.5 %shard_map.120 = bf16[256,2048]{1,0:T(8,128)(2,1)} custom-call(s32[4]{0:T(128)S(1)} %copy-done.15, bf16[512,256]{1,0:T(8,128)(2,1)S(1)} %copy-done.8, bf16[512,2048]{1,0:T(8,128)(2,1)S(1)} %bitcast.41, bf16[256,128]{1,0:T(8,128)(2,1)S(1)} %copy-done.13, bf16[2048,128]{1,0:T(8,128)(2,1)S(1)} %copy-done.10), custom_call_target="tpu_custom_call" | custom-call | flops 1000 | bytes 1000 | tf_op jit(solution)/shard_map/pallas_call | solution.py:49
  158.5 0.8 collective-permute-done.13
  159.4 0.7 collective-permute-start.14
  160.1 0.9 collective-permute-start.15
  161.0 2.5 %collective-permute-start.16 = (f32[8,2048]{1,0:T(8,128)S(1)}, f32[8,2048]{1,0:T(8,128)S(1)}, u32[]{:S(2)}, u32[]{:S(2)}) collective-permute-start(f32[8,2048]{1,0:T(8,128)S(1)} %add_add_fusion.1), channel_id=1, source_target_pairs={{0,128},{64,192},{128,0},{192,64},{1,129},{65,193},{129,1},{193,65... | collective-permute-start | bytes 196616 | tf_op jit(solution)/shard_map/ppermute | solution.py:36
  163.6 0.7 collective-permute-done.14
  164.2 1.4 collective-permute-done.15
  165.6 1.2 collective-permute-done.16
  166.9 1.2 collective-permute-done.17
  168.2 1.4 collective-permute-start.18
  169.6 8.4 %collective-permute-done.18 = f32[8,2048]{1,0:T(8,128)S(1)} collective-permute-done((f32[8,2048]{1,0:T(8,128)S(1)}, f32[8,2048]{1,0:T(8,128)S(1)}, u32[]{:S(2)}, u32[]{:S(2)}) %collective-permute-start.18) | collective-permute-done | bytes 65568 | tf_op jit(solution)/shard_map/ppermute | solution.py:36
  178.0 0.6 add.83
  178.6 1.8 %all-to-all-done.4.got = bf16[8,64,1024]{2,1,0:T(8,128)(2,1)} async-done(((bf16[8,64,1024]{2,1,0:T(8,128)(2,1)}), bf16[8,64,1024]{2,1,0:T(8,128)(2,1)}, u32[]{:S(2)}, u32[]{:S(2)}) %all-to-all-start.4) | async-done | bytes 1048608 | tf_op jit(solution)/shard_map/all_to_all | solution.py:40
  180.4 2.1 %shard_map.121 = (f32[32,2048]{1,0:T(8,128)}, f32[64,1024]{1,0:T(8,128)}) custom-call(s32[4]{0:T(128)S(1)} %copy-done.15, bf16[8,64,1024]{2,1,0:T(8,128)(2,1)} %all-to-all-done.4.got), custom_call_target="tpu_custom_call" | custom-call | flops 1000 | bytes 1000 | tf_op jit(solution)/shard_map/pallas_call | solution.py:49
  (81 shorter events, 1.3 us)
Async XLA Ops:
  0.6 14.2 %copy-start = (bf16[256,2048]{1,0:T(8,128)(2,1)S(1)}, bf16[256,2048]{1,0:T(8,128)(2,1)}, u32[]{:S(2)}) copy-start(bf16[256,2048]{1,0:T(8,128)(2,1)} %param.9) | copy-start | bytes 3145732
  1.4 13.4 %copy-start.22 = (s32[256,1]{0,1:T(1,128)}, s32[256,1]{0,1:T(1,128)S(1)}, u32[]{:S(2)}) copy-start(s32[256,1]{0,1:T(1,128)S(1)} %get-tuple-element.167) | copy-start | bytes 3076
  2.2 12.6 %copy-start.24 = (pred[256]{0:T(512)(128)(4,1)}, pred[256]{0:T(512)(128)(4,1)S(1)}, u32[]{:S(2)}) copy-start(pred[256]{0:T(512)(128)(4,1)S(1)} %get-tuple-element.160) | copy-start | bytes 772
  2.2 12.6 %copy-start.25 = (pred[256]{0:T(512)(128)(4,1)}, pred[256]{0:T(512)(128)(4,1)S(1)}, u32[]{:S(2)}) copy-start(pred[256]{0:T(512)(128)(4,1)S(1)} %get-tuple-element.161) | copy-start | bytes 772
  5.6 6.3 %copy-start.20 = (s32[256,2]{0,1:T(2,128)S(1)}, s32[256,2]{0,1:T(2,128)}, u32[]{:S(2)}) copy-start(s32[256,2]{0,1:T(2,128)} %param.15) | copy-start | bytes 6148
  5.6 6.3 %copy-start.18 = (bf16[2048,8]{0,1:T(8,128)(2,1)S(1)}, bf16[2048,8]{0,1:T(8,128)(2,1)}, u32[]{:S(2)}) copy-start(bf16[2048,8]{0,1:T(8,128)(2,1)} %param.10) | copy-start | bytes 98308
  5.6 8.3 %copy-start.21 = (s32[256,2]{0,1:T(2,128)S(1)}, s32[256,2]{0,1:T(2,128)}, u32[]{:S(2)}) copy-start(s32[256,2]{0,1:T(2,128)} %param.13) | copy-start | bytes 6148
  5.6 31.5 %all-to-all-start.1 = ((bf16[8,64,2048]{2,1,0:T(8,128)(2,1)}), bf16[8,64,2048]{2,1,0:T(8,128)(2,1)S(1)}, u32[]{:S(2)}, u32[]{:S(2)}) async-start(bf16[8,64,2048]{2,1,0:T(8,128)(2,1)} %bitcast.44), calls=%async_computation.1 | async-start | bytes 4194304 | tf_op jit(solution)/shard_map/all_to_all | solution.py:40
  13.9 0.6 copy-start.23
  37.1 43.3 %copy-start.1 = (bf16[8,64,2048]{2,1,0:T(8,128)(2,1)}, bf16[8,64,2048]{2,1,0:T(8,128)(2,1)S(1)}, u32[]{:S(2)}) copy-start(bf16[8,64,2048]{2,1,0:T(8,128)(2,1)S(1)} %all-to-all-done.1) | copy-start | bytes 6291460
  37.1 31.5 %all-to-all-start = ((bf16[8,64,2176]{2,1,0:T(8,128)(2,1)}), bf16[8,64,2176]{2,1,0:T(8,128)(2,1)}, u32[]{:S(2)}, u32[]{:S(2)}) async-start(bf16[8,64,2176]{2,1,0:T(8,128)(2,1)} %bitcast.43), calls=%async_computation | async-start | bytes 4456448 | tf_op jit(solution)/shard_map/all_to_all | solution.py:40
  43.1 25.5 %collective-permute-start = (bf16[512,2048]{1,0:T(8,128)(2,1)S(1)}, bf16[512,2048]{1,0:T(8,128)(2,1)}, u32[]{:S(2)}, u32[]{:S(2)}) collective-permute-start(bf16[512,2048]{1,0:T(8,128)(2,1)S(1)} %bitcast.36), channel_id=1, source_target_pairs={{0,8},{8,0},{1,9},{9,1},{2,10},{10,2},{3,11},{11,3},{4,12},{12,4},... | collective-permute-start | bytes 6291464 | tf_op jit(solution)/shard_map/ppermute | solution.py:36
  49.6 19.0 %collective-permute-start.1 = (bf16[512,1024]{1,0:T(8,128)(2,1)}, bf16[512,1024]{1,0:T(8,128)(2,1)}, u32[]{:S(2)}, u32[]{:S(2)}) collective-permute-start(bf16[512,1024]{1,0:T(8,128)(2,1)} %get-tuple-element.118.act_ref.refs_4_.refs_0_), channel_id=1, source_target_pairs={{0,8},{8,0},{1,9},{9,1},{2,10},{10,2},{3,11},{11,3},{4,12},{12,4},... | collective-permute-start | bytes 3145736 | tf_op jit(solution)/shard_map/ppermute | solution.py:36
  53.4 27.0 %copy-start.14 = (s32[4]{0:T(128)}, s32[4]{0:T(128)S(1)}, u32[]{:S(2)}) copy-start(s32[4]{0:T(128)S(1)} %pad_add_fusion.pos_ref) | copy-start | bytes 52
  68.6 2.3 %copy-start.9 = (f32[512,1024]{1,0:T(8,128)S(1)}, f32[512,1024]{1,0:T(8,128)}, u32[]{:S(2)}) copy-start(f32[512,1024]{1,0:T(8,128)} %get-tuple-element.86.slope_ref) | copy-start | bytes 6291460
  70.8 9.6 %copy-start.3 = (bf16[512,1024]{1,0:T(8,128)(2,1)}, bf16[512,1024]{1,0:T(8,128)(2,1)S(1)}, u32[]{:S(2)}) copy-start(bf16[512,1024]{1,0:T(8,128)(2,1)S(1)} %get-tuple-element.122.refs_0_.refs_4_) | copy-start | bytes 3145732
  70.9 9.6 %collective-permute-start.2 = (bf16[512,1024]{1,0:T(8,128)(2,1)S(1)}, bf16[512,1024]{1,0:T(8,128)(2,1)S(1)}, u32[]{:S(2)}, u32[]{:S(2)}) collective-permute-start(bf16[512,1024]{1,0:T(8,128)(2,1)S(1)} %get-tuple-element.83), channel_id=1, source_target_pairs={{0,8},{8,0},{1,9},{9,1},{2,10},{10,2},{3,11},{11,3},{4,12},{12,4},... | collective-permute-start | bytes 3145736 | tf_op jit(solution)/shard_map/ppermute | solution.py:36
  71.0 2.5 %copy-start.7 = (bf16[1,1024,2048]{2,1,0:T(8,128)(2,1)S(1)}, bf16[1,1024,2048]{2,1,0:T(8,128)(2,1)}, u32[]{:S(2)}) copy-start(bf16[1,1024,2048]{2,1,0:T(8,128)(2,1)} %param.12) | copy-start | bytes 12582916
  78.5 7.6 %copy-start.2 = (bf16[512,1024]{1,0:T(8,128)(2,1)}, bf16[512,1024]{1,0:T(8,128)(2,1)S(1)}, u32[]{:S(2)}) copy-start(bf16[512,1024]{1,0:T(8,128)(2,1)S(1)} %get-tuple-element.124.refs_2_.grad.refs_6_) | copy-start | bytes 3145732
  78.5 1.9 %collective-permute-start.3 = (bf16[512,512]{1,0:T(8,128)(2,1)S(1)}, bf16[512,512]{1,0:T(8,128)(2,1)S(1)}, u32[]{:S(2)}, u32[]{:S(2)}) collective-permute-start(bf16[512,512]{1,0:T(8,128)(2,1)S(1)} %get-tuple-element.90), channel_id=1, source_target_pairs={{0,8},{8,0},{1,9},{9,1},{2,10},{10,2},{3,11},{11,3},{4,12},{12,4},... | collective-permute-start | bytes 1572872 | tf_op jit(solution)/shard_map/ppermute | solution.py:36
  80.4 5.7 %copy-start.5 = (bf16[512,512]{1,0:T(8,128)(2,1)}, bf16[512,512]{1,0:T(8,128)(2,1)S(1)}, u32[]{:S(2)}) copy-start(bf16[512,512]{1,0:T(8,128)(2,1)S(1)} %collective-permute-done.3.refs_3_.refs_7_) | copy-start | bytes 1572868
  80.4 5.7 %copy-start.4 = (bf16[512,1024]{1,0:T(8,128)(2,1)}, bf16[512,1024]{1,0:T(8,128)(2,1)S(1)}, u32[]{:S(2)}) copy-start(bf16[512,1024]{1,0:T(8,128)(2,1)S(1)} %collective-permute-done.2.refs_1_.refs_5_) | copy-start | bytes 3145732
  86.1 31.1 %collective-permute-start.4 = (bf16[1024,512]{1,0:T(8,128)(2,1)}, bf16[1024,512]{1,0:T(8,128)(2,1)}, u32[]{:S(2)}, u32[]{:S(2)}) collective-permute-start(bf16[1024,512]{1,0:T(8,128)(2,1)} %get-tuple-element.94), channel_id=1, source_target_pairs={{0,64},{64,0},{128,192},{192,128},{1,65},{65,1},{129,193},{193,129... | collective-permute-start | bytes 3145736 | tf_op jit(solution)/shard_map/ppermute | solution.py:36
  88.0 29.3 %collective-permute-start.5 = (bf16[1024,512]{1,0:T(8,128)(2,1)}, bf16[1024,512]{1,0:T(8,128)(2,1)}, u32[]{:S(2)}, u32[]{:S(2)}) collective-permute-start(bf16[1024,512]{1,0:T(8,128)(2,1)} %get-tuple-element.95), channel_id=1, source_target_pairs={{0,192},{64,128},{128,64},{192,0},{1,193},{65,129},{129,65},{193,1... | collective-permute-start | bytes 3145736 | tf_op jit(solution)/shard_map/ppermute | solution.py:36
  90.2 12.2 %all-to-all-start.2 = ((bf16[8,64,128]{2,1,0:T(8,128)(2,1)}), bf16[8,64,128]{2,1,0:T(8,128)(2,1)S(1)}, u32[]{:S(2)}, u32[]{:S(2)}) async-start(bf16[8,64,128]{2,1,0:T(8,128)(2,1)} %bitcast.16), calls=%async_computation.2 | async-start | bytes 262144 | tf_op jit(solution)/shard_map/all_to_all | solution.py:40
  102.4 0.7 copy-start.17
  102.4 9.8 %copy-start.15 = (s32[4]{0:T(128)S(1)}, s32[4]{0:T(128)}, u32[]{:S(2)}) copy-start(s32[4]{0:T(128)} %copy-done.14) | copy-start | bytes 52
  103.0 43.3 %all-to-all-start.3 = ((bf16[8,64,2048]{2,1,0:T(8,128)(2,1)}), bf16[8,64,2048]{2,1,0:T(8,128)(2,1)S(1)}, u32[]{:S(2)}, u32[]{:S(2)}) async-start(bf16[8,64,2048]{2,1,0:T(8,128)(2,1)} %bitcast.45), calls=%async_computation.3 | async-start | bytes 4194304 | tf_op jit(solution)/shard_map/all_to_all | solution.py:40
  108.8 3.4 %copy-start.6 = (bf16[512,512]{1,0:T(8,128)(2,1)S(1)}, bf16[512,512]{1,0:T(8,128)(2,1)}, u32[]{:S(2)}) copy-start(bf16[512,512]{1,0:T(8,128)(2,1)} %copy-done.5) | copy-start | bytes 1572868
  117.3 1.2 copy-start.11
  118.5 2.9 %copy-start.19 = (f32[8,2048]{1,0:T(8,128)S(1)}, f32[8,2048]{1,0:T(8,128)}, u32[]{:S(2)}) copy-start(f32[8,2048]{1,0:T(8,128)} %get-tuple-element.131) | copy-start | bytes 196612
  120.3 22.2 %collective-permute-start.6 = (bf16[512,512]{1,0:T(8,128)(2,1)S(1)}, bf16[512,512]{1,0:T(8,128)(2,1)S(1)}, u32[]{:S(2)}, u32[]{:S(2)}) collective-permute-start(bf16[512,512]{1,0:T(8,128)(2,1)S(1)} %get-tuple-element.117), channel_id=1, source_target_pairs={{0,192},{64,128},{128,64},{192,0},{1,193},{65,129},{129,65},{193,1... | collective-permute-start | bytes 1572872 | tf_op jit(solution)/shard_map/ppermute | solution.py:36
  121.4 21.0 %collective-permute-start.7 = (bf16[512,512]{1,0:T(8,128)(2,1)S(1)}, bf16[512,512]{1,0:T(8,128)(2,1)S(1)}, u32[]{:S(2)}, u32[]{:S(2)}) collective-permute-start(bf16[512,512]{1,0:T(8,128)(2,1)S(1)} %get-tuple-element.130), channel_id=1, source_target_pairs={{0,64},{64,0},{128,192},{192,128},{1,65},{65,1},{129,193},{193,129... | collective-permute-start | bytes 1572872 | tf_op jit(solution)/shard_map/ppermute | solution.py:36
  121.4 12.8 %collective-permute-start.8 = (f32[8,2048]{1,0:T(8,128)S(1)}, f32[8,2048]{1,0:T(8,128)S(1)}, u32[]{:S(2)}, u32[]{:S(2)}) collective-permute-start(f32[8,2048]{1,0:T(8,128)S(1)} %copy-done.19), channel_id=1, source_target_pairs={{0,16},{16,0},{32,48},{48,32},{1,17},{17,1},{33,49},{49,33},{2,18}... | collective-permute-start | bytes 196616 | tf_op jit(solution)/shard_map/ppermute | solution.py:36
  124.7 16.1 %collective-permute-start.9 = (f32[8,2048]{1,0:T(8,128)S(1)}, f32[8,2048]{1,0:T(8,128)S(1)}, u32[]{:S(2)}, u32[]{:S(2)}) collective-permute-start(f32[8,2048]{1,0:T(8,128)S(1)} %copy-done.19), channel_id=1, source_target_pairs={{0,48},{16,32},{32,16},{48,0},{1,49},{17,33},{33,17},{49,1},{2,50}... | collective-permute-start | bytes 196616 | tf_op jit(solution)/shard_map/ppermute | solution.py:36
  128.3 14.1 %collective-permute-start.10 = (f32[8,2048]{1,0:T(8,128)S(1)}, f32[8,2048]{1,0:T(8,128)S(1)}, u32[]{:S(2)}, u32[]{:S(2)}) collective-permute-start(f32[8,2048]{1,0:T(8,128)S(1)} %copy-done.19), channel_id=1, source_target_pairs={{0,32},{16,48},{32,0},{48,16},{1,33},{17,49},{33,1},{49,17},{2,34}... | collective-permute-start | bytes 196616 | tf_op jit(solution)/shard_map/ppermute | solution.py:36
  142.4 1.0 copy-start.16
  145.4 1.0 copy-start.12
  146.4 8.6 %copy-start.8 = (bf16[512,256]{1,0:T(8,128)(2,1)S(1)}, bf16[512,256]{1,0:T(8,128)(2,1)}, u32[]{:S(2)}) copy-start(bf16[512,256]{1,0:T(8,128)(2,1)} %fusion.12.disp) | copy-start | bytes 786436
  146.4 8.6 %copy-start.13 = (bf16[256,128]{1,0:T(8,128)(2,1)S(1)}, bf16[256,128]{1,0:T(8,128)(2,1)}, u32[]{:S(2)}) copy-start(bf16[256,128]{1,0:T(8,128)(2,1)} %get-tuple-element.143.logit) | copy-start | bytes 196612
  146.4 34.0 %all-to-all-start.4 = ((bf16[8,64,1024]{2,1,0:T(8,128)(2,1)}), bf16[8,64,1024]{2,1,0:T(8,128)(2,1)}, u32[]{:S(2)}, u32[]{:S(2)}) async-start(bf16[8,64,1024]{2,1,0:T(8,128)(2,1)} %copy-done.12), calls=%async_computation.4 | async-start | bytes 2097152 | tf_op jit(solution)/shard_map/all_to_all | solution.py:40
  150.8 7.7 %collective-permute-start.11 = (f32[8,2048]{1,0:T(8,128)S(1)}, f32[8,2048]{1,0:T(8,128)S(1)}, u32[]{:S(2)}, u32[]{:S(2)}) collective-permute-start(f32[8,2048]{1,0:T(8,128)S(1)} %add_add_fusion.2), channel_id=1, source_target_pairs={{0,2},{2,0},{4,6},{6,4},{1,3},{3,1},{5,7},{7,5},{8,10},{10,8},{12,... | collective-permute-start | bytes 196616 | tf_op jit(solution)/shard_map/ppermute | solution.py:36
  152.0 6.5 %collective-permute-start.12 = (f32[8,2048]{1,0:T(8,128)S(1)}, f32[8,2048]{1,0:T(8,128)S(1)}, u32[]{:S(2)}, u32[]{:S(2)}) collective-permute-start(f32[8,2048]{1,0:T(8,128)S(1)} %add_add_fusion.2), channel_id=1, source_target_pairs={{0,6},{2,4},{4,2},{6,0},{1,7},{3,5},{5,3},{7,1},{8,14},{10,12},{12... | collective-permute-start | bytes 196616 | tf_op jit(solution)/shard_map/ppermute | solution.py:36
  153.6 5.8 %collective-permute-start.13 = (f32[8,2048]{1,0:T(8,128)S(1)}, f32[8,2048]{1,0:T(8,128)S(1)}, u32[]{:S(2)}, u32[]{:S(2)}) collective-permute-start(f32[8,2048]{1,0:T(8,128)S(1)} %add_add_fusion.2), channel_id=1, source_target_pairs={{0,4},{2,6},{4,0},{6,2},{1,5},{3,7},{5,1},{7,3},{8,12},{10,14},{12... | collective-permute-start | bytes 196616 | tf_op jit(solution)/shard_map/ppermute | solution.py:36
  155.0 1.0 copy-start.10
  159.4 4.9 %collective-permute-start.14 = (f32[8,2048]{1,0:T(8,128)S(1)}, f32[8,2048]{1,0:T(8,128)S(1)}, u32[]{:S(2)}, u32[]{:S(2)}) collective-permute-start(f32[8,2048]{1,0:T(8,128)S(1)} %add_add_fusion.1), channel_id=1, source_target_pairs={{0,64},{64,0},{128,192},{192,128},{1,65},{65,1},{129,193},{193,129... | collective-permute-start | bytes 196616 | tf_op jit(solution)/shard_map/ppermute | solution.py:36
  160.1 5.5 %collective-permute-start.15 = (f32[8,2048]{1,0:T(8,128)S(1)}, f32[8,2048]{1,0:T(8,128)S(1)}, u32[]{:S(2)}, u32[]{:S(2)}) collective-permute-start(f32[8,2048]{1,0:T(8,128)S(1)} %add_add_fusion.1), channel_id=1, source_target_pairs={{0,192},{64,128},{128,64},{192,0},{1,193},{65,129},{129,65},{193,1... | collective-permute-start | bytes 196616 | tf_op jit(solution)/shard_map/ppermute | solution.py:36
  161.0 5.8 %collective-permute-start.16 = (f32[8,2048]{1,0:T(8,128)S(1)}, f32[8,2048]{1,0:T(8,128)S(1)}, u32[]{:S(2)}, u32[]{:S(2)}) collective-permute-start(f32[8,2048]{1,0:T(8,128)S(1)} %add_add_fusion.1), channel_id=1, source_target_pairs={{0,128},{64,192},{128,0},{192,64},{1,129},{65,193},{129,1},{193,65... | collective-permute-start | bytes 196616 | tf_op jit(solution)/shard_map/ppermute | solution.py:36
  166.8 1.3 collective-permute-start.17
  168.2 9.8 %collective-permute-start.18 = (f32[8,2048]{1,0:T(8,128)S(1)}, f32[8,2048]{1,0:T(8,128)S(1)}, u32[]{:S(2)}, u32[]{:S(2)}) collective-permute-start(f32[8,2048]{1,0:T(8,128)S(1)} %add.82), channel_id=1, source_target_pairs={{0,1},{1,0},{2,3},{3,2},{4,5},{5,4},{6,7},{7,6},{8,9},{9,8},{10,11... | collective-permute-start | bytes 196616 | tf_op jit(solution)/shard_map/ppermute | solution.py:36

commit v12 on v11

--- a/solution.py
+++ b/solution.py
@@ -496,7 +496,9 @@
         left_in, left_out, right_in, right_out, far_a
     )
     near = near_parts(pos, left_out, right_out, left_in, right_in)
-    router_part = router_round(router_part, "zh", 1, 3, near)
+    other_router = swap(router_part, "core", 1)
+    router_part, other_router, _ = tie(router_part, other_router, near)
+    router_part = router_part + other_router
 
     near, far, router_part = tie(near, far, router_part)
     pieces = zh_pieces(pos, near[:2], near[2:], got, far, grad_scale)
@@ -506,8 +508,16 @@
     grad_tokens = token_grads(pos, dispatch, back, logit_lanes, weight_lanes)
     router_part = router_round(router_part, "x", 1, 3, grad_tokens)
     router_part = router_round(router_part, "y", 1, 3)
+    place = lambda c, z: 4 * (z // 2) + 2 * c + z % 2
+    terms = []
+    for k in range(4):
+        pairs = [
+            (place(c, z), place(c, z ^ (4 * c + k))) for c in range(2) for z in range(8) if c or k
+        ]
+        terms.append(lax.ppermute(router_part, ("zh", "core", "zl"), pairs))
+    terms[0] = jnp.where(core == 0, router_part, terms[0])
+    router_part = (terms[0] + terms[1]) + (terms[2] + terms[3])
     router_part = router_part + swap(router_part, "core", 1)
-    router_part = router_part + swap(router_part, "zl", 1)
     got, router_part = tie(got, router_part)
     outer_share, inner_share = shares(pos, got, near[0].shape[0] // 8)
     return (grad_tokens, router_part.T, inner_share, outer_share)

time: 184 us -> 187 us (1.016)
  starting transfers between devices: 51.4 us -> 54 us
    ppermute x0 -> x4, waiting for transfers between devices: none -> 10.1 us  [per_device(): terms.append(lax.ppermute(router_part, ('zh', 'core', 'zl'), pairs))]
    ppermute x19 -> x16, waiting for transfers between devices: 24 us -> 15.2 us  [swap(): return lax.ppermute(values, axis, [(i, i ^ mask) for i in range(size)])]
    ppermute x19 -> x16, starting transfers between devices: 23.6 us -> 17.7 us  [swap(): return lax.ppermute(values, axis, [(i, i ^ mask) for i in range(size)])]
    ppermute x0 -> x4, starting transfers between devices: none -> 5.13 us  [per_device(): terms.append(lax.ppermute(router_part, ('zh', 'core', 'zl'), pairs))]
    all_to_all x5, starting transfers between devices: 27.8 us -> 31.1 us  [exchange(): return lax.all_to_all(values, axes, split_axis=0, concat_axis=0, tiled=True)]
  transfers between devices with their start and end apart: 24 -> 25, of which waited for: 13 -> 11; matrix products, arithmetic and copies ran while one was open for 10% -> 10% of each run, Pallas kernels for 17% -> 17%
where the time goes in v12:
time: 187 us; the launch traced here: 185 us
  waiting for transfers between devices  57.3 us (31%)
  starting transfers between devices  54 us (29%)
  Pallas kernels  41.1 us (22%)
  matrix products  12.5 us (7%)
  local copies, waits for them, and re-layouts  12.2 us (7%)
  other arithmetic  6.52 us (3%)
    pallas_call x11, Pallas kernels, call(): pl.pallas_call(body, in_specs=[pl.BlockSpec(memory_space=pltpu.SMEM)] + [...  41.1 us
    all_to_all x5, waiting for transfers between devices, exchange(): return lax.all_to_all(values, axes, split_axis=0, concat_axis=0, tiled=True)  31.9 us
    all_to_all x5, starting transfers between devices, exchange(): return lax.all_to_all(values, axes, split_axis=0, concat_axis=0, tiled=True)  31.1 us
    ppermute x16, starting transfers between devices, swap(): return lax.ppermute(values, axis, [(i, i ^ mask) for i in range(size)])  17.7 us
    ppermute x16, waiting for transfers between devices, swap(): return lax.ppermute(values, axis, [(i, i ^ mask) for i in range(size)])  15.2 us
    ppermute x4, waiting for transfers between devices, per_device(): terms.append(lax.ppermute(router_part, ('zh', 'core', 'zl'), pairs))  10.1 us
    unnamed x53, local copies, waits for them, and re-layouts  9.04 us
    dot_general x1, matrix products, per_device(): hidden_pre = jnp.dot(slot_tokens, weight_in, preferred_element_type=F32)  6.49 us
  transfers between devices with their start and end apart: 25, of which 11 were waited for; matrix products, arithmetic and copies ran while one was open for 10% of the time, Pallas kernels for 17%

profile of v12, /device:TPU:2, one launch (start us, length us, event | category | flops | bytes accessed | tf_op | source)
XLA Modules:
  0.0 184.7 jit_solution(4112436376645956277)
XLA Ops:
  0.6 0.8 multiply_add_fusion
  1.4 0.8 compare_reduce_fusion.1
  2.2 3.3 %convolution_convert_fusion = bf16[512,2048]{1,0:T(8,128)(2,1)} fusion(bf16[256,2048]{1,0:T(8,128)(2,1)} %tok.1, s32[256]{0:T(256)S(1)} %bitcast.53, s32[256]{0:T(256)S(1)} %bitcast.49, pred[256]{0:T(512)(128)(4,1)S(1)} %get-tuple-element.157, pred[256]{0:T(512)(128)(4,1)S(1)} %get-tuple-element.156), kind=kOutput, calls=%fused_computation.1 | convolution fusion | flops 538574848 | bytes 3148288 | tf_op jit(solution)/shard_map/dot_general | solution.py:406
  5.6 6.3 %all-to-all-start.1 = ((bf16[8,64,2048]{2,1,0:T(8,128)(2,1)}), bf16[8,64,2048]{2,1,0:T(8,128)(2,1)S(1)}, u32[]{:S(2)}, u32[]{:S(2)}) async-start(bf16[8,64,2048]{2,1,0:T(8,128)(2,1)} %bitcast.44), calls=%async_computation.1 | async-start | bytes 4194304 | tf_op jit(solution)/shard_map/all_to_all | solution.py:40
  11.9 1.6 fusion.17
  13.5 0.1 copy.24
  13.9 0.6 copy-done.23
  14.5 0.3 convolution_convert_fusion.2
  14.8 0.7 convolution_convert_fusion.1
  15.6 1.6 pad_maximum_fusion
  17.2 19.9 %all-to-all-done.1 = bf16[8,64,2048]{2,1,0:T(8,128)(2,1)S(1)} async-done(((bf16[8,64,2048]{2,1,0:T(8,128)(2,1)}), bf16[8,64,2048]{2,1,0:T(8,128)(2,1)S(1)}, u32[]{:S(2)}, u32[]{:S(2)}) %all-to-all-start.1) | async-done | bytes 2097184 | tf_op jit(solution)/shard_map/all_to_all | solution.py:40
  37.1 6.0 %all-to-all-start = ((bf16[8,64,2176]{2,1,0:T(8,128)(2,1)}), bf16[8,64,2176]{2,1,0:T(8,128)(2,1)}, u32[]{:S(2)}, u32[]{:S(2)}) async-start(bf16[8,64,2176]{2,1,0:T(8,128)(2,1)} %bitcast.43), calls=%async_computation | async-start | bytes 4456448 | tf_op jit(solution)/shard_map/all_to_all | solution.py:40
  43.1 6.5 %fusion.3 = (f32[512,1024]{1,0:T(8,128)}, bf16[512,1024]{1,0:T(8,128)(2,1)}) fusion(bf16[512,2048]{1,0:T(8,128)(2,1)S(1)} %bitcast.37, bf16[1,2048,1024]{2,1,0:T(8,128)(2,1)} %param.11), kind=kOutput, calls=%fused_computation.7 | convolution fusion | flops 2152726528 | bytes 9437184 | tf_op jit(solution)/shard_map/dot_general | solution.py:445
  49.6 0.5 collective-permute-start.1
  50.1 1.0 copy.27
  51.4 1.9 %pad.22.weight = bf16[2048,128]{1,0:T(8,128)(2,1)} pad(bf16[2048,8]{1,0:T(8,128)(2,1)} %copy.27, bf16[]{:T(256)} %constant.39.clone.1), padding=0_0x0_120 | pad | bytes 557058 | tf_op jit(solution)/shard_map/jit(_pad)/pad | solution.py:420
  53.5 0.8 broadcast_in_dim.52
  54.3 0.8 pad_maximum_fusion.1.side
  55.1 1.6 fusion.12.disp
  56.7 12.0 %all-to-all-done = bf16[8,64,2176]{2,1,0:T(8,128)(2,1)} async-done(((bf16[8,64,2176]{2,1,0:T(8,128)(2,1)}), bf16[8,64,2176]{2,1,0:T(8,128)(2,1)}, u32[]{:S(2)}, u32[]{:S(2)}) %all-to-all-start) | async-done | bytes 2228256 | tf_op jit(solution)/shard_map/all_to_all | solution.py:40
  68.6 2.2 %shard_map.111 = (bf16[512,1024]{1,0:T(8,128)(2,1)S(1)}, bf16[512,1024]{1,0:T(8,128)(2,1)S(1)}) custom-call(s32[4]{0:T(128)S(1)} %pad_add_fusion.pos_ref, bf16[512,2176]{1,0:T(8,128)(2,1)} %bitcast.7.rec), custom_call_target="tpu_custom_call" | custom-call | flops 1000 | bytes 1000 | tf_op jit(solution)/shard_map/pallas_call | solution.py:49
  71.0 2.4 %copy-done.7 = bf16[1,1024,2048]{2,1,0:T(8,128)(2,1)S(1)} copy-done((bf16[1,1024,2048]{2,1,0:T(8,128)(2,1)S(1)}, bf16[1,1024,2048]{2,1,0:T(8,128)(2,1)}, u32[]{:S(2)}) %copy-start.7) | copy-done | bytes 4194328
  73.4 5.1 %shard_map.112 = (bf16[512,1024]{1,0:T(8,128)(2,1)S(1)}, bf16[512,512]{1,0:T(8,128)(2,1)S(1)}, bf16[512,128]{1,0:T(8,128)(2,1)}) custom-call(s32[4]{0:T(128)S(1)} %pad_add_fusion.pos_ref, bf16[512,2176]{1,0:T(8,128)(2,1)} %bitcast.7.rec, bf16[1024,2048]{1,0:T(8,128)(2,1)S(1)} %bitcast.42, bf16[512,1024]{1,0:T(8,128)(2,1)} %get-tuple-element.116.act_ref.refs_4_.refs_0_, ...), custom_call_target="tpu_custom_call" | custom-call | flops 1000 | bytes 1000 | tf_op jit(solution)/shard_map/pallas_call | solution.py:49
  78.5 0.2 collective-permute-start.3
  78.7 1.7 collective-permute-done.3.refs_3_.refs_7_
  80.4 5.7 %shard_map.113 = (bf16[1024,512]{1,0:T(8,128)(2,1)}, bf16[1024,512]{1,0:T(8,128)(2,1)}) custom-call(s32[4]{0:T(128)S(1)} %pad_add_fusion.pos_ref, bf16[512,1024]{1,0:T(8,128)(2,1)S(1)} %get-tuple-element.120.refs_0_.refs_4_, bf16[512,1024]{1,0:T(8,128)(2,1)S(1)} %collective-permute-done.2.refs_1_.refs_5_, ...), custom_call_target="tpu_custom_call" | custom-call | flops 1000 | bytes 1000 | tf_op jit(solution)/shard_map/pallas_call | solution.py:49
  86.1 1.8 collective-permute-start.4
  88.0 2.2 %collective-permute-start.5 = (bf16[1024,512]{1,0:T(8,128)(2,1)}, bf16[1024,512]{1,0:T(8,128)(2,1)}, u32[]{:S(2)}, u32[]{:S(2)}) collective-permute-start(bf16[1024,512]{1,0:T(8,128)(2,1)} %get-tuple-element.93), channel_id=1, source_target_pairs={{0,192},{64,128},{128,64},{192,0},{1,193},{65,129},{129,65},{193,1... | collective-permute-start | bytes 3145736 | tf_op jit(solution)/shard_map/ppermute | solution.py:36
  90.2 5.4 %all-to-all-start.2 = ((bf16[8,64,128]{2,1,0:T(8,128)(2,1)}), bf16[8,64,128]{2,1,0:T(8,128)(2,1)S(1)}, u32[]{:S(2)}, u32[]{:S(2)}) async-start(bf16[8,64,128]{2,1,0:T(8,128)(2,1)} %bitcast.16), calls=%async_computation.2 | async-start | bytes 262144 | tf_op jit(solution)/shard_map/all_to_all | solution.py:40
  95.6 6.8 %shard_map.114 = bf16[512,2048]{1,0:T(8,128)(2,1)} custom-call(s32[4]{0:T(128)} %copy-done.14, bf16[512,1024]{1,0:T(8,128)(2,1)} %copy-done.2, bf16[2048,1024]{1,0:T(8,128)(2,1)} %bitcast.46), custom_call_target="tpu_custom_call" | custom-call | flops 1000 | bytes 1000 | tf_op jit(solution)/shard_map/pallas_call | solution.py:49
  102.4 0.6 copy-done.17
  103.0 5.7 %all-to-all-start.3 = ((bf16[8,64,2048]{2,1,0:T(8,128)(2,1)}), bf16[8,64,2048]{2,1,0:T(8,128)(2,1)S(1)}, u32[]{:S(2)}, u32[]{:S(2)}) async-start(bf16[8,64,2048]{2,1,0:T(8,128)(2,1)} %bitcast.45), calls=%async_computation.3 | async-start | bytes 4194304 | tf_op jit(solution)/shard_map/all_to_all | solution.py:40
  108.8 3.4 %shard_map.115 = (bf16[256,128]{1,0:T(8,128)(2,1)}, f32[8,2048]{1,0:T(8,128)}) custom-call(s32[4]{0:T(128)} %copy-done.14, bf16[512,256]{1,0:T(8,128)(2,1)} %fusion.12.disp, bf16[512,128]{1,0:T(8,128)(2,1)} %bitcast.47, f32[4,256,128]{2,1,0:T(8,128)} %pad_maximum_fusion.1.side, bf16[256,2048]{1,0:T(8,128)(2,1)} %tok.1), custom_call_target="tpu_custom_call" | custom-call | flops 1000 | bytes 1000 | tf_op jit(solution)/shard_map/pallas_call | solution.py:49
  112.2 5.1 %shard_map.116 = (f32[512,512]{1,0:T(8,128)S(1)}, f32[512,512]{1,0:T(8,128)}) custom-call(s32[4]{0:T(128)S(1)} %copy-done.15, bf16[512,1024]{1,0:T(8,128)(2,1)} %get-tuple-element.116.act_ref.refs_4_.refs_0_, bf16[512,1024]{1,0:T(8,128)(2,1)} %collective-permute-done.1.refs_5_.refs_1_, bf16[512,2048]{1,0:T(8,128)(2,1)} %bitcast.39, ...), custom_call_target="tpu_custom_call" | custom-call | flops 1000 | bytes 1000 | tf_op jit(solution)/shard_map/pallas_call | solution.py:49
  117.3 1.2 copy-done.11
  118.5 1.8 shard_map.117
  120.3 1.1 collective-permute-start.6
  121.4 4.6 %shard_map.118 = (f32[256,512]{1,0:T(8,128)S(1)}, f32[256,512]{1,0:T(8,128)S(1)}, f32[512,256]{1,0:T(8,128)S(1)}, f32[512,256]{1,0:T(8,128)}) custom-call(s32[4]{0:T(128)S(1)} %copy-done.15, bf16[512,1024]{1,0:T(8,128)(2,1)} %get-tuple-element.116.act_ref.refs_4_.refs_0_, bf16[512,1024]{1,0:T(8,128)(2,1)} %collective-permute-done.1.refs_5_.refs_1_, ...), custom_call_target="tpu_custom_call" | custom-call | flops 1000 | bytes 1000 | tf_op jit(solution)/shard_map/pallas_call | solution.py:49
  126.1 8.1 %collective-permute-done.6.far_a = bf16[512,512]{1,0:T(8,128)(2,1)S(1)} collective-permute-done((bf16[512,512]{1,0:T(8,128)(2,1)S(1)}, bf16[512,512]{1,0:T(8,128)(2,1)S(1)}, u32[]{:S(2)}, u32[]{:S(2)}) %collective-permute-start.6) | collective-permute-done | bytes 524320 | tf_op jit(solution)/shard_map/ppermute | solution.py:36
  134.2 1.0 copy-done.16
  135.3 1.9 %shard_map.119 = bf16[8,64,1024]{2,1,0:T(8,128)(2,1)S(1)} custom-call(s32[4]{0:T(128)S(1)} %copy-done.15, f32[256,512]{1,0:T(8,128)S(1)} %get-tuple-element.132.out_a, f32[256,512]{1,0:T(8,128)S(1)} %get-tuple-element.133.out_b, f32[512,256]{1,0:T(8,128)S(1)} %get-tuple-element.134.in_a, f32[512,256]{1,0:T(8,128)S(1)} %copy-done.16, ...), custom_call_target="tpu_custom_call" | custom-call | flops 28000000000 | bytes 1000 | tf_op jit(solution)/shard_map/pallas_call | solution.py:49
  137.2 1.0 copy-done.12
  138.2 7.7 %all-to-all-start.4 = ((bf16[8,64,1024]{2,1,0:T(8,128)(2,1)}), bf16[8,64,1024]{2,1,0:T(8,128)(2,1)}, u32[]{:S(2)}, u32[]{:S(2)}) async-start(bf16[8,64,1024]{2,1,0:T(8,128)(2,1)} %copy-done.12), calls=%async_computation.4 | async-start | bytes 2097152 | tf_op jit(solution)/shard_map/all_to_all | solution.py:40
  145.9 0.3 collective-permute-start.9
  146.2 2.3 %collective-permute-start.10 = (f32[8,2048]{1,0:T(8,128)S(1)}, f32[8,2048]{1,0:T(8,128)S(1)}, u32[]{:S(2)}, u32[]{:S(2)}) collective-permute-start(f32[8,2048]{1,0:T(8,128)S(1)} %add.73), channel_id=1, source_target_pairs={{0,6},{2,4},{4,2},{6,0},{1,7},{3,5},{5,3},{7,1},{8,14},{10,12},{12... | collective-permute-start | bytes 196616 | tf_op jit(solution)/shard_map/ppermute | solution.py:36
  148.5 1.5 collective-permute-start.11
  150.0 1.0 copy-done.10
  151.0 2.5 %shard_map.120 = bf16[256,2048]{1,0:T(8,128)(2,1)} custom-call(s32[4]{0:T(128)S(1)} %copy-done.15, bf16[512,256]{1,0:T(8,128)(2,1)S(1)} %copy-done.8, bf16[512,2048]{1,0:T(8,128)(2,1)S(1)} %bitcast.41, bf16[256,128]{1,0:T(8,128)(2,1)S(1)} %copy-done.13, bf16[2048,128]{1,0:T(8,128)(2,1)S(1)} %copy-done.10), custom_call_target="tpu_custom_call" | custom-call | flops 1000 | bytes 1000 | tf_op jit(solution)/shard_map/pallas_call | solution.py:49
  153.5 0.7 collective-permute-done.11
  154.4 2.0 %collective-permute-start.13 = (f32[8,2048]{1,0:T(8,128)S(1)}, f32[8,2048]{1,0:T(8,128)S(1)}, u32[]{:S(2)}, u32[]{:S(2)}) collective-permute-start(f32[8,2048]{1,0:T(8,128)S(1)} %add_add_fusion.2), channel_id=1, source_target_pairs={{0,192},{64,128},{128,64},{192,0},{1,193},{65,129},{129,65},{193,1... | collective-permute-start | bytes 196616 | tf_op jit(solution)/shard_map/ppermute | solution.py:36
  156.4 2.0 %collective-permute-start.14 = (f32[8,2048]{1,0:T(8,128)S(1)}, f32[8,2048]{1,0:T(8,128)S(1)}, u32[]{:S(2)}, u32[]{:S(2)}) collective-permute-start(f32[8,2048]{1,0:T(8,128)S(1)} %add_add_fusion.2), channel_id=1, source_target_pairs={{0,128},{64,192},{128,0},{192,64},{1,129},{65,193},{129,1},{193,65... | collective-permute-start | bytes 196616 | tf_op jit(solution)/shard_map/ppermute | solution.py:36
  158.5 0.5 collective-permute-done.12
  159.0 1.9 %collective-permute-done.13 = f32[8,2048]{1,0:T(8,128)S(1)} collective-permute-done((f32[8,2048]{1,0:T(8,128)S(1)}, f32[8,2048]{1,0:T(8,128)S(1)}, u32[]{:S(2)}, u32[]{:S(2)}) %collective-permute-start.13) | collective-permute-done | bytes 65568 | tf_op jit(solution)/shard_map/ppermute | solution.py:36
  160.9 1.3 collective-permute-done.14
  162.2 3.0 %collective-permute-start.17 = (f32[8,2048]{1,0:T(8,128)S(1)}, f32[8,2048]{1,0:T(8,128)S(1)}, u32[]{:S(2)}, u32[]{:S(2)}) collective-permute-start(f32[8,2048]{1,0:T(8,128)S(1)} %add_add_fusion.1), channel_id=1, source_target_pairs={{0,16},{1,17},{16,0},{17,1},{32,48},{33,49},{48,32},{49,33},{8,56}... | collective-permute-start | bytes 196616 | tf_op jit(solution)/shard_map/ppermute | solution.py:517
  165.2 1.0 collective-permute-start.18
  166.2 0.5 collective-permute-start.16
  166.7 0.7 collective-permute-start.15
  167.4 8.9 %collective-permute-done.17 = f32[8,2048]{1,0:T(8,128)S(1)} collective-permute-done((f32[8,2048]{1,0:T(8,128)S(1)}, f32[8,2048]{1,0:T(8,128)S(1)}, u32[]{:S(2)}, u32[]{:S(2)}) %collective-permute-start.17) | collective-permute-done | bytes 65568 | tf_op jit(solution)/shard_map/ppermute | solution.py:517
  176.2 1.3 collective-permute-done.16
  177.5 3.5 %collective-permute-start.19 = (f32[8,2048]{1,0:T(8,128)S(1)}, f32[8,2048]{1,0:T(8,128)S(1)}, u32[]{:S(2)}, u32[]{:S(2)}) collective-permute-start(f32[8,2048]{1,0:T(8,128)S(1)} %add_add_fusion), channel_id=1, source_target_pairs={{0,8},{8,0},{1,9},{9,1},{2,10},{10,2},{3,11},{11,3},{4,12},{12,4},... | collective-permute-start | bytes 196616 | tf_op jit(solution)/shard_map/ppermute | solution.py:36
  181.0 0.9 collective-permute-done.19
  181.9 0.6 add.83
  182.6 2.1 %shard_map.121 = (f32[32,2048]{1,0:T(8,128)}, f32[64,1024]{1,0:T(8,128)}) custom-call(s32[4]{0:T(128)S(1)} %copy-done.15, bf16[8,64,1024]{2,1,0:T(8,128)(2,1)} %all-to-all-done.4.got), custom_call_target="tpu_custom_call" | custom-call | flops 1000 | bytes 1000 | tf_op jit(solution)/shard_map/pallas_call | solution.py:49
  (83 shorter events, 1.0 us)
Async XLA Ops:
  0.6 14.2 %copy-start = (bf16[256,2048]{1,0:T(8,128)(2,1)S(1)}, bf16[256,2048]{1,0:T(8,128)(2,1)}, u32[]{:S(2)}) copy-start(bf16[256,2048]{1,0:T(8,128)(2,1)} %param.9) | copy-start | bytes 3145732
  1.4 13.4 %copy-start.22 = (s32[256,1]{0,1:T(1,128)}, s32[256,1]{0,1:T(1,128)S(1)}, u32[]{:S(2)}) copy-start(s32[256,1]{0,1:T(1,128)S(1)} %get-tuple-element.163) | copy-start | bytes 3076
  2.2 12.6 %copy-start.24 = (pred[256]{0:T(512)(128)(4,1)}, pred[256]{0:T(512)(128)(4,1)S(1)}, u32[]{:S(2)}) copy-start(pred[256]{0:T(512)(128)(4,1)S(1)} %get-tuple-element.156) | copy-start | bytes 772
  2.2 12.6 %copy-start.25 = (pred[256]{0:T(512)(128)(4,1)}, pred[256]{0:T(512)(128)(4,1)S(1)}, u32[]{:S(2)}) copy-start(pred[256]{0:T(512)(128)(4,1)S(1)} %get-tuple-element.157) | copy-start | bytes 772
  5.6 6.3 %copy-start.20 = (s32[256,2]{0,1:T(2,128)S(1)}, s32[256,2]{0,1:T(2,128)}, u32[]{:S(2)}) copy-start(s32[256,2]{0,1:T(2,128)} %param.15) | copy-start | bytes 6148
  5.6 6.3 %copy-start.18 = (bf16[2048,8]{0,1:T(8,128)(2,1)S(1)}, bf16[2048,8]{0,1:T(8,128)(2,1)}, u32[]{:S(2)}) copy-start(bf16[2048,8]{0,1:T(8,128)(2,1)} %param.10) | copy-start | bytes 98308
  5.6 8.3 %copy-start.21 = (s32[256,2]{0,1:T(2,128)S(1)}, s32[256,2]{0,1:T(2,128)}, u32[]{:S(2)}) copy-start(s32[256,2]{0,1:T(2,128)} %param.13) | copy-start | bytes 6148
  5.6 31.5 %all-to-all-start.1 = ((bf16[8,64,2048]{2,1,0:T(8,128)(2,1)}), bf16[8,64,2048]{2,1,0:T(8,128)(2,1)S(1)}, u32[]{:S(2)}, u32[]{:S(2)}) async-start(bf16[8,64,2048]{2,1,0:T(8,128)(2,1)} %bitcast.44), calls=%async_computation.1 | async-start | bytes 4194304 | tf_op jit(solution)/shard_map/all_to_all | solution.py:40
  13.9 0.6 copy-start.23
  37.1 43.3 %copy-start.1 = (bf16[8,64,2048]{2,1,0:T(8,128)(2,1)}, bf16[8,64,2048]{2,1,0:T(8,128)(2,1)S(1)}, u32[]{:S(2)}) copy-start(bf16[8,64,2048]{2,1,0:T(8,128)(2,1)S(1)} %all-to-all-done.1) | copy-start | bytes 6291460
  37.1 31.5 %all-to-all-start = ((bf16[8,64,2176]{2,1,0:T(8,128)(2,1)}), bf16[8,64,2176]{2,1,0:T(8,128)(2,1)}, u32[]{:S(2)}, u32[]{:S(2)}) async-start(bf16[8,64,2176]{2,1,0:T(8,128)(2,1)} %bitcast.43), calls=%async_computation | async-start | bytes 4456448 | tf_op jit(solution)/shard_map/all_to_all | solution.py:40
  43.1 25.5 %collective-permute-start = (bf16[512,2048]{1,0:T(8,128)(2,1)S(1)}, bf16[512,2048]{1,0:T(8,128)(2,1)}, u32[]{:S(2)}, u32[]{:S(2)}) collective-permute-start(bf16[512,2048]{1,0:T(8,128)(2,1)S(1)} %bitcast.36), channel_id=1, source_target_pairs={{0,8},{8,0},{1,9},{9,1},{2,10},{10,2},{3,11},{11,3},{4,12},{12,4},... | collective-permute-start | bytes 6291464 | tf_op jit(solution)/shard_map/ppermute | solution.py:36
  49.6 19.0 %collective-permute-start.1 = (bf16[512,1024]{1,0:T(8,128)(2,1)}, bf16[512,1024]{1,0:T(8,128)(2,1)}, u32[]{:S(2)}, u32[]{:S(2)}) collective-permute-start(bf16[512,1024]{1,0:T(8,128)(2,1)} %get-tuple-element.116.act_ref.refs_4_.refs_0_), channel_id=1, source_target_pairs={{0,8},{8,0},{1,9},{9,1},{2,10},{10,2},{3,11},{11,3},{4,12},{12,4},... | collective-permute-start | bytes 3145736 | tf_op jit(solution)/shard_map/ppermute | solution.py:36
  53.4 27.0 %copy-start.14 = (s32[4]{0:T(128)}, s32[4]{0:T(128)S(1)}, u32[]{:S(2)}) copy-start(s32[4]{0:T(128)S(1)} %pad_add_fusion.pos_ref) | copy-start | bytes 52
  68.6 2.3 %copy-start.9 = (f32[512,1024]{1,0:T(8,128)S(1)}, f32[512,1024]{1,0:T(8,128)}, u32[]{:S(2)}) copy-start(f32[512,1024]{1,0:T(8,128)} %get-tuple-element.84.slope_ref) | copy-start | bytes 6291460
  70.8 9.6 %copy-start.3 = (bf16[512,1024]{1,0:T(8,128)(2,1)}, bf16[512,1024]{1,0:T(8,128)(2,1)S(1)}, u32[]{:S(2)}) copy-start(bf16[512,1024]{1,0:T(8,128)(2,1)S(1)} %get-tuple-element.120.refs_0_.refs_4_) | copy-start | bytes 3145732
  70.8 9.6 %collective-permute-start.2 = (bf16[512,1024]{1,0:T(8,128)(2,1)S(1)}, bf16[512,1024]{1,0:T(8,128)(2,1)S(1)}, u32[]{:S(2)}, u32[]{:S(2)}) collective-permute-start(bf16[512,1024]{1,0:T(8,128)(2,1)S(1)} %get-tuple-element.81), channel_id=1, source_target_pairs={{0,8},{8,0},{1,9},{9,1},{2,10},{10,2},{3,11},{11,3},{4,12},{12,4},... | collective-permute-start | bytes 3145736 | tf_op jit(solution)/shard_map/ppermute | solution.py:36
  71.0 2.5 %copy-start.7 = (bf16[1,1024,2048]{2,1,0:T(8,128)(2,1)S(1)}, bf16[1,1024,2048]{2,1,0:T(8,128)(2,1)}, u32[]{:S(2)}) copy-start(bf16[1,1024,2048]{2,1,0:T(8,128)(2,1)} %param.12) | copy-start | bytes 12582916
  78.5 7.6 %copy-start.2 = (bf16[512,1024]{1,0:T(8,128)(2,1)}, bf16[512,1024]{1,0:T(8,128)(2,1)S(1)}, u32[]{:S(2)}) copy-start(bf16[512,1024]{1,0:T(8,128)(2,1)S(1)} %get-tuple-element.122.refs_2_.grad.refs_6_) | copy-start | bytes 3145732
  78.5 1.9 %collective-permute-start.3 = (bf16[512,512]{1,0:T(8,128)(2,1)S(1)}, bf16[512,512]{1,0:T(8,128)(2,1)S(1)}, u32[]{:S(2)}, u32[]{:S(2)}) collective-permute-start(bf16[512,512]{1,0:T(8,128)(2,1)S(1)} %get-tuple-element.88), channel_id=1, source_target_pairs={{0,8},{8,0},{1,9},{9,1},{2,10},{10,2},{3,11},{11,3},{4,12},{12,4},... | collective-permute-start | bytes 1572872 | tf_op jit(solution)/shard_map/ppermute | solution.py:36
  80.4 5.7 %copy-start.5 = (bf16[512,512]{1,0:T(8,128)(2,1)}, bf16[512,512]{1,0:T(8,128)(2,1)S(1)}, u32[]{:S(2)}) copy-start(bf16[512,512]{1,0:T(8,128)(2,1)S(1)} %collective-permute-done.3.refs_3_.refs_7_) | copy-start | bytes 1572868
  80.4 5.7 %copy-start.4 = (bf16[512,1024]{1,0:T(8,128)(2,1)}, bf16[512,1024]{1,0:T(8,128)(2,1)S(1)}, u32[]{:S(2)}) copy-start(bf16[512,1024]{1,0:T(8,128)(2,1)S(1)} %collective-permute-done.2.refs_1_.refs_5_) | copy-start | bytes 3145732
  86.1 31.1 %collective-permute-start.4 = (bf16[1024,512]{1,0:T(8,128)(2,1)}, bf16[1024,512]{1,0:T(8,128)(2,1)}, u32[]{:S(2)}, u32[]{:S(2)}) collective-permute-start(bf16[1024,512]{1,0:T(8,128)(2,1)} %get-tuple-element.92), channel_id=1, source_target_pairs={{0,64},{64,0},{128,192},{192,128},{1,65},{65,1},{129,193},{193,129... | collective-permute-start | bytes 3145736 | tf_op jit(solution)/shard_map/ppermute | solution.py:36
  88.0 29.3 %collective-permute-start.5 = (bf16[1024,512]{1,0:T(8,128)(2,1)}, bf16[1024,512]{1,0:T(8,128)(2,1)}, u32[]{:S(2)}, u32[]{:S(2)}) collective-permute-start(bf16[1024,512]{1,0:T(8,128)(2,1)} %get-tuple-element.93), channel_id=1, source_target_pairs={{0,192},{64,128},{128,64},{192,0},{1,193},{65,129},{129,65},{193,1... | collective-permute-start | bytes 3145736 | tf_op jit(solution)/shard_map/ppermute | solution.py:36
  90.2 12.2 %all-to-all-start.2 = ((bf16[8,64,128]{2,1,0:T(8,128)(2,1)}), bf16[8,64,128]{2,1,0:T(8,128)(2,1)S(1)}, u32[]{:S(2)}, u32[]{:S(2)}) async-start(bf16[8,64,128]{2,1,0:T(8,128)(2,1)} %bitcast.16), calls=%async_computation.2 | async-start | bytes 262144 | tf_op jit(solution)/shard_map/all_to_all | solution.py:40
  102.4 0.7 copy-start.17
  102.4 9.8 %copy-start.15 = (s32[4]{0:T(128)S(1)}, s32[4]{0:T(128)}, u32[]{:S(2)}) copy-start(s32[4]{0:T(128)} %copy-done.14) | copy-start | bytes 52
  103.0 35.1 %all-to-all-start.3 = ((bf16[8,64,2048]{2,1,0:T(8,128)(2,1)}), bf16[8,64,2048]{2,1,0:T(8,128)(2,1)S(1)}, u32[]{:S(2)}, u32[]{:S(2)}) async-start(bf16[8,64,2048]{2,1,0:T(8,128)(2,1)} %bitcast.45), calls=%async_computation.3 | async-start | bytes 4194304 | tf_op jit(solution)/shard_map/all_to_all | solution.py:40
  108.8 3.4 %copy-start.6 = (bf16[512,512]{1,0:T(8,128)(2,1)S(1)}, bf16[512,512]{1,0:T(8,128)(2,1)}, u32[]{:S(2)}) copy-start(bf16[512,512]{1,0:T(8,128)(2,1)} %copy-done.5) | copy-start | bytes 1572868
  117.3 1.2 copy-start.11
  118.5 2.9 %copy-start.19 = (f32[8,2048]{1,0:T(8,128)S(1)}, f32[8,2048]{1,0:T(8,128)}, u32[]{:S(2)}) copy-start(f32[8,2048]{1,0:T(8,128)} %get-tuple-element.129) | copy-start | bytes 196612
  120.3 13.9 %collective-permute-start.6 = (bf16[512,512]{1,0:T(8,128)(2,1)S(1)}, bf16[512,512]{1,0:T(8,128)(2,1)S(1)}, u32[]{:S(2)}, u32[]{:S(2)}) collective-permute-start(bf16[512,512]{1,0:T(8,128)(2,1)S(1)} %get-tuple-element.115), channel_id=1, source_target_pairs={{0,192},{64,128},{128,64},{192,0},{1,193},{65,129},{129,65},{193,1... | collective-permute-start | bytes 1572872 | tf_op jit(solution)/shard_map/ppermute | solution.py:36
  121.4 12.8 %collective-permute-start.7 = (bf16[512,512]{1,0:T(8,128)(2,1)S(1)}, bf16[512,512]{1,0:T(8,128)(2,1)S(1)}, u32[]{:S(2)}, u32[]{:S(2)}) collective-permute-start(bf16[512,512]{1,0:T(8,128)(2,1)S(1)} %get-tuple-element.128), channel_id=1, source_target_pairs={{0,64},{64,0},{128,192},{192,128},{1,65},{65,1},{129,193},{193,129... | collective-permute-start | bytes 1572872 | tf_op jit(solution)/shard_map/ppermute | solution.py:36
  121.4 4.6 %collective-permute-start.8 = (f32[8,2048]{1,0:T(8,128)S(1)}, f32[8,2048]{1,0:T(8,128)S(1)}, u32[]{:S(2)}, u32[]{:S(2)}) collective-permute-start(f32[8,2048]{1,0:T(8,128)S(1)} %copy-done.19), channel_id=1, source_target_pairs={{0,8},{8,0},{1,9},{9,1},{2,10},{10,2},{3,11},{11,3},{4,12},{12,4},... | collective-permute-start | bytes 196616 | tf_op jit(solution)/shard_map/ppermute | solution.py:36
  134.2 1.0 copy-start.16
  137.2 1.0 copy-start.12
  138.2 11.8 %copy-start.8 = (bf16[512,256]{1,0:T(8,128)(2,1)S(1)}, bf16[512,256]{1,0:T(8,128)(2,1)}, u32[]{:S(2)}) copy-start(bf16[512,256]{1,0:T(8,128)(2,1)} %fusion.12.disp) | copy-start | bytes 786436
  138.2 11.8 %copy-start.13 = (bf16[256,128]{1,0:T(8,128)(2,1)S(1)}, bf16[256,128]{1,0:T(8,128)(2,1)}, u32[]{:S(2)}) copy-start(bf16[256,128]{1,0:T(8,128)(2,1)} %get-tuple-element.139.logit) | copy-start | bytes 196612
  138.2 44.4 %all-to-all-start.4 = ((bf16[8,64,1024]{2,1,0:T(8,128)(2,1)}), bf16[8,64,1024]{2,1,0:T(8,128)(2,1)}, u32[]{:S(2)}, u32[]{:S(2)}) async-start(bf16[8,64,1024]{2,1,0:T(8,128)(2,1)} %copy-done.12), calls=%async_computation.4 | async-start | bytes 2097152 | tf_op jit(solution)/shard_map/all_to_all | solution.py:40
  145.9 7.7 %collective-permute-start.9 = (f32[8,2048]{1,0:T(8,128)S(1)}, f32[8,2048]{1,0:T(8,128)S(1)}, u32[]{:S(2)}, u32[]{:S(2)}) collective-permute-start(f32[8,2048]{1,0:T(8,128)S(1)} %add.73), channel_id=1, source_target_pairs={{0,2},{2,0},{4,6},{6,4},{1,3},{3,1},{5,7},{7,5},{8,10},{10,8},{12,... | collective-permute-start | bytes 196616 | tf_op jit(solution)/shard_map/ppermute | solution.py:36
  146.2 7.4 %collective-permute-start.10 = (f32[8,2048]{1,0:T(8,128)S(1)}, f32[8,2048]{1,0:T(8,128)S(1)}, u32[]{:S(2)}, u32[]{:S(2)}) collective-permute-start(f32[8,2048]{1,0:T(8,128)S(1)} %add.73), channel_id=1, source_target_pairs={{0,6},{2,4},{4,2},{6,0},{1,7},{3,5},{5,3},{7,1},{8,14},{10,12},{12... | collective-permute-start | bytes 196616 | tf_op jit(solution)/shard_map/ppermute | solution.py:36
  148.5 5.8 %collective-permute-start.11 = (f32[8,2048]{1,0:T(8,128)S(1)}, f32[8,2048]{1,0:T(8,128)S(1)}, u32[]{:S(2)}, u32[]{:S(2)}) collective-permute-start(f32[8,2048]{1,0:T(8,128)S(1)} %add.73), channel_id=1, source_target_pairs={{0,4},{2,6},{4,0},{6,2},{1,5},{3,7},{5,1},{7,3},{8,12},{10,14},{12... | collective-permute-start | bytes 196616 | tf_op jit(solution)/shard_map/ppermute | solution.py:36
  150.0 1.0 copy-start.10
  154.3 4.7 %collective-permute-start.12 = (f32[8,2048]{1,0:T(8,128)S(1)}, f32[8,2048]{1,0:T(8,128)S(1)}, u32[]{:S(2)}, u32[]{:S(2)}) collective-permute-start(f32[8,2048]{1,0:T(8,128)S(1)} %add_add_fusion.2), channel_id=1, source_target_pairs={{0,64},{64,0},{128,192},{192,128},{1,65},{65,1},{129,193},{193,129... | collective-permute-start | bytes 196616 | tf_op jit(solution)/shard_map/ppermute | solution.py:36
  154.4 6.5 %collective-permute-start.13 = (f32[8,2048]{1,0:T(8,128)S(1)}, f32[8,2048]{1,0:T(8,128)S(1)}, u32[]{:S(2)}, u32[]{:S(2)}) collective-permute-start(f32[8,2048]{1,0:T(8,128)S(1)} %add_add_fusion.2), channel_id=1, source_target_pairs={{0,192},{64,128},{128,64},{192,0},{1,193},{65,129},{129,65},{193,1... | collective-permute-start | bytes 196616 | tf_op jit(solution)/shard_map/ppermute | solution.py:36
  156.4 5.8 %collective-permute-start.14 = (f32[8,2048]{1,0:T(8,128)S(1)}, f32[8,2048]{1,0:T(8,128)S(1)}, u32[]{:S(2)}, u32[]{:S(2)}) collective-permute-start(f32[8,2048]{1,0:T(8,128)S(1)} %add_add_fusion.2), channel_id=1, source_target_pairs={{0,128},{64,192},{128,0},{192,64},{1,129},{65,193},{129,1},{193,65... | collective-permute-start | bytes 196616 | tf_op jit(solution)/shard_map/ppermute | solution.py:36
  162.2 14.0 %collective-permute-start.17 = (f32[8,2048]{1,0:T(8,128)S(1)}, f32[8,2048]{1,0:T(8,128)S(1)}, u32[]{:S(2)}, u32[]{:S(2)}) collective-permute-start(f32[8,2048]{1,0:T(8,128)S(1)} %add_add_fusion.1), channel_id=1, source_target_pairs={{0,16},{1,17},{16,0},{17,1},{32,48},{33,49},{48,32},{49,33},{8,56}... | collective-permute-start | bytes 196616 | tf_op jit(solution)/shard_map/ppermute | solution.py:517
  165.2 11.0 %collective-permute-start.18 = (f32[8,2048]{1,0:T(8,128)S(1)}, f32[8,2048]{1,0:T(8,128)S(1)}, u32[]{:S(2)}, u32[]{:S(2)}) collective-permute-start(f32[8,2048]{1,0:T(8,128)S(1)} %add_add_fusion.1), channel_id=1, source_target_pairs={{0,17},{1,16},{16,1},{17,0},{32,49},{33,48},{48,33},{49,32},{8,57}... | collective-permute-start | bytes 196616 | tf_op jit(solution)/shard_map/ppermute | solution.py:517
  166.2 11.3 %collective-permute-start.16 = (f32[8,2048]{1,0:T(8,128)S(1)}, f32[8,2048]{1,0:T(8,128)S(1)}, u32[]{:S(2)}, u32[]{:S(2)}) collective-permute-start(f32[8,2048]{1,0:T(8,128)S(1)} %add_add_fusion.1), channel_id=1, source_target_pairs={{0,1},{1,0},{16,17},{17,16},{32,33},{33,32},{48,49},{49,48},{8,41}... | collective-permute-start | bytes 196616 | tf_op jit(solution)/shard_map/ppermute | solution.py:517
  166.7 10.8 %collective-permute-start.15 = (f32[8,2048]{1,0:T(8,128)S(1)}, f32[8,2048]{1,0:T(8,128)S(1)}, u32[]{:S(2)}, u32[]{:S(2)}) collective-permute-start(f32[8,2048]{1,0:T(8,128)S(1)} %add_add_fusion.1), channel_id=1, source_target_pairs={{8,40},{9,41},{24,56},{25,57},{40,8},{41,9},{56,24},{57,25},{10,42... | collective-permute-start | bytes 196616 | tf_op jit(solution)/shard_map/ppermute | solution.py:517
  177.5 4.4 %collective-permute-start.19 = (f32[8,2048]{1,0:T(8,128)S(1)}, f32[8,2048]{1,0:T(8,128)S(1)}, u32[]{:S(2)}, u32[]{:S(2)}) collective-permute-start(f32[8,2048]{1,0:T(8,128)S(1)} %add_add_fusion), channel_id=1, source_target_pairs={{0,8},{8,0},{1,9},{9,1},{2,10},{10,2},{3,11},{11,3},{4,12},{12,4},... | collective-permute-start | bytes 196616 | tf_op jit(solution)/shard_map/ppermute | solution.py:36

commit v13 on v12

--- a/solution.py
+++ b/solution.py
@@ -11,7 +11,6 @@
 EXTRA = 128
 VMEM_LIMIT = 20 * 1024 * 1024
 ALL_VMEM = 58 * 1024 * 1024
-MOST_VMEM = 52 * 1024 * 1024
 LONG = 28_000_000_000
 F32 = jnp.float32
 BF16 = jnp.bfloat16
@@ -190,7 +189,7 @@
         outputs,
         far=lefts if near else lefts + rights,
         scratch=scratch,
-        vmem_limit=VMEM_LIMIT if near else MOST_VMEM,
+        vmem_limit=VMEM_LIMIT,
     )
 
 
@@ -302,12 +301,12 @@
     return outer[None], inner[None]
 
 
-def slot_grads_of(pos, grad_pre, weight_in):
+def slot_grads_of(pos, grad_pre, weight_in, gate_grad):
     slots, hidden = grad_pre.shape
     width = weight_in.shape[0]
     step = width // 4
 
-    def body(pos_ref, grad, weight, out, held, sems):
+    def body(pos_ref, grad, gate, weight, out, held, sems):
         copies = []
         for i in range(4):
             at = pl.ds(i * step, step)
@@ -319,28 +318,31 @@
             out[:, at] = lax.dot_general(
                 grad[...], held[at, :], (((1,), (1,)), ((), ())), preferred_element_type=F32
             ).astype(BF16)
+        out[:, width:] = gate[...]
 
     return call(
         body,
         pos,
-        [grad_pre],
-        [((slots, width), BF16)],
+        [grad_pre, gate_grad],
+        [((slots, width + EXTRA), BF16)],
         far=[weight_in],
         scratch=[pltpu.VMEM((width, hidden), BF16), pltpu.SemaphoreType.DMA((4,))],
         vmem_limit=ALL_VMEM,
     )[0]
 
 
-def router_grads(pos, dispatch, gate_back, token_lanes, tokens, scale):
+def router_grads(pos, dispatch, back, token_lanes, tokens, scale):
     rows, width = tokens.shape
     experts = 8
     step = width // 4
 
-    def body(pos_ref, disp, back, side, tok, logit, router, held, sem):
+    def body(pos_ref, disp, flat, side, tok, logit, router, held, sem):
         copy = pltpu.make_async_copy(tok, held, sem)
         copy.start()
         dims = (((0,), (0,)), ((), ()))
-        combine_grad = lax.dot_general(disp[...], back[...], dims, preferred_element_type=F32)
+        combine_grad = lax.dot_general(
+            disp[...], flat[:, width:], dims, preferred_element_type=F32
+        )
         probs, combine, keep, denominator = (side[k] for k in range(4))
         weighted = jnp.sum(combine_grad * combine, axis=1, keepdims=True)
         probs_grad = keep * (combine_grad - weighted) / denominator
@@ -356,7 +358,7 @@
     return call(
         body,
         pos,
-        [dispatch, gate_back, token_lanes],
+        [dispatch, back, token_lanes],
         [((rows, EXTRA), BF16), ((experts, width), F32)],
         far=[tokens],
         scratch=[pltpu.VMEM((rows, width), BF16), pltpu.SemaphoreType.DMA],
@@ -365,7 +367,7 @@
 
 
 def token_grads(pos, dispatch, back, logit_lanes, weight_lanes):
-    rows, width = dispatch.shape[1], back.shape[1]
+    rows, width = dispatch.shape[1], back.shape[1] - EXTRA
     step = width // 4
 
     def body(pos_ref, disp, flat, logit, weight, out):
@@ -465,20 +467,11 @@
 
     sent = sent_parts(pos, left_out, right_out, left_in, right_in)
     got = (swap(sent[0], "y", 1), swap(sent[1], "y", 3))
-    pre_for_slots, gate_grad, _ = tie(grad_pre, gate_grad, sent)
-    gate_back = exchange(gate_grad.reshape(experts, capacity, EXTRA), GROUP).reshape(
-        slot_count, EXTRA
-    )
-    grad_slots = slot_grads_of(pos, pre_for_slots, weight_in)
-    grad_slots, gate_back = tie(grad_slots, gate_back)
+    pre_for_slots, _ = tie(grad_pre, sent)
+    grad_slots = slot_grads_of(pos, pre_for_slots, weight_in, gate_grad)
     back = exchange(
-        grad_slots.reshape(experts, capacity, model_width), GROUP
-    ).reshape(slot_count, model_width)
-
-    gate_back, _ = tie(gate_back, grad_slots)
-    logit_lanes, router_part = router_grads(
-        pos, dispatch, gate_back, token_lanes, tokens, grad_scale
-    )
+        grad_slots.reshape(experts, capacity, model_width + EXTRA), GROUP
+    ).reshape(slot_count, model_width + EXTRA)
 
     def router_round(value, axes, one, two, *until):
         near, far, both = (swap(value, axes, mask) for mask in (one, two, one ^ two))
@@ -486,7 +479,7 @@
         return (value + near) + (far + both)
 
     left_in, left_out, right_in, right_out, _ = tie(
-        left_in, left_out, right_in, right_out, router_part
+        left_in, left_out, right_in, right_out, grad_slots
     )
     far_a, far_b = far_parts(pos, left_out, right_out, left_in, right_in)
     got, far_a, far_b = tie(got, far_a, far_b)
@@ -496,15 +489,16 @@
         left_in, left_out, right_in, right_out, far_a
     )
     near = near_parts(pos, left_out, right_out, left_in, right_in)
-    other_router = swap(router_part, "core", 1)
-    router_part, other_router, _ = tie(router_part, other_router, near)
-    router_part = router_part + other_router
-
-    near, far, router_part = tie(near, far, router_part)
+    near, far = tie(near, far)
     pieces = zh_pieces(pos, near[:2], near[2:], got, far, grad_scale)
     got = exchange(pieces, ("zh", "core"))
 
-    back, router_part, _ = tie(back, router_part, pieces)
+    back, _ = tie(back, pieces)
+    logit_lanes, router_part = router_grads(
+        pos, dispatch, back, token_lanes, tokens, grad_scale
+    )
+    back, other_router = tie(back, swap(router_part, "core", 1))
+    router_part = router_part + other_router
     grad_tokens = token_grads(pos, dispatch, back, logit_lanes, weight_lanes)
     router_part = router_round(router_part, "x", 1, 3, grad_tokens)
     router_part = router_round(router_part, "y", 1, 3)

time: 187 us -> 187 us (level)
  waiting for transfers between devices: 57.3 us -> 55.1 us
    ppermute x4, waiting for transfers between devices: 10.1 us -> 3.87 us  [per_device(): terms.append(lax.ppermute(router_part, ('zh', 'core', 'zl'), pairs))]
    ppermute x16, starting transfers between devices: 17.7 us -> 23.1 us  [swap(): return lax.ppermute(values, axis, [(i, i ^ mask) for i in range(size)])]
    all_to_all x5 -> x4, starting transfers between devices: 31.1 us -> 26.3 us  [exchange(): return lax.all_to_all(values, axes, split_axis=0, concat_axis=0, tiled=True)]
    ppermute x16, waiting for transfers between devices: 15.2 us -> 19.5 us  [swap(): return lax.ppermute(values, axis, [(i, i ^ mask) for i in range(size)])]
    unnamed x53 -> x55, local copies, waits for them, and re-layouts: 9.04 us -> 10.3 us
    all_to_all x5 -> x4, waiting for transfers between devices: 31.9 us -> 31.8 us  [exchange(): return lax.all_to_all(values, axes, split_axis=0, concat_axis=0, tiled=True)]
  transfers between devices with their start and end apart: 25 -> 24, of which waited for: 11 -> 13; matrix products, arithmetic and copies ran while one was open for 10% -> 10% of each run, Pallas kernels for 17% -> 16%
where the time goes in v13:
time: 187 us; the launch traced here: 184 us
  waiting for transfers between devices  55.1 us (29%)
  starting transfers between devices  54.5 us (29%)
  Pallas kernels  39.5 us (21%)
  local copies, waits for them, and re-layouts  13.5 us (7%)
  matrix products  12.6 us (7%)
  other arithmetic  7.33 us (4%)
    pallas_call x11, Pallas kernels, call(): pl.pallas_call(body, in_specs=[pl.BlockSpec(memory_space=pltpu.SMEM)] + [...  39.5 us
    all_to_all x4, waiting for transfers between devices, exchange(): return lax.all_to_all(values, axes, split_axis=0, concat_axis=0, tiled=True)  31.8 us
    all_to_all x4, starting transfers between devices, exchange(): return lax.all_to_all(values, axes, split_axis=0, concat_axis=0, tiled=True)  26.3 us
    ppermute x16, starting transfers between devices, swap(): return lax.ppermute(values, axis, [(i, i ^ mask) for i in range(size)])  23.1 us
    ppermute x16, waiting for transfers between devices, swap(): return lax.ppermute(values, axis, [(i, i ^ mask) for i in range(size)])  19.5 us
    unnamed x55, local copies, waits for them, and re-layouts  10.3 us
    dot_general x1, matrix products, per_device(): hidden_pre = jnp.dot(slot_tokens, weight_in, preferred_element_type=F32)  6.58 us
    ppermute x4, starting transfers between devices, per_device(): terms.append(lax.ppermute(router_part, ('zh', 'core', 'zl'), pairs))  5.13 us
  transfers between devices with their start and end apart: 24, of which 13 were waited for; matrix products, arithmetic and copies ran while one was open for 10% of the time, Pallas kernels for 16%

profile of v13, /device:TPU:2, one launch (start us, length us, event | category | flops | bytes accessed | tf_op | source)
XLA Modules:
  0.0 183.6 jit_solution(18059197349576072824)
XLA Ops:
  0.6 0.8 compare_reduce_fusion.1
  1.5 0.7 multiply_add_fusion
  2.2 3.3 %convolution_convert_fusion = bf16[512,2048]{1,0:T(8,128)(2,1)} fusion(bf16[256,2048]{1,0:T(8,128)(2,1)} %tok.1, s32[256]{0:T(256)S(1)} %bitcast.49, s32[256]{0:T(256)S(1)} %bitcast.45, pred[256]{0:T(512)(128)(4,1)S(1)} %get-tuple-element.145, pred[256]{0:T(512)(128)(4,1)S(1)} %get-tuple-element.144), kind=kOutput, calls=%fused_computation.1 | convolution fusion | flops 538574848 | bytes 3148288 | tf_op jit(solution)/shard_map/dot_general | solution.py:408
  5.5 6.3 %all-to-all-start.1 = ((bf16[8,64,2048]{2,1,0:T(8,128)(2,1)}), bf16[8,64,2048]{2,1,0:T(8,128)(2,1)S(1)}, u32[]{:S(2)}, u32[]{:S(2)}) async-start(bf16[8,64,2048]{2,1,0:T(8,128)(2,1)} %bitcast.42), calls=%async_computation.1 | async-start | bytes 4194304 | tf_op jit(solution)/shard_map/all_to_all | solution.py:39
  11.9 1.6 fusion.17
  13.9 0.6 copy-done.24
  14.8 0.7 convolution_convert_fusion.1
  15.5 1.6 pad_maximum_fusion
  17.1 19.9 %all-to-all-done.1 = bf16[8,64,2048]{2,1,0:T(8,128)(2,1)S(1)} async-done(((bf16[8,64,2048]{2,1,0:T(8,128)(2,1)}), bf16[8,64,2048]{2,1,0:T(8,128)(2,1)S(1)}, u32[]{:S(2)}, u32[]{:S(2)}) %all-to-all-start.1) | async-done | bytes 2097184 | tf_op jit(solution)/shard_map/all_to_all | solution.py:39
  37.0 6.0 %all-to-all-start = ((bf16[8,64,2176]{2,1,0:T(8,128)(2,1)}), bf16[8,64,2176]{2,1,0:T(8,128)(2,1)}, u32[]{:S(2)}, u32[]{:S(2)}) async-start(bf16[8,64,2176]{2,1,0:T(8,128)(2,1)} %bitcast.40), calls=%async_computation | async-start | bytes 4456448 | tf_op jit(solution)/shard_map/all_to_all | solution.py:39
  43.1 6.6 %fusion.3 = (f32[512,1024]{1,0:T(8,128)}, bf16[512,1024]{1,0:T(8,128)(2,1)}) fusion(bf16[512,2048]{1,0:T(8,128)(2,1)S(1)} %bitcast.35, bf16[1,2048,1024]{2,1,0:T(8,128)(2,1)} %param.11), kind=kOutput, calls=%fused_computation.7 | convolution fusion | flops 2152726528 | bytes 9437184 | tf_op jit(solution)/shard_map/dot_general | solution.py:447
  49.7 0.5 collective-permute-start.1
  50.3 1.0 copy.27
  51.5 1.9 %pad.22.weight = bf16[2048,128]{1,0:T(8,128)(2,1)} pad(bf16[2048,8]{1,0:T(8,128)(2,1)} %copy.27, bf16[]{:T(256)} %constant.39.clone.1), padding=0_0x0_120 | pad | bytes 557058 | tf_op jit(solution)/shard_map/jit(_pad)/pad | solution.py:422
  53.5 0.8 broadcast_in_dim.52
  54.3 0.8 pad_maximum_fusion.1.side
  55.1 1.6 fusion.12.disp
  56.7 11.9 %all-to-all-done = bf16[8,64,2176]{2,1,0:T(8,128)(2,1)} async-done(((bf16[8,64,2176]{2,1,0:T(8,128)(2,1)}), bf16[8,64,2176]{2,1,0:T(8,128)(2,1)}, u32[]{:S(2)}, u32[]{:S(2)}) %all-to-all-start) | async-done | bytes 2228256 | tf_op jit(solution)/shard_map/all_to_all | solution.py:39
  68.6 2.2 %shard_map.111 = (bf16[512,1024]{1,0:T(8,128)(2,1)S(1)}, bf16[512,1024]{1,0:T(8,128)(2,1)S(1)}) custom-call(s32[4]{0:T(128)S(1)} %pad_add_fusion.pos_ref, bf16[512,2176]{1,0:T(8,128)(2,1)} %bitcast.7.rec), custom_call_target="tpu_custom_call" | custom-call | flops 1000 | bytes 1000 | tf_op jit(solution)/shard_map/pallas_call | solution.py:48
  70.9 2.4 %copy-done.11 = bf16[1,1024,2048]{2,1,0:T(8,128)(2,1)S(1)} copy-done((bf16[1,1024,2048]{2,1,0:T(8,128)(2,1)S(1)}, bf16[1,1024,2048]{2,1,0:T(8,128)(2,1)}, u32[]{:S(2)}) %copy-start.11) | copy-done | bytes 4194328
  73.4 4.4 %shard_map.112 = (bf16[512,1024]{1,0:T(8,128)(2,1)S(1)}, bf16[512,512]{1,0:T(8,128)(2,1)S(1)}, bf16[512,128]{1,0:T(8,128)(2,1)S(1)}) custom-call(s32[4]{0:T(128)S(1)} %pad_add_fusion.pos_ref, bf16[512,2176]{1,0:T(8,128)(2,1)} %bitcast.7.rec, bf16[1024,2048]{1,0:T(8,128)(2,1)S(1)} %bitcast.39, bf16[512,1024]{1,0:T(8,128)(2,1)} %get-tuple-element.104.act_ref.refs_4_.refs_0_, ...), custom_call_target="tpu_custom_call" | custom-call | flops 1000 | bytes 1000 | tf_op jit(solution)/shard_map/pallas_call | solution.py:48
  77.8 0.6 copy-done.15
  78.7 1.7 collective-permute-done.3.refs_3_.refs_7_
  80.4 5.6 %shard_map.113 = (bf16[1024,512]{1,0:T(8,128)(2,1)}, bf16[1024,512]{1,0:T(8,128)(2,1)}) custom-call(s32[4]{0:T(128)S(1)} %pad_add_fusion.pos_ref, bf16[512,1024]{1,0:T(8,128)(2,1)S(1)} %get-tuple-element.108.refs_0_.refs_4_, bf16[512,1024]{1,0:T(8,128)(2,1)S(1)} %collective-permute-done.2.refs_1_.refs_5_, ...), custom_call_target="tpu_custom_call" | custom-call | flops 1000 | bytes 1000 | tf_op jit(solution)/shard_map/pallas_call | solution.py:48
  86.1 1.8 %collective-permute-start.4 = (bf16[1024,512]{1,0:T(8,128)(2,1)}, bf16[1024,512]{1,0:T(8,128)(2,1)}, u32[]{:S(2)}, u32[]{:S(2)}) collective-permute-start(bf16[1024,512]{1,0:T(8,128)(2,1)} %get-tuple-element.85), channel_id=1, source_target_pairs={{0,64},{64,0},{128,192},{192,128},{1,65},{65,1},{129,193},{193,129... | collective-permute-start | bytes 3145736 | tf_op jit(solution)/shard_map/ppermute | solution.py:35
  87.9 2.2 %collective-permute-start.5 = (bf16[1024,512]{1,0:T(8,128)(2,1)}, bf16[1024,512]{1,0:T(8,128)(2,1)}, u32[]{:S(2)}, u32[]{:S(2)}) collective-permute-start(bf16[1024,512]{1,0:T(8,128)(2,1)} %get-tuple-element.86), channel_id=1, source_target_pairs={{0,192},{64,128},{128,64},{192,0},{1,193},{65,129},{129,65},{193,1... | collective-permute-start | bytes 3145736 | tf_op jit(solution)/shard_map/ppermute | solution.py:35
  90.1 6.9 %shard_map.114 = bf16[512,2176]{1,0:T(8,128)(2,1)} custom-call(s32[4]{0:T(128)} %copy-done.17, bf16[512,1024]{1,0:T(8,128)(2,1)} %copy-done.1, bf16[512,128]{1,0:T(8,128)(2,1)} %copy-done.15, bf16[2048,1024]{1,0:T(8,128)(2,1)} %bitcast.43), custom_call_target="tpu_custom_call" | custom-call | flops 1000 | bytes 1000 | tf_op jit(solution)/shard_map/pallas_call | solution.py:48
  97.0 6.4 %all-to-all-start.2 = ((bf16[8,64,2176]{2,1,0:T(8,128)(2,1)}), bf16[8,64,2176]{2,1,0:T(8,128)(2,1)}, u32[]{:S(2)}, u32[]{:S(2)}) async-start(bf16[8,64,2176]{2,1,0:T(8,128)(2,1)} %bitcast.41), calls=%async_computation.2 | async-start | bytes 4456448 | tf_op jit(solution)/shard_map/all_to_all | solution.py:39
  103.4 1.2 copy-done.2
  104.6 1.2 copy-done.5
  105.8 1.2 copy-done.8
  107.1 1.0 copy-done.10
  108.1 3.4 %shard_map.115 = (f32[512,512]{1,0:T(8,128)S(1)}, f32[512,512]{1,0:T(8,128)S(1)}) custom-call(s32[4]{0:T(128)S(1)} %copy-done.18, bf16[512,1024]{1,0:T(8,128)(2,1)} %get-tuple-element.104.act_ref.refs_4_.refs_0_, bf16[512,1024]{1,0:T(8,128)(2,1)} %collective-permute-done.1.refs_5_.refs_1_, bf16[512,2048]{1,0:T(8,128)(2,1)S(1)} %bitcast.37, ...), custom_call_target="tpu_custom_call" | custom-call | flops 1000 | bytes 1000 | tf_op jit(solution)/shard_map/pallas_call | solution.py:48
  111.5 0.5 collective-permute-done.4.got_a
  111.9 2.5 %collective-permute-done.5.got_b = bf16[1024,512]{1,0:T(8,128)(2,1)} collective-permute-done((bf16[1024,512]{1,0:T(8,128)(2,1)}, bf16[1024,512]{1,0:T(8,128)(2,1)}, u32[]{:S(2)}, u32[]{:S(2)}) %collective-permute-start.5) | collective-permute-done | bytes 1048608 | tf_op jit(solution)/shard_map/ppermute | solution.py:35
  114.4 1.9 %shard_map.116 = (bf16[512,512]{1,0:T(8,128)(2,1)S(1)}, bf16[512,512]{1,0:T(8,128)(2,1)S(1)}) custom-call(s32[4]{0:T(128)S(1)} %copy-done.18, f32[512,512]{1,0:T(8,128)S(1)} %get-tuple-element.99.far_a, f32[512,512]{1,0:T(8,128)S(1)} %get-tuple-element.100.far_b, bf16[1024,512]{1,0:T(8,128)(2,1)} %collective-permute-done.4.got_a, ...), custom_call_target="tpu_custom_call" | custom-call | flops 1000 | bytes 1000 | tf_op jit(solution)/shard_map/pallas_call | solution.py:48
  116.4 2.3 %collective-permute-start.6 = (bf16[512,512]{1,0:T(8,128)(2,1)S(1)}, bf16[512,512]{1,0:T(8,128)(2,1)S(1)}, u32[]{:S(2)}, u32[]{:S(2)}) collective-permute-start(bf16[512,512]{1,0:T(8,128)(2,1)S(1)} %get-tuple-element.103), channel_id=1, source_target_pairs={{0,192},{64,128},{128,64},{192,0},{1,193},{65,129},{129,65},{193,1... | collective-permute-start | bytes 1572872 | tf_op jit(solution)/shard_map/ppermute | solution.py:35
  118.7 3.2 %shard_map.117 = (f32[256,512]{1,0:T(8,128)S(1)}, f32[256,512]{1,0:T(8,128)S(1)}, f32[512,256]{1,0:T(8,128)S(1)}, f32[512,256]{1,0:T(8,128)S(1)}) custom-call(s32[4]{0:T(128)S(1)} %copy-done.18, bf16[512,1024]{1,0:T(8,128)(2,1)} %get-tuple-element.104.act_ref.refs_4_.refs_0_, bf16[512,1024]{1,0:T(8,128)(2,1)} %collective-permute-done.1.refs_5_.refs_1_, ...), custom_call_target="tpu_custom_call" | custom-call | flops 1000 | bytes 1000 | tf_op jit(solution)/shard_map/pallas_call | solution.py:48
  121.8 7.5 %collective-permute-done.7.far_b = bf16[512,512]{1,0:T(8,128)(2,1)S(1)} collective-permute-done((bf16[512,512]{1,0:T(8,128)(2,1)S(1)}, bf16[512,512]{1,0:T(8,128)(2,1)S(1)}, u32[]{:S(2)}, u32[]{:S(2)}) %collective-permute-start.7) | collective-permute-done | bytes 524320 | tf_op jit(solution)/shard_map/ppermute | solution.py:35
  129.3 1.3 collective-permute-done.6.far_a
  130.6 2.9 %shard_map.118 = bf16[8,64,1024]{2,1,0:T(8,128)(2,1)} custom-call(s32[4]{0:T(128)S(1)} %copy-done.18, f32[256,512]{1,0:T(8,128)S(1)} %get-tuple-element.117.out_a, f32[256,512]{1,0:T(8,128)S(1)} %get-tuple-element.118.out_b, f32[512,256]{1,0:T(8,128)S(1)} %get-tuple-element.119.in_a, f32[512,256]{1,0:T(8,128)S(1)} %get-tuple-element.120.in_b, ...), custom_call_target="tpu_custom_call" | custom-call | flops 28000000000 | bytes 1000 | tf_op jit(solution)/shard_map/pallas_call | solution.py:48
  133.5 7.6 %all-to-all-start.3 = ((bf16[8,64,1024]{2,1,0:T(8,128)(2,1)}), bf16[8,64,1024]{2,1,0:T(8,128)(2,1)S(1)}, u32[]{:S(2)}, u32[]{:S(2)}) async-start(bf16[8,64,1024]{2,1,0:T(8,128)(2,1)} %shard_map.118), calls=%async_computation.3 | async-start | bytes 2097152 | tf_op jit(solution)/shard_map/all_to_all | solution.py:39
  141.1 4.0 %shard_map.119 = (bf16[256,128]{1,0:T(8,128)(2,1)}, f32[8,2048]{1,0:T(8,128)}) custom-call(s32[4]{0:T(128)} %copy-done.17, bf16[512,256]{1,0:T(8,128)(2,1)} %fusion.12.disp, bf16[512,2176]{1,0:T(8,128)(2,1)} %bitcast.17.flat, f32[4,256,128]{2,1,0:T(8,128)} %pad_maximum_fusion.1.side, bf16[256,2048]{1,0:T(8,128)(2,1)} %tok.1), custom_call_target="tpu_custom_call" | custom-call | flops 1000 | bytes 1000 | tf_op jit(solution)/shard_map/pallas_call | solution.py:48
  145.2 0.6 collective-permute-start.8
  145.7 1.1 collective-permute-done.8
  146.8 0.9 add.73
  147.7 2.3 %collective-permute-start.11 = (f32[8,2048]{1,0:T(8,128)S(1)}, f32[8,2048]{1,0:T(8,128)S(1)}, u32[]{:S(2)}, u32[]{:S(2)}) collective-permute-start(f32[8,2048]{1,0:T(8,128)S(1)} %add.73), channel_id=1, source_target_pairs={{0,4},{2,6},{4,0},{6,2},{1,5},{3,7},{5,1},{7,3},{8,12},{10,14},{12... | collective-permute-start | bytes 196616 | tf_op jit(solution)/shard_map/ppermute | solution.py:35
  150.0 1.3 collective-permute-start.10
  151.4 1.1 collective-permute-start.9
  152.5 0.8 copy-done.16
  153.3 3.6 %shard_map.120 = bf16[256,2048]{1,0:T(8,128)(2,1)} custom-call(s32[4]{0:T(128)S(1)} %copy-done.19, bf16[512,256]{1,0:T(8,128)(2,1)S(1)} %copy-done.12, bf16[512,2176]{1,0:T(8,128)(2,1)} %bitcast.17.flat, bf16[256,128]{1,0:T(8,128)(2,1)S(1)} %copy-done.16, bf16[2048,128]{1,0:T(8,128)(2,1)S(1)} %copy-done.14), custom_call_target="tpu_custom_call" | custom-call | flops 1000 | bytes 1000 | tf_op jit(solution)/shard_map/pallas_call | solution.py:48
  157.0 2.1 %collective-permute-start.14 = (f32[8,2048]{1,0:T(8,128)S(1)}, f32[8,2048]{1,0:T(8,128)S(1)}, u32[]{:S(2)}, u32[]{:S(2)}) collective-permute-start(f32[8,2048]{1,0:T(8,128)S(1)} %add_add_fusion.2), channel_id=1, source_target_pairs={{0,128},{64,192},{128,0},{192,64},{1,129},{65,193},{129,1},{193,65... | collective-permute-start | bytes 196616 | tf_op jit(solution)/shard_map/ppermute | solution.py:35
  159.1 1.1 collective-permute-start.13
  160.5 2.4 %collective-permute-done.14 = f32[8,2048]{1,0:T(8,128)S(1)} collective-permute-done((f32[8,2048]{1,0:T(8,128)S(1)}, f32[8,2048]{1,0:T(8,128)S(1)}, u32[]{:S(2)}, u32[]{:S(2)}) %collective-permute-start.14) | collective-permute-done | bytes 65568 | tf_op jit(solution)/shard_map/ppermute | solution.py:35
  162.9 1.7 collective-permute-done.13
  164.6 3.8 %collective-permute-start.18 = (f32[8,2048]{1,0:T(8,128)S(1)}, f32[8,2048]{1,0:T(8,128)S(1)}, u32[]{:S(2)}, u32[]{:S(2)}) collective-permute-start(f32[8,2048]{1,0:T(8,128)S(1)} %add_add_fusion.1), channel_id=1, source_target_pairs={{0,17},{1,16},{16,1},{17,0},{32,49},{33,48},{48,33},{49,32},{8,57}... | collective-permute-start | bytes 196616 | tf_op jit(solution)/shard_map/ppermute | solution.py:511
  168.4 0.7 collective-permute-start.16
  169.1 0.7 collective-permute-start.15
  169.7 2.6 %collective-permute-done.18 = f32[8,2048]{1,0:T(8,128)S(1)} collective-permute-done((f32[8,2048]{1,0:T(8,128)S(1)}, f32[8,2048]{1,0:T(8,128)S(1)}, u32[]{:S(2)}, u32[]{:S(2)}) %collective-permute-start.18) | collective-permute-done | bytes 65568 | tf_op jit(solution)/shard_map/ppermute | solution.py:511
  172.3 1.3 collective-permute-done.17
  173.6 7.0 %collective-permute-start.19 = (f32[8,2048]{1,0:T(8,128)S(1)}, f32[8,2048]{1,0:T(8,128)S(1)}, u32[]{:S(2)}, u32[]{:S(2)}) collective-permute-start(f32[8,2048]{1,0:T(8,128)S(1)} %add_add_fusion), channel_id=1, source_target_pairs={{0,8},{8,0},{1,9},{9,1},{2,10},{10,2},{3,11},{11,3},{4,12},{12,4},... | collective-permute-start | bytes 196616 | tf_op jit(solution)/shard_map/ppermute | solution.py:35
  180.6 0.9 collective-permute-done.19
  181.5 0.6 add.83
  182.2 1.4 shard_map.121
  (83 shorter events, 2.0 us)
Async XLA Ops:
  0.6 14.1 %copy-start = (bf16[256,2048]{1,0:T(8,128)(2,1)S(1)}, bf16[256,2048]{1,0:T(8,128)(2,1)}, u32[]{:S(2)}) copy-start(bf16[256,2048]{1,0:T(8,128)(2,1)} %param.9) | copy-start | bytes 3145732
  1.5 13.3 %copy-start.25 = (pred[256]{0:T(512)(128)(4,1)}, pred[256]{0:T(512)(128)(4,1)S(1)}, u32[]{:S(2)}) copy-start(pred[256]{0:T(512)(128)(4,1)S(1)} %get-tuple-element.144) | copy-start | bytes 772
  1.5 13.3 %copy-start.26 = (pred[256]{0:T(512)(128)(4,1)}, pred[256]{0:T(512)(128)(4,1)S(1)}, u32[]{:S(2)}) copy-start(pred[256]{0:T(512)(128)(4,1)S(1)} %get-tuple-element.145) | copy-start | bytes 772
  2.2 12.6 %copy-start.23 = (s32[256,1]{0,1:T(1,128)}, s32[256,1]{0,1:T(1,128)S(1)}, u32[]{:S(2)}) copy-start(s32[256,1]{0,1:T(1,128)S(1)} %get-tuple-element.151) | copy-start | bytes 3076
  5.5 6.3 %copy-start.21 = (s32[256,2]{0,1:T(2,128)S(1)}, s32[256,2]{0,1:T(2,128)}, u32[]{:S(2)}) copy-start(s32[256,2]{0,1:T(2,128)} %param.15) | copy-start | bytes 6148
  5.5 6.3 %copy-start.20 = (bf16[2048,8]{0,1:T(8,128)(2,1)S(1)}, bf16[2048,8]{0,1:T(8,128)(2,1)}, u32[]{:S(2)}) copy-start(bf16[2048,8]{0,1:T(8,128)(2,1)} %param.10) | copy-start | bytes 98308
  5.5 8.3 %copy-start.22 = (s32[256,2]{0,1:T(2,128)S(1)}, s32[256,2]{0,1:T(2,128)}, u32[]{:S(2)}) copy-start(s32[256,2]{0,1:T(2,128)} %param.13) | copy-start | bytes 6148
  5.5 31.5 %all-to-all-start.1 = ((bf16[8,64,2048]{2,1,0:T(8,128)(2,1)}), bf16[8,64,2048]{2,1,0:T(8,128)(2,1)S(1)}, u32[]{:S(2)}, u32[]{:S(2)}) async-start(bf16[8,64,2048]{2,1,0:T(8,128)(2,1)} %bitcast.42), calls=%async_computation.1 | async-start | bytes 4194304 | tf_op jit(solution)/shard_map/all_to_all | solution.py:39
  13.9 0.6 copy-start.24
  37.0 31.5 %all-to-all-start = ((bf16[8,64,2176]{2,1,0:T(8,128)(2,1)}), bf16[8,64,2176]{2,1,0:T(8,128)(2,1)}, u32[]{:S(2)}, u32[]{:S(2)}) async-start(bf16[8,64,2176]{2,1,0:T(8,128)(2,1)} %bitcast.40), calls=%async_computation | async-start | bytes 4456448 | tf_op jit(solution)/shard_map/all_to_all | solution.py:39
  43.1 25.5 %collective-permute-start = (bf16[512,2048]{1,0:T(8,128)(2,1)S(1)}, bf16[512,2048]{1,0:T(8,128)(2,1)}, u32[]{:S(2)}, u32[]{:S(2)}) collective-permute-start(bf16[512,2048]{1,0:T(8,128)(2,1)S(1)} %bitcast.34), channel_id=1, source_target_pairs={{0,8},{8,0},{1,9},{9,1},{2,10},{10,2},{3,11},{11,3},{4,12},{12,4},... | collective-permute-start | bytes 6291464 | tf_op jit(solution)/shard_map/ppermute | solution.py:35
  49.7 18.9 %collective-permute-start.1 = (bf16[512,1024]{1,0:T(8,128)(2,1)}, bf16[512,1024]{1,0:T(8,128)(2,1)}, u32[]{:S(2)}, u32[]{:S(2)}) collective-permute-start(bf16[512,1024]{1,0:T(8,128)(2,1)} %get-tuple-element.104.act_ref.refs_4_.refs_0_), channel_id=1, source_target_pairs={{0,8},{8,0},{1,9},{9,1},{2,10},{10,2},{3,11},{11,3},{4,12},{12,4},... | collective-permute-start | bytes 3145736 | tf_op jit(solution)/shard_map/ppermute | solution.py:35
  53.5 26.9 %copy-start.17 = (s32[4]{0:T(128)}, s32[4]{0:T(128)S(1)}, u32[]{:S(2)}) copy-start(s32[4]{0:T(128)S(1)} %pad_add_fusion.pos_ref) | copy-start | bytes 52
  68.6 2.3 %copy-start.13 = (f32[512,1024]{1,0:T(8,128)S(1)}, f32[512,1024]{1,0:T(8,128)}, u32[]{:S(2)}) copy-start(f32[512,1024]{1,0:T(8,128)} %get-tuple-element.78.slope_ref) | copy-start | bytes 6291460
  70.8 9.6 %copy-start.4 = (bf16[512,1024]{1,0:T(8,128)(2,1)}, bf16[512,1024]{1,0:T(8,128)(2,1)S(1)}, u32[]{:S(2)}) copy-start(bf16[512,1024]{1,0:T(8,128)(2,1)S(1)} %get-tuple-element.108.refs_0_.refs_4_) | copy-start | bytes 3145732
  70.8 9.6 %collective-permute-start.2 = (bf16[512,1024]{1,0:T(8,128)(2,1)S(1)}, bf16[512,1024]{1,0:T(8,128)(2,1)S(1)}, u32[]{:S(2)}, u32[]{:S(2)}) collective-permute-start(bf16[512,1024]{1,0:T(8,128)(2,1)S(1)} %get-tuple-element.75), channel_id=1, source_target_pairs={{0,8},{8,0},{1,9},{9,1},{2,10},{10,2},{3,11},{11,3},{4,12},{12,4},... | collective-permute-start | bytes 3145736 | tf_op jit(solution)/shard_map/ppermute | solution.py:35
  70.9 2.5 %copy-start.11 = (bf16[1,1024,2048]{2,1,0:T(8,128)(2,1)S(1)}, bf16[1,1024,2048]{2,1,0:T(8,128)(2,1)}, u32[]{:S(2)}) copy-start(bf16[1,1024,2048]{2,1,0:T(8,128)(2,1)} %param.12) | copy-start | bytes 12582916
  77.8 0.7 copy-start.15
  78.4 7.6 %copy-start.1 = (bf16[512,1024]{1,0:T(8,128)(2,1)}, bf16[512,1024]{1,0:T(8,128)(2,1)S(1)}, u32[]{:S(2)}) copy-start(bf16[512,1024]{1,0:T(8,128)(2,1)S(1)} %get-tuple-element.110.refs_2_.grad.refs_6_) | copy-start | bytes 3145732
  78.4 1.9 %collective-permute-start.3 = (bf16[512,512]{1,0:T(8,128)(2,1)S(1)}, bf16[512,512]{1,0:T(8,128)(2,1)S(1)}, u32[]{:S(2)}, u32[]{:S(2)}) collective-permute-start(bf16[512,512]{1,0:T(8,128)(2,1)S(1)} %get-tuple-element.81), channel_id=1, source_target_pairs={{0,8},{8,0},{1,9},{9,1},{2,10},{10,2},{3,11},{11,3},{4,12},{12,4},... | collective-permute-start | bytes 1572872 | tf_op jit(solution)/shard_map/ppermute | solution.py:35
  80.4 5.7 %copy-start.9 = (bf16[512,512]{1,0:T(8,128)(2,1)}, bf16[512,512]{1,0:T(8,128)(2,1)S(1)}, u32[]{:S(2)}) copy-start(bf16[512,512]{1,0:T(8,128)(2,1)S(1)} %collective-permute-done.3.refs_3_.refs_7_) | copy-start | bytes 1572868
  80.4 5.7 %copy-start.7 = (bf16[512,1024]{1,0:T(8,128)(2,1)}, bf16[512,1024]{1,0:T(8,128)(2,1)S(1)}, u32[]{:S(2)}) copy-start(bf16[512,1024]{1,0:T(8,128)(2,1)S(1)} %collective-permute-done.2.refs_1_.refs_5_) | copy-start | bytes 3145732
  86.1 25.9 %collective-permute-start.4 = (bf16[1024,512]{1,0:T(8,128)(2,1)}, bf16[1024,512]{1,0:T(8,128)(2,1)}, u32[]{:S(2)}, u32[]{:S(2)}) collective-permute-start(bf16[1024,512]{1,0:T(8,128)(2,1)} %get-tuple-element.85), channel_id=1, source_target_pairs={{0,64},{64,0},{128,192},{192,128},{1,65},{65,1},{129,193},{193,129... | collective-permute-start | bytes 3145736 | tf_op jit(solution)/shard_map/ppermute | solution.py:35
  87.9 26.5 %collective-permute-start.5 = (bf16[1024,512]{1,0:T(8,128)(2,1)}, bf16[1024,512]{1,0:T(8,128)(2,1)}, u32[]{:S(2)}, u32[]{:S(2)}) collective-permute-start(bf16[1024,512]{1,0:T(8,128)(2,1)} %get-tuple-element.86), channel_id=1, source_target_pairs={{0,192},{64,128},{128,64},{192,0},{1,193},{65,129},{129,65},{193,1... | collective-permute-start | bytes 3145736 | tf_op jit(solution)/shard_map/ppermute | solution.py:35
  97.0 6.4 %copy-start.18 = (s32[4]{0:T(128)S(1)}, s32[4]{0:T(128)}, u32[]{:S(2)}) copy-start(s32[4]{0:T(128)} %copy-done.17) | copy-start | bytes 52
  97.0 36.5 %all-to-all-start.2 = ((bf16[8,64,2176]{2,1,0:T(8,128)(2,1)}), bf16[8,64,2176]{2,1,0:T(8,128)(2,1)}, u32[]{:S(2)}, u32[]{:S(2)}) async-start(bf16[8,64,2176]{2,1,0:T(8,128)(2,1)} %bitcast.41), calls=%async_computation.2 | async-start | bytes 4456448 | tf_op jit(solution)/shard_map/all_to_all | solution.py:39
  103.4 1.2 copy-start.2
  104.6 1.2 copy-start.5
  105.8 1.2 copy-start.8
  107.1 1.0 copy-start.10
  114.4 4.3 %copy-start.3 = (bf16[512,1024]{1,0:T(8,128)(2,1)S(1)}, bf16[512,1024]{1,0:T(8,128)(2,1)}, u32[]{:S(2)}) copy-start(bf16[512,1024]{1,0:T(8,128)(2,1)} %copy-done.1) | copy-start | bytes 3145732
  114.4 4.3 %copy-start.6 = (bf16[512,1024]{1,0:T(8,128)(2,1)S(1)}, bf16[512,1024]{1,0:T(8,128)(2,1)}, u32[]{:S(2)}) copy-start(bf16[512,1024]{1,0:T(8,128)(2,1)} %copy-done.4) | copy-start | bytes 3145732
  116.3 13.0 %collective-permute-start.7 = (bf16[512,512]{1,0:T(8,128)(2,1)S(1)}, bf16[512,512]{1,0:T(8,128)(2,1)S(1)}, u32[]{:S(2)}, u32[]{:S(2)}) collective-permute-start(bf16[512,512]{1,0:T(8,128)(2,1)S(1)} %get-tuple-element.116), channel_id=1, source_target_pairs={{0,64},{64,0},{128,192},{192,128},{1,65},{65,1},{129,193},{193,129... | collective-permute-start | bytes 1572872 | tf_op jit(solution)/shard_map/ppermute | solution.py:35
  116.4 14.2 %collective-permute-start.6 = (bf16[512,512]{1,0:T(8,128)(2,1)S(1)}, bf16[512,512]{1,0:T(8,128)(2,1)S(1)}, u32[]{:S(2)}, u32[]{:S(2)}) collective-permute-start(bf16[512,512]{1,0:T(8,128)(2,1)S(1)} %get-tuple-element.103), channel_id=1, source_target_pairs={{0,192},{64,128},{128,64},{192,0},{1,193},{65,129},{129,65},{193,1... | collective-permute-start | bytes 1572872 | tf_op jit(solution)/shard_map/ppermute | solution.py:35
  133.5 48.6 %all-to-all-start.3 = ((bf16[8,64,1024]{2,1,0:T(8,128)(2,1)}), bf16[8,64,1024]{2,1,0:T(8,128)(2,1)S(1)}, u32[]{:S(2)}, u32[]{:S(2)}) async-start(bf16[8,64,1024]{2,1,0:T(8,128)(2,1)} %shard_map.118), calls=%async_computation.3 | async-start | bytes 2097152 | tf_op jit(solution)/shard_map/all_to_all | solution.py:39
  141.1 11.4 %copy-start.12 = (bf16[512,256]{1,0:T(8,128)(2,1)S(1)}, bf16[512,256]{1,0:T(8,128)(2,1)}, u32[]{:S(2)}) copy-start(bf16[512,256]{1,0:T(8,128)(2,1)} %fusion.12.disp) | copy-start | bytes 786436
  141.1 11.4 %copy-start.14 = (bf16[2048,128]{1,0:T(8,128)(2,1)S(1)}, bf16[2048,128]{1,0:T(8,128)(2,1)}, u32[]{:S(2)}) copy-start(bf16[2048,128]{1,0:T(8,128)(2,1)} %pad.22.weight) | copy-start | bytes 1572868
  141.1 11.4 %copy-start.19 = (s32[4]{0:T(128)S(1)}, s32[4]{0:T(128)}, u32[]{:S(2)}) copy-start(s32[4]{0:T(128)} %copy-done.17) | copy-start | bytes 52
  145.2 1.7 collective-permute-start.8
  147.7 9.2 %collective-permute-start.11 = (f32[8,2048]{1,0:T(8,128)S(1)}, f32[8,2048]{1,0:T(8,128)S(1)}, u32[]{:S(2)}, u32[]{:S(2)}) collective-permute-start(f32[8,2048]{1,0:T(8,128)S(1)} %add.73), channel_id=1, source_target_pairs={{0,4},{2,6},{4,0},{6,2},{1,5},{3,7},{5,1},{7,3},{8,12},{10,14},{12... | collective-permute-start | bytes 196616 | tf_op jit(solution)/shard_map/ppermute | solution.py:35
  150.0 6.9 %collective-permute-start.10 = (f32[8,2048]{1,0:T(8,128)S(1)}, f32[8,2048]{1,0:T(8,128)S(1)}, u32[]{:S(2)}, u32[]{:S(2)}) collective-permute-start(f32[8,2048]{1,0:T(8,128)S(1)} %add.73), channel_id=1, source_target_pairs={{0,6},{2,4},{4,2},{6,0},{1,7},{3,5},{5,3},{7,1},{8,14},{10,12},{12... | collective-permute-start | bytes 196616 | tf_op jit(solution)/shard_map/ppermute | solution.py:35
  151.4 5.6 %collective-permute-start.9 = (f32[8,2048]{1,0:T(8,128)S(1)}, f32[8,2048]{1,0:T(8,128)S(1)}, u32[]{:S(2)}, u32[]{:S(2)}) collective-permute-start(f32[8,2048]{1,0:T(8,128)S(1)} %add.73), channel_id=1, source_target_pairs={{0,2},{2,0},{4,6},{6,4},{1,3},{3,1},{5,7},{7,5},{8,10},{10,8},{12,... | collective-permute-start | bytes 196616 | tf_op jit(solution)/shard_map/ppermute | solution.py:35
  152.5 0.8 copy-start.16
  157.0 5.9 %collective-permute-start.14 = (f32[8,2048]{1,0:T(8,128)S(1)}, f32[8,2048]{1,0:T(8,128)S(1)}, u32[]{:S(2)}, u32[]{:S(2)}) collective-permute-start(f32[8,2048]{1,0:T(8,128)S(1)} %add_add_fusion.2), channel_id=1, source_target_pairs={{0,128},{64,192},{128,0},{192,64},{1,129},{65,193},{129,1},{193,65... | collective-permute-start | bytes 196616 | tf_op jit(solution)/shard_map/ppermute | solution.py:35
  159.1 5.5 %collective-permute-start.13 = (f32[8,2048]{1,0:T(8,128)S(1)}, f32[8,2048]{1,0:T(8,128)S(1)}, u32[]{:S(2)}, u32[]{:S(2)}) collective-permute-start(f32[8,2048]{1,0:T(8,128)S(1)} %add_add_fusion.2), channel_id=1, source_target_pairs={{0,192},{64,128},{128,64},{192,0},{1,193},{65,129},{129,65},{193,1... | collective-permute-start | bytes 196616 | tf_op jit(solution)/shard_map/ppermute | solution.py:35
  160.2 4.4 %collective-permute-start.12 = (f32[8,2048]{1,0:T(8,128)S(1)}, f32[8,2048]{1,0:T(8,128)S(1)}, u32[]{:S(2)}, u32[]{:S(2)}) collective-permute-start(f32[8,2048]{1,0:T(8,128)S(1)} %add_add_fusion.2), channel_id=1, source_target_pairs={{0,64},{64,0},{128,192},{192,128},{1,65},{65,1},{129,193},{193,129... | collective-permute-start | bytes 196616 | tf_op jit(solution)/shard_map/ppermute | solution.py:35
  164.6 7.7 %collective-permute-start.18 = (f32[8,2048]{1,0:T(8,128)S(1)}, f32[8,2048]{1,0:T(8,128)S(1)}, u32[]{:S(2)}, u32[]{:S(2)}) collective-permute-start(f32[8,2048]{1,0:T(8,128)S(1)} %add_add_fusion.1), channel_id=1, source_target_pairs={{0,17},{1,16},{16,1},{17,0},{32,49},{33,48},{48,33},{49,32},{8,57}... | collective-permute-start | bytes 196616 | tf_op jit(solution)/shard_map/ppermute | solution.py:511
  168.4 5.2 %collective-permute-start.17 = (f32[8,2048]{1,0:T(8,128)S(1)}, f32[8,2048]{1,0:T(8,128)S(1)}, u32[]{:S(2)}, u32[]{:S(2)}) collective-permute-start(f32[8,2048]{1,0:T(8,128)S(1)} %add_add_fusion.1), channel_id=1, source_target_pairs={{0,16},{1,17},{16,0},{17,1},{32,48},{33,49},{48,32},{49,33},{8,56}... | collective-permute-start | bytes 196616 | tf_op jit(solution)/shard_map/ppermute | solution.py:511
  168.4 5.2 %collective-permute-start.16 = (f32[8,2048]{1,0:T(8,128)S(1)}, f32[8,2048]{1,0:T(8,128)S(1)}, u32[]{:S(2)}, u32[]{:S(2)}) collective-permute-start(f32[8,2048]{1,0:T(8,128)S(1)} %add_add_fusion.1), channel_id=1, source_target_pairs={{0,1},{1,0},{16,17},{17,16},{32,33},{33,32},{48,49},{49,48},{8,41}... | collective-permute-start | bytes 196616 | tf_op jit(solution)/shard_map/ppermute | solution.py:511
  169.1 4.5 %collective-permute-start.15 = (f32[8,2048]{1,0:T(8,128)S(1)}, f32[8,2048]{1,0:T(8,128)S(1)}, u32[]{:S(2)}, u32[]{:S(2)}) collective-permute-start(f32[8,2048]{1,0:T(8,128)S(1)} %add_add_fusion.1), channel_id=1, source_target_pairs={{8,40},{9,41},{24,56},{25,57},{40,8},{41,9},{56,24},{57,25},{10,42... | collective-permute-start | bytes 196616 | tf_op jit(solution)/shard_map/ppermute | solution.py:511
  173.6 7.9 %collective-permute-start.19 = (f32[8,2048]{1,0:T(8,128)S(1)}, f32[8,2048]{1,0:T(8,128)S(1)}, u32[]{:S(2)}, u32[]{:S(2)}) collective-permute-start(f32[8,2048]{1,0:T(8,128)S(1)} %add_add_fusion), channel_id=1, source_target_pairs={{0,8},{8,0},{1,9},{9,1},{2,10},{10,2},{3,11},{11,3},{4,12},{12,4},... | collective-permute-start | bytes 196616 | tf_op jit(solution)/shard_map/ppermute | solution.py:35

commit v14 on v9

--- a/solution.py
+++ b/solution.py
@@ -482,7 +482,9 @@
     got, far_a, far_b = tie(got, far_a, far_b)
     far_a, far_b = far_sums(pos, (far_a, far_b), got)
     far = (swap(far_a, "y", 3), swap(far_b, "y", 1))
-    router_part = router_round(router_part, "zh", 1, 3, far_a)
+    router_part, other_router, _ = tie(router_part, swap(router_part, "core", 1), far_a)
+    router_part = router_part + other_router
+    router_part = router_round(router_part, "zh", 1, 3)
 
     near, far, router_part = tie(near, far, router_part)
     pieces = zh_pieces(pos, near[:2], near[2:], got, far, grad_scale)
@@ -490,10 +492,9 @@
 
     back, router_part, _ = tie(back, router_part, pieces)
     grad_tokens = token_grads(pos, dispatch, back, logit_lanes, weight_lanes)
-    router_part, _ = tie(router_part, grad_tokens)
-    router_part = router_round(router_part, "x", 1, 3)
+    router_part = router_round(router_part, "x", 1, 3, grad_tokens)
     router_part = router_round(router_part, "y", 1, 3)
-    router_part = router_round(router_part, ("core", "zl"), 1, 2)
+    router_part = router_part + swap(router_part, "zl", 1)
     got, router_part = tie(got, router_part)
     outer_share, inner_share = shares(pos, got, near[0].shape[0] // 8)
     return (grad_tokens, router_part.T, inner_share, outer_share)

time: 182 us -> 181 us (level)
    ppermute x20 -> x19, starting transfers between devices: 24.7 us -> 23.8 us  [swap(): return lax.ppermute(values, axis, [(i, i ^ mask) for i in range(size)])]
    ppermute x20 -> x19, waiting for transfers between devices: 26.8 us -> 26.3 us  [swap(): return lax.ppermute(values, axis, [(i, i ^ mask) for i in range(size)])]
  transfers between devices with their start and end apart: 25 -> 24, of which waited for: 13 -> 10; matrix products, arithmetic and copies ran while one was open for 11% -> 11% of each run, Pallas kernels for 12% -> 12%
where the time goes in v14:
time: 181 us; the launch traced here: 180 us
  waiting for transfers between devices  58.8 us (32%)
  starting transfers between devices  50 us (28%)
  Pallas kernels  29.1 us (16%)
  local copies, waits for them, and re-layouts  22.3 us (12%)
  matrix products  13.5 us (7%)
  other arithmetic  5.08 us (3%)
    all_to_all x5, waiting for transfers between devices, exchange(): return lax.all_to_all(values, axes, split_axis=0, concat_axis=0, tiled=True)  32.5 us
    pallas_call x10, Pallas kernels, call(): pl.pallas_call(body, in_specs=[pl.BlockSpec(memory_space=pltpu.SMEM)] + [...  29.1 us
    ppermute x19, waiting for transfers between devices, swap(): return lax.ppermute(values, axis, [(i, i ^ mask) for i in range(size)])  26.3 us
    all_to_all x5, starting transfers between devices, exchange(): return lax.all_to_all(values, axes, split_axis=0, concat_axis=0, tiled=True)  26.2 us
    ppermute x19, starting transfers between devices, swap(): return lax.ppermute(values, axis, [(i, i ^ mask) for i in range(size)])  23.8 us
    unnamed x73, local copies, waits for them, and re-layouts  17.5 us
    dot_general x1, matrix products, per_device(): hidden_pre = jnp.dot(slot_tokens, weight_in, preferred_element_type=F32)  7.47 us
  transfers between devices with their start and end apart: 24, of which 10 were waited for; matrix products, arithmetic and copies ran while one was open for 11% of the time, Pallas kernels for 12%

profile of v14, /device:TPU:2, one launch (start us, length us, event | category | flops | bytes accessed | tf_op | source)
XLA Modules:
  0.0 179.9 jit_solution(4861869301049385691)
XLA Ops:
  0.6 0.8 compare_reduce_fusion.1
  1.5 0.7 multiply_add_fusion
  2.2 3.3 %convolution_convert_fusion = bf16[512,2048]{1,0:T(8,128)(2,1)} fusion(bf16[256,2048]{1,0:T(8,128)(2,1)} %tok.1, s32[256]{0:T(256)S(1)} %bitcast.54, s32[256]{0:T(256)S(1)} %bitcast.50, pred[256]{0:T(512)(128)(4,1)S(1)} %get-tuple-element.149, pred[256]{0:T(512)(128)(4,1)S(1)} %get-tuple-element.148), kind=kOutput, calls=%fused_computation.1 | convolution fusion | flops 538574848 | bytes 3148288 | tf_op jit(solution)/shard_map/dot_general | solution.py:396
  5.6 6.3 %all-to-all-start.1 = ((bf16[8,64,2048]{2,1,0:T(8,128)(2,1)}), bf16[8,64,2048]{2,1,0:T(8,128)(2,1)S(1)}, u32[]{:S(2)}, u32[]{:S(2)}) async-start(bf16[8,64,2048]{2,1,0:T(8,128)(2,1)} %bitcast.48), calls=%async_computation.1 | async-start | bytes 4194304 | tf_op jit(solution)/shard_map/all_to_all | solution.py:38
  11.9 1.6 fusion.17
  13.9 0.5 copy-done.31
  14.8 0.7 convolution_convert_fusion.1
  15.5 1.6 pad_maximum_fusion
  17.1 20.0 %all-to-all-done.1 = bf16[8,64,2048]{2,1,0:T(8,128)(2,1)S(1)} async-done(((bf16[8,64,2048]{2,1,0:T(8,128)(2,1)}), bf16[8,64,2048]{2,1,0:T(8,128)(2,1)S(1)}, u32[]{:S(2)}, u32[]{:S(2)}) %all-to-all-start.1) | async-done | bytes 2097184 | tf_op jit(solution)/shard_map/all_to_all | solution.py:38
  37.1 1.4 copy-done.1
  38.4 5.3 %all-to-all-start = ((bf16[8,64,2176]{2,1,0:T(8,128)(2,1)}), bf16[8,64,2176]{2,1,0:T(8,128)(2,1)S(1)}, u32[]{:S(2)}, u32[]{:S(2)}) async-start(bf16[8,64,2176]{2,1,0:T(8,128)(2,1)} %bitcast.47), calls=%async_computation | async-start | bytes 4456448 | tf_op jit(solution)/shard_map/all_to_all | solution.py:38
  43.7 7.5 %fusion.3 = (f32[512,1024]{1,0:T(8,128)}, bf16[512,1024]{1,0:T(8,128)(2,1)}) fusion(bf16[512,2048]{1,0:T(8,128)(2,1)} %bitcast.39, bf16[1,2048,1024]{2,1,0:T(8,128)(2,1)} %param.11), kind=kOutput, calls=%fused_computation.7 | convolution fusion | flops 2152726528 | bytes 9437184 | tf_op jit(solution)/shard_map/dot_general | solution.py:435
  51.2 0.5 collective-permute-start.1
  51.9 1.8 %copy.27 = bf16[2048,8]{1,0:T(8,128)(2,1)} copy(bf16[2048,8]{0,1:T(8,128)(2,1)} %param.10) | data formatting | bytes 65536 | tf_op args[2]
  53.7 0.8 copy.29
  54.5 2.0 %pad.22.weight = bf16[2048,128]{1,0:T(8,128)(2,1)} pad(bf16[2048,8]{1,0:T(8,128)(2,1)} %copy.27, bf16[]{:T(256)} %constant.38.clone.1), padding=0_0x0_120 | pad | bytes 557058 | tf_op jit(solution)/shard_map/jit(_pad)/pad | solution.py:410
  56.5 0.7 broadcast_in_dim.52
  57.2 0.9 pad_bitcast_fusion
  58.2 0.9 pad_maximum_fusion.1.side
  59.2 10.5 %all-to-all-done = bf16[8,64,2176]{2,1,0:T(8,128)(2,1)S(1)} async-done(((bf16[8,64,2176]{2,1,0:T(8,128)(2,1)}), bf16[8,64,2176]{2,1,0:T(8,128)(2,1)S(1)}, u32[]{:S(2)}, u32[]{:S(2)}) %all-to-all-start) | async-done | bytes 2228256 | tf_op jit(solution)/shard_map/all_to_all | solution.py:38
  69.7 1.0 shard_map.111
  70.8 0.5 copy-done.15
  71.3 2.2 %copy-done.13 = bf16[1,1024,2048]{2,1,0:T(8,128)(2,1)S(1)} copy-done((bf16[1,1024,2048]{2,1,0:T(8,128)(2,1)S(1)}, bf16[1,1024,2048]{2,1,0:T(8,128)(2,1)}, u32[]{:S(2)}) %copy-start.13) | copy-done | bytes 4194328
  73.5 3.9 %shard_map.112 = (bf16[512,1024]{1,0:T(8,128)(2,1)S(1)}, bf16[512,512]{1,0:T(8,128)(2,1)S(1)}, bf16[512,128]{1,0:T(8,128)(2,1)S(1)}) custom-call(s32[4]{0:T(128)S(1)} %pad_add_fusion.pos_ref, bf16[512,2176]{1,0:T(8,128)(2,1)S(1)} %bitcast.37, bf16[1024,2048]{1,0:T(8,128)(2,1)S(1)} %bitcast.43, bf16[512,1024]{1,0:T(8,128)(2,1)} %get-tuple-element.97.act_ref.refs_4_.refs_0_, ...), custom_call_target="tpu_custom_call" | custom-call | flops 1000 | bytes 1000 | tf_op jit(solution)/shard_map/pallas_call | solution.py:47
  77.7 1.9 %collective-permute-done.3.refs_3_.refs_7_ = bf16[512,512]{1,0:T(8,128)(2,1)S(1)} collective-permute-done((bf16[512,512]{1,0:T(8,128)(2,1)S(1)}, bf16[512,512]{1,0:T(8,128)(2,1)S(1)}, u32[]{:S(2)}, u32[]{:S(2)}) %collective-permute-start.3) | collective-permute-done | bytes 524320 | tf_op jit(solution)/shard_map/ppermute | solution.py:34
  79.6 5.7 %shard_map.113 = (bf16[1024,512]{1,0:T(8,128)(2,1)}, bf16[1024,512]{1,0:T(8,128)(2,1)}) custom-call(s32[4]{0:T(128)S(1)} %pad_add_fusion.pos_ref, bf16[512,1024]{1,0:T(8,128)(2,1)S(1)} %get-tuple-element.101.refs_0_.refs_4_, bf16[512,1024]{1,0:T(8,128)(2,1)S(1)} %collective-permute-done.2.refs_1_.refs_5_, ...), custom_call_target="tpu_custom_call" | custom-call | flops 1000 | bytes 1000 | tf_op jit(solution)/shard_map/pallas_call | solution.py:47
  85.4 1.7 collective-permute-start.4
  87.0 2.2 %collective-permute-start.5 = (bf16[1024,512]{1,0:T(8,128)(2,1)}, bf16[1024,512]{1,0:T(8,128)(2,1)}, u32[]{:S(2)}, u32[]{:S(2)}) collective-permute-start(bf16[1024,512]{1,0:T(8,128)(2,1)} %get-tuple-element.89), channel_id=1, source_target_pairs={{0,192},{64,128},{128,64},{192,0},{1,193},{65,129},{129,65},{193,1... | collective-permute-start | bytes 3145736 | tf_op jit(solution)/shard_map/ppermute | solution.py:34
  89.2 5.1 %all-to-all-start.2 = ((bf16[8,64,128]{2,1,0:T(8,128)(2,1)}), bf16[8,64,128]{2,1,0:T(8,128)(2,1)S(1)}, u32[]{:S(2)}, u32[]{:S(2)}) async-start(bf16[8,64,128]{2,1,0:T(8,128)(2,1)} %bitcast.46), calls=%async_computation.2 | async-start | bytes 262144 | tf_op jit(solution)/shard_map/all_to_all | solution.py:38
  94.3 1.2 copy-done.6
  95.5 2.2 %copy-done.14 = bf16[1,2048,1024]{2,1,0:T(8,128)(2,1)S(1)} copy-done((bf16[1,2048,1024]{2,1,0:T(8,128)(2,1)S(1)}, bf16[1,2048,1024]{2,1,0:T(8,128)(2,1)}, u32[]{:S(2)}) %copy-start.14) | copy-done | bytes 4194328
  97.7 3.8 %shard_map.114 = bf16[512,2048]{1,0:T(8,128)(2,1)S(1)} custom-call(s32[4]{0:T(128)S(1)} %pad_add_fusion.pos_ref, bf16[512,1024]{1,0:T(8,128)(2,1)S(1)} %copy-done.6, bf16[2048,1024]{1,0:T(8,128)(2,1)S(1)} %bitcast.44), custom_call_target="tpu_custom_call" | custom-call | flops 1000 | bytes 1000 | tf_op jit(solution)/shard_map/pallas_call | solution.py:47
  101.5 1.4 copy-done.8
  102.9 5.9 %all-to-all-start.3 = ((bf16[8,64,2048]{2,1,0:T(8,128)(2,1)}), bf16[8,64,2048]{2,1,0:T(8,128)(2,1)}, u32[]{:S(2)}, u32[]{:S(2)}) async-start(bf16[8,64,2048]{2,1,0:T(8,128)(2,1)} %bitcast.42), calls=%async_computation.3 | async-start | bytes 4194304 | tf_op jit(solution)/shard_map/all_to_all | solution.py:38
  108.8 1.2 copy-done.4
  110.0 1.0 copy-done.18
  111.0 1.4 shard_map.115
  112.4 0.6 copy-done.22
  113.1 1.2 copy-done.10
  114.3 1.2 copy-done.12
  115.5 4.7 %shard_map.116 = (f32[256,512]{1,0:T(8,128)S(1)}, f32[256,512]{1,0:T(8,128)S(1)}, f32[512,256]{1,0:T(8,128)S(1)}, f32[512,256]{1,0:T(8,128)S(1)}, f32[512,512]{1,0:T(8,128)S(1)}, /*index=5*/f32[512,512]{1,0:T(8,128)S(1)}) custom-call(s32[4]{0:T(128)S(1)} %pad_add_fusion.pos_ref, bf16[512,1024]{1,0:T(8,128)(2,1)} %get-tuple-element.97.act_ref.refs_4_.refs_0_, ...), custom_call_target="tpu_custom_call" | custom-call | flops 1000 | bytes 1000 | tf_op jit(solution)/shard_map/pallas_call | solution.py:47
  120.2 1.8 shard_map.117
  122.0 0.8 collective-permute-start.7
  122.7 0.6 collective-permute-start.6
  123.4 6.4 %collective-permute-start.11 = (f32[8,2048]{1,0:T(8,128)S(1)}, f32[8,2048]{1,0:T(8,128)S(1)}, u32[]{:S(2)}, u32[]{:S(2)}) collective-permute-start(f32[8,2048]{1,0:T(8,128)S(1)} %add.73), channel_id=1, source_target_pairs={{0,32},{16,48},{32,0},{48,16},{1,33},{17,49},{33,1},{49,17},{2,34}... | collective-permute-start | bytes 196616 | tf_op jit(solution)/shard_map/ppermute | solution.py:34
  129.8 0.6 collective-permute-start.10
  130.3 0.9 collective-permute-start.9
  131.2 10.5 %collective-permute-done.11 = f32[8,2048]{1,0:T(8,128)S(1)} collective-permute-done((f32[8,2048]{1,0:T(8,128)S(1)}, f32[8,2048]{1,0:T(8,128)S(1)}, u32[]{:S(2)}, u32[]{:S(2)}) %collective-permute-start.11) | collective-permute-done | bytes 65568 | tf_op jit(solution)/shard_map/ppermute | solution.py:34
  142.2 1.9 %shard_map.118 = bf16[8,64,1024]{2,1,0:T(8,128)(2,1)S(1)} custom-call(s32[4]{0:T(128)S(1)} %pad_add_fusion.pos_ref, f32[256,512]{1,0:T(8,128)S(1)} %get-tuple-element.124.out_a, f32[256,512]{1,0:T(8,128)S(1)} %get-tuple-element.125.out_b, f32[512,256]{1,0:T(8,128)S(1)} %get-tuple-element.126.in_a, f32[512,256]{1,0:T(8,128)S(1)} %get-tuple-element.127.in_b, ...), custom_call_target="tpu_custom_call" | custom-call | flops 30000001024 | bytes 1000 | tf_op jit(solution)/shard_map/pallas_call | solution.py:47
  144.1 1.0 copy-done.20
  145.1 3.7 %all-to-all-start.4 = ((bf16[8,64,1024]{2,1,0:T(8,128)(2,1)}), bf16[8,64,1024]{2,1,0:T(8,128)(2,1)S(1)}, u32[]{:S(2)}, u32[]{:S(2)}) async-start(bf16[8,64,1024]{2,1,0:T(8,128)(2,1)} %copy-done.20), calls=%async_computation.4 | async-start | bytes 2097152 | tf_op jit(solution)/shard_map/all_to_all | solution.py:38
  148.8 2.2 %collective-permute-start.14 = (f32[8,2048]{1,0:T(8,128)S(1)}, f32[8,2048]{1,0:T(8,128)S(1)}, u32[]{:S(2)}, u32[]{:S(2)}) collective-permute-start(f32[8,2048]{1,0:T(8,128)S(1)} %add_add_fusion.2), channel_id=1, source_target_pairs={{0,4},{2,6},{4,0},{6,2},{1,5},{3,7},{5,1},{7,3},{8,12},{10,14},{12... | collective-permute-start | bytes 196616 | tf_op jit(solution)/shard_map/ppermute | solution.py:34
  151.1 2.5 %collective-permute-start.12 = (f32[8,2048]{1,0:T(8,128)S(1)}, f32[8,2048]{1,0:T(8,128)S(1)}, u32[]{:S(2)}, u32[]{:S(2)}) collective-permute-start(f32[8,2048]{1,0:T(8,128)S(1)} %add_add_fusion.2), channel_id=1, source_target_pairs={{0,2},{2,0},{4,6},{6,4},{1,3},{3,1},{5,7},{7,5},{8,10},{10,8},{12,... | collective-permute-start | bytes 196616 | tf_op jit(solution)/shard_map/ppermute | solution.py:34
  153.6 3.6 %shard_map.119 = bf16[256,2048]{1,0:T(8,128)(2,1)} custom-call(s32[4]{0:T(128)S(1)} %pad_add_fusion.pos_ref, bf16[512,256]{1,0:T(8,128)(2,1)S(1)} %fusion.12.disp, bf16[512,2048]{1,0:T(8,128)(2,1)} %bitcast.19.flat, bf16[256,128]{1,0:T(8,128)(2,1)S(1)} %copy-done.23, bf16[2048,128]{1,0:T(8,128)(2,1)S(1)} %copy-done.19), custom_call_target="tpu_custom_call" | custom-call | flops 1000 | bytes 1000 | tf_op jit(solution)/shard_map/pallas_call | solution.py:47
  157.2 1.3 collective-permute-start.17
  158.5 2.1 %collective-permute-start.16 = (f32[8,2048]{1,0:T(8,128)S(1)}, f32[8,2048]{1,0:T(8,128)S(1)}, u32[]{:S(2)}, u32[]{:S(2)}) collective-permute-start(f32[8,2048]{1,0:T(8,128)S(1)} %add_add_fusion.1), channel_id=1, source_target_pairs={{0,192},{64,128},{128,64},{192,0},{1,193},{65,129},{129,65},{193,1... | collective-permute-start | bytes 196616 | tf_op jit(solution)/shard_map/ppermute | solution.py:34
  160.8 2.7 %collective-permute-done.17 = f32[8,2048]{1,0:T(8,128)S(1)} collective-permute-done((f32[8,2048]{1,0:T(8,128)S(1)}, f32[8,2048]{1,0:T(8,128)S(1)}, u32[]{:S(2)}, u32[]{:S(2)}) %collective-permute-start.17) | collective-permute-done | bytes 65568 | tf_op jit(solution)/shard_map/ppermute | solution.py:34
  163.4 0.6 collective-permute-done.16
  164.0 0.8 collective-permute-done.15
  164.9 1.5 collective-permute-start.18
  166.4 9.3 %collective-permute-done.18 = f32[8,2048]{1,0:T(8,128)S(1)} collective-permute-done((f32[8,2048]{1,0:T(8,128)S(1)}, f32[8,2048]{1,0:T(8,128)S(1)}, u32[]{:S(2)}, u32[]{:S(2)}) %collective-permute-start.18) | collective-permute-done | bytes 65568 | tf_op jit(solution)/shard_map/ppermute | solution.py:34
  175.7 0.6 add.83
  176.4 2.1 %all-to-all-done.4.got = bf16[8,64,1024]{2,1,0:T(8,128)(2,1)S(1)} async-done(((bf16[8,64,1024]{2,1,0:T(8,128)(2,1)}), bf16[8,64,1024]{2,1,0:T(8,128)(2,1)S(1)}, u32[]{:S(2)}, u32[]{:S(2)}) %all-to-all-start.4) | async-done | bytes 1048608 | tf_op jit(solution)/shard_map/all_to_all | solution.py:38
  178.5 1.4 shard_map.120
  (100 shorter events, 2.2 us)
Async XLA Ops:
  0.6 14.1 %copy-start = (bf16[256,2048]{1,0:T(8,128)(2,1)S(1)}, bf16[256,2048]{1,0:T(8,128)(2,1)}, u32[]{:S(2)}) copy-start(bf16[256,2048]{1,0:T(8,128)(2,1)} %param.9) | copy-start | bytes 3145732
  1.5 13.3 %copy-start.32 = (pred[256]{0:T(512)(128)(4,1)}, pred[256]{0:T(512)(128)(4,1)S(1)}, u32[]{:S(2)}) copy-start(pred[256]{0:T(512)(128)(4,1)S(1)} %get-tuple-element.148) | copy-start | bytes 772
  1.5 13.3 %copy-start.34 = (pred[256]{0:T(512)(128)(4,1)}, pred[256]{0:T(512)(128)(4,1)S(1)}, u32[]{:S(2)}) copy-start(pred[256]{0:T(512)(128)(4,1)S(1)} %get-tuple-element.149) | copy-start | bytes 772
  2.2 12.5 %copy-start.27 = (s32[256,1]{0,1:T(1,128)}, s32[256,1]{0,1:T(1,128)S(1)}, u32[]{:S(2)}) copy-start(s32[256,1]{0,1:T(1,128)S(1)} %get-tuple-element.154) | copy-start | bytes 3076
  2.2 12.5 %copy-start.29 = (s32[256,1]{0,1:T(1,128)}, s32[256,1]{0,1:T(1,128)S(1)}, u32[]{:S(2)}) copy-start(s32[256,1]{0,1:T(1,128)S(1)} %get-tuple-element.155) | copy-start | bytes 3076
  5.5 6.3 %copy-start.25 = (s32[256,2]{0,1:T(2,128)S(1)}, s32[256,2]{0,1:T(2,128)}, u32[]{:S(2)}) copy-start(s32[256,2]{0,1:T(2,128)} %param.15) | copy-start | bytes 6148
  5.6 6.3 %copy-start.24 = (bf16[2048,8]{0,1:T(8,128)(2,1)S(1)}, bf16[2048,8]{0,1:T(8,128)(2,1)}, u32[]{:S(2)}) copy-start(bf16[2048,8]{0,1:T(8,128)(2,1)} %param.10) | copy-start | bytes 98308
  5.6 8.3 %copy-start.26 = (s32[256,2]{0,1:T(2,128)S(1)}, s32[256,2]{0,1:T(2,128)}, u32[]{:S(2)}) copy-start(s32[256,2]{0,1:T(2,128)} %param.13) | copy-start | bytes 6148
  5.6 31.5 %all-to-all-start.1 = ((bf16[8,64,2048]{2,1,0:T(8,128)(2,1)}), bf16[8,64,2048]{2,1,0:T(8,128)(2,1)S(1)}, u32[]{:S(2)}, u32[]{:S(2)}) async-start(bf16[8,64,2048]{2,1,0:T(8,128)(2,1)} %bitcast.48), calls=%async_computation.1 | async-start | bytes 4194304 | tf_op jit(solution)/shard_map/all_to_all | solution.py:38
  13.9 0.5 copy-start.31
  37.1 1.4 copy-start.1
  38.4 31.3 %all-to-all-start = ((bf16[8,64,2176]{2,1,0:T(8,128)(2,1)}), bf16[8,64,2176]{2,1,0:T(8,128)(2,1)S(1)}, u32[]{:S(2)}, u32[]{:S(2)}) async-start(bf16[8,64,2176]{2,1,0:T(8,128)(2,1)} %bitcast.47), calls=%async_computation | async-start | bytes 4456448 | tf_op jit(solution)/shard_map/all_to_all | solution.py:38
  43.7 26.0 %collective-permute-start = (bf16[512,2048]{1,0:T(8,128)(2,1)}, bf16[512,2048]{1,0:T(8,128)(2,1)}, u32[]{:S(2)}, u32[]{:S(2)}) collective-permute-start(bf16[512,2048]{1,0:T(8,128)(2,1)} %bitcast.38), channel_id=1, source_target_pairs={{0,8},{8,0},{1,9},{9,1},{2,10},{10,2},{3,11},{11,3},{4,12},{12,4},... | collective-permute-start | bytes 6291464 | tf_op jit(solution)/shard_map/ppermute | solution.py:34
  51.2 18.5 %collective-permute-start.1 = (bf16[512,1024]{1,0:T(8,128)(2,1)}, bf16[512,1024]{1,0:T(8,128)(2,1)}, u32[]{:S(2)}, u32[]{:S(2)}) collective-permute-start(bf16[512,1024]{1,0:T(8,128)(2,1)} %get-tuple-element.97.act_ref.refs_4_.refs_0_), channel_id=1, source_target_pairs={{0,8},{8,0},{1,9},{9,1},{2,10},{10,2},{3,11},{11,3},{4,12},{12,4},... | collective-permute-start | bytes 3145736 | tf_op jit(solution)/shard_map/ppermute | solution.py:34
  51.9 7.2 %copy-start.28 = (s32[256,1]{0,1:T(1,128)S(1)}, s32[256,1]{0,1:T(1,128)}, u32[]{:S(2)}) copy-start(s32[256,1]{0,1:T(1,128)} %copy-done.27) | copy-start | bytes 3076
  54.5 4.6 %copy-start.30 = (s32[256,1]{0,1:T(1,128)S(1)}, s32[256,1]{0,1:T(1,128)}, u32[]{:S(2)}) copy-start(s32[256,1]{0,1:T(1,128)} %copy-done.29) | copy-start | bytes 3076
  54.5 4.6 %copy-start.33 = (pred[256]{0:T(512)(128)(4,1)S(1)}, pred[256]{0:T(512)(128)(4,1)}, u32[]{:S(2)}) copy-start(pred[256]{0:T(512)(128)(4,1)} %copy-done.32) | copy-start | bytes 772
  54.5 4.6 %copy-start.35 = (pred[256]{0:T(512)(128)(4,1)S(1)}, pred[256]{0:T(512)(128)(4,1)}, u32[]{:S(2)}) copy-start(pred[256]{0:T(512)(128)(4,1)} %copy-done.34) | copy-start | bytes 772
  69.7 1.6 copy-start.15
  70.7 8.9 %copy-start.9 = (bf16[512,1024]{1,0:T(8,128)(2,1)}, bf16[512,1024]{1,0:T(8,128)(2,1)S(1)}, u32[]{:S(2)}) copy-start(bf16[512,1024]{1,0:T(8,128)(2,1)S(1)} %get-tuple-element.101.refs_0_.refs_4_) | copy-start | bytes 3145732
  70.7 8.9 %collective-permute-start.2 = (bf16[512,1024]{1,0:T(8,128)(2,1)S(1)}, bf16[512,1024]{1,0:T(8,128)(2,1)S(1)}, u32[]{:S(2)}, u32[]{:S(2)}) collective-permute-start(bf16[512,1024]{1,0:T(8,128)(2,1)S(1)} %get-tuple-element.77), channel_id=1, source_target_pairs={{0,8},{8,0},{1,9},{9,1},{2,10},{10,2},{3,11},{11,3},{4,12},{12,4},... | collective-permute-start | bytes 3145736 | tf_op jit(solution)/shard_map/ppermute | solution.py:34
  71.3 2.2 %copy-start.13 = (bf16[1,1024,2048]{2,1,0:T(8,128)(2,1)S(1)}, bf16[1,1024,2048]{2,1,0:T(8,128)(2,1)}, u32[]{:S(2)}) copy-start(bf16[1,1024,2048]{2,1,0:T(8,128)(2,1)} %param.12) | copy-start | bytes 12582916
  73.5 6.1 %copy-start.2 = (bf16[8,64,2048]{2,1,0:T(8,128)(2,1)S(1)}, bf16[8,64,2048]{2,1,0:T(8,128)(2,1)}, u32[]{:S(2)}) copy-start(bf16[8,64,2048]{2,1,0:T(8,128)(2,1)} %copy-done.1) | copy-start | bytes 6291460
  77.4 7.9 %copy-start.5 = (bf16[512,1024]{1,0:T(8,128)(2,1)}, bf16[512,1024]{1,0:T(8,128)(2,1)S(1)}, u32[]{:S(2)}) copy-start(bf16[512,1024]{1,0:T(8,128)(2,1)S(1)} %get-tuple-element.103.refs_2_.grad.refs_6_) | copy-start | bytes 3145732
  77.4 7.9 %copy-start.21 = (bf16[512,128]{1,0:T(8,128)(2,1)}, bf16[512,128]{1,0:T(8,128)(2,1)S(1)}, u32[]{:S(2)}) copy-start(bf16[512,128]{1,0:T(8,128)(2,1)S(1)} %get-tuple-element.91) | copy-start | bytes 393220
  77.4 2.2 %collective-permute-start.3 = (bf16[512,512]{1,0:T(8,128)(2,1)S(1)}, bf16[512,512]{1,0:T(8,128)(2,1)S(1)}, u32[]{:S(2)}, u32[]{:S(2)}) collective-permute-start(bf16[512,512]{1,0:T(8,128)(2,1)S(1)} %get-tuple-element.84), channel_id=1, source_target_pairs={{0,8},{8,0},{1,9},{9,1},{2,10},{10,2},{3,11},{11,3},{4,12},{12,4},... | collective-permute-start | bytes 1572872 | tf_op jit(solution)/shard_map/ppermute | solution.py:34
  79.6 5.7 %copy-start.16 = (bf16[512,512]{1,0:T(8,128)(2,1)}, bf16[512,512]{1,0:T(8,128)(2,1)S(1)}, u32[]{:S(2)}) copy-start(bf16[512,512]{1,0:T(8,128)(2,1)S(1)} %collective-permute-done.3.refs_3_.refs_7_) | copy-start | bytes 1572868
  79.6 5.8 %copy-start.11 = (bf16[512,1024]{1,0:T(8,128)(2,1)}, bf16[512,1024]{1,0:T(8,128)(2,1)S(1)}, u32[]{:S(2)}) copy-start(bf16[512,1024]{1,0:T(8,128)(2,1)S(1)} %collective-permute-done.2.refs_1_.refs_5_) | copy-start | bytes 3145732
  85.4 34.8 %collective-permute-start.4 = (bf16[1024,512]{1,0:T(8,128)(2,1)}, bf16[1024,512]{1,0:T(8,128)(2,1)}, u32[]{:S(2)}, u32[]{:S(2)}) collective-permute-start(bf16[1024,512]{1,0:T(8,128)(2,1)} %get-tuple-element.88), channel_id=1, source_target_pairs={{0,64},{64,0},{128,192},{192,128},{1,65},{65,1},{129,193},{193,129... | collective-permute-start | bytes 3145736 | tf_op jit(solution)/shard_map/ppermute | solution.py:34
  87.0 33.2 %collective-permute-start.5 = (bf16[1024,512]{1,0:T(8,128)(2,1)}, bf16[1024,512]{1,0:T(8,128)(2,1)}, u32[]{:S(2)}, u32[]{:S(2)}) collective-permute-start(bf16[1024,512]{1,0:T(8,128)(2,1)} %get-tuple-element.89), channel_id=1, source_target_pairs={{0,192},{64,128},{128,64},{192,0},{1,193},{65,129},{129,65},{193,1... | collective-permute-start | bytes 3145736 | tf_op jit(solution)/shard_map/ppermute | solution.py:34
  89.2 13.7 %all-to-all-start.2 = ((bf16[8,64,128]{2,1,0:T(8,128)(2,1)}), bf16[8,64,128]{2,1,0:T(8,128)(2,1)S(1)}, u32[]{:S(2)}, u32[]{:S(2)}) async-start(bf16[8,64,128]{2,1,0:T(8,128)(2,1)} %bitcast.46), calls=%async_computation.2 | async-start | bytes 262144 | tf_op jit(solution)/shard_map/all_to_all | solution.py:38
  94.3 1.2 copy-start.6
  95.5 2.2 %copy-start.14 = (bf16[1,2048,1024]{2,1,0:T(8,128)(2,1)S(1)}, bf16[1,2048,1024]{2,1,0:T(8,128)(2,1)}, u32[]{:S(2)}) copy-start(bf16[1,2048,1024]{2,1,0:T(8,128)(2,1)} %param.11) | copy-start | bytes 12582916
  101.5 1.4 copy-start.8
  102.9 10.2 %copy-start.3 = (bf16[8,64,2048]{2,1,0:T(8,128)(2,1)S(1)}, bf16[8,64,2048]{2,1,0:T(8,128)(2,1)}, u32[]{:S(2)}) copy-start(bf16[8,64,2048]{2,1,0:T(8,128)(2,1)} %copy-done.1) | copy-start | bytes 6291460
  102.9 42.2 %all-to-all-start.3 = ((bf16[8,64,2048]{2,1,0:T(8,128)(2,1)}), bf16[8,64,2048]{2,1,0:T(8,128)(2,1)}, u32[]{:S(2)}, u32[]{:S(2)}) async-start(bf16[8,64,2048]{2,1,0:T(8,128)(2,1)} %bitcast.42), calls=%async_computation.3 | async-start | bytes 4194304 | tf_op jit(solution)/shard_map/all_to_all | solution.py:38
  108.8 1.2 copy-start.4
  110.0 1.0 copy-start.18
  111.0 2.0 %copy-start.7 = (bf16[512,1024]{1,0:T(8,128)(2,1)S(1)}, bf16[512,1024]{1,0:T(8,128)(2,1)}, u32[]{:S(2)}) copy-start(bf16[512,1024]{1,0:T(8,128)(2,1)} %copy-done.5) | copy-start | bytes 3145732
  111.0 2.0 %copy-start.17 = (bf16[512,512]{1,0:T(8,128)(2,1)S(1)}, bf16[512,512]{1,0:T(8,128)(2,1)}, u32[]{:S(2)}) copy-start(bf16[512,512]{1,0:T(8,128)(2,1)} %copy-done.16) | copy-start | bytes 1572868
  112.4 0.6 copy-start.22
  113.1 10.3 %collective-permute-start.8 = (f32[8,2048]{1,0:T(8,128)S(1)}, f32[8,2048]{1,0:T(8,128)S(1)}, u32[]{:S(2)}, u32[]{:S(2)}) collective-permute-start(f32[8,2048]{1,0:T(8,128)S(1)} %get-tuple-element.117), channel_id=1, source_target_pairs={{0,8},{8,0},{1,9},{9,1},{2,10},{10,2},{3,11},{11,3},{4,12},{12,4},... | collective-permute-start | bytes 196616 | tf_op jit(solution)/shard_map/ppermute | solution.py:34
  113.1 1.2 copy-start.10
  114.3 1.2 copy-start.12
  122.0 20.2 %collective-permute-start.7 = (bf16[512,512]{1,0:T(8,128)(2,1)S(1)}, bf16[512,512]{1,0:T(8,128)(2,1)S(1)}, u32[]{:S(2)}, u32[]{:S(2)}) collective-permute-start(bf16[512,512]{1,0:T(8,128)(2,1)S(1)} %get-tuple-element.116), channel_id=1, source_target_pairs={{0,64},{64,0},{128,192},{192,128},{1,65},{65,1},{129,193},{193,129... | collective-permute-start | bytes 1572872 | tf_op jit(solution)/shard_map/ppermute | solution.py:34
  122.7 19.4 %collective-permute-start.6 = (bf16[512,512]{1,0:T(8,128)(2,1)S(1)}, bf16[512,512]{1,0:T(8,128)(2,1)S(1)}, u32[]{:S(2)}, u32[]{:S(2)}) collective-permute-start(bf16[512,512]{1,0:T(8,128)(2,1)S(1)} %get-tuple-element.115), channel_id=1, source_target_pairs={{0,192},{64,128},{128,64},{192,0},{1,193},{65,129},{129,65},{193,1... | collective-permute-start | bytes 1572872 | tf_op jit(solution)/shard_map/ppermute | solution.py:34
  123.4 18.3 %collective-permute-start.11 = (f32[8,2048]{1,0:T(8,128)S(1)}, f32[8,2048]{1,0:T(8,128)S(1)}, u32[]{:S(2)}, u32[]{:S(2)}) collective-permute-start(f32[8,2048]{1,0:T(8,128)S(1)} %add.73), channel_id=1, source_target_pairs={{0,32},{16,48},{32,0},{48,16},{1,33},{17,49},{33,1},{49,17},{2,34}... | collective-permute-start | bytes 196616 | tf_op jit(solution)/shard_map/ppermute | solution.py:34
  129.8 12.4 %collective-permute-start.10 = (f32[8,2048]{1,0:T(8,128)S(1)}, f32[8,2048]{1,0:T(8,128)S(1)}, u32[]{:S(2)}, u32[]{:S(2)}) collective-permute-start(f32[8,2048]{1,0:T(8,128)S(1)} %add.73), channel_id=1, source_target_pairs={{0,48},{16,32},{32,16},{48,0},{1,49},{17,33},{33,17},{49,1},{2,50}... | collective-permute-start | bytes 196616 | tf_op jit(solution)/shard_map/ppermute | solution.py:34
  130.3 11.8 %collective-permute-start.9 = (f32[8,2048]{1,0:T(8,128)S(1)}, f32[8,2048]{1,0:T(8,128)S(1)}, u32[]{:S(2)}, u32[]{:S(2)}) collective-permute-start(f32[8,2048]{1,0:T(8,128)S(1)} %add.73), channel_id=1, source_target_pairs={{0,16},{16,0},{32,48},{48,32},{1,17},{17,1},{33,49},{49,33},{2,18}... | collective-permute-start | bytes 196616 | tf_op jit(solution)/shard_map/ppermute | solution.py:34
  144.1 1.0 copy-start.20
  145.1 8.5 %copy-start.19 = (bf16[2048,128]{1,0:T(8,128)(2,1)S(1)}, bf16[2048,128]{1,0:T(8,128)(2,1)}, u32[]{:S(2)}) copy-start(bf16[2048,128]{1,0:T(8,128)(2,1)} %pad.22.weight) | copy-start | bytes 1572868
  145.1 8.5 %copy-start.23 = (bf16[256,128]{1,0:T(8,128)(2,1)S(1)}, bf16[256,128]{1,0:T(8,128)(2,1)}, u32[]{:S(2)}) copy-start(bf16[256,128]{1,0:T(8,128)(2,1)} %copy-done.22) | copy-start | bytes 196612
  145.1 33.4 %all-to-all-start.4 = ((bf16[8,64,1024]{2,1,0:T(8,128)(2,1)}), bf16[8,64,1024]{2,1,0:T(8,128)(2,1)S(1)}, u32[]{:S(2)}, u32[]{:S(2)}) async-start(bf16[8,64,1024]{2,1,0:T(8,128)(2,1)} %copy-done.20), calls=%async_computation.4 | async-start | bytes 2097152 | tf_op jit(solution)/shard_map/all_to_all | solution.py:38
  148.8 8.4 %collective-permute-start.14 = (f32[8,2048]{1,0:T(8,128)S(1)}, f32[8,2048]{1,0:T(8,128)S(1)}, u32[]{:S(2)}, u32[]{:S(2)}) collective-permute-start(f32[8,2048]{1,0:T(8,128)S(1)} %add_add_fusion.2), channel_id=1, source_target_pairs={{0,4},{2,6},{4,0},{6,2},{1,5},{3,7},{5,1},{7,3},{8,12},{10,14},{12... | collective-permute-start | bytes 196616 | tf_op jit(solution)/shard_map/ppermute | solution.py:34
  151.0 6.1 %collective-permute-start.13 = (f32[8,2048]{1,0:T(8,128)S(1)}, f32[8,2048]{1,0:T(8,128)S(1)}, u32[]{:S(2)}, u32[]{:S(2)}) collective-permute-start(f32[8,2048]{1,0:T(8,128)S(1)} %add_add_fusion.2), channel_id=1, source_target_pairs={{0,6},{2,4},{4,2},{6,0},{1,7},{3,5},{5,3},{7,1},{8,14},{10,12},{12... | collective-permute-start | bytes 196616 | tf_op jit(solution)/shard_map/ppermute | solution.py:34
  151.1 6.1 %collective-permute-start.12 = (f32[8,2048]{1,0:T(8,128)S(1)}, f32[8,2048]{1,0:T(8,128)S(1)}, u32[]{:S(2)}, u32[]{:S(2)}) collective-permute-start(f32[8,2048]{1,0:T(8,128)S(1)} %add_add_fusion.2), channel_id=1, source_target_pairs={{0,2},{2,0},{4,6},{6,4},{1,3},{3,1},{5,7},{7,5},{8,10},{10,8},{12,... | collective-permute-start | bytes 196616 | tf_op jit(solution)/shard_map/ppermute | solution.py:34
  157.2 6.2 %collective-permute-start.17 = (f32[8,2048]{1,0:T(8,128)S(1)}, f32[8,2048]{1,0:T(8,128)S(1)}, u32[]{:S(2)}, u32[]{:S(2)}) collective-permute-start(f32[8,2048]{1,0:T(8,128)S(1)} %add_add_fusion.1), channel_id=1, source_target_pairs={{0,128},{64,192},{128,0},{192,64},{1,129},{65,193},{129,1},{193,65... | collective-permute-start | bytes 196616 | tf_op jit(solution)/shard_map/ppermute | solution.py:34
  158.5 5.6 %collective-permute-start.16 = (f32[8,2048]{1,0:T(8,128)S(1)}, f32[8,2048]{1,0:T(8,128)S(1)}, u32[]{:S(2)}, u32[]{:S(2)}) collective-permute-start(f32[8,2048]{1,0:T(8,128)S(1)} %add_add_fusion.1), channel_id=1, source_target_pairs={{0,192},{64,128},{128,64},{192,0},{1,193},{65,129},{129,65},{193,1... | collective-permute-start | bytes 196616 | tf_op jit(solution)/shard_map/ppermute | solution.py:34
  160.6 4.3 %collective-permute-start.15 = (f32[8,2048]{1,0:T(8,128)S(1)}, f32[8,2048]{1,0:T(8,128)S(1)}, u32[]{:S(2)}, u32[]{:S(2)}) collective-permute-start(f32[8,2048]{1,0:T(8,128)S(1)} %add_add_fusion.1), channel_id=1, source_target_pairs={{0,64},{64,0},{128,192},{192,128},{1,65},{65,1},{129,193},{193,129... | collective-permute-start | bytes 196616 | tf_op jit(solution)/shard_map/ppermute | solution.py:34
  164.9 10.8 %collective-permute-start.18 = (f32[8,2048]{1,0:T(8,128)S(1)}, f32[8,2048]{1,0:T(8,128)S(1)}, u32[]{:S(2)}, u32[]{:S(2)}) collective-permute-start(f32[8,2048]{1,0:T(8,128)S(1)} %add_add_fusion), channel_id=1, source_target_pairs={{0,1},{1,0},{2,3},{3,2},{4,5},{5,4},{6,7},{7,6},{8,9},{9,8},{10,11... | collective-permute-start | bytes 196616 | tf_op jit(solution)/shard_map/ppermute | solution.py:34

commit v15 on v14

--- a/solution.py
+++ b/solution.py
@@ -322,36 +322,19 @@
     )[0]
 
 
-def router_grads(pos, dispatch, gate_back, token_lanes, tokens, scale):
-    rows, width = tokens.shape
-    experts = 8
-    step = width // 4
-
-    def body(pos_ref, disp, back, side, tok, logit, router, held, sem):
-        copy = pltpu.make_async_copy(tok, held, sem)
-        copy.start()
+def router_grads(pos, dispatch, gate_back, token_lanes):
+    rows = dispatch.shape[1]
+
+    def body(pos_ref, disp, back, side, logit):
         dims = (((0,), (0,)), ((), ()))
         combine_grad = lax.dot_general(disp[...], back[...], dims, preferred_element_type=F32)
         probs, combine, keep, denominator = (side[k] for k in range(4))
         weighted = jnp.sum(combine_grad * combine, axis=1, keepdims=True)
         probs_grad = keep * (combine_grad - weighted) / denominator
         inner = jnp.sum(probs_grad * probs, axis=1, keepdims=True)
-        logit_b = (probs * (probs_grad - inner)).astype(BF16)
-        logit[...] = logit_b
-        copy.wait()
-        for i in range(4):
-            at = slice(i * step, (i + 1) * step)
-            part = lax.dot_general(logit_b, held[:, at], dims, preferred_element_type=F32)
-            router[:, at] = part[:experts] * scale
-
-    return call(
-        body,
-        pos,
-        [dispatch, gate_back, token_lanes],
-        [((rows, EXTRA), BF16), ((experts, width), F32)],
-        far=[tokens],
-        scratch=[pltpu.VMEM((rows, width), BF16), pltpu.SemaphoreType.DMA],
-    )
+        logit[...] = (probs * (probs_grad - inner)).astype(BF16)
+
+    return call(body, pos, [dispatch, gate_back, token_lanes], [((rows, EXTRA), BF16)])[0]
 
 
 def token_grads(pos, dispatch, back, logit_lanes, weight_lanes):
@@ -466,9 +449,8 @@
     ).reshape(slot_count, model_width)
 
     gate_back, _ = tie(gate_back, grad_slots)
-    logit_lanes, router_part = router_grads(
-        pos, dispatch, gate_back, token_lanes, tokens, grad_scale
-    )
+    logit_lanes = router_grads(pos, dispatch, gate_back, token_lanes)
+    router_part = contract_rows(logit_lanes[:, :experts], tokens) * grad_scale
 
     def router_round(value, axes, one, two, *until):
         near, far, both = (swap(value, axes, mask) for mask in (one, two, one ^ two))

time: 181 us -> 181 us (level)
    unnamed x73 -> x75, local copies, waits for them, and re-layouts: 17.5 us -> 16.9 us
  transfers between devices with their start and end apart: 24 -> 24, of which waited for: 10 -> 10; matrix products, arithmetic and copies ran while one was open for 11% -> 11% of each run, Pallas kernels for 12% -> 11%
where the time goes in v15:
time: 181 us; the launch traced here: 179 us
  waiting for transfers between devices  60.3 us (33%)
  starting transfers between devices  50 us (28%)
  Pallas kernels  28.6 us (16%)
  local copies, waits for them, and re-layouts  21.6 us (12%)
  matrix products  12.6 us (7%)
  other arithmetic  5.09 us (3%)
    all_to_all x5, waiting for transfers between devices, exchange(): return lax.all_to_all(values, axes, split_axis=0, concat_axis=0, tiled=True)  33 us
    pallas_call x10, Pallas kernels, call(): pl.pallas_call(body, in_specs=[pl.BlockSpec(memory_space=pltpu.SMEM)] + [...  28.6 us
    ppermute x19, waiting for transfers between devices, swap(): return lax.ppermute(values, axis, [(i, i ^ mask) for i in range(size)])  27.3 us
    all_to_all x5, starting transfers between devices, exchange(): return lax.all_to_all(values, axes, split_axis=0, concat_axis=0, tiled=True)  26.2 us
    ppermute x19, starting transfers between devices, swap(): return lax.ppermute(values, axis, [(i, i ^ mask) for i in range(size)])  23.8 us
    unnamed x75, local copies, waits for them, and re-layouts  16.9 us
    dot_general x1, matrix products, per_device(): hidden_pre = jnp.dot(slot_tokens, weight_in, preferred_element_type=F32)  7.5 us
  transfers between devices with their start and end apart: 24, of which 10 were waited for; matrix products, arithmetic and copies ran while one was open for 11% of the time, Pallas kernels for 11%

profile of v15, /device:TPU:2, one launch (start us, length us, event | category | flops | bytes accessed | tf_op | source)
XLA Modules:
  0.0 179.3 jit_solution(17986641091837121576)
XLA Ops:
  0.6 0.8 compare_reduce_fusion.1
  1.5 0.7 multiply_add_fusion
  2.2 2.1 %convolution_convert_fusion = bf16[512,2048]{1,0:T(8,128)(2,1)} fusion(bf16[256,2048]{1,0:T(8,128)(2,1)S(1)} %copy-done, s32[256]{0:T(256)S(1)} %bitcast.55, s32[256]{0:T(256)S(1)} %bitcast.51, pred[256]{0:T(512)(128)(4,1)S(1)} %get-tuple-element.145, pred[256]{0:T(512)(128)(4,1)S(1)} %get-tuple-element.144), kind=kOutput, calls=%fused_computation.1 | convolution fusion | flops 538574848 | bytes 3148288 | tf_op jit(solution)/shard_map/dot_general | solution.py:379
  4.3 6.3 %all-to-all-start.1 = ((bf16[8,64,2048]{2,1,0:T(8,128)(2,1)}), bf16[8,64,2048]{2,1,0:T(8,128)(2,1)S(1)}, u32[]{:S(2)}, u32[]{:S(2)}) async-start(bf16[8,64,2048]{2,1,0:T(8,128)(2,1)} %bitcast.49), calls=%async_computation.1 | async-start | bytes 4194304 | tf_op jit(solution)/shard_map/all_to_all | solution.py:38
  10.7 0.4 fusion.18
  11.8 2.0 %convolution_convert_fusion.1 = bf16[512,2048]{1,0:T(8,128)(2,1)S(1)} fusion(bf16[256,2048]{1,0:T(8,128)(2,1)} %param.9, s32[256]{0:T(256)S(1)} %bitcast.57, s32[256]{0:T(256)S(1)} %bitcast.53, pred[256]{0:T(512)(128)(4,1)S(1)} %get-tuple-element.145, pred[256]{0:T(512)(128)(4,1)S(1)} %get-tuple-element.144), kind=kOutput, calls=%fused_computation.2 | convolution fusion | flops 538574848 | bytes 3148288 | tf_op jit(solution)/shard_map/dot_general | solution.py:409
  13.8 1.6 pad_maximum_fusion
  15.4 20.5 %all-to-all-done.1 = bf16[8,64,2048]{2,1,0:T(8,128)(2,1)S(1)} async-done(((bf16[8,64,2048]{2,1,0:T(8,128)(2,1)}), bf16[8,64,2048]{2,1,0:T(8,128)(2,1)S(1)}, u32[]{:S(2)}, u32[]{:S(2)}) %all-to-all-start.1) | async-done | bytes 2097184 | tf_op jit(solution)/shard_map/all_to_all | solution.py:38
  35.9 1.4 copy-done.1
  37.2 5.3 %all-to-all-start = ((bf16[8,64,2176]{2,1,0:T(8,128)(2,1)}), bf16[8,64,2176]{2,1,0:T(8,128)(2,1)S(1)}, u32[]{:S(2)}, u32[]{:S(2)}) async-start(bf16[8,64,2176]{2,1,0:T(8,128)(2,1)} %bitcast.48), calls=%async_computation | async-start | bytes 4456448 | tf_op jit(solution)/shard_map/all_to_all | solution.py:38
  42.5 7.5 %fusion.3 = (f32[512,1024]{1,0:T(8,128)}, bf16[512,1024]{1,0:T(8,128)(2,1)}) fusion(bf16[512,2048]{1,0:T(8,128)(2,1)} %bitcast.40, bf16[1,2048,1024]{2,1,0:T(8,128)(2,1)} %param.11), kind=kOutput, calls=%fused_computation.8 | convolution fusion | flops 2152726528 | bytes 9437184 | tf_op jit(solution)/shard_map/dot_general | solution.py:418
  50.0 0.5 collective-permute-start.1
  50.6 1.8 %copy.27 = bf16[2048,8]{1,0:T(8,128)(2,1)} copy(bf16[2048,8]{0,1:T(8,128)(2,1)} %param.10) | data formatting | bytes 65536 | tf_op args[2]
  52.4 0.8 copy.29
  53.2 2.0 %pad.22.weight = bf16[2048,128]{1,0:T(8,128)(2,1)} pad(bf16[2048,8]{1,0:T(8,128)(2,1)} %copy.27, bf16[]{:T(256)} %constant.39.clone.1), padding=0_0x0_120 | pad | bytes 557058 | tf_op jit(solution)/shard_map/jit(_pad)/pad | solution.py:393
  55.3 0.8 broadcast_in_dim.52
  56.1 0.9 pad_bitcast_fusion
  57.0 0.9 pad_maximum_fusion.1.side
  58.1 10.4 %all-to-all-done = bf16[8,64,2176]{2,1,0:T(8,128)(2,1)S(1)} async-done(((bf16[8,64,2176]{2,1,0:T(8,128)(2,1)}), bf16[8,64,2176]{2,1,0:T(8,128)(2,1)S(1)}, u32[]{:S(2)}, u32[]{:S(2)}) %all-to-all-start) | async-done | bytes 2228256 | tf_op jit(solution)/shard_map/all_to_all | solution.py:38
  68.5 1.0 shard_map.111
  69.6 0.5 copy-done.14
  70.1 2.2 %copy-done.12 = bf16[1,1024,2048]{2,1,0:T(8,128)(2,1)S(1)} copy-done((bf16[1,1024,2048]{2,1,0:T(8,128)(2,1)S(1)}, bf16[1,1024,2048]{2,1,0:T(8,128)(2,1)}, u32[]{:S(2)}) %copy-start.12) | copy-done | bytes 4194328
  72.3 3.9 %shard_map.112 = (bf16[512,1024]{1,0:T(8,128)(2,1)S(1)}, bf16[512,512]{1,0:T(8,128)(2,1)S(1)}, bf16[512,128]{1,0:T(8,128)(2,1)S(1)}) custom-call(s32[4]{0:T(128)S(1)} %pad_add_fusion.pos_ref, bf16[512,2176]{1,0:T(8,128)(2,1)S(1)} %bitcast.38, bf16[1024,2048]{1,0:T(8,128)(2,1)S(1)} %bitcast.44, bf16[512,1024]{1,0:T(8,128)(2,1)} %get-tuple-element.94.act_ref.refs_4_.refs_0_, ...), custom_call_target="tpu_custom_call" | custom-call | flops 1000 | bytes 1000 | tf_op jit(solution)/shard_map/pallas_call | solution.py:47
  76.5 1.9 %collective-permute-done.3.refs_3_.refs_7_ = bf16[512,512]{1,0:T(8,128)(2,1)S(1)} collective-permute-done((bf16[512,512]{1,0:T(8,128)(2,1)S(1)}, bf16[512,512]{1,0:T(8,128)(2,1)S(1)}, u32[]{:S(2)}, u32[]{:S(2)}) %collective-permute-start.3) | collective-permute-done | bytes 524320 | tf_op jit(solution)/shard_map/ppermute | solution.py:34
  78.4 5.6 %shard_map.113 = (bf16[1024,512]{1,0:T(8,128)(2,1)}, bf16[1024,512]{1,0:T(8,128)(2,1)}) custom-call(s32[4]{0:T(128)S(1)} %pad_add_fusion.pos_ref, bf16[512,1024]{1,0:T(8,128)(2,1)S(1)} %get-tuple-element.98.refs_0_.refs_4_, bf16[512,1024]{1,0:T(8,128)(2,1)S(1)} %collective-permute-done.2.refs_1_.refs_5_, ...), custom_call_target="tpu_custom_call" | custom-call | flops 1000 | bytes 1000 | tf_op jit(solution)/shard_map/pallas_call | solution.py:47
  84.1 1.7 collective-permute-start.4
  85.7 2.2 %collective-permute-start.5 = (bf16[1024,512]{1,0:T(8,128)(2,1)}, bf16[1024,512]{1,0:T(8,128)(2,1)}, u32[]{:S(2)}, u32[]{:S(2)}) collective-permute-start(bf16[1024,512]{1,0:T(8,128)(2,1)} %get-tuple-element.87), channel_id=1, source_target_pairs={{0,192},{64,128},{128,64},{192,0},{1,193},{65,129},{129,65},{193,1... | collective-permute-start | bytes 3145736 | tf_op jit(solution)/shard_map/ppermute | solution.py:34
  87.9 5.1 %all-to-all-start.2 = ((bf16[8,64,128]{2,1,0:T(8,128)(2,1)}), bf16[8,64,128]{2,1,0:T(8,128)(2,1)S(1)}, u32[]{:S(2)}, u32[]{:S(2)}) async-start(bf16[8,64,128]{2,1,0:T(8,128)(2,1)} %bitcast.47), calls=%async_computation.2 | async-start | bytes 262144 | tf_op jit(solution)/shard_map/all_to_all | solution.py:38
  93.0 1.2 copy-done.5
  94.2 2.2 %copy-done.13 = bf16[1,2048,1024]{2,1,0:T(8,128)(2,1)S(1)} copy-done((bf16[1,2048,1024]{2,1,0:T(8,128)(2,1)S(1)}, bf16[1,2048,1024]{2,1,0:T(8,128)(2,1)}, u32[]{:S(2)}) %copy-start.13) | copy-done | bytes 4194328
  96.4 3.8 %shard_map.114 = bf16[512,2048]{1,0:T(8,128)(2,1)S(1)} custom-call(s32[4]{0:T(128)S(1)} %pad_add_fusion.pos_ref, bf16[512,1024]{1,0:T(8,128)(2,1)S(1)} %copy-done.5, bf16[2048,1024]{1,0:T(8,128)(2,1)S(1)} %bitcast.45), custom_call_target="tpu_custom_call" | custom-call | flops 1000 | bytes 1000 | tf_op jit(solution)/shard_map/pallas_call | solution.py:47
  100.3 1.4 copy-done.7
  101.6 0.7 copy-done.20
  102.3 5.9 %all-to-all-start.3 = ((bf16[8,64,2048]{2,1,0:T(8,128)(2,1)}), bf16[8,64,2048]{2,1,0:T(8,128)(2,1)}, u32[]{:S(2)}, u32[]{:S(2)}) async-start(bf16[8,64,2048]{2,1,0:T(8,128)(2,1)} %bitcast.43), calls=%async_computation.3 | async-start | bytes 4194304 | tf_op jit(solution)/shard_map/all_to_all | solution.py:38
  108.1 1.0 copy-done.18
  109.2 0.9 copy-done.21
  110.1 1.0 shard_map.115.logit
  111.7 1.2 copy-done.11
  112.9 1.0 copy-done.16
  113.9 4.6 %shard_map.116 = (f32[256,512]{1,0:T(8,128)S(1)}, f32[256,512]{1,0:T(8,128)S(1)}, f32[512,256]{1,0:T(8,128)S(1)}, f32[512,256]{1,0:T(8,128)S(1)}, f32[512,512]{1,0:T(8,128)S(1)}, /*index=5*/f32[512,512]{1,0:T(8,128)S(1)}) custom-call(s32[4]{0:T(128)S(1)} %pad_add_fusion.pos_ref, bf16[512,1024]{1,0:T(8,128)(2,1)} %get-tuple-element.94.act_ref.refs_4_.refs_0_, ...), custom_call_target="tpu_custom_call" | custom-call | flops 1000 | bytes 1000 | tf_op jit(solution)/shard_map/pallas_call | solution.py:47
  118.6 1.7 shard_map.117
  120.4 0.8 collective-permute-start.7
  121.1 0.6 collective-permute-start.6
  121.7 6.4 %collective-permute-start.11 = (f32[8,2048]{1,0:T(8,128)S(1)}, f32[8,2048]{1,0:T(8,128)S(1)}, u32[]{:S(2)}, u32[]{:S(2)}) collective-permute-start(f32[8,2048]{1,0:T(8,128)S(1)} %add.73), channel_id=1, source_target_pairs={{0,32},{16,48},{32,0},{48,16},{1,33},{17,49},{33,1},{49,17},{2,34}... | collective-permute-start | bytes 196616 | tf_op jit(solution)/shard_map/ppermute | solution.py:34
  128.1 0.6 collective-permute-start.10
  128.7 0.9 collective-permute-start.9
  129.6 11.5 %collective-permute-done.11 = f32[8,2048]{1,0:T(8,128)S(1)} collective-permute-done((f32[8,2048]{1,0:T(8,128)S(1)}, f32[8,2048]{1,0:T(8,128)S(1)}, u32[]{:S(2)}, u32[]{:S(2)}) %collective-permute-start.11) | collective-permute-done | bytes 65568 | tf_op jit(solution)/shard_map/ppermute | solution.py:34
  141.1 0.4 collective-permute-done.10
  141.6 1.9 %shard_map.118 = bf16[8,64,1024]{2,1,0:T(8,128)(2,1)S(1)} custom-call(s32[4]{0:T(128)S(1)} %pad_add_fusion.pos_ref, f32[256,512]{1,0:T(8,128)S(1)} %get-tuple-element.121.out_a, f32[256,512]{1,0:T(8,128)S(1)} %get-tuple-element.122.out_b, f32[512,256]{1,0:T(8,128)S(1)} %get-tuple-element.123.in_a, f32[512,256]{1,0:T(8,128)S(1)} %get-tuple-element.124.in_b, ...), custom_call_target="tpu_custom_call" | custom-call | flops 30000001024 | bytes 1000 | tf_op jit(solution)/shard_map/pallas_call | solution.py:47
  143.5 1.0 copy-done.19
  144.5 3.7 %all-to-all-start.4 = ((bf16[8,64,1024]{2,1,0:T(8,128)(2,1)}), bf16[8,64,1024]{2,1,0:T(8,128)(2,1)S(1)}, u32[]{:S(2)}, u32[]{:S(2)}) async-start(bf16[8,64,1024]{2,1,0:T(8,128)(2,1)} %copy-done.19), calls=%async_computation.4 | async-start | bytes 2097152 | tf_op jit(solution)/shard_map/all_to_all | solution.py:38
  148.2 2.2 %collective-permute-start.14 = (f32[8,2048]{1,0:T(8,128)S(1)}, f32[8,2048]{1,0:T(8,128)S(1)}, u32[]{:S(2)}, u32[]{:S(2)}) collective-permute-start(f32[8,2048]{1,0:T(8,128)S(1)} %add_add_fusion.2), channel_id=1, source_target_pairs={{0,4},{2,6},{4,0},{6,2},{1,5},{3,7},{5,1},{7,3},{8,12},{10,14},{12... | collective-permute-start | bytes 196616 | tf_op jit(solution)/shard_map/ppermute | solution.py:34
  150.4 2.5 %collective-permute-start.12 = (f32[8,2048]{1,0:T(8,128)S(1)}, f32[8,2048]{1,0:T(8,128)S(1)}, u32[]{:S(2)}, u32[]{:S(2)}) collective-permute-start(f32[8,2048]{1,0:T(8,128)S(1)} %add_add_fusion.2), channel_id=1, source_target_pairs={{0,2},{2,0},{4,6},{6,4},{1,3},{3,1},{5,7},{7,5},{8,10},{10,8},{12,... | collective-permute-start | bytes 196616 | tf_op jit(solution)/shard_map/ppermute | solution.py:34
  153.0 3.6 %shard_map.119 = bf16[256,2048]{1,0:T(8,128)(2,1)} custom-call(s32[4]{0:T(128)S(1)} %pad_add_fusion.pos_ref, bf16[512,256]{1,0:T(8,128)(2,1)S(1)} %fusion.13.disp, bf16[512,2048]{1,0:T(8,128)(2,1)} %bitcast.19.flat, bf16[256,128]{1,0:T(8,128)(2,1)S(1)} %shard_map.115.logit, bf16[2048,128]{1,0:T(8,128)(2,1)S(1)} %copy-done.17), custom_call_target="tpu_custom_call" | custom-call | flops 1000 | bytes 1000 | tf_op jit(solution)/shard_map/pallas_call | solution.py:47
  156.6 1.1 collective-permute-start.17
  157.7 2.3 %collective-permute-start.16 = (f32[8,2048]{1,0:T(8,128)S(1)}, f32[8,2048]{1,0:T(8,128)S(1)}, u32[]{:S(2)}, u32[]{:S(2)}) collective-permute-start(f32[8,2048]{1,0:T(8,128)S(1)} %add_add_fusion.1), channel_id=1, source_target_pairs={{0,192},{64,128},{128,64},{192,0},{1,193},{65,129},{129,65},{193,1... | collective-permute-start | bytes 196616 | tf_op jit(solution)/shard_map/ppermute | solution.py:34
  160.2 2.9 %collective-permute-done.17 = f32[8,2048]{1,0:T(8,128)S(1)} collective-permute-done((f32[8,2048]{1,0:T(8,128)S(1)}, f32[8,2048]{1,0:T(8,128)S(1)}, u32[]{:S(2)}, u32[]{:S(2)}) %collective-permute-start.17) | collective-permute-done | bytes 65568 | tf_op jit(solution)/shard_map/ppermute | solution.py:34
  163.0 0.4 collective-permute-done.16
  163.4 0.8 collective-permute-done.15
  164.3 1.5 collective-permute-start.18
  165.8 9.3 %collective-permute-done.18 = f32[8,2048]{1,0:T(8,128)S(1)} collective-permute-done((f32[8,2048]{1,0:T(8,128)S(1)}, f32[8,2048]{1,0:T(8,128)S(1)}, u32[]{:S(2)}, u32[]{:S(2)}) %collective-permute-start.18) | collective-permute-done | bytes 65568 | tf_op jit(solution)/shard_map/ppermute | solution.py:34
  175.1 0.6 add.83
  175.8 2.1 %all-to-all-done.4.got = bf16[8,64,1024]{2,1,0:T(8,128)(2,1)S(1)} async-done(((bf16[8,64,1024]{2,1,0:T(8,128)(2,1)}), bf16[8,64,1024]{2,1,0:T(8,128)(2,1)S(1)}, u32[]{:S(2)}, u32[]{:S(2)}) %all-to-all-start.4) | async-done | bytes 1048608 | tf_op jit(solution)/shard_map/all_to_all | solution.py:38
  177.9 1.4 shard_map.120
  (103 shorter events, 2.4 us)
Async XLA Ops:
  0.6 1.6 copy-start
  1.5 10.3 %copy-start.33 = (pred[256]{0:T(512)(128)(4,1)}, pred[256]{0:T(512)(128)(4,1)S(1)}, u32[]{:S(2)}) copy-start(pred[256]{0:T(512)(128)(4,1)S(1)} %get-tuple-element.144) | copy-start | bytes 772
  1.5 10.3 %copy-start.35 = (pred[256]{0:T(512)(128)(4,1)}, pred[256]{0:T(512)(128)(4,1)S(1)}, u32[]{:S(2)}) copy-start(pred[256]{0:T(512)(128)(4,1)S(1)} %get-tuple-element.145) | copy-start | bytes 772
  2.2 9.6 %copy-start.28 = (s32[256,1]{0,1:T(1,128)}, s32[256,1]{0,1:T(1,128)S(1)}, u32[]{:S(2)}) copy-start(s32[256,1]{0,1:T(1,128)S(1)} %get-tuple-element.150) | copy-start | bytes 3076
  2.2 9.6 %copy-start.30 = (s32[256,1]{0,1:T(1,128)}, s32[256,1]{0,1:T(1,128)S(1)}, u32[]{:S(2)}) copy-start(s32[256,1]{0,1:T(1,128)S(1)} %get-tuple-element.151) | copy-start | bytes 3076
  4.3 6.3 %copy-start.26 = (s32[256,2]{0,1:T(2,128)S(1)}, s32[256,2]{0,1:T(2,128)}, u32[]{:S(2)}) copy-start(s32[256,2]{0,1:T(2,128)} %param.15) | copy-start | bytes 6148
  4.3 6.3 %copy-start.25 = (bf16[2048,8]{0,1:T(8,128)(2,1)S(1)}, bf16[2048,8]{0,1:T(8,128)(2,1)}, u32[]{:S(2)}) copy-start(bf16[2048,8]{0,1:T(8,128)(2,1)} %param.10) | copy-start | bytes 98308
  4.3 7.1 %copy-start.27 = (s32[256,2]{0,1:T(2,128)S(1)}, s32[256,2]{0,1:T(2,128)}, u32[]{:S(2)}) copy-start(s32[256,2]{0,1:T(2,128)} %param.13) | copy-start | bytes 6148
  4.3 31.5 %all-to-all-start.1 = ((bf16[8,64,2048]{2,1,0:T(8,128)(2,1)}), bf16[8,64,2048]{2,1,0:T(8,128)(2,1)S(1)}, u32[]{:S(2)}, u32[]{:S(2)}) async-start(bf16[8,64,2048]{2,1,0:T(8,128)(2,1)} %bitcast.49), calls=%async_computation.1 | async-start | bytes 4194304 | tf_op jit(solution)/shard_map/all_to_all | solution.py:38
  11.3 4.1 %copy-start.23 = (f32[256,8]{1,0:T(8,128)}, f32[256,8]{1,0:T(8,128)S(1)}, u32[]{:S(2)}) copy-start(f32[256,8]{1,0:T(8,128)S(1)} %broadcast_divide_fusion) | copy-start | bytes 24580
  11.5 3.9 %copy-start.32 = (f32[256]{0:T(256)}, f32[256]{0:T(256)S(1)}, u32[]{:S(2)}) copy-start(f32[256]{0:T(256)S(1)} %subtract_add_fusion) | copy-start | bytes 3076
  35.9 1.4 copy-start.1
  37.2 31.3 %all-to-all-start = ((bf16[8,64,2176]{2,1,0:T(8,128)(2,1)}), bf16[8,64,2176]{2,1,0:T(8,128)(2,1)S(1)}, u32[]{:S(2)}, u32[]{:S(2)}) async-start(bf16[8,64,2176]{2,1,0:T(8,128)(2,1)} %bitcast.48), calls=%async_computation | async-start | bytes 4456448 | tf_op jit(solution)/shard_map/all_to_all | solution.py:38
  42.5 12.8 %copy-start.24 = (f32[256,8]{1,0:T(8,128)S(1)}, f32[256,8]{1,0:T(8,128)}, u32[]{:S(2)}) copy-start(f32[256,8]{1,0:T(8,128)} %copy-done.23) | copy-start | bytes 24580
  42.5 26.0 %collective-permute-start = (bf16[512,2048]{1,0:T(8,128)(2,1)}, bf16[512,2048]{1,0:T(8,128)(2,1)}, u32[]{:S(2)}, u32[]{:S(2)}) collective-permute-start(bf16[512,2048]{1,0:T(8,128)(2,1)} %bitcast.39), channel_id=1, source_target_pairs={{0,8},{8,0},{1,9},{9,1},{2,10},{10,2},{3,11},{11,3},{4,12},{12,4},... | collective-permute-start | bytes 6291464 | tf_op jit(solution)/shard_map/ppermute | solution.py:34
  50.0 18.5 %collective-permute-start.1 = (bf16[512,1024]{1,0:T(8,128)(2,1)}, bf16[512,1024]{1,0:T(8,128)(2,1)}, u32[]{:S(2)}, u32[]{:S(2)}) collective-permute-start(bf16[512,1024]{1,0:T(8,128)(2,1)} %get-tuple-element.94.act_ref.refs_4_.refs_0_), channel_id=1, source_target_pairs={{0,8},{8,0},{1,9},{9,1},{2,10},{10,2},{3,11},{11,3},{4,12},{12,4},... | collective-permute-start | bytes 3145736 | tf_op jit(solution)/shard_map/ppermute | solution.py:34
  50.6 7.2 %copy-start.29 = (s32[256,1]{0,1:T(1,128)S(1)}, s32[256,1]{0,1:T(1,128)}, u32[]{:S(2)}) copy-start(s32[256,1]{0,1:T(1,128)} %copy-done.28) | copy-start | bytes 3076
  53.2 4.6 %copy-start.31 = (s32[256,1]{0,1:T(1,128)S(1)}, s32[256,1]{0,1:T(1,128)}, u32[]{:S(2)}) copy-start(s32[256,1]{0,1:T(1,128)} %copy-done.30) | copy-start | bytes 3076
  53.2 4.6 %copy-start.34 = (pred[256]{0:T(512)(128)(4,1)S(1)}, pred[256]{0:T(512)(128)(4,1)}, u32[]{:S(2)}) copy-start(pred[256]{0:T(512)(128)(4,1)} %copy-done.33) | copy-start | bytes 772
  53.2 4.6 %copy-start.36 = (pred[256]{0:T(512)(128)(4,1)S(1)}, pred[256]{0:T(512)(128)(4,1)}, u32[]{:S(2)}) copy-start(pred[256]{0:T(512)(128)(4,1)} %copy-done.35) | copy-start | bytes 772
  68.5 1.6 copy-start.14
  69.4 8.9 %copy-start.8 = (bf16[512,1024]{1,0:T(8,128)(2,1)}, bf16[512,1024]{1,0:T(8,128)(2,1)S(1)}, u32[]{:S(2)}) copy-start(bf16[512,1024]{1,0:T(8,128)(2,1)S(1)} %get-tuple-element.98.refs_0_.refs_4_) | copy-start | bytes 3145732
  69.5 8.9 %collective-permute-start.2 = (bf16[512,1024]{1,0:T(8,128)(2,1)S(1)}, bf16[512,1024]{1,0:T(8,128)(2,1)S(1)}, u32[]{:S(2)}, u32[]{:S(2)}) collective-permute-start(bf16[512,1024]{1,0:T(8,128)(2,1)S(1)} %get-tuple-element.75), channel_id=1, source_target_pairs={{0,8},{8,0},{1,9},{9,1},{2,10},{10,2},{3,11},{11,3},{4,12},{12,4},... | collective-permute-start | bytes 3145736 | tf_op jit(solution)/shard_map/ppermute | solution.py:34
  70.1 2.2 %copy-start.12 = (bf16[1,1024,2048]{2,1,0:T(8,128)(2,1)S(1)}, bf16[1,1024,2048]{2,1,0:T(8,128)(2,1)}, u32[]{:S(2)}) copy-start(bf16[1,1024,2048]{2,1,0:T(8,128)(2,1)} %param.12) | copy-start | bytes 12582916
  72.3 6.1 %copy-start.2 = (bf16[8,64,2048]{2,1,0:T(8,128)(2,1)S(1)}, bf16[8,64,2048]{2,1,0:T(8,128)(2,1)}, u32[]{:S(2)}) copy-start(bf16[8,64,2048]{2,1,0:T(8,128)(2,1)} %copy-done.1) | copy-start | bytes 6291460
  76.2 7.9 %copy-start.4 = (bf16[512,1024]{1,0:T(8,128)(2,1)}, bf16[512,1024]{1,0:T(8,128)(2,1)S(1)}, u32[]{:S(2)}) copy-start(bf16[512,1024]{1,0:T(8,128)(2,1)S(1)} %get-tuple-element.100.refs_2_.grad.refs_6_) | copy-start | bytes 3145732
  76.2 7.9 %copy-start.22 = (bf16[512,128]{1,0:T(8,128)(2,1)}, bf16[512,128]{1,0:T(8,128)(2,1)S(1)}, u32[]{:S(2)}) copy-start(bf16[512,128]{1,0:T(8,128)(2,1)S(1)} %get-tuple-element.89) | copy-start | bytes 393220
  76.2 2.2 %collective-permute-start.3 = (bf16[512,512]{1,0:T(8,128)(2,1)S(1)}, bf16[512,512]{1,0:T(8,128)(2,1)S(1)}, u32[]{:S(2)}, u32[]{:S(2)}) collective-permute-start(bf16[512,512]{1,0:T(8,128)(2,1)S(1)} %get-tuple-element.82), channel_id=1, source_target_pairs={{0,8},{8,0},{1,9},{9,1},{2,10},{10,2},{3,11},{11,3},{4,12},{12,4},... | collective-permute-start | bytes 1572872 | tf_op jit(solution)/shard_map/ppermute | solution.py:34
  78.4 5.7 %copy-start.15 = (bf16[512,512]{1,0:T(8,128)(2,1)}, bf16[512,512]{1,0:T(8,128)(2,1)S(1)}, u32[]{:S(2)}) copy-start(bf16[512,512]{1,0:T(8,128)(2,1)S(1)} %collective-permute-done.3.refs_3_.refs_7_) | copy-start | bytes 1572868
  78.4 5.7 %copy-start.10 = (bf16[512,1024]{1,0:T(8,128)(2,1)}, bf16[512,1024]{1,0:T(8,128)(2,1)S(1)}, u32[]{:S(2)}) copy-start(bf16[512,1024]{1,0:T(8,128)(2,1)S(1)} %collective-permute-done.2.refs_1_.refs_5_) | copy-start | bytes 3145732
  84.1 34.5 %collective-permute-start.4 = (bf16[1024,512]{1,0:T(8,128)(2,1)}, bf16[1024,512]{1,0:T(8,128)(2,1)}, u32[]{:S(2)}, u32[]{:S(2)}) collective-permute-start(bf16[1024,512]{1,0:T(8,128)(2,1)} %get-tuple-element.86), channel_id=1, source_target_pairs={{0,64},{64,0},{128,192},{192,128},{1,65},{65,1},{129,193},{193,129... | collective-permute-start | bytes 3145736 | tf_op jit(solution)/shard_map/ppermute | solution.py:34
  85.7 32.9 %collective-permute-start.5 = (bf16[1024,512]{1,0:T(8,128)(2,1)}, bf16[1024,512]{1,0:T(8,128)(2,1)}, u32[]{:S(2)}, u32[]{:S(2)}) collective-permute-start(bf16[1024,512]{1,0:T(8,128)(2,1)} %get-tuple-element.87), channel_id=1, source_target_pairs={{0,192},{64,128},{128,64},{192,0},{1,193},{65,129},{129,65},{193,1... | collective-permute-start | bytes 3145736 | tf_op jit(solution)/shard_map/ppermute | solution.py:34
  87.9 13.7 %all-to-all-start.2 = ((bf16[8,64,128]{2,1,0:T(8,128)(2,1)}), bf16[8,64,128]{2,1,0:T(8,128)(2,1)S(1)}, u32[]{:S(2)}, u32[]{:S(2)}) async-start(bf16[8,64,128]{2,1,0:T(8,128)(2,1)} %bitcast.47), calls=%async_computation.2 | async-start | bytes 262144 | tf_op jit(solution)/shard_map/all_to_all | solution.py:38
  93.0 1.2 copy-start.5
  94.2 2.2 %copy-start.13 = (bf16[1,2048,1024]{2,1,0:T(8,128)(2,1)S(1)}, bf16[1,2048,1024]{2,1,0:T(8,128)(2,1)}, u32[]{:S(2)}) copy-start(bf16[1,2048,1024]{2,1,0:T(8,128)(2,1)} %param.11) | copy-start | bytes 12582916
  100.2 1.4 copy-start.7
  101.6 0.7 copy-start.20
  102.3 9.1 %copy-start.6 = (bf16[512,1024]{1,0:T(8,128)(2,1)S(1)}, bf16[512,1024]{1,0:T(8,128)(2,1)}, u32[]{:S(2)}) copy-start(bf16[512,1024]{1,0:T(8,128)(2,1)} %copy-done.4) | copy-start | bytes 3145732
  102.3 9.1 %copy-start.9 = (bf16[512,1024]{1,0:T(8,128)(2,1)S(1)}, bf16[512,1024]{1,0:T(8,128)(2,1)}, u32[]{:S(2)}) copy-start(bf16[512,1024]{1,0:T(8,128)(2,1)} %copy-done.8) | copy-start | bytes 3145732
  102.3 42.2 %all-to-all-start.3 = ((bf16[8,64,2048]{2,1,0:T(8,128)(2,1)}), bf16[8,64,2048]{2,1,0:T(8,128)(2,1)}, u32[]{:S(2)}, u32[]{:S(2)}) async-start(bf16[8,64,2048]{2,1,0:T(8,128)(2,1)} %bitcast.43), calls=%async_computation.3 | async-start | bytes 4194304 | tf_op jit(solution)/shard_map/all_to_all | solution.py:38
  108.1 1.0 copy-start.18
  109.2 0.9 copy-start.21
  110.1 1.6 copy-start.3
  111.3 10.4 %collective-permute-start.8 = (f32[8,2048]{1,0:T(8,128)S(1)}, f32[8,2048]{1,0:T(8,128)S(1)}, u32[]{:S(2)}, u32[]{:S(2)}) collective-permute-start(f32[8,2048]{1,0:T(8,128)S(1)} %convolution_multiply_fusion), channel_id=1, source_target_pairs={{0,8},{8,0},{1,9},{9,1},{2,10},{10,2},{3,11},{11,3},{4,12},{12,4},... | collective-permute-start | bytes 196616 | tf_op jit(solution)/shard_map/ppermute | solution.py:34
  111.7 1.2 copy-start.11
  112.9 1.0 copy-start.16
  120.4 21.2 %collective-permute-start.7 = (bf16[512,512]{1,0:T(8,128)(2,1)S(1)}, bf16[512,512]{1,0:T(8,128)(2,1)S(1)}, u32[]{:S(2)}, u32[]{:S(2)}) collective-permute-start(bf16[512,512]{1,0:T(8,128)(2,1)S(1)} %get-tuple-element.113), channel_id=1, source_target_pairs={{0,64},{64,0},{128,192},{192,128},{1,65},{65,1},{129,193},{193,129... | collective-permute-start | bytes 1572872 | tf_op jit(solution)/shard_map/ppermute | solution.py:34
  121.1 20.4 %collective-permute-start.6 = (bf16[512,512]{1,0:T(8,128)(2,1)S(1)}, bf16[512,512]{1,0:T(8,128)(2,1)S(1)}, u32[]{:S(2)}, u32[]{:S(2)}) collective-permute-start(bf16[512,512]{1,0:T(8,128)(2,1)S(1)} %get-tuple-element.112), channel_id=1, source_target_pairs={{0,192},{64,128},{128,64},{192,0},{1,193},{65,129},{129,65},{193,1... | collective-permute-start | bytes 1572872 | tf_op jit(solution)/shard_map/ppermute | solution.py:34
  121.7 19.3 %collective-permute-start.11 = (f32[8,2048]{1,0:T(8,128)S(1)}, f32[8,2048]{1,0:T(8,128)S(1)}, u32[]{:S(2)}, u32[]{:S(2)}) collective-permute-start(f32[8,2048]{1,0:T(8,128)S(1)} %add.73), channel_id=1, source_target_pairs={{0,32},{16,48},{32,0},{48,16},{1,33},{17,49},{33,1},{49,17},{2,34}... | collective-permute-start | bytes 196616 | tf_op jit(solution)/shard_map/ppermute | solution.py:34
  128.1 13.4 %collective-permute-start.10 = (f32[8,2048]{1,0:T(8,128)S(1)}, f32[8,2048]{1,0:T(8,128)S(1)}, u32[]{:S(2)}, u32[]{:S(2)}) collective-permute-start(f32[8,2048]{1,0:T(8,128)S(1)} %add.73), channel_id=1, source_target_pairs={{0,48},{16,32},{32,16},{48,0},{1,49},{17,33},{33,17},{49,1},{2,50}... | collective-permute-start | bytes 196616 | tf_op jit(solution)/shard_map/ppermute | solution.py:34
  128.7 12.8 %collective-permute-start.9 = (f32[8,2048]{1,0:T(8,128)S(1)}, f32[8,2048]{1,0:T(8,128)S(1)}, u32[]{:S(2)}, u32[]{:S(2)}) collective-permute-start(f32[8,2048]{1,0:T(8,128)S(1)} %add.73), channel_id=1, source_target_pairs={{0,16},{16,0},{32,48},{48,32},{1,17},{17,1},{33,49},{49,33},{2,18}... | collective-permute-start | bytes 196616 | tf_op jit(solution)/shard_map/ppermute | solution.py:34
  143.5 1.0 copy-start.19
  144.5 8.5 %copy-start.17 = (bf16[2048,128]{1,0:T(8,128)(2,1)S(1)}, bf16[2048,128]{1,0:T(8,128)(2,1)}, u32[]{:S(2)}) copy-start(bf16[2048,128]{1,0:T(8,128)(2,1)} %pad.22.weight) | copy-start | bytes 1572868
  144.5 33.4 %all-to-all-start.4 = ((bf16[8,64,1024]{2,1,0:T(8,128)(2,1)}), bf16[8,64,1024]{2,1,0:T(8,128)(2,1)S(1)}, u32[]{:S(2)}, u32[]{:S(2)}) async-start(bf16[8,64,1024]{2,1,0:T(8,128)(2,1)} %copy-done.19), calls=%async_computation.4 | async-start | bytes 2097152 | tf_op jit(solution)/shard_map/all_to_all | solution.py:38
  148.2 8.4 %collective-permute-start.14 = (f32[8,2048]{1,0:T(8,128)S(1)}, f32[8,2048]{1,0:T(8,128)S(1)}, u32[]{:S(2)}, u32[]{:S(2)}) collective-permute-start(f32[8,2048]{1,0:T(8,128)S(1)} %add_add_fusion.2), channel_id=1, source_target_pairs={{0,4},{2,6},{4,0},{6,2},{1,5},{3,7},{5,1},{7,3},{8,12},{10,14},{12... | collective-permute-start | bytes 196616 | tf_op jit(solution)/shard_map/ppermute | solution.py:34
  150.4 6.1 %collective-permute-start.13 = (f32[8,2048]{1,0:T(8,128)S(1)}, f32[8,2048]{1,0:T(8,128)S(1)}, u32[]{:S(2)}, u32[]{:S(2)}) collective-permute-start(f32[8,2048]{1,0:T(8,128)S(1)} %add_add_fusion.2), channel_id=1, source_target_pairs={{0,6},{2,4},{4,2},{6,0},{1,7},{3,5},{5,3},{7,1},{8,14},{10,12},{12... | collective-permute-start | bytes 196616 | tf_op jit(solution)/shard_map/ppermute | solution.py:34
  150.4 6.1 %collective-permute-start.12 = (f32[8,2048]{1,0:T(8,128)S(1)}, f32[8,2048]{1,0:T(8,128)S(1)}, u32[]{:S(2)}, u32[]{:S(2)}) collective-permute-start(f32[8,2048]{1,0:T(8,128)S(1)} %add_add_fusion.2), channel_id=1, source_target_pairs={{0,2},{2,0},{4,6},{6,4},{1,3},{3,1},{5,7},{7,5},{8,10},{10,8},{12,... | collective-permute-start | bytes 196616 | tf_op jit(solution)/shard_map/ppermute | solution.py:34
  156.6 6.4 %collective-permute-start.17 = (f32[8,2048]{1,0:T(8,128)S(1)}, f32[8,2048]{1,0:T(8,128)S(1)}, u32[]{:S(2)}, u32[]{:S(2)}) collective-permute-start(f32[8,2048]{1,0:T(8,128)S(1)} %add_add_fusion.1), channel_id=1, source_target_pairs={{0,128},{64,192},{128,0},{192,64},{1,129},{65,193},{129,1},{193,65... | collective-permute-start | bytes 196616 | tf_op jit(solution)/shard_map/ppermute | solution.py:34
  157.7 5.8 %collective-permute-start.16 = (f32[8,2048]{1,0:T(8,128)S(1)}, f32[8,2048]{1,0:T(8,128)S(1)}, u32[]{:S(2)}, u32[]{:S(2)}) collective-permute-start(f32[8,2048]{1,0:T(8,128)S(1)} %add_add_fusion.1), channel_id=1, source_target_pairs={{0,192},{64,128},{128,64},{192,0},{1,193},{65,129},{129,65},{193,1... | collective-permute-start | bytes 196616 | tf_op jit(solution)/shard_map/ppermute | solution.py:34
  160.0 4.3 %collective-permute-start.15 = (f32[8,2048]{1,0:T(8,128)S(1)}, f32[8,2048]{1,0:T(8,128)S(1)}, u32[]{:S(2)}, u32[]{:S(2)}) collective-permute-start(f32[8,2048]{1,0:T(8,128)S(1)} %add_add_fusion.1), channel_id=1, source_target_pairs={{0,64},{64,0},{128,192},{192,128},{1,65},{65,1},{129,193},{193,129... | collective-permute-start | bytes 196616 | tf_op jit(solution)/shard_map/ppermute | solution.py:34
  164.3 10.8 %collective-permute-start.18 = (f32[8,2048]{1,0:T(8,128)S(1)}, f32[8,2048]{1,0:T(8,128)S(1)}, u32[]{:S(2)}, u32[]{:S(2)}) collective-permute-start(f32[8,2048]{1,0:T(8,128)S(1)} %add_add_fusion), channel_id=1, source_target_pairs={{0,1},{1,0},{2,3},{3,2},{4,5},{5,4},{6,7},{7,6},{8,9},{9,8},{10,11... | collective-permute-start | bytes 196616 | tf_op jit(solution)/shard_map/ppermute | solution.py:34
